TPU v7x, 32 devices: a whole 2x2x4 slice. The times are simulated.
32 devices in a mesh: groups: 2 (over y), doc: 16 (over z, x, core), term: 1.
Axes of the slice: x: 2, y: 2, z: 4, core: 2. Of those that a mesh axis runs over, the one named last changes fastest.
Arguments:
- hidden_states: bfloat16 [4096, 768], P(('groups', 'doc')), parts along dimension 0, may hold values from -6 to 6
- doc_lengths: int32 [32], P(('groups', 'doc')), parts along dimension 0, may hold values from 1 to 128, 1536 in all
- transform_weight: bfloat16 [768, 768], P('doc', 'term'), may hold values from -0.21875 to 0.21875
- transform_bias: float32 [768], replicated, may hold values from -3 to 3
- norm_gain: float32 [768], replicated, may hold values from 0.5 to 1.5
- norm_bias: float32 [768], replicated, may hold values from -2 to 2
- decoder_weight: bfloat16 [1, 768, 15360], P('term', None, 'doc'), may hold values from -0.21875 to 0.21875
- decoder_bias: float32 [15360], P('term'), may hold values from -3 to 3
- tile_ids: int32 [1, 32, 32], P('term', ('groups', 'doc')), parts along dimension 1, may hold values from 0 to 119, all different within a row
- owner_ids: int32 [1, 32, 32, 1], P('term', ('groups', 'doc')), parts along dimension 1, may hold values from 0 to 15; in each aligned block of 32 rows (0 to 31, 32 to 63, ..., all dimensions but the last counted through in order) at most 4 rows name the same one
- block_slots: int32 [1, 32, 32], P('term', ('groups', 'doc')), parts along dimension 1, may hold values from 0 to 1
Outputs:
- impacts: bfloat16 [32, 15360], P(('groups', 'doc'), 'term'), parts along dimension 0
- summaries: bfloat16 [64, 15360], P(('groups', 'doc'), 'term'), parts along dimension 0
There are 2 independent parts, one for each index of `groups`. A program takes and returns all parts, laid end to end along the dimension named above; an argument that names none is the same for every part. Nothing has to cross between parts.
Inputs may be any that keep to these rules, and one draw needn't show every extreme that they name: `tile_ids`: the 32 tiles of one half and document are different. `owner_ids`: among the 32 entries of one index of doc and one half, no owner is named more than 4 times, a bound that some block reaches. `doc_lengths`: some document of each group has all 128 tokens; the stated total is that of one group's 16 documents, 1536, and each group's lengths sum to it separately.
All inputs are finite; a program needn't handle non-finite values.
Results may differ from a plain program's by a relative error of at most 0.0034.
Values may be sent and summed in bfloat16 or wider, within the bound.
No kernel may reach another device: no remote copies, remote signals or barrier semaphores. Data moves between devices by JAX's collectives and lax.ppermute only.
A program may use at most 128 MiB of HBM per device.

v0:
```python
import jax
import jax.numpy as jnp
from jax import lax
from jax.sharding import PartitionSpec as P

TILE = 128
BLK_DEV = 2


def layer_norm(activated, norm_gain, norm_bias):
    values = activated.astype(jnp.float32)
    centre = jnp.mean(values, axis=-1, keepdims=True)
    centred = values - centre
    spread = jnp.mean(centred * centred, axis=-1, keepdims=True)
    return (centred * lax.rsqrt(spread + 1e-05) * norm_gain + norm_bias).astype(jnp.bfloat16)


def pool_docs(logits, keep):
    docs_here = keep.shape[0]
    saturated = jnp.log1p(jnp.maximum(logits, 0.0)).reshape(
        docs_here, keep.shape[1], logits.shape[1]
    )
    return jnp.max(jnp.where(keep[:, :, None], saturated, 0.0), axis=1)


def local(
    hidden_states,
    doc_lengths,
    transform_weight,
    transform_bias,
    norm_gain,
    norm_bias,
    decoder_weight,
    decoder_bias,
    tile_ids,
    owner_ids,
    block_slots,
):
    tok_rows = hidden_states.shape[0]
    docs_here = doc_lengths.shape[0]
    seq_len = tok_rows // docs_here
    cols = transform_weight.shape[1]
    pre_half = jnp.dot(
        hidden_states,
        lax.all_gather(transform_weight, "doc", axis=0, tiled=True),
        preferred_element_type=jnp.float32,
    )
    bias_half = lax.dynamic_slice_in_dim(transform_bias, lax.axis_index("term") * cols, cols, 0)
    act_half = jax.nn.gelu(pre_half + bias_half, approximate=False).astype(jnp.bfloat16)
    activated = lax.all_gather(act_half, "term", axis=1, tiled=True)
    normed = layer_norm(activated, norm_gain, norm_bias)
    keep = jnp.arange(seq_len, dtype=jnp.int32)[None, :] < doc_lengths[:, None]
    logits = jnp.dot(
        normed,
        lax.all_gather(decoder_weight, "doc", axis=2, tiled=True)[0],
        preferred_element_type=jnp.float32,
    )
    logits = logits + decoder_bias
    impacts = pool_docs(logits, keep).astype(jnp.bfloat16)
    tiles_t = impacts.shape[1] // TILE
    slots_total = BLK_DEV * tiles_t
    tiles = impacts.reshape(docs_here * tiles_t, TILE)
    chosen = tile_ids[0]
    doc_index = jnp.arange(docs_here, dtype=jnp.int32)[:, None]
    posted = tiles[(doc_index * tiles_t + chosen).reshape(-1)]
    owners = owner_ids[0, :, :, 0].reshape(-1)
    target = block_slots[0].reshape(-1) * tiles_t + chosen.reshape(-1)
    owner_count = lax.axis_size("doc")
    capacity = max(2, 2 * posted.shape[0] // owner_count)
    onehot = (owners[:, None] == jnp.arange(owner_count, dtype=jnp.int32)[None, :]).astype(
        jnp.int32
    )
    before = jnp.cumsum(onehot, axis=0) - onehot
    position = jnp.sum(before * onehot, axis=1)
    dest = owners * capacity + position
    outgoing = jnp.zeros((owner_count * capacity, TILE), jnp.bfloat16).at[dest].set(posted)
    out_tags = jnp.full((owner_count * capacity,), slots_total, jnp.int32).at[dest].set(target)
    got_vals, got_tags = (
        lax.all_to_all(
            outgoing.reshape(owner_count, capacity, TILE),
            "doc",
            split_axis=0,
            concat_axis=0,
            tiled=True,
        ),
        lax.all_to_all(
            out_tags.reshape(owner_count, capacity), "doc", split_axis=0, concat_axis=0, tiled=True
        ),
    )
    got_vals = got_vals.reshape(-1, TILE)
    local_tags = got_tags.reshape(-1)
    summary = jnp.zeros((slots_total, TILE), jnp.bfloat16).at[local_tags].max(got_vals, mode="drop")
    return (impacts, summary.reshape(BLK_DEV, tiles_t * TILE))


def solution(mesh):
    placed = (
        P(("groups", "doc"), None),
        P(("groups", "doc")),
        P("doc", "term"),
        P(),
        P(),
        P(),
        P("term", None, "doc"),
        P("term"),
        P("term", ("groups", "doc"), None),
        P("term", ("groups", "doc"), None, None),
        P("term", ("groups", "doc"), None),
    )
    return jax.shard_map(
        local,
        mesh=mesh,
        in_specs=placed,
        out_specs=(P(("groups", "doc"), "term"), P(("groups", "doc"), "term")),
        check_vma=False,
    )
```

profile of v0, /device:TPU:0, one launch (start us, length us, event | category | flops | bytes accessed | tf_op | source)
XLA Modules:
  0.0 206.9 jit_solution(18115880106351156402)
XLA Ops:
  7.2 0.0 copy-start
  7.2 0.0 copy-start.3
  7.2 0.0 copy-start.2
  7.2 0.0 copy-start.1
  7.2 0.0 all-gather.3.cloned.1.call-start
  7.3 0.7 all-gather.3.cloned.1.call-update
  7.9 0.0 all-gather.5.cloned.1.call-start
  8.0 0.7 all-gather.5.cloned.1.call-update
  8.7 0.7 fusion.40
  9.4 0.1 reduce_window_sum.11
  9.5 0.8 select_reduce_fusion
  10.3 0.7 fusion.44
  11.0 0.7 add_bitcast_fusion
  11.7 0.7 scatter_custom_fusion
  12.3 0.7 all_to_all.9
  13.0 7.4 %all-to-all-start = ((s32[16,1,4]{2,1,0:T(1,128)}), s32[16,1,4]{2,1,0:T(1,128)S(1)}, u32[]{:S(2)}, u32[]{:S(2)}) async-start(s32[16,1,4]{2,1,0:T(1,128)} %bitcast.7), calls=%async_computation | async-start | bytes 16384 | tf_op jit(solution)/shard_map/all_to_all | solution.py:86
  21.0 0.7 fusion.46
  21.7 5.0 %all-to-all-done = s32[16,1,4]{2,1,0:T(1,128)S(1)} async-done(((s32[16,1,4]{2,1,0:T(1,128)}), s32[16,1,4]{2,1,0:T(1,128)S(1)}, u32[]{:S(2)}, u32[]{:S(2)}) %all-to-all-start) | async-done | bytes 288 | tf_op jit(solution)/shard_map/all_to_all | solution.py:86
  26.7 0.5 broadcast.137
  27.2 0.7 reduce.5
  27.9 0.1 reshape.152
  28.0 23.4 %all-gather.3.cloned.1.call-done = bf16[768,768]{1,0:T(8,128)(2,1)} async-done(((bf16[48,768]{1,0:T(8,128)(2,1)}), bf16[768,768]{1,0:T(8,128)(2,1)}) %all-gather.3.cloned.1.call-update) | async-done | bytes 1179664 | tf_op jit(solution)/shard_map/all_gather | solution.py:45
  51.4 0.0 copy-done
  51.4 2.5 %convert_reduce_fusion = (f32[128]{0:T(128)S(1)}, bf16[128,768]{1,0:T(8,128)(2,1)S(1)}) fusion(f32[768]{0:T(1024)} %param.14, bf16[128,768]{1,0:T(8,128)(2,1)S(1)} %copy-done, bf16[768,768]{1,0:T(8,128)(2,1)} %all-gather.3.cloned.1.call-done), kind=kOutput, calls=%fused_computation.14 | convolution fusion | flops 157679488 | bytes 1576448 | tf_op jit(solution)/shard_map/dot_general | solution.py:43
  53.9 0.2 fusion.19
  54.1 119.1 %all-gather.5.cloned.1.call-done = bf16[1,768,15360]{1,2,0:T(8,128)(2,1)} async-done(((bf16[1,768,960]{1,2,0:T(8,128)(2,1)}), bf16[1,768,15360]{1,2,0:T(8,128)(2,1)}) %all-gather.5.cloned.1.call-update) | async-done | bytes 23592976 | tf_op jit(solution)/shard_map/all_gather | solution.py:55
  173.2 0.0 copy-done.3
  173.2 0.0 copy-done.2
  173.2 0.0 copy-done.1
  173.2 12.8 %fusion.14 = bf16[15360]{0:T(1024)(128)(2,1)S(1)} fusion(f32[15360]{0:T(1024)S(1)} %copy-done.1, bf16[1,768,15360]{1,2,0:T(8,128)(2,1)} %all-gather.5.cloned.1.call-done, pred[128]{0:T(512)(128)(4,1)S(1)} %iota_compare_fusion.1, bf16[128,768]{1,0:T(8,128)(2,1)S(1)} %get-tuple-element.3, f32[768]{0:T(1024)S(1)} %copy-done.2, f32[768]{0:T(1024)S(1)} %copy-done.3, ...), kind=kOutput, calls=%fused_computation.10 | convolution fusion | flops 3028337664 | bytes 23889024 | tf_op jit(solution)/shard_map/dot_general | solution.py:53
  185.9 1.3 scatter_custom_fusion.1
  187.3 4.7 %all-to-all-start.1 = ((bf16[16,4,128]{2,1,0:T(4,128)(2,1)}), bf16[16,4,128]{2,1,0:T(4,128)(2,1)S(1)}, u32[]{:S(2)}, u32[]{:S(2)}) async-start(bf16[16,4,128]{2,1,0:T(4,128)(2,1)} %bitcast.12), calls=%async_computation.1 | async-start | bytes 32768 | tf_op jit(solution)/shard_map/all_to_all | solution.py:79
  192.0 0.7 convert_element_type.34
  192.6 5.8 %all-to-all-done.1 = bf16[16,4,128]{2,1,0:T(4,128)(2,1)S(1)} async-done(((bf16[16,4,128]{2,1,0:T(4,128)(2,1)}), bf16[16,4,128]{2,1,0:T(4,128)(2,1)S(1)}, u32[]{:S(2)}, u32[]{:S(2)}) %all-to-all-start.1) | async-done | bytes 16416 | tf_op jit(solution)/shard_map/all_to_all | solution.py:79
  198.5 0.9 scatter_custom_fusion.2
  199.4 0.6 reshape.155
  (5 shorter events, 0.0 us)
Async XLA Ops:
  7.2 44.2 %copy-start = (bf16[128,768]{1,0:T(8,128)(2,1)S(1)}, bf16[128,768]{1,0:T(8,128)(2,1)}, u32[]{:S(2)}) copy-start(bf16[128,768]{1,0:T(8,128)(2,1)} %param.11) | copy-start | bytes 589828
  7.2 166.0 %copy-start.3 = (f32[768]{0:T(1024)S(1)}, f32[768]{0:T(1024)}, u32[]{:S(2)}) copy-start(f32[768]{0:T(1024)} %param.15) | copy-start | bytes 9220
  7.2 166.0 %copy-start.2 = (f32[768]{0:T(1024)S(1)}, f32[768]{0:T(1024)}, u32[]{:S(2)}) copy-start(f32[768]{0:T(1024)} %param.16) | copy-start | bytes 9220
  7.2 166.0 %copy-start.1 = (f32[15360]{0:T(1024)S(1)}, f32[15360]{0:T(1024)}, u32[]{:S(2)}) copy-start(f32[15360]{0:T(1024)} %param.18) | copy-start | bytes 184324
  7.2 44.2 %all-gather.3.cloned.1.call-start = ((), (), s32[]{:S(2)}) async-start(), calls=%async_computation.2 | async-start | bytes 1253376 | tf_op jit(solution)/shard_map/all_gather | solution.py:45
  7.9 165.2 %all-gather.5.cloned.1.call-start = ((), (), s32[]{:S(2)}) async-start(), calls=%async_computation.3 | async-start | bytes 25067520 | tf_op jit(solution)/shard_map/all_gather | solution.py:55
  13.0 13.7 %all-to-all-start = ((s32[16,1,4]{2,1,0:T(1,128)}), s32[16,1,4]{2,1,0:T(1,128)S(1)}, u32[]{:S(2)}, u32[]{:S(2)}) async-start(s32[16,1,4]{2,1,0:T(1,128)} %bitcast.7), calls=%async_computation | async-start | bytes 16384 | tf_op jit(solution)/shard_map/all_to_all | solution.py:86
  187.3 11.2 %all-to-all-start.1 = ((bf16[16,4,128]{2,1,0:T(4,128)(2,1)}), bf16[16,4,128]{2,1,0:T(4,128)(2,1)S(1)}, u32[]{:S(2)}, u32[]{:S(2)}) async-start(bf16[16,4,128]{2,1,0:T(4,128)(2,1)} %bitcast.12), calls=%async_computation.1 | async-start | bytes 32768 | tf_op jit(solution)/shard_map/all_to_all | solution.py:79
Sparse Core Ops, SparseCore 0:
  10.3 41.0 all-gather.2
  53.0 120.1 all-gather.4
where the time goes:
time: 207 us
  waiting for transfers between devices  155 us (75%)
  matrix products  15.2 us (7%)
  between operations  14.8 us (7%)
  starting transfers between devices  12.1 us (6%)
  other arithmetic  5.45 us (3%)
  local copies, waits for them, and re-layouts  4.62 us (2%)
    all_gather x1, waiting for transfers between devices, local(): lax.all_gather(decoder_weight, 'doc', axis=2, tiled=True)[0]  119 us
    all_gather x1, waiting for transfers between devices, local(): lax.all_gather(transform_weight, 'doc', axis=0, tiled=True)  23.4 us
    dot_general x1, matrix products, local(): jnp.dot(normed, lax.all_gather(decoder_weight, 'doc', axis=2, tiled=True)...  12.8 us
    all_to_all x1, starting transfers between devices, local(): lax.all_to_all(out_tags.reshape(owner_count, capacity), 'doc', split_axis...  7.36 us
    all_to_all x1, waiting for transfers between devices, local(): lax.all_to_all(outgoing.reshape(owner_count, capacity, TILE), 'doc', spli...  5.83 us
    all_to_all x1, waiting for transfers between devices, local(): lax.all_to_all(out_tags.reshape(owner_count, capacity), 'doc', split_axis...  5.01 us
    all_to_all x1, starting transfers between devices, local(): lax.all_to_all(outgoing.reshape(owner_count, capacity, TILE), 'doc', spli...  4.69 us
  transfers between devices with their start and end apart: 4, of which 4 were waited for; matrix products, arithmetic and copies ran while one was open for 4% of the time, Pallas kernels for 0%

commit v1 on v0

--- a/solution.py
+++ b/solution.py
@@ -1,10 +1,13 @@
 import jax
 import jax.numpy as jnp
 from jax import lax
+from jax.experimental import pallas as pl
+from jax.experimental.pallas import tpu as pltpu
 from jax.sharding import PartitionSpec as P
 
 TILE = 128
 BLK_DEV = 2
+SLOT_ROWS = 16
 
 
 def layer_norm(activated, norm_gain, norm_bias):
@@ -23,7 +26,7 @@
     return jnp.max(jnp.where(keep[:, :, None], saturated, 0.0), axis=1)
 
 
-def local(
+def move_weights(
     hidden_states,
     doc_lengths,
     transform_weight,
@@ -93,6 +96,176 @@
     return (impacts, summary.reshape(BLK_DEV, tiles_t * TILE))
 
 
+def dot_t(left, right):
+    return lax.dot_general(
+        left, right, (((1,), (1,)), ((), ())), preferred_element_type=jnp.float32
+    )
+
+
+def head_kernel(chips, order, *refs):
+    places = len(order)
+    (place_ref, meta_ref), refs = refs[:2], refs[2:]
+    hidden_refs, refs = refs[:places], refs[places:]
+    weight_refs, refs = refs[:places], refs[places:]
+    other_weight_ref, refs = refs[0], refs[1:]
+    tbias_ref, gain_ref, nbias_ref, mine_ref, theirs_ref, dbias_ref, out_ref = refs[:7]
+    tokens, weight, best_mine, best_theirs, send = refs[7:]
+    core = place_ref[0]
+    chip = place_ref[1]
+    seq = hidden_refs[0].shape[0]
+    rows = weight_refs[0].shape[0]
+    half = mine_ref.shape[0]
+    tiles = 2 * half // TILE
+    for k in range(places):
+        source = place_ref[2 + k]
+        doc = 2 * source + core
+        length = meta_ref[doc, TILE - 1]
+        here = hidden_refs[k][...]
+        keep = lax.broadcasted_iota(jnp.int32, here.shape, 0) < length
+        first = jnp.broadcast_to(here[0:1, :].astype(jnp.float32), here.shape).astype(here.dtype)
+        tokens[pl.ds(pl.multiple_of(source * seq, seq), seq), :] = jnp.where(keep, here, first)
+        at = pl.multiple_of(doc * rows, 16)
+        weight[pl.ds(at, rows), :] = weight_refs[k][...]
+        at = pl.multiple_of((2 * source + 1 - core) * rows, 16)
+        weight[pl.ds(at, rows), :] = other_weight_ref[k * rows : (k + 1) * rows, :]
+
+    def two_docs(step, carry):
+        at = pl.multiple_of(step * 2 * seq, 2 * seq)
+        pre = jnp.dot(
+            tokens[pl.ds(at, 2 * seq), :], weight[...], preferred_element_type=jnp.float32
+        )
+        pre = pre + tbias_ref[...]
+        act = 0.5 * pre * (1.0 + lax.erf(pre * (0.5**0.5)))
+        normed = layer_norm(act.astype(jnp.bfloat16), gain_ref[...], nbias_ref[...])
+        for w_ref, best in ((mine_ref, best_mine), (theirs_ref, best_theirs)):
+            logits = dot_t(normed, w_ref[...])
+            for j in range(2):
+                top = jnp.max(logits[j * seq : (j + 1) * seq], axis=0, keepdims=True)
+                best[pl.ds(2 * step + j, 1), :] = top
+        return carry
+
+    lax.fori_loop(0, places // 2, two_docs, 0)
+    mine, theirs = best_mine[...], best_theirs[...]
+    low = jnp.where(core == 0, mine, theirs)
+    high = jnp.where(core == 0, theirs, mine)
+    logits = jnp.concatenate([low, high], axis=1) + dbias_ref[...]
+    impacts = jnp.log1p(jnp.maximum(logits, 0.0)).astype(jnp.bfloat16).astype(jnp.float32)
+    send[...] = jnp.zeros(send.shape, jnp.float32)
+    devices = 2 * chips
+    stride = out_ref.shape[1]
+    target = lax.broadcasted_iota(jnp.int32, (BLK_DEV * devices, TILE), 0)
+    for t in range(tiles):
+        tile = impacts[:, t * TILE : (t + 1) * TILE]
+        for c in range(2):
+            send[pl.ds(c * stride + t, chips, stride=2 * stride), :] = tile
+        blocks = jnp.zeros((BLK_DEV * devices, TILE), jnp.float32)
+        for k in range(chips):
+            block = meta_ref[2 * k + core, chip * tiles + t]
+            blocks = jnp.maximum(blocks, jnp.where(target == block, tile[k : k + 1, :], 0.0))
+        for s in range(BLK_DEV):
+            send[pl.ds((1 + s) * SLOT_ROWS + t, devices, stride=stride), :] = blocks[
+                s * devices : (s + 1) * devices
+            ]
+    out_ref[...] = send[...].astype(jnp.bfloat16).reshape(out_ref.shape)
+
+
+def move_tokens(
+    hidden_states,
+    doc_lengths,
+    transform_weight,
+    transform_bias,
+    norm_gain,
+    norm_bias,
+    decoder_weight,
+    decoder_bias,
+    tile_ids,
+    owner_ids,
+    block_slots,
+):
+    devices = lax.axis_size("doc")
+    chips = devices // 2
+    layers = chips // 2
+    seq, width = hidden_states.shape
+    half = decoder_weight.shape[2]
+    tiles = 2 * half // TILE
+    me = lax.axis_index("doc")
+    core, chip = me % 2, me // 2
+    layer, side = chip // 2, chip % 2
+
+    def flip(value, bit):
+        return lax.ppermute(value, "doc", [(i, i ^ bit) for i in range(devices)])
+
+    def shift(value, by):
+        return lax.ppermute(value, "doc", [(i, (i + 4 * by) % devices) for i in range(devices)])
+
+    wanted = block_slots[0, 0] * devices + owner_ids[0, 0, :, 0]
+    lane = jnp.arange(TILE, dtype=jnp.int32)
+    posted = tile_ids[0, 0][:, None] == lane[None, :]
+    table = jnp.sum(jnp.where(posted, wanted[:, None] + 1, 0), axis=0) - 1
+    table = jnp.where(lane == TILE - 1, doc_lengths[0], table)
+    meta = lax.all_gather(table[None, :], "doc", axis=0, tiled=True)
+
+    weight_rows = jnp.swapaxes(decoder_weight[0], 0, 1)
+    by_layer = [transform_weight] + [shift(transform_weight, s) for s in range(1, layers)]
+    other_half = flip(weight_rows, 1)
+    hidden = [hidden_states] + [shift(hidden_states, s) for s in range(1, layers)]
+    by_layer_across = [flip(value, 2) for value in by_layer]
+    hidden_across = [flip(value, 2) for value in hidden]
+    weights = by_layer + by_layer_across
+    other_weights = flip(jnp.concatenate(weights, axis=0), 1)
+    hiddens = hidden + hidden_across
+    order = [(s, f) for f in range(2) for s in range(layers)]
+    sources = [((layer - s) % layers) * 2 + (side ^ f) for s, f in order]
+    place = jnp.stack([core, chip] + sources).astype(jnp.int32)
+    bias = lax.dynamic_slice_in_dim(decoder_bias, chip * 2 * half, 2 * half, 0)
+
+    smem = pl.BlockSpec(memory_space=pltpu.SMEM)
+    vmem = pl.BlockSpec(memory_space=pltpu.VMEM)
+    send = pl.pallas_call(
+        lambda *refs: head_kernel(chips, order, *refs),
+        out_shape=jax.ShapeDtypeStruct(
+            (devices, (1 + BLK_DEV) * SLOT_ROWS, TILE), jnp.bfloat16
+        ),
+        in_specs=[smem, smem] + [vmem] * (2 * chips + 1 + 6),
+        out_specs=vmem,
+        scratch_shapes=[
+            pltpu.VMEM((chips * seq, width), jnp.bfloat16),
+            pltpu.VMEM((width, width), jnp.bfloat16),
+            pltpu.VMEM((chips, half), jnp.float32),
+            pltpu.VMEM((chips, half), jnp.float32),
+            pltpu.VMEM((devices * (1 + BLK_DEV) * SLOT_ROWS, TILE), jnp.float32),
+        ],
+        compiler_params=pltpu.CompilerParams(vmem_limit_bytes=32 * 1024 * 1024),
+        cost_estimate=pl.CostEstimate(
+            flops=2 * chips * seq * width * (width + 2 * half),
+            bytes_accessed=6 * 1024 * 1024,
+            transcendentals=chips * seq * width,
+        ),
+    )(
+        place,
+        meta,
+        *hiddens,
+        *weights,
+        other_weights,
+        transform_bias[None, :],
+        norm_gain[None, :],
+        norm_bias[None, :],
+        weight_rows,
+        other_half,
+        bias[None, :],
+    )
+    got = lax.all_to_all(send, "doc", split_axis=0, concat_axis=0, tiled=True)
+    got = got.reshape(chips, 2, 1 + BLK_DEV, SLOT_ROWS, TILE)[:, :, :, :tiles]
+    impacts = lax.dynamic_index_in_dim(got[:, :, 0], core, 1, keepdims=False)
+    summaries = jnp.maximum(got[:, 0, 1:], got[:, 1, 1:])
+    summaries = jnp.swapaxes(summaries, 0, 1)
+    return (impacts.reshape(1, -1), summaries.reshape(BLK_DEV, -1))
+
+
+def tokens_move(mesh):
+    return mesh.shape["term"] == 1 and mesh.shape["doc"] % 4 == 0
+
+
 def solution(mesh):
     placed = (
         P(("groups", "doc"), None),
@@ -107,6 +280,15 @@
         P("term", ("groups", "doc"), None, None),
         P("term", ("groups", "doc"), None),
     )
+
+    def local(*args):
+        pair = 2 * args[6].shape[2]
+        tiles = pair * (mesh.shape["doc"] // 2) // TILE
+        fits = pair % TILE == 0 and tiles < TILE and pair // TILE <= SLOT_ROWS
+        if tokens_move(mesh) and args[1].shape[0] == 1 and fits:
+            return move_tokens(*args)
+        return move_weights(*args)
+
     return jax.shard_map(
         local,
         mesh=mesh,

time: 207 us -> 91.6 us (0.44)
  waiting for transfers between devices: 155 us -> 20.7 us
  blocking collectives: 0 us -> 23.5 us
  matrix products: 15.2 us -> 0 us
  between operations: 14.8 us -> 1.39 us
  starting transfers between devices: 12.1 us -> 23.3 us
  Pallas kernels: 0 us -> 9.24 us
  local copies, waits for them, and re-layouts: 4.62 us -> 11.6 us
  other arithmetic: 5.45 us -> 1.44 us
    all_gather x2 -> x0, waiting for transfers between devices: 142 us -> none  [the longest x1 119 us: local(): lax.all_gather(decoder_weight, 'doc', axis=2, tiled=True)[0]]
    all_gather x0 -> x1, blocking collectives: none -> 23.5 us  [move_tokens(): meta = lax.all_gather(table[None, :], 'doc', axis=0, tiled=True)]
    ppermute x0 -> x16, starting transfers between devices: none -> 19.7 us  [the longest x6 11.1 us: shift(): lax.ppermute(value, 'doc', [(i, (i + 4 * by) % devices) for i in range(de...]
    dot_general x2 -> x0, matrix products: 15.2 us -> none  [the longest x1 12.8 us: local(): jnp.dot(normed, lax.all_gather(decoder_weight, 'doc', axis=2, tiled=True)...]
    ppermute x0 -> x16, waiting for transfers between devices: none -> 11.8 us  [the longest x6 8.56 us: shift(): lax.ppermute(value, 'doc', [(i, (i + 4 * by) % devices) for i in range(de...]
    pallas_call x0 -> x1, Pallas kernels: none -> 9.24 us  [move_tokens(): pl.pallas_call(lambda *refs: head_kernel(chips, order, *refs), out_shape=...]
    all_to_all x2 -> x1, starting transfers between devices: 12 us -> 3.52 us  [move_tokens(): got = lax.all_to_all(send, 'doc', split_axis=0, concat_axis=0, tiled=True)]
    unnamed x8 -> x14, local copies, waits for them, and re-layouts: 0.02 us -> 6.72 us
  transfers between devices with their start and end apart: 4 -> 17, of which waited for: 4 -> 4; matrix products, arithmetic and copies ran while one was open for 4% -> 11% of each run, Pallas kernels for 0% -> 0%
where the time goes in v1:
time: 91.6 us; the launch traced here: 91.1 us
  blocking collectives  23.5 us (26%)
  starting transfers between devices  23.3 us (25%)
  waiting for transfers between devices  20.7 us (23%)
  local copies, waits for them, and re-layouts  11.6 us (13%)
  Pallas kernels  9.24 us (10%)
  other arithmetic  1.44 us (2%)
  between operations  1.39 us (2%)
    all_gather x1, blocking collectives, move_tokens(): meta = lax.all_gather(table[None, :], 'doc', axis=0, tiled=True)  23.5 us
    ppermute x6, starting transfers between devices, shift(): lax.ppermute(value, 'doc', [(i, (i + 4 * by) % devices) for i in range(de...  11.1 us
    pallas_call x1, Pallas kernels, move_tokens(): pl.pallas_call(lambda *refs: head_kernel(chips, order, *refs), out_shape=...  9.24 us
    all_to_all x1, waiting for transfers between devices, move_tokens(): got = lax.all_to_all(send, 'doc', split_axis=0, concat_axis=0, tiled=True)  8.96 us
    ppermute x10, starting transfers between devices, flip(): return lax.ppermute(value, 'doc', [(i, i ^ bit) for i in range(devices)])  8.67 us
    ppermute x6, waiting for transfers between devices, shift(): lax.ppermute(value, 'doc', [(i, (i + 4 * by) % devices) for i in range(de...  8.56 us
    unnamed x14, local copies, waits for them, and re-layouts  6.72 us
    all_to_all x1, starting transfers between devices, move_tokens(): got = lax.all_to_all(send, 'doc', split_axis=0, concat_axis=0, tiled=True)  3.52 us
  transfers between devices with their start and end apart: 17, of which 4 were waited for; matrix products, arithmetic and copies ran while one was open for 11% of the time, Pallas kernels for 0%

profile of v1, /device:TPU:0, one launch (start us, length us, event | category | flops | bytes accessed | tf_op | source)
XLA Modules:
  0.0 91.1 jit_solution(10292848773961858882)
XLA Ops:
  0.6 0.0 copy-start.2
  0.7 3.0 %collective-permute-start.10 = (bf16[48,768]{1,0:T(8,128)(2,1)}, bf16[48,768]{1,0:T(8,128)(2,1)S(1)}, u32[]{:S(2)}, u32[]{:S(2)}) collective-permute-start(bf16[48,768]{1,0:T(8,128)(2,1)} %refs_10_.1), channel_id=1, source_target_pairs={{0,2},{1,3},{2,0},{3,1},{4,6},{5,7},{6,4},{7,5},{8,10},{9,11},{10,... | collective-permute-start | bytes 221192 | tf_op jit(solution)/shard_map/ppermute | solution.py:196
  3.7 3.6 %collective-permute-start.9 = (bf16[48,768]{1,0:T(8,128)(2,1)}, bf16[48,768]{1,0:T(8,128)(2,1)S(1)}, u32[]{:S(2)}, u32[]{:S(2)}) collective-permute-start(bf16[48,768]{1,0:T(8,128)(2,1)} %refs_10_.1), channel_id=1, source_target_pairs={{0,12},{1,13},{2,14},{3,15},{4,0},{5,1},{6,2},{7,3},{8,4},{9,5},{1... | collective-permute-start | bytes 221192 | tf_op jit(solution)/shard_map/ppermute | solution.py:199
  7.3 0.0 collective-permute-start.8
  7.3 1.0 %collective-permute-start.7 = (bf16[48,768]{1,0:T(8,128)(2,1)}, bf16[48,768]{1,0:T(8,128)(2,1)S(1)}, u32[]{:S(2)}, u32[]{:S(2)}) collective-permute-start(bf16[48,768]{1,0:T(8,128)(2,1)} %refs_10_.1), channel_id=1, source_target_pairs={{0,4},{1,5},{2,6},{3,7},{4,8},{5,9},{6,10},{7,11},{8,12},{9,13},{1... | collective-permute-start | bytes 221192 | tf_op jit(solution)/shard_map/ppermute | solution.py:199
  8.3 1.5 %constant_dynamic-update-slice_fusion.7 = bf16[384,768]{1,0:T(8,128)(2,1)} fusion(bf16[48,768]{1,0:T(8,128)(2,1)} %refs_10_.1), kind=kLoop, calls=%fused_computation.10 | loop fusion | bytes 147456
  9.8 0.5 collective-permute-done.9.refs_13_
  10.3 4.2 %collective-permute-start.2 = (bf16[128,768]{1,0:T(8,128)(2,1)}, bf16[128,768]{1,0:T(8,128)(2,1)S(1)}, u32[]{:S(2)}, u32[]{:S(2)}) collective-permute-start(bf16[128,768]{1,0:T(8,128)(2,1)} %refs_2_.1), channel_id=1, source_target_pairs={{0,12},{1,13},{2,14},{3,15},{4,0},{5,1},{6,2},{7,3},{8,4},{9,5},{1... | collective-permute-start | bytes 589832 | tf_op jit(solution)/shard_map/ppermute | solution.py:199
  14.5 0.0 collective-permute-done.8.refs_12_
  14.5 0.5 collective-permute-start.13
  15.0 0.0 collective-permute-done.7.refs_11_
  15.0 1.5 %collective-permute-start.12 = (bf16[48,768]{1,0:T(8,128)(2,1)S(1)}, bf16[48,768]{1,0:T(8,128)(2,1)S(1)}, u32[]{:S(2)}, u32[]{:S(2)}) collective-permute-start(bf16[48,768]{1,0:T(8,128)(2,1)S(1)} %collective-permute-done.8.refs_12_), channel_id=1, source_target_pairs={{0,2},{1,3},{2,0},{3,1},{4,6},{5,7},{6,4},{7,5},{8,10},{9,11},{10,... | collective-permute-start | bytes 221192 | tf_op jit(solution)/shard_map/ppermute | solution.py:196
  16.5 0.6 constant_dynamic-update-slice_fusion.6
  17.1 0.6 constant_dynamic-update-slice_fusion.5
  17.8 0.6 constant_dynamic-update-slice_fusion.4
  18.4 0.5 collective-permute-start.11
  18.9 0.6 constant_dynamic-update-slice_fusion.3
  19.6 3.2 %collective-permute-done.11.refs_15_ = bf16[48,768]{1,0:T(8,128)(2,1)S(1)} collective-permute-done((bf16[48,768]{1,0:T(8,128)(2,1)S(1)}, bf16[48,768]{1,0:T(8,128)(2,1)S(1)}, u32[]{:S(2)}, u32[]{:S(2)}) %collective-permute-start.11) | collective-permute-done | bytes 73760 | tf_op jit(solution)/shard_map/ppermute | solution.py:196
  22.8 0.6 constant_dynamic-update-slice_fusion.2
  23.4 0.6 constant_dynamic-update-slice_fusion.1
  24.0 0.0 collective-permute-done.13.refs_17_
  24.0 0.6 constant_dynamic-update-slice_fusion
  24.7 0.1 collective-permute-start.1
  24.8 2.1 %collective-permute-start = (bf16[128,768]{1,0:T(8,128)(2,1)}, bf16[128,768]{1,0:T(8,128)(2,1)S(1)}, u32[]{:S(2)}, u32[]{:S(2)}) collective-permute-start(bf16[128,768]{1,0:T(8,128)(2,1)} %refs_2_.1), channel_id=1, source_target_pairs={{0,4},{1,5},{2,6},{3,7},{4,8},{5,9},{6,10},{7,11},{8,12},{9,13},{1... | collective-permute-start | bytes 589832 | tf_op jit(solution)/shard_map/ppermute | solution.py:199
  26.9 0.0 collective-permute-done.2.refs_5_
  26.9 0.5 collective-permute-start.3
  27.5 0.7 fusion.2
  28.8 0.7 broadcast_in_dim.34.refs_19_
  29.5 0.7 broadcast_in_dim.35.refs_20_
  30.2 0.7 broadcast_in_dim.36.refs_21_
  30.9 0.8 dynamic_slice.7
  31.7 0.1 stack.43.refs_0_
  31.7 0.7 select_reduce_fusion
  32.5 8.1 %collective-permute-done.1.refs_4_ = bf16[128,768]{1,0:T(8,128)(2,1)S(1)} collective-permute-done((bf16[128,768]{1,0:T(8,128)(2,1)}, bf16[128,768]{1,0:T(8,128)(2,1)S(1)}, u32[]{:S(2)}, u32[]{:S(2)}) %collective-permute-start.1) | collective-permute-done | bytes 196640 | tf_op jit(solution)/shard_map/ppermute | solution.py:199
  40.6 0.5 collective-permute-start.6
  41.1 0.0 collective-permute-done.refs_3_
  41.1 1.5 %collective-permute-start.5 = (bf16[128,768]{1,0:T(8,128)(2,1)S(1)}, bf16[128,768]{1,0:T(8,128)(2,1)S(1)}, u32[]{:S(2)}, u32[]{:S(2)}) collective-permute-start(bf16[128,768]{1,0:T(8,128)(2,1)S(1)} %collective-permute-done.1.refs_4_), channel_id=1, source_target_pairs={{0,2},{1,3},{2,0},{3,1},{4,6},{5,7},{6,4},{7,5},{8,10},{9,11},{10,... | collective-permute-start | bytes 589832 | tf_op jit(solution)/shard_map/ppermute | solution.py:196
  42.6 0.0 collective-permute-done.3.refs_6_
  42.6 0.5 collective-permute-start.4
  43.1 23.5 %all-gather = s32[16,1,128]{2,1,0:T(1,128)S(1)} all-gather(s32[1,1,128]{2,1,0:T(1,128)S(1)} %fusion.1), channel_id=1, replica_groups=mesh['groups'=2,'doc'=16,'term'=1] {'doc'}, dimensions={0}, use_global_device_ids=true | all-gather | bytes 8704 | tf_op jit(solution)/shard_map/all_gather | solution.py:206
  66.6 0.0 collective-permute-done.6.refs_9_
  66.7 0.0 copy-start.1
  66.7 1.4 %copy-done.1 = bf16[1,768,960]{1,2,0:T(8,128)(2,1)S(1)} copy-done((bf16[1,768,960]{1,2,0:T(8,128)(2,1)S(1)}, bf16[1,768,960]{1,2,0:T(8,128)(2,1)}, u32[]{:S(2)}) %copy-start.1) | copy-done | bytes 1474584
  68.0 9.2 %shard_map.122 = bf16[16,48,128]{2,1,0:T(8,128)(2,1)} custom-call(s32[10]{0:T(128)S(1)} %stack.43.refs_0_, s32[16,128]{1,0:T(8,128)S(1)} %bitcast.36, bf16[128,768]{1,0:T(8,128)(2,1)S(1)} %copy-done.2, bf16[128,768]{1,0:T(8,128)(2,1)S(1)} %collective-permute-done.refs_3_, bf16[128,768]{1,0:T(8,128)(2,1)S(1)} %collective-permute-done.1.refs_4_, ...), custom_call_target="tpu_custom_call" | custom-call | flops 4227858432 | bytes 6291456 | tf_op jit(solution)/shard_map/pallas_call | solution.py:224
  77.3 3.5 %all-to-all-start = ((bf16[16,48,128]{2,1,0:T(8,128)(2,1)}), bf16[16,48,128]{2,1,0:T(8,128)(2,1)S(1)}, u32[]{:S(2)}, u32[]{:S(2)}) async-start(bf16[16,48,128]{2,1,0:T(8,128)(2,1)} %shard_map.122), calls=%async_computation | async-start | bytes 393216 | tf_op jit(solution)/shard_map/all_to_all | solution.py:257
  80.8 9.0 %all-to-all-done = bf16[16,48,128]{2,1,0:T(8,128)(2,1)S(1)} async-done(((bf16[16,48,128]{2,1,0:T(8,128)(2,1)}), bf16[16,48,128]{2,1,0:T(8,128)(2,1)S(1)}, u32[]{:S(2)}, u32[]{:S(2)}) %all-to-all-start) | async-done | bytes 196640 | tf_op jit(solution)/shard_map/all_to_all | solution.py:257
  89.8 0.7 reshape.53
  90.5 0.6 reshape.52
  (17 shorter events, 0.1 us)
Async XLA Ops:
  0.6 66.0 %copy-start = (bf16[48,768]{1,0:T(8,128)(2,1)S(1)}, bf16[48,768]{1,0:T(8,128)(2,1)}, u32[]{:S(2)}) copy-start(bf16[48,768]{1,0:T(8,128)(2,1)} %refs_10_.1) | copy-start | bytes 221188
  0.6 66.0 %copy-start.2 = (bf16[128,768]{1,0:T(8,128)(2,1)S(1)}, bf16[128,768]{1,0:T(8,128)(2,1)}, u32[]{:S(2)}) copy-start(bf16[128,768]{1,0:T(8,128)(2,1)} %refs_2_.1) | copy-start | bytes 589828
  0.7 17.7 %collective-permute-start.10 = (bf16[48,768]{1,0:T(8,128)(2,1)}, bf16[48,768]{1,0:T(8,128)(2,1)S(1)}, u32[]{:S(2)}, u32[]{:S(2)}) collective-permute-start(bf16[48,768]{1,0:T(8,128)(2,1)} %refs_10_.1), channel_id=1, source_target_pairs={{0,2},{1,3},{2,0},{3,1},{4,6},{5,7},{6,4},{7,5},{8,10},{9,11},{10,... | collective-permute-start | bytes 221192 | tf_op jit(solution)/shard_map/ppermute | solution.py:196
  3.7 6.6 %collective-permute-start.9 = (bf16[48,768]{1,0:T(8,128)(2,1)}, bf16[48,768]{1,0:T(8,128)(2,1)S(1)}, u32[]{:S(2)}, u32[]{:S(2)}) collective-permute-start(bf16[48,768]{1,0:T(8,128)(2,1)} %refs_10_.1), channel_id=1, source_target_pairs={{0,12},{1,13},{2,14},{3,15},{4,0},{5,1},{6,2},{7,3},{8,4},{9,5},{1... | collective-permute-start | bytes 221192 | tf_op jit(solution)/shard_map/ppermute | solution.py:199
  7.3 7.2 %collective-permute-start.8 = (bf16[48,768]{1,0:T(8,128)(2,1)}, bf16[48,768]{1,0:T(8,128)(2,1)S(1)}, u32[]{:S(2)}, u32[]{:S(2)}) collective-permute-start(bf16[48,768]{1,0:T(8,128)(2,1)} %refs_10_.1), channel_id=1, source_target_pairs={{0,8},{1,9},{2,10},{3,11},{4,12},{5,13},{6,14},{7,15},{8,0},{9,1},... | collective-permute-start | bytes 221192 | tf_op jit(solution)/shard_map/ppermute | solution.py:199
  7.3 7.7 %collective-permute-start.7 = (bf16[48,768]{1,0:T(8,128)(2,1)}, bf16[48,768]{1,0:T(8,128)(2,1)S(1)}, u32[]{:S(2)}, u32[]{:S(2)}) collective-permute-start(bf16[48,768]{1,0:T(8,128)(2,1)} %refs_10_.1), channel_id=1, source_target_pairs={{0,4},{1,5},{2,6},{3,7},{4,8},{5,9},{6,10},{7,11},{8,12},{9,13},{1... | collective-permute-start | bytes 221192 | tf_op jit(solution)/shard_map/ppermute | solution.py:199
  8.3 58.4 %collective-permute-start.15 = (bf16[960,768]{1,0:T(8,128)(2,1)}, bf16[960,768]{1,0:T(8,128)(2,1)S(1)}, u32[]{:S(2)}, u32[]{:S(2)}) collective-permute-start(bf16[960,768]{1,0:T(8,128)(2,1)} %bitcast.37), channel_id=1, source_target_pairs={{0,1},{1,0},{2,3},{3,2},{4,5},{5,4},{6,7},{7,6},{8,9},{9,8},{10,11... | collective-permute-start | bytes 4423688 | tf_op jit(solution)/shard_map/ppermute | solution.py:196
  10.3 16.6 %collective-permute-start.2 = (bf16[128,768]{1,0:T(8,128)(2,1)}, bf16[128,768]{1,0:T(8,128)(2,1)S(1)}, u32[]{:S(2)}, u32[]{:S(2)}) collective-permute-start(bf16[128,768]{1,0:T(8,128)(2,1)} %refs_2_.1), channel_id=1, source_target_pairs={{0,12},{1,13},{2,14},{3,15},{4,0},{5,1},{6,2},{7,3},{8,4},{9,5},{1... | collective-permute-start | bytes 589832 | tf_op jit(solution)/shard_map/ppermute | solution.py:199
  14.5 9.6 %collective-permute-start.13 = (bf16[48,768]{1,0:T(8,128)(2,1)S(1)}, bf16[48,768]{1,0:T(8,128)(2,1)S(1)}, u32[]{:S(2)}, u32[]{:S(2)}) collective-permute-start(bf16[48,768]{1,0:T(8,128)(2,1)S(1)} %collective-permute-done.9.refs_13_), channel_id=1, source_target_pairs={{0,2},{1,3},{2,0},{3,1},{4,6},{5,7},{6,4},{7,5},{8,10},{9,11},{10,... | collective-permute-start | bytes 221192 | tf_op jit(solution)/shard_map/ppermute | solution.py:196
  15.0 8.4 %collective-permute-start.12 = (bf16[48,768]{1,0:T(8,128)(2,1)S(1)}, bf16[48,768]{1,0:T(8,128)(2,1)S(1)}, u32[]{:S(2)}, u32[]{:S(2)}) collective-permute-start(bf16[48,768]{1,0:T(8,128)(2,1)S(1)} %collective-permute-done.8.refs_12_), channel_id=1, source_target_pairs={{0,2},{1,3},{2,0},{3,1},{4,6},{5,7},{6,4},{7,5},{8,10},{9,11},{10,... | collective-permute-start | bytes 221192 | tf_op jit(solution)/shard_map/ppermute | solution.py:196
  18.4 4.4 %collective-permute-start.11 = (bf16[48,768]{1,0:T(8,128)(2,1)S(1)}, bf16[48,768]{1,0:T(8,128)(2,1)S(1)}, u32[]{:S(2)}, u32[]{:S(2)}) collective-permute-start(bf16[48,768]{1,0:T(8,128)(2,1)S(1)} %collective-permute-done.7.refs_11_), channel_id=1, source_target_pairs={{0,2},{1,3},{2,0},{3,1},{4,6},{5,7},{6,4},{7,5},{8,10},{9,11},{10,... | collective-permute-start | bytes 221192 | tf_op jit(solution)/shard_map/ppermute | solution.py:196
  24.6 42.0 %collective-permute-start.14 = (bf16[384,768]{1,0:T(8,128)(2,1)}, bf16[384,768]{1,0:T(8,128)(2,1)S(1)}, u32[]{:S(2)}, u32[]{:S(2)}) collective-permute-start(bf16[384,768]{1,0:T(8,128)(2,1)} %constant_dynamic-update-slice_fusion), channel_id=1, source_target_pairs={{0,1},{1,0},{2,3},{3,2},{4,5},{5,4},{6,7},{7,6},{8,9},{9,8},{10,11... | collective-permute-start | bytes 1769480 | tf_op jit(solution)/shard_map/ppermute | solution.py:196
  24.7 15.9 %collective-permute-start.1 = (bf16[128,768]{1,0:T(8,128)(2,1)}, bf16[128,768]{1,0:T(8,128)(2,1)S(1)}, u32[]{:S(2)}, u32[]{:S(2)}) collective-permute-start(bf16[128,768]{1,0:T(8,128)(2,1)} %refs_2_.1), channel_id=1, source_target_pairs={{0,8},{1,9},{2,10},{3,11},{4,12},{5,13},{6,14},{7,15},{8,0},{9,1},... | collective-permute-start | bytes 589832 | tf_op jit(solution)/shard_map/ppermute | solution.py:199
  24.8 16.3 %collective-permute-start = (bf16[128,768]{1,0:T(8,128)(2,1)}, bf16[128,768]{1,0:T(8,128)(2,1)S(1)}, u32[]{:S(2)}, u32[]{:S(2)}) collective-permute-start(bf16[128,768]{1,0:T(8,128)(2,1)} %refs_2_.1), channel_id=1, source_target_pairs={{0,4},{1,5},{2,6},{3,7},{4,8},{5,9},{6,10},{7,11},{8,12},{9,13},{1... | collective-permute-start | bytes 589832 | tf_op jit(solution)/shard_map/ppermute | solution.py:199
  26.9 15.7 %collective-permute-start.3 = (bf16[128,768]{1,0:T(8,128)(2,1)}, bf16[128,768]{1,0:T(8,128)(2,1)}, u32[]{:S(2)}, u32[]{:S(2)}) collective-permute-start(bf16[128,768]{1,0:T(8,128)(2,1)} %refs_2_.1), channel_id=1, source_target_pairs={{0,2},{1,3},{2,0},{3,1},{4,6},{5,7},{6,4},{7,5},{8,10},{9,11},{10,... | collective-permute-start | bytes 589832 | tf_op jit(solution)/shard_map/ppermute | solution.py:196
  40.6 26.0 %collective-permute-start.6 = (bf16[128,768]{1,0:T(8,128)(2,1)S(1)}, bf16[128,768]{1,0:T(8,128)(2,1)S(1)}, u32[]{:S(2)}, u32[]{:S(2)}) collective-permute-start(bf16[128,768]{1,0:T(8,128)(2,1)S(1)} %collective-permute-done.2.refs_5_), channel_id=1, source_target_pairs={{0,2},{1,3},{2,0},{3,1},{4,6},{5,7},{6,4},{7,5},{8,10},{9,11},{10,... | collective-permute-start | bytes 589832 | tf_op jit(solution)/shard_map/ppermute | solution.py:196
  41.1 25.5 %collective-permute-start.5 = (bf16[128,768]{1,0:T(8,128)(2,1)S(1)}, bf16[128,768]{1,0:T(8,128)(2,1)S(1)}, u32[]{:S(2)}, u32[]{:S(2)}) collective-permute-start(bf16[128,768]{1,0:T(8,128)(2,1)S(1)} %collective-permute-done.1.refs_4_), channel_id=1, source_target_pairs={{0,2},{1,3},{2,0},{3,1},{4,6},{5,7},{6,4},{7,5},{8,10},{9,11},{10,... | collective-permute-start | bytes 589832 | tf_op jit(solution)/shard_map/ppermute | solution.py:196
  42.6 24.0 %collective-permute-start.4 = (bf16[128,768]{1,0:T(8,128)(2,1)S(1)}, bf16[128,768]{1,0:T(8,128)(2,1)S(1)}, u32[]{:S(2)}, u32[]{:S(2)}) collective-permute-start(bf16[128,768]{1,0:T(8,128)(2,1)S(1)} %collective-permute-done.refs_3_), channel_id=1, source_target_pairs={{0,2},{1,3},{2,0},{3,1},{4,6},{5,7},{6,4},{7,5},{8,10},{9,11},{10,... | collective-permute-start | bytes 589832 | tf_op jit(solution)/shard_map/ppermute | solution.py:196
  66.7 1.4 %copy-start.1 = (bf16[1,768,960]{1,2,0:T(8,128)(2,1)S(1)}, bf16[1,768,960]{1,2,0:T(8,128)(2,1)}, u32[]{:S(2)}) copy-start(bf16[1,768,960]{1,2,0:T(8,128)(2,1)} %param.17) | copy-start | bytes 4423684
  77.3 12.5 %all-to-all-start = ((bf16[16,48,128]{2,1,0:T(8,128)(2,1)}), bf16[16,48,128]{2,1,0:T(8,128)(2,1)S(1)}, u32[]{:S(2)}, u32[]{:S(2)}) async-start(bf16[16,48,128]{2,1,0:T(8,128)(2,1)} %shard_map.122), calls=%async_computation | async-start | bytes 393216 | tf_op jit(solution)/shard_map/all_to_all | solution.py:257

commit v2 on v0

--- a/solution.py
+++ b/solution.py
@@ -1,10 +1,13 @@
 import jax
 import jax.numpy as jnp
 from jax import lax
+from jax.experimental import pallas as pl
+from jax.experimental.pallas import tpu as pltpu
 from jax.sharding import PartitionSpec as P
 
 TILE = 128
 BLK_DEV = 2
+SLOT_ROWS = 16
 
 
 def layer_norm(activated, norm_gain, norm_bias):
@@ -23,7 +26,7 @@
     return jnp.max(jnp.where(keep[:, :, None], saturated, 0.0), axis=1)
 
 
-def local(
+def move_weights(
     hidden_states,
     doc_lengths,
     transform_weight,
@@ -93,6 +96,292 @@
     return (impacts, summary.reshape(BLK_DEV, tiles_t * TILE))
 
 
+def dot_t(left, right):
+    return lax.dot_general(
+        left, right, (((1,), (1,)), ((), ())), preferred_element_type=jnp.float32
+    )
+
+
+def ring_of(layers):
+    return [2 * z for z in range(layers)] + [2 * z + 1 for z in reversed(range(layers))]
+
+
+def chip_after(chip, by, layers):
+    layer, side = chip // 2, chip % 2
+    here = jnp.where(side == 0, layer, 2 * layers - 1 - layer)
+    there = (here + by + 2 * layers) % (2 * layers)
+    return jnp.where(there < layers, 2 * there, 2 * (2 * layers - 1 - there) + 1)
+
+
+def doc_of(me, step, own, layers):
+    core = me % 2
+    chip = chip_after(me // 2, jnp.where(core == 0, -step, step), layers)
+    return 2 * chip + (core if own else 1 - core)
+
+
+def masked(ref, length):
+    here = ref[...]
+    keep = lax.broadcasted_iota(jnp.int32, here.shape, 0) < length
+    first = jnp.broadcast_to(here[0:1, :].astype(jnp.float32), here.shape).astype(here.dtype)
+    return jnp.where(keep, here, first)
+
+
+def best_logits(pair, lengths, weight, tbias, gain, nbias, mine_ref, theirs_ref):
+    seq = pair[0].shape[0]
+    rows = jnp.concatenate([masked(ref, length) for ref, length in zip(pair, lengths)], axis=0)
+    pre = jnp.dot(rows, weight[...], preferred_element_type=jnp.float32) + tbias
+    act = 0.5 * pre * (1.0 + lax.erf(pre * (0.5**0.5)))
+    normed = layer_norm(act.astype(jnp.bfloat16), gain, nbias)
+    tops = []
+    for w_ref in (mine_ref, theirs_ref):
+        logits = dot_t(normed, w_ref[...])
+        tops.append(
+            [
+                jnp.max(logits[j * seq : (j + 1) * seq], axis=0, keepdims=True)
+                for j in range(len(pair))
+            ]
+        )
+    return tops
+
+
+def pack_kernel(*refs):
+    rows = refs[0].shape[0]
+    for k, ref in enumerate(refs[:-1]):
+        refs[-1][k * rows : (k + 1) * rows, :] = ref[...]
+
+
+def docs_kernel(places, layers, blocks, *refs):
+    (me_ref, meta_ref), refs = refs[:2], refs[2:]
+    docs, refs = refs[: len(places)], refs[len(places) :]
+    me = me_ref[0]
+    core = me % 2
+    if blocks:
+        mine_blocks, other_blocks, refs = refs[0], refs[1], refs[2:]
+        tbias_ref, gain_ref, nbias_ref, mine_ref, theirs_ref, best_mine, best_theirs, weight = refs
+        rows = weight.shape[0] // (2 * len(blocks))
+        for k, by in enumerate(blocks):
+            chip = chip_after(me // 2, by, layers)
+            at = pl.multiple_of((2 * chip + core) * rows, 16)
+            weight[pl.ds(at, rows), :] = mine_blocks[k * rows : (k + 1) * rows, :]
+            at = pl.multiple_of((2 * chip + 1 - core) * rows, 16)
+            weight[pl.ds(at, rows), :] = other_blocks[k * rows : (k + 1) * rows, :]
+    else:
+        weight, refs = refs[0], refs[1:]
+        tbias_ref, gain_ref, nbias_ref, mine_ref, theirs_ref, best_mine, best_theirs = refs
+    lengths = [meta_ref[doc_of(me, s, o, layers) ^ me, TILE - 1] for s, o in places]
+    for first in range(0, len(places), 2):
+        part = slice(first, first + 2)
+        mine, theirs = best_logits(
+            docs[part],
+            lengths[part],
+            weight,
+            tbias_ref[...],
+            gain_ref[...],
+            nbias_ref[...],
+            mine_ref,
+            theirs_ref,
+        )
+        for j in range(len(mine)):
+            best_mine[first + j : first + j + 1, :] = mine[j]
+            best_theirs[first + j : first + j + 1, :] = theirs[j]
+
+
+def last_kernel(places, before, layers, *refs):
+    (me_ref, meta_ref), refs = refs[:2], refs[2:]
+    docs, refs = refs[: len(places)], refs[len(places) :]
+    weight, tbias_ref, gain_ref, nbias_ref, mine_ref, theirs_ref, dbias_ref = refs[:7]
+    refs = refs[7:]
+    earlier, refs = refs[: 2 * len(before)], refs[2 * len(before) :]
+    out_ref, best, send = refs
+    me = me_ref[0]
+    core, chip = me % 2, me // 2
+    devices = 4 * layers
+    half = mine_ref.shape[0]
+    tiles = 2 * half // TILE
+    best[...] = jnp.zeros(best.shape, jnp.float32)
+    handled = []
+
+    def keep(place, mine, theirs):
+        low = jnp.where(core == 0, mine, theirs)
+        high = jnp.where(core == 0, theirs, mine)
+        logits = jnp.concatenate([low, high], axis=1) + dbias_ref[...]
+        impacts = jnp.log1p(jnp.maximum(logits, 0.0)).astype(jnp.bfloat16).astype(jnp.float32)
+        for k, (s, o) in enumerate(place):
+            doc = doc_of(me, s, o, layers)
+            best[pl.ds(doc, 1), :] = impacts[k : k + 1, :]
+            handled.append((doc, impacts[k : k + 1, :]))
+
+    for n, place in enumerate(before):
+        count = len(place)
+        keep(place, earlier[2 * n][0:count, :], earlier[2 * n + 1][0:count, :])
+    lengths = [meta_ref[doc_of(me, s, o, layers) ^ me, TILE - 1] for s, o in places]
+    mine, theirs = best_logits(
+        docs,
+        lengths,
+        weight,
+        tbias_ref[...],
+        gain_ref[...],
+        nbias_ref[...],
+        mine_ref,
+        theirs_ref,
+    )
+    keep(places, jnp.concatenate(mine, axis=0), jnp.concatenate(theirs, axis=0))
+    send[...] = jnp.zeros(send.shape, jnp.float32)
+    stride = out_ref.shape[1]
+    target = lax.broadcasted_iota(jnp.int32, (BLK_DEV * devices, TILE), 0)
+    for t in range(tiles):
+        lanes = slice(t * TILE, (t + 1) * TILE)
+        send[pl.ds(t, devices, stride=stride), :] = best[:, lanes]
+        blocks = jnp.zeros((BLK_DEV * devices, TILE), jnp.float32)
+        for doc, impacts in handled:
+            block = meta_ref[doc ^ me, chip * tiles + t]
+            blocks = jnp.maximum(blocks, jnp.where(target == block, impacts[:, lanes], 0.0))
+        for s in range(BLK_DEV):
+            send[pl.ds((1 + s) * SLOT_ROWS + t, devices, stride=stride), :] = blocks[
+                s * devices : (s + 1) * devices
+            ]
+    out_ref[...] = send[...].astype(jnp.bfloat16).reshape(out_ref.shape)
+
+
+def move_tokens(
+    hidden_states,
+    doc_lengths,
+    transform_weight,
+    transform_bias,
+    norm_gain,
+    norm_bias,
+    decoder_weight,
+    decoder_bias,
+    tile_ids,
+    owner_ids,
+    block_slots,
+):
+    devices = lax.axis_size("doc")
+    chips = devices // 2
+    layers = chips // 2
+    seq, width = hidden_states.shape
+    half = decoder_weight.shape[2]
+    tiles = 2 * half // TILE
+    me = lax.axis_index("doc").astype(jnp.int32)
+    ring = ring_of(layers)
+
+    def flip(value, bit):
+        return lax.ppermute(value, "doc", [(i, i ^ bit) for i in range(devices)])
+
+    def onward(value, ways):
+        moves = []
+        for n, chip in enumerate(ring):
+            for core, way in enumerate(ways):
+                moves.append((2 * chip + core, 2 * ring[(n + way) % chips] + core))
+        return lax.ppermute(value, "doc", moves)
+
+    smem = pl.BlockSpec(memory_space=pltpu.SMEM)
+    vmem = pl.BlockSpec(memory_space=pltpu.VMEM)
+    limit = pltpu.CompilerParams(vmem_limit_bytes=24 * 1024 * 1024)
+
+    wanted = block_slots[0, 0] * devices + owner_ids[0, 0, :, 0]
+    lane = jnp.arange(TILE, dtype=jnp.int32)
+    posted = tile_ids[0, 0][:, None] == lane[None, :]
+    table = jnp.sum(jnp.where(posted, wanted[:, None] + 1, 0), axis=0) - 1
+    meta = jnp.where(lane == TILE - 1, doc_lengths[0], table)[None, :]
+    bit = 1
+    while bit < devices:
+        meta = jnp.concatenate([meta, flip(meta, bit)], axis=0)
+        bit *= 2
+
+    blocks, onto = [0], [transform_weight]
+    for way, steps in ((1, chips // 2), (-1, (chips - 1) // 2)):
+        moving = transform_weight
+        for step in range(1, steps + 1):
+            moving = onward(moving, (way, way))
+            blocks.append(-way * step)
+            onto.append(moving)
+    mine_blocks = pl.pallas_call(
+        pack_kernel,
+        out_shape=jax.ShapeDtypeStruct((chips * transform_weight.shape[0], width), jnp.bfloat16),
+        in_specs=[vmem] * chips,
+        out_specs=vmem,
+        compiler_params=limit,
+    )(*onto)
+    other_blocks = flip(mine_blocks, 1)
+
+    weight_rows = jnp.swapaxes(decoder_weight[0], 0, 1)
+    other_half = flip(weight_rows, 1)
+
+    own, partner = hidden_states, flip(hidden_states, 1)
+    arrived = {(0, True): hidden_states}
+    for step in range(1, chips // 2 + 1):
+        own = onward(own, (1, -1))
+        arrived[(step, True)] = own
+        if step < chips // 2:
+            partner = onward(partner, (1, -1))
+            arrived[(step, False)] = partner
+    places = list(arrived)
+    groups = [places[: len(places) // 2], places[len(places) // 2 : -2], places[-2:]]
+    groups = [group for group in groups if group]
+
+    where = me[None]
+    params = (transform_bias[None, :], norm_gain[None, :], norm_bias[None, :])
+    halves = (weight_rows, other_half)
+    best_shape = jax.ShapeDtypeStruct((8, half), jnp.float32)
+    weight = None
+    results = []
+    for group in groups[:-1]:
+        first = weight is None
+        outs = [best_shape] * 2
+        if first:
+            outs.append(jax.ShapeDtypeStruct((width, width), jnp.bfloat16))
+        dense = (mine_blocks, other_blocks) if first else (weight,)
+        args = [arrived[place] for place in group] + [*dense, *params, *halves]
+        found = pl.pallas_call(
+            lambda *refs, group=group, first=first: docs_kernel(
+                group, layers, blocks if first else None, *refs
+            ),
+            out_shape=outs,
+            in_specs=[smem, smem] + [vmem] * len(args),
+            out_specs=[vmem] * len(outs),
+            compiler_params=limit,
+            cost_estimate=pl.CostEstimate(
+                flops=2 * len(group) * seq * width * (width + 2 * half),
+                bytes_accessed=1024 * 1024,
+                transcendentals=len(group) * seq * width,
+            ),
+        )(where, meta, *args)
+        results.extend(found[:2])
+        if first:
+            weight = found[2]
+
+    bias = lax.dynamic_slice_in_dim(decoder_bias, (me // 2) * 2 * half, 2 * half, 0)[None, :]
+    args = [arrived[place] for place in groups[-1]] + [weight, *params, *halves, bias, *results]
+    send = pl.pallas_call(
+        lambda *refs: last_kernel(groups[-1], groups[:-1], layers, *refs),
+        out_shape=jax.ShapeDtypeStruct(
+            (devices, (1 + BLK_DEV) * SLOT_ROWS, TILE), jnp.bfloat16
+        ),
+        in_specs=[smem, smem] + [vmem] * len(args),
+        out_specs=vmem,
+        scratch_shapes=[
+            pltpu.VMEM((devices, 2 * half), jnp.float32),
+            pltpu.VMEM((devices * (1 + BLK_DEV) * SLOT_ROWS, TILE), jnp.float32),
+        ],
+        compiler_params=limit,
+        cost_estimate=pl.CostEstimate(
+            flops=2 * len(groups[-1]) * seq * width * (width + 2 * half),
+            bytes_accessed=1024 * 1024,
+            transcendentals=len(groups[-1]) * seq * width,
+        ),
+    )(where, meta, *args)
+    got = lax.all_to_all(send, "doc", split_axis=0, concat_axis=0, tiled=True)
+    got = got.reshape(chips, 2, 1 + BLK_DEV, SLOT_ROWS, TILE)[:, :, :, :tiles]
+    whole = jnp.swapaxes(jnp.maximum(got[:, 0], got[:, 1]), 0, 1).reshape(1 + BLK_DEV, -1)
+    return (whole[:1], whole[1:])
+
+
+def tokens_move(mesh):
+    devices = mesh.shape["doc"]
+    return mesh.shape["term"] == 1 and devices >= 8 and devices & (devices - 1) == 0
+
+
 def solution(mesh):
     placed = (
         P(("groups", "doc"), None),
@@ -107,6 +396,15 @@
         P("term", ("groups", "doc"), None, None),
         P("term", ("groups", "doc"), None),
     )
+
+    def local(*args):
+        pair = 2 * args[6].shape[2]
+        tiles = pair * (mesh.shape["doc"] // 2) // TILE
+        fits = pair % TILE == 0 and tiles < TILE and pair // TILE <= SLOT_ROWS
+        if tokens_move(mesh) and args[1].shape[0] == 1 and fits:
+            return move_tokens(*args)
+        return move_weights(*args)
+
     return jax.shard_map(
         local,
         mesh=mesh,

time: 207 us -> 70.5 us (0.34)
  waiting for transfers between devices: 155 us -> 12.6 us
  matrix products: 15.2 us -> 0 us
  between operations: 14.8 us -> 1.42 us
  blocking collectives: 0 us -> 12.9 us
  starting transfers between devices: 12.1 us -> 24.7 us
  Pallas kernels: 0 us -> 9.63 us
  other arithmetic: 5.45 us -> 1.46 us
  local copies, waits for them, and re-layouts: 4.62 us -> 7.39 us
    all_gather x2 -> x0, waiting for transfers between devices: 142 us -> none  [the longest x1 119 us: local(): lax.all_gather(decoder_weight, 'doc', axis=2, tiled=True)[0]]
    ppermute x0 -> x21, starting transfers between devices: none -> 24.7 us  [the longest x14 19.1 us: onward(): return lax.ppermute(value, 'doc', moves)]
    dot_general x2 -> x0, matrix products: 15.2 us -> none  [the longest x1 12.8 us: local(): jnp.dot(normed, lax.all_gather(decoder_weight, 'doc', axis=2, tiled=True)...]
    all_to_all x0 -> x1, blocking collectives: none -> 12.9 us  [move_tokens(): got = lax.all_to_all(send, 'doc', split_axis=0, concat_axis=0, tiled=True)]
    ppermute x0 -> x21, waiting for transfers between devices: none -> 12.6 us  [the longest x14 9.48 us: onward(): return lax.ppermute(value, 'doc', moves)]
    all_to_all x2 -> x0, starting transfers between devices: 12 us -> none  [the longest x1 7.36 us: local(): lax.all_to_all(out_tags.reshape(owner_count, capacity), 'doc', split_axis...]
    all_to_all x2 -> x0, waiting for transfers between devices: 10.8 us -> none  [the longest x1 5.83 us: local(): lax.all_to_all(outgoing.reshape(owner_count, capacity, TILE), 'doc', spli...]
    pallas_call x0 -> x4, Pallas kernels: none -> 9.63 us  [the longest x2 6.86 us: move_tokens(): pl.pallas_call(lambda *refs, group=group, first=first: docs_kernel(group,...]
  transfers between devices with their start and end apart: 4 -> 21, of which waited for: 4 -> 9; matrix products, arithmetic and copies ran while one was open for 4% -> 6% of each run, Pallas kernels for 0% -> 10%
where the time goes in v2:
time: 70.5 us; the launch traced here: 70.1 us
  starting transfers between devices  24.7 us (35%)
  blocking collectives  12.9 us (18%)
  waiting for transfers between devices  12.6 us (18%)
  Pallas kernels  9.63 us (14%)
  local copies, waits for them, and re-layouts  7.39 us (10%)
  other arithmetic  1.46 us (2%)
  between operations  1.42 us (2%)
    ppermute x14, starting transfers between devices, onward(): return lax.ppermute(value, 'doc', moves)  19.1 us
    all_to_all x1, blocking collectives, move_tokens(): got = lax.all_to_all(send, 'doc', split_axis=0, concat_axis=0, tiled=True)  12.9 us
    ppermute x14, waiting for transfers between devices, onward(): return lax.ppermute(value, 'doc', moves)  9.48 us
    pallas_call x2, Pallas kernels, move_tokens(): pl.pallas_call(lambda *refs, group=group, first=first: docs_kernel(group,...  6.86 us
    ppermute x7, starting transfers between devices, flip(): return lax.ppermute(value, 'doc', [(i, i ^ bit) for i in range(devices)])  5.6 us
    unnamed x8, local copies, waits for them, and re-layouts  3.19 us
    ppermute x7, waiting for transfers between devices, flip(): return lax.ppermute(value, 'doc', [(i, i ^ bit) for i in range(devices)])  3.14 us
    pallas_call x1, Pallas kernels, move_tokens(): pl.pallas_call(lambda *refs: last_kernel(groups[-1], groups[:-1], layers,...  2.73 us
  transfers between devices with their start and end apart: 21, of which 9 were waited for; matrix products, arithmetic and copies ran while one was open for 6% of the time, Pallas kernels for 10%

profile of v2, /device:TPU:0, one launch (start us, length us, event | category | flops | bytes accessed | tf_op | source)
XLA Modules:
  0.0 70.1 jit_solution(9024599090867264866)
XLA Ops:
  0.6 0.5 collective-permute-start.20
  1.1 2.6 %collective-permute-start.12 = (bf16[48,768]{1,0:T(8,128)(2,1)}, bf16[48,768]{1,0:T(8,128)(2,1)S(1)}, u32[]{:S(2)}, u32[]{:S(2)}) collective-permute-start(bf16[48,768]{1,0:T(8,128)(2,1)} %refs_0_.1), channel_id=1, source_target_pairs={{0,4},{1,5},{4,8},{5,9},{8,12},{9,13},{12,14},{13,15},{14,10},{15,... | collective-permute-start | bytes 221192 | tf_op jit(solution)/shard_map/ppermute | solution.py:276
  3.8 3.0 %collective-permute-done.12.refs_1_ = bf16[48,768]{1,0:T(8,128)(2,1)S(1)} collective-permute-done((bf16[48,768]{1,0:T(8,128)(2,1)}, bf16[48,768]{1,0:T(8,128)(2,1)S(1)}, u32[]{:S(2)}, u32[]{:S(2)}) %collective-permute-start.12) | collective-permute-done | bytes 73760 | tf_op jit(solution)/shard_map/ppermute | solution.py:276
  6.8 1.8 %collective-permute-start.13 = (bf16[48,768]{1,0:T(8,128)(2,1)S(1)}, bf16[48,768]{1,0:T(8,128)(2,1)S(1)}, u32[]{:S(2)}, u32[]{:S(2)}) collective-permute-start(bf16[48,768]{1,0:T(8,128)(2,1)S(1)} %collective-permute-done.12.refs_1_), channel_id=1, source_target_pairs={{0,4},{1,5},{4,8},{5,9},{8,12},{9,13},{12,14},{13,15},{14,10},{15,... | collective-permute-start | bytes 221192 | tf_op jit(solution)/shard_map/ppermute | solution.py:276
  8.6 0.2 collective-permute-start.17
  8.8 2.3 %collective-permute-done.13.refs_2_ = bf16[48,768]{1,0:T(8,128)(2,1)S(1)} collective-permute-done((bf16[48,768]{1,0:T(8,128)(2,1)S(1)}, bf16[48,768]{1,0:T(8,128)(2,1)S(1)}, u32[]{:S(2)}, u32[]{:S(2)}) %collective-permute-start.13) | collective-permute-done | bytes 73760 | tf_op jit(solution)/shard_map/ppermute | solution.py:276
  11.1 1.8 %collective-permute-start.14 = (bf16[48,768]{1,0:T(8,128)(2,1)S(1)}, bf16[48,768]{1,0:T(8,128)(2,1)S(1)}, u32[]{:S(2)}, u32[]{:S(2)}) collective-permute-start(bf16[48,768]{1,0:T(8,128)(2,1)S(1)} %collective-permute-done.13.refs_2_), channel_id=1, source_target_pairs={{0,4},{1,5},{4,8},{5,9},{8,12},{9,13},{12,14},{13,15},{14,10},{15,... | collective-permute-start | bytes 221192 | tf_op jit(solution)/shard_map/ppermute | solution.py:276
  13.0 1.6 %collective-permute-start.8 = (bf16[128,768]{1,0:T(8,128)(2,1)}, bf16[128,768]{1,0:T(8,128)(2,1)S(1)}, u32[]{:S(2)}, u32[]{:S(2)}) collective-permute-start(bf16[128,768]{1,0:T(8,128)(2,1)} %refs_2_.1), channel_id=1, source_target_pairs={{0,4},{1,3},{4,8},{5,1},{8,12},{9,5},{12,14},{13,9},{14,10},{15,13... | collective-permute-start | bytes 589832 | tf_op jit(solution)/shard_map/ppermute | solution.py:276
  14.5 0.0 collective-permute-start.4
  14.6 0.5 collective-permute-start.18
  15.0 0.5 collective-permute-done.14.refs_3_
  15.5 1.8 %collective-permute-start.15 = (bf16[48,768]{1,0:T(8,128)(2,1)S(1)}, bf16[48,768]{1,0:T(8,128)(2,1)S(1)}, u32[]{:S(2)}, u32[]{:S(2)}) collective-permute-start(bf16[48,768]{1,0:T(8,128)(2,1)S(1)} %collective-permute-done.14.refs_3_), channel_id=1, source_target_pairs={{0,4},{1,5},{4,8},{5,9},{8,12},{9,13},{12,14},{13,15},{14,10},{15,... | collective-permute-start | bytes 221192 | tf_op jit(solution)/shard_map/ppermute | solution.py:276
  17.3 0.7 fusion.1
  18.0 1.2 %collective-permute-done.18.refs_7_ = bf16[48,768]{1,0:T(8,128)(2,1)S(1)} collective-permute-done((bf16[48,768]{1,0:T(8,128)(2,1)S(1)}, bf16[48,768]{1,0:T(8,128)(2,1)S(1)}, u32[]{:S(2)}, u32[]{:S(2)}) %collective-permute-start.18) | collective-permute-done | bytes 73760 | tf_op jit(solution)/shard_map/ppermute | solution.py:276
  19.2 1.2 %collective-permute-done.15.refs_4_ = bf16[48,768]{1,0:T(8,128)(2,1)S(1)} collective-permute-done((bf16[48,768]{1,0:T(8,128)(2,1)S(1)}, bf16[48,768]{1,0:T(8,128)(2,1)S(1)}, u32[]{:S(2)}, u32[]{:S(2)}) %collective-permute-start.15) | collective-permute-done | bytes 73760 | tf_op jit(solution)/shard_map/ppermute | solution.py:276
  20.4 0.9 %copy-done.2 = bf16[48,768]{1,0:T(8,128)(2,1)S(1)} copy-done((bf16[48,768]{1,0:T(8,128)(2,1)S(1)}, bf16[48,768]{1,0:T(8,128)(2,1)}, u32[]{:S(2)}) %copy-start.2) | copy-done | bytes 73752
  21.4 0.1 collective-permute-start.19
  21.4 0.7 %select_reduce_fusion = s32[128]{0:T(128)S(1)} fusion(s32[32]{0:T(128)S(1)} %fusion.1, s32[32]{0:T(128)} %bitcast.25), kind=kLoop, calls=%fused_computation.2 | loop fusion | flops 12160 | bytes 768 | tf_op jit(solution)/shard_map/reduce_sum | solution.py:285
  22.8 0.0 collective-permute-done.8.refs_3_
  22.8 1.6 %collective-permute-start.9 = (bf16[128,768]{1,0:T(8,128)(2,1)S(1)}, bf16[128,768]{1,0:T(8,128)(2,1)S(1)}, u32[]{:S(2)}, u32[]{:S(2)}) collective-permute-start(bf16[128,768]{1,0:T(8,128)(2,1)S(1)} %collective-permute-done.8.refs_3_), channel_id=1, source_target_pairs={{0,4},{1,3},{4,8},{5,1},{8,12},{9,5},{12,14},{13,9},{14,10},{15,13... | collective-permute-start | bytes 589832 | tf_op jit(solution)/shard_map/ppermute | solution.py:276
  24.5 1.6 %collective-permute-start.5 = (bf16[128,768]{1,0:T(8,128)(2,1)S(1)}, bf16[128,768]{1,0:T(8,128)(2,1)}, u32[]{:S(2)}, u32[]{:S(2)}) collective-permute-start(bf16[128,768]{1,0:T(8,128)(2,1)S(1)} %collective-permute-done.4), channel_id=1, source_target_pairs={{0,4},{1,3},{4,8},{5,1},{8,12},{9,5},{12,14},{13,9},{14,10},{15,13... | collective-permute-start | bytes 589832 | tf_op jit(solution)/shard_map/ppermute | solution.py:276
  26.1 0.0 collective-permute-start
  26.1 1.1 %collective-permute-done = s32[1,128]{1,0:T(1,128)S(1)} collective-permute-done((s32[1,128]{1,0:T(1,128)S(1)}, s32[1,128]{1,0:T(1,128)S(1)}, u32[]{:S(2)}, u32[]{:S(2)}) %collective-permute-start) | collective-permute-done | bytes 544 | tf_op jit(solution)/shard_map/ppermute | solution.py:269
  27.2 0.8 %collective-permute-start.1 = (s32[2,128]{1,0:T(2,128)S(1)}, s32[2,128]{1,0:T(2,128)S(1)}, u32[]{:S(2)}, u32[]{:S(2)}) collective-permute-start(s32[2,128]{1,0:T(2,128)S(1)} %pad_add_fusion.2), channel_id=1, source_target_pairs={{0,2},{1,3},{2,0},{3,1},{4,6},{5,7},{6,4},{7,5},{8,10},{9,11},{10,... | collective-permute-start | bytes 3080 | tf_op jit(solution)/shard_map/ppermute | solution.py:269
  28.0 0.6 collective-permute-done.9.refs_5_
  28.6 1.6 %collective-permute-start.10 = (bf16[128,768]{1,0:T(8,128)(2,1)S(1)}, bf16[128,768]{1,0:T(8,128)(2,1)S(1)}, u32[]{:S(2)}, u32[]{:S(2)}) collective-permute-start(bf16[128,768]{1,0:T(8,128)(2,1)S(1)} %collective-permute-done.9.refs_5_), channel_id=1, source_target_pairs={{0,4},{1,3},{4,8},{5,1},{8,12},{9,5},{12,14},{13,9},{14,10},{15,13... | collective-permute-start | bytes 589832 | tf_op jit(solution)/shard_map/ppermute | solution.py:276
  30.1 0.6 collective-permute-done.5.refs_4_
  30.8 1.6 %collective-permute-start.6 = (bf16[128,768]{1,0:T(8,128)(2,1)}, bf16[128,768]{1,0:T(8,128)(2,1)S(1)}, u32[]{:S(2)}, u32[]{:S(2)}) collective-permute-start(bf16[128,768]{1,0:T(8,128)(2,1)} %collective-permute-done.5.refs_4_), channel_id=1, source_target_pairs={{0,4},{1,3},{4,8},{5,1},{8,12},{9,5},{12,14},{13,9},{14,10},{15,13... | collective-permute-start | bytes 589832 | tf_op jit(solution)/shard_map/ppermute | solution.py:276
  32.4 0.0 collective-permute-done.1
  32.4 1.6 %collective-permute-start.2 = (s32[4,128]{1,0:T(4,128)S(1)}, s32[4,128]{1,0:T(4,128)S(1)}, u32[]{:S(2)}, u32[]{:S(2)}) collective-permute-start(s32[4,128]{1,0:T(4,128)S(1)} %pad_add_fusion.1), channel_id=1, source_target_pairs={{0,4},{1,5},{2,6},{3,7},{4,0},{5,1},{6,2},{7,3},{8,12},{9,13},{10,... | collective-permute-start | bytes 6152 | tf_op jit(solution)/shard_map/ppermute | solution.py:269
  34.0 2.0 %collective-permute-done.2 = s32[4,128]{1,0:T(4,128)S(1)} collective-permute-done((s32[4,128]{1,0:T(4,128)S(1)}, s32[4,128]{1,0:T(4,128)S(1)}, u32[]{:S(2)}, u32[]{:S(2)}) %collective-permute-start.2) | collective-permute-done | bytes 2080 | tf_op jit(solution)/shard_map/ppermute | solution.py:269
  36.0 2.6 %collective-permute-start.3 = (s32[8,128]{1,0:T(8,128)S(1)}, s32[8,128]{1,0:T(8,128)S(1)}, u32[]{:S(2)}, u32[]{:S(2)}) collective-permute-start(s32[8,128]{1,0:T(8,128)S(1)} %pad_add_fusion), channel_id=1, source_target_pairs={{0,8},{1,9},{2,10},{3,11},{4,12},{5,13},{6,14},{7,15},{8,0},{9,1},... | collective-permute-start | bytes 12296 | tf_op jit(solution)/shard_map/ppermute | solution.py:269
  38.6 0.7 broadcast_in_dim.38.refs_8_.refs_5_
  39.3 0.7 broadcast_in_dim.39.refs_9_.refs_6_
  40.0 0.7 broadcast_in_dim.40.refs_10_.refs_7_
  40.7 0.8 %dynamic_slice.3 = f32[1920]{0:T(1024)S(1)} dynamic-slice(f32[15360]{0:T(1024)} %param.18, s32[]{:T(128)S(6)} %select_n.26), dynamic_slice_sizes={1920} | dynamic-slice | bytes 15364 | tf_op jit(solution)/shard_map/dynamic_slice | solution.py:354
  41.5 0.0 collective-permute-done.3
  41.5 0.0 collective-permute-done.10.refs_3_
  41.5 2.3 %collective-permute-start.11 = (bf16[128,768]{1,0:T(8,128)(2,1)S(1)}, bf16[128,768]{1,0:T(8,128)(2,1)S(1)}, u32[]{:S(2)}, u32[]{:S(2)}) collective-permute-start(bf16[128,768]{1,0:T(8,128)(2,1)S(1)} %collective-permute-done.10.refs_3_), channel_id=1, source_target_pairs={{0,4},{1,3},{4,8},{5,1},{8,12},{9,5},{12,14},{13,9},{14,10},{15,13... | collective-permute-start | bytes 589832 | tf_op jit(solution)/shard_map/ppermute | solution.py:276
  43.8 0.1 collective-permute-start.7
  43.9 1.4 %copy-done = bf16[1,768,960]{1,2,0:T(8,128)(2,1)S(1)} copy-done((bf16[1,768,960]{1,2,0:T(8,128)(2,1)S(1)}, bf16[1,768,960]{1,2,0:T(8,128)(2,1)}, u32[]{:S(2)}) %copy-start) | copy-done | bytes 1474584
  45.2 0.9 %copy-done.3 = bf16[128,768]{1,0:T(8,128)(2,1)S(1)} copy-done((bf16[128,768]{1,0:T(8,128)(2,1)S(1)}, bf16[128,768]{1,0:T(8,128)(2,1)}, u32[]{:S(2)}) %copy-start.3) | copy-done | bytes 196632
  46.2 4.5 %shard_map.123 = (f32[8,960]{1,0:T(8,128)S(1)}, f32[8,960]{1,0:T(8,128)S(1)}, bf16[768,768]{1,0:T(8,128)(2,1)S(1)}) custom-call(s32[1]{0:T(128)} %bitcast.refs_0_, s32[16,128]{1,0:T(8,128)S(1)} %concatenate.18.refs_1_, bf16[128,768]{1,0:T(8,128)(2,1)S(1)} %copy-done.3, bf16[128,768]{1,0:T(8,128)(2,1)S(1)} %collective-permute-done.8.refs_3_, ...), custom_call_target="tpu_custom_call" | custom-call | flops 2113929216 | bytes 1048576 | tf_op jit(solution)/shard_map/pallas_call | solution.py:336
  50.7 2.4 %shard_map.124 = (f32[8,960]{1,0:T(8,128)S(1)}, f32[8,960]{1,0:T(8,128)S(1)}) custom-call(s32[1]{0:T(128)} %bitcast.refs_0_, s32[16,128]{1,0:T(8,128)S(1)} %concatenate.18.refs_1_, bf16[128,768]{1,0:T(8,128)(2,1)S(1)} %collective-permute-done.6.refs_2_, bf16[128,768]{1,0:T(8,128)(2,1)S(1)} %collective-permute-done.10.refs_3_, ...), custom_call_target="tpu_custom_call" | custom-call | flops 1056964608 | bytes 1048576 | tf_op jit(solution)/shard_map/pallas_call | solution.py:336
  53.1 2.7 %shard_map.125 = bf16[16,48,128]{2,1,0:T(8,128)(2,1)S(1)} custom-call(s32[1]{0:T(128)} %bitcast.refs_0_, s32[16,128]{1,0:T(8,128)S(1)} %concatenate.18.refs_1_, bf16[128,768]{1,0:T(8,128)(2,1)S(1)} %collective-permute-done.7.refs_2_, bf16[128,768]{1,0:T(8,128)(2,1)S(1)} %collective-permute-done.11.refs_3_, bf16[768,768]{1,0:T(8,128)(2,1)S(1)} %get-tuple-element.7.refs_4_, ...), custom_call_target="tpu_custom_call" | custom-call | flops 1056964608 | bytes 1048576 | tf_op jit(solution)/shard_map/pallas_call | solution.py:356
  55.8 12.9 %all_to_all.5 = bf16[16,48,128]{2,1,0:T(8,128)(2,1)S(1)} all-to-all(bf16[16,48,128]{2,1,0:T(8,128)(2,1)S(1)} %shard_map.125), channel_id=1, replica_groups=mesh['groups'=2,'doc'=16,'term'=1] {'doc'}, dimensions={0} | all-to-all | bytes 393216 | tf_op jit(solution)/shard_map/all_to_all | solution.py:374
  68.8 0.7 slice.26
  69.4 0.6 slice.24
  (25 shorter events, 0.2 us)
Async XLA Ops:
  0.6 43.2 %collective-permute-start.20 = (bf16[960,768]{1,0:T(8,128)(2,1)}, bf16[960,768]{1,0:T(8,128)(2,1)S(1)}, u32[]{:S(2)}, u32[]{:S(2)}) collective-permute-start(bf16[960,768]{1,0:T(8,128)(2,1)} %bitcast.20), channel_id=1, source_target_pairs={{0,1},{1,0},{2,3},{3,2},{4,5},{5,4},{6,7},{7,6},{8,9},{9,8},{10,11... | collective-permute-start | bytes 4423688 | tf_op jit(solution)/shard_map/ppermute | solution.py:269
  1.1 5.6 %collective-permute-start.12 = (bf16[48,768]{1,0:T(8,128)(2,1)}, bf16[48,768]{1,0:T(8,128)(2,1)S(1)}, u32[]{:S(2)}, u32[]{:S(2)}) collective-permute-start(bf16[48,768]{1,0:T(8,128)(2,1)} %refs_0_.1), channel_id=1, source_target_pairs={{0,4},{1,5},{4,8},{5,9},{8,12},{9,13},{12,14},{13,15},{14,10},{15,... | collective-permute-start | bytes 221192 | tf_op jit(solution)/shard_map/ppermute | solution.py:276
  3.8 4.8 %collective-permute-start.16 = (bf16[48,768]{1,0:T(8,128)(2,1)}, bf16[48,768]{1,0:T(8,128)(2,1)S(1)}, u32[]{:S(2)}, u32[]{:S(2)}) collective-permute-start(bf16[48,768]{1,0:T(8,128)(2,1)} %refs_0_.1), channel_id=1, source_target_pairs={{0,2},{1,3},{4,0},{5,1},{8,4},{9,5},{12,8},{13,9},{14,12},{15,13},... | collective-permute-start | bytes 221192 | tf_op jit(solution)/shard_map/ppermute | solution.py:276
  6.8 4.4 %collective-permute-start.13 = (bf16[48,768]{1,0:T(8,128)(2,1)S(1)}, bf16[48,768]{1,0:T(8,128)(2,1)S(1)}, u32[]{:S(2)}, u32[]{:S(2)}) collective-permute-start(bf16[48,768]{1,0:T(8,128)(2,1)S(1)} %collective-permute-done.12.refs_1_), channel_id=1, source_target_pairs={{0,4},{1,5},{4,8},{5,9},{8,12},{9,13},{12,14},{13,15},{14,10},{15,... | collective-permute-start | bytes 221192 | tf_op jit(solution)/shard_map/ppermute | solution.py:276
  8.6 5.9 %collective-permute-start.17 = (bf16[48,768]{1,0:T(8,128)(2,1)S(1)}, bf16[48,768]{1,0:T(8,128)(2,1)S(1)}, u32[]{:S(2)}, u32[]{:S(2)}) collective-permute-start(bf16[48,768]{1,0:T(8,128)(2,1)S(1)} %collective-permute-done.16.refs_5_), channel_id=1, source_target_pairs={{0,2},{1,3},{4,0},{5,1},{8,4},{9,5},{12,8},{13,9},{14,12},{15,13},... | collective-permute-start | bytes 221192 | tf_op jit(solution)/shard_map/ppermute | solution.py:276
  11.1 4.4 %collective-permute-start.14 = (bf16[48,768]{1,0:T(8,128)(2,1)S(1)}, bf16[48,768]{1,0:T(8,128)(2,1)S(1)}, u32[]{:S(2)}, u32[]{:S(2)}) collective-permute-start(bf16[48,768]{1,0:T(8,128)(2,1)S(1)} %collective-permute-done.13.refs_2_), channel_id=1, source_target_pairs={{0,4},{1,5},{4,8},{5,9},{8,12},{9,13},{12,14},{13,15},{14,10},{15,... | collective-permute-start | bytes 221192 | tf_op jit(solution)/shard_map/ppermute | solution.py:276
  13.0 9.9 %collective-permute-start.8 = (bf16[128,768]{1,0:T(8,128)(2,1)}, bf16[128,768]{1,0:T(8,128)(2,1)S(1)}, u32[]{:S(2)}, u32[]{:S(2)}) collective-permute-start(bf16[128,768]{1,0:T(8,128)(2,1)} %refs_2_.1), channel_id=1, source_target_pairs={{0,4},{1,3},{4,8},{5,1},{8,12},{9,5},{12,14},{13,9},{14,10},{15,13... | collective-permute-start | bytes 589832 | tf_op jit(solution)/shard_map/ppermute | solution.py:276
  14.5 9.9 %collective-permute-start.4 = (bf16[128,768]{1,0:T(8,128)(2,1)}, bf16[128,768]{1,0:T(8,128)(2,1)S(1)}, u32[]{:S(2)}, u32[]{:S(2)}) collective-permute-start(bf16[128,768]{1,0:T(8,128)(2,1)} %refs_2_.1), channel_id=1, source_target_pairs={{0,1},{1,0},{2,3},{3,2},{4,5},{5,4},{6,7},{7,6},{8,9},{9,8},{10,11... | collective-permute-start | bytes 589832 | tf_op jit(solution)/shard_map/ppermute | solution.py:269
  14.6 4.7 %collective-permute-start.18 = (bf16[48,768]{1,0:T(8,128)(2,1)S(1)}, bf16[48,768]{1,0:T(8,128)(2,1)S(1)}, u32[]{:S(2)}, u32[]{:S(2)}) collective-permute-start(bf16[48,768]{1,0:T(8,128)(2,1)S(1)} %collective-permute-done.17.refs_6_), channel_id=1, source_target_pairs={{0,2},{1,3},{4,0},{5,1},{8,4},{9,5},{12,8},{13,9},{14,12},{15,13},... | collective-permute-start | bytes 221192 | tf_op jit(solution)/shard_map/ppermute | solution.py:276
  15.5 4.9 %collective-permute-start.15 = (bf16[48,768]{1,0:T(8,128)(2,1)S(1)}, bf16[48,768]{1,0:T(8,128)(2,1)S(1)}, u32[]{:S(2)}, u32[]{:S(2)}) collective-permute-start(bf16[48,768]{1,0:T(8,128)(2,1)S(1)} %collective-permute-done.14.refs_3_), channel_id=1, source_target_pairs={{0,4},{1,5},{4,8},{5,9},{8,12},{9,13},{12,14},{13,15},{14,10},{15,... | collective-permute-start | bytes 221192 | tf_op jit(solution)/shard_map/ppermute | solution.py:276
  20.4 0.9 %copy-start.2 = (bf16[48,768]{1,0:T(8,128)(2,1)S(1)}, bf16[48,768]{1,0:T(8,128)(2,1)}, u32[]{:S(2)}) copy-start(bf16[48,768]{1,0:T(8,128)(2,1)} %refs_0_.1) | copy-start | bytes 221188
  21.4 22.5 %collective-permute-start.19 = (bf16[384,768]{1,0:T(8,128)(2,1)S(1)}, bf16[384,768]{1,0:T(8,128)(2,1)S(1)}, u32[]{:S(2)}, u32[]{:S(2)}) collective-permute-start(bf16[384,768]{1,0:T(8,128)(2,1)S(1)} %shard_map.122.refs_6_), channel_id=1, source_target_pairs={{0,1},{1,0},{2,3},{3,2},{4,5},{5,4},{6,7},{7,6},{8,9},{9,8},{10,11... | collective-permute-start | bytes 1769480 | tf_op jit(solution)/shard_map/ppermute | solution.py:269
  22.8 5.7 %collective-permute-start.9 = (bf16[128,768]{1,0:T(8,128)(2,1)S(1)}, bf16[128,768]{1,0:T(8,128)(2,1)S(1)}, u32[]{:S(2)}, u32[]{:S(2)}) collective-permute-start(bf16[128,768]{1,0:T(8,128)(2,1)S(1)} %collective-permute-done.8.refs_3_), channel_id=1, source_target_pairs={{0,4},{1,3},{4,8},{5,1},{8,12},{9,5},{12,14},{13,9},{14,10},{15,13... | collective-permute-start | bytes 589832 | tf_op jit(solution)/shard_map/ppermute | solution.py:276
  24.5 6.3 %collective-permute-start.5 = (bf16[128,768]{1,0:T(8,128)(2,1)S(1)}, bf16[128,768]{1,0:T(8,128)(2,1)}, u32[]{:S(2)}, u32[]{:S(2)}) collective-permute-start(bf16[128,768]{1,0:T(8,128)(2,1)S(1)} %collective-permute-done.4), channel_id=1, source_target_pairs={{0,4},{1,3},{4,8},{5,1},{8,12},{9,5},{12,14},{13,9},{14,10},{15,13... | collective-permute-start | bytes 589832 | tf_op jit(solution)/shard_map/ppermute | solution.py:276
  26.1 1.1 %collective-permute-start = (s32[1,128]{1,0:T(1,128)S(1)}, s32[1,128]{1,0:T(1,128)S(1)}, u32[]{:S(2)}, u32[]{:S(2)}) collective-permute-start(s32[1,128]{1,0:T(1,128)S(1)} %compare_select_fusion), channel_id=1, source_target_pairs={{0,1},{1,0},{2,3},{3,2},{4,5},{5,4},{6,7},{7,6},{8,9},{9,8},{10,11... | collective-permute-start | bytes 1544 | tf_op jit(solution)/shard_map/ppermute | solution.py:269
  27.2 5.2 %collective-permute-start.1 = (s32[2,128]{1,0:T(2,128)S(1)}, s32[2,128]{1,0:T(2,128)S(1)}, u32[]{:S(2)}, u32[]{:S(2)}) collective-permute-start(s32[2,128]{1,0:T(2,128)S(1)} %pad_add_fusion.2), channel_id=1, source_target_pairs={{0,2},{1,3},{2,0},{3,1},{4,6},{5,7},{6,4},{7,5},{8,10},{9,11},{10,... | collective-permute-start | bytes 3080 | tf_op jit(solution)/shard_map/ppermute | solution.py:269
  28.6 12.9 %collective-permute-start.10 = (bf16[128,768]{1,0:T(8,128)(2,1)S(1)}, bf16[128,768]{1,0:T(8,128)(2,1)S(1)}, u32[]{:S(2)}, u32[]{:S(2)}) collective-permute-start(bf16[128,768]{1,0:T(8,128)(2,1)S(1)} %collective-permute-done.9.refs_5_), channel_id=1, source_target_pairs={{0,4},{1,3},{4,8},{5,1},{8,12},{9,5},{12,14},{13,9},{14,10},{15,13... | collective-permute-start | bytes 589832 | tf_op jit(solution)/shard_map/ppermute | solution.py:276
  30.8 13.0 %collective-permute-start.6 = (bf16[128,768]{1,0:T(8,128)(2,1)}, bf16[128,768]{1,0:T(8,128)(2,1)S(1)}, u32[]{:S(2)}, u32[]{:S(2)}) collective-permute-start(bf16[128,768]{1,0:T(8,128)(2,1)} %collective-permute-done.5.refs_4_), channel_id=1, source_target_pairs={{0,4},{1,3},{4,8},{5,1},{8,12},{9,5},{12,14},{13,9},{14,10},{15,13... | collective-permute-start | bytes 589832 | tf_op jit(solution)/shard_map/ppermute | solution.py:276
  32.4 3.7 %collective-permute-start.2 = (s32[4,128]{1,0:T(4,128)S(1)}, s32[4,128]{1,0:T(4,128)S(1)}, u32[]{:S(2)}, u32[]{:S(2)}) collective-permute-start(s32[4,128]{1,0:T(4,128)S(1)} %pad_add_fusion.1), channel_id=1, source_target_pairs={{0,4},{1,5},{2,6},{3,7},{4,0},{5,1},{6,2},{7,3},{8,12},{9,13},{10,... | collective-permute-start | bytes 6152 | tf_op jit(solution)/shard_map/ppermute | solution.py:269
  36.0 5.4 %collective-permute-start.3 = (s32[8,128]{1,0:T(8,128)S(1)}, s32[8,128]{1,0:T(8,128)S(1)}, u32[]{:S(2)}, u32[]{:S(2)}) collective-permute-start(s32[8,128]{1,0:T(8,128)S(1)} %pad_add_fusion), channel_id=1, source_target_pairs={{0,8},{1,9},{2,10},{3,11},{4,12},{5,13},{6,14},{7,15},{8,0},{9,1},... | collective-permute-start | bytes 12296 | tf_op jit(solution)/shard_map/ppermute | solution.py:269
  41.5 11.6 %collective-permute-start.11 = (bf16[128,768]{1,0:T(8,128)(2,1)S(1)}, bf16[128,768]{1,0:T(8,128)(2,1)S(1)}, u32[]{:S(2)}, u32[]{:S(2)}) collective-permute-start(bf16[128,768]{1,0:T(8,128)(2,1)S(1)} %collective-permute-done.10.refs_3_), channel_id=1, source_target_pairs={{0,4},{1,3},{4,8},{5,1},{8,12},{9,5},{12,14},{13,9},{14,10},{15,13... | collective-permute-start | bytes 589832 | tf_op jit(solution)/shard_map/ppermute | solution.py:276
  43.8 9.3 %collective-permute-start.7 = (bf16[128,768]{1,0:T(8,128)(2,1)S(1)}, bf16[128,768]{1,0:T(8,128)(2,1)S(1)}, u32[]{:S(2)}, u32[]{:S(2)}) collective-permute-start(bf16[128,768]{1,0:T(8,128)(2,1)S(1)} %collective-permute-done.6.refs_2_), channel_id=1, source_target_pairs={{0,4},{1,3},{4,8},{5,1},{8,12},{9,5},{12,14},{13,9},{14,10},{15,13... | collective-permute-start | bytes 589832 | tf_op jit(solution)/shard_map/ppermute | solution.py:276
  43.9 1.4 %copy-start = (bf16[1,768,960]{1,2,0:T(8,128)(2,1)S(1)}, bf16[1,768,960]{1,2,0:T(8,128)(2,1)}, u32[]{:S(2)}) copy-start(bf16[1,768,960]{1,2,0:T(8,128)(2,1)} %param.17) | copy-start | bytes 4423684
  45.2 0.9 %copy-start.3 = (bf16[128,768]{1,0:T(8,128)(2,1)S(1)}, bf16[128,768]{1,0:T(8,128)(2,1)}, u32[]{:S(2)}) copy-start(bf16[128,768]{1,0:T(8,128)(2,1)} %refs_2_.1) | copy-start | bytes 589828
  46.2 4.5 %copy-start.1 = (bf16[1,768,960]{1,2,0:T(8,128)(2,1)S(1)}, bf16[1,768,960]{1,2,0:T(8,128)(2,1)}, u32[]{:S(2)}) copy-start(bf16[1,768,960]{1,2,0:T(8,128)(2,1)} %param.17) | copy-start | bytes 4423684

commit v3 on v0

--- a/solution.py
+++ b/solution.py
@@ -1,10 +1,13 @@
 import jax
 import jax.numpy as jnp
 from jax import lax
+from jax.experimental import pallas as pl
+from jax.experimental.pallas import tpu as pltpu
 from jax.sharding import PartitionSpec as P
 
 TILE = 128
 BLK_DEV = 2
+SLOT_ROWS = 16
 
 
 def layer_norm(activated, norm_gain, norm_bias):
@@ -23,7 +26,7 @@
     return jnp.max(jnp.where(keep[:, :, None], saturated, 0.0), axis=1)
 
 
-def local(
+def move_weights(
     hidden_states,
     doc_lengths,
     transform_weight,
@@ -93,6 +96,319 @@
     return (impacts, summary.reshape(BLK_DEV, tiles_t * TILE))
 
 
+def dot_t(left, right):
+    return lax.dot_general(
+        left, right, (((1,), (1,)), ((), ())), preferred_element_type=jnp.float32
+    )
+
+
+def chip_at(me, shift, across, layers):
+    chip = me // 2
+    layer = (chip // 2 - shift + layers) % layers
+    return 2 * layer + ((chip % 2) ^ across)
+
+
+def masked(ref, length):
+    here = ref[...]
+    keep = lax.broadcasted_iota(jnp.int32, here.shape, 0).astype(jnp.float32) < length
+    first = jnp.broadcast_to(here[0:1, :].astype(jnp.float32), here.shape).astype(here.dtype)
+    return jnp.where(keep, here, first)
+
+
+def normed_rows(docs, lengths, weight, params):
+    rows = jnp.concatenate([masked(ref, length) for ref, length in zip(docs, lengths)], axis=0)
+    pre = jnp.dot(rows, weight[...], preferred_element_type=jnp.float32) + params[0][...]
+    act = 0.5 * pre * (1.0 + lax.erf(pre * (0.5**0.5)))
+    return layer_norm(act.astype(jnp.bfloat16), params[1][...], params[2][...])
+
+
+def tops_of(normed, w_ref, count):
+    logits = dot_t(normed, w_ref[...])
+    seq = normed.shape[0] // count
+    return [
+        jnp.max(logits[j * seq : (j + 1) * seq], axis=0, keepdims=True) for j in range(count)
+    ]
+
+
+def start_kernel(tiles_ref, owners_ref, slots_ref, length_ref, weight_ref, out_ref, sem):
+    rows, width = weight_ref.shape
+    copy = pltpu.make_async_copy(weight_ref, out_ref.at[:, pl.ds(0, width)], sem)
+    copy.start()
+    lane = lax.broadcasted_iota(jnp.int32, (rows, TILE), 1)
+    table = jnp.where(lane == TILE - 1, length_ref[0], -1)
+    devices = lax.axis_size("doc")
+    for k in range(tiles_ref.shape[2]):
+        block = slots_ref[0, 0, k] * devices + owners_ref[0, 0, k]
+        table = jnp.where(lane == tiles_ref[0, 0, k], block, table)
+    out_ref[:, width:] = table.astype(jnp.float32).astype(jnp.bfloat16)
+    copy.wait()
+
+
+def pack_kernel(*refs):
+    blocks, out_ref = refs[:-1], refs[-1]
+    rows, width = blocks[0].shape[0], out_ref.shape[1]
+    tables = jnp.zeros((SLOT_ROWS, width), jnp.float32)
+    row = lax.broadcasted_iota(jnp.int32, (SLOT_ROWS, TILE), 0)
+    tables = jnp.zeros((SLOT_ROWS, TILE), jnp.float32)
+    for k, ref in enumerate(blocks):
+        out_ref[k * rows : (k + 1) * rows, :] = ref[:, 0:width]
+        tables = jnp.where(row == k, ref[0:SLOT_ROWS, width:].astype(jnp.float32), tables)
+    last = len(blocks) * rows
+    out_ref[last : last + SLOT_ROWS, :] = jnp.zeros((SLOT_ROWS, width), out_ref.dtype)
+    out_ref[last : last + SLOT_ROWS, 0:TILE] = tables.astype(out_ref.dtype)
+
+
+def fetch(ref, slot, sem):
+    copy = pltpu.make_async_copy(ref, slot, sem)
+    copy.start()
+    return copy
+
+
+def first_kernel(layers, *refs):
+    me_ref, refs = refs[0], refs[1:]
+    docs, refs = refs[:layers], refs[layers:]
+    packed, refs = refs[:4], refs[4:]
+    params, refs = refs[:3], refs[3:]
+    mine_ref, theirs_ref, refs = refs[0], refs[1], refs[2:]
+    best_refs, weight, meta_ref, mine, own, sems = refs[:2], refs[2], refs[3], *refs[4:]
+    mine_copy = fetch(mine_ref, mine, sems.at[0])
+    own_copy = fetch(docs[0], own, sems.at[1])
+    me = me_ref[0]
+    core = me % 2
+    rows = weight.shape[0] // (4 * layers)
+    for across in range(2):
+        for shift in range(layers):
+            chip = chip_at(me, shift, across, layers)
+            block = slice(shift * rows, (shift + 1) * rows)
+            at = pl.multiple_of((2 * chip + core) * rows, SLOT_ROWS)
+            weight[pl.ds(at, rows), :] = packed[across][block, :]
+            at = pl.multiple_of((2 * chip + 1 - core) * rows, SLOT_ROWS)
+            weight[pl.ds(at, rows), :] = packed[2 + across][block, :]
+    tables = [
+        ref[layers * rows : layers * rows + SLOT_ROWS, 0:TILE].astype(jnp.float32)
+        for ref in packed[:2]
+    ]
+    meta_ref[...] = jnp.concatenate([t[0:layers] for t in tables], axis=0).astype(jnp.int32)
+    lengths = [tables[0][k : k + 1, TILE - 1 : TILE] for k in range(layers)]
+    docs = [own, *docs[1:]]
+    order = [*range(1, layers), 0]
+    for first in range(0, layers, 2):
+        pair = order[first : first + 2]
+        if 0 in pair:
+            own_copy.wait()
+        normed = normed_rows(
+            [docs[k] for k in pair], [lengths[k] for k in pair], weight, params
+        )
+        if first == 0:
+            mine_copy.wait()
+        for w_ref, best in zip((mine, theirs_ref), best_refs):
+            for k, top in zip(pair, tops_of(normed, w_ref, 2)):
+                best[k : k + 1, :] = top
+
+
+def next_kernel(layers, first, *refs):
+    meta_ref, refs = refs[0], refs[1:]
+    docs, weight, params, refs = refs[:2], refs[2], refs[3:6], refs[6:]
+    mine_ref, theirs_ref, best_refs, mine, sem = refs[0], refs[1], refs[2:4], *refs[4:]
+    copy = fetch(mine_ref, mine, sem)
+    lengths = [
+        meta_ref[layers + first + k : layers + first + k + 1, TILE - 1 : TILE].astype(jnp.float32)
+        for k in range(2)
+    ]
+    normed = normed_rows(docs, lengths, weight, params)
+    copy.wait()
+    for w_ref, best in zip((mine, theirs_ref), best_refs):
+        for j, top in enumerate(tops_of(normed, w_ref, 2)):
+            best[j : j + 1, :] = top
+
+
+def last_kernel(layers, counts, *refs):
+    me_ref, table_ref, meta_ref, refs = refs[0], refs[1], refs[2], refs[3:]
+    docs, weight, params, refs = refs[:2], refs[2], refs[3:6], refs[6:]
+    mine_ref, theirs_ref, dbias_ref, refs = refs[0], refs[1], refs[2], refs[3:]
+    earlier, refs = refs[: 2 * len(counts)], refs[2 * len(counts) :]
+    out_ref, best, send, mine, sem = refs
+    copy = fetch(mine_ref, mine, sem)
+    me = me_ref[0]
+    core, chip = me % 2, me // 2
+    devices = 4 * layers
+    tiles = 2 * mine_ref.shape[0] // TILE
+    lengths = [
+        meta_ref[2 * layers - 2 + k : 2 * layers - 1 + k, TILE - 1 : TILE].astype(jnp.float32)
+        for k in range(2)
+    ]
+    normed = normed_rows(docs, lengths, weight, params)
+    found = []
+    copy.wait()
+    for k, w_ref in enumerate((mine, theirs_ref)):
+        parts = [earlier[2 * n + k][0:count, :] for n, count in enumerate(counts)]
+        found.append(jnp.concatenate([*parts, *tops_of(normed, w_ref, 2)], axis=0))
+    low = jnp.where(core == 0, found[0], found[1])
+    high = jnp.where(core == 0, found[1], found[0])
+    logits = jnp.concatenate([low, high], axis=1) + dbias_ref[...]
+    impacts = jnp.log1p(jnp.maximum(logits, 0.0)).astype(jnp.bfloat16).astype(jnp.float32)
+    best[...] = jnp.zeros(best.shape, jnp.float32)
+    for k in range(2 * layers):
+        doc = 2 * chip_at(me, k % layers, k // layers, layers) + core
+        best[pl.ds(doc, 1), :] = impacts[k : k + 1, :]
+    send[...] = jnp.zeros(send.shape, jnp.float32)
+    stride = out_ref.shape[1]
+    target = lax.broadcasted_iota(jnp.int32, (BLK_DEV * devices, TILE), 0)
+    for t in range(tiles):
+        lanes = slice(t * TILE, (t + 1) * TILE)
+        send[pl.ds(t, devices, stride=stride), :] = best[:, lanes]
+        blocks = jnp.zeros((BLK_DEV * devices, TILE), jnp.float32)
+        for k in range(2 * layers):
+            block = table_ref[k, chip * tiles + t]
+            blocks = jnp.maximum(
+                blocks, jnp.where(target == block, impacts[k : k + 1, lanes], 0.0)
+            )
+        for s in range(BLK_DEV):
+            send[pl.ds((1 + s) * SLOT_ROWS + t, devices, stride=stride), :] = blocks[
+                s * devices : (s + 1) * devices
+            ]
+    out_ref[...] = send[...].astype(jnp.bfloat16).reshape(out_ref.shape)
+
+
+def move_tokens(
+    hidden_states,
+    doc_lengths,
+    transform_weight,
+    transform_bias,
+    norm_gain,
+    norm_bias,
+    decoder_weight,
+    decoder_bias,
+    tile_ids,
+    owner_ids,
+    block_slots,
+):
+    devices = lax.axis_size("doc")
+    chips = devices // 2
+    layers = chips // 2
+    seq, width = hidden_states.shape
+    rows = transform_weight.shape[0]
+    half = decoder_weight.shape[2]
+    tiles = 2 * half // TILE
+    me = lax.axis_index("doc").astype(jnp.int32)
+
+    def flip(value, bit):
+        return lax.ppermute(value, "doc", [(i, i ^ bit) for i in range(devices)])
+
+    def shift(value, by):
+        return lax.ppermute(value, "doc", [(i, (i + 4 * by) % devices) for i in range(devices)])
+
+    smem = pl.BlockSpec(memory_space=pltpu.SMEM)
+    vmem = pl.BlockSpec(memory_space=pltpu.VMEM)
+    hbm = pl.BlockSpec(memory_space=pltpu.HBM)
+
+    def stay(value):
+        return pltpu.with_memory_space_constraint(value, pltpu.HBM)
+
+    limit = pltpu.CompilerParams(vmem_limit_bytes=24 * 1024 * 1024)
+
+    def cost(docs):
+        return pl.CostEstimate(
+            flops=2 * docs * seq * width * (width + 2 * half),
+            bytes_accessed=1024 * 1024,
+            transcendentals=docs * seq * width,
+        )
+
+    def shape(dims, dtype):
+        return jax.ShapeDtypeStruct(dims, dtype)
+
+    block = pl.pallas_call(
+        start_kernel,
+        out_shape=shape((rows, width + TILE), jnp.bfloat16),
+        in_specs=[smem] * 4 + [hbm],
+        out_specs=vmem,
+        scratch_shapes=[pltpu.SemaphoreType.DMA],
+        compiler_params=limit,
+    )(
+        stay(tile_ids),
+        stay(owner_ids[..., 0]),
+        stay(block_slots),
+        doc_lengths,
+        stay(transform_weight),
+    )
+    blocks = [block] + [shift(block, by) for by in range(1, layers)]
+    near = [hidden_states] + [shift(hidden_states, by) for by in range(1, layers)]
+    far = [flip(value, 2) for value in near]
+    blocks, near[1], far[0] = lax.optimization_barrier((blocks, near[1], far[0]))
+    packed = pl.pallas_call(
+        pack_kernel,
+        out_shape=shape((layers * rows + SLOT_ROWS, width), jnp.bfloat16),
+        in_specs=[vmem] * layers,
+        out_specs=vmem,
+        compiler_params=limit,
+    )(*blocks)
+    packed_across = flip(packed, 2)
+    packed_across, near[2] = lax.optimization_barrier((packed_across, near[2]))
+    packed_all = [packed, packed_across, flip(packed, 1), flip(packed_across, 1)]
+
+    weight_rows = jnp.swapaxes(decoder_weight[0], 0, 1)
+    halves = (stay(weight_rows), flip(weight_rows, 1))
+
+    where = me[None]
+    params = (transform_bias[None, :], norm_gain[None, :], norm_bias[None, :])
+    slot = pltpu.VMEM((half, width), jnp.bfloat16)
+    best_shape = shape((8, half), jnp.float32)
+    *best, weight, meta = pl.pallas_call(
+        lambda *refs: first_kernel(layers, *refs),
+        out_shape=[
+            best_shape,
+            best_shape,
+            shape((width, width), jnp.bfloat16),
+            shape((chips, TILE), jnp.int32),
+        ],
+        in_specs=[smem, hbm] + [vmem] * (layers - 1 + 4 + 3) + [hbm, vmem],
+        out_specs=[vmem] * 4,
+        scratch_shapes=[
+            slot,
+            pltpu.VMEM((seq, width), jnp.bfloat16),
+            pltpu.SemaphoreType.DMA((2,)),
+        ],
+        compiler_params=limit,
+        cost_estimate=cost(layers),
+    )(where, stay(hidden_states), *near[1:], *packed_all, *params, *halves)
+    counts = [layers]
+    for first in range(0, layers - 2, 2):
+        best += pl.pallas_call(
+            lambda *refs, first=first: next_kernel(layers, first, *refs),
+            out_shape=[best_shape] * 2,
+            in_specs=[vmem] * 7 + [hbm, vmem],
+            out_specs=[vmem] * 2,
+            scratch_shapes=[slot, pltpu.SemaphoreType.DMA],
+            compiler_params=limit,
+            cost_estimate=cost(2),
+        )(meta, *far[first : first + 2], weight, *params, *halves)
+        counts.append(2)
+    bias = lax.dynamic_slice_in_dim(decoder_bias, (me // 2) * 2 * half, 2 * half, 0)[None, :]
+    send = pl.pallas_call(
+        lambda *refs: last_kernel(layers, counts, *refs),
+        out_shape=shape((devices, (1 + BLK_DEV) * SLOT_ROWS, TILE), jnp.bfloat16),
+        in_specs=[smem] * 2 + [vmem] * 7 + [hbm] + [vmem] * (2 + len(best)),
+        out_specs=vmem,
+        scratch_shapes=[
+            pltpu.VMEM((devices, 2 * half), jnp.float32),
+            pltpu.VMEM((devices * (1 + BLK_DEV) * SLOT_ROWS, TILE), jnp.float32),
+            slot,
+            pltpu.SemaphoreType.DMA,
+        ],
+        compiler_params=limit,
+        cost_estimate=cost(2),
+    )(where, meta, meta, *far[layers - 2 :], weight, *params, *halves, bias, *best)
+    got = lax.all_to_all(send, "doc", split_axis=0, concat_axis=0, tiled=True)
+    got = got.reshape(chips, 2, 1 + BLK_DEV, SLOT_ROWS, TILE)[:, :, :, :tiles]
+    whole = jnp.swapaxes(jnp.maximum(got[:, 0], got[:, 1]), 0, 1).reshape(1 + BLK_DEV, -1)
+    return (whole[:1], whole[1:])
+
+
+def tokens_move(mesh):
+    devices = mesh.shape["doc"]
+    return mesh.shape["term"] == 1 and devices >= 8 and devices & (devices - 1) == 0
+
+
 def solution(mesh):
     placed = (
         P(("groups", "doc"), None),
@@ -107,6 +423,15 @@
         P("term", ("groups", "doc"), None, None),
         P("term", ("groups", "doc"), None),
     )
+
+    def local(*args):
+        pair = 2 * args[6].shape[2]
+        tiles = pair * (mesh.shape["doc"] // 2) // TILE
+        fits = pair % TILE == 0 and tiles < TILE and pair // TILE <= SLOT_ROWS
+        if tokens_move(mesh) and args[1].shape[0] == 1 and fits:
+            return move_tokens(*args)
+        return move_weights(*args)
+
     return jax.shard_map(
         local,
         mesh=mesh,

time: 207 us -> 68.7 us (0.33)
  waiting for transfers between devices: 155 us -> 21.9 us
  matrix products: 15.2 us -> 0 us
  between operations: 14.8 us -> 1.38 us
  Pallas kernels: 0 us -> 12.5 us
  blocking collectives: 0 us -> 11.9 us
  other arithmetic: 5.45 us -> 0.01 us
  starting transfers between devices: 12.1 us -> 16.4 us
    all_gather x2 -> x0, waiting for transfers between devices: 142 us -> none  [the longest x1 119 us: local(): lax.all_gather(decoder_weight, 'doc', axis=2, tiled=True)[0]]
    ppermute x0 -> x14, waiting for transfers between devices: none -> 21.9 us  [the longest x6 18.7 us: shift(): lax.ppermute(value, 'doc', [(i, (i + 4 * by) % devices) for i in range(de...]
    ppermute x0 -> x14, starting transfers between devices: none -> 16.4 us  [the longest x6 10.4 us: shift(): lax.ppermute(value, 'doc', [(i, (i + 4 * by) % devices) for i in range(de...]
    dot_general x2 -> x0, matrix products: 15.2 us -> none  [the longest x1 12.8 us: local(): jnp.dot(normed, lax.all_gather(decoder_weight, 'doc', axis=2, tiled=True)...]
    pallas_call x0 -> x5, Pallas kernels: none -> 12.5 us  [the longest x1 4.39 us: move_tokens(): pl.pallas_call(lambda *refs: first_kernel(layers, *refs), out_shape=[best...]
    all_to_all x2 -> x0, starting transfers between devices: 12 us -> none  [the longest x1 7.36 us: local(): lax.all_to_all(out_tags.reshape(owner_count, capacity), 'doc', split_axis...]
    all_to_all x0 -> x1, blocking collectives: none -> 11.9 us  [move_tokens(): got = lax.all_to_all(send, 'doc', split_axis=0, concat_axis=0, tiled=True)]
    all_to_all x2 -> x0, waiting for transfers between devices: 10.8 us -> none  [the longest x1 5.83 us: local(): lax.all_to_all(outgoing.reshape(owner_count, capacity, TILE), 'doc', spli...]
  transfers between devices with their start and end apart: 4 -> 14, of which waited for: 4 -> 6; matrix products, arithmetic and copies ran while one was open for 4% -> 4% of each run, Pallas kernels for 0% -> 13%
where the time goes in v3:
time: 68.7 us; the launch traced here: 68.2 us
  waiting for transfers between devices  21.9 us (32%)
  starting transfers between devices  16.4 us (24%)
  Pallas kernels  12.5 us (18%)
  blocking collectives  11.9 us (17%)
  local copies, waits for them, and re-layouts  4.18 us (6%)
  between operations  1.38 us (2%)
    ppermute x6, waiting for transfers between devices, shift(): lax.ppermute(value, 'doc', [(i, (i + 4 * by) % devices) for i in range(de...  18.7 us
    all_to_all x1, blocking collectives, move_tokens(): got = lax.all_to_all(send, 'doc', split_axis=0, concat_axis=0, tiled=True)  11.9 us
    ppermute x6, starting transfers between devices, shift(): lax.ppermute(value, 'doc', [(i, (i + 4 * by) % devices) for i in range(de...  10.4 us
    ppermute x8, starting transfers between devices, flip(): return lax.ppermute(value, 'doc', [(i, i ^ bit) for i in range(devices)])  5.99 us
    pallas_call x1, Pallas kernels, move_tokens(): pl.pallas_call(lambda *refs: first_kernel(layers, *refs), out_shape=[best...  4.39 us
    pallas_call x1, Pallas kernels, move_tokens(): pl.pallas_call(lambda *refs: last_kernel(layers, counts, *refs), out_shap...  3.49 us
    ppermute x8, waiting for transfers between devices, flip(): return lax.ppermute(value, 'doc', [(i, i ^ bit) for i in range(devices)])  3.23 us
    pallas_call x1, Pallas kernels, move_tokens(): pl.pallas_call(lambda *refs, first=first: next_kernel(layers, first, *ref...  3.03 us
  transfers between devices with their start and end apart: 14, of which 6 were waited for; matrix products, arithmetic and copies ran while one was open for 4% of the time, Pallas kernels for 13%

profile of v3, /device:TPU:0, one launch (start us, length us, event | category | flops | bytes accessed | tf_op | source)
XLA Modules:
  0.0 68.2 jit_solution(5372751966813320830)
XLA Ops:
  0.6 0.5 collective-permute-start.10
  1.1 2.6 %collective-permute-start.3 = (bf16[128,768]{1,0:T(8,128)(2,1)}, bf16[128,768]{1,0:T(8,128)(2,1)S(1)}, u32[]{:S(2)}, u32[]{:S(2)}) collective-permute-start(bf16[128,768]{1,0:T(8,128)(2,1)} %refs_1_.1), channel_id=1, source_target_pairs={{0,4},{1,5},{2,6},{3,7},{4,8},{5,9},{6,10},{7,11},{8,12},{9,13},{1... | collective-permute-start | bytes 589832 | tf_op jit(solution)/shard_map/ppermute | solution.py:299
  3.8 1.5 %collective-permute-start.4 = (bf16[128,768]{1,0:T(8,128)(2,1)}, bf16[128,768]{1,0:T(8,128)(2,1)S(1)}, u32[]{:S(2)}, u32[]{:S(2)}) collective-permute-start(bf16[128,768]{1,0:T(8,128)(2,1)} %refs_1_.1), channel_id=1, source_target_pairs={{0,2},{1,3},{2,0},{3,1},{4,6},{5,7},{6,4},{7,5},{8,10},{9,11},{10,... | collective-permute-start | bytes 589832 | tf_op jit(solution)/shard_map/ppermute | solution.py:296
  5.9 1.6 %shard_map.122.refs_0_ = bf16[48,896]{1,0:T(8,128)(2,1)S(1)} custom-call(s32[1,1,32]{2,1,0:T(1,128)} %tiles_ref.1, s32[1,1,32]{2,1,0:T(1,128)} %bitcast.15, s32[1,1,32]{2,1,0:T(1,128)} %slots_ref.1, s32[1]{0:T(128)S(6)} %copy.22.length_ref, bf16[48,768]{1,0:T(8,128)(2,1)} %weight_ref.1), custom_call_target="tpu_custom_call" | custom-call | tf_op jit(solution)/shard_map/pallas_call | solution.py:320
  7.5 1.6 %collective-permute-start = (bf16[48,896]{1,0:T(8,128)(2,1)S(1)}, bf16[48,896]{1,0:T(8,128)(2,1)S(1)}, u32[]{:S(2)}, u32[]{:S(2)}) collective-permute-start(bf16[48,896]{1,0:T(8,128)(2,1)S(1)} %shard_map.122.refs_0_), channel_id=1, source_target_pairs={{0,4},{1,5},{2,6},{3,7},{4,8},{5,9},{6,10},{7,11},{8,12},{9,13},{1... | collective-permute-start | bytes 258056 | tf_op jit(solution)/shard_map/ppermute | solution.py:299
  9.1 1.2 %collective-permute-start.1 = (bf16[48,896]{1,0:T(8,128)(2,1)S(1)}, bf16[48,896]{1,0:T(8,128)(2,1)S(1)}, u32[]{:S(2)}, u32[]{:S(2)}) collective-permute-start(bf16[48,896]{1,0:T(8,128)(2,1)S(1)} %shard_map.122.refs_0_), channel_id=1, source_target_pairs={{0,8},{1,9},{2,10},{3,11},{4,12},{5,13},{6,14},{7,15},{8,0},{9,1},... | collective-permute-start | bytes 258056 | tf_op jit(solution)/shard_map/ppermute | solution.py:299
  10.4 4.1 %collective-permute-done.refs_1_ = bf16[48,896]{1,0:T(8,128)(2,1)S(1)} collective-permute-done((bf16[48,896]{1,0:T(8,128)(2,1)S(1)}, bf16[48,896]{1,0:T(8,128)(2,1)S(1)}, u32[]{:S(2)}, u32[]{:S(2)}) %collective-permute-start) | collective-permute-done | bytes 86048 | tf_op jit(solution)/shard_map/ppermute | solution.py:299
  14.5 0.9 %collective-permute-start.2 = (bf16[48,896]{1,0:T(8,128)(2,1)S(1)}, bf16[48,896]{1,0:T(8,128)(2,1)S(1)}, u32[]{:S(2)}, u32[]{:S(2)}) collective-permute-start(bf16[48,896]{1,0:T(8,128)(2,1)S(1)} %shard_map.122.refs_0_), channel_id=1, source_target_pairs={{0,12},{1,13},{2,14},{3,15},{4,0},{5,1},{6,2},{7,3},{8,4},{9,5},{1... | collective-permute-start | bytes 258056 | tf_op jit(solution)/shard_map/ppermute | solution.py:299
  15.4 2.2 %collective-permute-done.1.refs_2_ = bf16[48,896]{1,0:T(8,128)(2,1)S(1)} collective-permute-done((bf16[48,896]{1,0:T(8,128)(2,1)S(1)}, bf16[48,896]{1,0:T(8,128)(2,1)S(1)}, u32[]{:S(2)}, u32[]{:S(2)}) %collective-permute-start.1) | collective-permute-done | bytes 86048 | tf_op jit(solution)/shard_map/ppermute | solution.py:299
  17.6 1.4 %collective-permute-done.2.refs_3_ = bf16[48,896]{1,0:T(8,128)(2,1)S(1)} collective-permute-done((bf16[48,896]{1,0:T(8,128)(2,1)S(1)}, bf16[48,896]{1,0:T(8,128)(2,1)S(1)}, u32[]{:S(2)}, u32[]{:S(2)}) %collective-permute-start.2) | collective-permute-done | bytes 86048 | tf_op jit(solution)/shard_map/ppermute | solution.py:299
  18.9 0.0 collective-permute-done.3.refs_2_
  18.9 0.0 collective-permute-done.4.refs_1_
  19.0 1.5 %collective-permute-start.5 = (bf16[208,768]{1,0:T(8,128)(2,1)S(1)}, bf16[208,768]{1,0:T(8,128)(2,1)S(1)}, u32[]{:S(2)}, u32[]{:S(2)}) collective-permute-start(bf16[208,768]{1,0:T(8,128)(2,1)S(1)} %shard_map.123.refs_5_), channel_id=1, source_target_pairs={{0,2},{1,3},{2,0},{3,1},{4,6},{5,7},{6,4},{7,5},{8,10},{9,11},{10,... | collective-permute-start | bytes 958472 | tf_op jit(solution)/shard_map/ppermute | solution.py:296
  20.5 2.1 %collective-permute-start.6 = (bf16[128,768]{1,0:T(8,128)(2,1)}, bf16[128,768]{1,0:T(8,128)(2,1)S(1)}, u32[]{:S(2)}, u32[]{:S(2)}) collective-permute-start(bf16[128,768]{1,0:T(8,128)(2,1)} %refs_1_.1), channel_id=1, source_target_pairs={{0,8},{1,9},{2,10},{3,11},{4,12},{5,13},{6,14},{7,15},{8,0},{9,1},... | collective-permute-start | bytes 589832 | tf_op jit(solution)/shard_map/ppermute | solution.py:299
  22.6 0.0 collective-permute-start.8
  22.6 8.7 %collective-permute-done.6.refs_3_ = bf16[128,768]{1,0:T(8,128)(2,1)S(1)} collective-permute-done((bf16[128,768]{1,0:T(8,128)(2,1)}, bf16[128,768]{1,0:T(8,128)(2,1)S(1)}, u32[]{:S(2)}, u32[]{:S(2)}) %collective-permute-start.6) | collective-permute-done | bytes 196640 | tf_op jit(solution)/shard_map/ppermute | solution.py:299
  31.2 0.0 collective-permute-done.5.refs_6_
  31.2 0.0 collective-permute-start.9
  31.3 1.9 %collective-permute-start.7 = (bf16[128,768]{1,0:T(8,128)(2,1)}, bf16[128,768]{1,0:T(8,128)(2,1)S(1)}, u32[]{:S(2)}, u32[]{:S(2)}) collective-permute-start(bf16[128,768]{1,0:T(8,128)(2,1)} %refs_1_.1), channel_id=1, source_target_pairs={{0,12},{1,13},{2,14},{3,15},{4,0},{5,1},{6,2},{7,3},{8,4},{9,5},{1... | collective-permute-start | bytes 589832 | tf_op jit(solution)/shard_map/ppermute | solution.py:299
  33.1 0.7 %broadcast_in_dim.16.refs_9_.refs_4_.refs_6_ = f32[1,768]{1,0:T(1,128)S(1)} reshape(f32[768]{0:T(1024)} %param.14) | data formatting | bytes 6144 | tf_op jit(solution)/shard_map/broadcast_in_dim | solution.py:353
  33.8 0.7 %broadcast_in_dim.17.refs_10_.refs_5_.refs_7_ = f32[1,768]{1,0:T(1,128)S(1)} reshape(f32[768]{0:T(1024)} %param.15) | data formatting | bytes 6144 | tf_op jit(solution)/shard_map/broadcast_in_dim | solution.py:353
  34.5 0.7 %broadcast_in_dim.18.refs_11_.refs_6_.refs_8_ = f32[1,768]{1,0:T(1,128)S(1)} reshape(f32[768]{0:T(1024)} %param.16) | data formatting | bytes 6144 | tf_op jit(solution)/shard_map/broadcast_in_dim | solution.py:353
  35.2 0.8 %dynamic_slice.3 = f32[1920]{0:T(1024)S(1)} dynamic-slice(f32[15360]{0:T(1024)} %param.18, s32[]{:T(128)S(6)} %select_n.9), dynamic_slice_sizes={1920} | dynamic-slice | bytes 15364 | tf_op jit(solution)/shard_map/dynamic_slice | solution.py:386
  36.0 0.4 collective-permute-start.13
  36.4 2.4 %collective-permute-done.7.refs_4_ = bf16[128,768]{1,0:T(8,128)(2,1)S(1)} collective-permute-done((bf16[128,768]{1,0:T(8,128)(2,1)}, bf16[128,768]{1,0:T(8,128)(2,1)S(1)}, u32[]{:S(2)}, u32[]{:S(2)}) %collective-permute-start.7) | collective-permute-done | bytes 196640 | tf_op jit(solution)/shard_map/ppermute | solution.py:299
  38.8 0.9 %collective-permute-start.11 = (bf16[128,768]{1,0:T(8,128)(2,1)S(1)}, bf16[128,768]{1,0:T(8,128)(2,1)S(1)}, u32[]{:S(2)}, u32[]{:S(2)}) collective-permute-start(bf16[128,768]{1,0:T(8,128)(2,1)S(1)} %collective-permute-done.6.refs_3_), channel_id=1, source_target_pairs={{0,2},{1,3},{2,0},{3,1},{4,6},{5,7},{6,4},{7,5},{8,10},{9,11},{10,... | collective-permute-start | bytes 589832 | tf_op jit(solution)/shard_map/ppermute | solution.py:296
  39.7 0.0 collective-permute-done.8.refs_7_
  39.7 1.1 %collective-permute-start.12 = (bf16[128,768]{1,0:T(8,128)(2,1)S(1)}, bf16[128,768]{1,0:T(8,128)(2,1)S(1)}, u32[]{:S(2)}, u32[]{:S(2)}) collective-permute-start(bf16[128,768]{1,0:T(8,128)(2,1)S(1)} %collective-permute-done.7.refs_4_), channel_id=1, source_target_pairs={{0,2},{1,3},{2,0},{3,1},{4,6},{5,7},{6,4},{7,5},{8,10},{9,11},{10,... | collective-permute-start | bytes 589832 | tf_op jit(solution)/shard_map/ppermute | solution.py:296
  40.8 0.0 collective-permute-done.9.refs_8_
  40.8 0.0 collective-permute-done.10.refs_13_.refs_8_.refs_10_
  40.8 4.4 %shard_map.124 = (f32[8,960]{1,0:T(8,128)S(1)}, f32[8,960]{1,0:T(8,128)S(1)}, bf16[768,768]{1,0:T(8,128)(2,1)S(1)}, s32[8,128]{1,0:T(8,128)S(1)}) custom-call(s32[1]{0:T(128)} %bitcast.refs_0_, bf16[128,768]{1,0:T(8,128)(2,1)} %refs_1_.1, bf16[128,768]{1,0:T(8,128)(2,1)S(1)} %collective-permute-done.3.refs_2_, ...), custom_call_target="tpu_custom_call" | custom-call | flops 2113929216 | bytes 1048576 | tf_op jit(solution)/shard_map/pallas_call | solution.py:356
  45.2 0.0 collective-permute-done.13.refs_2_
  45.2 3.0 %shard_map.125 = (f32[8,960]{1,0:T(8,128)S(1)}, f32[8,960]{1,0:T(8,128)S(1)}) custom-call(s32[8,128]{1,0:T(8,128)S(1)} %get-tuple-element.23.refs_0_.refs_1_.refs_2_, bf16[128,768]{1,0:T(8,128)(2,1)S(1)} %collective-permute-done.4.refs_1_, bf16[128,768]{1,0:T(8,128)(2,1)S(1)} %collective-permute-done.13.refs_2_, ...), custom_call_target="tpu_custom_call" | custom-call | flops 1056964608 | bytes 1048576 | tf_op jit(solution)/shard_map/pallas_call | solution.py:376
  48.3 0.0 collective-permute-done.11.refs_3_
  48.3 3.2 %collective-permute-done.12.refs_4_ = bf16[128,768]{1,0:T(8,128)(2,1)S(1)} collective-permute-done((bf16[128,768]{1,0:T(8,128)(2,1)S(1)}, bf16[128,768]{1,0:T(8,128)(2,1)S(1)}, u32[]{:S(2)}, u32[]{:S(2)}) %collective-permute-start.12) | collective-permute-done | bytes 196640 | tf_op jit(solution)/shard_map/ppermute | solution.py:296
  51.5 3.5 %shard_map.126 = bf16[16,48,128]{2,1,0:T(8,128)(2,1)S(1)} custom-call(s32[1]{0:T(128)} %bitcast.refs_0_, s32[8,128]{1,0:T(8,128)S(1)} %get-tuple-element.23.refs_0_.refs_1_.refs_2_, s32[8,128]{1,0:T(8,128)S(1)} %get-tuple-element.23.refs_0_.refs_1_.refs_2_, bf16[128,768]{1,0:T(8,128)(2,1)S(1)} %collective-permute-done.11.refs_3_, ...), custom_call_target="tpu_custom_call" | custom-call | flops 1056964608 | bytes 1048576 | tf_op jit(solution)/shard_map/pallas_call | solution.py:387
  55.0 11.9 %all_to_all.5 = bf16[16,48,128]{2,1,0:T(8,128)(2,1)S(1)} all-to-all(bf16[16,48,128]{2,1,0:T(8,128)(2,1)S(1)} %shard_map.126), channel_id=1, replica_groups=mesh['groups'=2,'doc'=16,'term'=1] {'doc'}, dimensions={0} | all-to-all | bytes 393216 | tf_op jit(solution)/shard_map/all_to_all | solution.py:401
  66.9 0.7 slice.26
  67.6 0.6 slice.24
  (6 shorter events, 0.1 us)
Async XLA Ops:
  0.6 40.2 %collective-permute-start.10 = (bf16[960,768]{1,0:T(8,128)(2,1)}, bf16[960,768]{1,0:T(8,128)(2,1)S(1)}, u32[]{:S(2)}, u32[]{:S(2)}) collective-permute-start(bf16[960,768]{1,0:T(8,128)(2,1)} %bitcast.10), channel_id=1, source_target_pairs={{0,1},{1,0},{2,3},{3,2},{4,5},{5,4},{6,7},{7,6},{8,9},{9,8},{10,11... | collective-permute-start | bytes 4423688 | tf_op jit(solution)/shard_map/ppermute | solution.py:296
  1.1 17.8 %collective-permute-start.3 = (bf16[128,768]{1,0:T(8,128)(2,1)}, bf16[128,768]{1,0:T(8,128)(2,1)S(1)}, u32[]{:S(2)}, u32[]{:S(2)}) collective-permute-start(bf16[128,768]{1,0:T(8,128)(2,1)} %refs_1_.1), channel_id=1, source_target_pairs={{0,4},{1,5},{2,6},{3,7},{4,8},{5,9},{6,10},{7,11},{8,12},{9,13},{1... | collective-permute-start | bytes 589832 | tf_op jit(solution)/shard_map/ppermute | solution.py:299
  3.8 15.2 %collective-permute-start.4 = (bf16[128,768]{1,0:T(8,128)(2,1)}, bf16[128,768]{1,0:T(8,128)(2,1)S(1)}, u32[]{:S(2)}, u32[]{:S(2)}) collective-permute-start(bf16[128,768]{1,0:T(8,128)(2,1)} %refs_1_.1), channel_id=1, source_target_pairs={{0,2},{1,3},{2,0},{3,1},{4,6},{5,7},{6,4},{7,5},{8,10},{9,11},{10,... | collective-permute-start | bytes 589832 | tf_op jit(solution)/shard_map/ppermute | solution.py:296
  7.5 6.9 %collective-permute-start = (bf16[48,896]{1,0:T(8,128)(2,1)S(1)}, bf16[48,896]{1,0:T(8,128)(2,1)S(1)}, u32[]{:S(2)}, u32[]{:S(2)}) collective-permute-start(bf16[48,896]{1,0:T(8,128)(2,1)S(1)} %shard_map.122.refs_0_), channel_id=1, source_target_pairs={{0,4},{1,5},{2,6},{3,7},{4,8},{5,9},{6,10},{7,11},{8,12},{9,13},{1... | collective-permute-start | bytes 258056 | tf_op jit(solution)/shard_map/ppermute | solution.py:299
  9.1 8.4 %collective-permute-start.1 = (bf16[48,896]{1,0:T(8,128)(2,1)S(1)}, bf16[48,896]{1,0:T(8,128)(2,1)S(1)}, u32[]{:S(2)}, u32[]{:S(2)}) collective-permute-start(bf16[48,896]{1,0:T(8,128)(2,1)S(1)} %shard_map.122.refs_0_), channel_id=1, source_target_pairs={{0,8},{1,9},{2,10},{3,11},{4,12},{5,13},{6,14},{7,15},{8,0},{9,1},... | collective-permute-start | bytes 258056 | tf_op jit(solution)/shard_map/ppermute | solution.py:299
  14.5 4.5 %collective-permute-start.2 = (bf16[48,896]{1,0:T(8,128)(2,1)S(1)}, bf16[48,896]{1,0:T(8,128)(2,1)S(1)}, u32[]{:S(2)}, u32[]{:S(2)}) collective-permute-start(bf16[48,896]{1,0:T(8,128)(2,1)S(1)} %shard_map.122.refs_0_), channel_id=1, source_target_pairs={{0,12},{1,13},{2,14},{3,15},{4,0},{5,1},{6,2},{7,3},{8,4},{9,5},{1... | collective-permute-start | bytes 258056 | tf_op jit(solution)/shard_map/ppermute | solution.py:299
  19.0 12.3 %collective-permute-start.5 = (bf16[208,768]{1,0:T(8,128)(2,1)S(1)}, bf16[208,768]{1,0:T(8,128)(2,1)S(1)}, u32[]{:S(2)}, u32[]{:S(2)}) collective-permute-start(bf16[208,768]{1,0:T(8,128)(2,1)S(1)} %shard_map.123.refs_5_), channel_id=1, source_target_pairs={{0,2},{1,3},{2,0},{3,1},{4,6},{5,7},{6,4},{7,5},{8,10},{9,11},{10,... | collective-permute-start | bytes 958472 | tf_op jit(solution)/shard_map/ppermute | solution.py:296
  20.5 10.7 %collective-permute-start.6 = (bf16[128,768]{1,0:T(8,128)(2,1)}, bf16[128,768]{1,0:T(8,128)(2,1)S(1)}, u32[]{:S(2)}, u32[]{:S(2)}) collective-permute-start(bf16[128,768]{1,0:T(8,128)(2,1)} %refs_1_.1), channel_id=1, source_target_pairs={{0,8},{1,9},{2,10},{3,11},{4,12},{5,13},{6,14},{7,15},{8,0},{9,1},... | collective-permute-start | bytes 589832 | tf_op jit(solution)/shard_map/ppermute | solution.py:299
  22.6 17.1 %collective-permute-start.8 = (bf16[208,768]{1,0:T(8,128)(2,1)S(1)}, bf16[208,768]{1,0:T(8,128)(2,1)S(1)}, u32[]{:S(2)}, u32[]{:S(2)}) collective-permute-start(bf16[208,768]{1,0:T(8,128)(2,1)S(1)} %shard_map.123.refs_5_), channel_id=1, source_target_pairs={{0,1},{1,0},{2,3},{3,2},{4,5},{5,4},{6,7},{7,6},{8,9},{9,8},{10,11... | collective-permute-start | bytes 958472 | tf_op jit(solution)/shard_map/ppermute | solution.py:296
  31.2 9.6 %collective-permute-start.9 = (bf16[208,768]{1,0:T(8,128)(2,1)S(1)}, bf16[208,768]{1,0:T(8,128)(2,1)S(1)}, u32[]{:S(2)}, u32[]{:S(2)}) collective-permute-start(bf16[208,768]{1,0:T(8,128)(2,1)S(1)} %collective-permute-done.5.refs_6_), channel_id=1, source_target_pairs={{0,1},{1,0},{2,3},{3,2},{4,5},{5,4},{6,7},{7,6},{8,9},{9,8},{10,11... | collective-permute-start | bytes 958472 | tf_op jit(solution)/shard_map/ppermute | solution.py:296
  31.3 7.5 %collective-permute-start.7 = (bf16[128,768]{1,0:T(8,128)(2,1)}, bf16[128,768]{1,0:T(8,128)(2,1)S(1)}, u32[]{:S(2)}, u32[]{:S(2)}) collective-permute-start(bf16[128,768]{1,0:T(8,128)(2,1)} %refs_1_.1), channel_id=1, source_target_pairs={{0,12},{1,13},{2,14},{3,15},{4,0},{5,1},{6,2},{7,3},{8,4},{9,5},{1... | collective-permute-start | bytes 589832 | tf_op jit(solution)/shard_map/ppermute | solution.py:299
  36.0 9.3 %collective-permute-start.13 = (bf16[128,768]{1,0:T(8,128)(2,1)S(1)}, bf16[128,768]{1,0:T(8,128)(2,1)S(1)}, u32[]{:S(2)}, u32[]{:S(2)}) collective-permute-start(bf16[128,768]{1,0:T(8,128)(2,1)S(1)} %collective-permute-done.3.refs_2_), channel_id=1, source_target_pairs={{0,2},{1,3},{2,0},{3,1},{4,6},{5,7},{6,4},{7,5},{8,10},{9,11},{10,... | collective-permute-start | bytes 589832 | tf_op jit(solution)/shard_map/ppermute | solution.py:296
  38.8 9.5 %collective-permute-start.11 = (bf16[128,768]{1,0:T(8,128)(2,1)S(1)}, bf16[128,768]{1,0:T(8,128)(2,1)S(1)}, u32[]{:S(2)}, u32[]{:S(2)}) collective-permute-start(bf16[128,768]{1,0:T(8,128)(2,1)S(1)} %collective-permute-done.6.refs_3_), channel_id=1, source_target_pairs={{0,2},{1,3},{2,0},{3,1},{4,6},{5,7},{6,4},{7,5},{8,10},{9,11},{10,... | collective-permute-start | bytes 589832 | tf_op jit(solution)/shard_map/ppermute | solution.py:296
  39.7 11.8 %collective-permute-start.12 = (bf16[128,768]{1,0:T(8,128)(2,1)S(1)}, bf16[128,768]{1,0:T(8,128)(2,1)S(1)}, u32[]{:S(2)}, u32[]{:S(2)}) collective-permute-start(bf16[128,768]{1,0:T(8,128)(2,1)S(1)} %collective-permute-done.7.refs_4_), channel_id=1, source_target_pairs={{0,2},{1,3},{2,0},{3,1},{4,6},{5,7},{6,4},{7,5},{8,10},{9,11},{10,... | collective-permute-start | bytes 589832 | tf_op jit(solution)/shard_map/ppermute | solution.py:296

commit v4 on v3

--- a/solution.py
+++ b/solution.py
@@ -117,9 +117,9 @@
 
 def normed_rows(docs, lengths, weight, params):
     rows = jnp.concatenate([masked(ref, length) for ref, length in zip(docs, lengths)], axis=0)
-    pre = jnp.dot(rows, weight[...], preferred_element_type=jnp.float32) + params[0][...]
+    pre = jnp.dot(rows, weight[...], preferred_element_type=jnp.float32) + params[0:1, :]
     act = 0.5 * pre * (1.0 + lax.erf(pre * (0.5**0.5)))
-    return layer_norm(act.astype(jnp.bfloat16), params[1][...], params[2][...])
+    return layer_norm(act.astype(jnp.bfloat16), params[1:2, :], params[2:3, :])
 
 
 def tops_of(normed, w_ref, count):
@@ -130,10 +130,12 @@
     ]
 
 
-def start_kernel(tiles_ref, owners_ref, slots_ref, length_ref, weight_ref, out_ref, sem):
+def start_kernel(tiles_ref, owners_ref, slots_ref, length_ref, *refs):
+    weight_ref, vectors, (out_ref, rows_ref, kept, sems) = refs[0], refs[1:4], refs[4:]
     rows, width = weight_ref.shape
-    copy = pltpu.make_async_copy(weight_ref, out_ref.at[:, pl.ds(0, width)], sem)
-    copy.start()
+    copies = [fetch(weight_ref, out_ref.at[:, pl.ds(0, width)], sems.at[0])]
+    for k, ref in enumerate(vectors):
+        copies.append(fetch(ref, kept.at[pl.ds(k * width, width)], sems.at[1 + k]))
     lane = lax.broadcasted_iota(jnp.int32, (rows, TILE), 1)
     table = jnp.where(lane == TILE - 1, length_ref[0], -1)
     devices = lax.axis_size("doc")
@@ -141,21 +143,22 @@
         block = slots_ref[0, 0, k] * devices + owners_ref[0, 0, k]
         table = jnp.where(lane == tiles_ref[0, 0, k], block, table)
     out_ref[:, width:] = table.astype(jnp.float32).astype(jnp.bfloat16)
-    copy.wait()
+    for copy in copies:
+        copy.wait()
+    for k in range(len(vectors)):
+        rows_ref[k : k + 1, :] = kept[pl.ds(k * width, width)][None, :]
 
 
 def pack_kernel(*refs):
-    blocks, out_ref = refs[:-1], refs[-1]
+    blocks, out_ref, meta_ref = refs[:-2], refs[-2], refs[-1]
     rows, width = blocks[0].shape[0], out_ref.shape[1]
-    tables = jnp.zeros((SLOT_ROWS, width), jnp.float32)
-    row = lax.broadcasted_iota(jnp.int32, (SLOT_ROWS, TILE), 0)
-    tables = jnp.zeros((SLOT_ROWS, TILE), jnp.float32)
+    row = lax.broadcasted_iota(jnp.int32, meta_ref.shape, 0)
+    tables = jnp.zeros(meta_ref.shape, jnp.float32)
     for k, ref in enumerate(blocks):
         out_ref[k * rows : (k + 1) * rows, :] = ref[:, 0:width]
-        tables = jnp.where(row == k, ref[0:SLOT_ROWS, width:].astype(jnp.float32), tables)
-    last = len(blocks) * rows
-    out_ref[last : last + SLOT_ROWS, :] = jnp.zeros((SLOT_ROWS, width), out_ref.dtype)
-    out_ref[last : last + SLOT_ROWS, 0:TILE] = tables.astype(out_ref.dtype)
+        table = ref[0:SLOT_ROWS, width:].astype(jnp.float32)
+        tables = jnp.where(row == k, table[0 : len(blocks)], tables)
+    meta_ref[...] = tables.astype(jnp.int32)
 
 
 def fetch(ref, slot, sem):
@@ -164,57 +167,47 @@
     return copy
 
 
-def first_kernel(layers, *refs):
-    me_ref, refs = refs[0], refs[1:]
-    docs, refs = refs[:layers], refs[layers:]
-    packed, refs = refs[:4], refs[4:]
-    params, refs = refs[:3], refs[3:]
-    mine_ref, theirs_ref, refs = refs[0], refs[1], refs[2:]
-    best_refs, weight, meta_ref, mine, own, sems = refs[:2], refs[2], refs[3], *refs[4:]
+def length_of(meta_ref, k):
+    return meta_ref[k : k + 1, TILE - 1 : TILE].astype(jnp.float32)
+
+
+def first_kernel(layers, order, *refs):
+    (me_ref, meta_ref), refs = refs[:2], refs[2:]
+    docs, refs = refs[: len(order)], refs[len(order) :]
+    packed, refs = refs[:2], refs[2:]
+    params, mine_ref, theirs_ref, refs = refs[0], refs[1], refs[2], refs[3:]
+    best_refs, weight, mine, own, sems = refs[:2], refs[2], *refs[3:]
     mine_copy = fetch(mine_ref, mine, sems.at[0])
-    own_copy = fetch(docs[0], own, sems.at[1])
+    own_copy = fetch(docs[-1], own, sems.at[1])
     me = me_ref[0]
     core = me % 2
     rows = weight.shape[0] // (4 * layers)
-    for across in range(2):
-        for shift in range(layers):
-            chip = chip_at(me, shift, across, layers)
-            block = slice(shift * rows, (shift + 1) * rows)
-            at = pl.multiple_of((2 * chip + core) * rows, SLOT_ROWS)
-            weight[pl.ds(at, rows), :] = packed[across][block, :]
-            at = pl.multiple_of((2 * chip + 1 - core) * rows, SLOT_ROWS)
-            weight[pl.ds(at, rows), :] = packed[2 + across][block, :]
-    tables = [
-        ref[layers * rows : layers * rows + SLOT_ROWS, 0:TILE].astype(jnp.float32)
-        for ref in packed[:2]
-    ]
-    meta_ref[...] = jnp.concatenate([t[0:layers] for t in tables], axis=0).astype(jnp.int32)
-    lengths = [tables[0][k : k + 1, TILE - 1 : TILE] for k in range(layers)]
-    docs = [own, *docs[1:]]
-    order = [*range(1, layers), 0]
-    for first in range(0, layers, 2):
-        pair = order[first : first + 2]
-        if 0 in pair:
+    for k in range(2 * layers):
+        chip = chip_at(me, k % layers, k // layers, layers)
+        block = slice(k * rows, (k + 1) * rows)
+        at = pl.multiple_of((2 * chip + core) * rows, SLOT_ROWS)
+        weight[pl.ds(at, rows), :] = packed[0][block, :]
+        at = pl.multiple_of((2 * chip + 1 - core) * rows, SLOT_ROWS)
+        weight[pl.ds(at, rows), :] = packed[1][block, :]
+    docs = [*docs[:-1], own]
+    for first in range(0, len(order), 2):
+        if first + 2 == len(order):
             own_copy.wait()
-        normed = normed_rows(
-            [docs[k] for k in pair], [lengths[k] for k in pair], weight, params
-        )
+        lengths = [length_of(meta_ref, k) for k in order[first : first + 2]]
+        normed = normed_rows(docs[first : first + 2], lengths, weight, params)
         if first == 0:
             mine_copy.wait()
         for w_ref, best in zip((mine, theirs_ref), best_refs):
-            for k, top in zip(pair, tops_of(normed, w_ref, 2)):
-                best[k : k + 1, :] = top
-
-
-def next_kernel(layers, first, *refs):
+            for j, top in enumerate(tops_of(normed, w_ref, 2)):
+                best[first + j : first + j + 1, :] = top
+
+
+def next_kernel(order, *refs):
     meta_ref, refs = refs[0], refs[1:]
-    docs, weight, params, refs = refs[:2], refs[2], refs[3:6], refs[6:]
+    docs, weight, params, refs = refs[:2], refs[2], refs[3], refs[4:]
     mine_ref, theirs_ref, best_refs, mine, sem = refs[0], refs[1], refs[2:4], *refs[4:]
     copy = fetch(mine_ref, mine, sem)
-    lengths = [
-        meta_ref[layers + first + k : layers + first + k + 1, TILE - 1 : TILE].astype(jnp.float32)
-        for k in range(2)
-    ]
+    lengths = [length_of(meta_ref, k) for k in order]
     normed = normed_rows(docs, lengths, weight, params)
     copy.wait()
     for w_ref, best in zip((mine, theirs_ref), best_refs):
@@ -222,21 +215,19 @@
             best[j : j + 1, :] = top
 
 
-def last_kernel(layers, counts, *refs):
+def last_kernel(layers, orders, *refs):
     me_ref, table_ref, meta_ref, refs = refs[0], refs[1], refs[2], refs[3:]
-    docs, weight, params, refs = refs[:2], refs[2], refs[3:6], refs[6:]
+    docs, weight, params, refs = refs[:2], refs[2], refs[3], refs[4:]
     mine_ref, theirs_ref, dbias_ref, refs = refs[0], refs[1], refs[2], refs[3:]
+    counts = [len(order) for order in orders[:-1]]
     earlier, refs = refs[: 2 * len(counts)], refs[2 * len(counts) :]
-    out_ref, best, send, mine, sem = refs
+    out_ref, send, mine, sem = refs
     copy = fetch(mine_ref, mine, sem)
     me = me_ref[0]
     core, chip = me % 2, me // 2
     devices = 4 * layers
     tiles = 2 * mine_ref.shape[0] // TILE
-    lengths = [
-        meta_ref[2 * layers - 2 + k : 2 * layers - 1 + k, TILE - 1 : TILE].astype(jnp.float32)
-        for k in range(2)
-    ]
+    lengths = [length_of(meta_ref, k) for k in orders[-1]]
     normed = normed_rows(docs, lengths, weight, params)
     found = []
     copy.wait()
@@ -245,24 +236,24 @@
         found.append(jnp.concatenate([*parts, *tops_of(normed, w_ref, 2)], axis=0))
     low = jnp.where(core == 0, found[0], found[1])
     high = jnp.where(core == 0, found[1], found[0])
-    logits = jnp.concatenate([low, high], axis=1) + dbias_ref[...]
-    impacts = jnp.log1p(jnp.maximum(logits, 0.0)).astype(jnp.bfloat16).astype(jnp.float32)
-    best[...] = jnp.zeros(best.shape, jnp.float32)
-    for k in range(2 * layers):
-        doc = 2 * chip_at(me, k % layers, k // layers, layers) + core
-        best[pl.ds(doc, 1), :] = impacts[k : k + 1, :]
+    logits = jnp.concatenate([low, high], axis=1)
+    order = [k for group in orders for k in group]
+    docs_at = [2 * chip_at(me, k % layers, k // layers, layers) + core for k in order]
+    bias = dbias_ref[...]
+    bias = pltpu.roll(bias, bias.shape[0] - chip * tiles, 0)
     send[...] = jnp.zeros(send.shape, jnp.float32)
     stride = out_ref.shape[1]
     target = lax.broadcasted_iota(jnp.int32, (BLK_DEV * devices, TILE), 0)
     for t in range(tiles):
         lanes = slice(t * TILE, (t + 1) * TILE)
-        send[pl.ds(t, devices, stride=stride), :] = best[:, lanes]
+        impacts = jnp.log1p(jnp.maximum(logits[:, lanes] + bias[t : t + 1, :], 0.0))
+        impacts = impacts.astype(jnp.bfloat16).astype(jnp.float32)
         blocks = jnp.zeros((BLK_DEV * devices, TILE), jnp.float32)
-        for k in range(2 * layers):
+        for n, k in enumerate(order):
+            row = impacts[n : n + 1, :]
+            send[pl.ds(docs_at[n] * stride + t, 1), :] = row
             block = table_ref[k, chip * tiles + t]
-            blocks = jnp.maximum(
-                blocks, jnp.where(target == block, impacts[k : k + 1, lanes], 0.0)
-            )
+            blocks = jnp.maximum(blocks, jnp.where(target == block, row, 0.0))
         for s in range(BLK_DEV):
             send[pl.ds((1 + s) * SLOT_ROWS + t, devices, stride=stride), :] = blocks[
                 s * devices : (s + 1) * devices
@@ -317,12 +308,23 @@
     def shape(dims, dtype):
         return jax.ShapeDtypeStruct(dims, dtype)
 
-    block = pl.pallas_call(
+    def after(value, *done):
+        return lax.optimization_barrier((value, *done))[0]
+
+    near = {1: shift(hidden_states, 1)}
+    far = {0: flip(hidden_states, 2)}
+    block, params = pl.pallas_call(
         start_kernel,
-        out_shape=shape((rows, width + TILE), jnp.bfloat16),
-        in_specs=[smem] * 4 + [hbm],
-        out_specs=vmem,
-        scratch_shapes=[pltpu.SemaphoreType.DMA],
+        out_shape=[
+            shape((rows, width + TILE), jnp.bfloat16),
+            shape((8, width), jnp.float32),
+        ],
+        in_specs=[smem] * 4 + [hbm] * 4,
+        out_specs=[vmem] * 2,
+        scratch_shapes=[
+            pltpu.VMEM((3 * width,), jnp.float32),
+            pltpu.SemaphoreType.DMA((4,)),
+        ],
         compiler_params=limit,
     )(
         stay(tile_ids),
@@ -330,74 +332,87 @@
         stay(block_slots),
         doc_lengths,
         stay(transform_weight),
-    )
-    blocks = [block] + [shift(block, by) for by in range(1, layers)]
-    near = [hidden_states] + [shift(hidden_states, by) for by in range(1, layers)]
-    far = [flip(value, 2) for value in near]
-    blocks, near[1], far[0] = lax.optimization_barrier((blocks, near[1], far[0]))
-    packed = pl.pallas_call(
+        stay(transform_bias),
+        stay(norm_gain),
+        stay(norm_bias),
+    )
+    blocks = [block]
+    for by in range(1, layers):
+        blocks.append(shift(after(block, far[0]) if by > 2 else block, by))
+    weight_rows = jnp.swapaxes(decoder_weight[0], 0, 1)
+    theirs = flip(weight_rows, 1)
+    blocks += [flip(after(value, near[1]) if k > 1 else value, 2) for k, value in enumerate(blocks)]
+    for by in range(2, layers):
+        near[by] = shift(after(hidden_states, blocks[by - 1]), by)
+    for by in range(1, layers):
+        far[by] = flip(near[by], 2)
+    blocks[0] = after(block, far[1], theirs)
+    packed, meta = pl.pallas_call(
         pack_kernel,
-        out_shape=shape((layers * rows + SLOT_ROWS, width), jnp.bfloat16),
-        in_specs=[vmem] * layers,
-        out_specs=vmem,
+        out_shape=[
+            shape((chips * rows, width), jnp.bfloat16),
+            shape((chips, TILE), jnp.int32),
+        ],
+        in_specs=[vmem] * chips,
+        out_specs=[vmem] * 2,
         compiler_params=limit,
     )(*blocks)
-    packed_across = flip(packed, 2)
-    packed_across, near[2] = lax.optimization_barrier((packed_across, near[2]))
-    packed_all = [packed, packed_across, flip(packed, 1), flip(packed_across, 1)]
-
-    weight_rows = jnp.swapaxes(decoder_weight[0], 0, 1)
-    halves = (stay(weight_rows), flip(weight_rows, 1))
-
+    other_packed = flip(after(packed, *near.values()), 1)
+
+    orders = [[1, layers, layers + 1, 0]]
+    orders += [[by, layers + by] for by in range(2, layers)]
+    arrived = {layers + by: value for by, value in far.items()} | near
     where = me[None]
-    params = (transform_bias[None, :], norm_gain[None, :], norm_bias[None, :])
+    halves = (stay(weight_rows), theirs)
     slot = pltpu.VMEM((half, width), jnp.bfloat16)
     best_shape = shape((8, half), jnp.float32)
-    *best, weight, meta = pl.pallas_call(
-        lambda *refs: first_kernel(layers, *refs),
-        out_shape=[
-            best_shape,
-            best_shape,
-            shape((width, width), jnp.bfloat16),
-            shape((chips, TILE), jnp.int32),
-        ],
-        in_specs=[smem, hbm] + [vmem] * (layers - 1 + 4 + 3) + [hbm, vmem],
-        out_specs=[vmem] * 4,
+    first_docs = [arrived[k] for k in orders[0][:-1]]
+    *best, weight = pl.pallas_call(
+        lambda *refs: first_kernel(layers, orders[0], *refs),
+        out_shape=[best_shape, best_shape, shape((width, width), jnp.bfloat16)],
+        in_specs=[smem] + [vmem] * len(orders[0]) + [hbm] + [vmem] * 3 + [hbm, vmem],
+        out_specs=[vmem] * 3,
         scratch_shapes=[
             slot,
             pltpu.VMEM((seq, width), jnp.bfloat16),
             pltpu.SemaphoreType.DMA((2,)),
         ],
         compiler_params=limit,
-        cost_estimate=cost(layers),
-    )(where, stay(hidden_states), *near[1:], *packed_all, *params, *halves)
-    counts = [layers]
-    for first in range(0, layers - 2, 2):
+        cost_estimate=cost(len(orders[0])),
+    )(where, meta, *first_docs, stay(hidden_states), packed, other_packed, params, *halves)
+    for order in orders[1:-1]:
         best += pl.pallas_call(
-            lambda *refs, first=first: next_kernel(layers, first, *refs),
+            lambda *refs, order=order: next_kernel(order, *refs),
             out_shape=[best_shape] * 2,
-            in_specs=[vmem] * 7 + [hbm, vmem],
+            in_specs=[vmem] * 5 + [hbm, vmem],
             out_specs=[vmem] * 2,
             scratch_shapes=[slot, pltpu.SemaphoreType.DMA],
             compiler_params=limit,
             cost_estimate=cost(2),
-        )(meta, *far[first : first + 2], weight, *params, *halves)
-        counts.append(2)
-    bias = lax.dynamic_slice_in_dim(decoder_bias, (me // 2) * 2 * half, 2 * half, 0)[None, :]
+        )(meta, *[arrived[k] for k in order], weight, params, *halves)
     send = pl.pallas_call(
-        lambda *refs: last_kernel(layers, counts, *refs),
+        lambda *refs: last_kernel(layers, orders, *refs),
         out_shape=shape((devices, (1 + BLK_DEV) * SLOT_ROWS, TILE), jnp.bfloat16),
-        in_specs=[smem] * 2 + [vmem] * 7 + [hbm] + [vmem] * (2 + len(best)),
+        in_specs=[smem] * 2 + [vmem] * 5 + [hbm] + [vmem] * (2 + len(best)),
         out_specs=vmem,
         scratch_shapes=[
-            pltpu.VMEM((devices, 2 * half), jnp.float32),
             pltpu.VMEM((devices * (1 + BLK_DEV) * SLOT_ROWS, TILE), jnp.float32),
             slot,
             pltpu.SemaphoreType.DMA,
         ],
         compiler_params=limit,
         cost_estimate=cost(2),
-    )(where, meta, meta, *far[layers - 2 :], weight, *params, *halves, bias, *best)
+    )(
+        where,
+        meta,
+        meta,
+        *[arrived[k] for k in orders[-1]],
+        weight,
+        params,
+        *halves,
+        decoder_bias.reshape(-1, TILE),
+        *best,
+    )
     got = lax.all_to_all(send, "doc", split_axis=0, concat_axis=0, tiled=True)
     got = got.reshape(chips, 2, 1 + BLK_DEV, SLOT_ROWS, TILE)[:, :, :, :tiles]
     whole = jnp.swapaxes(jnp.maximum(got[:, 0], got[:, 1]), 0, 1).reshape(1 + BLK_DEV, -1)

time: 68.7 us -> 65.2 us (0.949)
  waiting for transfers between devices: 21.9 us -> 15.2 us
  blocking collectives: 11.9 us -> 14.5 us
  local copies, waits for them, and re-layouts: 4.18 us -> 2.92 us
  starting transfers between devices: 16.4 us -> 17.5 us
  Pallas kernels: 12.5 us -> 13.3 us
    ppermute x6, waiting for transfers between devices: 18.7 us -> 4.68 us  [shift(): lax.ppermute(value, 'doc', [(i, (i + 4 * by) % devices) for i in range(de...]
    ppermute x8 -> x10, waiting for transfers between devices: 3.23 us -> 10.5 us  [flip(): return lax.ppermute(value, 'doc', [(i, i ^ bit) for i in range(devices)])]
    all_to_all x1, blocking collectives: 11.9 us -> 14.5 us  [move_tokens(): got = lax.all_to_all(send, 'doc', split_axis=0, concat_axis=0, tiled=True)]
    ppermute x8 -> x10, starting transfers between devices: 5.99 us -> 8.25 us  [flip(): return lax.ppermute(value, 'doc', [(i, i ^ bit) for i in range(devices)])]
    broadcast_in_dim x4 -> x0, local copies, waits for them, and re-layouts: 2.07 us -> none  [the longest x3 2.07 us: move_tokens(): params = (transform_bias[None, :], norm_gain[None, :], norm_bias[None, :])]
    unnamed x0 -> x6, local copies, waits for them, and re-layouts: none -> 1.6 us
    ppermute x6, starting transfers between devices: 10.4 us -> 9.27 us  [shift(): lax.ppermute(value, 'doc', [(i, (i + 4 * by) % devices) for i in range(de...]
    pallas_call x5, Pallas kernels: 12.5 us -> 13.3 us  [the longest x1 4.4 us: move_tokens(): pl.pallas_call(lambda *refs: first_kernel(layers, orders[0], *refs), out_...]
  transfers between devices with their start and end apart: 14 -> 16, of which waited for: 6 -> 8; matrix products, arithmetic and copies ran while one was open for 4% -> 0% of each run, Pallas kernels for 13% -> 14%
where the time goes in v4:
time: 65.2 us; the launch traced here: 64.9 us
  starting transfers between devices  17.5 us (27%)
  waiting for transfers between devices  15.2 us (23%)
  blocking collectives  14.5 us (22%)
  Pallas kernels  13.3 us (20%)
  local copies, waits for them, and re-layouts  2.92 us (4%)
  between operations  1.4 us (2%)
    all_to_all x1, blocking collectives, move_tokens(): got = lax.all_to_all(send, 'doc', split_axis=0, concat_axis=0, tiled=True)  14.5 us
    ppermute x10, waiting for transfers between devices, flip(): return lax.ppermute(value, 'doc', [(i, i ^ bit) for i in range(devices)])  10.5 us
    ppermute x6, starting transfers between devices, shift(): lax.ppermute(value, 'doc', [(i, (i + 4 * by) % devices) for i in range(de...  9.27 us
    ppermute x10, starting transfers between devices, flip(): return lax.ppermute(value, 'doc', [(i, i ^ bit) for i in range(devices)])  8.25 us
    ppermute x6, waiting for transfers between devices, shift(): lax.ppermute(value, 'doc', [(i, (i + 4 * by) % devices) for i in range(de...  4.68 us
    pallas_call x1, Pallas kernels, move_tokens(): pl.pallas_call(lambda *refs: first_kernel(layers, orders[0], *refs), out_...  4.4 us
    pallas_call x1, Pallas kernels, move_tokens(): pl.pallas_call(lambda *refs: last_kernel(layers, orders, *refs), out_shap...  4.09 us
    pallas_call x1, Pallas kernels, move_tokens(): pl.pallas_call(lambda *refs, order=order: next_kernel(order, *refs), out_...  3.17 us
  transfers between devices with their start and end apart: 16, of which 8 were waited for; matrix products, arithmetic and copies ran while one was open for 0% of the time, Pallas kernels for 14%

profile of v4, /device:TPU:0, one launch (start us, length us, event | category | flops | bytes accessed | tf_op | source)
XLA Modules:
  0.0 64.9 jit_solution(17009733356045743117)
XLA Ops:
  0.6 0.5 collective-permute-start.2
  1.2 2.6 %collective-permute-start = (bf16[128,768]{1,0:T(8,128)(2,1)}, bf16[128,768]{1,0:T(8,128)(2,1)S(1)}, u32[]{:S(2)}, u32[]{:S(2)}) collective-permute-start(bf16[128,768]{1,0:T(8,128)(2,1)} %refs_5_.1), channel_id=1, source_target_pairs={{0,4},{1,5},{2,6},{3,7},{4,8},{5,9},{6,10},{7,11},{8,12},{9,13},{1... | collective-permute-start | bytes 589832 | tf_op jit(solution)/shard_map/ppermute | solution.py:290
  3.8 1.5 %collective-permute-start.5 = (bf16[128,768]{1,0:T(8,128)(2,1)}, bf16[128,768]{1,0:T(8,128)(2,1)S(1)}, u32[]{:S(2)}, u32[]{:S(2)}) collective-permute-start(bf16[128,768]{1,0:T(8,128)(2,1)} %refs_5_.1), channel_id=1, source_target_pairs={{0,2},{1,3},{2,0},{3,1},{4,6},{5,7},{6,4},{7,5},{8,10},{9,11},{10,... | collective-permute-start | bytes 589832 | tf_op jit(solution)/shard_map/ppermute | solution.py:287
  5.9 1.6 %shard_map.122 = (bf16[48,896]{1,0:T(8,128)(2,1)S(1)}, f32[8,768]{1,0:T(8,128)S(1)}) custom-call(s32[1,1,32]{2,1,0:T(1,128)} %tiles_ref.1, s32[1,1,32]{2,1,0:T(1,128)} %bitcast.17, s32[1,1,32]{2,1,0:T(1,128)} %slots_ref.1, s32[1]{0:T(128)S(6)} %copy.22.length_ref, bf16[48,768]{1,0:T(8,128)(2,1)} %refs_0_.1, f32[768]{0:T(1024)} %refs_1_.1, f32[768]{0:T(1024)} %refs_2_.1, ...), custom_call_target="tpu_custom_call" | custom-call | tf_op jit(solution)/shard_map/pallas_call | solution.py:316
  7.5 2.7 %collective-permute-start.4 = (bf16[48,896]{1,0:T(8,128)(2,1)S(1)}, bf16[48,896]{1,0:T(8,128)(2,1)S(1)}, u32[]{:S(2)}, u32[]{:S(2)}) collective-permute-start(bf16[48,896]{1,0:T(8,128)(2,1)S(1)} %get-tuple-element.20.refs_0_), channel_id=1, source_target_pairs={{0,8},{1,9},{2,10},{3,11},{4,12},{5,13},{6,14},{7,15},{8,0},{9,1},... | collective-permute-start | bytes 258056 | tf_op jit(solution)/shard_map/ppermute | solution.py:290
  10.2 1.4 %collective-permute-done.refs_2_ = bf16[128,768]{1,0:T(8,128)(2,1)S(1)} collective-permute-done((bf16[128,768]{1,0:T(8,128)(2,1)}, bf16[128,768]{1,0:T(8,128)(2,1)S(1)}, u32[]{:S(2)}, u32[]{:S(2)}) %collective-permute-start) | collective-permute-done | bytes 196640 | tf_op jit(solution)/shard_map/ppermute | solution.py:290
  11.6 1.9 %collective-permute-start.1 = (bf16[128,768]{1,0:T(8,128)(2,1)S(1)}, bf16[128,768]{1,0:T(8,128)(2,1)S(1)}, u32[]{:S(2)}, u32[]{:S(2)}) collective-permute-start(bf16[128,768]{1,0:T(8,128)(2,1)S(1)} %collective-permute-done.refs_2_), channel_id=1, source_target_pairs={{0,2},{1,3},{2,0},{3,1},{4,6},{5,7},{6,4},{7,5},{8,10},{9,11},{10,... | collective-permute-start | bytes 589832 | tf_op jit(solution)/shard_map/ppermute | solution.py:287
  13.5 0.0 collective-permute-start.3
  13.5 0.0 collective-permute-done.5.refs_3_
  13.5 3.8 %collective-permute-start.6 = (bf16[48,896]{1,0:T(8,128)(2,1)S(1)}, bf16[48,896]{1,0:T(8,128)(2,1)S(1)}, u32[]{:S(2)}, u32[]{:S(2)}) collective-permute-start(bf16[48,896]{1,0:T(8,128)(2,1)S(1)} %get-tuple-element.20.refs_0_), channel_id=1, source_target_pairs={{0,12},{1,13},{2,14},{3,15},{4,0},{5,1},{6,2},{7,3},{8,4},{9,5},{1... | collective-permute-start | bytes 258056 | tf_op jit(solution)/shard_map/ppermute | solution.py:290
  17.3 0.0 collective-permute-done.4.refs_2_
  17.3 0.2 collective-permute-start.11
  17.5 3.3 %collective-permute-done.3.refs_1_ = bf16[48,896]{1,0:T(8,128)(2,1)S(1)} collective-permute-done((bf16[48,896]{1,0:T(8,128)(2,1)S(1)}, bf16[48,896]{1,0:T(8,128)(2,1)S(1)}, u32[]{:S(2)}, u32[]{:S(2)}) %collective-permute-start.3) | collective-permute-done | bytes 86048 | tf_op jit(solution)/shard_map/ppermute | solution.py:290
  20.8 0.0 collective-permute-start.13
  20.8 0.0 collective-permute-done.6.refs_3_
  20.8 0.1 collective-permute-start.7
  20.9 5.1 %collective-permute-done.7.refs_4_ = bf16[48,896]{1,0:T(8,128)(2,1)S(1)} collective-permute-done((bf16[48,896]{1,0:T(8,128)(2,1)S(1)}, bf16[48,896]{1,0:T(8,128)(2,1)S(1)}, u32[]{:S(2)}, u32[]{:S(2)}) %collective-permute-start.7) | collective-permute-done | bytes 86048 | tf_op jit(solution)/shard_map/ppermute | solution.py:287
  26.0 0.0 collective-permute-start.8
  26.0 0.0 collective-permute-done.1.refs_4_
  26.0 0.0 copy-start.1
  26.0 0.7 %copy-done.1 = bf16[128,768]{1,0:T(8,128)(2,1)} copy-done((bf16[128,768]{1,0:T(8,128)(2,1)}, bf16[128,768]{1,0:T(8,128)(2,1)S(1)}, u32[]{:S(2)}) %copy-start.1) | copy-done | bytes 196632
  26.7 2.0 %collective-permute-start.9 = (bf16[48,896]{1,0:T(8,128)(2,1)S(1)}, bf16[48,896]{1,0:T(8,128)(2,1)S(1)}, u32[]{:S(2)}, u32[]{:S(2)}) collective-permute-start(bf16[48,896]{1,0:T(8,128)(2,1)S(1)} %collective-permute-done.4.refs_2_), channel_id=1, source_target_pairs={{0,2},{1,3},{2,0},{3,1},{4,6},{5,7},{6,4},{7,5},{8,10},{9,11},{10,... | collective-permute-start | bytes 258056 | tf_op jit(solution)/shard_map/ppermute | solution.py:287
  28.7 0.0 collective-permute-done.2.refs_10_.refs_6_.refs_8_
  28.7 0.0 collective-permute-start.10
  28.7 1.8 %collective-permute-done.8.refs_5_ = bf16[48,896]{1,0:T(8,128)(2,1)S(1)} collective-permute-done((bf16[48,896]{1,0:T(8,128)(2,1)S(1)}, bf16[48,896]{1,0:T(8,128)(2,1)S(1)}, u32[]{:S(2)}, u32[]{:S(2)}) %collective-permute-start.8) | collective-permute-done | bytes 86048 | tf_op jit(solution)/shard_map/ppermute | solution.py:287
  30.5 0.9 %collective-permute-done.9.refs_6_ = bf16[48,896]{1,0:T(8,128)(2,1)S(1)} collective-permute-done((bf16[48,896]{1,0:T(8,128)(2,1)S(1)}, bf16[48,896]{1,0:T(8,128)(2,1)S(1)}, u32[]{:S(2)}, u32[]{:S(2)}) %collective-permute-start.9) | collective-permute-done | bytes 86048 | tf_op jit(solution)/shard_map/ppermute | solution.py:287
  31.4 1.8 %collective-permute-done.10.refs_7_ = bf16[48,896]{1,0:T(8,128)(2,1)S(1)} collective-permute-done((bf16[48,896]{1,0:T(8,128)(2,1)S(1)}, bf16[48,896]{1,0:T(8,128)(2,1)S(1)}, u32[]{:S(2)}, u32[]{:S(2)}) %collective-permute-start.10) | collective-permute-done | bytes 86048 | tf_op jit(solution)/shard_map/ppermute | solution.py:287
  33.2 0.0 collective-permute-done.11.refs_3_
  33.2 0.0 collective-permute-done.13.refs_1_
  33.3 0.1 collective-permute-start.14
  33.3 1.0 %collective-permute-start.15 = (bf16[128,768]{1,0:T(8,128)(2,1)S(1)}, bf16[128,768]{1,0:T(8,128)(2,1)S(1)}, u32[]{:S(2)}, u32[]{:S(2)}) collective-permute-start(bf16[128,768]{1,0:T(8,128)(2,1)S(1)} %collective-permute-done.13.refs_1_), channel_id=1, source_target_pairs={{0,2},{1,3},{2,0},{3,1},{4,6},{5,7},{6,4},{7,5},{8,10},{9,11},{10,... | collective-permute-start | bytes 589832 | tf_op jit(solution)/shard_map/ppermute | solution.py:287
  34.3 1.1 %collective-permute-start.12 = (bf16[128,768]{1,0:T(8,128)(2,1)S(1)}, bf16[128,768]{1,0:T(8,128)(2,1)S(1)}, u32[]{:S(2)}, u32[]{:S(2)}) collective-permute-start(bf16[128,768]{1,0:T(8,128)(2,1)S(1)} %collective-permute-done.11.refs_3_), channel_id=1, source_target_pairs={{0,2},{1,3},{2,0},{3,1},{4,6},{5,7},{6,4},{7,5},{8,10},{9,11},{10,... | collective-permute-start | bytes 589832 | tf_op jit(solution)/shard_map/ppermute | solution.py:287
  35.4 0.0 collective-permute-done.14.refs_7_
  35.4 0.0 copy-start.2
  35.4 0.9 %copy-done.2 = bf16[128,768]{1,0:T(8,128)(2,1)S(1)} copy-done((bf16[128,768]{1,0:T(8,128)(2,1)S(1)}, bf16[128,768]{1,0:T(8,128)(2,1)}, u32[]{:S(2)}) %copy-start.2) | copy-done | bytes 196632
  36.4 4.4 %shard_map.124 = (f32[8,960]{1,0:T(8,128)S(1)}, f32[8,960]{1,0:T(8,128)S(1)}, bf16[768,768]{1,0:T(8,128)(2,1)S(1)}) custom-call(s32[1]{0:T(128)} %bitcast.refs_0_, s32[8,128]{1,0:T(8,128)S(1)} %get-tuple-element.23.refs_1_.refs_0_.refs_2_, bf16[128,768]{1,0:T(8,128)(2,1)S(1)} %collective-permute-done.refs_2_, ...), custom_call_target="tpu_custom_call" | custom-call | flops 2113929216 | bytes 1048576 | tf_op jit(solution)/shard_map/pallas_call | solution.py:370
  40.8 0.3 collective-permute-done.15.refs_2_
  41.1 0.0 copy-start
  41.1 3.2 %shard_map.125 = (f32[8,960]{1,0:T(8,128)S(1)}, f32[8,960]{1,0:T(8,128)S(1)}) custom-call(s32[8,128]{1,0:T(8,128)S(1)} %get-tuple-element.23.refs_1_.refs_0_.refs_2_, bf16[128,768]{1,0:T(8,128)(2,1)S(1)} %collective-permute-done.13.refs_1_, bf16[128,768]{1,0:T(8,128)(2,1)S(1)} %collective-permute-done.15.refs_2_, ...), custom_call_target="tpu_custom_call" | custom-call | flops 1056964608 | bytes 1048576 | tf_op jit(solution)/shard_map/pallas_call | solution.py:384
  44.3 0.6 collective-permute-done.12.refs_4_
  44.9 0.0 copy-done
  44.9 4.1 %shard_map.126 = bf16[16,48,128]{2,1,0:T(8,128)(2,1)S(1)} custom-call(s32[1]{0:T(128)} %bitcast.refs_0_, s32[8,128]{1,0:T(8,128)S(1)} %get-tuple-element.23.refs_1_.refs_0_.refs_2_, s32[8,128]{1,0:T(8,128)S(1)} %get-tuple-element.23.refs_1_.refs_0_.refs_2_, bf16[128,768]{1,0:T(8,128)(2,1)S(1)} %collective-permute-done.11.refs_3_, ...), custom_call_target="tpu_custom_call" | custom-call | flops 1056964608 | bytes 1048576 | tf_op jit(solution)/shard_map/pallas_call | solution.py:393
  49.0 14.5 %all_to_all.5 = bf16[16,48,128]{2,1,0:T(8,128)(2,1)S(1)} all-to-all(bf16[16,48,128]{2,1,0:T(8,128)(2,1)S(1)} %shard_map.126), channel_id=1, replica_groups=mesh['groups'=2,'doc'=16,'term'=1] {'doc'}, dimensions={0} | all-to-all | bytes 393216 | tf_op jit(solution)/shard_map/all_to_all | solution.py:416
  63.6 0.7 %slice.26 = bf16[2,15360]{1,0:T(2,128)(2,1)} reshape(bf16[2,8,15,128]{3,2,1,0:T(8,128)(2,1)S(1)} %slice.30) | data formatting | bytes 122880 | tf_op jit(solution)/shard_map/slice | solution.py:419
  64.2 0.6 slice.24
  (5 shorter events, 0.1 us)
Async XLA Ops:
  0.6 28.1 %collective-permute-start.2 = (bf16[960,768]{1,0:T(8,128)(2,1)}, bf16[960,768]{1,0:T(8,128)(2,1)S(1)}, u32[]{:S(2)}, u32[]{:S(2)}) collective-permute-start(bf16[960,768]{1,0:T(8,128)(2,1)} %bitcast.12), channel_id=1, source_target_pairs={{0,1},{1,0},{2,3},{3,2},{4,5},{5,4},{6,7},{7,6},{8,9},{9,8},{10,11... | collective-permute-start | bytes 4423688 | tf_op jit(solution)/shard_map/ppermute | solution.py:287
  1.2 10.4 %collective-permute-start = (bf16[128,768]{1,0:T(8,128)(2,1)}, bf16[128,768]{1,0:T(8,128)(2,1)S(1)}, u32[]{:S(2)}, u32[]{:S(2)}) collective-permute-start(bf16[128,768]{1,0:T(8,128)(2,1)} %refs_5_.1), channel_id=1, source_target_pairs={{0,4},{1,5},{2,6},{3,7},{4,8},{5,9},{6,10},{7,11},{8,12},{9,13},{1... | collective-permute-start | bytes 589832 | tf_op jit(solution)/shard_map/ppermute | solution.py:290
  3.8 9.7 %collective-permute-start.5 = (bf16[128,768]{1,0:T(8,128)(2,1)}, bf16[128,768]{1,0:T(8,128)(2,1)S(1)}, u32[]{:S(2)}, u32[]{:S(2)}) collective-permute-start(bf16[128,768]{1,0:T(8,128)(2,1)} %refs_5_.1), channel_id=1, source_target_pairs={{0,2},{1,3},{2,0},{3,1},{4,6},{5,7},{6,4},{7,5},{8,10},{9,11},{10,... | collective-permute-start | bytes 589832 | tf_op jit(solution)/shard_map/ppermute | solution.py:287
  7.5 9.8 %collective-permute-start.4 = (bf16[48,896]{1,0:T(8,128)(2,1)S(1)}, bf16[48,896]{1,0:T(8,128)(2,1)S(1)}, u32[]{:S(2)}, u32[]{:S(2)}) collective-permute-start(bf16[48,896]{1,0:T(8,128)(2,1)S(1)} %get-tuple-element.20.refs_0_), channel_id=1, source_target_pairs={{0,8},{1,9},{2,10},{3,11},{4,12},{5,13},{6,14},{7,15},{8,0},{9,1},... | collective-permute-start | bytes 258056 | tf_op jit(solution)/shard_map/ppermute | solution.py:290
  11.6 14.4 %collective-permute-start.1 = (bf16[128,768]{1,0:T(8,128)(2,1)S(1)}, bf16[128,768]{1,0:T(8,128)(2,1)S(1)}, u32[]{:S(2)}, u32[]{:S(2)}) collective-permute-start(bf16[128,768]{1,0:T(8,128)(2,1)S(1)} %collective-permute-done.refs_2_), channel_id=1, source_target_pairs={{0,2},{1,3},{2,0},{3,1},{4,6},{5,7},{6,4},{7,5},{8,10},{9,11},{10,... | collective-permute-start | bytes 589832 | tf_op jit(solution)/shard_map/ppermute | solution.py:287
  13.5 7.3 %collective-permute-start.3 = (bf16[48,896]{1,0:T(8,128)(2,1)S(1)}, bf16[48,896]{1,0:T(8,128)(2,1)S(1)}, u32[]{:S(2)}, u32[]{:S(2)}) collective-permute-start(bf16[48,896]{1,0:T(8,128)(2,1)S(1)} %get-tuple-element.20.refs_0_), channel_id=1, source_target_pairs={{0,4},{1,5},{2,6},{3,7},{4,8},{5,9},{6,10},{7,11},{8,12},{9,13},{1... | collective-permute-start | bytes 258056 | tf_op jit(solution)/shard_map/ppermute | solution.py:290
  13.5 7.3 %collective-permute-start.6 = (bf16[48,896]{1,0:T(8,128)(2,1)S(1)}, bf16[48,896]{1,0:T(8,128)(2,1)S(1)}, u32[]{:S(2)}, u32[]{:S(2)}) collective-permute-start(bf16[48,896]{1,0:T(8,128)(2,1)S(1)} %get-tuple-element.20.refs_0_), channel_id=1, source_target_pairs={{0,12},{1,13},{2,14},{3,15},{4,0},{5,1},{6,2},{7,3},{8,4},{9,5},{1... | collective-permute-start | bytes 258056 | tf_op jit(solution)/shard_map/ppermute | solution.py:290
  17.3 15.9 %collective-permute-start.11 = (bf16[128,768]{1,0:T(8,128)(2,1)}, bf16[128,768]{1,0:T(8,128)(2,1)S(1)}, u32[]{:S(2)}, u32[]{:S(2)}) collective-permute-start(bf16[128,768]{1,0:T(8,128)(2,1)} %refs_5_.1), channel_id=1, source_target_pairs={{0,12},{1,13},{2,14},{3,15},{4,0},{5,1},{6,2},{7,3},{8,4},{9,5},{1... | collective-permute-start | bytes 589832 | tf_op jit(solution)/shard_map/ppermute | solution.py:290
  20.8 12.5 %collective-permute-start.13 = (bf16[128,768]{1,0:T(8,128)(2,1)}, bf16[128,768]{1,0:T(8,128)(2,1)S(1)}, u32[]{:S(2)}, u32[]{:S(2)}) collective-permute-start(bf16[128,768]{1,0:T(8,128)(2,1)} %refs_5_.1), channel_id=1, source_target_pairs={{0,8},{1,9},{2,10},{3,11},{4,12},{5,13},{6,14},{7,15},{8,0},{9,1},... | collective-permute-start | bytes 589832 | tf_op jit(solution)/shard_map/ppermute | solution.py:290
  20.8 5.2 %collective-permute-start.7 = (bf16[48,896]{1,0:T(8,128)(2,1)S(1)}, bf16[48,896]{1,0:T(8,128)(2,1)S(1)}, u32[]{:S(2)}, u32[]{:S(2)}) collective-permute-start(bf16[48,896]{1,0:T(8,128)(2,1)S(1)} %get-tuple-element.20.refs_0_), channel_id=1, source_target_pairs={{0,2},{1,3},{2,0},{3,1},{4,6},{5,7},{6,4},{7,5},{8,10},{9,11},{10,... | collective-permute-start | bytes 258056 | tf_op jit(solution)/shard_map/ppermute | solution.py:287
  26.0 4.5 %collective-permute-start.8 = (bf16[48,896]{1,0:T(8,128)(2,1)S(1)}, bf16[48,896]{1,0:T(8,128)(2,1)S(1)}, u32[]{:S(2)}, u32[]{:S(2)}) collective-permute-start(bf16[48,896]{1,0:T(8,128)(2,1)S(1)} %collective-permute-done.3.refs_1_), channel_id=1, source_target_pairs={{0,2},{1,3},{2,0},{3,1},{4,6},{5,7},{6,4},{7,5},{8,10},{9,11},{10,... | collective-permute-start | bytes 258056 | tf_op jit(solution)/shard_map/ppermute | solution.py:287
  26.0 0.7 %copy-start.1 = (bf16[128,768]{1,0:T(8,128)(2,1)}, bf16[128,768]{1,0:T(8,128)(2,1)S(1)}, u32[]{:S(2)}) copy-start(bf16[128,768]{1,0:T(8,128)(2,1)S(1)} %collective-permute-done.1.refs_4_) | copy-start | bytes 589828
  26.7 4.7 %collective-permute-start.9 = (bf16[48,896]{1,0:T(8,128)(2,1)S(1)}, bf16[48,896]{1,0:T(8,128)(2,1)S(1)}, u32[]{:S(2)}, u32[]{:S(2)}) collective-permute-start(bf16[48,896]{1,0:T(8,128)(2,1)S(1)} %collective-permute-done.4.refs_2_), channel_id=1, source_target_pairs={{0,2},{1,3},{2,0},{3,1},{4,6},{5,7},{6,4},{7,5},{8,10},{9,11},{10,... | collective-permute-start | bytes 258056 | tf_op jit(solution)/shard_map/ppermute | solution.py:287
  28.7 4.5 %collective-permute-start.10 = (bf16[48,896]{1,0:T(8,128)(2,1)S(1)}, bf16[48,896]{1,0:T(8,128)(2,1)S(1)}, u32[]{:S(2)}, u32[]{:S(2)}) collective-permute-start(bf16[48,896]{1,0:T(8,128)(2,1)S(1)} %collective-permute-done.6.refs_3_), channel_id=1, source_target_pairs={{0,2},{1,3},{2,0},{3,1},{4,6},{5,7},{6,4},{7,5},{8,10},{9,11},{10,... | collective-permute-start | bytes 258056 | tf_op jit(solution)/shard_map/ppermute | solution.py:287
  33.3 2.2 %collective-permute-start.14 = (bf16[384,768]{1,0:T(8,128)(2,1)S(1)}, bf16[384,768]{1,0:T(8,128)(2,1)S(1)}, u32[]{:S(2)}, u32[]{:S(2)}) collective-permute-start(bf16[384,768]{1,0:T(8,128)(2,1)S(1)} %get-tuple-element.27.refs_6_), channel_id=1, source_target_pairs={{0,1},{1,0},{2,3},{3,2},{4,5},{5,4},{6,7},{7,6},{8,9},{9,8},{10,11... | collective-permute-start | bytes 1769480 | tf_op jit(solution)/shard_map/ppermute | solution.py:287
  33.3 7.8 %collective-permute-start.15 = (bf16[128,768]{1,0:T(8,128)(2,1)S(1)}, bf16[128,768]{1,0:T(8,128)(2,1)S(1)}, u32[]{:S(2)}, u32[]{:S(2)}) collective-permute-start(bf16[128,768]{1,0:T(8,128)(2,1)S(1)} %collective-permute-done.13.refs_1_), channel_id=1, source_target_pairs={{0,2},{1,3},{2,0},{3,1},{4,6},{5,7},{6,4},{7,5},{8,10},{9,11},{10,... | collective-permute-start | bytes 589832 | tf_op jit(solution)/shard_map/ppermute | solution.py:287
  34.3 10.5 %collective-permute-start.12 = (bf16[128,768]{1,0:T(8,128)(2,1)S(1)}, bf16[128,768]{1,0:T(8,128)(2,1)S(1)}, u32[]{:S(2)}, u32[]{:S(2)}) collective-permute-start(bf16[128,768]{1,0:T(8,128)(2,1)S(1)} %collective-permute-done.11.refs_3_), channel_id=1, source_target_pairs={{0,2},{1,3},{2,0},{3,1},{4,6},{5,7},{6,4},{7,5},{8,10},{9,11},{10,... | collective-permute-start | bytes 589832 | tf_op jit(solution)/shard_map/ppermute | solution.py:287
  35.4 0.9 %copy-start.2 = (bf16[128,768]{1,0:T(8,128)(2,1)S(1)}, bf16[128,768]{1,0:T(8,128)(2,1)}, u32[]{:S(2)}) copy-start(bf16[128,768]{1,0:T(8,128)(2,1)} %copy-done.1) | copy-start | bytes 589828
  41.1 3.8 %copy-start = (f32[15360]{0:T(1024)S(1)}, f32[15360]{0:T(1024)}, u32[]{:S(2)}) copy-start(f32[15360]{0:T(1024)} %param.18) | copy-start | bytes 184324

commit v5 on v4

--- a/solution.py
+++ b/solution.py
@@ -102,12 +102,6 @@
     )
 
 
-def chip_at(me, shift, across, layers):
-    chip = me // 2
-    layer = (chip // 2 - shift + layers) % layers
-    return 2 * layer + ((chip % 2) ^ across)
-
-
 def masked(ref, length):
     here = ref[...]
     keep = lax.broadcasted_iota(jnp.int32, here.shape, 0).astype(jnp.float32) < length
@@ -149,15 +143,25 @@
         rows_ref[k : k + 1, :] = kept[pl.ds(k * width, width)][None, :]
 
 
+def pile_kernel(*refs):
+    at = 0
+    for ref in refs[:-1]:
+        refs[-1][at : at + ref.shape[0], :] = ref[...]
+        at += ref.shape[0]
+
+
 def pack_kernel(*refs):
-    blocks, out_ref, meta_ref = refs[:-2], refs[-2], refs[-1]
-    rows, width = blocks[0].shape[0], out_ref.shape[1]
+    arrays, out_ref, meta_ref = refs[:-2], refs[-2], refs[-1]
+    rows, width = arrays[0].shape[0], out_ref.shape[1]
     row = lax.broadcasted_iota(jnp.int32, meta_ref.shape, 0)
     tables = jnp.zeros(meta_ref.shape, jnp.float32)
-    for k, ref in enumerate(blocks):
-        out_ref[k * rows : (k + 1) * rows, :] = ref[:, 0:width]
-        table = ref[0:SLOT_ROWS, width:].astype(jnp.float32)
-        tables = jnp.where(row == k, table[0 : len(blocks)], tables)
+    k = 0
+    for ref in arrays:
+        for first in range(0, ref.shape[0], rows):
+            out_ref[k * rows : (k + 1) * rows, :] = ref[first : first + rows, 0:width]
+            table = ref[first : first + SLOT_ROWS, width:].astype(jnp.float32)
+            tables = jnp.where(row == k, table[0 : meta_ref.shape[0]], tables)
+            k += 1
     meta_ref[...] = tables.astype(jnp.int32)
 
 
@@ -171,7 +175,7 @@
     return meta_ref[k : k + 1, TILE - 1 : TILE].astype(jnp.float32)
 
 
-def first_kernel(layers, order, *refs):
+def first_kernel(masks, order, *refs):
     (me_ref, meta_ref), refs = refs[:2], refs[2:]
     docs, refs = refs[: len(order)], refs[len(order) :]
     packed, refs = refs[:2], refs[2:]
@@ -181,9 +185,9 @@
     own_copy = fetch(docs[-1], own, sems.at[1])
     me = me_ref[0]
     core = me % 2
-    rows = weight.shape[0] // (4 * layers)
-    for k in range(2 * layers):
-        chip = chip_at(me, k % layers, k // layers, layers)
+    rows = weight.shape[0] // (2 * len(masks))
+    for k, mask in enumerate(masks):
+        chip = (me // 2) ^ mask
         block = slice(k * rows, (k + 1) * rows)
         at = pl.multiple_of((2 * chip + core) * rows, SLOT_ROWS)
         weight[pl.ds(at, rows), :] = packed[0][block, :]
@@ -193,7 +197,7 @@
     for first in range(0, len(order), 2):
         if first + 2 == len(order):
             own_copy.wait()
-        lengths = [length_of(meta_ref, k) for k in order[first : first + 2]]
+        lengths = [length_of(meta_ref, masks.index(m)) for m in order[first : first + 2]]
         normed = normed_rows(docs[first : first + 2], lengths, weight, params)
         if first == 0:
             mine_copy.wait()
@@ -202,12 +206,12 @@
                 best[first + j : first + j + 1, :] = top
 
 
-def next_kernel(order, *refs):
+def next_kernel(masks, order, *refs):
     meta_ref, refs = refs[0], refs[1:]
     docs, weight, params, refs = refs[:2], refs[2], refs[3], refs[4:]
     mine_ref, theirs_ref, best_refs, mine, sem = refs[0], refs[1], refs[2:4], *refs[4:]
     copy = fetch(mine_ref, mine, sem)
-    lengths = [length_of(meta_ref, k) for k in order]
+    lengths = [length_of(meta_ref, masks.index(m)) for m in order]
     normed = normed_rows(docs, lengths, weight, params)
     copy.wait()
     for w_ref, best in zip((mine, theirs_ref), best_refs):
@@ -215,7 +219,7 @@
             best[j : j + 1, :] = top
 
 
-def last_kernel(layers, orders, *refs):
+def last_kernel(masks, orders, *refs):
     me_ref, table_ref, meta_ref, refs = refs[0], refs[1], refs[2], refs[3:]
     docs, weight, params, refs = refs[:2], refs[2], refs[3], refs[4:]
     mine_ref, theirs_ref, dbias_ref, refs = refs[0], refs[1], refs[2], refs[3:]
@@ -225,9 +229,9 @@
     copy = fetch(mine_ref, mine, sem)
     me = me_ref[0]
     core, chip = me % 2, me // 2
-    devices = 4 * layers
+    devices = 2 * len(masks)
     tiles = 2 * mine_ref.shape[0] // TILE
-    lengths = [length_of(meta_ref, k) for k in orders[-1]]
+    lengths = [length_of(meta_ref, masks.index(m)) for m in orders[-1]]
     normed = normed_rows(docs, lengths, weight, params)
     found = []
     copy.wait()
@@ -237,8 +241,8 @@
     low = jnp.where(core == 0, found[0], found[1])
     high = jnp.where(core == 0, found[1], found[0])
     logits = jnp.concatenate([low, high], axis=1)
-    order = [k for group in orders for k in group]
-    docs_at = [2 * chip_at(me, k % layers, k // layers, layers) + core for k in order]
+    order = [mask for group in orders for mask in group]
+    docs_at = [me ^ (2 * mask) for mask in order]
     bias = dbias_ref[...]
     bias = pltpu.roll(bias, bias.shape[0] - chip * tiles, 0)
     send[...] = jnp.zeros(send.shape, jnp.float32)
@@ -249,10 +253,10 @@
         impacts = jnp.log1p(jnp.maximum(logits[:, lanes] + bias[t : t + 1, :], 0.0))
         impacts = impacts.astype(jnp.bfloat16).astype(jnp.float32)
         blocks = jnp.zeros((BLK_DEV * devices, TILE), jnp.float32)
-        for n, k in enumerate(order):
+        for n, mask in enumerate(order):
             row = impacts[n : n + 1, :]
             send[pl.ds(docs_at[n] * stride + t, 1), :] = row
-            block = table_ref[k, chip * tiles + t]
+            block = table_ref[masks.index(mask), chip * tiles + t]
             blocks = jnp.maximum(blocks, jnp.where(target == block, row, 0.0))
         for s in range(BLK_DEV):
             send[pl.ds((1 + s) * SLOT_ROWS + t, devices, stride=stride), :] = blocks[
@@ -276,18 +280,17 @@
 ):
     devices = lax.axis_size("doc")
     chips = devices // 2
-    layers = chips // 2
     seq, width = hidden_states.shape
     rows = transform_weight.shape[0]
     half = decoder_weight.shape[2]
     tiles = 2 * half // TILE
     me = lax.axis_index("doc").astype(jnp.int32)
 
-    def flip(value, bit):
-        return lax.ppermute(value, "doc", [(i, i ^ bit) for i in range(devices)])
-
-    def shift(value, by):
-        return lax.ppermute(value, "doc", [(i, (i + 4 * by) % devices) for i in range(devices)])
+    def cross(value, mask):
+        return lax.ppermute(value, "doc", [(i, i ^ (2 * mask)) for i in range(devices)])
+
+    def swap(value):
+        return lax.ppermute(value, "doc", [(i, i ^ 1) for i in range(devices)])
 
     smem = pl.BlockSpec(memory_space=pltpu.SMEM)
     vmem = pl.BlockSpec(memory_space=pltpu.VMEM)
@@ -311,8 +314,8 @@
     def after(value, *done):
         return lax.optimization_barrier((value, *done))[0]
 
-    near = {1: shift(hidden_states, 1)}
-    far = {0: flip(hidden_states, 2)}
+    docs = {0: hidden_states, 6: cross(hidden_states, 6), 2: cross(hidden_states, 2)}
+    docs[1] = cross(hidden_states, 1)
     block, params = pl.pallas_call(
         start_kernel,
         out_shape=[
@@ -336,39 +339,49 @@
         stay(norm_gain),
         stay(norm_bias),
     )
-    blocks = [block]
-    for by in range(1, layers):
-        blocks.append(shift(after(block, far[0]) if by > 2 else block, by))
     weight_rows = jnp.swapaxes(decoder_weight[0], 0, 1)
-    theirs = flip(weight_rows, 1)
-    blocks += [flip(after(value, near[1]) if k > 1 else value, 2) for k, value in enumerate(blocks)]
-    for by in range(2, layers):
-        near[by] = shift(after(hidden_states, blocks[by - 1]), by)
-    for by in range(1, layers):
-        far[by] = flip(near[by], 2)
-    blocks[0] = after(block, far[1], theirs)
+    theirs = swap(weight_rows)
+
+    def pile(*values):
+        total = sum(value.shape[0] for value in values)
+        return pl.pallas_call(
+            pile_kernel,
+            out_shape=shape((total, values[0].shape[1]), values[0].dtype),
+            in_specs=[vmem] * len(values),
+            out_specs=vmem,
+            compiler_params=limit,
+        )(*values)
+
+    block_6 = cross(block, 6)
+    block_2 = cross(after(block, docs[1]), 2)
+    block_4 = cross(after(block_6, docs[2]), 2)
+    docs[4] = cross(docs[6], 2)
+    docs[3] = cross(docs[2], 1)
+    docs[7] = cross(docs[6], 1)
+    docs[5] = cross(docs[4], 1)
+    near_pile = cross(pile(block, block_2), 1)
+    far_pile = cross(pile(block_6, block_4), 1)
+    masks = [0, 2, 6, 4, 1, 3, 7, 5]
     packed, meta = pl.pallas_call(
         pack_kernel,
         out_shape=[
             shape((chips * rows, width), jnp.bfloat16),
             shape((chips, TILE), jnp.int32),
         ],
-        in_specs=[vmem] * chips,
+        in_specs=[vmem] * 6,
         out_specs=[vmem] * 2,
         compiler_params=limit,
-    )(*blocks)
-    other_packed = flip(after(packed, *near.values()), 1)
-
-    orders = [[1, layers, layers + 1, 0]]
-    orders += [[by, layers + by] for by in range(2, layers)]
-    arrived = {layers + by: value for by, value in far.items()} | near
+    )(after(block, docs[4], docs[3], theirs), block_2, block_6, block_4, near_pile, far_pile)
+    other_packed = swap(after(packed, docs[7]))
+
+    orders = [[2, 1, 3, 0], [6, 7], [4, 5]]
     where = me[None]
     halves = (stay(weight_rows), theirs)
     slot = pltpu.VMEM((half, width), jnp.bfloat16)
     best_shape = shape((8, half), jnp.float32)
-    first_docs = [arrived[k] for k in orders[0][:-1]]
+    first_docs = [docs[mask] for mask in orders[0][:-1]]
     *best, weight = pl.pallas_call(
-        lambda *refs: first_kernel(layers, orders[0], *refs),
+        lambda *refs: first_kernel(masks, orders[0], *refs),
         out_shape=[best_shape, best_shape, shape((width, width), jnp.bfloat16)],
         in_specs=[smem] + [vmem] * len(orders[0]) + [hbm] + [vmem] * 3 + [hbm, vmem],
         out_specs=[vmem] * 3,
@@ -382,16 +395,16 @@
     )(where, meta, *first_docs, stay(hidden_states), packed, other_packed, params, *halves)
     for order in orders[1:-1]:
         best += pl.pallas_call(
-            lambda *refs, order=order: next_kernel(order, *refs),
+            lambda *refs, order=order: next_kernel(masks, order, *refs),
             out_shape=[best_shape] * 2,
             in_specs=[vmem] * 5 + [hbm, vmem],
             out_specs=[vmem] * 2,
             scratch_shapes=[slot, pltpu.SemaphoreType.DMA],
             compiler_params=limit,
             cost_estimate=cost(2),
-        )(meta, *[arrived[k] for k in order], weight, params, *halves)
+        )(meta, *[docs[mask] for mask in order], weight, params, *halves)
     send = pl.pallas_call(
-        lambda *refs: last_kernel(layers, orders, *refs),
+        lambda *refs: last_kernel(masks, orders, *refs),
         out_shape=shape((devices, (1 + BLK_DEV) * SLOT_ROWS, TILE), jnp.bfloat16),
         in_specs=[smem] * 2 + [vmem] * 5 + [hbm] + [vmem] * (2 + len(best)),
         out_specs=vmem,
@@ -406,7 +419,7 @@
         where,
         meta,
         meta,
-        *[arrived[k] for k in orders[-1]],
+        *[docs[mask] for mask in orders[-1]],
         weight,
         params,
         *halves,
@@ -420,8 +433,7 @@
 
 
 def tokens_move(mesh):
-    devices = mesh.shape["doc"]
-    return mesh.shape["term"] == 1 and devices >= 8 and devices & (devices - 1) == 0
+    return mesh.shape["term"] == 1 and mesh.shape["doc"] == 16
 
 
 def solution(mesh):

time: 65.2 us -> 70.1 us (1.075)
  starting transfers between devices: 17.5 us -> 20.3 us
  waiting for transfers between devices: 15.2 us -> 16.3 us
  local copies, waits for them, and re-layouts: 2.92 us -> 3.86 us
    ppermute x16 -> x14, starting transfers between devices: 17.5 us -> 20.3 us  [the longest x12 19.7 us: cross(): lax.ppermute(value, 'doc', [(i, i ^ 2 * mask) for i in range(devices)])]
    ppermute x16 -> x14, waiting for transfers between devices: 15.2 us -> 16.3 us  [the longest x12 15.7 us: cross(): lax.ppermute(value, 'doc', [(i, i ^ 2 * mask) for i in range(devices)])]
    unnamed x6 -> x10, local copies, waits for them, and re-layouts: 1.6 us -> 2.53 us
    pallas_call x3 -> x5, Pallas kernels: 11.7 us -> 11.6 us  [the longest x1 4.31 us: move_tokens(): pl.pallas_call(lambda *refs: first_kernel(masks, orders[0], *refs), out_s...]
  transfers between devices with their start and end apart: 16 -> 14, of which waited for: 8 -> 7; matrix products, arithmetic and copies ran while one was open for 0% -> 0% of each run, Pallas kernels for 14% -> 13%
where the time goes in v5:
time: 70.1 us; the launch traced here: 69.7 us
  starting transfers between devices  20.3 us (29%)
  waiting for transfers between devices  16.3 us (23%)
  blocking collectives  14.6 us (21%)
  Pallas kernels  13.3 us (19%)
  local copies, waits for them, and re-layouts  3.86 us (6%)
  between operations  1.43 us (2%)
    ppermute x12, starting transfers between devices, cross(): lax.ppermute(value, 'doc', [(i, i ^ 2 * mask) for i in range(devices)])  19.7 us
    ppermute x12, waiting for transfers between devices, cross(): lax.ppermute(value, 'doc', [(i, i ^ 2 * mask) for i in range(devices)])  15.7 us
    all_to_all x1, blocking collectives, move_tokens(): got = lax.all_to_all(send, 'doc', split_axis=0, concat_axis=0, tiled=True)  14.6 us
    pallas_call x1, Pallas kernels, move_tokens(): pl.pallas_call(lambda *refs: first_kernel(masks, orders[0], *refs), out_s...  4.31 us
    pallas_call x1, Pallas kernels, move_tokens(): pl.pallas_call(lambda *refs: last_kernel(masks, orders, *refs), out_shape...  4.1 us
    pallas_call x1, Pallas kernels, move_tokens(): pl.pallas_call(lambda *refs, order=order: next_kernel(masks, order, *refs...  3.17 us
    unnamed x10, local copies, waits for them, and re-layouts  2.53 us
    pallas_call x1, Pallas kernels, move_tokens(): pl.pallas_call(start_kernel, out_shape=[shape((rows, width + TILE), jnp.b...  1.61 us
  transfers between devices with their start and end apart: 14, of which 7 were waited for; matrix products, arithmetic and copies ran while one was open for 0% of the time, Pallas kernels for 13%

profile of v5, /device:TPU:0, one launch (start us, length us, event | category | flops | bytes accessed | tf_op | source)
XLA Modules:
  0.0 69.7 jit_solution(1728423052040202382)
XLA Ops:
  0.6 0.5 collective-permute-start.4
  1.2 4.7 %collective-permute-start = (bf16[128,768]{1,0:T(8,128)(2,1)}, bf16[128,768]{1,0:T(8,128)(2,1)S(1)}, u32[]{:S(2)}, u32[]{:S(2)}) collective-permute-start(bf16[128,768]{1,0:T(8,128)(2,1)} %refs_5_.1), channel_id=1, source_target_pairs={{0,12},{1,13},{2,14},{3,15},{4,8},{5,9},{6,10},{7,11},{8,4},{9,5},... | collective-permute-start | bytes 589832 | tf_op jit(solution)/shard_map/ppermute | solution.py:290
  5.8 0.0 collective-permute-start.2
  5.8 1.5 %collective-permute-start.5 = (bf16[128,768]{1,0:T(8,128)(2,1)}, bf16[128,768]{1,0:T(8,128)(2,1)S(1)}, u32[]{:S(2)}, u32[]{:S(2)}) collective-permute-start(bf16[128,768]{1,0:T(8,128)(2,1)} %refs_5_.1), channel_id=1, source_target_pairs={{0,2},{1,3},{2,0},{3,1},{4,6},{5,7},{6,4},{7,5},{8,10},{9,11},{10,... | collective-permute-start | bytes 589832 | tf_op jit(solution)/shard_map/ppermute | solution.py:290
  8.0 1.6 %shard_map.122 = (bf16[48,896]{1,0:T(8,128)(2,1)S(1)}, f32[8,768]{1,0:T(8,128)S(1)}) custom-call(s32[1,1,32]{2,1,0:T(1,128)} %tiles_ref.1, s32[1,1,32]{2,1,0:T(1,128)} %bitcast.17, s32[1,1,32]{2,1,0:T(1,128)} %slots_ref.1, s32[1]{0:T(128)S(6)} %copy.22.length_ref, bf16[48,768]{1,0:T(8,128)(2,1)} %refs_0_.1, f32[768]{0:T(1024)} %refs_1_.1, f32[768]{0:T(1024)} %refs_2_.1, ...), custom_call_target="tpu_custom_call" | custom-call | tf_op jit(solution)/shard_map/pallas_call | solution.py:319
  9.6 1.0 %collective-permute-start.7 = (bf16[48,896]{1,0:T(8,128)(2,1)S(1)}, bf16[48,896]{1,0:T(8,128)(2,1)S(1)}, u32[]{:S(2)}, u32[]{:S(2)}) collective-permute-start(bf16[48,896]{1,0:T(8,128)(2,1)S(1)} %get-tuple-element.17.refs_0_), channel_id=1, source_target_pairs={{0,12},{1,13},{2,14},{3,15},{4,8},{5,9},{6,10},{7,11},{8,4},{9,5},... | collective-permute-start | bytes 258056 | tf_op jit(solution)/shard_map/ppermute | solution.py:290
  10.6 1.3 %collective-permute-done.refs_1_ = bf16[128,768]{1,0:T(8,128)(2,1)S(1)} collective-permute-done((bf16[128,768]{1,0:T(8,128)(2,1)}, bf16[128,768]{1,0:T(8,128)(2,1)S(1)}, u32[]{:S(2)}, u32[]{:S(2)}) %collective-permute-start) | collective-permute-done | bytes 196640 | tf_op jit(solution)/shard_map/ppermute | solution.py:290
  11.9 4.1 %collective-permute-start.1 = (bf16[128,768]{1,0:T(8,128)(2,1)S(1)}, bf16[128,768]{1,0:T(8,128)(2,1)S(1)}, u32[]{:S(2)}, u32[]{:S(2)}) collective-permute-start(bf16[128,768]{1,0:T(8,128)(2,1)S(1)} %collective-permute-done.refs_1_), channel_id=1, source_target_pairs={{0,4},{1,5},{2,6},{3,7},{4,0},{5,1},{6,2},{7,3},{8,12},{9,13},{10,... | collective-permute-start | bytes 589832 | tf_op jit(solution)/shard_map/ppermute | solution.py:290
  15.9 1.9 %collective-permute-done.7.refs_0_.refs_2_ = bf16[48,896]{1,0:T(8,128)(2,1)S(1)} collective-permute-done((bf16[48,896]{1,0:T(8,128)(2,1)S(1)}, bf16[48,896]{1,0:T(8,128)(2,1)S(1)}, u32[]{:S(2)}, u32[]{:S(2)}) %collective-permute-start.7) | collective-permute-done | bytes 86048 | tf_op jit(solution)/shard_map/ppermute | solution.py:290
  17.8 0.0 collective-permute-done.2.refs_2_
  17.8 1.4 %collective-permute-start.8 = (bf16[48,896]{1,0:T(8,128)(2,1)S(1)}, bf16[48,896]{1,0:T(8,128)(2,1)S(1)}, u32[]{:S(2)}, u32[]{:S(2)}) collective-permute-start(bf16[48,896]{1,0:T(8,128)(2,1)S(1)} %collective-permute-done.7.refs_0_.refs_2_), channel_id=1, source_target_pairs={{0,4},{1,5},{2,6},{3,7},{4,0},{5,1},{6,2},{7,3},{8,12},{9,13},{10,... | collective-permute-start | bytes 258056 | tf_op jit(solution)/shard_map/ppermute | solution.py:290
  19.2 0.0 collective-permute-done.5.refs_3_
  19.2 0.0 copy-start.1
  19.2 0.7 copy-done.1
  19.8 0.7 collective-permute-start.6
  20.5 1.5 %collective-permute-start.3 = (bf16[128,768]{1,0:T(8,128)(2,1)S(1)}, bf16[128,768]{1,0:T(8,128)(2,1)S(1)}, u32[]{:S(2)}, u32[]{:S(2)}) collective-permute-start(bf16[128,768]{1,0:T(8,128)(2,1)S(1)} %collective-permute-done.2.refs_2_), channel_id=1, source_target_pairs={{0,2},{1,3},{2,0},{3,1},{4,6},{5,7},{6,4},{7,5},{8,10},{9,11},{10,... | collective-permute-start | bytes 589832 | tf_op jit(solution)/shard_map/ppermute | solution.py:290
  22.0 1.9 %collective-permute-done.8.refs_1_.refs_3_ = bf16[48,896]{1,0:T(8,128)(2,1)S(1)} collective-permute-done((bf16[48,896]{1,0:T(8,128)(2,1)S(1)}, bf16[48,896]{1,0:T(8,128)(2,1)S(1)}, u32[]{:S(2)}, u32[]{:S(2)}) %collective-permute-start.8) | collective-permute-done | bytes 86048 | tf_op jit(solution)/shard_map/ppermute | solution.py:290
  23.9 1.5 %collective-permute-start.12 = (bf16[128,768]{1,0:T(8,128)(2,1)S(1)}, bf16[128,768]{1,0:T(8,128)(2,1)S(1)}, u32[]{:S(2)}, u32[]{:S(2)}) collective-permute-start(bf16[128,768]{1,0:T(8,128)(2,1)S(1)} %collective-permute-done.refs_1_), channel_id=1, source_target_pairs={{0,2},{1,3},{2,0},{3,1},{4,6},{5,7},{6,4},{7,5},{8,10},{9,11},{10,... | collective-permute-start | bytes 589832 | tf_op jit(solution)/shard_map/ppermute | solution.py:290
  25.4 0.2 collective-permute-done.6.refs_1_
  25.6 1.5 %collective-permute-start.10 = (bf16[96,896]{1,0:T(8,128)(2,1)S(1)}, bf16[96,896]{1,0:T(8,128)(2,1)S(1)}, u32[]{:S(2)}, u32[]{:S(2)}) collective-permute-start(bf16[96,896]{1,0:T(8,128)(2,1)S(1)} %shard_map.124), channel_id=1, source_target_pairs={{0,2},{1,3},{2,0},{3,1},{4,6},{5,7},{6,4},{7,5},{8,10},{9,11},{10,... | collective-permute-start | bytes 516104 | tf_op jit(solution)/shard_map/ppermute | solution.py:290
  27.1 0.0 collective-permute-done.1.refs_3_
  27.1 0.6 collective-permute-start.9
  27.7 0.0 collective-permute-done.3.refs_4_
  27.7 0.0 copy-start.3
  27.7 0.0 collective-permute-done.4.refs_10_.refs_6_.refs_8_
  27.7 7.7 %collective-permute-done.10.refs_5_ = bf16[96,896]{1,0:T(8,128)(2,1)S(1)} collective-permute-done((bf16[96,896]{1,0:T(8,128)(2,1)S(1)}, bf16[96,896]{1,0:T(8,128)(2,1)S(1)}, u32[]{:S(2)}, u32[]{:S(2)}) %collective-permute-start.10) | collective-permute-done | bytes 172064 | tf_op jit(solution)/shard_map/ppermute | solution.py:290
  35.4 2.7 %collective-permute-done.9.refs_4_ = bf16[96,896]{1,0:T(8,128)(2,1)S(1)} collective-permute-done((bf16[96,896]{1,0:T(8,128)(2,1)S(1)}, bf16[96,896]{1,0:T(8,128)(2,1)S(1)}, u32[]{:S(2)}, u32[]{:S(2)}) %collective-permute-start.9) | collective-permute-done | bytes 172064 | tf_op jit(solution)/shard_map/ppermute | solution.py:290
  38.1 0.0 collective-permute-done.12.refs_2_
  38.1 0.0 copy-done.3
  38.1 0.1 collective-permute-start.13
  38.2 1.4 %collective-permute-start.11 = (bf16[128,768]{1,0:T(8,128)(2,1)S(1)}, bf16[128,768]{1,0:T(8,128)(2,1)S(1)}, u32[]{:S(2)}, u32[]{:S(2)}) collective-permute-start(bf16[128,768]{1,0:T(8,128)(2,1)S(1)} %collective-permute-done.1.refs_3_), channel_id=1, source_target_pairs={{0,2},{1,3},{2,0},{3,1},{4,6},{5,7},{6,4},{7,5},{8,10},{9,11},{10,... | collective-permute-start | bytes 589832 | tf_op jit(solution)/shard_map/ppermute | solution.py:290
  39.6 0.6 collective-permute-done.13.refs_7_
  40.2 0.0 copy-start.2
  40.2 0.9 %copy-done.2 = bf16[128,768]{1,0:T(8,128)(2,1)S(1)} copy-done((bf16[128,768]{1,0:T(8,128)(2,1)S(1)}, bf16[128,768]{1,0:T(8,128)(2,1)}, u32[]{:S(2)}) %copy-start.2) | copy-done | bytes 196632
  41.1 0.0 copy-start.4
  41.1 0.9 %copy-done.4 = bf16[128,768]{1,0:T(8,128)(2,1)S(1)} copy-done((bf16[128,768]{1,0:T(8,128)(2,1)S(1)}, bf16[128,768]{1,0:T(8,128)(2,1)}, u32[]{:S(2)}) %copy-start.4) | copy-done | bytes 196632
  42.1 4.3 %shard_map.126 = (f32[8,960]{1,0:T(8,128)S(1)}, f32[8,960]{1,0:T(8,128)S(1)}, bf16[768,768]{1,0:T(8,128)(2,1)S(1)}) custom-call(s32[1]{0:T(128)} %bitcast.refs_0_, s32[8,128]{1,0:T(8,128)S(1)} %get-tuple-element.19.refs_1_.refs_0_.refs_2_, bf16[128,768]{1,0:T(8,128)(2,1)S(1)} %collective-permute-done.2.refs_2_, bf16[128,768]{1,0:T(8,128)(2,1)S(1)} %copy-done.2, ...), custom_call_target="tpu_custom_call" | custom-call | flops 2113929216 | bytes 1048576 | tf_op jit(solution)/shard_map/pallas_call | solution.py:383
  46.4 0.0 copy-start
  46.4 3.2 %shard_map.127 = (f32[8,960]{1,0:T(8,128)S(1)}, f32[8,960]{1,0:T(8,128)S(1)}) custom-call(s32[8,128]{1,0:T(8,128)S(1)} %get-tuple-element.19.refs_1_.refs_0_.refs_2_, bf16[128,768]{1,0:T(8,128)(2,1)S(1)} %collective-permute-done.refs_1_, bf16[128,768]{1,0:T(8,128)(2,1)S(1)} %collective-permute-done.12.refs_2_, ...), custom_call_target="tpu_custom_call" | custom-call | flops 1056964608 | bytes 1048576 | tf_op jit(solution)/shard_map/pallas_call | solution.py:397
  49.6 0.0 collective-permute-done.11.refs_4_
  49.6 0.0 copy-done
  49.6 4.1 %shard_map.128 = bf16[16,48,128]{2,1,0:T(8,128)(2,1)S(1)} custom-call(s32[1]{0:T(128)} %bitcast.refs_0_, s32[8,128]{1,0:T(8,128)S(1)} %get-tuple-element.19.refs_1_.refs_0_.refs_2_, s32[8,128]{1,0:T(8,128)S(1)} %get-tuple-element.19.refs_1_.refs_0_.refs_2_, bf16[128,768]{1,0:T(8,128)(2,1)S(1)} %collective-permute-done.1.refs_3_, ...), custom_call_target="tpu_custom_call" | custom-call | flops 1056964608 | bytes 1048576 | tf_op jit(solution)/shard_map/pallas_call | solution.py:406
  53.7 14.6 %all_to_all.5 = bf16[16,48,128]{2,1,0:T(8,128)(2,1)S(1)} all-to-all(bf16[16,48,128]{2,1,0:T(8,128)(2,1)S(1)} %shard_map.128), channel_id=1, replica_groups=mesh['groups'=2,'doc'=16,'term'=1] {'doc'}, dimensions={0} | all-to-all | bytes 393216 | tf_op jit(solution)/shard_map/all_to_all | solution.py:429
  68.4 0.7 slice.26
  69.1 0.6 slice.24
  (7 shorter events, 0.1 us)
Async XLA Ops:
  0.6 27.1 %collective-permute-start.4 = (bf16[960,768]{1,0:T(8,128)(2,1)}, bf16[960,768]{1,0:T(8,128)(2,1)S(1)}, u32[]{:S(2)}, u32[]{:S(2)}) collective-permute-start(bf16[960,768]{1,0:T(8,128)(2,1)} %bitcast.12), channel_id=1, source_target_pairs={{0,1},{1,0},{2,3},{3,2},{4,5},{5,4},{6,7},{7,6},{8,9},{9,8},{10,11... | collective-permute-start | bytes 4423688 | tf_op jit(solution)/shard_map/ppermute | solution.py:293
  1.2 10.7 %collective-permute-start = (bf16[128,768]{1,0:T(8,128)(2,1)}, bf16[128,768]{1,0:T(8,128)(2,1)S(1)}, u32[]{:S(2)}, u32[]{:S(2)}) collective-permute-start(bf16[128,768]{1,0:T(8,128)(2,1)} %refs_5_.1), channel_id=1, source_target_pairs={{0,12},{1,13},{2,14},{3,15},{4,8},{5,9},{6,10},{7,11},{8,4},{9,5},... | collective-permute-start | bytes 589832 | tf_op jit(solution)/shard_map/ppermute | solution.py:290
  5.8 12.0 %collective-permute-start.2 = (bf16[128,768]{1,0:T(8,128)(2,1)}, bf16[128,768]{1,0:T(8,128)(2,1)S(1)}, u32[]{:S(2)}, u32[]{:S(2)}) collective-permute-start(bf16[128,768]{1,0:T(8,128)(2,1)} %refs_5_.1), channel_id=1, source_target_pairs={{0,4},{1,5},{2,6},{3,7},{4,0},{5,1},{6,2},{7,3},{8,12},{9,13},{10,... | collective-permute-start | bytes 589832 | tf_op jit(solution)/shard_map/ppermute | solution.py:290
  5.8 13.3 %collective-permute-start.5 = (bf16[128,768]{1,0:T(8,128)(2,1)}, bf16[128,768]{1,0:T(8,128)(2,1)S(1)}, u32[]{:S(2)}, u32[]{:S(2)}) collective-permute-start(bf16[128,768]{1,0:T(8,128)(2,1)} %refs_5_.1), channel_id=1, source_target_pairs={{0,2},{1,3},{2,0},{3,1},{4,6},{5,7},{6,4},{7,5},{8,10},{9,11},{10,... | collective-permute-start | bytes 589832 | tf_op jit(solution)/shard_map/ppermute | solution.py:290
  9.6 8.2 %collective-permute-start.7 = (bf16[48,896]{1,0:T(8,128)(2,1)S(1)}, bf16[48,896]{1,0:T(8,128)(2,1)S(1)}, u32[]{:S(2)}, u32[]{:S(2)}) collective-permute-start(bf16[48,896]{1,0:T(8,128)(2,1)S(1)} %get-tuple-element.17.refs_0_), channel_id=1, source_target_pairs={{0,12},{1,13},{2,14},{3,15},{4,8},{5,9},{6,10},{7,11},{8,4},{9,5},... | collective-permute-start | bytes 258056 | tf_op jit(solution)/shard_map/ppermute | solution.py:290
  11.9 15.2 %collective-permute-start.1 = (bf16[128,768]{1,0:T(8,128)(2,1)S(1)}, bf16[128,768]{1,0:T(8,128)(2,1)S(1)}, u32[]{:S(2)}, u32[]{:S(2)}) collective-permute-start(bf16[128,768]{1,0:T(8,128)(2,1)S(1)} %collective-permute-done.refs_1_), channel_id=1, source_target_pairs={{0,4},{1,5},{2,6},{3,7},{4,0},{5,1},{6,2},{7,3},{8,12},{9,13},{10,... | collective-permute-start | bytes 589832 | tf_op jit(solution)/shard_map/ppermute | solution.py:290
  17.8 6.1 %collective-permute-start.8 = (bf16[48,896]{1,0:T(8,128)(2,1)S(1)}, bf16[48,896]{1,0:T(8,128)(2,1)S(1)}, u32[]{:S(2)}, u32[]{:S(2)}) collective-permute-start(bf16[48,896]{1,0:T(8,128)(2,1)S(1)} %collective-permute-done.7.refs_0_.refs_2_), channel_id=1, source_target_pairs={{0,4},{1,5},{2,6},{3,7},{4,0},{5,1},{6,2},{7,3},{8,12},{9,13},{10,... | collective-permute-start | bytes 258056 | tf_op jit(solution)/shard_map/ppermute | solution.py:290
  19.2 0.7 copy-start.1
  19.8 5.7 %collective-permute-start.6 = (bf16[48,896]{1,0:T(8,128)(2,1)S(1)}, bf16[48,896]{1,0:T(8,128)(2,1)S(1)}, u32[]{:S(2)}, u32[]{:S(2)}) collective-permute-start(bf16[48,896]{1,0:T(8,128)(2,1)S(1)} %get-tuple-element.17.refs_0_), channel_id=1, source_target_pairs={{0,4},{1,5},{2,6},{3,7},{4,0},{5,1},{6,2},{7,3},{8,12},{9,13},{10,... | collective-permute-start | bytes 258056 | tf_op jit(solution)/shard_map/ppermute | solution.py:290
  20.5 7.2 %collective-permute-start.3 = (bf16[128,768]{1,0:T(8,128)(2,1)S(1)}, bf16[128,768]{1,0:T(8,128)(2,1)S(1)}, u32[]{:S(2)}, u32[]{:S(2)}) collective-permute-start(bf16[128,768]{1,0:T(8,128)(2,1)S(1)} %collective-permute-done.2.refs_2_), channel_id=1, source_target_pairs={{0,2},{1,3},{2,0},{3,1},{4,6},{5,7},{6,4},{7,5},{8,10},{9,11},{10,... | collective-permute-start | bytes 589832 | tf_op jit(solution)/shard_map/ppermute | solution.py:290
  23.9 14.2 %collective-permute-start.12 = (bf16[128,768]{1,0:T(8,128)(2,1)S(1)}, bf16[128,768]{1,0:T(8,128)(2,1)S(1)}, u32[]{:S(2)}, u32[]{:S(2)}) collective-permute-start(bf16[128,768]{1,0:T(8,128)(2,1)S(1)} %collective-permute-done.refs_1_), channel_id=1, source_target_pairs={{0,2},{1,3},{2,0},{3,1},{4,6},{5,7},{6,4},{7,5},{8,10},{9,11},{10,... | collective-permute-start | bytes 589832 | tf_op jit(solution)/shard_map/ppermute | solution.py:290
  25.6 9.8 %collective-permute-start.10 = (bf16[96,896]{1,0:T(8,128)(2,1)S(1)}, bf16[96,896]{1,0:T(8,128)(2,1)S(1)}, u32[]{:S(2)}, u32[]{:S(2)}) collective-permute-start(bf16[96,896]{1,0:T(8,128)(2,1)S(1)} %shard_map.124), channel_id=1, source_target_pairs={{0,2},{1,3},{2,0},{3,1},{4,6},{5,7},{6,4},{7,5},{8,10},{9,11},{10,... | collective-permute-start | bytes 516104 | tf_op jit(solution)/shard_map/ppermute | solution.py:290
  27.1 11.0 %collective-permute-start.9 = (bf16[96,896]{1,0:T(8,128)(2,1)S(1)}, bf16[96,896]{1,0:T(8,128)(2,1)S(1)}, u32[]{:S(2)}, u32[]{:S(2)}) collective-permute-start(bf16[96,896]{1,0:T(8,128)(2,1)S(1)} %shard_map.123), channel_id=1, source_target_pairs={{0,2},{1,3},{2,0},{3,1},{4,6},{5,7},{6,4},{7,5},{8,10},{9,11},{10,... | collective-permute-start | bytes 516104 | tf_op jit(solution)/shard_map/ppermute | solution.py:290
  27.7 10.4 %copy-start.3 = (bf16[128,768]{1,0:T(8,128)(2,1)}, bf16[128,768]{1,0:T(8,128)(2,1)S(1)}, u32[]{:S(2)}) copy-start(bf16[128,768]{1,0:T(8,128)(2,1)S(1)} %collective-permute-done.3.refs_4_) | copy-start | bytes 589828
  38.1 2.1 %collective-permute-start.13 = (bf16[384,768]{1,0:T(8,128)(2,1)S(1)}, bf16[384,768]{1,0:T(8,128)(2,1)S(1)}, u32[]{:S(2)}, u32[]{:S(2)}) collective-permute-start(bf16[384,768]{1,0:T(8,128)(2,1)S(1)} %get-tuple-element.21.refs_6_), channel_id=1, source_target_pairs={{0,1},{1,0},{2,3},{3,2},{4,5},{5,4},{6,7},{7,6},{8,9},{9,8},{10,11... | collective-permute-start | bytes 1769480 | tf_op jit(solution)/shard_map/ppermute | solution.py:293
  38.2 11.4 %collective-permute-start.11 = (bf16[128,768]{1,0:T(8,128)(2,1)S(1)}, bf16[128,768]{1,0:T(8,128)(2,1)S(1)}, u32[]{:S(2)}, u32[]{:S(2)}) collective-permute-start(bf16[128,768]{1,0:T(8,128)(2,1)S(1)} %collective-permute-done.1.refs_3_), channel_id=1, source_target_pairs={{0,2},{1,3},{2,0},{3,1},{4,6},{5,7},{6,4},{7,5},{8,10},{9,11},{10,... | collective-permute-start | bytes 589832 | tf_op jit(solution)/shard_map/ppermute | solution.py:290
  40.2 0.9 %copy-start.2 = (bf16[128,768]{1,0:T(8,128)(2,1)S(1)}, bf16[128,768]{1,0:T(8,128)(2,1)}, u32[]{:S(2)}) copy-start(bf16[128,768]{1,0:T(8,128)(2,1)} %copy-done.1) | copy-start | bytes 589828
  41.1 0.9 %copy-start.4 = (bf16[128,768]{1,0:T(8,128)(2,1)S(1)}, bf16[128,768]{1,0:T(8,128)(2,1)}, u32[]{:S(2)}) copy-start(bf16[128,768]{1,0:T(8,128)(2,1)} %copy-done.3) | copy-start | bytes 589828
  46.4 3.2 %copy-start = (f32[15360]{0:T(1024)S(1)}, f32[15360]{0:T(1024)}, u32[]{:S(2)}) copy-start(f32[15360]{0:T(1024)} %param.18) | copy-start | bytes 184324

commit v6 on v5

--- a/solution.py
+++ b/solution.py
@@ -180,9 +180,9 @@
     docs, refs = refs[: len(order)], refs[len(order) :]
     packed, refs = refs[:2], refs[2:]
     params, mine_ref, theirs_ref, refs = refs[0], refs[1], refs[2], refs[3:]
-    best_refs, weight, mine, own, sems = refs[:2], refs[2], *refs[3:]
+    best_refs, weight, mine, late, sems = refs[:2], refs[2], *refs[3:]
     mine_copy = fetch(mine_ref, mine, sems.at[0])
-    own_copy = fetch(docs[-1], own, sems.at[1])
+    late_copies = [fetch(docs[k - 2], late.at[k], sems.at[1 + k]) for k in range(2)]
     me = me_ref[0]
     core = me % 2
     rows = weight.shape[0] // (2 * len(masks))
@@ -193,10 +193,11 @@
         weight[pl.ds(at, rows), :] = packed[0][block, :]
         at = pl.multiple_of((2 * chip + 1 - core) * rows, SLOT_ROWS)
         weight[pl.ds(at, rows), :] = packed[1][block, :]
-    docs = [*docs[:-1], own]
+    docs = [*docs[:-2], late.at[0], late.at[1]]
     for first in range(0, len(order), 2):
         if first + 2 == len(order):
-            own_copy.wait()
+            for copy in late_copies:
+                copy.wait()
         lengths = [length_of(meta_ref, masks.index(m)) for m in order[first : first + 2]]
         normed = normed_rows(docs[first : first + 2], lengths, weight, params)
         if first == 0:
@@ -314,8 +315,6 @@
     def after(value, *done):
         return lax.optimization_barrier((value, *done))[0]
 
-    docs = {0: hidden_states, 6: cross(hidden_states, 6), 2: cross(hidden_states, 2)}
-    docs[1] = cross(hidden_states, 1)
     block, params = pl.pallas_call(
         start_kernel,
         out_shape=[
@@ -339,9 +338,6 @@
         stay(norm_gain),
         stay(norm_bias),
     )
-    weight_rows = jnp.swapaxes(decoder_weight[0], 0, 1)
-    theirs = swap(weight_rows)
-
     def pile(*values):
         total = sum(value.shape[0] for value in values)
         return pl.pallas_call(
@@ -353,14 +349,18 @@
         )(*values)
 
     block_6 = cross(block, 6)
-    block_2 = cross(after(block, docs[1]), 2)
-    block_4 = cross(after(block_6, docs[2]), 2)
+    block_2 = cross(block, 2)
+    docs = {0: hidden_states, 1: cross(hidden_states, 1), 2: cross(hidden_states, 2)}
+    near_pile = cross(pile(block, block_2), 1)
+    block_4 = cross(block_6, 2)
+    docs[6] = cross(after(hidden_states, block_6), 6)
+    docs[3] = cross(docs[2], 1)
+    far_pile = cross(pile(block_6, after(block_4, docs[1], docs[2])), 1)
     docs[4] = cross(docs[6], 2)
-    docs[3] = cross(docs[2], 1)
     docs[7] = cross(docs[6], 1)
     docs[5] = cross(docs[4], 1)
-    near_pile = cross(pile(block, block_2), 1)
-    far_pile = cross(pile(block_6, block_4), 1)
+    weight_rows = jnp.swapaxes(decoder_weight[0], 0, 1)
+    theirs = swap(after(weight_rows, block_6, block_2))
     masks = [0, 2, 6, 4, 1, 3, 7, 5]
     packed, meta = pl.pallas_call(
         pack_kernel,
@@ -371,28 +371,27 @@
         in_specs=[vmem] * 6,
         out_specs=[vmem] * 2,
         compiler_params=limit,
-    )(after(block, docs[4], docs[3], theirs), block_2, block_6, block_4, near_pile, far_pile)
-    other_packed = swap(after(packed, docs[7]))
-
-    orders = [[2, 1, 3, 0], [6, 7], [4, 5]]
+    )(after(block, docs[6]), block_2, block_6, block_4, near_pile, far_pile)
+    other_packed = swap(after(packed, docs[3], docs[4]))
+
+    orders = [[2, 3, 1, 0], [6, 7], [4, 5]]
     where = me[None]
     halves = (stay(weight_rows), theirs)
     slot = pltpu.VMEM((half, width), jnp.bfloat16)
     best_shape = shape((8, half), jnp.float32)
-    first_docs = [docs[mask] for mask in orders[0][:-1]]
     *best, weight = pl.pallas_call(
         lambda *refs: first_kernel(masks, orders[0], *refs),
         out_shape=[best_shape, best_shape, shape((width, width), jnp.bfloat16)],
-        in_specs=[smem] + [vmem] * len(orders[0]) + [hbm] + [vmem] * 3 + [hbm, vmem],
+        in_specs=[smem] + [vmem] * 3 + [hbm] * 2 + [vmem] * 3 + [hbm, vmem],
         out_specs=[vmem] * 3,
         scratch_shapes=[
             slot,
-            pltpu.VMEM((seq, width), jnp.bfloat16),
-            pltpu.SemaphoreType.DMA((2,)),
+            pltpu.VMEM((2, seq, width), jnp.bfloat16),
+            pltpu.SemaphoreType.DMA((3,)),
         ],
         compiler_params=limit,
         cost_estimate=cost(len(orders[0])),
-    )(where, meta, *first_docs, stay(hidden_states), packed, other_packed, params, *halves)
+    )(where, meta, docs[2], docs[3], stay(docs[1]), stay(hidden_states), packed, other_packed, params, *halves)
     for order in orders[1:-1]:
         best += pl.pallas_call(
             lambda *refs, order=order: next_kernel(masks, order, *refs),

time: 70.1 us -> 66.8 us (0.953)
  starting transfers between devices: 20.3 us -> 16.9 us
  waiting for transfers between devices: 16.3 us -> 19.5 us
  local copies, waits for them, and re-layouts: 3.86 us -> 2 us
  blocking collectives: 14.6 us -> 13.5 us
    ppermute x12, waiting for transfers between devices: 15.7 us -> 19.5 us  [cross(): lax.ppermute(value, 'doc', [(i, i ^ 2 * mask) for i in range(devices)])]
    ppermute x12, starting transfers between devices: 19.7 us -> 16.8 us  [cross(): lax.ppermute(value, 'doc', [(i, i ^ 2 * mask) for i in range(devices)])]
    unnamed x10 -> x4, local copies, waits for them, and re-layouts: 2.53 us -> 0.67 us
    all_to_all x1, blocking collectives: 14.6 us -> 13.5 us  [move_tokens(): got = lax.all_to_all(send, 'doc', split_axis=0, concat_axis=0, tiled=True)]
  transfers between devices with their start and end apart: 14 -> 14, of which waited for: 7 -> 9; matrix products, arithmetic and copies ran while one was open for 0% -> 0% of each run, Pallas kernels for 13% -> 11%
where the time goes in v6:
time: 66.8 us; the launch traced here: 66.5 us
  waiting for transfers between devices  19.5 us (29%)
  starting transfers between devices  16.9 us (25%)
  blocking collectives  13.5 us (20%)
  Pallas kernels  13.2 us (20%)
  local copies, waits for them, and re-layouts  2 us (3%)
  between operations  1.39 us (2%)
    ppermute x12, waiting for transfers between devices, cross(): lax.ppermute(value, 'doc', [(i, i ^ 2 * mask) for i in range(devices)])  19.5 us
    ppermute x12, starting transfers between devices, cross(): lax.ppermute(value, 'doc', [(i, i ^ 2 * mask) for i in range(devices)])  16.8 us
    all_to_all x1, blocking collectives, move_tokens(): got = lax.all_to_all(send, 'doc', split_axis=0, concat_axis=0, tiled=True)  13.5 us
    pallas_call x1, Pallas kernels, move_tokens(): pl.pallas_call(lambda *refs: first_kernel(masks, orders[0], *refs), out_s...  4.31 us
    pallas_call x1, Pallas kernels, move_tokens(): pl.pallas_call(lambda *refs: last_kernel(masks, orders, *refs), out_shape...  4.09 us
    pallas_call x1, Pallas kernels, move_tokens(): pl.pallas_call(lambda *refs, order=order: next_kernel(masks, order, *refs...  3.17 us
    pallas_call x1, Pallas kernels, move_tokens(): pl.pallas_call(start_kernel, out_shape=[shape((rows, width + TILE), jnp.b...  1.61 us
  transfers between devices with their start and end apart: 14, of which 9 were waited for; matrix products, arithmetic and copies ran while one was open for 0% of the time, Pallas kernels for 11%

profile of v6, /device:TPU:0, one launch (start us, length us, event | category | flops | bytes accessed | tf_op | source)
XLA Modules:
  0.0 66.5 jit_solution(3893696786964465436)
XLA Ops:
  1.3 1.6 %shard_map.122 = (bf16[48,896]{1,0:T(8,128)(2,1)S(1)}, f32[8,768]{1,0:T(8,128)S(1)}) custom-call(s32[1,1,32]{2,1,0:T(1,128)} %tiles_ref.1, s32[1,1,32]{2,1,0:T(1,128)} %bitcast.17, s32[1,1,32]{2,1,0:T(1,128)} %slots_ref.1, s32[1]{0:T(128)S(6)} %copy.22.length_ref, bf16[48,768]{1,0:T(8,128)(2,1)} %refs_0_.1, f32[768]{0:T(1024)} %refs_1_.1, f32[768]{0:T(1024)} %refs_2_.1, ...), custom_call_target="tpu_custom_call" | custom-call | tf_op jit(solution)/shard_map/pallas_call | solution.py:318
  2.9 5.1 %collective-permute-start = (bf16[48,896]{1,0:T(8,128)(2,1)S(1)}, bf16[48,896]{1,0:T(8,128)(2,1)S(1)}, u32[]{:S(2)}, u32[]{:S(2)}) collective-permute-start(bf16[48,896]{1,0:T(8,128)(2,1)S(1)} %get-tuple-element.18.refs_0_), channel_id=1, source_target_pairs={{0,12},{1,13},{2,14},{3,15},{4,8},{5,9},{6,10},{7,11},{8,4},{9,5},... | collective-permute-start | bytes 258056 | tf_op jit(solution)/shard_map/ppermute | solution.py:291
  8.0 0.0 collective-permute-start.2
  8.0 3.4 %collective-permute-done.refs_0_.refs_2_ = bf16[48,896]{1,0:T(8,128)(2,1)S(1)} collective-permute-done((bf16[48,896]{1,0:T(8,128)(2,1)S(1)}, bf16[48,896]{1,0:T(8,128)(2,1)S(1)}, u32[]{:S(2)}, u32[]{:S(2)}) %collective-permute-start) | collective-permute-done | bytes 86048 | tf_op jit(solution)/shard_map/ppermute | solution.py:291
  11.4 1.2 %collective-permute-done.2.refs_1_ = bf16[48,896]{1,0:T(8,128)(2,1)S(1)} collective-permute-done((bf16[48,896]{1,0:T(8,128)(2,1)S(1)}, bf16[48,896]{1,0:T(8,128)(2,1)S(1)}, u32[]{:S(2)}, u32[]{:S(2)}) %collective-permute-start.2) | collective-permute-done | bytes 86048 | tf_op jit(solution)/shard_map/ppermute | solution.py:291
  12.6 0.0 collective-permute-start.12
  12.6 1.5 %collective-permute-start.6 = (bf16[128,768]{1,0:T(8,128)(2,1)}, bf16[128,768]{1,0:T(8,128)(2,1)S(1)}, u32[]{:S(2)}, u32[]{:S(2)}) collective-permute-start(bf16[128,768]{1,0:T(8,128)(2,1)} %refs_5_.1), channel_id=1, source_target_pairs={{0,4},{1,5},{2,6},{3,7},{4,0},{5,1},{6,2},{7,3},{8,12},{9,13},{10,... | collective-permute-start | bytes 589832 | tf_op jit(solution)/shard_map/ppermute | solution.py:291
  14.1 1.0 %collective-permute-start.1 = (bf16[128,768]{1,0:T(8,128)(2,1)}, bf16[128,768]{1,0:T(8,128)(2,1)S(1)}, u32[]{:S(2)}, u32[]{:S(2)}) collective-permute-start(bf16[128,768]{1,0:T(8,128)(2,1)} %refs_5_.1), channel_id=1, source_target_pairs={{0,12},{1,13},{2,14},{3,15},{4,8},{5,9},{6,10},{7,11},{8,4},{9,5},... | collective-permute-start | bytes 589832 | tf_op jit(solution)/shard_map/ppermute | solution.py:291
  15.1 1.5 %collective-permute-start.5 = (bf16[128,768]{1,0:T(8,128)(2,1)}, bf16[128,768]{1,0:T(8,128)(2,1)S(1)}, u32[]{:S(2)}, u32[]{:S(2)}) collective-permute-start(bf16[128,768]{1,0:T(8,128)(2,1)} %refs_5_.1), channel_id=1, source_target_pairs={{0,2},{1,3},{2,0},{3,1},{4,6},{5,7},{6,4},{7,5},{8,10},{9,11},{10,... | collective-permute-start | bytes 589832 | tf_op jit(solution)/shard_map/ppermute | solution.py:291
  16.6 1.1 %collective-permute-start.3 = (bf16[48,896]{1,0:T(8,128)(2,1)S(1)}, bf16[48,896]{1,0:T(8,128)(2,1)S(1)}, u32[]{:S(2)}, u32[]{:S(2)}) collective-permute-start(bf16[48,896]{1,0:T(8,128)(2,1)S(1)} %collective-permute-done.refs_0_.refs_2_), channel_id=1, source_target_pairs={{0,4},{1,5},{2,6},{3,7},{4,0},{5,1},{6,2},{7,3},{8,12},{9,13},{10,... | collective-permute-start | bytes 258056 | tf_op jit(solution)/shard_map/ppermute | solution.py:291
  17.6 2.9 %collective-permute-done.6.refs_2_ = bf16[128,768]{1,0:T(8,128)(2,1)S(1)} collective-permute-done((bf16[128,768]{1,0:T(8,128)(2,1)}, bf16[128,768]{1,0:T(8,128)(2,1)S(1)}, u32[]{:S(2)}, u32[]{:S(2)}) %collective-permute-start.6) | collective-permute-done | bytes 196640 | tf_op jit(solution)/shard_map/ppermute | solution.py:291
  20.5 1.6 %collective-permute-start.10 = (bf16[128,768]{1,0:T(8,128)(2,1)S(1)}, bf16[128,768]{1,0:T(8,128)(2,1)S(1)}, u32[]{:S(2)}, u32[]{:S(2)}) collective-permute-start(bf16[128,768]{1,0:T(8,128)(2,1)S(1)} %collective-permute-done.6.refs_2_), channel_id=1, source_target_pairs={{0,2},{1,3},{2,0},{3,1},{4,6},{5,7},{6,4},{7,5},{8,10},{9,11},{10,... | collective-permute-start | bytes 589832 | tf_op jit(solution)/shard_map/ppermute | solution.py:291
  22.2 3.1 %collective-permute-done.1.refs_1_ = bf16[128,768]{1,0:T(8,128)(2,1)S(1)} collective-permute-done((bf16[128,768]{1,0:T(8,128)(2,1)}, bf16[128,768]{1,0:T(8,128)(2,1)S(1)}, u32[]{:S(2)}, u32[]{:S(2)}) %collective-permute-start.1) | collective-permute-done | bytes 196640 | tf_op jit(solution)/shard_map/ppermute | solution.py:291
  25.2 0.9 %collective-permute-start.8 = (bf16[128,768]{1,0:T(8,128)(2,1)S(1)}, bf16[128,768]{1,0:T(8,128)(2,1)S(1)}, u32[]{:S(2)}, u32[]{:S(2)}) collective-permute-start(bf16[128,768]{1,0:T(8,128)(2,1)S(1)} %collective-permute-done.1.refs_1_), channel_id=1, source_target_pairs={{0,4},{1,5},{2,6},{3,7},{4,0},{5,1},{6,2},{7,3},{8,12},{9,13},{10,... | collective-permute-start | bytes 589832 | tf_op jit(solution)/shard_map/ppermute | solution.py:291
  26.1 0.1 collective-permute-done.3.refs_1_.refs_3_
  26.2 1.6 %collective-permute-start.4 = (bf16[96,896]{1,0:T(8,128)(2,1)S(1)}, bf16[96,896]{1,0:T(8,128)(2,1)S(1)}, u32[]{:S(2)}, u32[]{:S(2)}) collective-permute-start(bf16[96,896]{1,0:T(8,128)(2,1)S(1)} %shard_map.123), channel_id=1, source_target_pairs={{0,2},{1,3},{2,0},{3,1},{4,6},{5,7},{6,4},{7,5},{8,10},{9,11},{10,... | collective-permute-start | bytes 516104 | tf_op jit(solution)/shard_map/ppermute | solution.py:291
  27.8 0.0 collective-permute-done.5.refs_4_
  27.8 0.0 copy-start.1
  27.8 0.7 copy-done.1
  28.5 0.5 collective-permute-start.7
  29.0 4.5 %collective-permute-done.4.refs_4_ = bf16[96,896]{1,0:T(8,128)(2,1)S(1)} collective-permute-done((bf16[96,896]{1,0:T(8,128)(2,1)S(1)}, bf16[96,896]{1,0:T(8,128)(2,1)S(1)}, u32[]{:S(2)}, u32[]{:S(2)}) %collective-permute-start.4) | collective-permute-done | bytes 172064 | tf_op jit(solution)/shard_map/ppermute | solution.py:291
  33.5 2.4 %collective-permute-done.7.refs_5_ = bf16[96,896]{1,0:T(8,128)(2,1)S(1)} collective-permute-done((bf16[96,896]{1,0:T(8,128)(2,1)S(1)}, bf16[96,896]{1,0:T(8,128)(2,1)S(1)}, u32[]{:S(2)}, u32[]{:S(2)}) %collective-permute-start.7) | collective-permute-done | bytes 172064 | tf_op jit(solution)/shard_map/ppermute | solution.py:291
  35.9 0.0 collective-permute-done.10.refs_3_
  36.0 0.0 collective-permute-done.8.refs_3_
  36.0 0.1 collective-permute-start.11
  36.0 1.7 %collective-permute-start.13 = (bf16[128,768]{1,0:T(8,128)(2,1)S(1)}, bf16[128,768]{1,0:T(8,128)(2,1)S(1)}, u32[]{:S(2)}, u32[]{:S(2)}) collective-permute-start(bf16[128,768]{1,0:T(8,128)(2,1)S(1)} %collective-permute-done.1.refs_1_), channel_id=1, source_target_pairs={{0,2},{1,3},{2,0},{3,1},{4,6},{5,7},{6,4},{7,5},{8,10},{9,11},{10,... | collective-permute-start | bytes 589832 | tf_op jit(solution)/shard_map/ppermute | solution.py:291
  37.7 0.4 collective-permute-start.9
  38.1 0.0 collective-permute-done.11.refs_7_
  38.1 0.0 collective-permute-done.12.refs_10_.refs_6_.refs_8_
  38.1 4.3 %shard_map.126 = (f32[8,960]{1,0:T(8,128)S(1)}, f32[8,960]{1,0:T(8,128)S(1)}, bf16[768,768]{1,0:T(8,128)(2,1)S(1)}) custom-call(s32[1]{0:T(128)} %bitcast.refs_0_, s32[8,128]{1,0:T(8,128)S(1)} %get-tuple-element.20.refs_1_.refs_0_.refs_2_, bf16[128,768]{1,0:T(8,128)(2,1)S(1)} %collective-permute-done.6.refs_2_, ...), custom_call_target="tpu_custom_call" | custom-call | flops 2113929216 | bytes 1048576 | tf_op jit(solution)/shard_map/pallas_call | solution.py:382
  42.5 1.4 %collective-permute-done.13.refs_2_ = bf16[128,768]{1,0:T(8,128)(2,1)S(1)} collective-permute-done((bf16[128,768]{1,0:T(8,128)(2,1)S(1)}, bf16[128,768]{1,0:T(8,128)(2,1)S(1)}, u32[]{:S(2)}, u32[]{:S(2)}) %collective-permute-start.13) | collective-permute-done | bytes 196640 | tf_op jit(solution)/shard_map/ppermute | solution.py:291
  43.8 0.0 copy-start
  43.8 3.2 %shard_map.127 = (f32[8,960]{1,0:T(8,128)S(1)}, f32[8,960]{1,0:T(8,128)S(1)}) custom-call(s32[8,128]{1,0:T(8,128)S(1)} %get-tuple-element.20.refs_1_.refs_0_.refs_2_, bf16[128,768]{1,0:T(8,128)(2,1)S(1)} %collective-permute-done.1.refs_1_, bf16[128,768]{1,0:T(8,128)(2,1)S(1)} %collective-permute-done.13.refs_2_, ...), custom_call_target="tpu_custom_call" | custom-call | flops 1056964608 | bytes 1048576 | tf_op jit(solution)/shard_map/pallas_call | solution.py:396
  47.0 0.6 collective-permute-done.9.refs_4_
  47.6 0.0 copy-done
  47.6 4.1 %shard_map.128 = bf16[16,48,128]{2,1,0:T(8,128)(2,1)S(1)} custom-call(s32[1]{0:T(128)} %bitcast.refs_0_, s32[8,128]{1,0:T(8,128)S(1)} %get-tuple-element.20.refs_1_.refs_0_.refs_2_, s32[8,128]{1,0:T(8,128)S(1)} %get-tuple-element.20.refs_1_.refs_0_.refs_2_, bf16[128,768]{1,0:T(8,128)(2,1)S(1)} %collective-permute-done.8.refs_3_, ...), custom_call_target="tpu_custom_call" | custom-call | flops 1056964608 | bytes 1048576 | tf_op jit(solution)/shard_map/pallas_call | solution.py:405
  51.7 13.5 %all_to_all.5 = bf16[16,48,128]{2,1,0:T(8,128)(2,1)S(1)} all-to-all(bf16[16,48,128]{2,1,0:T(8,128)(2,1)S(1)} %shard_map.128), channel_id=1, replica_groups=mesh['groups'=2,'doc'=16,'term'=1] {'doc'}, dimensions={0} | all-to-all | bytes 393216 | tf_op jit(solution)/shard_map/all_to_all | solution.py:428
  65.2 0.7 slice.26
  65.9 0.6 slice.24
  (7 shorter events, 0.1 us)
Async XLA Ops:
  2.9 8.5 %collective-permute-start = (bf16[48,896]{1,0:T(8,128)(2,1)S(1)}, bf16[48,896]{1,0:T(8,128)(2,1)S(1)}, u32[]{:S(2)}, u32[]{:S(2)}) collective-permute-start(bf16[48,896]{1,0:T(8,128)(2,1)S(1)} %get-tuple-element.18.refs_0_), channel_id=1, source_target_pairs={{0,12},{1,13},{2,14},{3,15},{4,8},{5,9},{6,10},{7,11},{8,4},{9,5},... | collective-permute-start | bytes 258056 | tf_op jit(solution)/shard_map/ppermute | solution.py:291
  8.0 4.6 %collective-permute-start.2 = (bf16[48,896]{1,0:T(8,128)(2,1)S(1)}, bf16[48,896]{1,0:T(8,128)(2,1)S(1)}, u32[]{:S(2)}, u32[]{:S(2)}) collective-permute-start(bf16[48,896]{1,0:T(8,128)(2,1)S(1)} %get-tuple-element.18.refs_0_), channel_id=1, source_target_pairs={{0,4},{1,5},{2,6},{3,7},{4,0},{5,1},{6,2},{7,3},{8,12},{9,13},{10,... | collective-permute-start | bytes 258056 | tf_op jit(solution)/shard_map/ppermute | solution.py:291
  12.6 25.5 %collective-permute-start.12 = (bf16[960,768]{1,0:T(8,128)(2,1)}, bf16[960,768]{1,0:T(8,128)(2,1)S(1)}, u32[]{:S(2)}, u32[]{:S(2)}) collective-permute-start(bf16[960,768]{1,0:T(8,128)(2,1)} %bitcast.12), channel_id=1, source_target_pairs={{0,1},{1,0},{2,3},{3,2},{4,5},{5,4},{6,7},{7,6},{8,9},{9,8},{10,11... | collective-permute-start | bytes 4423688 | tf_op jit(solution)/shard_map/ppermute | solution.py:294
  12.6 7.9 %collective-permute-start.6 = (bf16[128,768]{1,0:T(8,128)(2,1)}, bf16[128,768]{1,0:T(8,128)(2,1)S(1)}, u32[]{:S(2)}, u32[]{:S(2)}) collective-permute-start(bf16[128,768]{1,0:T(8,128)(2,1)} %refs_5_.1), channel_id=1, source_target_pairs={{0,4},{1,5},{2,6},{3,7},{4,0},{5,1},{6,2},{7,3},{8,12},{9,13},{10,... | collective-permute-start | bytes 589832 | tf_op jit(solution)/shard_map/ppermute | solution.py:291
  14.1 11.1 %collective-permute-start.1 = (bf16[128,768]{1,0:T(8,128)(2,1)}, bf16[128,768]{1,0:T(8,128)(2,1)S(1)}, u32[]{:S(2)}, u32[]{:S(2)}) collective-permute-start(bf16[128,768]{1,0:T(8,128)(2,1)} %refs_5_.1), channel_id=1, source_target_pairs={{0,12},{1,13},{2,14},{3,15},{4,8},{5,9},{6,10},{7,11},{8,4},{9,5},... | collective-permute-start | bytes 589832 | tf_op jit(solution)/shard_map/ppermute | solution.py:291
  15.1 12.7 %collective-permute-start.5 = (bf16[128,768]{1,0:T(8,128)(2,1)}, bf16[128,768]{1,0:T(8,128)(2,1)S(1)}, u32[]{:S(2)}, u32[]{:S(2)}) collective-permute-start(bf16[128,768]{1,0:T(8,128)(2,1)} %refs_5_.1), channel_id=1, source_target_pairs={{0,2},{1,3},{2,0},{3,1},{4,6},{5,7},{6,4},{7,5},{8,10},{9,11},{10,... | collective-permute-start | bytes 589832 | tf_op jit(solution)/shard_map/ppermute | solution.py:291
  16.6 9.6 %collective-permute-start.3 = (bf16[48,896]{1,0:T(8,128)(2,1)S(1)}, bf16[48,896]{1,0:T(8,128)(2,1)S(1)}, u32[]{:S(2)}, u32[]{:S(2)}) collective-permute-start(bf16[48,896]{1,0:T(8,128)(2,1)S(1)} %collective-permute-done.refs_0_.refs_2_), channel_id=1, source_target_pairs={{0,4},{1,5},{2,6},{3,7},{4,0},{5,1},{6,2},{7,3},{8,12},{9,13},{10,... | collective-permute-start | bytes 258056 | tf_op jit(solution)/shard_map/ppermute | solution.py:291
  20.5 15.4 %collective-permute-start.10 = (bf16[128,768]{1,0:T(8,128)(2,1)S(1)}, bf16[128,768]{1,0:T(8,128)(2,1)S(1)}, u32[]{:S(2)}, u32[]{:S(2)}) collective-permute-start(bf16[128,768]{1,0:T(8,128)(2,1)S(1)} %collective-permute-done.6.refs_2_), channel_id=1, source_target_pairs={{0,2},{1,3},{2,0},{3,1},{4,6},{5,7},{6,4},{7,5},{8,10},{9,11},{10,... | collective-permute-start | bytes 589832 | tf_op jit(solution)/shard_map/ppermute | solution.py:291
  25.2 10.7 %collective-permute-start.8 = (bf16[128,768]{1,0:T(8,128)(2,1)S(1)}, bf16[128,768]{1,0:T(8,128)(2,1)S(1)}, u32[]{:S(2)}, u32[]{:S(2)}) collective-permute-start(bf16[128,768]{1,0:T(8,128)(2,1)S(1)} %collective-permute-done.1.refs_1_), channel_id=1, source_target_pairs={{0,4},{1,5},{2,6},{3,7},{4,0},{5,1},{6,2},{7,3},{8,12},{9,13},{10,... | collective-permute-start | bytes 589832 | tf_op jit(solution)/shard_map/ppermute | solution.py:291
  26.2 7.3 %collective-permute-start.4 = (bf16[96,896]{1,0:T(8,128)(2,1)S(1)}, bf16[96,896]{1,0:T(8,128)(2,1)S(1)}, u32[]{:S(2)}, u32[]{:S(2)}) collective-permute-start(bf16[96,896]{1,0:T(8,128)(2,1)S(1)} %shard_map.123), channel_id=1, source_target_pairs={{0,2},{1,3},{2,0},{3,1},{4,6},{5,7},{6,4},{7,5},{8,10},{9,11},{10,... | collective-permute-start | bytes 516104 | tf_op jit(solution)/shard_map/ppermute | solution.py:291
  27.8 0.7 %copy-start.1 = (bf16[128,768]{1,0:T(8,128)(2,1)}, bf16[128,768]{1,0:T(8,128)(2,1)S(1)}, u32[]{:S(2)}) copy-start(bf16[128,768]{1,0:T(8,128)(2,1)S(1)} %collective-permute-done.5.refs_4_) | copy-start | bytes 589828
  28.5 7.4 %collective-permute-start.7 = (bf16[96,896]{1,0:T(8,128)(2,1)S(1)}, bf16[96,896]{1,0:T(8,128)(2,1)S(1)}, u32[]{:S(2)}, u32[]{:S(2)}) collective-permute-start(bf16[96,896]{1,0:T(8,128)(2,1)S(1)} %shard_map.124), channel_id=1, source_target_pairs={{0,2},{1,3},{2,0},{3,1},{4,6},{5,7},{6,4},{7,5},{8,10},{9,11},{10,... | collective-permute-start | bytes 516104 | tf_op jit(solution)/shard_map/ppermute | solution.py:291
  36.0 2.2 %collective-permute-start.11 = (bf16[384,768]{1,0:T(8,128)(2,1)S(1)}, bf16[384,768]{1,0:T(8,128)(2,1)S(1)}, u32[]{:S(2)}, u32[]{:S(2)}) collective-permute-start(bf16[384,768]{1,0:T(8,128)(2,1)S(1)} %get-tuple-element.22.refs_6_), channel_id=1, source_target_pairs={{0,1},{1,0},{2,3},{3,2},{4,5},{5,4},{6,7},{7,6},{8,9},{9,8},{10,11... | collective-permute-start | bytes 1769480 | tf_op jit(solution)/shard_map/ppermute | solution.py:294
  36.0 7.8 %collective-permute-start.13 = (bf16[128,768]{1,0:T(8,128)(2,1)S(1)}, bf16[128,768]{1,0:T(8,128)(2,1)S(1)}, u32[]{:S(2)}, u32[]{:S(2)}) collective-permute-start(bf16[128,768]{1,0:T(8,128)(2,1)S(1)} %collective-permute-done.1.refs_1_), channel_id=1, source_target_pairs={{0,2},{1,3},{2,0},{3,1},{4,6},{5,7},{6,4},{7,5},{8,10},{9,11},{10,... | collective-permute-start | bytes 589832 | tf_op jit(solution)/shard_map/ppermute | solution.py:291
  37.7 9.9 %collective-permute-start.9 = (bf16[128,768]{1,0:T(8,128)(2,1)S(1)}, bf16[128,768]{1,0:T(8,128)(2,1)S(1)}, u32[]{:S(2)}, u32[]{:S(2)}) collective-permute-start(bf16[128,768]{1,0:T(8,128)(2,1)S(1)} %collective-permute-done.8.refs_3_), channel_id=1, source_target_pairs={{0,2},{1,3},{2,0},{3,1},{4,6},{5,7},{6,4},{7,5},{8,10},{9,11},{10,... | collective-permute-start | bytes 589832 | tf_op jit(solution)/shard_map/ppermute | solution.py:291
  43.8 3.8 %copy-start = (f32[15360]{0:T(1024)S(1)}, f32[15360]{0:T(1024)}, u32[]{:S(2)}) copy-start(f32[15360]{0:T(1024)} %param.18) | copy-start | bytes 184324

commit v7 on v6

--- a/solution.py
+++ b/solution.py
@@ -180,7 +180,7 @@
     docs, refs = refs[: len(order)], refs[len(order) :]
     packed, refs = refs[:2], refs[2:]
     params, mine_ref, theirs_ref, refs = refs[0], refs[1], refs[2], refs[3:]
-    best_refs, weight, mine, late, sems = refs[:2], refs[2], *refs[3:]
+    best_refs, weight, mine, late, sems = refs[:2], refs[2], refs[3], *refs[4:]
     mine_copy = fetch(mine_ref, mine, sems.at[0])
     late_copies = [fetch(docs[k - 2], late.at[k], sems.at[1 + k]) for k in range(2)]
     me = me_ref[0]
@@ -210,12 +210,10 @@
 def next_kernel(masks, order, *refs):
     meta_ref, refs = refs[0], refs[1:]
     docs, weight, params, refs = refs[:2], refs[2], refs[3], refs[4:]
-    mine_ref, theirs_ref, best_refs, mine, sem = refs[0], refs[1], refs[2:4], *refs[4:]
-    copy = fetch(mine_ref, mine, sem)
+    halves, best_refs = refs[:2], refs[2:]
     lengths = [length_of(meta_ref, masks.index(m)) for m in order]
     normed = normed_rows(docs, lengths, weight, params)
-    copy.wait()
-    for w_ref, best in zip((mine, theirs_ref), best_refs):
+    for w_ref, best in zip(halves, best_refs):
         for j, top in enumerate(tops_of(normed, w_ref, 2)):
             best[j : j + 1, :] = top
 
@@ -223,20 +221,18 @@
 def last_kernel(masks, orders, *refs):
     me_ref, table_ref, meta_ref, refs = refs[0], refs[1], refs[2], refs[3:]
     docs, weight, params, refs = refs[:2], refs[2], refs[3], refs[4:]
-    mine_ref, theirs_ref, dbias_ref, refs = refs[0], refs[1], refs[2], refs[3:]
+    halves, dbias_ref, refs = refs[:2], refs[2], refs[3:]
     counts = [len(order) for order in orders[:-1]]
     earlier, refs = refs[: 2 * len(counts)], refs[2 * len(counts) :]
-    out_ref, send, mine, sem = refs
-    copy = fetch(mine_ref, mine, sem)
+    out_ref, send = refs
     me = me_ref[0]
     core, chip = me % 2, me // 2
     devices = 2 * len(masks)
-    tiles = 2 * mine_ref.shape[0] // TILE
+    tiles = 2 * halves[0].shape[0] // TILE
     lengths = [length_of(meta_ref, masks.index(m)) for m in orders[-1]]
     normed = normed_rows(docs, lengths, weight, params)
     found = []
-    copy.wait()
-    for k, w_ref in enumerate((mine, theirs_ref)):
+    for k, w_ref in enumerate(halves):
         parts = [earlier[2 * n + k][0:count, :] for n, count in enumerate(counts)]
         found.append(jnp.concatenate([*parts, *tops_of(normed, w_ref, 2)], axis=0))
     low = jnp.where(core == 0, found[0], found[1])
@@ -348,19 +344,20 @@
             compiler_params=limit,
         )(*values)
 
+    weight_rows = jnp.swapaxes(decoder_weight[0], 0, 1)
+    theirs = swap(weight_rows)
+    docs = {0: hidden_states, 1: cross(hidden_states, 1)}
     block_6 = cross(block, 6)
     block_2 = cross(block, 2)
-    docs = {0: hidden_states, 1: cross(hidden_states, 1), 2: cross(hidden_states, 2)}
+    docs[6] = cross(hidden_states, 6)
+    docs[2] = cross(hidden_states, 2)
     near_pile = cross(pile(block, block_2), 1)
-    block_4 = cross(block_6, 2)
-    docs[6] = cross(after(hidden_states, block_6), 6)
+    block_4 = cross(after(block_6, docs[1], theirs), 2)
+    docs[4] = cross(docs[6], 2)
     docs[3] = cross(docs[2], 1)
-    far_pile = cross(pile(block_6, after(block_4, docs[1], docs[2])), 1)
-    docs[4] = cross(docs[6], 2)
+    far_pile = cross(pile(block_6, after(block_4, near_pile)), 1)
     docs[7] = cross(docs[6], 1)
     docs[5] = cross(docs[4], 1)
-    weight_rows = jnp.swapaxes(decoder_weight[0], 0, 1)
-    theirs = swap(after(weight_rows, block_6, block_2))
     masks = [0, 2, 6, 4, 1, 3, 7, 5]
     packed, meta = pl.pallas_call(
         pack_kernel,
@@ -371,46 +368,57 @@
         in_specs=[vmem] * 6,
         out_specs=[vmem] * 2,
         compiler_params=limit,
-    )(after(block, docs[6]), block_2, block_6, block_4, near_pile, far_pile)
-    other_packed = swap(after(packed, docs[3], docs[4]))
+    )(after(block, docs[4]), block_2, block_6, block_4, near_pile, far_pile)
+    other_packed = swap(after(packed, docs[3]))
 
     orders = [[2, 3, 1, 0], [6, 7], [4, 5]]
     where = me[None]
-    halves = (stay(weight_rows), theirs)
-    slot = pltpu.VMEM((half, width), jnp.bfloat16)
     best_shape = shape((8, half), jnp.float32)
-    *best, weight = pl.pallas_call(
+    *best, weight, mine = pl.pallas_call(
         lambda *refs: first_kernel(masks, orders[0], *refs),
-        out_shape=[best_shape, best_shape, shape((width, width), jnp.bfloat16)],
+        out_shape=[
+            best_shape,
+            best_shape,
+            shape((width, width), jnp.bfloat16),
+            shape((half, width), jnp.bfloat16),
+        ],
         in_specs=[smem] + [vmem] * 3 + [hbm] * 2 + [vmem] * 3 + [hbm, vmem],
-        out_specs=[vmem] * 3,
+        out_specs=[vmem] * 4,
         scratch_shapes=[
-            slot,
             pltpu.VMEM((2, seq, width), jnp.bfloat16),
             pltpu.SemaphoreType.DMA((3,)),
         ],
         compiler_params=limit,
         cost_estimate=cost(len(orders[0])),
-    )(where, meta, docs[2], docs[3], stay(docs[1]), stay(hidden_states), packed, other_packed, params, *halves)
+    )(
+        where,
+        meta,
+        docs[2],
+        docs[3],
+        stay(docs[1]),
+        stay(hidden_states),
+        packed,
+        other_packed,
+        params,
+        stay(weight_rows),
+        theirs,
+    )
     for order in orders[1:-1]:
         best += pl.pallas_call(
             lambda *refs, order=order: next_kernel(masks, order, *refs),
             out_shape=[best_shape] * 2,
-            in_specs=[vmem] * 5 + [hbm, vmem],
+            in_specs=[vmem] * 7,
             out_specs=[vmem] * 2,
-            scratch_shapes=[slot, pltpu.SemaphoreType.DMA],
             compiler_params=limit,
             cost_estimate=cost(2),
-        )(meta, *[docs[mask] for mask in order], weight, params, *halves)
+        )(meta, *[docs[mask] for mask in order], weight, params, mine, theirs)
     send = pl.pallas_call(
         lambda *refs: last_kernel(masks, orders, *refs),
         out_shape=shape((devices, (1 + BLK_DEV) * SLOT_ROWS, TILE), jnp.bfloat16),
-        in_specs=[smem] * 2 + [vmem] * 5 + [hbm] + [vmem] * (2 + len(best)),
+        in_specs=[smem] * 2 + [vmem] * (8 + len(best)),
         out_specs=vmem,
         scratch_shapes=[
             pltpu.VMEM((devices * (1 + BLK_DEV) * SLOT_ROWS, TILE), jnp.float32),
-            slot,
-            pltpu.SemaphoreType.DMA,
         ],
         compiler_params=limit,
         cost_estimate=cost(2),
@@ -421,7 +429,8 @@
         *[docs[mask] for mask in orders[-1]],
         weight,
         params,
-        *halves,
+        mine,
+        theirs,
         decoder_bias.reshape(-1, TILE),
         *best,
     )

time: 66.8 us -> 61.9 us (0.927)
  waiting for transfers between devices: 19.5 us -> 13.6 us
  starting transfers between devices: 16.9 us -> 22.2 us
  Pallas kernels: 13.2 us -> 10.5 us
  blocking collectives: 13.5 us -> 12.6 us
  local copies, waits for them, and re-layouts: 2 us -> 1.33 us
    ppermute x12, waiting for transfers between devices: 19.5 us -> 13.6 us  [cross(): lax.ppermute(value, 'doc', [(i, i ^ 2 * mask) for i in range(devices)])]
    ppermute x12, starting transfers between devices: 16.8 us -> 21.6 us  [cross(): lax.ppermute(value, 'doc', [(i, i ^ 2 * mask) for i in range(devices)])]
    pallas_call x1, Pallas kernels: 3.17 us -> 1.77 us  [move_tokens(): pl.pallas_call(lambda *refs, order=order: next_kernel(masks, order, *refs...]
    pallas_call x1, Pallas kernels: 4.09 us -> 2.69 us  [move_tokens(): pl.pallas_call(lambda *refs: last_kernel(masks, orders, *refs), out_shape...]
    all_to_all x1, blocking collectives: 13.5 us -> 12.6 us  [move_tokens(): got = lax.all_to_all(send, 'doc', split_axis=0, concat_axis=0, tiled=True)]
  transfers between devices with their start and end apart: 14 -> 14, of which waited for: 9 -> 6; matrix products, arithmetic and copies ran while one was open for 0% -> 0% of each run, Pallas kernels for 11% -> 13%
where the time goes in v7:
time: 61.9 us; the launch traced here: 61.6 us
  starting transfers between devices  22.2 us (36%)
  waiting for transfers between devices  13.6 us (22%)
  blocking collectives  12.6 us (20%)
  Pallas kernels  10.5 us (17%)
  between operations  1.39 us (2%)
  local copies, waits for them, and re-layouts  1.33 us (2%)
    ppermute x12, starting transfers between devices, cross(): lax.ppermute(value, 'doc', [(i, i ^ 2 * mask) for i in range(devices)])  21.6 us
    ppermute x12, waiting for transfers between devices, cross(): lax.ppermute(value, 'doc', [(i, i ^ 2 * mask) for i in range(devices)])  13.6 us
    all_to_all x1, blocking collectives, move_tokens(): got = lax.all_to_all(send, 'doc', split_axis=0, concat_axis=0, tiled=True)  12.6 us
    pallas_call x1, Pallas kernels, move_tokens(): pl.pallas_call(lambda *refs: first_kernel(masks, orders[0], *refs), out_s...  4.34 us
    pallas_call x1, Pallas kernels, move_tokens(): pl.pallas_call(lambda *refs: last_kernel(masks, orders, *refs), out_shape...  2.69 us
    pallas_call x1, Pallas kernels, move_tokens(): pl.pallas_call(lambda *refs, order=order: next_kernel(masks, order, *refs...  1.77 us
    pallas_call x1, Pallas kernels, move_tokens(): pl.pallas_call(start_kernel, out_shape=[shape((rows, width + TILE), jnp.b...  1.61 us
    slice x4, local copies, waits for them, and re-layouts, move_tokens(): return (whole[:1], whole[1:])  1.31 us
  transfers between devices with their start and end apart: 14, of which 6 were waited for; matrix products, arithmetic and copies ran while one was open for 0% of the time, Pallas kernels for 13%

profile of v7, /device:TPU:0, one launch (start us, length us, event | category | flops | bytes accessed | tf_op | source)
XLA Modules:
  0.0 61.6 jit_solution(2527797925675442756)
XLA Ops:
  0.6 0.5 collective-permute-start.5
  1.8 1.6 %shard_map.122 = (bf16[48,896]{1,0:T(8,128)(2,1)S(1)}, f32[8,768]{1,0:T(8,128)S(1)}) custom-call(s32[1,1,32]{2,1,0:T(1,128)} %tiles_ref.1, s32[1,1,32]{2,1,0:T(1,128)} %bitcast.13, s32[1,1,32]{2,1,0:T(1,128)} %slots_ref.1, s32[1]{0:T(128)S(6)} %copy.22.length_ref, bf16[48,768]{1,0:T(8,128)(2,1)} %refs_0_.1, f32[768]{0:T(1024)} %refs_1_.1, f32[768]{0:T(1024)} %refs_2_.1, ...), custom_call_target="tpu_custom_call" | custom-call | tf_op jit(solution)/shard_map/pallas_call | solution.py:314
  3.4 2.6 %collective-permute-start.2 = (bf16[48,896]{1,0:T(8,128)(2,1)S(1)}, bf16[48,896]{1,0:T(8,128)(2,1)S(1)}, u32[]{:S(2)}, u32[]{:S(2)}) collective-permute-start(bf16[48,896]{1,0:T(8,128)(2,1)S(1)} %get-tuple-element.17.refs_0_), channel_id=1, source_target_pairs={{0,4},{1,5},{2,6},{3,7},{4,0},{5,1},{6,2},{7,3},{8,12},{9,13},{10,... | collective-permute-start | bytes 258056 | tf_op jit(solution)/shard_map/ppermute | solution.py:287
  6.1 1.5 %collective-permute-start.4 = (bf16[128,768]{1,0:T(8,128)(2,1)}, bf16[128,768]{1,0:T(8,128)(2,1)S(1)}, u32[]{:S(2)}, u32[]{:S(2)}) collective-permute-start(bf16[128,768]{1,0:T(8,128)(2,1)} %refs_5_.1), channel_id=1, source_target_pairs={{0,2},{1,3},{2,0},{3,1},{4,6},{5,7},{6,4},{7,5},{8,10},{9,11},{10,... | collective-permute-start | bytes 589832 | tf_op jit(solution)/shard_map/ppermute | solution.py:287
  7.6 2.5 %collective-permute-start.3 = (bf16[48,896]{1,0:T(8,128)(2,1)S(1)}, bf16[48,896]{1,0:T(8,128)(2,1)S(1)}, u32[]{:S(2)}, u32[]{:S(2)}) collective-permute-start(bf16[48,896]{1,0:T(8,128)(2,1)S(1)} %get-tuple-element.17.refs_0_), channel_id=1, source_target_pairs={{0,12},{1,13},{2,14},{3,15},{4,8},{5,9},{6,10},{7,11},{8,4},{9,5},... | collective-permute-start | bytes 258056 | tf_op jit(solution)/shard_map/ppermute | solution.py:287
  10.0 1.3 %collective-permute-start = (bf16[128,768]{1,0:T(8,128)(2,1)}, bf16[128,768]{1,0:T(8,128)(2,1)S(1)}, u32[]{:S(2)}, u32[]{:S(2)}) collective-permute-start(bf16[128,768]{1,0:T(8,128)(2,1)} %refs_5_.1), channel_id=1, source_target_pairs={{0,12},{1,13},{2,14},{3,15},{4,8},{5,9},{6,10},{7,11},{8,4},{9,5},... | collective-permute-start | bytes 589832 | tf_op jit(solution)/shard_map/ppermute | solution.py:287
  11.4 0.0 collective-permute-done.2.refs_1_
  11.4 0.0 collective-permute-start.10
  11.4 2.5 %collective-permute-done.3.refs_0_.refs_2_ = bf16[48,896]{1,0:T(8,128)(2,1)S(1)} collective-permute-done((bf16[48,896]{1,0:T(8,128)(2,1)S(1)}, bf16[48,896]{1,0:T(8,128)(2,1)S(1)}, u32[]{:S(2)}, u32[]{:S(2)}) %collective-permute-start.3) | collective-permute-done | bytes 86048 | tf_op jit(solution)/shard_map/ppermute | solution.py:287
  13.9 1.0 %collective-permute-start.7 = (bf16[96,896]{1,0:T(8,128)(2,1)S(1)}, bf16[96,896]{1,0:T(8,128)(2,1)S(1)}, u32[]{:S(2)}, u32[]{:S(2)}) collective-permute-start(bf16[96,896]{1,0:T(8,128)(2,1)S(1)} %shard_map.123), channel_id=1, source_target_pairs={{0,2},{1,3},{2,0},{3,1},{4,6},{5,7},{6,4},{7,5},{8,10},{9,11},{10,... | collective-permute-start | bytes 516104 | tf_op jit(solution)/shard_map/ppermute | solution.py:287
  15.0 0.0 collective-permute-done.4.refs_4_
  15.0 0.0 copy-start.1
  15.0 0.0 collective-permute-done.5.refs_10_.refs_6_.refs_8_
  15.0 5.2 %collective-permute-start.6 = (bf16[48,896]{1,0:T(8,128)(2,1)S(1)}, bf16[48,896]{1,0:T(8,128)(2,1)S(1)}, u32[]{:S(2)}, u32[]{:S(2)}) collective-permute-start(bf16[48,896]{1,0:T(8,128)(2,1)S(1)} %collective-permute-done.3.refs_0_.refs_2_), channel_id=1, source_target_pairs={{0,4},{1,5},{2,6},{3,7},{4,0},{5,1},{6,2},{7,3},{8,12},{9,13},{10,... | collective-permute-start | bytes 258056 | tf_op jit(solution)/shard_map/ppermute | solution.py:287
  20.2 0.0 copy-done.1
  20.2 0.0 collective-permute-done.refs_1_
  20.2 3.5 %collective-permute-start.1 = (bf16[128,768]{1,0:T(8,128)(2,1)S(1)}, bf16[128,768]{1,0:T(8,128)(2,1)S(1)}, u32[]{:S(2)}, u32[]{:S(2)}) collective-permute-start(bf16[128,768]{1,0:T(8,128)(2,1)S(1)} %collective-permute-done.refs_1_), channel_id=1, source_target_pairs={{0,4},{1,5},{2,6},{3,7},{4,0},{5,1},{6,2},{7,3},{8,12},{9,13},{10,... | collective-permute-start | bytes 589832 | tf_op jit(solution)/shard_map/ppermute | solution.py:287
  23.6 0.0 collective-permute-done.10.refs_2_
  23.6 0.5 collective-permute-start.11
  24.2 0.0 collective-permute-done.7.refs_4_
  24.2 0.2 collective-permute-done.6.refs_1_.refs_3_
  24.4 1.3 %collective-permute-start.8 = (bf16[96,896]{1,0:T(8,128)(2,1)S(1)}, bf16[96,896]{1,0:T(8,128)(2,1)S(1)}, u32[]{:S(2)}, u32[]{:S(2)}) collective-permute-start(bf16[96,896]{1,0:T(8,128)(2,1)S(1)} %shard_map.124), channel_id=1, source_target_pairs={{0,2},{1,3},{2,0},{3,1},{4,6},{5,7},{6,4},{7,5},{8,10},{9,11},{10,... | collective-permute-start | bytes 516104 | tf_op jit(solution)/shard_map/ppermute | solution.py:287
  25.7 2.6 %collective-permute-done.1.refs_3_ = bf16[128,768]{1,0:T(8,128)(2,1)S(1)} collective-permute-done((bf16[128,768]{1,0:T(8,128)(2,1)S(1)}, bf16[128,768]{1,0:T(8,128)(2,1)S(1)}, u32[]{:S(2)}, u32[]{:S(2)}) %collective-permute-start.1) | collective-permute-done | bytes 196640 | tf_op jit(solution)/shard_map/ppermute | solution.py:287
  28.4 4.9 %collective-permute-done.8.refs_5_ = bf16[96,896]{1,0:T(8,128)(2,1)S(1)} collective-permute-done((bf16[96,896]{1,0:T(8,128)(2,1)S(1)}, bf16[96,896]{1,0:T(8,128)(2,1)S(1)}, u32[]{:S(2)}, u32[]{:S(2)}) %collective-permute-start.8) | collective-permute-done | bytes 172064 | tf_op jit(solution)/shard_map/ppermute | solution.py:287
  33.3 0.0 collective-permute-done.11.refs_3_
  33.3 0.1 collective-permute-start.12
  33.4 0.8 %collective-permute-start.13 = (bf16[128,768]{1,0:T(8,128)(2,1)S(1)}, bf16[128,768]{1,0:T(8,128)(2,1)S(1)}, u32[]{:S(2)}, u32[]{:S(2)}) collective-permute-start(bf16[128,768]{1,0:T(8,128)(2,1)S(1)} %collective-permute-done.refs_1_), channel_id=1, source_target_pairs={{0,2},{1,3},{2,0},{3,1},{4,6},{5,7},{6,4},{7,5},{8,10},{9,11},{10,... | collective-permute-start | bytes 589832 | tf_op jit(solution)/shard_map/ppermute | solution.py:287
  34.2 1.3 %collective-permute-start.9 = (bf16[128,768]{1,0:T(8,128)(2,1)S(1)}, bf16[128,768]{1,0:T(8,128)(2,1)S(1)}, u32[]{:S(2)}, u32[]{:S(2)}) collective-permute-start(bf16[128,768]{1,0:T(8,128)(2,1)S(1)} %collective-permute-done.1.refs_3_), channel_id=1, source_target_pairs={{0,2},{1,3},{2,0},{3,1},{4,6},{5,7},{6,4},{7,5},{8,10},{9,11},{10,... | collective-permute-start | bytes 589832 | tf_op jit(solution)/shard_map/ppermute | solution.py:287
  35.5 0.0 collective-permute-done.12.refs_7_
  35.5 4.3 %shard_map.126 = (f32[8,960]{1,0:T(8,128)S(1)}, f32[8,960]{1,0:T(8,128)S(1)}, bf16[768,768]{1,0:T(8,128)(2,1)S(1)}, bf16[960,768]{1,0:T(8,128)(2,1)S(1)}) custom-call(s32[1]{0:T(128)} %bitcast.refs_0_, s32[8,128]{1,0:T(8,128)S(1)} %get-tuple-element.20.refs_1_.refs_0_.refs_2_, bf16[128,768]{1,0:T(8,128)(2,1)S(1)} %collective-permute-done.10.refs_2_, ...), custom_call_target="tpu_custom_call" | custom-call | flops 2113929216 | bytes 1048576 | tf_op jit(solution)/shard_map/pallas_call | solution.py:377
  39.8 1.3 %collective-permute-done.13.refs_2_ = bf16[128,768]{1,0:T(8,128)(2,1)S(1)} collective-permute-done((bf16[128,768]{1,0:T(8,128)(2,1)S(1)}, bf16[128,768]{1,0:T(8,128)(2,1)S(1)}, u32[]{:S(2)}, u32[]{:S(2)}) %collective-permute-start.13) | collective-permute-done | bytes 196640 | tf_op jit(solution)/shard_map/ppermute | solution.py:287
  41.1 0.0 copy-start
  41.2 1.8 %shard_map.127 = (f32[8,960]{1,0:T(8,128)S(1)}, f32[8,960]{1,0:T(8,128)S(1)}) custom-call(s32[8,128]{1,0:T(8,128)S(1)} %get-tuple-element.20.refs_1_.refs_0_.refs_2_, bf16[128,768]{1,0:T(8,128)(2,1)S(1)} %collective-permute-done.refs_1_, bf16[128,768]{1,0:T(8,128)(2,1)S(1)} %collective-permute-done.13.refs_2_, ...), custom_call_target="tpu_custom_call" | custom-call | flops 1056964608 | bytes 1048576 | tf_op jit(solution)/shard_map/pallas_call | solution.py:407
  42.9 2.0 %collective-permute-done.9.refs_4_ = bf16[128,768]{1,0:T(8,128)(2,1)S(1)} collective-permute-done((bf16[128,768]{1,0:T(8,128)(2,1)S(1)}, bf16[128,768]{1,0:T(8,128)(2,1)S(1)}, u32[]{:S(2)}, u32[]{:S(2)}) %collective-permute-start.9) | collective-permute-done | bytes 196640 | tf_op jit(solution)/shard_map/ppermute | solution.py:287
  44.9 0.0 copy-done
  44.9 2.7 %shard_map.128 = bf16[16,48,128]{2,1,0:T(8,128)(2,1)S(1)} custom-call(s32[1]{0:T(128)} %bitcast.refs_0_, s32[8,128]{1,0:T(8,128)S(1)} %get-tuple-element.20.refs_1_.refs_0_.refs_2_, s32[8,128]{1,0:T(8,128)S(1)} %get-tuple-element.20.refs_1_.refs_0_.refs_2_, bf16[128,768]{1,0:T(8,128)(2,1)S(1)} %collective-permute-done.1.refs_3_, ...), custom_call_target="tpu_custom_call" | custom-call | flops 1056964608 | bytes 1048576 | tf_op jit(solution)/shard_map/pallas_call | solution.py:415
  47.6 12.6 %all_to_all.5 = bf16[16,48,128]{2,1,0:T(8,128)(2,1)S(1)} all-to-all(bf16[16,48,128]{2,1,0:T(8,128)(2,1)S(1)} %shard_map.128), channel_id=1, replica_groups=mesh['groups'=2,'doc'=16,'term'=1] {'doc'}, dimensions={0} | all-to-all | bytes 393216 | tf_op jit(solution)/shard_map/all_to_all | solution.py:437
  60.3 0.7 %slice.26 = bf16[2,15360]{1,0:T(2,128)(2,1)} reshape(bf16[2,8,15,128]{3,2,1,0:T(8,128)(2,1)S(1)} %slice.30) | data formatting | bytes 122880 | tf_op jit(solution)/shard_map/slice | solution.py:440
  61.0 0.6 %slice.24 = bf16[1,15360]{1,0:T(2,128)(2,1)} reshape(bf16[1,8,15,128]{3,2,1,0:T(8,128)(2,1)S(1)} %slice.29) | data formatting | bytes 61440 | tf_op jit(solution)/shard_map/slice | solution.py:440
  (7 shorter events, 0.1 us)
Async XLA Ops:
  0.6 14.3 %collective-permute-start.5 = (bf16[960,768]{1,0:T(8,128)(2,1)}, bf16[960,768]{1,0:T(8,128)(2,1)S(1)}, u32[]{:S(2)}, u32[]{:S(2)}) collective-permute-start(bf16[960,768]{1,0:T(8,128)(2,1)} %bitcast.14), channel_id=1, source_target_pairs={{0,1},{1,0},{2,3},{3,2},{4,5},{5,4},{6,7},{7,6},{8,9},{9,8},{10,11... | collective-permute-start | bytes 4423688 | tf_op jit(solution)/shard_map/ppermute | solution.py:290
  3.4 8.0 %collective-permute-start.2 = (bf16[48,896]{1,0:T(8,128)(2,1)S(1)}, bf16[48,896]{1,0:T(8,128)(2,1)S(1)}, u32[]{:S(2)}, u32[]{:S(2)}) collective-permute-start(bf16[48,896]{1,0:T(8,128)(2,1)S(1)} %get-tuple-element.17.refs_0_), channel_id=1, source_target_pairs={{0,4},{1,5},{2,6},{3,7},{4,0},{5,1},{6,2},{7,3},{8,12},{9,13},{10,... | collective-permute-start | bytes 258056 | tf_op jit(solution)/shard_map/ppermute | solution.py:287
  6.1 8.9 %collective-permute-start.4 = (bf16[128,768]{1,0:T(8,128)(2,1)}, bf16[128,768]{1,0:T(8,128)(2,1)S(1)}, u32[]{:S(2)}, u32[]{:S(2)}) collective-permute-start(bf16[128,768]{1,0:T(8,128)(2,1)} %refs_5_.1), channel_id=1, source_target_pairs={{0,2},{1,3},{2,0},{3,1},{4,6},{5,7},{6,4},{7,5},{8,10},{9,11},{10,... | collective-permute-start | bytes 589832 | tf_op jit(solution)/shard_map/ppermute | solution.py:287
  7.6 6.4 %collective-permute-start.3 = (bf16[48,896]{1,0:T(8,128)(2,1)S(1)}, bf16[48,896]{1,0:T(8,128)(2,1)S(1)}, u32[]{:S(2)}, u32[]{:S(2)}) collective-permute-start(bf16[48,896]{1,0:T(8,128)(2,1)S(1)} %get-tuple-element.17.refs_0_), channel_id=1, source_target_pairs={{0,12},{1,13},{2,14},{3,15},{4,8},{5,9},{6,10},{7,11},{8,4},{9,5},... | collective-permute-start | bytes 258056 | tf_op jit(solution)/shard_map/ppermute | solution.py:287
  10.0 10.1 %collective-permute-start = (bf16[128,768]{1,0:T(8,128)(2,1)}, bf16[128,768]{1,0:T(8,128)(2,1)S(1)}, u32[]{:S(2)}, u32[]{:S(2)}) collective-permute-start(bf16[128,768]{1,0:T(8,128)(2,1)} %refs_5_.1), channel_id=1, source_target_pairs={{0,12},{1,13},{2,14},{3,15},{4,8},{5,9},{6,10},{7,11},{8,4},{9,5},... | collective-permute-start | bytes 589832 | tf_op jit(solution)/shard_map/ppermute | solution.py:287
  11.4 12.2 %collective-permute-start.10 = (bf16[128,768]{1,0:T(8,128)(2,1)}, bf16[128,768]{1,0:T(8,128)(2,1)S(1)}, u32[]{:S(2)}, u32[]{:S(2)}) collective-permute-start(bf16[128,768]{1,0:T(8,128)(2,1)} %refs_5_.1), channel_id=1, source_target_pairs={{0,4},{1,5},{2,6},{3,7},{4,0},{5,1},{6,2},{7,3},{8,12},{9,13},{10,... | collective-permute-start | bytes 589832 | tf_op jit(solution)/shard_map/ppermute | solution.py:287
  13.9 10.2 %collective-permute-start.7 = (bf16[96,896]{1,0:T(8,128)(2,1)S(1)}, bf16[96,896]{1,0:T(8,128)(2,1)S(1)}, u32[]{:S(2)}, u32[]{:S(2)}) collective-permute-start(bf16[96,896]{1,0:T(8,128)(2,1)S(1)} %shard_map.123), channel_id=1, source_target_pairs={{0,2},{1,3},{2,0},{3,1},{4,6},{5,7},{6,4},{7,5},{8,10},{9,11},{10,... | collective-permute-start | bytes 516104 | tf_op jit(solution)/shard_map/ppermute | solution.py:287
  15.0 5.2 %copy-start.1 = (bf16[128,768]{1,0:T(8,128)(2,1)}, bf16[128,768]{1,0:T(8,128)(2,1)S(1)}, u32[]{:S(2)}) copy-start(bf16[128,768]{1,0:T(8,128)(2,1)S(1)} %collective-permute-done.4.refs_4_) | copy-start | bytes 589828
  15.0 9.4 %collective-permute-start.6 = (bf16[48,896]{1,0:T(8,128)(2,1)S(1)}, bf16[48,896]{1,0:T(8,128)(2,1)S(1)}, u32[]{:S(2)}, u32[]{:S(2)}) collective-permute-start(bf16[48,896]{1,0:T(8,128)(2,1)S(1)} %collective-permute-done.3.refs_0_.refs_2_), channel_id=1, source_target_pairs={{0,4},{1,5},{2,6},{3,7},{4,0},{5,1},{6,2},{7,3},{8,12},{9,13},{10,... | collective-permute-start | bytes 258056 | tf_op jit(solution)/shard_map/ppermute | solution.py:287
  20.2 8.2 %collective-permute-start.1 = (bf16[128,768]{1,0:T(8,128)(2,1)S(1)}, bf16[128,768]{1,0:T(8,128)(2,1)S(1)}, u32[]{:S(2)}, u32[]{:S(2)}) collective-permute-start(bf16[128,768]{1,0:T(8,128)(2,1)S(1)} %collective-permute-done.refs_1_), channel_id=1, source_target_pairs={{0,4},{1,5},{2,6},{3,7},{4,0},{5,1},{6,2},{7,3},{8,12},{9,13},{10,... | collective-permute-start | bytes 589832 | tf_op jit(solution)/shard_map/ppermute | solution.py:287
  23.6 9.7 %collective-permute-start.11 = (bf16[128,768]{1,0:T(8,128)(2,1)S(1)}, bf16[128,768]{1,0:T(8,128)(2,1)S(1)}, u32[]{:S(2)}, u32[]{:S(2)}) collective-permute-start(bf16[128,768]{1,0:T(8,128)(2,1)S(1)} %collective-permute-done.10.refs_2_), channel_id=1, source_target_pairs={{0,2},{1,3},{2,0},{3,1},{4,6},{5,7},{6,4},{7,5},{8,10},{9,11},{10,... | collective-permute-start | bytes 589832 | tf_op jit(solution)/shard_map/ppermute | solution.py:287
  24.4 8.8 %collective-permute-start.8 = (bf16[96,896]{1,0:T(8,128)(2,1)S(1)}, bf16[96,896]{1,0:T(8,128)(2,1)S(1)}, u32[]{:S(2)}, u32[]{:S(2)}) collective-permute-start(bf16[96,896]{1,0:T(8,128)(2,1)S(1)} %shard_map.124), channel_id=1, source_target_pairs={{0,2},{1,3},{2,0},{3,1},{4,6},{5,7},{6,4},{7,5},{8,10},{9,11},{10,... | collective-permute-start | bytes 516104 | tf_op jit(solution)/shard_map/ppermute | solution.py:287
  33.3 2.2 %collective-permute-start.12 = (bf16[384,768]{1,0:T(8,128)(2,1)S(1)}, bf16[384,768]{1,0:T(8,128)(2,1)S(1)}, u32[]{:S(2)}, u32[]{:S(2)}) collective-permute-start(bf16[384,768]{1,0:T(8,128)(2,1)S(1)} %get-tuple-element.22.refs_6_), channel_id=1, source_target_pairs={{0,1},{1,0},{2,3},{3,2},{4,5},{5,4},{6,7},{7,6},{8,9},{9,8},{10,11... | collective-permute-start | bytes 1769480 | tf_op jit(solution)/shard_map/ppermute | solution.py:290
  33.4 7.8 %collective-permute-start.13 = (bf16[128,768]{1,0:T(8,128)(2,1)S(1)}, bf16[128,768]{1,0:T(8,128)(2,1)S(1)}, u32[]{:S(2)}, u32[]{:S(2)}) collective-permute-start(bf16[128,768]{1,0:T(8,128)(2,1)S(1)} %collective-permute-done.refs_1_), channel_id=1, source_target_pairs={{0,2},{1,3},{2,0},{3,1},{4,6},{5,7},{6,4},{7,5},{8,10},{9,11},{10,... | collective-permute-start | bytes 589832 | tf_op jit(solution)/shard_map/ppermute | solution.py:287
  34.2 10.7 %collective-permute-start.9 = (bf16[128,768]{1,0:T(8,128)(2,1)S(1)}, bf16[128,768]{1,0:T(8,128)(2,1)S(1)}, u32[]{:S(2)}, u32[]{:S(2)}) collective-permute-start(bf16[128,768]{1,0:T(8,128)(2,1)S(1)} %collective-permute-done.1.refs_3_), channel_id=1, source_target_pairs={{0,2},{1,3},{2,0},{3,1},{4,6},{5,7},{6,4},{7,5},{8,10},{9,11},{10,... | collective-permute-start | bytes 589832 | tf_op jit(solution)/shard_map/ppermute | solution.py:287
  41.1 3.8 %copy-start = (f32[15360]{0:T(1024)S(1)}, f32[15360]{0:T(1024)}, u32[]{:S(2)}) copy-start(f32[15360]{0:T(1024)} %param.18) | copy-start | bytes 184324

commit v8 on v7

--- a/solution.py
+++ b/solution.py
@@ -102,15 +102,16 @@
     )
 
 
-def masked(ref, length):
-    here = ref[...]
+def masked(ref, seq, length):
+    here = ref[0:seq, :]
     keep = lax.broadcasted_iota(jnp.int32, here.shape, 0).astype(jnp.float32) < length
     first = jnp.broadcast_to(here[0:1, :].astype(jnp.float32), here.shape).astype(here.dtype)
     return jnp.where(keep, here, first)
 
 
-def normed_rows(docs, lengths, weight, params):
-    rows = jnp.concatenate([masked(ref, length) for ref, length in zip(docs, lengths)], axis=0)
+def normed_rows(docs, seq, lengths, weight, params):
+    masks = [masked(ref, seq, length) for ref, length in zip(docs, lengths)]
+    rows = jnp.concatenate(masks, axis=0)
     pre = jnp.dot(rows, weight[...], preferred_element_type=jnp.float32) + params[0:1, :]
     act = 0.5 * pre * (1.0 + lax.erf(pre * (0.5**0.5)))
     return layer_norm(act.astype(jnp.bfloat16), params[1:2, :], params[2:3, :])
@@ -125,18 +126,26 @@
 
 
 def start_kernel(tiles_ref, owners_ref, slots_ref, length_ref, *refs):
-    weight_ref, vectors, (out_ref, rows_ref, kept, sems) = refs[0], refs[1:4], refs[4:]
-    rows, width = weight_ref.shape
-    copies = [fetch(weight_ref, out_ref.at[:, pl.ds(0, width)], sems.at[0])]
+    hidden_ref, weight_ref, vectors = refs[0], refs[1], refs[2:5]
+    load_ref, block_ref, rows_ref, kept, sems = refs[5:]
+    seq, (rows, width) = hidden_ref.shape[0], weight_ref.shape
+    copies = [
+        fetch(weight_ref, block_ref.at[:, pl.ds(0, width)], sems.at[0]),
+        fetch(weight_ref, load_ref.at[pl.ds(seq, rows), :], sems.at[1]),
+        fetch(hidden_ref, load_ref.at[pl.ds(0, seq), :], sems.at[2]),
+    ]
     for k, ref in enumerate(vectors):
-        copies.append(fetch(ref, kept.at[pl.ds(k * width, width)], sems.at[1 + k]))
+        copies.append(fetch(ref, kept.at[pl.ds(k * width, width)], sems.at[3 + k]))
     lane = lax.broadcasted_iota(jnp.int32, (rows, TILE), 1)
     table = jnp.where(lane == TILE - 1, length_ref[0], -1)
     devices = lax.axis_size("doc")
     for k in range(tiles_ref.shape[2]):
         block = slots_ref[0, 0, k] * devices + owners_ref[0, 0, k]
         table = jnp.where(lane == tiles_ref[0, 0, k], block, table)
-    out_ref[:, width:] = table.astype(jnp.float32).astype(jnp.bfloat16)
+    table = table.astype(jnp.float32).astype(jnp.bfloat16)
+    block_ref[:, width:] = table
+    for first in range(0, width, TILE):
+        load_ref[seq + rows :, first : first + TILE] = table[0:SLOT_ROWS]
     for copy in copies:
         copy.wait()
     for k in range(len(vectors)):
@@ -150,17 +159,24 @@
         at += ref.shape[0]
 
 
-def pack_kernel(*refs):
+def pack_kernel(seq, *refs):
     arrays, out_ref, meta_ref = refs[:-2], refs[-2], refs[-1]
-    rows, width = arrays[0].shape[0], out_ref.shape[1]
+    width = out_ref.shape[1]
+    rows = out_ref.shape[0] // meta_ref.shape[0]
     row = lax.broadcasted_iota(jnp.int32, meta_ref.shape, 0)
     tables = jnp.zeros(meta_ref.shape, jnp.float32)
     k = 0
     for ref in arrays:
-        for first in range(0, ref.shape[0], rows):
-            out_ref[k * rows : (k + 1) * rows, :] = ref[first : first + rows, 0:width]
-            table = ref[first : first + SLOT_ROWS, width:].astype(jnp.float32)
-            tables = jnp.where(row == k, table[0 : meta_ref.shape[0]], tables)
+        if ref.shape[1] == width:
+            parts = [(ref[seq : seq + rows, :], ref[seq + rows : seq + rows + SLOT_ROWS, 0:TILE])]
+        else:
+            parts = [
+                (ref[first : first + rows, 0:width], ref[first : first + SLOT_ROWS, width:])
+                for first in range(0, ref.shape[0], rows)
+            ]
+        for part, table in parts:
+            out_ref[k * rows : (k + 1) * rows, :] = part
+            tables = jnp.where(row == k, table.astype(jnp.float32)[0 : meta_ref.shape[0]], tables)
             k += 1
     meta_ref[...] = tables.astype(jnp.int32)
 
@@ -175,14 +191,12 @@
     return meta_ref[k : k + 1, TILE - 1 : TILE].astype(jnp.float32)
 
 
-def first_kernel(masks, order, *refs):
+def first_kernel(seq, masks, order, *refs):
     (me_ref, meta_ref), refs = refs[:2], refs[2:]
     docs, refs = refs[: len(order)], refs[len(order) :]
-    packed, refs = refs[:2], refs[2:]
-    params, mine_ref, theirs_ref, refs = refs[0], refs[1], refs[2], refs[3:]
-    best_refs, weight, mine, late, sems = refs[:2], refs[2], refs[3], *refs[4:]
-    mine_copy = fetch(mine_ref, mine, sems.at[0])
-    late_copies = [fetch(docs[k - 2], late.at[k], sems.at[1 + k]) for k in range(2)]
+    packed, params, mine_ref, theirs_ref, refs = refs[:2], refs[2], refs[3], refs[4], refs[5:]
+    best_mine, best_theirs, weight, mine, sem = refs
+    copy = fetch(mine_ref, mine, sem)
     me = me_ref[0]
     core = me % 2
     rows = weight.shape[0] // (2 * len(masks))
@@ -193,32 +207,28 @@
         weight[pl.ds(at, rows), :] = packed[0][block, :]
         at = pl.multiple_of((2 * chip + 1 - core) * rows, SLOT_ROWS)
         weight[pl.ds(at, rows), :] = packed[1][block, :]
-    docs = [*docs[:-2], late.at[0], late.at[1]]
     for first in range(0, len(order), 2):
-        if first + 2 == len(order):
-            for copy in late_copies:
+        lengths = [length_of(meta_ref, masks.index(m)) for m in order[first : first + 2]]
+        normed = normed_rows(docs[first : first + 2], seq, lengths, weight, params)
+        for w_ref, best in ((theirs_ref, best_theirs), (mine, best_mine)):
+            if first == 0 and w_ref is mine:
                 copy.wait()
-        lengths = [length_of(meta_ref, masks.index(m)) for m in order[first : first + 2]]
-        normed = normed_rows(docs[first : first + 2], lengths, weight, params)
-        if first == 0:
-            mine_copy.wait()
-        for w_ref, best in zip((mine, theirs_ref), best_refs):
             for j, top in enumerate(tops_of(normed, w_ref, 2)):
                 best[first + j : first + j + 1, :] = top
 
 
-def next_kernel(masks, order, *refs):
+def next_kernel(seq, masks, order, *refs):
     meta_ref, refs = refs[0], refs[1:]
     docs, weight, params, refs = refs[:2], refs[2], refs[3], refs[4:]
     halves, best_refs = refs[:2], refs[2:]
     lengths = [length_of(meta_ref, masks.index(m)) for m in order]
-    normed = normed_rows(docs, lengths, weight, params)
+    normed = normed_rows(docs, seq, lengths, weight, params)
     for w_ref, best in zip(halves, best_refs):
         for j, top in enumerate(tops_of(normed, w_ref, 2)):
             best[j : j + 1, :] = top
 
 
-def last_kernel(masks, orders, *refs):
+def last_kernel(seq, masks, orders, *refs):
     me_ref, table_ref, meta_ref, refs = refs[0], refs[1], refs[2], refs[3:]
     docs, weight, params, refs = refs[:2], refs[2], refs[3], refs[4:]
     halves, dbias_ref, refs = refs[:2], refs[2], refs[3:]
@@ -230,7 +240,7 @@
     devices = 2 * len(masks)
     tiles = 2 * halves[0].shape[0] // TILE
     lengths = [length_of(meta_ref, masks.index(m)) for m in orders[-1]]
-    normed = normed_rows(docs, lengths, weight, params)
+    normed = normed_rows(docs, seq, lengths, weight, params)
     found = []
     for k, w_ref in enumerate(halves):
         parts = [earlier[2 * n + k][0:count, :] for n, count in enumerate(counts)]
@@ -311,17 +321,18 @@
     def after(value, *done):
         return lax.optimization_barrier((value, *done))[0]
 
-    block, params = pl.pallas_call(
+    load, block, params = pl.pallas_call(
         start_kernel,
         out_shape=[
+            shape((seq + rows + SLOT_ROWS, width), jnp.bfloat16),
             shape((rows, width + TILE), jnp.bfloat16),
             shape((8, width), jnp.float32),
         ],
-        in_specs=[smem] * 4 + [hbm] * 4,
-        out_specs=[vmem] * 2,
+        in_specs=[smem] * 4 + [hbm] * 5,
+        out_specs=[vmem] * 3,
         scratch_shapes=[
             pltpu.VMEM((3 * width,), jnp.float32),
-            pltpu.SemaphoreType.DMA((4,)),
+            pltpu.SemaphoreType.DMA((6,)),
         ],
         compiler_params=limit,
     )(
@@ -329,6 +340,7 @@
         stay(owner_ids[..., 0]),
         stay(block_slots),
         doc_lengths,
+        stay(hidden_states),
         stay(transform_weight),
         stay(transform_bias),
         stay(norm_gain),
@@ -346,66 +358,57 @@
 
     weight_rows = jnp.swapaxes(decoder_weight[0], 0, 1)
     theirs = swap(weight_rows)
-    docs = {0: hidden_states, 1: cross(hidden_states, 1)}
     block_6 = cross(block, 6)
-    block_2 = cross(block, 2)
-    docs[6] = cross(hidden_states, 6)
-    docs[2] = cross(hidden_states, 2)
-    near_pile = cross(pile(block, block_2), 1)
-    block_4 = cross(after(block_6, docs[1], theirs), 2)
+    docs = {0: load, 2: cross(load, 2), 1: cross(load, 1)}
+    block_4 = cross(block_6, 2)
+    docs[6] = cross(after(hidden_states, block_6), 6)
+    docs[3] = cross(after(docs[2], block_6), 1)
+    far_pile = cross(pile(block_6, after(block_4, docs[1], docs[2], theirs)), 1)
     docs[4] = cross(docs[6], 2)
-    docs[3] = cross(docs[2], 1)
-    far_pile = cross(pile(block_6, after(block_4, near_pile)), 1)
     docs[7] = cross(docs[6], 1)
     docs[5] = cross(docs[4], 1)
-    masks = [0, 2, 6, 4, 1, 3, 7, 5]
+    masks = [0, 1, 2, 3, 6, 4, 7, 5]
     packed, meta = pl.pallas_call(
-        pack_kernel,
+        lambda *refs: pack_kernel(seq, *refs),
         out_shape=[
             shape((chips * rows, width), jnp.bfloat16),
             shape((chips, TILE), jnp.int32),
         ],
-        in_specs=[vmem] * 6,
+        in_specs=[vmem] * 7,
         out_specs=[vmem] * 2,
         compiler_params=limit,
-    )(after(block, docs[4]), block_2, block_6, block_4, near_pile, far_pile)
+    )(docs[0], docs[1], docs[2], docs[3], after(block_6, docs[6]), block_4, far_pile)
     other_packed = swap(after(packed, docs[3]))
 
     orders = [[2, 3, 1, 0], [6, 7], [4, 5]]
     where = me[None]
     best_shape = shape((8, half), jnp.float32)
     *best, weight, mine = pl.pallas_call(
-        lambda *refs: first_kernel(masks, orders[0], *refs),
+        lambda *refs: first_kernel(seq, masks, orders[0], *refs),
         out_shape=[
             best_shape,
             best_shape,
             shape((width, width), jnp.bfloat16),
             shape((half, width), jnp.bfloat16),
         ],
-        in_specs=[smem] + [vmem] * 3 + [hbm] * 2 + [vmem] * 3 + [hbm, vmem],
+        in_specs=[smem] + [vmem] * 8 + [hbm, vmem],
         out_specs=[vmem] * 4,
-        scratch_shapes=[
-            pltpu.VMEM((2, seq, width), jnp.bfloat16),
-            pltpu.SemaphoreType.DMA((3,)),
-        ],
+        scratch_shapes=[pltpu.SemaphoreType.DMA],
         compiler_params=limit,
         cost_estimate=cost(len(orders[0])),
     )(
         where,
         meta,
-        docs[2],
-        docs[3],
-        stay(docs[1]),
-        stay(hidden_states),
+        *[docs[mask] for mask in orders[0]],
         packed,
-        other_packed,
+        after(other_packed, docs[4]),
         params,
         stay(weight_rows),
         theirs,
     )
     for order in orders[1:-1]:
         best += pl.pallas_call(
-            lambda *refs, order=order: next_kernel(masks, order, *refs),
+            lambda *refs, order=order: next_kernel(seq, masks, order, *refs),
             out_shape=[best_shape] * 2,
             in_specs=[vmem] * 7,
             out_specs=[vmem] * 2,
@@ -413,7 +416,7 @@
             cost_estimate=cost(2),
         )(meta, *[docs[mask] for mask in order], weight, params, mine, theirs)
     send = pl.pallas_call(
-        lambda *refs: last_kernel(masks, orders, *refs),
+        lambda *refs: last_kernel(seq, masks, orders, *refs),
         out_shape=shape((devices, (1 + BLK_DEV) * SLOT_ROWS, TILE), jnp.bfloat16),
         in_specs=[smem] * 2 + [vmem] * (8 + len(best)),
         out_specs=vmem,

time: 61.9 us -> 65 us (1.050)
  waiting for transfers between devices: 13.6 us -> 26.5 us
  starting transfers between devices: 22.2 us -> 11.9 us
  Pallas kernels: 10.5 us -> 12 us
  blocking collectives: 12.6 us -> 11.7 us
    ppermute x12 -> x10, waiting for transfers between devices: 13.6 us -> 26.5 us  [cross(): lax.ppermute(value, 'doc', [(i, i ^ 2 * mask) for i in range(devices)])]
    ppermute x12 -> x10, starting transfers between devices: 21.6 us -> 11.4 us  [cross(): lax.ppermute(value, 'doc', [(i, i ^ 2 * mask) for i in range(devices)])]
    pallas_call x5, Pallas kernels: 10.5 us -> 12 us  [the longest x1 4.93 us: move_tokens(): pl.pallas_call(lambda *refs: first_kernel(seq, masks, orders[0], *refs),...]
    all_to_all x1, blocking collectives: 12.6 us -> 11.7 us  [move_tokens(): got = lax.all_to_all(send, 'doc', split_axis=0, concat_axis=0, tiled=True)]
  transfers between devices with their start and end apart: 14 -> 12, of which waited for: 6 -> 4; matrix products, arithmetic and copies ran while one was open for 0% -> 0% of each run, Pallas kernels for 13% -> 13%
where the time goes in v8:
time: 65 us; the launch traced here: 64.8 us
  waiting for transfers between devices  26.5 us (41%)
  Pallas kernels  12 us (18%)
  starting transfers between devices  11.9 us (18%)
  blocking collectives  11.7 us (18%)
  between operations  1.39 us (2%)
  local copies, waits for them, and re-layouts  1.33 us (2%)
    ppermute x10, waiting for transfers between devices, cross(): lax.ppermute(value, 'doc', [(i, i ^ 2 * mask) for i in range(devices)])  26.5 us
    all_to_all x1, blocking collectives, move_tokens(): got = lax.all_to_all(send, 'doc', split_axis=0, concat_axis=0, tiled=True)  11.7 us
    ppermute x10, starting transfers between devices, cross(): lax.ppermute(value, 'doc', [(i, i ^ 2 * mask) for i in range(devices)])  11.4 us
    pallas_call x1, Pallas kernels, move_tokens(): pl.pallas_call(lambda *refs: first_kernel(seq, masks, orders[0], *refs),...  4.93 us
    pallas_call x1, Pallas kernels, move_tokens(): pl.pallas_call(lambda *refs: last_kernel(seq, masks, orders, *refs), out_...  2.68 us
    pallas_call x1, Pallas kernels, move_tokens(): pl.pallas_call(lambda *refs, order=order: next_kernel(seq, masks, order,...  1.77 us
    pallas_call x1, Pallas kernels, move_tokens(): pl.pallas_call(start_kernel, out_shape=[shape((seq + rows + SLOT_ROWS, wi...  1.74 us
    slice x4, local copies, waits for them, and re-layouts, move_tokens(): return (whole[:1], whole[1:])  1.31 us
  transfers between devices with their start and end apart: 12, of which 4 were waited for; matrix products, arithmetic and copies ran while one was open for 0% of the time, Pallas kernels for 13%

profile of v8, /device:TPU:0, one launch (start us, length us, event | category | flops | bytes accessed | tf_op | source)
XLA Modules:
  0.0 64.8 jit_solution(3722407712820148001)
XLA Ops:
  0.6 0.5 collective-permute-start.6
  1.8 1.7 %shard_map.122 = (bf16[192,768]{1,0:T(8,128)(2,1)S(1)}, bf16[48,896]{1,0:T(8,128)(2,1)S(1)}, f32[8,768]{1,0:T(8,128)S(1)}) custom-call(s32[1,1,32]{2,1,0:T(1,128)} %tiles_ref.1, s32[1,1,32]{2,1,0:T(1,128)} %bitcast.13, s32[1,1,32]{2,1,0:T(1,128)} %slots_ref.1, s32[1]{0:T(128)S(6)} %copy.22.length_ref, bf16[128,768]{1,0:T(8,128)(2,1)} %refs_0_.1, ...), custom_call_target="tpu_custom_call" | custom-call | tf_op jit(solution)/shard_map/pallas_call | solution.py:324
  3.5 2.6 %collective-permute-start.1 = (bf16[192,768]{1,0:T(8,128)(2,1)S(1)}, bf16[192,768]{1,0:T(8,128)(2,1)S(1)}, u32[]{:S(2)}, u32[]{:S(2)}) collective-permute-start(bf16[192,768]{1,0:T(8,128)(2,1)S(1)} %get-tuple-element.19.refs_0_.refs_5_), channel_id=1, source_target_pairs={{0,4},{1,5},{2,6},{3,7},{4,0},{5,1},{6,2},{7,3},{8,12},{9,13},{10,... | collective-permute-start | bytes 884744 | tf_op jit(solution)/shard_map/ppermute | solution.py:297
  6.2 1.5 %collective-permute-start = (bf16[192,768]{1,0:T(8,128)(2,1)S(1)}, bf16[192,768]{1,0:T(8,128)(2,1)S(1)}, u32[]{:S(2)}, u32[]{:S(2)}) collective-permute-start(bf16[192,768]{1,0:T(8,128)(2,1)S(1)} %get-tuple-element.19.refs_0_.refs_5_), channel_id=1, source_target_pairs={{0,2},{1,3},{2,0},{3,1},{4,6},{5,7},{6,4},{7,5},{8,10},{9,11},{10,... | collective-permute-start | bytes 884744 | tf_op jit(solution)/shard_map/ppermute | solution.py:297
  7.7 2.5 %collective-permute-start.2 = (bf16[48,896]{1,0:T(8,128)(2,1)S(1)}, bf16[48,896]{1,0:T(8,128)(2,1)S(1)}, u32[]{:S(2)}, u32[]{:S(2)}) collective-permute-start(bf16[48,896]{1,0:T(8,128)(2,1)S(1)} %get-tuple-element.20), channel_id=1, source_target_pairs={{0,12},{1,13},{2,14},{3,15},{4,8},{5,9},{6,10},{7,11},{8,4},{9,5},... | collective-permute-start | bytes 258056 | tf_op jit(solution)/shard_map/ppermute | solution.py:297
  10.2 7.7 %collective-permute-done.2.refs_0_.refs_4_ = bf16[48,896]{1,0:T(8,128)(2,1)S(1)} collective-permute-done((bf16[48,896]{1,0:T(8,128)(2,1)S(1)}, bf16[48,896]{1,0:T(8,128)(2,1)S(1)}, u32[]{:S(2)}, u32[]{:S(2)}) %collective-permute-start.2) | collective-permute-done | bytes 86048 | tf_op jit(solution)/shard_map/ppermute | solution.py:297
  17.9 0.0 collective-permute-done.1.refs_2_
  17.9 1.5 %collective-permute-start.3 = (bf16[192,768]{1,0:T(8,128)(2,1)S(1)}, bf16[192,768]{1,0:T(8,128)(2,1)S(1)}, u32[]{:S(2)}, u32[]{:S(2)}) collective-permute-start(bf16[192,768]{1,0:T(8,128)(2,1)S(1)} %collective-permute-done.1.refs_2_), channel_id=1, source_target_pairs={{0,2},{1,3},{2,0},{3,1},{4,6},{5,7},{6,4},{7,5},{8,10},{9,11},{10,... | collective-permute-start | bytes 884744 | tf_op jit(solution)/shard_map/ppermute | solution.py:297
  19.4 0.0 collective-permute-start.5
  19.4 1.6 %collective-permute-start.4 = (bf16[128,768]{1,0:T(8,128)(2,1)}, bf16[128,768]{1,0:T(8,128)(2,1)S(1)}, u32[]{:S(2)}, u32[]{:S(2)}) collective-permute-start(bf16[128,768]{1,0:T(8,128)(2,1)} %refs_0_.1), channel_id=1, source_target_pairs={{0,12},{1,13},{2,14},{3,15},{4,8},{5,9},{6,10},{7,11},{8,4},{9,5},... | collective-permute-start | bytes 589832 | tf_op jit(solution)/shard_map/ppermute | solution.py:297
  21.0 7.1 %collective-permute-done.5.refs_1_.refs_5_ = bf16[48,896]{1,0:T(8,128)(2,1)S(1)} collective-permute-done((bf16[48,896]{1,0:T(8,128)(2,1)S(1)}, bf16[48,896]{1,0:T(8,128)(2,1)S(1)}, u32[]{:S(2)}, u32[]{:S(2)}) %collective-permute-start.5) | collective-permute-done | bytes 86048 | tf_op jit(solution)/shard_map/ppermute | solution.py:297
  28.1 0.0 collective-permute-done.refs_1_.refs_4_
  28.1 0.0 collective-permute-done.6.refs_10_.refs_6_.refs_8_
  28.1 0.6 collective-permute-start.7
  28.7 0.0 collective-permute-done.4.refs_1_
  28.7 0.0 collective-permute-done.3.refs_3_
  28.7 4.9 %collective-permute-done.7.refs_6_ = bf16[96,896]{1,0:T(8,128)(2,1)S(1)} collective-permute-done((bf16[96,896]{1,0:T(8,128)(2,1)S(1)}, bf16[96,896]{1,0:T(8,128)(2,1)S(1)}, u32[]{:S(2)}, u32[]{:S(2)}) %collective-permute-start.7) | collective-permute-done | bytes 172064 | tf_op jit(solution)/shard_map/ppermute | solution.py:297
  33.6 0.9 %shard_map.124 = (bf16[384,768]{1,0:T(8,128)(2,1)}, s32[8,128]{1,0:T(8,128)S(1)}) custom-call(bf16[192,768]{1,0:T(8,128)(2,1)S(1)} %get-tuple-element.19.refs_0_.refs_5_, bf16[192,768]{1,0:T(8,128)(2,1)S(1)} %collective-permute-done.refs_1_.refs_4_, bf16[192,768]{1,0:T(8,128)(2,1)S(1)} %collective-permute-done.1.refs_2_, ...), custom_call_target="tpu_custom_call" | custom-call | tf_op jit(solution)/shard_map/pallas_call | solution.py:371
  34.5 0.0 collective-permute-start.10
  34.5 0.0 collective-permute-start.8
  34.5 0.5 collective-permute-start.11
  35.0 6.8 %collective-permute-done.8.refs_3_ = bf16[128,768]{1,0:T(8,128)(2,1)S(1)} collective-permute-done((bf16[128,768]{1,0:T(8,128)(2,1)S(1)}, bf16[128,768]{1,0:T(8,128)(2,1)S(1)}, u32[]{:S(2)}, u32[]{:S(2)}) %collective-permute-start.8) | collective-permute-done | bytes 196640 | tf_op jit(solution)/shard_map/ppermute | solution.py:297
  41.8 0.5 collective-permute-start.9
  42.3 0.0 collective-permute-done.10.refs_7_
  42.3 4.9 %shard_map.125 = (f32[8,960]{1,0:T(8,128)S(1)}, f32[8,960]{1,0:T(8,128)S(1)}, bf16[768,768]{1,0:T(8,128)(2,1)S(1)}, bf16[960,768]{1,0:T(8,128)(2,1)S(1)}) custom-call(s32[1]{0:T(128)} %bitcast.refs_0_, s32[8,128]{1,0:T(8,128)S(1)} %get-tuple-element.25.refs_1_.refs_0_.refs_2_, bf16[192,768]{1,0:T(8,128)(2,1)S(1)} %collective-permute-done.1.refs_2_, ...), custom_call_target="tpu_custom_call" | custom-call | flops 2113929216 | bytes 1048576 | tf_op jit(solution)/shard_map/pallas_call | solution.py:386
  47.3 0.0 collective-permute-done.11.refs_2_
  47.3 0.0 copy-start
  47.3 1.8 %shard_map.126 = (f32[8,960]{1,0:T(8,128)S(1)}, f32[8,960]{1,0:T(8,128)S(1)}) custom-call(s32[8,128]{1,0:T(8,128)S(1)} %get-tuple-element.25.refs_1_.refs_0_.refs_2_, bf16[128,768]{1,0:T(8,128)(2,1)S(1)} %collective-permute-done.4.refs_1_, bf16[128,768]{1,0:T(8,128)(2,1)S(1)} %collective-permute-done.11.refs_2_, ...), custom_call_target="tpu_custom_call" | custom-call | flops 1056964608 | bytes 1048576 | tf_op jit(solution)/shard_map/pallas_call | solution.py:410
  49.0 0.0 collective-permute-done.9.refs_4_
  49.1 0.0 copy-done
  49.1 2.7 %shard_map.127 = bf16[16,48,128]{2,1,0:T(8,128)(2,1)S(1)} custom-call(s32[1]{0:T(128)} %bitcast.refs_0_, s32[8,128]{1,0:T(8,128)S(1)} %get-tuple-element.25.refs_1_.refs_0_.refs_2_, s32[8,128]{1,0:T(8,128)S(1)} %get-tuple-element.25.refs_1_.refs_0_.refs_2_, bf16[128,768]{1,0:T(8,128)(2,1)S(1)} %collective-permute-done.8.refs_3_, ...), custom_call_target="tpu_custom_call" | custom-call | flops 1056964608 | bytes 1048576 | tf_op jit(solution)/shard_map/pallas_call | solution.py:418
  51.8 11.7 %all_to_all.5 = bf16[16,48,128]{2,1,0:T(8,128)(2,1)S(1)} all-to-all(bf16[16,48,128]{2,1,0:T(8,128)(2,1)S(1)} %shard_map.127), channel_id=1, replica_groups=mesh['groups'=2,'doc'=16,'term'=1] {'doc'}, dimensions={0} | all-to-all | bytes 393216 | tf_op jit(solution)/shard_map/all_to_all | solution.py:440
  63.5 0.7 %slice.26 = bf16[2,15360]{1,0:T(2,128)(2,1)} reshape(bf16[2,8,15,128]{3,2,1,0:T(8,128)(2,1)S(1)} %slice.30) | data formatting | bytes 122880 | tf_op jit(solution)/shard_map/slice | solution.py:443
  64.1 0.6 slice.24
  (5 shorter events, 0.1 us)
Async XLA Ops:
  0.6 27.5 %collective-permute-start.6 = (bf16[960,768]{1,0:T(8,128)(2,1)}, bf16[960,768]{1,0:T(8,128)(2,1)S(1)}, u32[]{:S(2)}, u32[]{:S(2)}) collective-permute-start(bf16[960,768]{1,0:T(8,128)(2,1)} %bitcast.14), channel_id=1, source_target_pairs={{0,1},{1,0},{2,3},{3,2},{4,5},{5,4},{6,7},{7,6},{8,9},{9,8},{10,11... | collective-permute-start | bytes 4423688 | tf_op jit(solution)/shard_map/ppermute | solution.py:300
  3.5 14.4 %collective-permute-start.1 = (bf16[192,768]{1,0:T(8,128)(2,1)S(1)}, bf16[192,768]{1,0:T(8,128)(2,1)S(1)}, u32[]{:S(2)}, u32[]{:S(2)}) collective-permute-start(bf16[192,768]{1,0:T(8,128)(2,1)S(1)} %get-tuple-element.19.refs_0_.refs_5_), channel_id=1, source_target_pairs={{0,4},{1,5},{2,6},{3,7},{4,0},{5,1},{6,2},{7,3},{8,12},{9,13},{10,... | collective-permute-start | bytes 884744 | tf_op jit(solution)/shard_map/ppermute | solution.py:297
  6.2 21.9 %collective-permute-start = (bf16[192,768]{1,0:T(8,128)(2,1)S(1)}, bf16[192,768]{1,0:T(8,128)(2,1)S(1)}, u32[]{:S(2)}, u32[]{:S(2)}) collective-permute-start(bf16[192,768]{1,0:T(8,128)(2,1)S(1)} %get-tuple-element.19.refs_0_.refs_5_), channel_id=1, source_target_pairs={{0,2},{1,3},{2,0},{3,1},{4,6},{5,7},{6,4},{7,5},{8,10},{9,11},{10,... | collective-permute-start | bytes 884744 | tf_op jit(solution)/shard_map/ppermute | solution.py:297
  7.7 10.2 %collective-permute-start.2 = (bf16[48,896]{1,0:T(8,128)(2,1)S(1)}, bf16[48,896]{1,0:T(8,128)(2,1)S(1)}, u32[]{:S(2)}, u32[]{:S(2)}) collective-permute-start(bf16[48,896]{1,0:T(8,128)(2,1)S(1)} %get-tuple-element.20), channel_id=1, source_target_pairs={{0,12},{1,13},{2,14},{3,15},{4,8},{5,9},{6,10},{7,11},{8,4},{9,5},... | collective-permute-start | bytes 258056 | tf_op jit(solution)/shard_map/ppermute | solution.py:297
  17.9 10.8 %collective-permute-start.3 = (bf16[192,768]{1,0:T(8,128)(2,1)S(1)}, bf16[192,768]{1,0:T(8,128)(2,1)S(1)}, u32[]{:S(2)}, u32[]{:S(2)}) collective-permute-start(bf16[192,768]{1,0:T(8,128)(2,1)S(1)} %collective-permute-done.1.refs_2_), channel_id=1, source_target_pairs={{0,2},{1,3},{2,0},{3,1},{4,6},{5,7},{6,4},{7,5},{8,10},{9,11},{10,... | collective-permute-start | bytes 884744 | tf_op jit(solution)/shard_map/ppermute | solution.py:297
  19.4 8.7 %collective-permute-start.5 = (bf16[48,896]{1,0:T(8,128)(2,1)S(1)}, bf16[48,896]{1,0:T(8,128)(2,1)S(1)}, u32[]{:S(2)}, u32[]{:S(2)}) collective-permute-start(bf16[48,896]{1,0:T(8,128)(2,1)S(1)} %collective-permute-done.2.refs_0_.refs_4_), channel_id=1, source_target_pairs={{0,4},{1,5},{2,6},{3,7},{4,0},{5,1},{6,2},{7,3},{8,12},{9,13},{10,... | collective-permute-start | bytes 258056 | tf_op jit(solution)/shard_map/ppermute | solution.py:297
  19.4 9.3 %collective-permute-start.4 = (bf16[128,768]{1,0:T(8,128)(2,1)}, bf16[128,768]{1,0:T(8,128)(2,1)S(1)}, u32[]{:S(2)}, u32[]{:S(2)}) collective-permute-start(bf16[128,768]{1,0:T(8,128)(2,1)} %refs_0_.1), channel_id=1, source_target_pairs={{0,12},{1,13},{2,14},{3,15},{4,8},{5,9},{6,10},{7,11},{8,4},{9,5},... | collective-permute-start | bytes 589832 | tf_op jit(solution)/shard_map/ppermute | solution.py:297
  28.1 5.5 %collective-permute-start.7 = (bf16[96,896]{1,0:T(8,128)(2,1)S(1)}, bf16[96,896]{1,0:T(8,128)(2,1)S(1)}, u32[]{:S(2)}, u32[]{:S(2)}) collective-permute-start(bf16[96,896]{1,0:T(8,128)(2,1)S(1)} %shard_map.123), channel_id=1, source_target_pairs={{0,2},{1,3},{2,0},{3,1},{4,6},{5,7},{6,4},{7,5},{8,10},{9,11},{10,... | collective-permute-start | bytes 516104 | tf_op jit(solution)/shard_map/ppermute | solution.py:297
  34.5 7.9 %collective-permute-start.10 = (bf16[384,768]{1,0:T(8,128)(2,1)}, bf16[384,768]{1,0:T(8,128)(2,1)}, u32[]{:S(2)}, u32[]{:S(2)}) collective-permute-start(bf16[384,768]{1,0:T(8,128)(2,1)} %get-tuple-element.27.refs_6_), channel_id=1, source_target_pairs={{0,1},{1,0},{2,3},{3,2},{4,5},{5,4},{6,7},{7,6},{8,9},{9,8},{10,11... | collective-permute-start | bytes 1769480 | tf_op jit(solution)/shard_map/ppermute | solution.py:300
  34.5 7.3 %collective-permute-start.8 = (bf16[128,768]{1,0:T(8,128)(2,1)S(1)}, bf16[128,768]{1,0:T(8,128)(2,1)S(1)}, u32[]{:S(2)}, u32[]{:S(2)}) collective-permute-start(bf16[128,768]{1,0:T(8,128)(2,1)S(1)} %collective-permute-done.4.refs_1_), channel_id=1, source_target_pairs={{0,4},{1,5},{2,6},{3,7},{4,0},{5,1},{6,2},{7,3},{8,12},{9,13},{10,... | collective-permute-start | bytes 589832 | tf_op jit(solution)/shard_map/ppermute | solution.py:297
  34.5 12.8 %collective-permute-start.11 = (bf16[128,768]{1,0:T(8,128)(2,1)S(1)}, bf16[128,768]{1,0:T(8,128)(2,1)S(1)}, u32[]{:S(2)}, u32[]{:S(2)}) collective-permute-start(bf16[128,768]{1,0:T(8,128)(2,1)S(1)} %collective-permute-done.4.refs_1_), channel_id=1, source_target_pairs={{0,2},{1,3},{2,0},{3,1},{4,6},{5,7},{6,4},{7,5},{8,10},{9,11},{10,... | collective-permute-start | bytes 589832 | tf_op jit(solution)/shard_map/ppermute | solution.py:297
  41.8 7.3 %collective-permute-start.9 = (bf16[128,768]{1,0:T(8,128)(2,1)S(1)}, bf16[128,768]{1,0:T(8,128)(2,1)S(1)}, u32[]{:S(2)}, u32[]{:S(2)}) collective-permute-start(bf16[128,768]{1,0:T(8,128)(2,1)S(1)} %collective-permute-done.8.refs_3_), channel_id=1, source_target_pairs={{0,2},{1,3},{2,0},{3,1},{4,6},{5,7},{6,4},{7,5},{8,10},{9,11},{10,... | collective-permute-start | bytes 589832 | tf_op jit(solution)/shard_map/ppermute | solution.py:297
  47.3 1.8 %copy-start = (f32[15360]{0:T(1024)S(1)}, f32[15360]{0:T(1024)}, u32[]{:S(2)}) copy-start(f32[15360]{0:T(1024)} %param.18) | copy-start | bytes 184324

commit v9 on v8

--- a/solution.py
+++ b/solution.py
@@ -102,16 +102,20 @@
     )
 
 
-def masked(ref, seq, length):
+def table_of(ref, seq):
+    return ref[seq : seq + SLOT_ROWS, 0:TILE].astype(jnp.float32)[0:1, :]
+
+
+def masked(ref, seq):
     here = ref[0:seq, :]
+    length = table_of(ref, seq)[:, TILE - 1 :]
     keep = lax.broadcasted_iota(jnp.int32, here.shape, 0).astype(jnp.float32) < length
     first = jnp.broadcast_to(here[0:1, :].astype(jnp.float32), here.shape).astype(here.dtype)
     return jnp.where(keep, here, first)
 
 
-def normed_rows(docs, seq, lengths, weight, params):
-    masks = [masked(ref, seq, length) for ref, length in zip(docs, lengths)]
-    rows = jnp.concatenate(masks, axis=0)
+def normed_rows(docs, seq, weight, params):
+    rows = jnp.concatenate([masked(ref, seq) for ref in docs], axis=0)
     pre = jnp.dot(rows, weight[...], preferred_element_type=jnp.float32) + params[0:1, :]
     act = 0.5 * pre * (1.0 + lax.erf(pre * (0.5**0.5)))
     return layer_norm(act.astype(jnp.bfloat16), params[1:2, :], params[2:3, :])
@@ -128,24 +132,22 @@
 def start_kernel(tiles_ref, owners_ref, slots_ref, length_ref, *refs):
     hidden_ref, weight_ref, vectors = refs[0], refs[1], refs[2:5]
     load_ref, block_ref, rows_ref, kept, sems = refs[5:]
-    seq, (rows, width) = hidden_ref.shape[0], weight_ref.shape
+    seq, width = hidden_ref.shape
     copies = [
-        fetch(weight_ref, block_ref.at[:, pl.ds(0, width)], sems.at[0]),
-        fetch(weight_ref, load_ref.at[pl.ds(seq, rows), :], sems.at[1]),
-        fetch(hidden_ref, load_ref.at[pl.ds(0, seq), :], sems.at[2]),
+        fetch(hidden_ref, load_ref.at[pl.ds(0, seq), :], sems.at[0]),
+        fetch(weight_ref, block_ref, sems.at[1]),
     ]
     for k, ref in enumerate(vectors):
-        copies.append(fetch(ref, kept.at[pl.ds(k * width, width)], sems.at[3 + k]))
-    lane = lax.broadcasted_iota(jnp.int32, (rows, TILE), 1)
+        copies.append(fetch(ref, kept.at[pl.ds(k * width, width)], sems.at[2 + k]))
+    lane = lax.broadcasted_iota(jnp.int32, (SLOT_ROWS, TILE), 1)
     table = jnp.where(lane == TILE - 1, length_ref[0], -1)
     devices = lax.axis_size("doc")
     for k in range(tiles_ref.shape[2]):
         block = slots_ref[0, 0, k] * devices + owners_ref[0, 0, k]
         table = jnp.where(lane == tiles_ref[0, 0, k], block, table)
     table = table.astype(jnp.float32).astype(jnp.bfloat16)
-    block_ref[:, width:] = table
     for first in range(0, width, TILE):
-        load_ref[seq + rows :, first : first + TILE] = table[0:SLOT_ROWS]
+        load_ref[seq:, first : first + TILE] = table
     for copy in copies:
         copy.wait()
     for k in range(len(vectors)):
@@ -159,43 +161,21 @@
         at += ref.shape[0]
 
 
-def pack_kernel(seq, *refs):
-    arrays, out_ref, meta_ref = refs[:-2], refs[-2], refs[-1]
-    width = out_ref.shape[1]
-    rows = out_ref.shape[0] // meta_ref.shape[0]
-    row = lax.broadcasted_iota(jnp.int32, meta_ref.shape, 0)
-    tables = jnp.zeros(meta_ref.shape, jnp.float32)
-    k = 0
-    for ref in arrays:
-        if ref.shape[1] == width:
-            parts = [(ref[seq : seq + rows, :], ref[seq + rows : seq + rows + SLOT_ROWS, 0:TILE])]
-        else:
-            parts = [
-                (ref[first : first + rows, 0:width], ref[first : first + SLOT_ROWS, width:])
-                for first in range(0, ref.shape[0], rows)
-            ]
-        for part, table in parts:
-            out_ref[k * rows : (k + 1) * rows, :] = part
-            tables = jnp.where(row == k, table.astype(jnp.float32)[0 : meta_ref.shape[0]], tables)
-            k += 1
-    meta_ref[...] = tables.astype(jnp.int32)
-
-
 def fetch(ref, slot, sem):
     copy = pltpu.make_async_copy(ref, slot, sem)
     copy.start()
     return copy
 
 
-def length_of(meta_ref, k):
-    return meta_ref[k : k + 1, TILE - 1 : TILE].astype(jnp.float32)
-
-
-def first_kernel(seq, masks, order, *refs):
-    (me_ref, meta_ref), refs = refs[:2], refs[2:]
-    docs, refs = refs[: len(order)], refs[len(order) :]
-    packed, params, mine_ref, theirs_ref, refs = refs[:2], refs[2], refs[3], refs[4], refs[5:]
-    best_mine, best_theirs, weight, mine, sem = refs
+def keep_tops(normed, halves, bests):
+    for w_ref, best in zip(halves, bests):
+        for j, top in enumerate(tops_of(normed, w_ref, 2)):
+            best[j : j + 1, :] = top
+
+
+def first_kernel(seq, masks, *refs):
+    me_ref, docs, packed, refs = refs[0], refs[1:3], refs[3:5], refs[5:]
+    params, mine_ref, theirs_ref, best_mine, best_theirs, weight, mine, sem = refs
     copy = fetch(mine_ref, mine, sem)
     me = me_ref[0]
     core = me % 2
@@ -207,51 +187,38 @@
         weight[pl.ds(at, rows), :] = packed[0][block, :]
         at = pl.multiple_of((2 * chip + 1 - core) * rows, SLOT_ROWS)
         weight[pl.ds(at, rows), :] = packed[1][block, :]
-    for first in range(0, len(order), 2):
-        lengths = [length_of(meta_ref, masks.index(m)) for m in order[first : first + 2]]
-        normed = normed_rows(docs[first : first + 2], seq, lengths, weight, params)
-        for w_ref, best in ((theirs_ref, best_theirs), (mine, best_mine)):
-            if first == 0 and w_ref is mine:
-                copy.wait()
-            for j, top in enumerate(tops_of(normed, w_ref, 2)):
-                best[first + j : first + j + 1, :] = top
-
-
-def next_kernel(seq, masks, order, *refs):
-    meta_ref, refs = refs[0], refs[1:]
-    docs, weight, params, refs = refs[:2], refs[2], refs[3], refs[4:]
-    halves, best_refs = refs[:2], refs[2:]
-    lengths = [length_of(meta_ref, masks.index(m)) for m in order]
-    normed = normed_rows(docs, seq, lengths, weight, params)
-    for w_ref, best in zip(halves, best_refs):
-        for j, top in enumerate(tops_of(normed, w_ref, 2)):
-            best[j : j + 1, :] = top
-
-
-def last_kernel(seq, masks, orders, *refs):
-    me_ref, table_ref, meta_ref, refs = refs[0], refs[1], refs[2], refs[3:]
-    docs, weight, params, refs = refs[:2], refs[2], refs[3], refs[4:]
-    halves, dbias_ref, refs = refs[:2], refs[2], refs[3:]
-    counts = [len(order) for order in orders[:-1]]
-    earlier, refs = refs[: 2 * len(counts)], refs[2 * len(counts) :]
-    out_ref, send = refs
+    normed = normed_rows(docs, seq, weight, params)
+    keep_tops(normed, [theirs_ref], [best_theirs])
+    copy.wait()
+    keep_tops(normed, [mine], [best_mine])
+
+
+def next_kernel(seq, *refs):
+    docs, weight, params, halves, bests = refs[:2], refs[2], refs[3], refs[4:6], refs[6:]
+    keep_tops(normed_rows(docs, seq, weight, params), halves, bests)
+
+
+def last_kernel(seq, masks, *refs):
+    me_ref, docs, refs = refs[0], refs[1 : 1 + len(masks)], refs[1 + len(masks) :]
+    weight, params, halves, dbias_ref, refs = refs[0], refs[1], refs[2:4], refs[4], refs[5:]
+    earlier, out_ref, send = refs[:-2], refs[-2], refs[-1]
     me = me_ref[0]
     core, chip = me % 2, me // 2
     devices = 2 * len(masks)
     tiles = 2 * halves[0].shape[0] // TILE
-    lengths = [length_of(meta_ref, masks.index(m)) for m in orders[-1]]
-    normed = normed_rows(docs, seq, lengths, weight, params)
+    normed = normed_rows(docs[-2:], seq, weight, params)
     found = []
     for k, w_ref in enumerate(halves):
-        parts = [earlier[2 * n + k][0:count, :] for n, count in enumerate(counts)]
+        parts = [ref[0:2, :] for ref in earlier[k::2]]
         found.append(jnp.concatenate([*parts, *tops_of(normed, w_ref, 2)], axis=0))
     low = jnp.where(core == 0, found[0], found[1])
     high = jnp.where(core == 0, found[1], found[0])
     logits = jnp.concatenate([low, high], axis=1)
-    order = [mask for group in orders for mask in group]
-    docs_at = [me ^ (2 * mask) for mask in order]
+    docs_at = [me ^ (2 * mask) for mask in masks]
     bias = dbias_ref[...]
     bias = pltpu.roll(bias, bias.shape[0] - chip * tiles, 0)
+    tables = jnp.concatenate([table_of(ref, seq) for ref in docs], axis=0)
+    tables = pltpu.roll(tables, TILE - chip * tiles, 1).astype(jnp.int32)
     send[...] = jnp.zeros(send.shape, jnp.float32)
     stride = out_ref.shape[1]
     target = lax.broadcasted_iota(jnp.int32, (BLK_DEV * devices, TILE), 0)
@@ -260,10 +227,10 @@
         impacts = jnp.log1p(jnp.maximum(logits[:, lanes] + bias[t : t + 1, :], 0.0))
         impacts = impacts.astype(jnp.bfloat16).astype(jnp.float32)
         blocks = jnp.zeros((BLK_DEV * devices, TILE), jnp.float32)
-        for n, mask in enumerate(order):
+        for n in range(len(masks)):
             row = impacts[n : n + 1, :]
             send[pl.ds(docs_at[n] * stride + t, 1), :] = row
-            block = table_ref[masks.index(mask), chip * tiles + t]
+            block = jnp.broadcast_to(tables[n : n + 1, t : t + 1], target.shape)
             blocks = jnp.maximum(blocks, jnp.where(target == block, row, 0.0))
         for s in range(BLK_DEV):
             send[pl.ds((1 + s) * SLOT_ROWS + t, devices, stride=stride), :] = blocks[
@@ -309,11 +276,7 @@
     limit = pltpu.CompilerParams(vmem_limit_bytes=24 * 1024 * 1024)
 
     def cost(docs):
-        return pl.CostEstimate(
-            flops=2 * docs * seq * width * (width + 2 * half),
-            bytes_accessed=1024 * 1024,
-            transcendentals=docs * seq * width,
-        )
+        return pl.CostEstimate(flops=docs, bytes_accessed=docs, transcendentals=0)
 
     def shape(dims, dtype):
         return jax.ShapeDtypeStruct(dims, dtype)
@@ -321,18 +284,32 @@
     def after(value, *done):
         return lax.optimization_barrier((value, *done))[0]
 
+    def pile(*values):
+        total = sum(value.shape[0] for value in values)
+        return pl.pallas_call(
+            pile_kernel,
+            out_shape=shape((total, values[0].shape[1]), values[0].dtype),
+            in_specs=[vmem] * len(values),
+            out_specs=vmem,
+            compiler_params=limit,
+        )(*values)
+
+    weight_rows = jnp.swapaxes(decoder_weight[0], 0, 1)
+    block_6 = cross(transform_weight, 6)
+    block_2 = cross(transform_weight, 2)
+    theirs = swap(weight_rows)
     load, block, params = pl.pallas_call(
         start_kernel,
         out_shape=[
-            shape((seq + rows + SLOT_ROWS, width), jnp.bfloat16),
-            shape((rows, width + TILE), jnp.bfloat16),
+            shape((seq + SLOT_ROWS, width), jnp.bfloat16),
+            shape((rows, width), jnp.bfloat16),
             shape((8, width), jnp.float32),
         ],
         in_specs=[smem] * 4 + [hbm] * 5,
         out_specs=[vmem] * 3,
         scratch_shapes=[
             pltpu.VMEM((3 * width,), jnp.float32),
-            pltpu.SemaphoreType.DMA((6,)),
+            pltpu.SemaphoreType.DMA((5,)),
         ],
         compiler_params=limit,
     )(
@@ -346,79 +323,58 @@
         stay(norm_gain),
         stay(norm_bias),
     )
-    def pile(*values):
-        total = sum(value.shape[0] for value in values)
-        return pl.pallas_call(
-            pile_kernel,
-            out_shape=shape((total, values[0].shape[1]), values[0].dtype),
-            in_specs=[vmem] * len(values),
-            out_specs=vmem,
-            compiler_params=limit,
-        )(*values)
-
-    weight_rows = jnp.swapaxes(decoder_weight[0], 0, 1)
-    theirs = swap(weight_rows)
-    block_6 = cross(block, 6)
-    docs = {0: load, 2: cross(load, 2), 1: cross(load, 1)}
+    docs = {0: load, 1: cross(after(load, block_6), 1)}
+    near_pile = cross(pile(block, block_2), 1)
     block_4 = cross(block_6, 2)
-    docs[6] = cross(after(hidden_states, block_6), 6)
-    docs[3] = cross(after(docs[2], block_6), 1)
-    far_pile = cross(pile(block_6, after(block_4, docs[1], docs[2], theirs)), 1)
+    docs[6] = cross(after(load, block_6), 6)
+    docs[2] = cross(after(load, block_4), 2)
+    far_pile = cross(pile(block_6, after(block_4, near_pile, docs[1])), 1)
+    docs[3] = cross(docs[2], 1)
     docs[4] = cross(docs[6], 2)
     docs[7] = cross(docs[6], 1)
-    docs[5] = cross(docs[4], 1)
-    masks = [0, 1, 2, 3, 6, 4, 7, 5]
-    packed, meta = pl.pallas_call(
-        lambda *refs: pack_kernel(seq, *refs),
-        out_shape=[
-            shape((chips * rows, width), jnp.bfloat16),
-            shape((chips, TILE), jnp.int32),
-        ],
-        in_specs=[vmem] * 7,
-        out_specs=[vmem] * 2,
-        compiler_params=limit,
-    )(docs[0], docs[1], docs[2], docs[3], after(block_6, docs[6]), block_4, far_pile)
-    other_packed = swap(after(packed, docs[3]))
-
-    orders = [[2, 3, 1, 0], [6, 7], [4, 5]]
+    packed = pile(after(block, docs[6], docs[2], theirs), block_2, block_6, block_4, near_pile, far_pile)
+    other_packed = swap(packed)
+    block_masks = [0, 2, 6, 4, 1, 3, 7, 5]
+
+    masks = [0, 1, 2, 3, 6, 7, 4, 5]
     where = me[None]
     best_shape = shape((8, half), jnp.float32)
     *best, weight, mine = pl.pallas_call(
-        lambda *refs: first_kernel(seq, masks, orders[0], *refs),
+        lambda *refs: first_kernel(seq, block_masks, *refs),
         out_shape=[
             best_shape,
             best_shape,
             shape((width, width), jnp.bfloat16),
             shape((half, width), jnp.bfloat16),
         ],
-        in_specs=[smem] + [vmem] * 8 + [hbm, vmem],
+        in_specs=[smem] + [vmem] * 5 + [hbm, vmem],
         out_specs=[vmem] * 4,
         scratch_shapes=[pltpu.SemaphoreType.DMA],
         compiler_params=limit,
-        cost_estimate=cost(len(orders[0])),
+        cost_estimate=cost(2),
     )(
         where,
-        meta,
-        *[docs[mask] for mask in orders[0]],
+        *[docs[mask] for mask in masks[:2]],
         packed,
-        after(other_packed, docs[4]),
+        other_packed,
         params,
         stay(weight_rows),
         theirs,
     )
-    for order in orders[1:-1]:
+    docs[5] = cross(after(docs[4], weight), 1)
+    for first in range(2, len(masks) - 2, 2):
         best += pl.pallas_call(
-            lambda *refs, order=order: next_kernel(seq, masks, order, *refs),
+            lambda *refs: next_kernel(seq, *refs),
             out_shape=[best_shape] * 2,
-            in_specs=[vmem] * 7,
+            in_specs=[vmem] * 6,
             out_specs=[vmem] * 2,
             compiler_params=limit,
             cost_estimate=cost(2),
-        )(meta, *[docs[mask] for mask in order], weight, params, mine, theirs)
+        )(*[docs[mask] for mask in masks[first : first + 2]], weight, params, mine, theirs)
     send = pl.pallas_call(
-        lambda *refs: last_kernel(seq, masks, orders, *refs),
+        lambda *refs: last_kernel(seq, masks, *refs),
         out_shape=shape((devices, (1 + BLK_DEV) * SLOT_ROWS, TILE), jnp.bfloat16),
-        in_specs=[smem] * 2 + [vmem] * (8 + len(best)),
+        in_specs=[smem] + [vmem] * (len(masks) + 5 + len(best)),
         out_specs=vmem,
         scratch_shapes=[
             pltpu.VMEM((devices * (1 + BLK_DEV) * SLOT_ROWS, TILE), jnp.float32),
@@ -427,9 +383,7 @@
         cost_estimate=cost(2),
     )(
         where,
-        meta,
-        meta,
-        *[docs[mask] for mask in orders[-1]],
+        *[docs[mask] for mask in masks],
         weight,
         params,
         mine,

time: 65 us -> 61.4 us (0.945)
  waiting for transfers between devices: 26.5 us -> 14.9 us
  starting transfers between devices: 11.9 us -> 18.6 us
  Pallas kernels: 12 us -> 10.4 us
  blocking collectives: 11.7 us -> 13.1 us
  local copies, waits for them, and re-layouts: 1.33 us -> 2.67 us
    ppermute x10 -> x12, waiting for transfers between devices: 26.5 us -> 14.9 us  [cross(): lax.ppermute(value, 'doc', [(i, i ^ 2 * mask) for i in range(devices)])]
    ppermute x10 -> x12, starting transfers between devices: 11.4 us -> 18 us  [cross(): lax.ppermute(value, 'doc', [(i, i ^ 2 * mask) for i in range(devices)])]
    pallas_call x5, Pallas kernels: 12 us -> 10.4 us  [the longest x2 3.57 us: move_tokens(): pl.pallas_call(lambda *refs: next_kernel(seq, *refs), out_shape=[best_sha...]
    all_to_all x1, blocking collectives: 11.7 us -> 13.1 us  [move_tokens(): got = lax.all_to_all(send, 'doc', split_axis=0, concat_axis=0, tiled=True)]
    unnamed x2 -> x6, local copies, waits for them, and re-layouts: 0.01 us -> 1.35 us
  transfers between devices with their start and end apart: 12 -> 14, of which waited for: 4 -> 8; matrix products, arithmetic and copies ran while one was open for 0% -> 0% of each run, Pallas kernels for 13% -> 12%
where the time goes in v9:
time: 61.4 us; the launch traced here: 61.1 us
  starting transfers between devices  18.6 us (30%)
  waiting for transfers between devices  14.9 us (24%)
  blocking collectives  13.1 us (21%)
  Pallas kernels  10.4 us (17%)
  local copies, waits for them, and re-layouts  2.67 us (4%)
  between operations  1.4 us (2%)
    ppermute x12, starting transfers between devices, cross(): lax.ppermute(value, 'doc', [(i, i ^ 2 * mask) for i in range(devices)])  18 us
    ppermute x12, waiting for transfers between devices, cross(): lax.ppermute(value, 'doc', [(i, i ^ 2 * mask) for i in range(devices)])  14.9 us
    all_to_all x1, blocking collectives, move_tokens(): got = lax.all_to_all(send, 'doc', split_axis=0, concat_axis=0, tiled=True)  13.1 us
    pallas_call x2, Pallas kernels, move_tokens(): pl.pallas_call(lambda *refs: next_kernel(seq, *refs), out_shape=[best_sha...  3.57 us
    pallas_call x1, Pallas kernels, move_tokens(): pl.pallas_call(lambda *refs: last_kernel(seq, masks, *refs), out_shape=sh...  3.02 us
    pallas_call x1, Pallas kernels, move_tokens(): pl.pallas_call(lambda *refs: first_kernel(seq, block_masks, *refs), out_s...  2.06 us
    pallas_call x1, Pallas kernels, move_tokens(): pl.pallas_call(start_kernel, out_shape=[shape((seq + SLOT_ROWS, width), j...  1.71 us
    unnamed x6, local copies, waits for them, and re-layouts  1.35 us
  transfers between devices with their start and end apart: 14, of which 8 were waited for; matrix products, arithmetic and copies ran while one was open for 0% of the time, Pallas kernels for 12%

profile of v9, /device:TPU:0, one launch (start us, length us, event | category | flops | bytes accessed | tf_op | source)
XLA Modules:
  0.0 61.1 jit_solution(3785880455240458111)
XLA Ops:
  0.6 0.5 collective-permute-start.8
  1.2 4.7 %collective-permute-start = (bf16[48,768]{1,0:T(8,128)(2,1)}, bf16[48,768]{1,0:T(8,128)(2,1)S(1)}, u32[]{:S(2)}, u32[]{:S(2)}) collective-permute-start(bf16[48,768]{1,0:T(8,128)(2,1)} %refs_1_.1), channel_id=1, source_target_pairs={{0,12},{1,13},{2,14},{3,15},{4,8},{5,9},{6,10},{7,11},{8,4},{9,5},... | collective-permute-start | bytes 221192 | tf_op jit(solution)/shard_map/ppermute | solution.py:264
  5.8 0.0 collective-permute-start.9
  6.5 1.7 %shard_map.122 = (bf16[144,768]{1,0:T(8,128)(2,1)S(1)}, bf16[48,768]{1,0:T(8,128)(2,1)S(1)}, f32[8,768]{1,0:T(8,128)S(1)}) custom-call(s32[1,1,32]{2,1,0:T(1,128)} %tiles_ref.1, s32[1,1,32]{2,1,0:T(1,128)} %bitcast.15, s32[1,1,32]{2,1,0:T(1,128)} %slots_ref.1, s32[1]{0:T(128)S(6)} %copy.22.length_ref, bf16[128,768]{1,0:T(8,128)(2,1)} %refs_0_.1, ...), custom_call_target="tpu_custom_call" | custom-call | tf_op jit(solution)/shard_map/pallas_call | solution.py:301
  8.2 0.0 copy-start
  8.2 0.6 copy-done
  8.8 0.4 collective-permute-done.refs_0_.refs_2_
  9.2 1.6 %collective-permute-start.1 = (bf16[144,768]{1,0:T(8,128)(2,1)S(1)}, bf16[144,768]{1,0:T(8,128)(2,1)S(1)}, u32[]{:S(2)}, u32[]{:S(2)}) collective-permute-start(bf16[144,768]{1,0:T(8,128)(2,1)S(1)} %get-tuple-element.20.refs_1_), channel_id=1, source_target_pairs={{0,2},{1,3},{2,0},{3,1},{4,6},{5,7},{6,4},{7,5},{8,10},{9,11},{10,... | collective-permute-start | bytes 663560 | tf_op jit(solution)/shard_map/ppermute | solution.py:264
  10.8 1.5 %collective-permute-start.2 = (bf16[48,768]{1,0:T(8,128)(2,1)S(1)}, bf16[48,768]{1,0:T(8,128)(2,1)S(1)}, u32[]{:S(2)}, u32[]{:S(2)}) collective-permute-start(bf16[48,768]{1,0:T(8,128)(2,1)S(1)} %collective-permute-done.refs_0_.refs_2_), channel_id=1, source_target_pairs={{0,4},{1,5},{2,6},{3,7},{4,0},{5,1},{6,2},{7,3},{8,12},{9,13},{10,... | collective-permute-start | bytes 221192 | tf_op jit(solution)/shard_map/ppermute | solution.py:264
  12.3 0.0 collective-permute-done.9.refs_1_
  12.4 0.6 collective-permute-start.10
  13.0 2.1 %collective-permute-start.5 = (bf16[144,768]{1,0:T(8,128)(2,1)S(1)}, bf16[144,768]{1,0:T(8,128)(2,1)S(1)}, u32[]{:S(2)}, u32[]{:S(2)}) collective-permute-start(bf16[144,768]{1,0:T(8,128)(2,1)S(1)} %get-tuple-element.20.refs_1_), channel_id=1, source_target_pairs={{0,12},{1,13},{2,14},{3,15},{4,8},{5,9},{6,10},{7,11},{8,4},{9,5},... | collective-permute-start | bytes 663560 | tf_op jit(solution)/shard_map/ppermute | solution.py:264
  15.0 0.2 collective-permute-done.2.refs_1_.refs_3_
  15.2 2.0 %collective-permute-start.3 = (bf16[144,768]{1,0:T(8,128)(2,1)S(1)}, bf16[144,768]{1,0:T(8,128)(2,1)S(1)}, u32[]{:S(2)}, u32[]{:S(2)}) collective-permute-start(bf16[144,768]{1,0:T(8,128)(2,1)S(1)} %get-tuple-element.20.refs_1_), channel_id=1, source_target_pairs={{0,4},{1,5},{2,6},{3,7},{4,0},{5,1},{6,2},{7,3},{8,12},{9,13},{10,... | collective-permute-start | bytes 663560 | tf_op jit(solution)/shard_map/ppermute | solution.py:264
  17.2 2.3 %collective-permute-done.10.refs_4_ = bf16[96,768]{1,0:T(8,128)(2,1)S(1)} collective-permute-done((bf16[96,768]{1,0:T(8,128)(2,1)S(1)}, bf16[96,768]{1,0:T(8,128)(2,1)S(1)}, u32[]{:S(2)}, u32[]{:S(2)}) %collective-permute-start.10) | collective-permute-done | bytes 147488 | tf_op jit(solution)/shard_map/ppermute | solution.py:264
  19.5 0.0 collective-permute-done.1.refs_2_
  19.5 1.6 %collective-permute-start.11 = (bf16[96,768]{1,0:T(8,128)(2,1)S(1)}, bf16[96,768]{1,0:T(8,128)(2,1)S(1)}, u32[]{:S(2)}, u32[]{:S(2)}) collective-permute-start(bf16[96,768]{1,0:T(8,128)(2,1)S(1)} %shard_map.124), channel_id=1, source_target_pairs={{0,2},{1,3},{2,0},{3,1},{4,6},{5,7},{6,4},{7,5},{8,10},{9,11},{10,... | collective-permute-start | bytes 442376 | tf_op jit(solution)/shard_map/ppermute | solution.py:264
  21.1 2.1 %collective-permute-done.5.refs_0_.refs_5_ = bf16[144,768]{1,0:T(8,128)(2,1)S(1)} collective-permute-done((bf16[144,768]{1,0:T(8,128)(2,1)S(1)}, bf16[144,768]{1,0:T(8,128)(2,1)S(1)}, u32[]{:S(2)}, u32[]{:S(2)}) %collective-permute-start.5) | collective-permute-done | bytes 221216 | tf_op jit(solution)/shard_map/ppermute | solution.py:264
  23.1 2.6 %collective-permute-done.3.refs_0_.refs_3_ = bf16[144,768]{1,0:T(8,128)(2,1)S(1)} collective-permute-done((bf16[144,768]{1,0:T(8,128)(2,1)S(1)}, bf16[144,768]{1,0:T(8,128)(2,1)S(1)}, u32[]{:S(2)}, u32[]{:S(2)}) %collective-permute-start.3) | collective-permute-done | bytes 221216 | tf_op jit(solution)/shard_map/ppermute | solution.py:264
  25.8 0.0 collective-permute-done.8.refs_7_.refs_5_.refs_12_
  25.8 0.0 collective-permute-done.11.refs_5_
  25.8 0.1 collective-permute-start.12
  25.9 0.7 %collective-permute-start.7 = (bf16[144,768]{1,0:T(8,128)(2,1)S(1)}, bf16[144,768]{1,0:T(8,128)(2,1)}, u32[]{:S(2)}, u32[]{:S(2)}) collective-permute-start(bf16[144,768]{1,0:T(8,128)(2,1)S(1)} %collective-permute-done.5.refs_0_.refs_5_), channel_id=1, source_target_pairs={{0,4},{1,5},{2,6},{3,7},{4,0},{5,1},{6,2},{7,3},{8,12},{9,13},{10,... | collective-permute-start | bytes 663560 | tf_op jit(solution)/shard_map/ppermute | solution.py:264
  26.6 1.5 %collective-permute-start.6 = (bf16[144,768]{1,0:T(8,128)(2,1)S(1)}, bf16[144,768]{1,0:T(8,128)(2,1)S(1)}, u32[]{:S(2)}, u32[]{:S(2)}) collective-permute-start(bf16[144,768]{1,0:T(8,128)(2,1)S(1)} %collective-permute-done.5.refs_0_.refs_5_), channel_id=1, source_target_pairs={{0,2},{1,3},{2,0},{3,1},{4,6},{5,7},{6,4},{7,5},{8,10},{9,11},{10,... | collective-permute-start | bytes 663560 | tf_op jit(solution)/shard_map/ppermute | solution.py:264
  28.1 0.5 collective-permute-start.4
  28.7 0.0 collective-permute-done.12.refs_4_
  28.7 0.0 copy-start.1
  28.7 0.7 %copy-done.1 = f32[8,768]{1,0:T(8,128)S(1)} copy-done((f32[8,768]{1,0:T(8,128)S(1)}, f32[8,768]{1,0:T(8,128)}, u32[]{:S(2)}) %copy-start.1) | copy-done | bytes 24600
  29.4 2.1 %shard_map.126 = (f32[8,960]{1,0:T(8,128)S(1)}, f32[8,960]{1,0:T(8,128)S(1)}, bf16[768,768]{1,0:T(8,128)(2,1)S(1)}, bf16[960,768]{1,0:T(8,128)(2,1)S(1)}) custom-call(s32[1]{0:T(128)} %bitcast.refs_0_, bf16[144,768]{1,0:T(8,128)(2,1)S(1)} %get-tuple-element.20.refs_1_, bf16[144,768]{1,0:T(8,128)(2,1)S(1)} %collective-permute-done.1.refs_2_, ...), custom_call_target="tpu_custom_call" | custom-call | flops 2 | bytes 2 | tf_op jit(solution)/shard_map/pallas_call | solution.py:342
  31.5 2.4 %collective-permute-done.7.refs_7_ = bf16[144,768]{1,0:T(8,128)(2,1)} collective-permute-done((bf16[144,768]{1,0:T(8,128)(2,1)S(1)}, bf16[144,768]{1,0:T(8,128)(2,1)}, u32[]{:S(2)}, u32[]{:S(2)}) %collective-permute-start.7) | collective-permute-done | bytes 221216 | tf_op jit(solution)/shard_map/ppermute | solution.py:264
  33.8 1.2 %collective-permute-start.13 = (bf16[144,768]{1,0:T(8,128)(2,1)}, bf16[144,768]{1,0:T(8,128)(2,1)S(1)}, u32[]{:S(2)}, u32[]{:S(2)}) collective-permute-start(bf16[144,768]{1,0:T(8,128)(2,1)} %collective-permute-done.7.refs_7_), channel_id=1, source_target_pairs={{0,2},{1,3},{2,0},{3,1},{4,6},{5,7},{6,4},{7,5},{8,10},{9,11},{10,... | collective-permute-start | bytes 663560 | tf_op jit(solution)/shard_map/ppermute | solution.py:264
  35.0 0.0 collective-permute-done.6.refs_1_.refs_6_
  35.0 1.8 %shard_map.128 = (f32[8,960]{1,0:T(8,128)S(1)}, f32[8,960]{1,0:T(8,128)S(1)}) custom-call(bf16[144,768]{1,0:T(8,128)(2,1)S(1)} %collective-permute-done.5.refs_0_.refs_5_, bf16[144,768]{1,0:T(8,128)(2,1)S(1)} %collective-permute-done.6.refs_1_.refs_6_, bf16[768,768]{1,0:T(8,128)(2,1)S(1)} %get-tuple-element.25.refs_2_.refs_9_, f32[8,768]{1,0:T(8,128)S(1)} %copy-done.1, ...), custom_call_target="tpu_custom_call" | custom-call | flops 2 | bytes 2 | tf_op jit(solution)/shard_map/pallas_call | solution.py:366
  36.8 0.0 copy-start.2
  36.8 2.8 %collective-permute-done.4.refs_1_.refs_4_ = bf16[144,768]{1,0:T(8,128)(2,1)S(1)} collective-permute-done((bf16[144,768]{1,0:T(8,128)(2,1)S(1)}, bf16[144,768]{1,0:T(8,128)(2,1)S(1)}, u32[]{:S(2)}, u32[]{:S(2)}) %collective-permute-start.4) | collective-permute-done | bytes 221216 | tf_op jit(solution)/shard_map/ppermute | solution.py:264
  39.6 1.8 %shard_map.127 = (f32[8,960]{1,0:T(8,128)S(1)}, f32[8,960]{1,0:T(8,128)S(1)}) custom-call(bf16[144,768]{1,0:T(8,128)(2,1)S(1)} %collective-permute-done.3.refs_0_.refs_3_, bf16[144,768]{1,0:T(8,128)(2,1)S(1)} %collective-permute-done.4.refs_1_.refs_4_, bf16[768,768]{1,0:T(8,128)(2,1)S(1)} %get-tuple-element.25.refs_2_.refs_9_, f32[8,768]{1,0:T(8,128)S(1)} %copy-done.1, ...), custom_call_target="tpu_custom_call" | custom-call | flops 2 | bytes 2 | tf_op jit(solution)/shard_map/pallas_call | solution.py:366
  41.4 2.2 %collective-permute-done.13.refs_8_ = bf16[144,768]{1,0:T(8,128)(2,1)S(1)} collective-permute-done((bf16[144,768]{1,0:T(8,128)(2,1)}, bf16[144,768]{1,0:T(8,128)(2,1)S(1)}, u32[]{:S(2)}, u32[]{:S(2)}) %collective-permute-start.13) | collective-permute-done | bytes 221216 | tf_op jit(solution)/shard_map/ppermute | solution.py:264
  43.6 0.0 copy-done.2
  43.6 3.0 %shard_map.129 = bf16[16,48,128]{2,1,0:T(8,128)(2,1)S(1)} custom-call(s32[1]{0:T(128)} %bitcast.refs_0_, bf16[144,768]{1,0:T(8,128)(2,1)S(1)} %get-tuple-element.20.refs_1_, bf16[144,768]{1,0:T(8,128)(2,1)S(1)} %collective-permute-done.1.refs_2_, bf16[144,768]{1,0:T(8,128)(2,1)S(1)} %collective-permute-done.3.refs_0_.refs_3_, ...), custom_call_target="tpu_custom_call" | custom-call | flops 2 | bytes 2 | tf_op jit(solution)/shard_map/pallas_call | solution.py:374
  46.6 13.1 %all_to_all.5 = bf16[16,48,128]{2,1,0:T(8,128)(2,1)S(1)} all-to-all(bf16[16,48,128]{2,1,0:T(8,128)(2,1)S(1)} %shard_map.129), channel_id=1, replica_groups=mesh['groups'=2,'doc'=16,'term'=1] {'doc'}, dimensions={0} | all-to-all | bytes 393216 | tf_op jit(solution)/shard_map/all_to_all | solution.py:394
  59.8 0.7 %slice.26 = bf16[2,15360]{1,0:T(2,128)(2,1)} reshape(bf16[2,8,15,128]{3,2,1,0:T(8,128)(2,1)S(1)} %slice.30) | data formatting | bytes 122880 | tf_op jit(solution)/shard_map/slice | solution.py:397
  60.5 0.6 %slice.24 = bf16[1,15360]{1,0:T(2,128)(2,1)} reshape(bf16[1,8,15,128]{3,2,1,0:T(8,128)(2,1)S(1)} %slice.29) | data formatting | bytes 61440 | tf_op jit(solution)/shard_map/slice | solution.py:397
  (7 shorter events, 0.1 us)
Async XLA Ops:
  0.6 25.1 %collective-permute-start.8 = (bf16[960,768]{1,0:T(8,128)(2,1)}, bf16[960,768]{1,0:T(8,128)(2,1)S(1)}, u32[]{:S(2)}, u32[]{:S(2)}) collective-permute-start(bf16[960,768]{1,0:T(8,128)(2,1)} %bitcast.12), channel_id=1, source_target_pairs={{0,1},{1,0},{2,3},{3,2},{4,5},{5,4},{6,7},{7,6},{8,9},{9,8},{10,11... | collective-permute-start | bytes 4423688 | tf_op jit(solution)/shard_map/ppermute | solution.py:267
  1.2 8.1 %collective-permute-start = (bf16[48,768]{1,0:T(8,128)(2,1)}, bf16[48,768]{1,0:T(8,128)(2,1)S(1)}, u32[]{:S(2)}, u32[]{:S(2)}) collective-permute-start(bf16[48,768]{1,0:T(8,128)(2,1)} %refs_1_.1), channel_id=1, source_target_pairs={{0,12},{1,13},{2,14},{3,15},{4,8},{5,9},{6,10},{7,11},{8,4},{9,5},... | collective-permute-start | bytes 221192 | tf_op jit(solution)/shard_map/ppermute | solution.py:264
  5.8 6.5 %collective-permute-start.9 = (bf16[48,768]{1,0:T(8,128)(2,1)}, bf16[48,768]{1,0:T(8,128)(2,1)S(1)}, u32[]{:S(2)}, u32[]{:S(2)}) collective-permute-start(bf16[48,768]{1,0:T(8,128)(2,1)} %refs_1_.1), channel_id=1, source_target_pairs={{0,4},{1,5},{2,6},{3,7},{4,0},{5,1},{6,2},{7,3},{8,12},{9,13},{10,... | collective-permute-start | bytes 221192 | tf_op jit(solution)/shard_map/ppermute | solution.py:264
  8.2 0.6 copy-start
  9.2 10.3 %collective-permute-start.1 = (bf16[144,768]{1,0:T(8,128)(2,1)S(1)}, bf16[144,768]{1,0:T(8,128)(2,1)S(1)}, u32[]{:S(2)}, u32[]{:S(2)}) collective-permute-start(bf16[144,768]{1,0:T(8,128)(2,1)S(1)} %get-tuple-element.20.refs_1_), channel_id=1, source_target_pairs={{0,2},{1,3},{2,0},{3,1},{4,6},{5,7},{6,4},{7,5},{8,10},{9,11},{10,... | collective-permute-start | bytes 663560 | tf_op jit(solution)/shard_map/ppermute | solution.py:264
  10.8 4.4 %collective-permute-start.2 = (bf16[48,768]{1,0:T(8,128)(2,1)S(1)}, bf16[48,768]{1,0:T(8,128)(2,1)S(1)}, u32[]{:S(2)}, u32[]{:S(2)}) collective-permute-start(bf16[48,768]{1,0:T(8,128)(2,1)S(1)} %collective-permute-done.refs_0_.refs_2_), channel_id=1, source_target_pairs={{0,4},{1,5},{2,6},{3,7},{4,0},{5,1},{6,2},{7,3},{8,12},{9,13},{10,... | collective-permute-start | bytes 221192 | tf_op jit(solution)/shard_map/ppermute | solution.py:264
  12.4 7.1 %collective-permute-start.10 = (bf16[96,768]{1,0:T(8,128)(2,1)S(1)}, bf16[96,768]{1,0:T(8,128)(2,1)S(1)}, u32[]{:S(2)}, u32[]{:S(2)}) collective-permute-start(bf16[96,768]{1,0:T(8,128)(2,1)S(1)} %shard_map.123), channel_id=1, source_target_pairs={{0,2},{1,3},{2,0},{3,1},{4,6},{5,7},{6,4},{7,5},{8,10},{9,11},{10,... | collective-permute-start | bytes 442376 | tf_op jit(solution)/shard_map/ppermute | solution.py:264
  13.0 10.2 %collective-permute-start.5 = (bf16[144,768]{1,0:T(8,128)(2,1)S(1)}, bf16[144,768]{1,0:T(8,128)(2,1)S(1)}, u32[]{:S(2)}, u32[]{:S(2)}) collective-permute-start(bf16[144,768]{1,0:T(8,128)(2,1)S(1)} %get-tuple-element.20.refs_1_), channel_id=1, source_target_pairs={{0,12},{1,13},{2,14},{3,15},{4,8},{5,9},{6,10},{7,11},{8,4},{9,5},... | collective-permute-start | bytes 663560 | tf_op jit(solution)/shard_map/ppermute | solution.py:264
  15.2 10.6 %collective-permute-start.3 = (bf16[144,768]{1,0:T(8,128)(2,1)S(1)}, bf16[144,768]{1,0:T(8,128)(2,1)S(1)}, u32[]{:S(2)}, u32[]{:S(2)}) collective-permute-start(bf16[144,768]{1,0:T(8,128)(2,1)S(1)} %get-tuple-element.20.refs_1_), channel_id=1, source_target_pairs={{0,4},{1,5},{2,6},{3,7},{4,0},{5,1},{6,2},{7,3},{8,12},{9,13},{10,... | collective-permute-start | bytes 663560 | tf_op jit(solution)/shard_map/ppermute | solution.py:264
  19.5 6.3 %collective-permute-start.11 = (bf16[96,768]{1,0:T(8,128)(2,1)S(1)}, bf16[96,768]{1,0:T(8,128)(2,1)S(1)}, u32[]{:S(2)}, u32[]{:S(2)}) collective-permute-start(bf16[96,768]{1,0:T(8,128)(2,1)S(1)} %shard_map.124), channel_id=1, source_target_pairs={{0,2},{1,3},{2,0},{3,1},{4,6},{5,7},{6,4},{7,5},{8,10},{9,11},{10,... | collective-permute-start | bytes 442376 | tf_op jit(solution)/shard_map/ppermute | solution.py:264
  25.8 2.8 %collective-permute-start.12 = (bf16[384,768]{1,0:T(8,128)(2,1)S(1)}, bf16[384,768]{1,0:T(8,128)(2,1)S(1)}, u32[]{:S(2)}, u32[]{:S(2)}) collective-permute-start(bf16[384,768]{1,0:T(8,128)(2,1)S(1)} %shard_map.125.refs_3_), channel_id=1, source_target_pairs={{0,1},{1,0},{2,3},{3,2},{4,5},{5,4},{6,7},{7,6},{8,9},{9,8},{10,11... | collective-permute-start | bytes 1769480 | tf_op jit(solution)/shard_map/ppermute | solution.py:267
  25.9 7.9 %collective-permute-start.7 = (bf16[144,768]{1,0:T(8,128)(2,1)S(1)}, bf16[144,768]{1,0:T(8,128)(2,1)}, u32[]{:S(2)}, u32[]{:S(2)}) collective-permute-start(bf16[144,768]{1,0:T(8,128)(2,1)S(1)} %collective-permute-done.5.refs_0_.refs_5_), channel_id=1, source_target_pairs={{0,4},{1,5},{2,6},{3,7},{4,0},{5,1},{6,2},{7,3},{8,12},{9,13},{10,... | collective-permute-start | bytes 663560 | tf_op jit(solution)/shard_map/ppermute | solution.py:264
  26.6 8.4 %collective-permute-start.6 = (bf16[144,768]{1,0:T(8,128)(2,1)S(1)}, bf16[144,768]{1,0:T(8,128)(2,1)S(1)}, u32[]{:S(2)}, u32[]{:S(2)}) collective-permute-start(bf16[144,768]{1,0:T(8,128)(2,1)S(1)} %collective-permute-done.5.refs_0_.refs_5_), channel_id=1, source_target_pairs={{0,2},{1,3},{2,0},{3,1},{4,6},{5,7},{6,4},{7,5},{8,10},{9,11},{10,... | collective-permute-start | bytes 663560 | tf_op jit(solution)/shard_map/ppermute | solution.py:264
  28.1 11.5 %collective-permute-start.4 = (bf16[144,768]{1,0:T(8,128)(2,1)S(1)}, bf16[144,768]{1,0:T(8,128)(2,1)S(1)}, u32[]{:S(2)}, u32[]{:S(2)}) collective-permute-start(bf16[144,768]{1,0:T(8,128)(2,1)S(1)} %collective-permute-done.3.refs_0_.refs_3_), channel_id=1, source_target_pairs={{0,2},{1,3},{2,0},{3,1},{4,6},{5,7},{6,4},{7,5},{8,10},{9,11},{10,... | collective-permute-start | bytes 663560 | tf_op jit(solution)/shard_map/ppermute | solution.py:264
  28.7 0.7 %copy-start.1 = (f32[8,768]{1,0:T(8,128)S(1)}, f32[8,768]{1,0:T(8,128)}, u32[]{:S(2)}) copy-start(f32[8,768]{1,0:T(8,128)} %copy-done) | copy-start | bytes 73732
  33.8 9.8 %collective-permute-start.13 = (bf16[144,768]{1,0:T(8,128)(2,1)}, bf16[144,768]{1,0:T(8,128)(2,1)S(1)}, u32[]{:S(2)}, u32[]{:S(2)}) collective-permute-start(bf16[144,768]{1,0:T(8,128)(2,1)} %collective-permute-done.7.refs_7_), channel_id=1, source_target_pairs={{0,2},{1,3},{2,0},{3,1},{4,6},{5,7},{6,4},{7,5},{8,10},{9,11},{10,... | collective-permute-start | bytes 663560 | tf_op jit(solution)/shard_map/ppermute | solution.py:264
  36.8 6.8 %copy-start.2 = (f32[15360]{0:T(1024)S(1)}, f32[15360]{0:T(1024)}, u32[]{:S(2)}) copy-start(f32[15360]{0:T(1024)} %param.18) | copy-start | bytes 184324

commit v10 on v9

--- a/solution.py
+++ b/solution.py
@@ -102,20 +102,21 @@
     )
 
 
-def table_of(ref, seq):
-    return ref[seq : seq + SLOT_ROWS, 0:TILE].astype(jnp.float32)[0:1, :]
-
-
-def masked(ref, seq):
+def table_of(ref):
+    return ref[ref.shape[0] - SLOT_ROWS :, 0:TILE].astype(jnp.float32)[0:1, :]
+
+
+def masked(ref, table_ref, seq):
     here = ref[0:seq, :]
-    length = table_of(ref, seq)[:, TILE - 1 :]
+    length = table_of(table_ref)[:, TILE - 1 :]
     keep = lax.broadcasted_iota(jnp.int32, here.shape, 0).astype(jnp.float32) < length
     first = jnp.broadcast_to(here[0:1, :].astype(jnp.float32), here.shape).astype(here.dtype)
     return jnp.where(keep, here, first)
 
 
-def normed_rows(docs, seq, weight, params):
-    rows = jnp.concatenate([masked(ref, seq) for ref in docs], axis=0)
+def normed_rows(docs, tables, seq, weight, params):
+    rows = [masked(ref, table, seq) for ref, table in zip(docs, tables)]
+    rows = jnp.concatenate(rows, axis=0)
     pre = jnp.dot(rows, weight[...], preferred_element_type=jnp.float32) + params[0:1, :]
     act = 0.5 * pre * (1.0 + lax.erf(pre * (0.5**0.5)))
     return layer_norm(act.astype(jnp.bfloat16), params[1:2, :], params[2:3, :])
@@ -131,7 +132,7 @@
 
 def start_kernel(tiles_ref, owners_ref, slots_ref, length_ref, *refs):
     hidden_ref, weight_ref, vectors = refs[0], refs[1], refs[2:5]
-    load_ref, block_ref, rows_ref, kept, sems = refs[5:]
+    load_ref, block_ref, table_ref, rows_ref, kept, sems = refs[5:]
     seq, width = hidden_ref.shape
     copies = [
         fetch(hidden_ref, load_ref.at[pl.ds(0, seq), :], sems.at[0]),
@@ -148,17 +149,18 @@
     table = table.astype(jnp.float32).astype(jnp.bfloat16)
     for first in range(0, width, TILE):
         load_ref[seq:, first : first + TILE] = table
+        table_ref[:, first : first + TILE] = table
     for copy in copies:
         copy.wait()
     for k in range(len(vectors)):
         rows_ref[k : k + 1, :] = kept[pl.ds(k * width, width)][None, :]
 
 
-def pile_kernel(*refs):
+def pile_kernel(counts, *refs):
     at = 0
-    for ref in refs[:-1]:
-        refs[-1][at : at + ref.shape[0], :] = ref[...]
-        at += ref.shape[0]
+    for ref, count in zip(refs[:-1], counts):
+        refs[-1][at : at + count, :] = ref[0:count, :]
+        at += count
 
 
 def fetch(ref, slot, sem):
@@ -174,7 +176,7 @@
 
 
 def first_kernel(seq, masks, *refs):
-    me_ref, docs, packed, refs = refs[0], refs[1:3], refs[3:5], refs[5:]
+    me_ref, docs, tables, packed, refs = refs[0], refs[1:3], refs[3:5], refs[5:7], refs[7:]
     params, mine_ref, theirs_ref, best_mine, best_theirs, weight, mine, sem = refs
     copy = fetch(mine_ref, mine, sem)
     me = me_ref[0]
@@ -187,7 +189,7 @@
         weight[pl.ds(at, rows), :] = packed[0][block, :]
         at = pl.multiple_of((2 * chip + 1 - core) * rows, SLOT_ROWS)
         weight[pl.ds(at, rows), :] = packed[1][block, :]
-    normed = normed_rows(docs, seq, weight, params)
+    normed = normed_rows(docs, tables, seq, weight, params)
     keep_tops(normed, [theirs_ref], [best_theirs])
     copy.wait()
     keep_tops(normed, [mine], [best_mine])
@@ -195,18 +197,18 @@
 
 def next_kernel(seq, *refs):
     docs, weight, params, halves, bests = refs[:2], refs[2], refs[3], refs[4:6], refs[6:]
-    keep_tops(normed_rows(docs, seq, weight, params), halves, bests)
+    keep_tops(normed_rows(docs, docs, seq, weight, params), halves, bests)
 
 
 def last_kernel(seq, masks, *refs):
-    me_ref, docs, refs = refs[0], refs[1 : 1 + len(masks)], refs[1 + len(masks) :]
+    me_ref, docs, tables, refs = refs[0], refs[1:3], refs[3 : 3 + len(masks)], refs[3 + len(masks) :]
     weight, params, halves, dbias_ref, refs = refs[0], refs[1], refs[2:4], refs[4], refs[5:]
     earlier, out_ref, send = refs[:-2], refs[-2], refs[-1]
     me = me_ref[0]
     core, chip = me % 2, me // 2
     devices = 2 * len(masks)
     tiles = 2 * halves[0].shape[0] // TILE
-    normed = normed_rows(docs[-2:], seq, weight, params)
+    normed = normed_rows(docs, docs, seq, weight, params)
     found = []
     for k, w_ref in enumerate(halves):
         parts = [ref[0:2, :] for ref in earlier[k::2]]
@@ -217,7 +219,7 @@
     docs_at = [me ^ (2 * mask) for mask in masks]
     bias = dbias_ref[...]
     bias = pltpu.roll(bias, bias.shape[0] - chip * tiles, 0)
-    tables = jnp.concatenate([table_of(ref, seq) for ref in docs], axis=0)
+    tables = jnp.concatenate([table_of(ref) for ref in tables], axis=0)
     tables = pltpu.roll(tables, TILE - chip * tiles, 1).astype(jnp.int32)
     send[...] = jnp.zeros(send.shape, jnp.float32)
     stride = out_ref.shape[1]
@@ -284,11 +286,10 @@
     def after(value, *done):
         return lax.optimization_barrier((value, *done))[0]
 
-    def pile(*values):
-        total = sum(value.shape[0] for value in values)
+    def pile(values, counts):
         return pl.pallas_call(
-            pile_kernel,
-            out_shape=shape((total, values[0].shape[1]), values[0].dtype),
+            lambda *refs: pile_kernel(counts, *refs),
+            out_shape=shape((sum(counts), width), jnp.bfloat16),
             in_specs=[vmem] * len(values),
             out_specs=vmem,
             compiler_params=limit,
@@ -298,15 +299,17 @@
     block_6 = cross(transform_weight, 6)
     block_2 = cross(transform_weight, 2)
     theirs = swap(weight_rows)
-    load, block, params = pl.pallas_call(
+    docs = {1: cross(hidden_states, 1)}
+    load, block, table, params = pl.pallas_call(
         start_kernel,
         out_shape=[
             shape((seq + SLOT_ROWS, width), jnp.bfloat16),
             shape((rows, width), jnp.bfloat16),
+            shape((SLOT_ROWS, width), jnp.bfloat16),
             shape((8, width), jnp.float32),
         ],
         in_specs=[smem] * 4 + [hbm] * 5,
-        out_specs=[vmem] * 3,
+        out_specs=[vmem] * 4,
         scratch_shapes=[
             pltpu.VMEM((3 * width,), jnp.float32),
             pltpu.SemaphoreType.DMA((5,)),
@@ -323,16 +326,22 @@
         stay(norm_gain),
         stay(norm_bias),
     )
-    docs = {0: load, 1: cross(after(load, block_6), 1)}
-    near_pile = cross(pile(block, block_2), 1)
+    docs[0] = load
+    docs[2] = cross(after(load, block_2, block_6), 2)
+    near = (block, after(block_2, block_6, docs[1]), table)
+    near_pile = cross(pile(near, (rows, rows, SLOT_ROWS)), 1)
     block_4 = cross(block_6, 2)
     docs[6] = cross(after(load, block_6), 6)
-    docs[2] = cross(after(load, block_4), 2)
-    far_pile = cross(pile(block_6, after(block_4, near_pile, docs[1])), 1)
+    far = (block_6, after(block_4, near_pile, docs[2]))
+    far_pile = cross(pile(far, (rows, rows)), 1)
     docs[3] = cross(docs[2], 1)
     docs[4] = cross(docs[6], 2)
     docs[7] = cross(docs[6], 1)
-    packed = pile(after(block, docs[6], docs[2], theirs), block_2, block_6, block_4, near_pile, far_pile)
+    late = (docs[6], docs[3], theirs)
+    packed = pile(
+        (after(block, *late), block_2, block_6, block_4, near_pile, far_pile),
+        (rows, rows, rows, rows, 2 * rows, 2 * rows),
+    )
     other_packed = swap(packed)
     block_masks = [0, 2, 6, 4, 1, 3, 7, 5]
 
@@ -347,14 +356,17 @@
             shape((width, width), jnp.bfloat16),
             shape((half, width), jnp.bfloat16),
         ],
-        in_specs=[smem] + [vmem] * 5 + [hbm, vmem],
+        in_specs=[smem] + [vmem] * 7 + [hbm, vmem],
         out_specs=[vmem] * 4,
         scratch_shapes=[pltpu.SemaphoreType.DMA],
         compiler_params=limit,
         cost_estimate=cost(2),
     )(
         where,
-        *[docs[mask] for mask in masks[:2]],
+        docs[0],
+        docs[1],
+        docs[0],
+        near_pile,
         packed,
         other_packed,
         params,
@@ -374,7 +386,7 @@
     send = pl.pallas_call(
         lambda *refs: last_kernel(seq, masks, *refs),
         out_shape=shape((devices, (1 + BLK_DEV) * SLOT_ROWS, TILE), jnp.bfloat16),
-        in_specs=[smem] + [vmem] * (len(masks) + 5 + len(best)),
+        in_specs=[smem] + [vmem] * (2 + len(masks) + 5 + len(best)),
         out_specs=vmem,
         scratch_shapes=[
             pltpu.VMEM((devices * (1 + BLK_DEV) * SLOT_ROWS, TILE), jnp.float32),
@@ -383,7 +395,8 @@
         cost_estimate=cost(2),
     )(
         where,
-        *[docs[mask] for mask in masks],
+        *[docs[mask] for mask in masks[-2:]],
+        *[near_pile if mask == 1 else docs[mask] for mask in masks],
         weight,
         params,
         mine,

time: 61.4 us -> 62.2 us (1.013)
  waiting for transfers between devices: 14.9 us -> 21.9 us
  starting transfers between devices: 18.6 us -> 13.4 us
  blocking collectives: 13.1 us -> 11.6 us
    ppermute x12, waiting for transfers between devices: 14.9 us -> 20.9 us  [cross(): lax.ppermute(value, 'doc', [(i, i ^ 2 * mask) for i in range(devices)])]
    ppermute x12, starting transfers between devices: 18 us -> 12.8 us  [cross(): lax.ppermute(value, 'doc', [(i, i ^ 2 * mask) for i in range(devices)])]
    all_to_all x1, blocking collectives: 13.1 us -> 11.6 us  [move_tokens(): got = lax.all_to_all(send, 'doc', split_axis=0, concat_axis=0, tiled=True)]
    pallas_call x1, Pallas kernels: 2.06 us -> 3.13 us  [move_tokens(): pl.pallas_call(lambda *refs: first_kernel(seq, block_masks, *refs), out_s...]
    ppermute x2, waiting for transfers between devices: 0.01 us -> 1.01 us  [swap(): return lax.ppermute(value, 'doc', [(i, i ^ 1) for i in range(devices)])]
    pallas_call x1, Pallas kernels: 3.02 us -> 2.15 us  [move_tokens(): pl.pallas_call(lambda *refs: last_kernel(seq, masks, *refs), out_shape=sh...]
  transfers between devices with their start and end apart: 14 -> 14, of which waited for: 8 -> 9; matrix products, arithmetic and copies ran while one was open for 0% -> 0% of each run, Pallas kernels for 12% -> 14%
where the time goes in v10:
time: 62.2 us; the launch traced here: 61.9 us
  waiting for transfers between devices  21.9 us (35%)
  starting transfers between devices  13.4 us (22%)
  blocking collectives  11.6 us (19%)
  Pallas kernels  10.6 us (17%)
  local copies, waits for them, and re-layouts  2.94 us (5%)
  between operations  1.4 us (2%)
    ppermute x12, waiting for transfers between devices, cross(): lax.ppermute(value, 'doc', [(i, i ^ 2 * mask) for i in range(devices)])  20.9 us
    ppermute x12, starting transfers between devices, cross(): lax.ppermute(value, 'doc', [(i, i ^ 2 * mask) for i in range(devices)])  12.8 us
    all_to_all x1, blocking collectives, move_tokens(): got = lax.all_to_all(send, 'doc', split_axis=0, concat_axis=0, tiled=True)  11.6 us
    pallas_call x2, Pallas kernels, move_tokens(): pl.pallas_call(lambda *refs: next_kernel(seq, *refs), out_shape=[best_sha...  3.57 us
    pallas_call x1, Pallas kernels, move_tokens(): pl.pallas_call(lambda *refs: first_kernel(seq, block_masks, *refs), out_s...  3.13 us
    pallas_call x1, Pallas kernels, move_tokens(): pl.pallas_call(lambda *refs: last_kernel(seq, masks, *refs), out_shape=sh...  2.15 us
    pallas_call x1, Pallas kernels, move_tokens(): pl.pallas_call(start_kernel, out_shape=[shape((seq + SLOT_ROWS, width), j...  1.71 us
    unnamed x6, local copies, waits for them, and re-layouts  1.62 us
  transfers between devices with their start and end apart: 14, of which 9 were waited for; matrix products, arithmetic and copies ran while one was open for 0% of the time, Pallas kernels for 14%

profile of v10, /device:TPU:0, one launch (start us, length us, event | category | flops | bytes accessed | tf_op | source)
XLA Modules:
  0.0 61.9 jit_solution(2778066125933949716)
XLA Ops:
  0.6 0.5 collective-permute-start.8
  1.2 2.6 %collective-permute-start.3 = (bf16[128,768]{1,0:T(8,128)(2,1)}, bf16[128,768]{1,0:T(8,128)(2,1)S(1)}, u32[]{:S(2)}, u32[]{:S(2)}) collective-permute-start(bf16[128,768]{1,0:T(8,128)(2,1)} %refs_0_.1), channel_id=1, source_target_pairs={{0,2},{1,3},{2,0},{3,1},{4,6},{5,7},{6,4},{7,5},{8,10},{9,11},{10,... | collective-permute-start | bytes 589832 | tf_op jit(solution)/shard_map/ppermute | solution.py:266
  3.7 3.6 %collective-permute-start = (bf16[48,768]{1,0:T(8,128)(2,1)}, bf16[48,768]{1,0:T(8,128)(2,1)S(1)}, u32[]{:S(2)}, u32[]{:S(2)}) collective-permute-start(bf16[48,768]{1,0:T(8,128)(2,1)} %refs_1_.1), channel_id=1, source_target_pairs={{0,12},{1,13},{2,14},{3,15},{4,8},{5,9},{6,10},{7,11},{8,4},{9,5},... | collective-permute-start | bytes 221192 | tf_op jit(solution)/shard_map/ppermute | solution.py:266
  7.3 0.0 collective-permute-start.4
  8.0 1.7 %shard_map.122 = (bf16[144,768]{1,0:T(8,128)(2,1)S(1)}, bf16[48,768]{1,0:T(8,128)(2,1)S(1)}, bf16[16,768]{1,0:T(8,128)(2,1)S(1)}, f32[8,768]{1,0:T(8,128)S(1)}) custom-call(s32[1,1,32]{2,1,0:T(1,128)} %tiles_ref.1, s32[1,1,32]{2,1,0:T(1,128)} %bitcast.15, s32[1,1,32]{2,1,0:T(1,128)} %slots_ref.1, s32[1]{0:T(128)S(6)} %copy.22.length_ref, ...), custom_call_target="tpu_custom_call" | custom-call | tf_op jit(solution)/shard_map/pallas_call | solution.py:303
  9.7 1.1 %collective-permute-done.refs_0_.refs_2_ = bf16[48,768]{1,0:T(8,128)(2,1)S(1)} collective-permute-done((bf16[48,768]{1,0:T(8,128)(2,1)}, bf16[48,768]{1,0:T(8,128)(2,1)S(1)}, u32[]{:S(2)}, u32[]{:S(2)}) %collective-permute-start) | collective-permute-done | bytes 73760 | tf_op jit(solution)/shard_map/ppermute | solution.py:266
  10.8 1.2 %collective-permute-done.4.refs_1_ = bf16[48,768]{1,0:T(8,128)(2,1)S(1)} collective-permute-done((bf16[48,768]{1,0:T(8,128)(2,1)}, bf16[48,768]{1,0:T(8,128)(2,1)S(1)}, u32[]{:S(2)}, u32[]{:S(2)}) %collective-permute-start.4) | collective-permute-done | bytes 73760 | tf_op jit(solution)/shard_map/ppermute | solution.py:266
  12.0 1.4 %collective-permute-start.6 = (bf16[144,768]{1,0:T(8,128)(2,1)S(1)}, bf16[144,768]{1,0:T(8,128)(2,1)S(1)}, u32[]{:S(2)}, u32[]{:S(2)}) collective-permute-start(bf16[144,768]{1,0:T(8,128)(2,1)S(1)} %get-tuple-element.25.refs_1_.refs_3_), channel_id=1, source_target_pairs={{0,4},{1,5},{2,6},{3,7},{4,0},{5,1},{6,2},{7,3},{8,12},{9,13},{10,... | collective-permute-start | bytes 663560 | tf_op jit(solution)/shard_map/ppermute | solution.py:266
  13.4 0.0 collective-permute-done.3.refs_2_
  13.5 0.0 copy-start
  13.5 0.7 %copy-done = bf16[128,768]{1,0:T(8,128)(2,1)} copy-done((bf16[128,768]{1,0:T(8,128)(2,1)}, bf16[128,768]{1,0:T(8,128)(2,1)S(1)}, u32[]{:S(2)}) %copy-start) | copy-done | bytes 196632
  14.1 0.6 collective-permute-start.5
  14.8 1.0 %collective-permute-start.1 = (bf16[144,768]{1,0:T(8,128)(2,1)S(1)}, bf16[144,768]{1,0:T(8,128)(2,1)S(1)}, u32[]{:S(2)}, u32[]{:S(2)}) collective-permute-start(bf16[144,768]{1,0:T(8,128)(2,1)S(1)} %get-tuple-element.25.refs_1_.refs_3_), channel_id=1, source_target_pairs={{0,12},{1,13},{2,14},{3,15},{4,8},{5,9},{6,10},{7,11},{8,4},{9,5},... | collective-permute-start | bytes 663560 | tf_op jit(solution)/shard_map/ppermute | solution.py:266
  15.8 1.1 %collective-permute-start.9 = (bf16[48,768]{1,0:T(8,128)(2,1)S(1)}, bf16[48,768]{1,0:T(8,128)(2,1)S(1)}, u32[]{:S(2)}, u32[]{:S(2)}) collective-permute-start(bf16[48,768]{1,0:T(8,128)(2,1)S(1)} %collective-permute-done.refs_0_.refs_2_), channel_id=1, source_target_pairs={{0,4},{1,5},{2,6},{3,7},{4,0},{5,1},{6,2},{7,3},{8,12},{9,13},{10,... | collective-permute-start | bytes 221192 | tf_op jit(solution)/shard_map/ppermute | solution.py:266
  16.9 7.4 %collective-permute-done.6.refs_0_.refs_5_ = bf16[144,768]{1,0:T(8,128)(2,1)S(1)} collective-permute-done((bf16[144,768]{1,0:T(8,128)(2,1)S(1)}, bf16[144,768]{1,0:T(8,128)(2,1)S(1)}, u32[]{:S(2)}, u32[]{:S(2)}) %collective-permute-start.6) | collective-permute-done | bytes 221216 | tf_op jit(solution)/shard_map/ppermute | solution.py:266
  24.3 0.0 collective-permute-start.7
  24.3 0.8 %collective-permute-done.9.refs_1_.refs_3_ = bf16[48,768]{1,0:T(8,128)(2,1)S(1)} collective-permute-done((bf16[48,768]{1,0:T(8,128)(2,1)S(1)}, bf16[48,768]{1,0:T(8,128)(2,1)S(1)}, u32[]{:S(2)}, u32[]{:S(2)}) %collective-permute-start.9) | collective-permute-done | bytes 73760 | tf_op jit(solution)/shard_map/ppermute | solution.py:266
  25.1 0.0 collective-permute-done.5.refs_4_
  25.1 1.3 %collective-permute-start.10 = (bf16[96,768]{1,0:T(8,128)(2,1)S(1)}, bf16[96,768]{1,0:T(8,128)(2,1)S(1)}, u32[]{:S(2)}, u32[]{:S(2)}) collective-permute-start(bf16[96,768]{1,0:T(8,128)(2,1)S(1)} %shard_map.124), channel_id=1, source_target_pairs={{0,2},{1,3},{2,0},{3,1},{4,6},{5,7},{6,4},{7,5},{8,10},{9,11},{10,... | collective-permute-start | bytes 442376 | tf_op jit(solution)/shard_map/ppermute | solution.py:266
  26.4 0.0 collective-permute-done.1.refs_0_.refs_7_
  26.4 3.8 %collective-permute-done.7.refs_1_.refs_6_ = bf16[144,768]{1,0:T(8,128)(2,1)S(1)} collective-permute-done((bf16[144,768]{1,0:T(8,128)(2,1)S(1)}, bf16[144,768]{1,0:T(8,128)(2,1)S(1)}, u32[]{:S(2)}, u32[]{:S(2)}) %collective-permute-start.7) | collective-permute-done | bytes 221216 | tf_op jit(solution)/shard_map/ppermute | solution.py:266
  30.2 0.0 collective-permute-done.8.refs_9_.refs_5_.refs_14_
  30.2 1.6 %collective-permute-done.10.refs_5_ = bf16[96,768]{1,0:T(8,128)(2,1)S(1)} collective-permute-done((bf16[96,768]{1,0:T(8,128)(2,1)S(1)}, bf16[96,768]{1,0:T(8,128)(2,1)S(1)}, u32[]{:S(2)}, u32[]{:S(2)}) %collective-permute-start.10) | collective-permute-done | bytes 147488 | tf_op jit(solution)/shard_map/ppermute | solution.py:266
  31.8 0.1 collective-permute-start.11
  31.9 1.1 %collective-permute-start.2 = (bf16[144,768]{1,0:T(8,128)(2,1)S(1)}, bf16[144,768]{1,0:T(8,128)(2,1)S(1)}, u32[]{:S(2)}, u32[]{:S(2)}) collective-permute-start(bf16[144,768]{1,0:T(8,128)(2,1)S(1)} %collective-permute-done.1.refs_0_.refs_7_), channel_id=1, source_target_pairs={{0,4},{1,5},{2,6},{3,7},{4,0},{5,1},{6,2},{7,3},{8,12},{9,13},{10,... | collective-permute-start | bytes 663560 | tf_op jit(solution)/shard_map/ppermute | solution.py:266
  33.0 0.0 collective-permute-start.13
  33.0 1.0 %collective-permute-done.11.refs_6_ = bf16[384,768]{1,0:T(8,128)(2,1)} collective-permute-done((bf16[384,768]{1,0:T(8,128)(2,1)S(1)}, bf16[384,768]{1,0:T(8,128)(2,1)}, u32[]{:S(2)}, u32[]{:S(2)}) %collective-permute-start.11) | collective-permute-done | bytes 589856 | tf_op jit(solution)/shard_map/ppermute | solution.py:269
  34.0 0.0 copy-start.1
  34.0 0.9 %copy-done.1 = bf16[128,768]{1,0:T(8,128)(2,1)S(1)} copy-done((bf16[128,768]{1,0:T(8,128)(2,1)S(1)}, bf16[128,768]{1,0:T(8,128)(2,1)}, u32[]{:S(2)}) %copy-start.1) | copy-done | bytes 196632
  35.0 3.1 %shard_map.126 = (f32[8,960]{1,0:T(8,128)S(1)}, f32[8,960]{1,0:T(8,128)S(1)}, bf16[768,768]{1,0:T(8,128)(2,1)S(1)}, bf16[960,768]{1,0:T(8,128)(2,1)S(1)}) custom-call(s32[1]{0:T(128)} %bitcast.refs_0_, bf16[144,768]{1,0:T(8,128)(2,1)S(1)} %get-tuple-element.25.refs_1_.refs_3_, bf16[128,768]{1,0:T(8,128)(2,1)S(1)} %copy-done.1, ...), custom_call_target="tpu_custom_call" | custom-call | flops 2 | bytes 2 | tf_op jit(solution)/shard_map/pallas_call | solution.py:351
  38.1 1.7 %collective-permute-done.2.refs_1_.refs_9_ = bf16[144,768]{1,0:T(8,128)(2,1)S(1)} collective-permute-done((bf16[144,768]{1,0:T(8,128)(2,1)S(1)}, bf16[144,768]{1,0:T(8,128)(2,1)S(1)}, u32[]{:S(2)}, u32[]{:S(2)}) %collective-permute-start.2) | collective-permute-done | bytes 221216 | tf_op jit(solution)/shard_map/ppermute | solution.py:266
  39.8 0.0 collective-permute-start.12
  39.8 1.8 %shard_map.127 = (f32[8,960]{1,0:T(8,128)S(1)}, f32[8,960]{1,0:T(8,128)S(1)}) custom-call(bf16[144,768]{1,0:T(8,128)(2,1)S(1)} %collective-permute-done.6.refs_0_.refs_5_, bf16[144,768]{1,0:T(8,128)(2,1)S(1)} %collective-permute-done.7.refs_1_.refs_6_, bf16[768,768]{1,0:T(8,128)(2,1)S(1)} %get-tuple-element.29.refs_2_.refs_11_, ...), custom_call_target="tpu_custom_call" | custom-call | flops 2 | bytes 2 | tf_op jit(solution)/shard_map/pallas_call | solution.py:378
  41.6 0.0 copy-start.2
  41.6 0.0 collective-permute-done.13.refs_1_.refs_8_
  41.6 1.8 %shard_map.128 = (f32[8,960]{1,0:T(8,128)S(1)}, f32[8,960]{1,0:T(8,128)S(1)}) custom-call(bf16[144,768]{1,0:T(8,128)(2,1)S(1)} %collective-permute-done.1.refs_0_.refs_7_, bf16[144,768]{1,0:T(8,128)(2,1)S(1)} %collective-permute-done.13.refs_1_.refs_8_, bf16[768,768]{1,0:T(8,128)(2,1)S(1)} %get-tuple-element.29.refs_2_.refs_11_, ...), custom_call_target="tpu_custom_call" | custom-call | flops 2 | bytes 2 | tf_op jit(solution)/shard_map/pallas_call | solution.py:378
  43.4 3.4 %collective-permute-done.12.refs_2_.refs_10_ = bf16[144,768]{1,0:T(8,128)(2,1)S(1)} collective-permute-done((bf16[144,768]{1,0:T(8,128)(2,1)S(1)}, bf16[144,768]{1,0:T(8,128)(2,1)S(1)}, u32[]{:S(2)}, u32[]{:S(2)}) %collective-permute-start.12) | collective-permute-done | bytes 221216 | tf_op jit(solution)/shard_map/ppermute | solution.py:266
  46.8 0.0 copy-done.2
  46.8 2.2 %shard_map.129 = bf16[16,48,128]{2,1,0:T(8,128)(2,1)S(1)} custom-call(s32[1]{0:T(128)} %bitcast.refs_0_, bf16[144,768]{1,0:T(8,128)(2,1)S(1)} %collective-permute-done.2.refs_1_.refs_9_, bf16[144,768]{1,0:T(8,128)(2,1)S(1)} %collective-permute-done.12.refs_2_.refs_10_, bf16[144,768]{1,0:T(8,128)(2,1)S(1)} %get-tuple-element.25.refs_1_.refs_3_, ...), custom_call_target="tpu_custom_call" | custom-call | flops 2 | bytes 2 | tf_op jit(solution)/shard_map/pallas_call | solution.py:386
  48.9 11.6 %all_to_all.5 = bf16[16,48,128]{2,1,0:T(8,128)(2,1)S(1)} all-to-all(bf16[16,48,128]{2,1,0:T(8,128)(2,1)S(1)} %shard_map.129), channel_id=1, replica_groups=mesh['groups'=2,'doc'=16,'term'=1] {'doc'}, dimensions={0} | all-to-all | bytes 393216 | tf_op jit(solution)/shard_map/all_to_all | solution.py:407
  60.6 0.7 %slice.26 = bf16[2,15360]{1,0:T(2,128)(2,1)} reshape(bf16[2,8,15,128]{3,2,1,0:T(8,128)(2,1)S(1)} %slice.30) | data formatting | bytes 122880 | tf_op jit(solution)/shard_map/slice | solution.py:410
  61.2 0.6 %slice.24 = bf16[1,15360]{1,0:T(2,128)(2,1)} reshape(bf16[1,8,15,128]{3,2,1,0:T(8,128)(2,1)S(1)} %slice.29) | data formatting | bytes 61440 | tf_op jit(solution)/shard_map/slice | solution.py:410
  (7 shorter events, 0.1 us)
Async XLA Ops:
  0.6 29.6 %collective-permute-start.8 = (bf16[960,768]{1,0:T(8,128)(2,1)}, bf16[960,768]{1,0:T(8,128)(2,1)S(1)}, u32[]{:S(2)}, u32[]{:S(2)}) collective-permute-start(bf16[960,768]{1,0:T(8,128)(2,1)} %bitcast.12), channel_id=1, source_target_pairs={{0,1},{1,0},{2,3},{3,2},{4,5},{5,4},{6,7},{7,6},{8,9},{9,8},{10,11... | collective-permute-start | bytes 4423688 | tf_op jit(solution)/shard_map/ppermute | solution.py:269
  1.2 12.3 %collective-permute-start.3 = (bf16[128,768]{1,0:T(8,128)(2,1)}, bf16[128,768]{1,0:T(8,128)(2,1)S(1)}, u32[]{:S(2)}, u32[]{:S(2)}) collective-permute-start(bf16[128,768]{1,0:T(8,128)(2,1)} %refs_0_.1), channel_id=1, source_target_pairs={{0,2},{1,3},{2,0},{3,1},{4,6},{5,7},{6,4},{7,5},{8,10},{9,11},{10,... | collective-permute-start | bytes 589832 | tf_op jit(solution)/shard_map/ppermute | solution.py:266
  3.7 7.1 %collective-permute-start = (bf16[48,768]{1,0:T(8,128)(2,1)}, bf16[48,768]{1,0:T(8,128)(2,1)S(1)}, u32[]{:S(2)}, u32[]{:S(2)}) collective-permute-start(bf16[48,768]{1,0:T(8,128)(2,1)} %refs_1_.1), channel_id=1, source_target_pairs={{0,12},{1,13},{2,14},{3,15},{4,8},{5,9},{6,10},{7,11},{8,4},{9,5},... | collective-permute-start | bytes 221192 | tf_op jit(solution)/shard_map/ppermute | solution.py:266
  7.3 4.7 %collective-permute-start.4 = (bf16[48,768]{1,0:T(8,128)(2,1)}, bf16[48,768]{1,0:T(8,128)(2,1)S(1)}, u32[]{:S(2)}, u32[]{:S(2)}) collective-permute-start(bf16[48,768]{1,0:T(8,128)(2,1)} %refs_1_.1), channel_id=1, source_target_pairs={{0,4},{1,5},{2,6},{3,7},{4,0},{5,1},{6,2},{7,3},{8,12},{9,13},{10,... | collective-permute-start | bytes 221192 | tf_op jit(solution)/shard_map/ppermute | solution.py:266
  12.0 12.3 %collective-permute-start.6 = (bf16[144,768]{1,0:T(8,128)(2,1)S(1)}, bf16[144,768]{1,0:T(8,128)(2,1)S(1)}, u32[]{:S(2)}, u32[]{:S(2)}) collective-permute-start(bf16[144,768]{1,0:T(8,128)(2,1)S(1)} %get-tuple-element.25.refs_1_.refs_3_), channel_id=1, source_target_pairs={{0,4},{1,5},{2,6},{3,7},{4,0},{5,1},{6,2},{7,3},{8,12},{9,13},{10,... | collective-permute-start | bytes 663560 | tf_op jit(solution)/shard_map/ppermute | solution.py:266
  13.5 0.7 %copy-start = (bf16[128,768]{1,0:T(8,128)(2,1)}, bf16[128,768]{1,0:T(8,128)(2,1)S(1)}, u32[]{:S(2)}) copy-start(bf16[128,768]{1,0:T(8,128)(2,1)S(1)} %collective-permute-done.3.refs_2_) | copy-start | bytes 589828
  14.1 10.9 %collective-permute-start.5 = (bf16[112,768]{1,0:T(8,128)(2,1)S(1)}, bf16[112,768]{1,0:T(8,128)(2,1)S(1)}, u32[]{:S(2)}, u32[]{:S(2)}) collective-permute-start(bf16[112,768]{1,0:T(8,128)(2,1)S(1)} %shard_map.123), channel_id=1, source_target_pairs={{0,2},{1,3},{2,0},{3,1},{4,6},{5,7},{6,4},{7,5},{8,10},{9,11},{10,... | collective-permute-start | bytes 516104 | tf_op jit(solution)/shard_map/ppermute | solution.py:266
  14.8 11.7 %collective-permute-start.1 = (bf16[144,768]{1,0:T(8,128)(2,1)S(1)}, bf16[144,768]{1,0:T(8,128)(2,1)S(1)}, u32[]{:S(2)}, u32[]{:S(2)}) collective-permute-start(bf16[144,768]{1,0:T(8,128)(2,1)S(1)} %get-tuple-element.25.refs_1_.refs_3_), channel_id=1, source_target_pairs={{0,12},{1,13},{2,14},{3,15},{4,8},{5,9},{6,10},{7,11},{8,4},{9,5},... | collective-permute-start | bytes 663560 | tf_op jit(solution)/shard_map/ppermute | solution.py:266
  15.8 9.3 %collective-permute-start.9 = (bf16[48,768]{1,0:T(8,128)(2,1)S(1)}, bf16[48,768]{1,0:T(8,128)(2,1)S(1)}, u32[]{:S(2)}, u32[]{:S(2)}) collective-permute-start(bf16[48,768]{1,0:T(8,128)(2,1)S(1)} %collective-permute-done.refs_0_.refs_2_), channel_id=1, source_target_pairs={{0,4},{1,5},{2,6},{3,7},{4,0},{5,1},{6,2},{7,3},{8,12},{9,13},{10,... | collective-permute-start | bytes 221192 | tf_op jit(solution)/shard_map/ppermute | solution.py:266
  24.3 5.9 %collective-permute-start.7 = (bf16[144,768]{1,0:T(8,128)(2,1)S(1)}, bf16[144,768]{1,0:T(8,128)(2,1)S(1)}, u32[]{:S(2)}, u32[]{:S(2)}) collective-permute-start(bf16[144,768]{1,0:T(8,128)(2,1)S(1)} %collective-permute-done.6.refs_0_.refs_5_), channel_id=1, source_target_pairs={{0,2},{1,3},{2,0},{3,1},{4,6},{5,7},{6,4},{7,5},{8,10},{9,11},{10,... | collective-permute-start | bytes 663560 | tf_op jit(solution)/shard_map/ppermute | solution.py:266
  25.1 6.7 %collective-permute-start.10 = (bf16[96,768]{1,0:T(8,128)(2,1)S(1)}, bf16[96,768]{1,0:T(8,128)(2,1)S(1)}, u32[]{:S(2)}, u32[]{:S(2)}) collective-permute-start(bf16[96,768]{1,0:T(8,128)(2,1)S(1)} %shard_map.124), channel_id=1, source_target_pairs={{0,2},{1,3},{2,0},{3,1},{4,6},{5,7},{6,4},{7,5},{8,10},{9,11},{10,... | collective-permute-start | bytes 442376 | tf_op jit(solution)/shard_map/ppermute | solution.py:266
  31.8 2.2 %collective-permute-start.11 = (bf16[384,768]{1,0:T(8,128)(2,1)S(1)}, bf16[384,768]{1,0:T(8,128)(2,1)}, u32[]{:S(2)}, u32[]{:S(2)}) collective-permute-start(bf16[384,768]{1,0:T(8,128)(2,1)S(1)} %shard_map.125.refs_5_), channel_id=1, source_target_pairs={{0,1},{1,0},{2,3},{3,2},{4,5},{5,4},{6,7},{7,6},{8,9},{9,8},{10,11... | collective-permute-start | bytes 1769480 | tf_op jit(solution)/shard_map/ppermute | solution.py:269
  31.9 7.8 %collective-permute-start.2 = (bf16[144,768]{1,0:T(8,128)(2,1)S(1)}, bf16[144,768]{1,0:T(8,128)(2,1)S(1)}, u32[]{:S(2)}, u32[]{:S(2)}) collective-permute-start(bf16[144,768]{1,0:T(8,128)(2,1)S(1)} %collective-permute-done.1.refs_0_.refs_7_), channel_id=1, source_target_pairs={{0,4},{1,5},{2,6},{3,7},{4,0},{5,1},{6,2},{7,3},{8,12},{9,13},{10,... | collective-permute-start | bytes 663560 | tf_op jit(solution)/shard_map/ppermute | solution.py:266
  33.0 8.5 %collective-permute-start.13 = (bf16[144,768]{1,0:T(8,128)(2,1)S(1)}, bf16[144,768]{1,0:T(8,128)(2,1)S(1)}, u32[]{:S(2)}, u32[]{:S(2)}) collective-permute-start(bf16[144,768]{1,0:T(8,128)(2,1)S(1)} %collective-permute-done.1.refs_0_.refs_7_), channel_id=1, source_target_pairs={{0,2},{1,3},{2,0},{3,1},{4,6},{5,7},{6,4},{7,5},{8,10},{9,11},{10,... | collective-permute-start | bytes 663560 | tf_op jit(solution)/shard_map/ppermute | solution.py:266
  34.0 0.9 %copy-start.1 = (bf16[128,768]{1,0:T(8,128)(2,1)S(1)}, bf16[128,768]{1,0:T(8,128)(2,1)}, u32[]{:S(2)}) copy-start(bf16[128,768]{1,0:T(8,128)(2,1)} %copy-done) | copy-start | bytes 589828
  39.8 7.0 %collective-permute-start.12 = (bf16[144,768]{1,0:T(8,128)(2,1)S(1)}, bf16[144,768]{1,0:T(8,128)(2,1)S(1)}, u32[]{:S(2)}, u32[]{:S(2)}) collective-permute-start(bf16[144,768]{1,0:T(8,128)(2,1)S(1)} %collective-permute-done.2.refs_1_.refs_9_), channel_id=1, source_target_pairs={{0,2},{1,3},{2,0},{3,1},{4,6},{5,7},{6,4},{7,5},{8,10},{9,11},{10,... | collective-permute-start | bytes 663560 | tf_op jit(solution)/shard_map/ppermute | solution.py:266
  41.6 5.2 %copy-start.2 = (f32[15360]{0:T(1024)S(1)}, f32[15360]{0:T(1024)}, u32[]{:S(2)}) copy-start(f32[15360]{0:T(1024)} %param.18) | copy-start | bytes 184324

commit v11 on v10

--- a/solution.py
+++ b/solution.py
@@ -156,11 +156,14 @@
         rows_ref[k : k + 1, :] = kept[pl.ds(k * width, width)][None, :]
 
 
-def pile_kernel(counts, *refs):
+def pile_kernel(parts, heights, *refs):
+    rows = jnp.concatenate(
+        [ref[first : first + count, :] for ref, (first, count) in zip(refs, parts)], axis=0
+    )
     at = 0
-    for ref, count in zip(refs[:-1], counts):
-        refs[-1][at : at + count, :] = ref[0:count, :]
-        at += count
+    for ref, height in zip(refs[len(parts) :], heights):
+        ref[...] = rows[at : at + height, :]
+        at += height
 
 
 def fetch(ref, slot, sem):
@@ -176,28 +179,33 @@
 
 
 def first_kernel(seq, masks, *refs):
-    me_ref, docs, tables, packed, refs = refs[0], refs[1:3], refs[3:5], refs[5:7], refs[7:]
-    params, mine_ref, theirs_ref, best_mine, best_theirs, weight, mine, sem = refs
-    copy = fetch(mine_ref, mine, sem)
+    me_ref, docs, refs = refs[0], refs[1:3], refs[3:]
+    mine_parts, their_parts, refs = refs[:3], refs[3:6], refs[6:]
+    params, theirs_ref, late, refs = refs[0], refs[1], refs[2:5], refs[5:]
+    best_mine, best_theirs, weight, kept, sems = refs[0], refs[1], refs[2], refs[3:6], refs[6]
+    copies = [fetch(ref, to, sems.at[k]) for k, (ref, to) in enumerate(zip(late, kept))]
     me = me_ref[0]
     core = me % 2
     rows = weight.shape[0] // (2 * len(masks))
+    packed = jnp.concatenate([ref[...] for ref in mine_parts], axis=0)
+    others = jnp.concatenate([ref[...] for ref in their_parts], axis=0)
     for k, mask in enumerate(masks):
         chip = (me // 2) ^ mask
         block = slice(k * rows, (k + 1) * rows)
         at = pl.multiple_of((2 * chip + core) * rows, SLOT_ROWS)
-        weight[pl.ds(at, rows), :] = packed[0][block, :]
+        weight[pl.ds(at, rows), :] = packed[block, :]
         at = pl.multiple_of((2 * chip + 1 - core) * rows, SLOT_ROWS)
-        weight[pl.ds(at, rows), :] = packed[1][block, :]
-    normed = normed_rows(docs, tables, seq, weight, params)
+        weight[pl.ds(at, rows), :] = others[block, :]
+    normed = normed_rows(docs, docs, seq, weight, params)
     keep_tops(normed, [theirs_ref], [best_theirs])
-    copy.wait()
-    keep_tops(normed, [mine], [best_mine])
+    for copy in copies:
+        copy.wait()
+    keep_tops(normed, [kept[0]], [best_mine])
 
 
 def next_kernel(seq, *refs):
-    docs, weight, params, halves, bests = refs[:2], refs[2], refs[3], refs[4:6], refs[6:]
-    keep_tops(normed_rows(docs, docs, seq, weight, params), halves, bests)
+    docs, tables, weight, params, refs = refs[:2], refs[2:4], refs[4], refs[5], refs[6:]
+    keep_tops(normed_rows(docs, tables, seq, weight, params), refs[:2], refs[2:])
 
 
 def last_kernel(seq, masks, *refs):
@@ -286,14 +294,16 @@
     def after(value, *done):
         return lax.optimization_barrier((value, *done))[0]
 
-    def pile(values, counts):
-        return pl.pallas_call(
-            lambda *refs: pile_kernel(counts, *refs),
-            out_shape=shape((sum(counts), width), jnp.bfloat16),
+    def pile(values, parts, heights=()):
+        heights = heights or (sum(count for _, count in parts),)
+        piled = pl.pallas_call(
+            lambda *refs: pile_kernel(parts, heights, *refs),
+            out_shape=[shape((height, width), jnp.bfloat16) for height in heights],
             in_specs=[vmem] * len(values),
-            out_specs=vmem,
+            out_specs=[vmem] * len(heights),
             compiler_params=limit,
         )(*values)
+        return piled if len(heights) > 1 else piled[0]
 
     weight_rows = jnp.swapaxes(decoder_weight[0], 0, 1)
     block_6 = cross(transform_weight, 6)
@@ -326,63 +336,74 @@
         stay(norm_gain),
         stay(norm_bias),
     )
-    docs[0] = load
-    docs[2] = cross(after(load, block_2, block_6), 2)
     near = (block, after(block_2, block_6, docs[1]), table)
-    near_pile = cross(pile(near, (rows, rows, SLOT_ROWS)), 1)
+    near_pile = cross(pile(near, ((0, rows), (0, rows), (0, SLOT_ROWS))), 1)
     block_4 = cross(block_6, 2)
     docs[6] = cross(after(load, block_6), 6)
-    far = (block_6, after(block_4, near_pile, docs[2]))
-    far_pile = cross(pile(far, (rows, rows)), 1)
-    docs[3] = cross(docs[2], 1)
-    docs[4] = cross(docs[6], 2)
+    docs[2] = cross(after(load, block_4), 2)
+    load_1 = pile((docs[1], near_pile), ((0, seq), (2 * rows, SLOT_ROWS)))
+    far = (block_6, after(block_4, near_pile))
+    far = pile(far, ((0, rows), (0, rows)))
+    far_pile = cross(far, 1)
+    docs[3] = cross(after(load_1, far), 2)
+    docs[4] = cross(after(docs[6], far), 2)
     docs[7] = cross(docs[6], 1)
-    late = (docs[6], docs[3], theirs)
-    packed = pile(
-        (after(block, *late), block_2, block_6, block_4, near_pile, far_pile),
-        (rows, rows, rows, rows, 2 * rows, 2 * rows),
-    )
-    other_packed = swap(packed)
+    late = (docs[2], docs[3], docs[6], theirs)
+    one, two = (0, rows), (0, 2 * rows)
+    sources = (after(block, *late), block_2, block_6, block_4, near_pile, far_pile)
+    thirds = pile(sources, (one, one, one, one, two, two), (seq,) * 3)
+    other_thirds = [swap(third) for third in thirds]
     block_masks = [0, 2, 6, 4, 1, 3, 7, 5]
 
-    masks = [0, 1, 2, 3, 6, 7, 4, 5]
+    masks = [2, 3, 0, 1, 6, 7, 4, 5]
     where = me[None]
     best_shape = shape((8, half), jnp.float32)
-    *best, weight, mine = pl.pallas_call(
+    *best, weight, mine, own, beside = pl.pallas_call(
         lambda *refs: first_kernel(seq, block_masks, *refs),
         out_shape=[
             best_shape,
             best_shape,
             shape((width, width), jnp.bfloat16),
             shape((half, width), jnp.bfloat16),
+            shape((seq, width), jnp.bfloat16),
+            shape((seq, width), jnp.bfloat16),
         ],
-        in_specs=[smem] + [vmem] * 7 + [hbm, vmem],
-        out_specs=[vmem] * 4,
-        scratch_shapes=[pltpu.SemaphoreType.DMA],
+        in_specs=[smem] + [vmem] * 10 + [hbm] * 3,
+        out_specs=[vmem] * 6,
+        scratch_shapes=[pltpu.SemaphoreType.DMA((3,))],
         compiler_params=limit,
         cost_estimate=cost(2),
     )(
         where,
-        docs[0],
-        docs[1],
-        docs[0],
-        near_pile,
-        packed,
-        other_packed,
+        docs[2],
+        docs[3],
+        *thirds,
+        *other_thirds,
         params,
+        theirs,
         stay(weight_rows),
-        theirs,
-    )
-    docs[5] = cross(after(docs[4], weight), 1)
+        stay(hidden_states),
+        stay(docs[1]),
+    )
+    docs |= {0: own, 1: beside, 5: cross(after(docs[4], weight), 1)}
+    tables = docs | {0: table, 1: near_pile}
     for first in range(2, len(masks) - 2, 2):
+        pair = masks[first : first + 2]
         best += pl.pallas_call(
             lambda *refs: next_kernel(seq, *refs),
             out_shape=[best_shape] * 2,
-            in_specs=[vmem] * 6,
+            in_specs=[vmem] * 8,
             out_specs=[vmem] * 2,
             compiler_params=limit,
             cost_estimate=cost(2),
-        )(*[docs[mask] for mask in masks[first : first + 2]], weight, params, mine, theirs)
+        )(
+            *[docs[mask] for mask in pair],
+            *[tables[mask] for mask in pair],
+            weight,
+            params,
+            mine,
+            theirs,
+        )
     send = pl.pallas_call(
         lambda *refs: last_kernel(seq, masks, *refs),
         out_shape=shape((devices, (1 + BLK_DEV) * SLOT_ROWS, TILE), jnp.bfloat16),
@@ -396,7 +417,7 @@
     )(
         where,
         *[docs[mask] for mask in masks[-2:]],
-        *[near_pile if mask == 1 else docs[mask] for mask in masks],
+        *[tables[mask] for mask in masks],
         weight,
         params,
         mine,

time: 62.2 us -> 64 us (1.029)
  waiting for transfers between devices: 21.9 us -> 16.3 us
  starting transfers between devices: 13.4 us -> 18.9 us
  blocking collectives: 11.6 us -> 14.9 us
  local copies, waits for them, and re-layouts: 2.94 us -> 1.34 us
    ppermute x12, starting transfers between devices: 12.8 us -> 17.8 us  [cross(): lax.ppermute(value, 'doc', [(i, i ^ 2 * mask) for i in range(devices)])]
    ppermute x12, waiting for transfers between devices: 20.9 us -> 16.2 us  [cross(): lax.ppermute(value, 'doc', [(i, i ^ 2 * mask) for i in range(devices)])]
    all_to_all x1, blocking collectives: 11.6 us -> 14.9 us  [move_tokens(): got = lax.all_to_all(send, 'doc', split_axis=0, concat_axis=0, tiled=True)]
    unnamed x6 -> x4, local copies, waits for them, and re-layouts: 1.62 us -> 0.01 us
    ppermute x2 -> x4, waiting for transfers between devices: 1.01 us -> 0.02 us  [swap(): return lax.ppermute(value, 'doc', [(i, i ^ 1) for i in range(devices)])]
  transfers between devices with their start and end apart: 14 -> 16, of which waited for: 9 -> 8; matrix products, arithmetic and copies ran while one was open for 0% -> 0% of each run, Pallas kernels for 14% -> 14%
where the time goes in v11:
time: 64 us; the launch traced here: 63.7 us
  starting transfers between devices  18.9 us (30%)
  waiting for transfers between devices  16.3 us (25%)
  blocking collectives  14.9 us (23%)
  Pallas kernels  10.9 us (17%)
  between operations  1.42 us (2%)
  local copies, waits for them, and re-layouts  1.34 us (2%)
    ppermute x12, starting transfers between devices, cross(): lax.ppermute(value, 'doc', [(i, i ^ 2 * mask) for i in range(devices)])  17.8 us
    ppermute x12, waiting for transfers between devices, cross(): lax.ppermute(value, 'doc', [(i, i ^ 2 * mask) for i in range(devices)])  16.2 us
    all_to_all x1, blocking collectives, move_tokens(): got = lax.all_to_all(send, 'doc', split_axis=0, concat_axis=0, tiled=True)  14.9 us
    pallas_call x2, Pallas kernels, move_tokens(): pl.pallas_call(lambda *refs: next_kernel(seq, *refs), out_shape=[best_sha...  3.55 us
    pallas_call x1, Pallas kernels, move_tokens(): pl.pallas_call(lambda *refs: first_kernel(seq, block_masks, *refs), out_s...  3.41 us
    pallas_call x1, Pallas kernels, move_tokens(): pl.pallas_call(lambda *refs: last_kernel(seq, masks, *refs), out_shape=sh...  2.14 us
    pallas_call x1, Pallas kernels, move_tokens(): pl.pallas_call(start_kernel, out_shape=[shape((seq + SLOT_ROWS, width), j...  1.71 us
    slice x4, local copies, waits for them, and re-layouts, move_tokens(): return (whole[:1], whole[1:])  1.31 us
  transfers between devices with their start and end apart: 16, of which 8 were waited for; matrix products, arithmetic and copies ran while one was open for 0% of the time, Pallas kernels for 14%

profile of v11, /device:TPU:0, one launch (start us, length us, event | category | flops | bytes accessed | tf_op | source)
XLA Modules:
  0.0 63.7 jit_solution(7146049261914794402)
XLA Ops:
  0.6 0.5 collective-permute-start.9
  1.2 2.6 %collective-permute-start.4 = (bf16[128,768]{1,0:T(8,128)(2,1)}, bf16[128,768]{1,0:T(8,128)(2,1)S(1)}, u32[]{:S(2)}, u32[]{:S(2)}) collective-permute-start(bf16[128,768]{1,0:T(8,128)(2,1)} %refs_12_.1), channel_id=1, source_target_pairs={{0,2},{1,3},{2,0},{3,1},{4,6},{5,7},{6,4},{7,5},{8,10},{9,11},{10,... | collective-permute-start | bytes 589832 | tf_op jit(solution)/shard_map/ppermute | solution.py:274
  3.7 3.6 %collective-permute-start = (bf16[48,768]{1,0:T(8,128)(2,1)}, bf16[48,768]{1,0:T(8,128)(2,1)S(1)}, u32[]{:S(2)}, u32[]{:S(2)}) collective-permute-start(bf16[48,768]{1,0:T(8,128)(2,1)} %refs_1_.1), channel_id=1, source_target_pairs={{0,12},{1,13},{2,14},{3,15},{4,8},{5,9},{6,10},{7,11},{8,4},{9,5},... | collective-permute-start | bytes 221192 | tf_op jit(solution)/shard_map/ppermute | solution.py:274
  7.3 0.0 collective-permute-start.3
  8.0 1.7 %shard_map.122 = (bf16[144,768]{1,0:T(8,128)(2,1)S(1)}, bf16[48,768]{1,0:T(8,128)(2,1)S(1)}, bf16[16,768]{1,0:T(8,128)(2,1)S(1)}, f32[8,768]{1,0:T(8,128)S(1)}) custom-call(s32[1,1,32]{2,1,0:T(1,128)} %tiles_ref.1, s32[1,1,32]{2,1,0:T(1,128)} %bitcast.15, s32[1,1,32]{2,1,0:T(1,128)} %slots_ref.1, s32[1]{0:T(128)S(6)} %copy.22.length_ref, ...), custom_call_target="tpu_custom_call" | custom-call | tf_op jit(solution)/shard_map/pallas_call | solution.py:313
  9.7 1.1 %collective-permute-done.refs_0_.refs_2_ = bf16[48,768]{1,0:T(8,128)(2,1)S(1)} collective-permute-done((bf16[48,768]{1,0:T(8,128)(2,1)}, bf16[48,768]{1,0:T(8,128)(2,1)S(1)}, u32[]{:S(2)}, u32[]{:S(2)}) %collective-permute-start) | collective-permute-done | bytes 73760 | tf_op jit(solution)/shard_map/ppermute | solution.py:274
  10.8 1.2 %collective-permute-done.3.refs_1_ = bf16[48,768]{1,0:T(8,128)(2,1)S(1)} collective-permute-done((bf16[48,768]{1,0:T(8,128)(2,1)}, bf16[48,768]{1,0:T(8,128)(2,1)S(1)}, u32[]{:S(2)}, u32[]{:S(2)}) %collective-permute-start.3) | collective-permute-done | bytes 73760 | tf_op jit(solution)/shard_map/ppermute | solution.py:274
  12.0 0.0 collective-permute-done.4.refs_0_.refs_13_
  12.0 0.0 copy-start
  12.0 0.5 collective-permute-start.5
  12.5 1.6 %collective-permute-start.2 = (bf16[48,768]{1,0:T(8,128)(2,1)S(1)}, bf16[48,768]{1,0:T(8,128)(2,1)S(1)}, u32[]{:S(2)}, u32[]{:S(2)}) collective-permute-start(bf16[48,768]{1,0:T(8,128)(2,1)S(1)} %collective-permute-done.refs_0_.refs_2_), channel_id=1, source_target_pairs={{0,4},{1,5},{2,6},{3,7},{4,0},{5,1},{6,2},{7,3},{8,12},{9,13},{10,... | collective-permute-start | bytes 221192 | tf_op jit(solution)/shard_map/ppermute | solution.py:274
  14.1 1.2 %collective-permute-start.1 = (bf16[144,768]{1,0:T(8,128)(2,1)S(1)}, bf16[144,768]{1,0:T(8,128)(2,1)S(1)}, u32[]{:S(2)}, u32[]{:S(2)}) collective-permute-start(bf16[144,768]{1,0:T(8,128)(2,1)S(1)} %get-tuple-element.34), channel_id=1, source_target_pairs={{0,12},{1,13},{2,14},{3,15},{4,8},{5,9},{6,10},{7,11},{8,4},{9,5},... | collective-permute-start | bytes 663560 | tf_op jit(solution)/shard_map/ppermute | solution.py:274
  15.3 1.6 %collective-permute-done.2.refs_1_.refs_3_ = bf16[48,768]{1,0:T(8,128)(2,1)S(1)} collective-permute-done((bf16[48,768]{1,0:T(8,128)(2,1)S(1)}, bf16[48,768]{1,0:T(8,128)(2,1)S(1)}, u32[]{:S(2)}, u32[]{:S(2)}) %collective-permute-start.2) | collective-permute-done | bytes 73760 | tf_op jit(solution)/shard_map/ppermute | solution.py:274
  16.9 2.3 %collective-permute-start.7 = (bf16[144,768]{1,0:T(8,128)(2,1)S(1)}, bf16[144,768]{1,0:T(8,128)(2,1)S(1)}, u32[]{:S(2)}, u32[]{:S(2)}) collective-permute-start(bf16[144,768]{1,0:T(8,128)(2,1)S(1)} %get-tuple-element.34), channel_id=1, source_target_pairs={{0,4},{1,5},{2,6},{3,7},{4,0},{5,1},{6,2},{7,3},{8,12},{9,13},{10,... | collective-permute-start | bytes 663560 | tf_op jit(solution)/shard_map/ppermute | solution.py:274
  19.2 0.0 collective-permute-done.5.refs_1_.refs_4_.refs_3_.refs_6_
  19.2 0.1 collective-permute-start.8
  19.3 1.7 %collective-permute-start.10 = (bf16[96,768]{1,0:T(8,128)(2,1)S(1)}, bf16[96,768]{1,0:T(8,128)(2,1)S(1)}, u32[]{:S(2)}, u32[]{:S(2)}) collective-permute-start(bf16[96,768]{1,0:T(8,128)(2,1)S(1)} %shard_map.124), channel_id=1, source_target_pairs={{0,2},{1,3},{2,0},{3,1},{4,6},{5,7},{6,4},{7,5},{8,10},{9,11},{10,... | collective-permute-start | bytes 442376 | tf_op jit(solution)/shard_map/ppermute | solution.py:274
  21.0 3.3 %collective-permute-done.1.refs_0_.refs_2_.refs_7_ = bf16[144,768]{1,0:T(8,128)(2,1)S(1)} collective-permute-done((bf16[144,768]{1,0:T(8,128)(2,1)S(1)}, bf16[144,768]{1,0:T(8,128)(2,1)S(1)}, u32[]{:S(2)}, u32[]{:S(2)}) %collective-permute-start.1) | collective-permute-done | bytes 221216 | tf_op jit(solution)/shard_map/ppermute | solution.py:274
  24.2 1.2 %collective-permute-start.6 = (bf16[144,768]{1,0:T(8,128)(2,1)S(1)}, bf16[144,768]{1,0:T(8,128)(2,1)S(1)}, u32[]{:S(2)}, u32[]{:S(2)}) collective-permute-start(bf16[144,768]{1,0:T(8,128)(2,1)S(1)} %collective-permute-done.1.refs_0_.refs_2_.refs_7_), channel_id=1, source_target_pairs={{0,4},{1,5},{2,6},{3,7},{4,0},{5,1},{6,2},{7,3},{8,12},{9,13},{10,... | collective-permute-start | bytes 663560 | tf_op jit(solution)/shard_map/ppermute | solution.py:274
  25.4 1.9 %collective-permute-done.7.refs_1_.refs_3_ = bf16[144,768]{1,0:T(8,128)(2,1)S(1)} collective-permute-done((bf16[144,768]{1,0:T(8,128)(2,1)S(1)}, bf16[144,768]{1,0:T(8,128)(2,1)S(1)}, u32[]{:S(2)}, u32[]{:S(2)}) %collective-permute-start.7) | collective-permute-done | bytes 221216 | tf_op jit(solution)/shard_map/ppermute | solution.py:274
  27.3 4.7 %collective-permute-done.8.refs_2_.refs_4_ = bf16[144,768]{1,0:T(8,128)(2,1)S(1)} collective-permute-done((bf16[144,768]{1,0:T(8,128)(2,1)S(1)}, bf16[144,768]{1,0:T(8,128)(2,1)S(1)}, u32[]{:S(2)}, u32[]{:S(2)}) %collective-permute-start.8) | collective-permute-done | bytes 221216 | tf_op jit(solution)/shard_map/ppermute | solution.py:274
  32.0 0.0 collective-permute-done.9.refs_10_.refs_7_.refs_14_
  32.0 0.0 collective-permute-done.10.refs_5_
  32.1 0.1 collective-permute-start.11
  32.2 0.5 collective-permute-start.12
  32.7 0.1 collective-permute-start.13
  32.7 1.5 %collective-permute-start.15 = (bf16[144,768]{1,0:T(8,128)(2,1)S(1)}, bf16[144,768]{1,0:T(8,128)(2,1)S(1)}, u32[]{:S(2)}, u32[]{:S(2)}) collective-permute-start(bf16[144,768]{1,0:T(8,128)(2,1)S(1)} %collective-permute-done.1.refs_0_.refs_2_.refs_7_), channel_id=1, source_target_pairs={{0,2},{1,3},{2,0},{3,1},{4,6},{5,7},{6,4},{7,5},{8,10},{9,11},{10,... | collective-permute-start | bytes 663560 | tf_op jit(solution)/shard_map/ppermute | solution.py:274
  34.3 0.0 collective-permute-done.11.refs_6_
  34.3 0.0 collective-permute-done.12.refs_7_
  34.3 0.0 collective-permute-done.13.refs_8_
  34.3 0.0 copy-done
  34.3 3.4 %shard_map.127 = (f32[8,960]{1,0:T(8,128)S(1)}, f32[8,960]{1,0:T(8,128)S(1)}, bf16[768,768]{1,0:T(8,128)(2,1)S(1)}, bf16[960,768]{1,0:T(8,128)(2,1)S(1)}, bf16[1...) custom-call(s32[1]{0:T(128)} %bitcast.refs_0_, bf16[144,768]{1,0:T(8,128)(2,1)S(1)} %collective-permute-done.7.refs_1_.refs_3_, ...), custom_call_target="tpu_custom_call" | custom-call | flops 2 | bytes 2 | tf_op jit(solution)/shard_map/pallas_call | solution.py:361
  37.7 0.0 collective-permute-done.6.refs_1_.refs_9_
  37.7 1.6 %collective-permute-start.14 = (bf16[144,768]{1,0:T(8,128)(2,1)S(1)}, bf16[144,768]{1,0:T(8,128)(2,1)S(1)}, u32[]{:S(2)}, u32[]{:S(2)}) collective-permute-start(bf16[144,768]{1,0:T(8,128)(2,1)S(1)} %collective-permute-done.6.refs_1_.refs_9_), channel_id=1, source_target_pairs={{0,2},{1,3},{2,0},{3,1},{4,6},{5,7},{6,4},{7,5},{8,10},{9,11},{10,... | collective-permute-start | bytes 663560 | tf_op jit(solution)/shard_map/ppermute | solution.py:274
  39.3 1.2 %collective-permute-done.15.refs_1_.refs_3_.refs_8_ = bf16[144,768]{1,0:T(8,128)(2,1)S(1)} collective-permute-done((bf16[144,768]{1,0:T(8,128)(2,1)S(1)}, bf16[144,768]{1,0:T(8,128)(2,1)S(1)}, u32[]{:S(2)}, u32[]{:S(2)}) %collective-permute-start.15) | collective-permute-done | bytes 221216 | tf_op jit(solution)/shard_map/ppermute | solution.py:274
  40.5 1.8 %shard_map.129 = (f32[8,960]{1,0:T(8,128)S(1)}, f32[8,960]{1,0:T(8,128)S(1)}) custom-call(bf16[144,768]{1,0:T(8,128)(2,1)S(1)} %collective-permute-done.1.refs_0_.refs_2_.refs_7_, bf16[144,768]{1,0:T(8,128)(2,1)S(1)} %collective-permute-done.15.refs_1_.refs_3_.refs_8_, bf16[144,768]{1,0:T(8,128)(2,1)S(1)} %collective-permute-done.1.refs_0_.refs_2_.refs_7_, ...), custom_call_target="tpu_custom_call" | custom-call | flops 2 | bytes 2 | tf_op jit(solution)/shard_map/pallas_call | solution.py:392
  42.3 0.0 copy-start.1
  42.3 1.8 %shard_map.128 = (f32[8,960]{1,0:T(8,128)S(1)}, f32[8,960]{1,0:T(8,128)S(1)}) custom-call(bf16[128,768]{1,0:T(8,128)(2,1)S(1)} %get-tuple-element.46.refs_0_, bf16[128,768]{1,0:T(8,128)(2,1)S(1)} %get-tuple-element.47.refs_1_, bf16[16,768]{1,0:T(8,128)(2,1)S(1)} %get-tuple-element.31.refs_2_.refs_5_, ...), custom_call_target="tpu_custom_call" | custom-call | flops 2 | bytes 2 | tf_op jit(solution)/shard_map/pallas_call | solution.py:392
  44.1 1.2 %collective-permute-done.14.refs_2_.refs_10_ = bf16[144,768]{1,0:T(8,128)(2,1)S(1)} collective-permute-done((bf16[144,768]{1,0:T(8,128)(2,1)S(1)}, bf16[144,768]{1,0:T(8,128)(2,1)S(1)}, u32[]{:S(2)}, u32[]{:S(2)}) %collective-permute-start.14) | collective-permute-done | bytes 221216 | tf_op jit(solution)/shard_map/ppermute | solution.py:274
  45.3 0.0 copy-done.1
  45.3 2.1 %shard_map.130 = bf16[16,48,128]{2,1,0:T(8,128)(2,1)S(1)} custom-call(s32[1]{0:T(128)} %bitcast.refs_0_, bf16[144,768]{1,0:T(8,128)(2,1)S(1)} %collective-permute-done.6.refs_1_.refs_9_, bf16[144,768]{1,0:T(8,128)(2,1)S(1)} %collective-permute-done.14.refs_2_.refs_10_, bf16[144,768]{1,0:T(8,128)(2,1)S(1)} %collective-permute-done.7.refs_1_.refs_3_, ...), custom_call_target="tpu_custom_call" | custom-call | flops 2 | bytes 2 | tf_op jit(solution)/shard_map/pallas_call | solution.py:407
  47.5 14.9 %all_to_all.5 = bf16[16,48,128]{2,1,0:T(8,128)(2,1)S(1)} all-to-all(bf16[16,48,128]{2,1,0:T(8,128)(2,1)S(1)} %shard_map.130), channel_id=1, replica_groups=mesh['groups'=2,'doc'=16,'term'=1] {'doc'}, dimensions={0} | all-to-all | bytes 393216 | tf_op jit(solution)/shard_map/all_to_all | solution.py:428
  62.4 0.7 %slice.26 = bf16[2,15360]{1,0:T(2,128)(2,1)} reshape(bf16[2,8,15,128]{3,2,1,0:T(8,128)(2,1)S(1)} %slice.30) | data formatting | bytes 122880 | tf_op jit(solution)/shard_map/slice | solution.py:431
  63.1 0.6 %slice.24 = bf16[1,15360]{1,0:T(2,128)(2,1)} reshape(bf16[1,8,15,128]{3,2,1,0:T(8,128)(2,1)S(1)} %slice.29) | data formatting | bytes 61440 | tf_op jit(solution)/shard_map/slice | solution.py:431
  (8 shorter events, 0.1 us)
Async XLA Ops:
  0.6 31.4 %collective-permute-start.9 = (bf16[960,768]{1,0:T(8,128)(2,1)}, bf16[960,768]{1,0:T(8,128)(2,1)S(1)}, u32[]{:S(2)}, u32[]{:S(2)}) collective-permute-start(bf16[960,768]{1,0:T(8,128)(2,1)} %bitcast.12), channel_id=1, source_target_pairs={{0,1},{1,0},{2,3},{3,2},{4,5},{5,4},{6,7},{7,6},{8,9},{9,8},{10,11... | collective-permute-start | bytes 4423688 | tf_op jit(solution)/shard_map/ppermute | solution.py:277
  1.2 10.9 %collective-permute-start.4 = (bf16[128,768]{1,0:T(8,128)(2,1)}, bf16[128,768]{1,0:T(8,128)(2,1)S(1)}, u32[]{:S(2)}, u32[]{:S(2)}) collective-permute-start(bf16[128,768]{1,0:T(8,128)(2,1)} %refs_12_.1), channel_id=1, source_target_pairs={{0,2},{1,3},{2,0},{3,1},{4,6},{5,7},{6,4},{7,5},{8,10},{9,11},{10,... | collective-permute-start | bytes 589832 | tf_op jit(solution)/shard_map/ppermute | solution.py:274
  3.7 7.1 %collective-permute-start = (bf16[48,768]{1,0:T(8,128)(2,1)}, bf16[48,768]{1,0:T(8,128)(2,1)S(1)}, u32[]{:S(2)}, u32[]{:S(2)}) collective-permute-start(bf16[48,768]{1,0:T(8,128)(2,1)} %refs_1_.1), channel_id=1, source_target_pairs={{0,12},{1,13},{2,14},{3,15},{4,8},{5,9},{6,10},{7,11},{8,4},{9,5},... | collective-permute-start | bytes 221192 | tf_op jit(solution)/shard_map/ppermute | solution.py:274
  7.3 4.7 %collective-permute-start.3 = (bf16[48,768]{1,0:T(8,128)(2,1)}, bf16[48,768]{1,0:T(8,128)(2,1)S(1)}, u32[]{:S(2)}, u32[]{:S(2)}) collective-permute-start(bf16[48,768]{1,0:T(8,128)(2,1)} %refs_1_.1), channel_id=1, source_target_pairs={{0,4},{1,5},{2,6},{3,7},{4,0},{5,1},{6,2},{7,3},{8,12},{9,13},{10,... | collective-permute-start | bytes 221192 | tf_op jit(solution)/shard_map/ppermute | solution.py:274
  12.0 22.3 %copy-start = (bf16[128,768]{1,0:T(8,128)(2,1)}, bf16[128,768]{1,0:T(8,128)(2,1)S(1)}, u32[]{:S(2)}) copy-start(bf16[128,768]{1,0:T(8,128)(2,1)S(1)} %collective-permute-done.4.refs_0_.refs_13_) | copy-start | bytes 589828
  12.0 7.1 %collective-permute-start.5 = (bf16[112,768]{1,0:T(8,128)(2,1)S(1)}, bf16[112,768]{1,0:T(8,128)(2,1)S(1)}, u32[]{:S(2)}, u32[]{:S(2)}) collective-permute-start(bf16[112,768]{1,0:T(8,128)(2,1)S(1)} %shard_map.123), channel_id=1, source_target_pairs={{0,2},{1,3},{2,0},{3,1},{4,6},{5,7},{6,4},{7,5},{8,10},{9,11},{10,... | collective-permute-start | bytes 516104 | tf_op jit(solution)/shard_map/ppermute | solution.py:274
  12.5 4.4 %collective-permute-start.2 = (bf16[48,768]{1,0:T(8,128)(2,1)S(1)}, bf16[48,768]{1,0:T(8,128)(2,1)S(1)}, u32[]{:S(2)}, u32[]{:S(2)}) collective-permute-start(bf16[48,768]{1,0:T(8,128)(2,1)S(1)} %collective-permute-done.refs_0_.refs_2_), channel_id=1, source_target_pairs={{0,4},{1,5},{2,6},{3,7},{4,0},{5,1},{6,2},{7,3},{8,12},{9,13},{10,... | collective-permute-start | bytes 221192 | tf_op jit(solution)/shard_map/ppermute | solution.py:274
  14.1 10.2 %collective-permute-start.1 = (bf16[144,768]{1,0:T(8,128)(2,1)S(1)}, bf16[144,768]{1,0:T(8,128)(2,1)S(1)}, u32[]{:S(2)}, u32[]{:S(2)}) collective-permute-start(bf16[144,768]{1,0:T(8,128)(2,1)S(1)} %get-tuple-element.34), channel_id=1, source_target_pairs={{0,12},{1,13},{2,14},{3,15},{4,8},{5,9},{6,10},{7,11},{8,4},{9,5},... | collective-permute-start | bytes 663560 | tf_op jit(solution)/shard_map/ppermute | solution.py:274
  16.9 10.4 %collective-permute-start.7 = (bf16[144,768]{1,0:T(8,128)(2,1)S(1)}, bf16[144,768]{1,0:T(8,128)(2,1)S(1)}, u32[]{:S(2)}, u32[]{:S(2)}) collective-permute-start(bf16[144,768]{1,0:T(8,128)(2,1)S(1)} %get-tuple-element.34), channel_id=1, source_target_pairs={{0,4},{1,5},{2,6},{3,7},{4,0},{5,1},{6,2},{7,3},{8,12},{9,13},{10,... | collective-permute-start | bytes 663560 | tf_op jit(solution)/shard_map/ppermute | solution.py:274
  19.2 12.8 %collective-permute-start.8 = (bf16[144,768]{1,0:T(8,128)(2,1)S(1)}, bf16[144,768]{1,0:T(8,128)(2,1)S(1)}, u32[]{:S(2)}, u32[]{:S(2)}) collective-permute-start(bf16[144,768]{1,0:T(8,128)(2,1)S(1)} %shard_map.125), channel_id=1, source_target_pairs={{0,4},{1,5},{2,6},{3,7},{4,0},{5,1},{6,2},{7,3},{8,12},{9,13},{10,... | collective-permute-start | bytes 663560 | tf_op jit(solution)/shard_map/ppermute | solution.py:274
  19.3 12.8 %collective-permute-start.10 = (bf16[96,768]{1,0:T(8,128)(2,1)S(1)}, bf16[96,768]{1,0:T(8,128)(2,1)S(1)}, u32[]{:S(2)}, u32[]{:S(2)}) collective-permute-start(bf16[96,768]{1,0:T(8,128)(2,1)S(1)} %shard_map.124), channel_id=1, source_target_pairs={{0,2},{1,3},{2,0},{3,1},{4,6},{5,7},{6,4},{7,5},{8,10},{9,11},{10,... | collective-permute-start | bytes 442376 | tf_op jit(solution)/shard_map/ppermute | solution.py:274
  24.2 13.5 %collective-permute-start.6 = (bf16[144,768]{1,0:T(8,128)(2,1)S(1)}, bf16[144,768]{1,0:T(8,128)(2,1)S(1)}, u32[]{:S(2)}, u32[]{:S(2)}) collective-permute-start(bf16[144,768]{1,0:T(8,128)(2,1)S(1)} %collective-permute-done.1.refs_0_.refs_2_.refs_7_), channel_id=1, source_target_pairs={{0,4},{1,5},{2,6},{3,7},{4,0},{5,1},{6,2},{7,3},{8,12},{9,13},{10,... | collective-permute-start | bytes 663560 | tf_op jit(solution)/shard_map/ppermute | solution.py:274
  32.1 2.2 %collective-permute-start.11 = (bf16[128,768]{1,0:T(8,128)(2,1)S(1)}, bf16[128,768]{1,0:T(8,128)(2,1)}, u32[]{:S(2)}, u32[]{:S(2)}) collective-permute-start(bf16[128,768]{1,0:T(8,128)(2,1)S(1)} %get-tuple-element.37.refs_3_), channel_id=1, source_target_pairs={{0,1},{1,0},{2,3},{3,2},{4,5},{5,4},{6,7},{7,6},{8,9},{9,8},{10,11... | collective-permute-start | bytes 589832 | tf_op jit(solution)/shard_map/ppermute | solution.py:277
  32.2 2.1 %collective-permute-start.12 = (bf16[128,768]{1,0:T(8,128)(2,1)S(1)}, bf16[128,768]{1,0:T(8,128)(2,1)}, u32[]{:S(2)}, u32[]{:S(2)}) collective-permute-start(bf16[128,768]{1,0:T(8,128)(2,1)S(1)} %get-tuple-element.38.refs_4_), channel_id=1, source_target_pairs={{0,1},{1,0},{2,3},{3,2},{4,5},{5,4},{6,7},{7,6},{8,9},{9,8},{10,11... | collective-permute-start | bytes 589832 | tf_op jit(solution)/shard_map/ppermute | solution.py:277
  32.7 1.6 %collective-permute-start.13 = (bf16[128,768]{1,0:T(8,128)(2,1)S(1)}, bf16[128,768]{1,0:T(8,128)(2,1)}, u32[]{:S(2)}, u32[]{:S(2)}) collective-permute-start(bf16[128,768]{1,0:T(8,128)(2,1)S(1)} %get-tuple-element.39.refs_5_), channel_id=1, source_target_pairs={{0,1},{1,0},{2,3},{3,2},{4,5},{5,4},{6,7},{7,6},{8,9},{9,8},{10,11... | collective-permute-start | bytes 589832 | tf_op jit(solution)/shard_map/ppermute | solution.py:277
  32.7 7.8 %collective-permute-start.15 = (bf16[144,768]{1,0:T(8,128)(2,1)S(1)}, bf16[144,768]{1,0:T(8,128)(2,1)S(1)}, u32[]{:S(2)}, u32[]{:S(2)}) collective-permute-start(bf16[144,768]{1,0:T(8,128)(2,1)S(1)} %collective-permute-done.1.refs_0_.refs_2_.refs_7_), channel_id=1, source_target_pairs={{0,2},{1,3},{2,0},{3,1},{4,6},{5,7},{6,4},{7,5},{8,10},{9,11},{10,... | collective-permute-start | bytes 663560 | tf_op jit(solution)/shard_map/ppermute | solution.py:274
  37.7 7.6 %collective-permute-start.14 = (bf16[144,768]{1,0:T(8,128)(2,1)S(1)}, bf16[144,768]{1,0:T(8,128)(2,1)S(1)}, u32[]{:S(2)}, u32[]{:S(2)}) collective-permute-start(bf16[144,768]{1,0:T(8,128)(2,1)S(1)} %collective-permute-done.6.refs_1_.refs_9_), channel_id=1, source_target_pairs={{0,2},{1,3},{2,0},{3,1},{4,6},{5,7},{6,4},{7,5},{8,10},{9,11},{10,... | collective-permute-start | bytes 663560 | tf_op jit(solution)/shard_map/ppermute | solution.py:274
  42.3 3.0 %copy-start.1 = (f32[15360]{0:T(1024)S(1)}, f32[15360]{0:T(1024)}, u32[]{:S(2)}) copy-start(f32[15360]{0:T(1024)} %param.18) | copy-start | bytes 184324

commit v12 on v11

--- a/solution.py
+++ b/solution.py
@@ -178,12 +178,16 @@
             best[j : j + 1, :] = top
 
 
+def fetch_kernel(count, *refs):
+    copies = [fetch(refs[1 + k], refs[1 + count + k], refs[-1].at[k]) for k in range(count)]
+    for copy in copies:
+        copy.wait()
+
+
 def first_kernel(seq, masks, *refs):
-    me_ref, docs, refs = refs[0], refs[1:3], refs[3:]
-    mine_parts, their_parts, refs = refs[:3], refs[3:6], refs[6:]
-    params, theirs_ref, late, refs = refs[0], refs[1], refs[2:5], refs[5:]
-    best_mine, best_theirs, weight, kept, sems = refs[0], refs[1], refs[2], refs[3:6], refs[6]
-    copies = [fetch(ref, to, sems.at[k]) for k, (ref, to) in enumerate(zip(late, kept))]
+    me_ref, docs, tables, refs = refs[0], refs[1:3], refs[3:5], refs[5:]
+    mine_parts, their_parts, params, halves, refs = refs[:3], refs[3:6], refs[6], refs[7:9], refs[9:]
+    bests, weight = refs[:2], refs[2]
     me = me_ref[0]
     core = me % 2
     rows = weight.shape[0] // (2 * len(masks))
@@ -196,11 +200,7 @@
         weight[pl.ds(at, rows), :] = packed[block, :]
         at = pl.multiple_of((2 * chip + 1 - core) * rows, SLOT_ROWS)
         weight[pl.ds(at, rows), :] = others[block, :]
-    normed = normed_rows(docs, docs, seq, weight, params)
-    keep_tops(normed, [theirs_ref], [best_theirs])
-    for copy in copies:
-        copy.wait()
-    keep_tops(normed, [kept[0]], [best_mine])
+    keep_tops(normed_rows(docs, tables, seq, weight, params), halves, bests)
 
 
 def next_kernel(seq, *refs):
@@ -346,47 +346,49 @@
     far = pile(far, ((0, rows), (0, rows)))
     far_pile = cross(far, 1)
     docs[3] = cross(after(load_1, far), 2)
-    docs[4] = cross(after(docs[6], far), 2)
+    docs[4] = cross(after(docs[6], far, docs[2]), 2)
     docs[7] = cross(docs[6], 1)
-    late = (docs[2], docs[3], docs[6], theirs)
+    late = (docs[6], theirs)
     one, two = (0, rows), (0, 2 * rows)
     sources = (after(block, *late), block_2, block_6, block_4, near_pile, far_pile)
     thirds = pile(sources, (one, one, one, one, two, two), (seq,) * 3)
     other_thirds = [swap(third) for third in thirds]
     block_masks = [0, 2, 6, 4, 1, 3, 7, 5]
 
-    masks = [2, 3, 0, 1, 6, 7, 4, 5]
+    far_from = [stay(after(weight_rows, *thirds)), stay(docs[1])]
+    mine, beside = pl.pallas_call(
+        lambda *refs: fetch_kernel(2, *refs),
+        out_shape=[shape(value.shape, value.dtype) for value in far_from],
+        in_specs=[vmem] + [hbm] * 2,
+        out_specs=[vmem] * 2,
+        scratch_shapes=[pltpu.SemaphoreType.DMA((2,))],
+        compiler_params=limit,
+    )(thirds[0], *far_from)
+
+    masks = [0, 1, 6, 7, 2, 3, 4, 5]
     where = me[None]
     best_shape = shape((8, half), jnp.float32)
-    *best, weight, mine, own, beside = pl.pallas_call(
+    *best, weight = pl.pallas_call(
         lambda *refs: first_kernel(seq, block_masks, *refs),
-        out_shape=[
-            best_shape,
-            best_shape,
-            shape((width, width), jnp.bfloat16),
-            shape((half, width), jnp.bfloat16),
-            shape((seq, width), jnp.bfloat16),
-            shape((seq, width), jnp.bfloat16),
-        ],
-        in_specs=[smem] + [vmem] * 10 + [hbm] * 3,
-        out_specs=[vmem] * 6,
-        scratch_shapes=[pltpu.SemaphoreType.DMA((3,))],
+        out_shape=[best_shape, best_shape, shape((width, width), jnp.bfloat16)],
+        in_specs=[smem] + [vmem] * 13,
+        out_specs=[vmem] * 3,
         compiler_params=limit,
         cost_estimate=cost(2),
     )(
         where,
-        docs[2],
-        docs[3],
+        load,
+        beside,
+        table,
+        near_pile,
         *thirds,
         *other_thirds,
         params,
+        mine,
         theirs,
-        stay(weight_rows),
-        stay(hidden_states),
-        stay(docs[1]),
-    )
-    docs |= {0: own, 1: beside, 5: cross(after(docs[4], weight), 1)}
-    tables = docs | {0: table, 1: near_pile}
+    )
+    docs |= {0: load, 1: beside, 5: cross(after(docs[4], weight), 1)}
+    tables = docs | {1: near_pile}
     for first in range(2, len(masks) - 2, 2):
         pair = masks[first : first + 2]
         best += pl.pallas_call(
@@ -399,7 +401,7 @@
         )(
             *[docs[mask] for mask in pair],
             *[tables[mask] for mask in pair],
-            weight,
+            after(weight, best[-1]),
             params,
             mine,
             theirs,

time: 64 us -> 60 us (0.938)
  waiting for transfers between devices: 16.3 us -> 12.5 us
  blocking collectives: 14.9 us -> 13.4 us
  Pallas kernels: 10.9 us -> 11.7 us
    ppermute x12, waiting for transfers between devices: 16.2 us -> 12.5 us  [cross(): lax.ppermute(value, 'doc', [(i, i ^ 2 * mask) for i in range(devices)])]
    all_to_all x1, blocking collectives: 14.9 us -> 13.4 us  [move_tokens(): got = lax.all_to_all(send, 'doc', split_axis=0, concat_axis=0, tiled=True)]
    pallas_call x0 -> x1, Pallas kernels: none -> 1.4 us  [move_tokens(): pl.pallas_call(lambda *refs: fetch_kernel(2, *refs), out_shape=[shape(val...]
  transfers between devices with their start and end apart: 16 -> 16, of which waited for: 8 -> 7; matrix products, arithmetic and copies ran while one was open for 0% -> 0% of each run, Pallas kernels for 14% -> 16%
where the time goes in v12:
time: 60 us; the launch traced here: 59.8 us
  starting transfers between devices  19.2 us (32%)
  blocking collectives  13.4 us (22%)
  waiting for transfers between devices  12.5 us (21%)
  Pallas kernels  11.7 us (20%)
  between operations  1.44 us (2%)
  local copies, waits for them, and re-layouts  1.35 us (2%)
    ppermute x12, starting transfers between devices, cross(): lax.ppermute(value, 'doc', [(i, i ^ 2 * mask) for i in range(devices)])  18.1 us
    all_to_all x1, blocking collectives, move_tokens(): got = lax.all_to_all(send, 'doc', split_axis=0, concat_axis=0, tiled=True)  13.4 us
    ppermute x12, waiting for transfers between devices, cross(): lax.ppermute(value, 'doc', [(i, i ^ 2 * mask) for i in range(devices)])  12.5 us
    pallas_call x2, Pallas kernels, move_tokens(): pl.pallas_call(lambda *refs: next_kernel(seq, *refs), out_shape=[best_sha...  3.57 us
    pallas_call x1, Pallas kernels, move_tokens(): pl.pallas_call(lambda *refs: first_kernel(seq, block_masks, *refs), out_s...  2.83 us
    pallas_call x1, Pallas kernels, move_tokens(): pl.pallas_call(lambda *refs: last_kernel(seq, masks, *refs), out_shape=sh...  2.15 us
    pallas_call x1, Pallas kernels, move_tokens(): pl.pallas_call(start_kernel, out_shape=[shape((seq + SLOT_ROWS, width), j...  1.71 us
    pallas_call x1, Pallas kernels, move_tokens(): pl.pallas_call(lambda *refs: fetch_kernel(2, *refs), out_shape=[shape(val...  1.4 us
  transfers between devices with their start and end apart: 16, of which 7 were waited for; matrix products, arithmetic and copies ran while one was open for 0% of the time, Pallas kernels for 16%

profile of v12, /device:TPU:0, one launch (start us, length us, event | category | flops | bytes accessed | tf_op | source)
XLA Modules:
  0.0 59.8 jit_solution(4627956465527327230)
XLA Ops:
  0.6 0.5 collective-permute-start.8
  1.2 2.6 %collective-permute-start.4 = (bf16[128,768]{1,0:T(8,128)(2,1)}, bf16[128,768]{1,0:T(8,128)(2,1)S(1)}, u32[]{:S(2)}, u32[]{:S(2)}) collective-permute-start(bf16[128,768]{1,0:T(8,128)(2,1)} %refs_0_.1), channel_id=1, source_target_pairs={{0,2},{1,3},{2,0},{3,1},{4,6},{5,7},{6,4},{7,5},{8,10},{9,11},{10,... | collective-permute-start | bytes 589832 | tf_op jit(solution)/shard_map/ppermute | solution.py:274
  3.7 3.6 %collective-permute-start = (bf16[48,768]{1,0:T(8,128)(2,1)}, bf16[48,768]{1,0:T(8,128)(2,1)S(1)}, u32[]{:S(2)}, u32[]{:S(2)}) collective-permute-start(bf16[48,768]{1,0:T(8,128)(2,1)} %refs_1_.1), channel_id=1, source_target_pairs={{0,12},{1,13},{2,14},{3,15},{4,8},{5,9},{6,10},{7,11},{8,4},{9,5},... | collective-permute-start | bytes 221192 | tf_op jit(solution)/shard_map/ppermute | solution.py:274
  7.3 0.0 collective-permute-start.3
  8.0 1.7 %shard_map.122 = (bf16[144,768]{1,0:T(8,128)(2,1)S(1)}, bf16[48,768]{1,0:T(8,128)(2,1)S(1)}, bf16[16,768]{1,0:T(8,128)(2,1)S(1)}, f32[8,768]{1,0:T(8,128)S(1)}) custom-call(s32[1,1,32]{2,1,0:T(1,128)} %tiles_ref.1, s32[1,1,32]{2,1,0:T(1,128)} %bitcast.15, s32[1,1,32]{2,1,0:T(1,128)} %slots_ref.1, s32[1]{0:T(128)S(6)} %copy.22.length_ref, ...), custom_call_target="tpu_custom_call" | custom-call | tf_op jit(solution)/shard_map/pallas_call | solution.py:313
  9.7 0.0 copy-start.1
  9.7 1.1 %collective-permute-done.refs_0_.refs_2_ = bf16[48,768]{1,0:T(8,128)(2,1)S(1)} collective-permute-done((bf16[48,768]{1,0:T(8,128)(2,1)}, bf16[48,768]{1,0:T(8,128)(2,1)S(1)}, u32[]{:S(2)}, u32[]{:S(2)}) %collective-permute-start) | collective-permute-done | bytes 73760 | tf_op jit(solution)/shard_map/ppermute | solution.py:274
  10.8 1.2 %collective-permute-done.3.refs_1_ = bf16[48,768]{1,0:T(8,128)(2,1)S(1)} collective-permute-done((bf16[48,768]{1,0:T(8,128)(2,1)}, bf16[48,768]{1,0:T(8,128)(2,1)S(1)}, u32[]{:S(2)}, u32[]{:S(2)}) %collective-permute-start.3) | collective-permute-done | bytes 73760 | tf_op jit(solution)/shard_map/ppermute | solution.py:274
  12.0 0.0 collective-permute-done.4.refs_2_.refs_0_
  12.0 0.0 copy-start
  12.0 0.5 collective-permute-start.5
  12.5 1.6 %collective-permute-start.2 = (bf16[48,768]{1,0:T(8,128)(2,1)S(1)}, bf16[48,768]{1,0:T(8,128)(2,1)S(1)}, u32[]{:S(2)}, u32[]{:S(2)}) collective-permute-start(bf16[48,768]{1,0:T(8,128)(2,1)S(1)} %collective-permute-done.refs_0_.refs_2_), channel_id=1, source_target_pairs={{0,4},{1,5},{2,6},{3,7},{4,0},{5,1},{6,2},{7,3},{8,12},{9,13},{10,... | collective-permute-start | bytes 221192 | tf_op jit(solution)/shard_map/ppermute | solution.py:274
  14.1 1.2 %collective-permute-start.1 = (bf16[144,768]{1,0:T(8,128)(2,1)S(1)}, bf16[144,768]{1,0:T(8,128)(2,1)S(1)}, u32[]{:S(2)}, u32[]{:S(2)}) collective-permute-start(bf16[144,768]{1,0:T(8,128)(2,1)S(1)} %get-tuple-element.35.refs_1_.refs_3_), channel_id=1, source_target_pairs={{0,12},{1,13},{2,14},{3,15},{4,8},{5,9},{6,10},{7,11},{8,4},{9,5},... | collective-permute-start | bytes 663560 | tf_op jit(solution)/shard_map/ppermute | solution.py:274
  15.3 1.6 %collective-permute-done.2.refs_1_.refs_3_ = bf16[48,768]{1,0:T(8,128)(2,1)S(1)} collective-permute-done((bf16[48,768]{1,0:T(8,128)(2,1)S(1)}, bf16[48,768]{1,0:T(8,128)(2,1)S(1)}, u32[]{:S(2)}, u32[]{:S(2)}) %collective-permute-start.2) | collective-permute-done | bytes 73760 | tf_op jit(solution)/shard_map/ppermute | solution.py:274
  16.9 2.3 %collective-permute-start.6 = (bf16[144,768]{1,0:T(8,128)(2,1)S(1)}, bf16[144,768]{1,0:T(8,128)(2,1)S(1)}, u32[]{:S(2)}, u32[]{:S(2)}) collective-permute-start(bf16[144,768]{1,0:T(8,128)(2,1)S(1)} %get-tuple-element.35.refs_1_.refs_3_), channel_id=1, source_target_pairs={{0,4},{1,5},{2,6},{3,7},{4,0},{5,1},{6,2},{7,3},{8,12},{9,13},{10,... | collective-permute-start | bytes 663560 | tf_op jit(solution)/shard_map/ppermute | solution.py:274
  19.2 0.0 collective-permute-done.5.refs_4_.refs_1_
  19.2 1.7 %collective-permute-start.9 = (bf16[96,768]{1,0:T(8,128)(2,1)S(1)}, bf16[96,768]{1,0:T(8,128)(2,1)S(1)}, u32[]{:S(2)}, u32[]{:S(2)}) collective-permute-start(bf16[96,768]{1,0:T(8,128)(2,1)S(1)} %shard_map.124), channel_id=1, source_target_pairs={{0,2},{1,3},{2,0},{3,1},{4,6},{5,7},{6,4},{7,5},{8,10},{9,11},{10,... | collective-permute-start | bytes 442376 | tf_op jit(solution)/shard_map/ppermute | solution.py:274
  20.9 3.4 %collective-permute-done.1.refs_0_.refs_2_.refs_5_ = bf16[144,768]{1,0:T(8,128)(2,1)S(1)} collective-permute-done((bf16[144,768]{1,0:T(8,128)(2,1)S(1)}, bf16[144,768]{1,0:T(8,128)(2,1)S(1)}, u32[]{:S(2)}, u32[]{:S(2)}) %collective-permute-start.1) | collective-permute-done | bytes 221216 | tf_op jit(solution)/shard_map/ppermute | solution.py:274
  24.2 0.0 copy-done.1
  24.2 2.6 %collective-permute-done.6.refs_0_.refs_2_.refs_7_ = bf16[144,768]{1,0:T(8,128)(2,1)S(1)} collective-permute-done((bf16[144,768]{1,0:T(8,128)(2,1)S(1)}, bf16[144,768]{1,0:T(8,128)(2,1)S(1)}, u32[]{:S(2)}, u32[]{:S(2)}) %collective-permute-start.6) | collective-permute-done | bytes 221216 | tf_op jit(solution)/shard_map/ppermute | solution.py:274
  26.8 0.5 collective-permute-start.7
  27.3 0.0 collective-permute-done.8.refs_13_.refs_7_.refs_14_
  27.3 0.0 collective-permute-done.9.refs_5_
  27.3 0.1 collective-permute-start.10
  27.4 0.5 collective-permute-start.11
  27.9 0.1 collective-permute-start.12
  28.0 1.1 %collective-permute-start.14 = (bf16[144,768]{1,0:T(8,128)(2,1)S(1)}, bf16[144,768]{1,0:T(8,128)(2,1)S(1)}, u32[]{:S(2)}, u32[]{:S(2)}) collective-permute-start(bf16[144,768]{1,0:T(8,128)(2,1)S(1)} %collective-permute-done.1.refs_0_.refs_2_.refs_5_), channel_id=1, source_target_pairs={{0,2},{1,3},{2,0},{3,1},{4,6},{5,7},{6,4},{7,5},{8,10},{9,11},{10,... | collective-permute-start | bytes 663560 | tf_op jit(solution)/shard_map/ppermute | solution.py:274
  29.1 0.0 copy-done
  29.1 1.4 %shard_map.126 = (bf16[960,768]{1,0:T(8,128)(2,1)S(1)}, bf16[128,768]{1,0:T(8,128)(2,1)S(1)}) custom-call(bf16[128,768]{1,0:T(8,128)(2,1)S(1)} %get-tuple-element.38.refs_0_.refs_5_, bf16[960,768]{1,0:T(8,128)(2,1)} %bitcast.13, bf16[128,768]{1,0:T(8,128)(2,1)} %copy-done), custom_call_target="tpu_custom_call" | custom-call | tf_op jit(solution)/shard_map/pallas_call | solution.py:359
  30.6 0.0 collective-permute-done.10.refs_8_
  30.6 2.1 %collective-permute-start.15 = (bf16[144,768]{1,0:T(8,128)(2,1)S(1)}, bf16[144,768]{1,0:T(8,128)(2,1)S(1)}, u32[]{:S(2)}, u32[]{:S(2)}) collective-permute-start(bf16[144,768]{1,0:T(8,128)(2,1)S(1)} %shard_map.128), channel_id=1, source_target_pairs={{0,4},{1,5},{2,6},{3,7},{4,0},{5,1},{6,2},{7,3},{8,12},{9,13},{10,... | collective-permute-start | bytes 663560 | tf_op jit(solution)/shard_map/ppermute | solution.py:274
  32.6 0.0 collective-permute-done.11.refs_9_
  32.6 0.0 collective-permute-done.12.refs_10_
  32.7 0.0 copy-done.2
  32.7 2.8 %shard_map.127 = (f32[8,960]{1,0:T(8,128)S(1)}, f32[8,960]{1,0:T(8,128)S(1)}, bf16[768,768]{1,0:T(8,128)(2,1)S(1)}) custom-call(s32[1]{0:T(128)} %bitcast.refs_0_, bf16[144,768]{1,0:T(8,128)(2,1)S(1)} %get-tuple-element.35.refs_1_.refs_3_, bf16[128,768]{1,0:T(8,128)(2,1)S(1)} %get-tuple-element.42.refs_2_, bf16[16,768]{1,0:T(8,128)(2,1)S(1)} %copy-done.2, ...), custom_call_target="tpu_custom_call" | custom-call | flops 2 | bytes 2 | tf_op jit(solution)/shard_map/pallas_call | solution.py:371
  35.5 0.0 collective-permute-done.7.refs_1_.refs_9_
  35.5 1.0 %collective-permute-start.13 = (bf16[144,768]{1,0:T(8,128)(2,1)S(1)}, bf16[144,768]{1,0:T(8,128)(2,1)S(1)}, u32[]{:S(2)}, u32[]{:S(2)}) collective-permute-start(bf16[144,768]{1,0:T(8,128)(2,1)S(1)} %collective-permute-done.7.refs_1_.refs_9_), channel_id=1, source_target_pairs={{0,2},{1,3},{2,0},{3,1},{4,6},{5,7},{6,4},{7,5},{8,10},{9,11},{10,... | collective-permute-start | bytes 663560 | tf_op jit(solution)/shard_map/ppermute | solution.py:274
  36.5 0.0 collective-permute-done.14.refs_1_.refs_3_.refs_6_
  36.5 1.8 %shard_map.129 = (f32[8,960]{1,0:T(8,128)S(1)}, f32[8,960]{1,0:T(8,128)S(1)}) custom-call(bf16[144,768]{1,0:T(8,128)(2,1)S(1)} %collective-permute-done.1.refs_0_.refs_2_.refs_5_, bf16[144,768]{1,0:T(8,128)(2,1)S(1)} %collective-permute-done.14.refs_1_.refs_3_.refs_6_, bf16[144,768]{1,0:T(8,128)(2,1)S(1)} %collective-permute-done.1.refs_0_.refs_2_.refs_5_, ...), custom_call_target="tpu_custom_call" | custom-call | flops 2 | bytes 2 | tf_op jit(solution)/shard_map/pallas_call | solution.py:394
  38.3 0.0 copy-start.3
  38.3 0.2 collective-permute-done.15.refs_1_.refs_3_.refs_8_
  38.5 1.8 %shard_map.130 = (f32[8,960]{1,0:T(8,128)S(1)}, f32[8,960]{1,0:T(8,128)S(1)}) custom-call(bf16[144,768]{1,0:T(8,128)(2,1)S(1)} %collective-permute-done.6.refs_0_.refs_2_.refs_7_, bf16[144,768]{1,0:T(8,128)(2,1)S(1)} %collective-permute-done.15.refs_1_.refs_3_.refs_8_, bf16[144,768]{1,0:T(8,128)(2,1)S(1)} %collective-permute-done.6.refs_0_.refs_2_.refs_7_, ...), custom_call_target="tpu_custom_call" | custom-call | flops 2 | bytes 2 | tf_op jit(solution)/shard_map/pallas_call | solution.py:394
  40.3 2.5 %collective-permute-done.13.refs_2_.refs_10_ = bf16[144,768]{1,0:T(8,128)(2,1)S(1)} collective-permute-done((bf16[144,768]{1,0:T(8,128)(2,1)S(1)}, bf16[144,768]{1,0:T(8,128)(2,1)S(1)}, u32[]{:S(2)}, u32[]{:S(2)}) %collective-permute-start.13) | collective-permute-done | bytes 221216 | tf_op jit(solution)/shard_map/ppermute | solution.py:274
  42.8 0.0 copy-done.3
  42.8 2.1 %shard_map.131 = bf16[16,48,128]{2,1,0:T(8,128)(2,1)S(1)} custom-call(s32[1]{0:T(128)} %bitcast.refs_0_, bf16[144,768]{1,0:T(8,128)(2,1)S(1)} %collective-permute-done.7.refs_1_.refs_9_, bf16[144,768]{1,0:T(8,128)(2,1)S(1)} %collective-permute-done.13.refs_2_.refs_10_, bf16[144,768]{1,0:T(8,128)(2,1)S(1)} %get-tuple-element.35.refs_1_.refs_3_, ...), custom_call_target="tpu_custom_call" | custom-call | flops 2 | bytes 2 | tf_op jit(solution)/shard_map/pallas_call | solution.py:409
  45.0 13.4 %all_to_all.5 = bf16[16,48,128]{2,1,0:T(8,128)(2,1)S(1)} all-to-all(bf16[16,48,128]{2,1,0:T(8,128)(2,1)S(1)} %shard_map.131), channel_id=1, replica_groups=mesh['groups'=2,'doc'=16,'term'=1] {'doc'}, dimensions={0} | all-to-all | bytes 393216 | tf_op jit(solution)/shard_map/all_to_all | solution.py:430
  58.5 0.7 %slice.26 = bf16[2,15360]{1,0:T(2,128)(2,1)} reshape(bf16[2,8,15,128]{3,2,1,0:T(8,128)(2,1)S(1)} %slice.30) | data formatting | bytes 122880 | tf_op jit(solution)/shard_map/slice | solution.py:433
  59.1 0.6 %slice.24 = bf16[1,15360]{1,0:T(2,128)(2,1)} reshape(bf16[1,8,15,128]{3,2,1,0:T(8,128)(2,1)S(1)} %slice.29) | data formatting | bytes 61440 | tf_op jit(solution)/shard_map/slice | solution.py:433
  (9 shorter events, 0.1 us)
Async XLA Ops:
  0.6 26.6 %collective-permute-start.8 = (bf16[960,768]{1,0:T(8,128)(2,1)}, bf16[960,768]{1,0:T(8,128)(2,1)S(1)}, u32[]{:S(2)}, u32[]{:S(2)}) collective-permute-start(bf16[960,768]{1,0:T(8,128)(2,1)} %bitcast.12), channel_id=1, source_target_pairs={{0,1},{1,0},{2,3},{3,2},{4,5},{5,4},{6,7},{7,6},{8,9},{9,8},{10,11... | collective-permute-start | bytes 4423688 | tf_op jit(solution)/shard_map/ppermute | solution.py:277
  1.2 10.9 %collective-permute-start.4 = (bf16[128,768]{1,0:T(8,128)(2,1)}, bf16[128,768]{1,0:T(8,128)(2,1)S(1)}, u32[]{:S(2)}, u32[]{:S(2)}) collective-permute-start(bf16[128,768]{1,0:T(8,128)(2,1)} %refs_0_.1), channel_id=1, source_target_pairs={{0,2},{1,3},{2,0},{3,1},{4,6},{5,7},{6,4},{7,5},{8,10},{9,11},{10,... | collective-permute-start | bytes 589832 | tf_op jit(solution)/shard_map/ppermute | solution.py:274
  3.7 7.1 %collective-permute-start = (bf16[48,768]{1,0:T(8,128)(2,1)}, bf16[48,768]{1,0:T(8,128)(2,1)S(1)}, u32[]{:S(2)}, u32[]{:S(2)}) collective-permute-start(bf16[48,768]{1,0:T(8,128)(2,1)} %refs_1_.1), channel_id=1, source_target_pairs={{0,12},{1,13},{2,14},{3,15},{4,8},{5,9},{6,10},{7,11},{8,4},{9,5},... | collective-permute-start | bytes 221192 | tf_op jit(solution)/shard_map/ppermute | solution.py:274
  7.3 4.7 %collective-permute-start.3 = (bf16[48,768]{1,0:T(8,128)(2,1)}, bf16[48,768]{1,0:T(8,128)(2,1)S(1)}, u32[]{:S(2)}, u32[]{:S(2)}) collective-permute-start(bf16[48,768]{1,0:T(8,128)(2,1)} %refs_1_.1), channel_id=1, source_target_pairs={{0,4},{1,5},{2,6},{3,7},{4,0},{5,1},{6,2},{7,3},{8,12},{9,13},{10,... | collective-permute-start | bytes 221192 | tf_op jit(solution)/shard_map/ppermute | solution.py:274
  9.7 14.5 %copy-start.1 = (bf16[16,768]{1,0:T(8,128)(2,1)}, bf16[16,768]{1,0:T(8,128)(2,1)S(1)}, u32[]{:S(2)}) copy-start(bf16[16,768]{1,0:T(8,128)(2,1)S(1)} %get-tuple-element.33.refs_2_.refs_3_) | copy-start | bytes 73732
  12.0 17.1 %copy-start = (bf16[128,768]{1,0:T(8,128)(2,1)}, bf16[128,768]{1,0:T(8,128)(2,1)S(1)}, u32[]{:S(2)}) copy-start(bf16[128,768]{1,0:T(8,128)(2,1)S(1)} %collective-permute-done.4.refs_2_.refs_0_) | copy-start | bytes 589828
  12.0 7.1 %collective-permute-start.5 = (bf16[112,768]{1,0:T(8,128)(2,1)S(1)}, bf16[112,768]{1,0:T(8,128)(2,1)S(1)}, u32[]{:S(2)}, u32[]{:S(2)}) collective-permute-start(bf16[112,768]{1,0:T(8,128)(2,1)S(1)} %shard_map.123), channel_id=1, source_target_pairs={{0,2},{1,3},{2,0},{3,1},{4,6},{5,7},{6,4},{7,5},{8,10},{9,11},{10,... | collective-permute-start | bytes 516104 | tf_op jit(solution)/shard_map/ppermute | solution.py:274
  12.5 4.4 %collective-permute-start.2 = (bf16[48,768]{1,0:T(8,128)(2,1)S(1)}, bf16[48,768]{1,0:T(8,128)(2,1)S(1)}, u32[]{:S(2)}, u32[]{:S(2)}) collective-permute-start(bf16[48,768]{1,0:T(8,128)(2,1)S(1)} %collective-permute-done.refs_0_.refs_2_), channel_id=1, source_target_pairs={{0,4},{1,5},{2,6},{3,7},{4,0},{5,1},{6,2},{7,3},{8,12},{9,13},{10,... | collective-permute-start | bytes 221192 | tf_op jit(solution)/shard_map/ppermute | solution.py:274
  14.1 10.2 %collective-permute-start.1 = (bf16[144,768]{1,0:T(8,128)(2,1)S(1)}, bf16[144,768]{1,0:T(8,128)(2,1)S(1)}, u32[]{:S(2)}, u32[]{:S(2)}) collective-permute-start(bf16[144,768]{1,0:T(8,128)(2,1)S(1)} %get-tuple-element.35.refs_1_.refs_3_), channel_id=1, source_target_pairs={{0,12},{1,13},{2,14},{3,15},{4,8},{5,9},{6,10},{7,11},{8,4},{9,5},... | collective-permute-start | bytes 663560 | tf_op jit(solution)/shard_map/ppermute | solution.py:274
  16.9 10.0 %collective-permute-start.6 = (bf16[144,768]{1,0:T(8,128)(2,1)S(1)}, bf16[144,768]{1,0:T(8,128)(2,1)S(1)}, u32[]{:S(2)}, u32[]{:S(2)}) collective-permute-start(bf16[144,768]{1,0:T(8,128)(2,1)S(1)} %get-tuple-element.35.refs_1_.refs_3_), channel_id=1, source_target_pairs={{0,4},{1,5},{2,6},{3,7},{4,0},{5,1},{6,2},{7,3},{8,12},{9,13},{10,... | collective-permute-start | bytes 663560 | tf_op jit(solution)/shard_map/ppermute | solution.py:274
  19.2 8.1 %collective-permute-start.9 = (bf16[96,768]{1,0:T(8,128)(2,1)S(1)}, bf16[96,768]{1,0:T(8,128)(2,1)S(1)}, u32[]{:S(2)}, u32[]{:S(2)}) collective-permute-start(bf16[96,768]{1,0:T(8,128)(2,1)S(1)} %shard_map.124), channel_id=1, source_target_pairs={{0,2},{1,3},{2,0},{3,1},{4,6},{5,7},{6,4},{7,5},{8,10},{9,11},{10,... | collective-permute-start | bytes 442376 | tf_op jit(solution)/shard_map/ppermute | solution.py:274
  26.8 8.7 %collective-permute-start.7 = (bf16[144,768]{1,0:T(8,128)(2,1)S(1)}, bf16[144,768]{1,0:T(8,128)(2,1)S(1)}, u32[]{:S(2)}, u32[]{:S(2)}) collective-permute-start(bf16[144,768]{1,0:T(8,128)(2,1)S(1)} %collective-permute-done.1.refs_0_.refs_2_.refs_5_), channel_id=1, source_target_pairs={{0,4},{1,5},{2,6},{3,7},{4,0},{5,1},{6,2},{7,3},{8,12},{9,13},{10,... | collective-permute-start | bytes 663560 | tf_op jit(solution)/shard_map/ppermute | solution.py:274
  27.3 3.2 %collective-permute-start.10 = (bf16[128,768]{1,0:T(8,128)(2,1)S(1)}, bf16[128,768]{1,0:T(8,128)(2,1)S(1)}, u32[]{:S(2)}, u32[]{:S(2)}) collective-permute-start(bf16[128,768]{1,0:T(8,128)(2,1)S(1)} %get-tuple-element.38.refs_0_.refs_5_), channel_id=1, source_target_pairs={{0,1},{1,0},{2,3},{3,2},{4,5},{5,4},{6,7},{7,6},{8,9},{9,8},{10,11... | collective-permute-start | bytes 589832 | tf_op jit(solution)/shard_map/ppermute | solution.py:277
  27.4 5.2 %collective-permute-start.11 = (bf16[128,768]{1,0:T(8,128)(2,1)S(1)}, bf16[128,768]{1,0:T(8,128)(2,1)}, u32[]{:S(2)}, u32[]{:S(2)}) collective-permute-start(bf16[128,768]{1,0:T(8,128)(2,1)S(1)} %get-tuple-element.39.refs_6_), channel_id=1, source_target_pairs={{0,1},{1,0},{2,3},{3,2},{4,5},{5,4},{6,7},{7,6},{8,9},{9,8},{10,11... | collective-permute-start | bytes 589832 | tf_op jit(solution)/shard_map/ppermute | solution.py:277
  27.9 4.7 %collective-permute-start.12 = (bf16[128,768]{1,0:T(8,128)(2,1)S(1)}, bf16[128,768]{1,0:T(8,128)(2,1)}, u32[]{:S(2)}, u32[]{:S(2)}) collective-permute-start(bf16[128,768]{1,0:T(8,128)(2,1)S(1)} %get-tuple-element.40.refs_7_), channel_id=1, source_target_pairs={{0,1},{1,0},{2,3},{3,2},{4,5},{5,4},{6,7},{7,6},{8,9},{9,8},{10,11... | collective-permute-start | bytes 589832 | tf_op jit(solution)/shard_map/ppermute | solution.py:277
  28.0 4.7 %copy-start.2 = (bf16[16,768]{1,0:T(8,128)(2,1)S(1)}, bf16[16,768]{1,0:T(8,128)(2,1)}, u32[]{:S(2)}) copy-start(bf16[16,768]{1,0:T(8,128)(2,1)} %copy-done.1) | copy-start | bytes 73732
  28.0 8.5 %collective-permute-start.14 = (bf16[144,768]{1,0:T(8,128)(2,1)S(1)}, bf16[144,768]{1,0:T(8,128)(2,1)S(1)}, u32[]{:S(2)}, u32[]{:S(2)}) collective-permute-start(bf16[144,768]{1,0:T(8,128)(2,1)S(1)} %collective-permute-done.1.refs_0_.refs_2_.refs_5_), channel_id=1, source_target_pairs={{0,2},{1,3},{2,0},{3,1},{4,6},{5,7},{6,4},{7,5},{8,10},{9,11},{10,... | collective-permute-start | bytes 663560 | tf_op jit(solution)/shard_map/ppermute | solution.py:274
  30.6 8.0 %collective-permute-start.15 = (bf16[144,768]{1,0:T(8,128)(2,1)S(1)}, bf16[144,768]{1,0:T(8,128)(2,1)S(1)}, u32[]{:S(2)}, u32[]{:S(2)}) collective-permute-start(bf16[144,768]{1,0:T(8,128)(2,1)S(1)} %shard_map.128), channel_id=1, source_target_pairs={{0,4},{1,5},{2,6},{3,7},{4,0},{5,1},{6,2},{7,3},{8,12},{9,13},{10,... | collective-permute-start | bytes 663560 | tf_op jit(solution)/shard_map/ppermute | solution.py:274
  35.5 7.3 %collective-permute-start.13 = (bf16[144,768]{1,0:T(8,128)(2,1)S(1)}, bf16[144,768]{1,0:T(8,128)(2,1)S(1)}, u32[]{:S(2)}, u32[]{:S(2)}) collective-permute-start(bf16[144,768]{1,0:T(8,128)(2,1)S(1)} %collective-permute-done.7.refs_1_.refs_9_), channel_id=1, source_target_pairs={{0,2},{1,3},{2,0},{3,1},{4,6},{5,7},{6,4},{7,5},{8,10},{9,11},{10,... | collective-permute-start | bytes 663560 | tf_op jit(solution)/shard_map/ppermute | solution.py:274
  38.3 4.5 %copy-start.3 = (f32[15360]{0:T(1024)S(1)}, f32[15360]{0:T(1024)}, u32[]{:S(2)}) copy-start(f32[15360]{0:T(1024)} %param.18) | copy-start | bytes 184324

commit v13 on v12

--- a/solution.py
+++ b/solution.py
@@ -186,20 +186,19 @@
 
 def first_kernel(seq, masks, *refs):
     me_ref, docs, tables, refs = refs[0], refs[1:3], refs[3:5], refs[5:]
-    mine_parts, their_parts, params, halves, refs = refs[:3], refs[3:6], refs[6], refs[7:9], refs[9:]
+    parts, others, params, halves, refs = refs[:2], refs[2:4], refs[4], refs[5:7], refs[7:]
     bests, weight = refs[:2], refs[2]
     me = me_ref[0]
     core = me % 2
     rows = weight.shape[0] // (2 * len(masks))
-    packed = jnp.concatenate([ref[...] for ref in mine_parts], axis=0)
-    others = jnp.concatenate([ref[...] for ref in their_parts], axis=0)
     for k, mask in enumerate(masks):
         chip = (me // 2) ^ mask
-        block = slice(k * rows, (k + 1) * rows)
+        part, place = divmod(k * rows, parts[0].shape[0])
+        block = slice(place, place + rows)
         at = pl.multiple_of((2 * chip + core) * rows, SLOT_ROWS)
-        weight[pl.ds(at, rows), :] = packed[block, :]
+        weight[pl.ds(at, rows), :] = parts[part][block, :]
         at = pl.multiple_of((2 * chip + 1 - core) * rows, SLOT_ROWS)
-        weight[pl.ds(at, rows), :] = others[block, :]
+        weight[pl.ds(at, rows), :] = others[part][block, :]
     keep_tops(normed_rows(docs, tables, seq, weight, params), halves, bests)
 
 
@@ -309,7 +308,7 @@
     block_6 = cross(transform_weight, 6)
     block_2 = cross(transform_weight, 2)
     theirs = swap(weight_rows)
-    docs = {1: cross(hidden_states, 1)}
+    docs = {1: cross(hidden_states, 1), 2: cross(hidden_states, 2)}
     load, block, table, params = pl.pallas_call(
         start_kernel,
         out_shape=[
@@ -338,24 +337,23 @@
     )
     near = (block, after(block_2, block_6, docs[1]), table)
     near_pile = cross(pile(near, ((0, rows), (0, rows), (0, SLOT_ROWS))), 1)
-    block_4 = cross(block_6, 2)
+    one, two, below = (0, rows), (0, 2 * rows), (0, SLOT_ROWS)
+    block_4 = cross(pile((after(block_6, docs[2]), table), (one, below)), 2)
     docs[6] = cross(after(load, block_6), 6)
-    docs[2] = cross(after(load, block_4), 2)
     load_1 = pile((docs[1], near_pile), ((0, seq), (2 * rows, SLOT_ROWS)))
     far = (block_6, after(block_4, near_pile))
     far = pile(far, ((0, rows), (0, rows)))
     far_pile = cross(far, 1)
     docs[3] = cross(after(load_1, far), 2)
-    docs[4] = cross(after(docs[6], far, docs[2]), 2)
+    docs[4] = cross(after(docs[6], far, docs[3]), 2)
     docs[7] = cross(docs[6], 1)
     late = (docs[6], theirs)
-    one, two = (0, rows), (0, 2 * rows)
     sources = (after(block, *late), block_2, block_6, block_4, near_pile, far_pile)
-    thirds = pile(sources, (one, one, one, one, two, two), (seq,) * 3)
-    other_thirds = [swap(third) for third in thirds]
+    packed = pile(sources, (one, one, one, one, two, two), (chips // 2 * rows,) * 2)
+    other_packed = [swap(part) for part in packed]
     block_masks = [0, 2, 6, 4, 1, 3, 7, 5]
 
-    far_from = [stay(after(weight_rows, *thirds)), stay(docs[1])]
+    far_from = [stay(after(weight_rows, *packed)), stay(docs[1])]
     mine, beside = pl.pallas_call(
         lambda *refs: fetch_kernel(2, *refs),
         out_shape=[shape(value.shape, value.dtype) for value in far_from],
@@ -363,7 +361,7 @@
         out_specs=[vmem] * 2,
         scratch_shapes=[pltpu.SemaphoreType.DMA((2,))],
         compiler_params=limit,
-    )(thirds[0], *far_from)
+    )(packed[0], *far_from)
 
     masks = [0, 1, 6, 7, 2, 3, 4, 5]
     where = me[None]
@@ -371,7 +369,7 @@
     *best, weight = pl.pallas_call(
         lambda *refs: first_kernel(seq, block_masks, *refs),
         out_shape=[best_shape, best_shape, shape((width, width), jnp.bfloat16)],
-        in_specs=[smem] + [vmem] * 13,
+        in_specs=[smem] + [vmem] * 11,
         out_specs=[vmem] * 3,
         compiler_params=limit,
         cost_estimate=cost(2),
@@ -381,14 +379,14 @@
         beside,
         table,
         near_pile,
-        *thirds,
-        *other_thirds,
+        *packed,
+        *other_packed,
         params,
         mine,
         theirs,
     )
     docs |= {0: load, 1: beside, 5: cross(after(docs[4], weight), 1)}
-    tables = docs | {1: near_pile}
+    tables = docs | {1: near_pile, 2: block_4}
     for first in range(2, len(masks) - 2, 2):
         pair = masks[first : first + 2]
         best += pl.pallas_call(

time: 60 us -> 60.5 us (level)
  waiting for transfers between devices: 12.5 us -> 17.9 us
  starting transfers between devices: 19.2 us -> 15.3 us
  blocking collectives: 13.4 us -> 12.6 us
    ppermute x12, waiting for transfers between devices: 12.5 us -> 17.8 us  [cross(): lax.ppermute(value, 'doc', [(i, i ^ 2 * mask) for i in range(devices)])]
    ppermute x12, starting transfers between devices: 18.1 us -> 14.2 us  [cross(): lax.ppermute(value, 'doc', [(i, i ^ 2 * mask) for i in range(devices)])]
    all_to_all x1, blocking collectives: 13.4 us -> 12.6 us  [move_tokens(): got = lax.all_to_all(send, 'doc', split_axis=0, concat_axis=0, tiled=True)]
  transfers between devices with their start and end apart: 16 -> 15, of which waited for: 7 -> 7; matrix products, arithmetic and copies ran while one was open for 0% -> 0% of each run, Pallas kernels for 16% -> 16%
where the time goes in v13:
time: 60.5 us; the launch traced here: 60.2 us
  waiting for transfers between devices  17.9 us (30%)
  starting transfers between devices  15.3 us (25%)
  blocking collectives  12.6 us (21%)
  Pallas kernels  11.7 us (19%)
  between operations  1.44 us (2%)
  local copies, waits for them, and re-layouts  1.34 us (2%)
    ppermute x12, waiting for transfers between devices, cross(): lax.ppermute(value, 'doc', [(i, i ^ 2 * mask) for i in range(devices)])  17.8 us
    ppermute x12, starting transfers between devices, cross(): lax.ppermute(value, 'doc', [(i, i ^ 2 * mask) for i in range(devices)])  14.2 us
    all_to_all x1, blocking collectives, move_tokens(): got = lax.all_to_all(send, 'doc', split_axis=0, concat_axis=0, tiled=True)  12.6 us
    pallas_call x2, Pallas kernels, move_tokens(): pl.pallas_call(lambda *refs: next_kernel(seq, *refs), out_shape=[best_sha...  3.55 us
    pallas_call x1, Pallas kernels, move_tokens(): pl.pallas_call(lambda *refs: first_kernel(seq, block_masks, *refs), out_s...  2.84 us
    pallas_call x1, Pallas kernels, move_tokens(): pl.pallas_call(lambda *refs: last_kernel(seq, masks, *refs), out_shape=sh...  2.14 us
    pallas_call x1, Pallas kernels, move_tokens(): pl.pallas_call(start_kernel, out_shape=[shape((seq + SLOT_ROWS, width), j...  1.71 us
    pallas_call x1, Pallas kernels, move_tokens(): pl.pallas_call(lambda *refs: fetch_kernel(2, *refs), out_shape=[shape(val...  1.39 us
  transfers between devices with their start and end apart: 15, of which 7 were waited for; matrix products, arithmetic and copies ran while one was open for 0% of the time, Pallas kernels for 16%

profile of v13, /device:TPU:0, one launch (start us, length us, event | category | flops | bytes accessed | tf_op | source)
XLA Modules:
  0.0 60.2 jit_solution(4687032138508908377)
XLA Ops:
  0.6 0.5 collective-permute-start.9
  1.2 2.6 %collective-permute-start.5 = (bf16[128,768]{1,0:T(8,128)(2,1)}, bf16[128,768]{1,0:T(8,128)(2,1)S(1)}, u32[]{:S(2)}, u32[]{:S(2)}) collective-permute-start(bf16[128,768]{1,0:T(8,128)(2,1)} %refs_0_.1), channel_id=1, source_target_pairs={{0,2},{1,3},{2,0},{3,1},{4,6},{5,7},{6,4},{7,5},{8,10},{9,11},{10,... | collective-permute-start | bytes 589832 | tf_op jit(solution)/shard_map/ppermute | solution.py:273
  3.7 1.6 %collective-permute-start.2 = (bf16[128,768]{1,0:T(8,128)(2,1)}, bf16[128,768]{1,0:T(8,128)(2,1)S(1)}, u32[]{:S(2)}, u32[]{:S(2)}) collective-permute-start(bf16[128,768]{1,0:T(8,128)(2,1)} %refs_0_.1), channel_id=1, source_target_pairs={{0,4},{1,5},{2,6},{3,7},{4,0},{5,1},{6,2},{7,3},{8,12},{9,13},{10,... | collective-permute-start | bytes 589832 | tf_op jit(solution)/shard_map/ppermute | solution.py:273
  5.3 2.5 %collective-permute-start = (bf16[48,768]{1,0:T(8,128)(2,1)}, bf16[48,768]{1,0:T(8,128)(2,1)S(1)}, u32[]{:S(2)}, u32[]{:S(2)}) collective-permute-start(bf16[48,768]{1,0:T(8,128)(2,1)} %refs_1_.1), channel_id=1, source_target_pairs={{0,12},{1,13},{2,14},{3,15},{4,8},{5,9},{6,10},{7,11},{8,4},{9,5},... | collective-permute-start | bytes 221192 | tf_op jit(solution)/shard_map/ppermute | solution.py:273
  7.8 0.7 %collective-permute-start.4 = (bf16[48,768]{1,0:T(8,128)(2,1)}, bf16[48,768]{1,0:T(8,128)(2,1)S(1)}, u32[]{:S(2)}, u32[]{:S(2)}) collective-permute-start(bf16[48,768]{1,0:T(8,128)(2,1)} %refs_1_.1), channel_id=1, source_target_pairs={{0,4},{1,5},{2,6},{3,7},{4,0},{5,1},{6,2},{7,3},{8,12},{9,13},{10,... | collective-permute-start | bytes 221192 | tf_op jit(solution)/shard_map/ppermute | solution.py:273
  9.1 1.7 %shard_map.122 = (bf16[144,768]{1,0:T(8,128)(2,1)S(1)}, bf16[48,768]{1,0:T(8,128)(2,1)S(1)}, bf16[16,768]{1,0:T(8,128)(2,1)S(1)}, f32[8,768]{1,0:T(8,128)S(1)}) custom-call(s32[1,1,32]{2,1,0:T(1,128)} %tiles_ref.1, s32[1,1,32]{2,1,0:T(1,128)} %bitcast.15, s32[1,1,32]{2,1,0:T(1,128)} %slots_ref.1, s32[1]{0:T(128)S(6)} %copy.22.length_ref, ...), custom_call_target="tpu_custom_call" | custom-call | tf_op jit(solution)/shard_map/pallas_call | solution.py:312
  10.8 4.5 %collective-permute-done.refs_0_.refs_2_ = bf16[48,768]{1,0:T(8,128)(2,1)S(1)} collective-permute-done((bf16[48,768]{1,0:T(8,128)(2,1)}, bf16[48,768]{1,0:T(8,128)(2,1)S(1)}, u32[]{:S(2)}, u32[]{:S(2)}) %collective-permute-start) | collective-permute-done | bytes 73760 | tf_op jit(solution)/shard_map/ppermute | solution.py:273
  15.3 0.0 collective-permute-done.4.refs_1_
  15.3 0.0 collective-permute-done.5.refs_0_.refs_2_
  15.3 0.0 copy-start
  15.3 0.6 collective-permute-start.6
  15.9 0.0 collective-permute-done.2.refs_0_
  15.9 0.0 copy-start.1
  15.9 0.4 collective-permute-start.3
  16.3 2.5 %collective-permute-start.1 = (bf16[144,768]{1,0:T(8,128)(2,1)S(1)}, bf16[144,768]{1,0:T(8,128)(2,1)S(1)}, u32[]{:S(2)}, u32[]{:S(2)}) collective-permute-start(bf16[144,768]{1,0:T(8,128)(2,1)S(1)} %get-tuple-element.29.refs_1_.refs_3_), channel_id=1, source_target_pairs={{0,12},{1,13},{2,14},{3,15},{4,8},{5,9},{6,10},{7,11},{8,4},{9,5},... | collective-permute-start | bytes 663560 | tf_op jit(solution)/shard_map/ppermute | solution.py:273
  18.8 5.6 %collective-permute-done.3.refs_1_.refs_3_.refs_2_.refs_7_ = bf16[64,768]{1,0:T(8,128)(2,1)S(1)} collective-permute-done((bf16[64,768]{1,0:T(8,128)(2,1)S(1)}, bf16[64,768]{1,0:T(8,128)(2,1)S(1)}, u32[]{:S(2)}, u32[]{:S(2)}) %collective-permute-start.3) | collective-permute-done | bytes 98336 | tf_op jit(solution)/shard_map/ppermute | solution.py:273
  24.4 0.0 collective-permute-done.6.refs_1_.refs_4_
  24.4 1.8 %collective-permute-start.10 = (bf16[96,768]{1,0:T(8,128)(2,1)S(1)}, bf16[96,768]{1,0:T(8,128)(2,1)S(1)}, u32[]{:S(2)}, u32[]{:S(2)}) collective-permute-start(bf16[96,768]{1,0:T(8,128)(2,1)S(1)} %shard_map.125), channel_id=1, source_target_pairs={{0,2},{1,3},{2,0},{3,1},{4,6},{5,7},{6,4},{7,5},{8,10},{9,11},{10,... | collective-permute-start | bytes 442376 | tf_op jit(solution)/shard_map/ppermute | solution.py:273
  26.3 0.1 collective-permute-start.7
  26.3 0.6 %collective-permute-done.1.refs_0_.refs_2_.refs_5_ = bf16[144,768]{1,0:T(8,128)(2,1)S(1)} collective-permute-done((bf16[144,768]{1,0:T(8,128)(2,1)S(1)}, bf16[144,768]{1,0:T(8,128)(2,1)S(1)}, u32[]{:S(2)}, u32[]{:S(2)}) %collective-permute-start.1) | collective-permute-done | bytes 221216 | tf_op jit(solution)/shard_map/ppermute | solution.py:273
  27.0 0.0 collective-permute-done.9.refs_11_.refs_7_.refs_14_
  27.0 0.0 copy-done.1
  27.0 2.6 %collective-permute-done.10.refs_5_ = bf16[96,768]{1,0:T(8,128)(2,1)S(1)} collective-permute-done((bf16[96,768]{1,0:T(8,128)(2,1)S(1)}, bf16[96,768]{1,0:T(8,128)(2,1)S(1)}, u32[]{:S(2)}, u32[]{:S(2)}) %collective-permute-start.10) | collective-permute-done | bytes 147488 | tf_op jit(solution)/shard_map/ppermute | solution.py:273
  29.6 0.1 collective-permute-start.11
  29.7 0.5 collective-permute-start.12
  30.2 2.0 %collective-permute-done.7.refs_1_.refs_3_.refs_8_ = bf16[144,768]{1,0:T(8,128)(2,1)S(1)} collective-permute-done((bf16[144,768]{1,0:T(8,128)(2,1)S(1)}, bf16[144,768]{1,0:T(8,128)(2,1)S(1)}, u32[]{:S(2)}, u32[]{:S(2)}) %collective-permute-start.7) | collective-permute-done | bytes 221216 | tf_op jit(solution)/shard_map/ppermute | solution.py:273
  32.3 0.0 collective-permute-start.8
  32.3 0.2 collective-permute-start.14
  32.5 0.0 copy-done
  32.5 1.4 %shard_map.128 = (bf16[960,768]{1,0:T(8,128)(2,1)S(1)}, bf16[128,768]{1,0:T(8,128)(2,1)S(1)}) custom-call(bf16[192,768]{1,0:T(8,128)(2,1)S(1)} %get-tuple-element.38.refs_0_.refs_5_, bf16[960,768]{1,0:T(8,128)(2,1)} %bitcast.13, bf16[128,768]{1,0:T(8,128)(2,1)} %copy-done), custom_call_target="tpu_custom_call" | custom-call | tf_op jit(solution)/shard_map/pallas_call | solution.py:357
  33.9 0.0 collective-permute-done.11.refs_7_
  33.9 0.0 collective-permute-done.12.refs_8_
  33.9 2.8 %shard_map.129 = (f32[8,960]{1,0:T(8,128)S(1)}, f32[8,960]{1,0:T(8,128)S(1)}, bf16[768,768]{1,0:T(8,128)(2,1)S(1)}) custom-call(s32[1]{0:T(128)} %bitcast.refs_0_, bf16[144,768]{1,0:T(8,128)(2,1)S(1)} %get-tuple-element.29.refs_1_.refs_3_, bf16[128,768]{1,0:T(8,128)(2,1)S(1)} %get-tuple-element.41.refs_2_, ...), custom_call_target="tpu_custom_call" | custom-call | flops 2 | bytes 2 | tf_op jit(solution)/shard_map/pallas_call | solution.py:369
  36.8 1.4 %collective-permute-done.8.refs_1_.refs_9_ = bf16[144,768]{1,0:T(8,128)(2,1)S(1)} collective-permute-done((bf16[144,768]{1,0:T(8,128)(2,1)S(1)}, bf16[144,768]{1,0:T(8,128)(2,1)S(1)}, u32[]{:S(2)}, u32[]{:S(2)}) %collective-permute-start.8) | collective-permute-done | bytes 221216 | tf_op jit(solution)/shard_map/ppermute | solution.py:273
  38.2 1.2 %collective-permute-start.13 = (bf16[144,768]{1,0:T(8,128)(2,1)S(1)}, bf16[144,768]{1,0:T(8,128)(2,1)S(1)}, u32[]{:S(2)}, u32[]{:S(2)}) collective-permute-start(bf16[144,768]{1,0:T(8,128)(2,1)S(1)} %collective-permute-done.8.refs_1_.refs_9_), channel_id=1, source_target_pairs={{0,2},{1,3},{2,0},{3,1},{4,6},{5,7},{6,4},{7,5},{8,10},{9,11},{10,... | collective-permute-start | bytes 663560 | tf_op jit(solution)/shard_map/ppermute | solution.py:273
  39.4 0.0 copy-start.2
  39.4 0.0 collective-permute-done.14.refs_1_.refs_3_.refs_6_
  39.4 1.8 %shard_map.130 = (f32[8,960]{1,0:T(8,128)S(1)}, f32[8,960]{1,0:T(8,128)S(1)}) custom-call(bf16[144,768]{1,0:T(8,128)(2,1)S(1)} %collective-permute-done.1.refs_0_.refs_2_.refs_5_, bf16[144,768]{1,0:T(8,128)(2,1)S(1)} %collective-permute-done.14.refs_1_.refs_3_.refs_6_, bf16[144,768]{1,0:T(8,128)(2,1)S(1)} %collective-permute-done.1.refs_0_.refs_2_.refs_5_, ...), custom_call_target="tpu_custom_call" | custom-call | flops 2 | bytes 2 | tf_op jit(solution)/shard_map/pallas_call | solution.py:392
  41.2 0.0 copy-done.2
  41.2 0.0 copy-start.3
  41.2 1.8 %shard_map.131 = (f32[8,960]{1,0:T(8,128)S(1)}, f32[8,960]{1,0:T(8,128)S(1)}) custom-call(bf16[128,768]{1,0:T(8,128)(2,1)S(1)} %copy-done.2, bf16[144,768]{1,0:T(8,128)(2,1)S(1)} %collective-permute-done.7.refs_1_.refs_3_.refs_8_, bf16[64,768]{1,0:T(8,128)(2,1)S(1)} %collective-permute-done.3.refs_1_.refs_3_.refs_2_.refs_7_, ...), custom_call_target="tpu_custom_call" | custom-call | flops 2 | bytes 2 | tf_op jit(solution)/shard_map/pallas_call | solution.py:392
  43.0 1.1 %collective-permute-done.13.refs_2_.refs_10_ = bf16[144,768]{1,0:T(8,128)(2,1)S(1)} collective-permute-done((bf16[144,768]{1,0:T(8,128)(2,1)S(1)}, bf16[144,768]{1,0:T(8,128)(2,1)S(1)}, u32[]{:S(2)}, u32[]{:S(2)}) %collective-permute-start.13) | collective-permute-done | bytes 221216 | tf_op jit(solution)/shard_map/ppermute | solution.py:273
  44.1 0.0 copy-done.3
  44.1 2.1 %shard_map.132 = bf16[16,48,128]{2,1,0:T(8,128)(2,1)S(1)} custom-call(s32[1]{0:T(128)} %bitcast.refs_0_, bf16[144,768]{1,0:T(8,128)(2,1)S(1)} %collective-permute-done.8.refs_1_.refs_9_, bf16[144,768]{1,0:T(8,128)(2,1)S(1)} %collective-permute-done.13.refs_2_.refs_10_, bf16[144,768]{1,0:T(8,128)(2,1)S(1)} %get-tuple-element.29.refs_1_.refs_3_, ...), custom_call_target="tpu_custom_call" | custom-call | flops 2 | bytes 2 | tf_op jit(solution)/shard_map/pallas_call | solution.py:407
  46.3 12.6 %all_to_all.5 = bf16[16,48,128]{2,1,0:T(8,128)(2,1)S(1)} all-to-all(bf16[16,48,128]{2,1,0:T(8,128)(2,1)S(1)} %shard_map.132), channel_id=1, replica_groups=mesh['groups'=2,'doc'=16,'term'=1] {'doc'}, dimensions={0} | all-to-all | bytes 393216 | tf_op jit(solution)/shard_map/all_to_all | solution.py:428
  58.9 0.7 %slice.26 = bf16[2,15360]{1,0:T(2,128)(2,1)} reshape(bf16[2,8,15,128]{3,2,1,0:T(8,128)(2,1)S(1)} %slice.30) | data formatting | bytes 122880 | tf_op jit(solution)/shard_map/slice | solution.py:431
  59.6 0.6 %slice.24 = bf16[1,15360]{1,0:T(2,128)(2,1)} reshape(bf16[1,8,15,128]{3,2,1,0:T(8,128)(2,1)S(1)} %slice.29) | data formatting | bytes 61440 | tf_op jit(solution)/shard_map/slice | solution.py:431
  (9 shorter events, 0.1 us)
Async XLA Ops:
  0.6 26.3 %collective-permute-start.9 = (bf16[960,768]{1,0:T(8,128)(2,1)}, bf16[960,768]{1,0:T(8,128)(2,1)S(1)}, u32[]{:S(2)}, u32[]{:S(2)}) collective-permute-start(bf16[960,768]{1,0:T(8,128)(2,1)} %bitcast.12), channel_id=1, source_target_pairs={{0,1},{1,0},{2,3},{3,2},{4,5},{5,4},{6,7},{7,6},{8,9},{9,8},{10,11... | collective-permute-start | bytes 4423688 | tf_op jit(solution)/shard_map/ppermute | solution.py:276
  1.2 14.1 %collective-permute-start.5 = (bf16[128,768]{1,0:T(8,128)(2,1)}, bf16[128,768]{1,0:T(8,128)(2,1)S(1)}, u32[]{:S(2)}, u32[]{:S(2)}) collective-permute-start(bf16[128,768]{1,0:T(8,128)(2,1)} %refs_0_.1), channel_id=1, source_target_pairs={{0,2},{1,3},{2,0},{3,1},{4,6},{5,7},{6,4},{7,5},{8,10},{9,11},{10,... | collective-permute-start | bytes 589832 | tf_op jit(solution)/shard_map/ppermute | solution.py:273
  3.7 12.2 %collective-permute-start.2 = (bf16[128,768]{1,0:T(8,128)(2,1)}, bf16[128,768]{1,0:T(8,128)(2,1)S(1)}, u32[]{:S(2)}, u32[]{:S(2)}) collective-permute-start(bf16[128,768]{1,0:T(8,128)(2,1)} %refs_0_.1), channel_id=1, source_target_pairs={{0,4},{1,5},{2,6},{3,7},{4,0},{5,1},{6,2},{7,3},{8,12},{9,13},{10,... | collective-permute-start | bytes 589832 | tf_op jit(solution)/shard_map/ppermute | solution.py:273
  5.3 10.0 %collective-permute-start = (bf16[48,768]{1,0:T(8,128)(2,1)}, bf16[48,768]{1,0:T(8,128)(2,1)S(1)}, u32[]{:S(2)}, u32[]{:S(2)}) collective-permute-start(bf16[48,768]{1,0:T(8,128)(2,1)} %refs_1_.1), channel_id=1, source_target_pairs={{0,12},{1,13},{2,14},{3,15},{4,8},{5,9},{6,10},{7,11},{8,4},{9,5},... | collective-permute-start | bytes 221192 | tf_op jit(solution)/shard_map/ppermute | solution.py:273
  7.8 7.5 %collective-permute-start.4 = (bf16[48,768]{1,0:T(8,128)(2,1)}, bf16[48,768]{1,0:T(8,128)(2,1)S(1)}, u32[]{:S(2)}, u32[]{:S(2)}) collective-permute-start(bf16[48,768]{1,0:T(8,128)(2,1)} %refs_1_.1), channel_id=1, source_target_pairs={{0,4},{1,5},{2,6},{3,7},{4,0},{5,1},{6,2},{7,3},{8,12},{9,13},{10,... | collective-permute-start | bytes 221192 | tf_op jit(solution)/shard_map/ppermute | solution.py:273
  15.3 17.2 %copy-start = (bf16[128,768]{1,0:T(8,128)(2,1)}, bf16[128,768]{1,0:T(8,128)(2,1)S(1)}, u32[]{:S(2)}) copy-start(bf16[128,768]{1,0:T(8,128)(2,1)S(1)} %collective-permute-done.5.refs_0_.refs_2_) | copy-start | bytes 589828
  15.3 9.1 %collective-permute-start.6 = (bf16[112,768]{1,0:T(8,128)(2,1)S(1)}, bf16[112,768]{1,0:T(8,128)(2,1)S(1)}, u32[]{:S(2)}, u32[]{:S(2)}) collective-permute-start(bf16[112,768]{1,0:T(8,128)(2,1)S(1)} %shard_map.124), channel_id=1, source_target_pairs={{0,2},{1,3},{2,0},{3,1},{4,6},{5,7},{6,4},{7,5},{8,10},{9,11},{10,... | collective-permute-start | bytes 516104 | tf_op jit(solution)/shard_map/ppermute | solution.py:273
  15.9 11.0 %copy-start.1 = (bf16[128,768]{1,0:T(8,128)(2,1)}, bf16[128,768]{1,0:T(8,128)(2,1)S(1)}, u32[]{:S(2)}) copy-start(bf16[128,768]{1,0:T(8,128)(2,1)S(1)} %collective-permute-done.2.refs_0_) | copy-start | bytes 589828
  15.9 8.4 %collective-permute-start.3 = (bf16[64,768]{1,0:T(8,128)(2,1)S(1)}, bf16[64,768]{1,0:T(8,128)(2,1)S(1)}, u32[]{:S(2)}, u32[]{:S(2)}) collective-permute-start(bf16[64,768]{1,0:T(8,128)(2,1)S(1)} %shard_map.123), channel_id=1, source_target_pairs={{0,4},{1,5},{2,6},{3,7},{4,0},{5,1},{6,2},{7,3},{8,12},{9,13},{10,... | collective-permute-start | bytes 294920 | tf_op jit(solution)/shard_map/ppermute | solution.py:273
  16.3 10.6 %collective-permute-start.1 = (bf16[144,768]{1,0:T(8,128)(2,1)S(1)}, bf16[144,768]{1,0:T(8,128)(2,1)S(1)}, u32[]{:S(2)}, u32[]{:S(2)}) collective-permute-start(bf16[144,768]{1,0:T(8,128)(2,1)S(1)} %get-tuple-element.29.refs_1_.refs_3_), channel_id=1, source_target_pairs={{0,12},{1,13},{2,14},{3,15},{4,8},{5,9},{6,10},{7,11},{8,4},{9,5},... | collective-permute-start | bytes 663560 | tf_op jit(solution)/shard_map/ppermute | solution.py:273
  24.4 5.2 %collective-permute-start.10 = (bf16[96,768]{1,0:T(8,128)(2,1)S(1)}, bf16[96,768]{1,0:T(8,128)(2,1)S(1)}, u32[]{:S(2)}, u32[]{:S(2)}) collective-permute-start(bf16[96,768]{1,0:T(8,128)(2,1)S(1)} %shard_map.125), channel_id=1, source_target_pairs={{0,2},{1,3},{2,0},{3,1},{4,6},{5,7},{6,4},{7,5},{8,10},{9,11},{10,... | collective-permute-start | bytes 442376 | tf_op jit(solution)/shard_map/ppermute | solution.py:273
  26.3 6.0 %collective-permute-start.7 = (bf16[144,768]{1,0:T(8,128)(2,1)S(1)}, bf16[144,768]{1,0:T(8,128)(2,1)S(1)}, u32[]{:S(2)}, u32[]{:S(2)}) collective-permute-start(bf16[144,768]{1,0:T(8,128)(2,1)S(1)} %shard_map.126), channel_id=1, source_target_pairs={{0,4},{1,5},{2,6},{3,7},{4,0},{5,1},{6,2},{7,3},{8,12},{9,13},{10,... | collective-permute-start | bytes 663560 | tf_op jit(solution)/shard_map/ppermute | solution.py:273
  29.6 4.3 %collective-permute-start.11 = (bf16[192,768]{1,0:T(8,128)(2,1)S(1)}, bf16[192,768]{1,0:T(8,128)(2,1)}, u32[]{:S(2)}, u32[]{:S(2)}) collective-permute-start(bf16[192,768]{1,0:T(8,128)(2,1)S(1)} %get-tuple-element.38.refs_0_.refs_5_), channel_id=1, source_target_pairs={{0,1},{1,0},{2,3},{3,2},{4,5},{5,4},{6,7},{7,6},{8,9},{9,8},{10,11... | collective-permute-start | bytes 884744 | tf_op jit(solution)/shard_map/ppermute | solution.py:276
  29.7 4.2 %collective-permute-start.12 = (bf16[192,768]{1,0:T(8,128)(2,1)S(1)}, bf16[192,768]{1,0:T(8,128)(2,1)}, u32[]{:S(2)}, u32[]{:S(2)}) collective-permute-start(bf16[192,768]{1,0:T(8,128)(2,1)S(1)} %get-tuple-element.39.refs_6_), channel_id=1, source_target_pairs={{0,1},{1,0},{2,3},{3,2},{4,5},{5,4},{6,7},{7,6},{8,9},{9,8},{10,11... | collective-permute-start | bytes 884744 | tf_op jit(solution)/shard_map/ppermute | solution.py:276
  32.3 5.9 %collective-permute-start.8 = (bf16[144,768]{1,0:T(8,128)(2,1)S(1)}, bf16[144,768]{1,0:T(8,128)(2,1)S(1)}, u32[]{:S(2)}, u32[]{:S(2)}) collective-permute-start(bf16[144,768]{1,0:T(8,128)(2,1)S(1)} %collective-permute-done.1.refs_0_.refs_2_.refs_5_), channel_id=1, source_target_pairs={{0,4},{1,5},{2,6},{3,7},{4,0},{5,1},{6,2},{7,3},{8,12},{9,13},{10,... | collective-permute-start | bytes 663560 | tf_op jit(solution)/shard_map/ppermute | solution.py:273
  32.3 7.2 %collective-permute-start.14 = (bf16[144,768]{1,0:T(8,128)(2,1)S(1)}, bf16[144,768]{1,0:T(8,128)(2,1)S(1)}, u32[]{:S(2)}, u32[]{:S(2)}) collective-permute-start(bf16[144,768]{1,0:T(8,128)(2,1)S(1)} %collective-permute-done.1.refs_0_.refs_2_.refs_5_), channel_id=1, source_target_pairs={{0,2},{1,3},{2,0},{3,1},{4,6},{5,7},{6,4},{7,5},{8,10},{9,11},{10,... | collective-permute-start | bytes 663560 | tf_op jit(solution)/shard_map/ppermute | solution.py:273
  38.2 5.9 %collective-permute-start.13 = (bf16[144,768]{1,0:T(8,128)(2,1)S(1)}, bf16[144,768]{1,0:T(8,128)(2,1)S(1)}, u32[]{:S(2)}, u32[]{:S(2)}) collective-permute-start(bf16[144,768]{1,0:T(8,128)(2,1)S(1)} %collective-permute-done.8.refs_1_.refs_9_), channel_id=1, source_target_pairs={{0,2},{1,3},{2,0},{3,1},{4,6},{5,7},{6,4},{7,5},{8,10},{9,11},{10,... | collective-permute-start | bytes 663560 | tf_op jit(solution)/shard_map/ppermute | solution.py:273
  39.4 1.8 %copy-start.2 = (bf16[128,768]{1,0:T(8,128)(2,1)S(1)}, bf16[128,768]{1,0:T(8,128)(2,1)}, u32[]{:S(2)}) copy-start(bf16[128,768]{1,0:T(8,128)(2,1)} %copy-done.1) | copy-start | bytes 589828
  41.2 2.9 %copy-start.3 = (f32[15360]{0:T(1024)S(1)}, f32[15360]{0:T(1024)}, u32[]{:S(2)}) copy-start(f32[15360]{0:T(1024)} %param.18) | copy-start | bytes 184324

commit v14 on v13

--- a/solution.py
+++ b/solution.py
@@ -210,7 +210,7 @@
 def last_kernel(seq, masks, *refs):
     me_ref, docs, tables, refs = refs[0], refs[1:3], refs[3 : 3 + len(masks)], refs[3 + len(masks) :]
     weight, params, halves, dbias_ref, refs = refs[0], refs[1], refs[2:4], refs[4], refs[5:]
-    earlier, out_ref, send = refs[:-2], refs[-2], refs[-1]
+    earlier, keep_ref, give_ref, send = refs[:-3], *refs[-3:]
     me = me_ref[0]
     core, chip = me % 2, me // 2
     devices = 2 * len(masks)
@@ -229,7 +229,7 @@
     tables = jnp.concatenate([table_of(ref) for ref in tables], axis=0)
     tables = pltpu.roll(tables, TILE - chip * tiles, 1).astype(jnp.int32)
     send[...] = jnp.zeros(send.shape, jnp.float32)
-    stride = out_ref.shape[1]
+    stride = keep_ref.shape[1]
     target = lax.broadcasted_iota(jnp.int32, (BLK_DEV * devices, TILE), 0)
     for t in range(tiles):
         lanes = slice(t * TILE, (t + 1) * TILE)
@@ -245,7 +245,34 @@
             send[pl.ds((1 + s) * SLOT_ROWS + t, devices, stride=stride), :] = blocks[
                 s * devices : (s + 1) * devices
             ]
-    out_ref[...] = send[...].astype(jnp.bfloat16).reshape(out_ref.shape)
+    for k in range(len(masks)):
+        at = pl.multiple_of((2 * k + core) * stride, SLOT_ROWS)
+        keep_ref[k] = send[pl.ds(at, stride), :].astype(jnp.bfloat16)
+        at = pl.multiple_of((2 * k + 1 - core) * stride + SLOT_ROWS, SLOT_ROWS)
+        give_ref[k] = send[pl.ds(at, stride - SLOT_ROWS), :].astype(jnp.bfloat16)
+
+
+def merge_kernel(me_ref, keep_ref, got_ref, *out_refs):
+    for mask, out_ref in enumerate(out_refs):
+        chip = (me_ref[0] // 2) ^ mask
+        rows = keep_ref[chip].astype(jnp.float32)
+        other = got_ref[chip].astype(jnp.float32)
+        both = jnp.maximum(rows[SLOT_ROWS:], other)
+        out_ref[...] = jnp.concatenate([rows[:SLOT_ROWS], both], axis=0).astype(jnp.bfloat16)
+
+
+def place_kernel(tiles, me_ref, *refs):
+    parts, impacts_ref, summaries_ref = refs[:-2], refs[-2], refs[-1]
+    for mask, ref in enumerate(parts):
+        chip = (me_ref[0] // 2) ^ mask
+        rows = ref[...].astype(jnp.float32)
+        lanes = pl.ds(pl.multiple_of(chip * tiles * TILE, TILE), tiles * TILE)
+        lines = [
+            jnp.concatenate([rows[first + t : first + t + 1] for t in range(tiles)], axis=1)
+            for first in range(0, rows.shape[0], SLOT_ROWS)
+        ]
+        impacts_ref[:, lanes] = lines[0].astype(jnp.bfloat16)
+        summaries_ref[:, lanes] = jnp.concatenate(lines[1:], axis=0).astype(jnp.bfloat16)
 
 
 def move_tokens(
@@ -308,7 +335,7 @@
     block_6 = cross(transform_weight, 6)
     block_2 = cross(transform_weight, 2)
     theirs = swap(weight_rows)
-    docs = {1: cross(hidden_states, 1), 2: cross(hidden_states, 2)}
+    docs = {1: cross(hidden_states, 1)}
     load, block, table, params = pl.pallas_call(
         start_kernel,
         out_shape=[
@@ -337,15 +364,16 @@
     )
     near = (block, after(block_2, block_6, docs[1]), table)
     near_pile = cross(pile(near, ((0, rows), (0, rows), (0, SLOT_ROWS))), 1)
-    one, two, below = (0, rows), (0, 2 * rows), (0, SLOT_ROWS)
-    block_4 = cross(pile((after(block_6, docs[2]), table), (one, below)), 2)
+    one, two = (0, rows), (0, 2 * rows)
+    block_4 = cross(block_6, 2)
     docs[6] = cross(after(load, block_6), 6)
+    docs[2] = cross(after(load, block_4), 2)
     load_1 = pile((docs[1], near_pile), ((0, seq), (2 * rows, SLOT_ROWS)))
     far = (block_6, after(block_4, near_pile))
     far = pile(far, ((0, rows), (0, rows)))
     far_pile = cross(far, 1)
     docs[3] = cross(after(load_1, far), 2)
-    docs[4] = cross(after(docs[6], far, docs[3]), 2)
+    docs[4] = cross(after(docs[6], far, docs[2]), 2)
     docs[7] = cross(docs[6], 1)
     late = (docs[6], theirs)
     sources = (after(block, *late), block_2, block_6, block_4, near_pile, far_pile)
@@ -386,7 +414,7 @@
         theirs,
     )
     docs |= {0: load, 1: beside, 5: cross(after(docs[4], weight), 1)}
-    tables = docs | {1: near_pile, 2: block_4}
+    tables = docs | {1: near_pile}
     for first in range(2, len(masks) - 2, 2):
         pair = masks[first : first + 2]
         best += pl.pallas_call(
@@ -404,14 +432,16 @@
             mine,
             theirs,
         )
-    send = pl.pallas_call(
+    height = (1 + BLK_DEV) * SLOT_ROWS
+    keep, give = pl.pallas_call(
         lambda *refs: last_kernel(seq, masks, *refs),
-        out_shape=shape((devices, (1 + BLK_DEV) * SLOT_ROWS, TILE), jnp.bfloat16),
+        out_shape=[
+            shape((chips, height, TILE), jnp.bfloat16),
+            shape((chips, height - SLOT_ROWS, TILE), jnp.bfloat16),
+        ],
         in_specs=[smem] + [vmem] * (2 + len(masks) + 5 + len(best)),
-        out_specs=vmem,
-        scratch_shapes=[
-            pltpu.VMEM((devices * (1 + BLK_DEV) * SLOT_ROWS, TILE), jnp.float32),
-        ],
+        out_specs=[vmem] * 2,
+        scratch_shapes=[pltpu.VMEM((devices * height, TILE), jnp.float32)],
         compiler_params=limit,
         cost_estimate=cost(2),
     )(
@@ -425,10 +455,24 @@
         decoder_bias.reshape(-1, TILE),
         *best,
     )
-    got = lax.all_to_all(send, "doc", split_axis=0, concat_axis=0, tiled=True)
-    got = got.reshape(chips, 2, 1 + BLK_DEV, SLOT_ROWS, TILE)[:, :, :, :tiles]
-    whole = jnp.swapaxes(jnp.maximum(got[:, 0], got[:, 1]), 0, 1).reshape(1 + BLK_DEV, -1)
-    return (whole[:1], whole[1:])
+    parts = pl.pallas_call(
+        merge_kernel,
+        out_shape=[shape((height, TILE), jnp.bfloat16)] * chips,
+        in_specs=[smem] + [vmem] * 2,
+        out_specs=[vmem] * chips,
+        compiler_params=limit,
+    )(where, keep, swap(give))
+    parts = [cross(part, mask) if mask else part for mask, part in enumerate(parts)]
+    return pl.pallas_call(
+        lambda *refs: place_kernel(tiles, *refs),
+        out_shape=[
+            shape((1, chips * tiles * TILE), jnp.bfloat16),
+            shape((BLK_DEV, chips * tiles * TILE), jnp.bfloat16),
+        ],
+        in_specs=[smem] + [vmem] * chips,
+        out_specs=[vmem] * 2,
+        compiler_params=limit,
+    )(where, *parts)
 
 
 def tokens_move(mesh):

time: 60.5 us -> 61.7 us (1.020)
  starting transfers between devices: 15.3 us -> 29.5 us
  blocking collectives: 12.6 us -> 0 us
  local copies, waits for them, and re-layouts: 1.34 us -> 0.01 us
  Pallas kernels: 11.7 us -> 12.5 us
    ppermute x12 -> x19, starting transfers between devices: 14.2 us -> 28.3 us  [cross(): lax.ppermute(value, 'doc', [(i, i ^ 2 * mask) for i in range(devices)])]
    all_to_all x1 -> x0, blocking collectives: 12.6 us -> none  [move_tokens(): got = lax.all_to_all(send, 'doc', split_axis=0, concat_axis=0, tiled=True)]
    slice x5 -> x0, local copies, waits for them, and re-layouts: 1.33 us -> none  [the longest x4 1.31 us: move_tokens(): return (whole[:1], whole[1:])]
    ppermute x3 -> x4, waiting for transfers between devices: 0.01 us -> 1.25 us  [swap(): return lax.ppermute(value, 'doc', [(i, i ^ 1) for i in range(devices)])]
    ppermute x12 -> x19, waiting for transfers between devices: 17.8 us -> 16.8 us  [cross(): lax.ppermute(value, 'doc', [(i, i ^ 2 * mask) for i in range(devices)])]
    pallas_call x1 -> x3, Pallas kernels: 2.14 us -> 2.92 us  [the longest x1 2.13 us: move_tokens(): pl.pallas_call(lambda *refs: last_kernel(seq, masks, *refs), out_shape=[s...]
  transfers between devices with their start and end apart: 15 -> 23, of which waited for: 7 -> 11; matrix products, arithmetic and copies ran while one was open for 0% -> 0% of each run, Pallas kernels for 16% -> 16%
where the time goes in v14:
time: 61.7 us; the launch traced here: 61.5 us
  starting transfers between devices  29.5 us (48%)
  waiting for transfers between devices  18 us (29%)
  Pallas kernels  12.5 us (20%)
  between operations  1.42 us (2%)
    ppermute x19, starting transfers between devices, cross(): lax.ppermute(value, 'doc', [(i, i ^ 2 * mask) for i in range(devices)])  28.3 us
    ppermute x19, waiting for transfers between devices, cross(): lax.ppermute(value, 'doc', [(i, i ^ 2 * mask) for i in range(devices)])  16.8 us
    pallas_call x2, Pallas kernels, move_tokens(): pl.pallas_call(lambda *refs: next_kernel(seq, *refs), out_shape=[best_sha...  3.58 us
    pallas_call x1, Pallas kernels, move_tokens(): pl.pallas_call(lambda *refs: first_kernel(seq, block_masks, *refs), out_s...  2.86 us
    pallas_call x1, Pallas kernels, move_tokens(): pl.pallas_call(lambda *refs: last_kernel(seq, masks, *refs), out_shape=[s...  2.13 us
    pallas_call x1, Pallas kernels, move_tokens(): pl.pallas_call(start_kernel, out_shape=[shape((seq + SLOT_ROWS, width), j...  1.71 us
    pallas_call x1, Pallas kernels, move_tokens(): pl.pallas_call(lambda *refs: fetch_kernel(2, *refs), out_shape=[shape(val...  1.39 us
    ppermute x4, waiting for transfers between devices, swap(): return lax.ppermute(value, 'doc', [(i, i ^ 1) for i in range(devices)])  1.25 us
  transfers between devices with their start and end apart: 23, of which 11 were waited for; matrix products, arithmetic and copies ran while one was open for 0% of the time, Pallas kernels for 16%

profile of v14, /device:TPU:0, one launch (start us, length us, event | category | flops | bytes accessed | tf_op | source)
XLA Modules:
  0.0 61.5 jit_solution(1162260793431932838)
XLA Ops:
  0.6 0.5 collective-permute-start.8
  1.2 2.6 %collective-permute-start.4 = (bf16[128,768]{1,0:T(8,128)(2,1)}, bf16[128,768]{1,0:T(8,128)(2,1)S(1)}, u32[]{:S(2)}, u32[]{:S(2)}) collective-permute-start(bf16[128,768]{1,0:T(8,128)(2,1)} %refs_0_.1), channel_id=1, source_target_pairs={{0,2},{1,3},{2,0},{3,1},{4,6},{5,7},{6,4},{7,5},{8,10},{9,11},{10,... | collective-permute-start | bytes 589832 | tf_op jit(solution)/shard_map/ppermute | solution.py:300
  3.7 3.6 %collective-permute-start = (bf16[48,768]{1,0:T(8,128)(2,1)}, bf16[48,768]{1,0:T(8,128)(2,1)S(1)}, u32[]{:S(2)}, u32[]{:S(2)}) collective-permute-start(bf16[48,768]{1,0:T(8,128)(2,1)} %refs_1_.1), channel_id=1, source_target_pairs={{0,12},{1,13},{2,14},{3,15},{4,8},{5,9},{6,10},{7,11},{8,4},{9,5},... | collective-permute-start | bytes 221192 | tf_op jit(solution)/shard_map/ppermute | solution.py:300
  7.3 0.0 collective-permute-start.3
  8.0 1.7 %shard_map.122 = (bf16[144,768]{1,0:T(8,128)(2,1)S(1)}, bf16[48,768]{1,0:T(8,128)(2,1)S(1)}, bf16[16,768]{1,0:T(8,128)(2,1)S(1)}, f32[8,768]{1,0:T(8,128)S(1)}) custom-call(s32[1,1,32]{2,1,0:T(1,128)} %tiles_ref.1, s32[1,1,32]{2,1,0:T(1,128)} %bitcast.9, s32[1,1,32]{2,1,0:T(1,128)} %slots_ref.1, s32[1]{0:T(128)S(6)} %copy.13.length_ref, ...), custom_call_target="tpu_custom_call" | custom-call | tf_op jit(solution)/shard_map/pallas_call | solution.py:339
  9.7 1.1 %collective-permute-done.refs_0_.refs_2_ = bf16[48,768]{1,0:T(8,128)(2,1)S(1)} collective-permute-done((bf16[48,768]{1,0:T(8,128)(2,1)}, bf16[48,768]{1,0:T(8,128)(2,1)S(1)}, u32[]{:S(2)}, u32[]{:S(2)}) %collective-permute-start) | collective-permute-done | bytes 73760 | tf_op jit(solution)/shard_map/ppermute | solution.py:300
  10.8 1.2 %collective-permute-done.3.refs_1_ = bf16[48,768]{1,0:T(8,128)(2,1)S(1)} collective-permute-done((bf16[48,768]{1,0:T(8,128)(2,1)}, bf16[48,768]{1,0:T(8,128)(2,1)S(1)}, u32[]{:S(2)}, u32[]{:S(2)}) %collective-permute-start.3) | collective-permute-done | bytes 73760 | tf_op jit(solution)/shard_map/ppermute | solution.py:300
  12.0 0.5 collective-permute-start.5
  12.5 1.6 %collective-permute-start.2 = (bf16[48,768]{1,0:T(8,128)(2,1)S(1)}, bf16[48,768]{1,0:T(8,128)(2,1)S(1)}, u32[]{:S(2)}, u32[]{:S(2)}) collective-permute-start(bf16[48,768]{1,0:T(8,128)(2,1)S(1)} %collective-permute-done.refs_0_.refs_2_), channel_id=1, source_target_pairs={{0,4},{1,5},{2,6},{3,7},{4,0},{5,1},{6,2},{7,3},{8,12},{9,13},{10,... | collective-permute-start | bytes 221192 | tf_op jit(solution)/shard_map/ppermute | solution.py:300
  14.1 1.2 %collective-permute-start.1 = (bf16[144,768]{1,0:T(8,128)(2,1)S(1)}, bf16[144,768]{1,0:T(8,128)(2,1)S(1)}, u32[]{:S(2)}, u32[]{:S(2)}) collective-permute-start(bf16[144,768]{1,0:T(8,128)(2,1)S(1)} %get-tuple-element.44.refs_1_.refs_3_), channel_id=1, source_target_pairs={{0,12},{1,13},{2,14},{3,15},{4,8},{5,9},{6,10},{7,11},{8,4},{9,5},... | collective-permute-start | bytes 663560 | tf_op jit(solution)/shard_map/ppermute | solution.py:300
  15.3 1.6 %collective-permute-done.2.refs_1_.refs_3_ = bf16[48,768]{1,0:T(8,128)(2,1)S(1)} collective-permute-done((bf16[48,768]{1,0:T(8,128)(2,1)S(1)}, bf16[48,768]{1,0:T(8,128)(2,1)S(1)}, u32[]{:S(2)}, u32[]{:S(2)}) %collective-permute-start.2) | collective-permute-done | bytes 73760 | tf_op jit(solution)/shard_map/ppermute | solution.py:300
  16.9 0.9 %collective-permute-done.5.refs_4_.refs_1_ = bf16[112,768]{1,0:T(8,128)(2,1)S(1)} collective-permute-done((bf16[112,768]{1,0:T(8,128)(2,1)S(1)}, bf16[112,768]{1,0:T(8,128)(2,1)S(1)}, u32[]{:S(2)}, u32[]{:S(2)}) %collective-permute-start.5) | collective-permute-done | bytes 172064 | tf_op jit(solution)/shard_map/ppermute | solution.py:300
  17.8 0.7 %collective-permute-start.9 = (bf16[96,768]{1,0:T(8,128)(2,1)S(1)}, bf16[96,768]{1,0:T(8,128)(2,1)S(1)}, u32[]{:S(2)}, u32[]{:S(2)}) collective-permute-start(bf16[96,768]{1,0:T(8,128)(2,1)S(1)} %shard_map.124), channel_id=1, source_target_pairs={{0,2},{1,3},{2,0},{3,1},{4,6},{5,7},{6,4},{7,5},{8,10},{9,11},{10,... | collective-permute-start | bytes 442376 | tf_op jit(solution)/shard_map/ppermute | solution.py:300
  18.6 2.3 %collective-permute-start.6 = (bf16[144,768]{1,0:T(8,128)(2,1)S(1)}, bf16[144,768]{1,0:T(8,128)(2,1)S(1)}, u32[]{:S(2)}, u32[]{:S(2)}) collective-permute-start(bf16[144,768]{1,0:T(8,128)(2,1)S(1)} %get-tuple-element.44.refs_1_.refs_3_), channel_id=1, source_target_pairs={{0,4},{1,5},{2,6},{3,7},{4,0},{5,1},{6,2},{7,3},{8,12},{9,13},{10,... | collective-permute-start | bytes 663560 | tf_op jit(solution)/shard_map/ppermute | solution.py:300
  20.9 3.4 %collective-permute-done.1.refs_0_.refs_2_.refs_5_ = bf16[144,768]{1,0:T(8,128)(2,1)S(1)} collective-permute-done((bf16[144,768]{1,0:T(8,128)(2,1)S(1)}, bf16[144,768]{1,0:T(8,128)(2,1)S(1)}, u32[]{:S(2)}, u32[]{:S(2)}) %collective-permute-start.1) | collective-permute-done | bytes 221216 | tf_op jit(solution)/shard_map/ppermute | solution.py:300
  24.2 0.0 collective-permute-done.8.refs_11_.refs_7_.refs_14_
  24.2 0.0 collective-permute-done.9.refs_5_
  24.3 0.1 collective-permute-start.10
  24.4 0.5 collective-permute-start.11
  24.9 2.3 %collective-permute-done.6.refs_0_.refs_2_.refs_7_ = bf16[144,768]{1,0:T(8,128)(2,1)S(1)} collective-permute-done((bf16[144,768]{1,0:T(8,128)(2,1)S(1)}, bf16[144,768]{1,0:T(8,128)(2,1)S(1)}, u32[]{:S(2)}, u32[]{:S(2)}) %collective-permute-start.6) | collective-permute-done | bytes 221216 | tf_op jit(solution)/shard_map/ppermute | solution.py:300
  27.2 0.1 collective-permute-start.7
  27.3 1.2 %collective-permute-start.13 = (bf16[144,768]{1,0:T(8,128)(2,1)S(1)}, bf16[144,768]{1,0:T(8,128)(2,1)S(1)}, u32[]{:S(2)}, u32[]{:S(2)}) collective-permute-start(bf16[144,768]{1,0:T(8,128)(2,1)S(1)} %collective-permute-done.1.refs_0_.refs_2_.refs_5_), channel_id=1, source_target_pairs={{0,2},{1,3},{2,0},{3,1},{4,6},{5,7},{6,4},{7,5},{8,10},{9,11},{10,... | collective-permute-start | bytes 663560 | tf_op jit(solution)/shard_map/ppermute | solution.py:300
  28.5 2.1 %collective-permute-start.14 = (bf16[144,768]{1,0:T(8,128)(2,1)S(1)}, bf16[144,768]{1,0:T(8,128)(2,1)S(1)}, u32[]{:S(2)}, u32[]{:S(2)}) collective-permute-start(bf16[144,768]{1,0:T(8,128)(2,1)S(1)} %shard_map.128), channel_id=1, source_target_pairs={{0,4},{1,5},{2,6},{3,7},{4,0},{5,1},{6,2},{7,3},{8,12},{9,13},{10,... | collective-permute-start | bytes 663560 | tf_op jit(solution)/shard_map/ppermute | solution.py:300
  30.5 1.4 %shard_map.126 = (bf16[960,768]{1,0:T(8,128)(2,1)S(1)}, bf16[128,768]{1,0:T(8,128)(2,1)S(1)}) custom-call(bf16[192,768]{1,0:T(8,128)(2,1)S(1)} %get-tuple-element.47.refs_0_.refs_5_, bf16[960,768]{1,0:T(8,128)(2,1)} %bitcast.8, bf16[128,768]{1,0:T(8,128)(2,1)} %copy-done), custom_call_target="tpu_custom_call" | custom-call | tf_op jit(solution)/shard_map/pallas_call | solution.py:385
  31.9 0.0 collective-permute-done.10.refs_7_
  32.0 0.0 collective-permute-done.11.refs_8_
  32.0 2.9 %shard_map.127 = (f32[8,960]{1,0:T(8,128)S(1)}, f32[8,960]{1,0:T(8,128)S(1)}, bf16[768,768]{1,0:T(8,128)(2,1)S(1)}) custom-call(s32[1]{0:T(128)} %bitcast.refs_0_.me_ref, bf16[144,768]{1,0:T(8,128)(2,1)S(1)} %get-tuple-element.44.refs_1_.refs_3_, bf16[128,768]{1,0:T(8,128)(2,1)S(1)} %get-tuple-element.50.refs_2_, ...), custom_call_target="tpu_custom_call" | custom-call | flops 2 | bytes 2 | tf_op jit(solution)/shard_map/pallas_call | solution.py:397
  34.8 0.7 %collective-permute-done.7.refs_1_.refs_9_ = bf16[144,768]{1,0:T(8,128)(2,1)S(1)} collective-permute-done((bf16[144,768]{1,0:T(8,128)(2,1)S(1)}, bf16[144,768]{1,0:T(8,128)(2,1)S(1)}, u32[]{:S(2)}, u32[]{:S(2)}) %collective-permute-start.7) | collective-permute-done | bytes 221216 | tf_op jit(solution)/shard_map/ppermute | solution.py:300
  35.5 1.3 %collective-permute-start.12 = (bf16[144,768]{1,0:T(8,128)(2,1)S(1)}, bf16[144,768]{1,0:T(8,128)(2,1)S(1)}, u32[]{:S(2)}, u32[]{:S(2)}) collective-permute-start(bf16[144,768]{1,0:T(8,128)(2,1)S(1)} %collective-permute-done.7.refs_1_.refs_9_), channel_id=1, source_target_pairs={{0,2},{1,3},{2,0},{3,1},{4,6},{5,7},{6,4},{7,5},{8,10},{9,11},{10,... | collective-permute-start | bytes 663560 | tf_op jit(solution)/shard_map/ppermute | solution.py:300
  36.8 1.8 %shard_map.129 = (f32[8,960]{1,0:T(8,128)S(1)}, f32[8,960]{1,0:T(8,128)S(1)}) custom-call(bf16[144,768]{1,0:T(8,128)(2,1)S(1)} %collective-permute-done.1.refs_0_.refs_2_.refs_5_, bf16[144,768]{1,0:T(8,128)(2,1)S(1)} %collective-permute-done.13.refs_1_.refs_3_.refs_6_, bf16[144,768]{1,0:T(8,128)(2,1)S(1)} %collective-permute-done.1.refs_0_.refs_2_.refs_5_, ...), custom_call_target="tpu_custom_call" | custom-call | flops 2 | bytes 2 | tf_op jit(solution)/shard_map/pallas_call | solution.py:420
  38.6 0.0 copy-start.1
  38.6 0.0 collective-permute-done.14.refs_1_.refs_3_.refs_8_
  38.6 1.8 %shard_map.130 = (f32[8,960]{1,0:T(8,128)S(1)}, f32[8,960]{1,0:T(8,128)S(1)}) custom-call(bf16[144,768]{1,0:T(8,128)(2,1)S(1)} %collective-permute-done.6.refs_0_.refs_2_.refs_7_, bf16[144,768]{1,0:T(8,128)(2,1)S(1)} %collective-permute-done.14.refs_1_.refs_3_.refs_8_, bf16[144,768]{1,0:T(8,128)(2,1)S(1)} %collective-permute-done.6.refs_0_.refs_2_.refs_7_, ...), custom_call_target="tpu_custom_call" | custom-call | flops 2 | bytes 2 | tf_op jit(solution)/shard_map/pallas_call | solution.py:420
  40.4 1.1 %collective-permute-done.12.refs_2_.refs_10_ = bf16[144,768]{1,0:T(8,128)(2,1)S(1)} collective-permute-done((bf16[144,768]{1,0:T(8,128)(2,1)S(1)}, bf16[144,768]{1,0:T(8,128)(2,1)S(1)}, u32[]{:S(2)}, u32[]{:S(2)}) %collective-permute-start.12) | collective-permute-done | bytes 221216 | tf_op jit(solution)/shard_map/ppermute | solution.py:300
  41.5 2.1 %shard_map.131 = (bf16[8,48,128]{2,1,0:T(8,128)(2,1)S(1)}, bf16[8,32,128]{2,1,0:T(8,128)(2,1)S(1)}) custom-call(s32[1]{0:T(128)} %bitcast.refs_0_.me_ref, bf16[144,768]{1,0:T(8,128)(2,1)S(1)} %collective-permute-done.7.refs_1_.refs_9_, bf16[144,768]{1,0:T(8,128)(2,1)S(1)} %collective-permute-done.12.refs_2_.refs_10_, ...), custom_call_target="tpu_custom_call" | custom-call | flops 2 | bytes 2 | tf_op jit(solution)/shard_map/pallas_call | solution.py:436
  43.6 0.1 collective-permute-start.15
  43.7 1.2 %collective-permute-done.15.got_ref = bf16[8,32,128]{2,1,0:T(8,128)(2,1)S(1)} collective-permute-done((bf16[8,32,128]{2,1,0:T(8,128)(2,1)S(1)}, bf16[8,32,128]{2,1,0:T(8,128)(2,1)S(1)}, u32[]{:S(2)}, u32[]{:S(2)}) %collective-permute-start.15) | collective-permute-done | bytes 65568 | tf_op jit(solution)/shard_map/ppermute | solution.py:303
  45.0 1.3 %collective-permute-start.16 = (bf16[48,128]{1,0:T(8,128)(2,1)S(1)}, bf16[48,128]{1,0:T(8,128)(2,1)S(1)}, u32[]{:S(2)}, u32[]{:S(2)}) collective-permute-start(bf16[48,128]{1,0:T(8,128)(2,1)S(1)} %get-tuple-element.67), channel_id=1, source_target_pairs={{0,2},{1,3},{2,0},{3,1},{4,6},{5,7},{6,4},{7,5},{8,10},{9,11},{10,... | collective-permute-start | bytes 36872 | tf_op jit(solution)/shard_map/ppermute | solution.py:300
  46.3 0.0 collective-permute-start.17
  46.3 2.2 %collective-permute-start.18 = (bf16[48,128]{1,0:T(8,128)(2,1)S(1)}, bf16[48,128]{1,0:T(8,128)(2,1)S(1)}, u32[]{:S(2)}, u32[]{:S(2)}) collective-permute-start(bf16[48,128]{1,0:T(8,128)(2,1)S(1)} %get-tuple-element.69), channel_id=1, source_target_pairs={{0,6},{1,7},{2,4},{3,5},{4,2},{5,3},{6,0},{7,1},{8,14},{9,15},{10,... | collective-permute-start | bytes 36872 | tf_op jit(solution)/shard_map/ppermute | solution.py:300
  48.5 1.3 %collective-permute-start.19 = (bf16[48,128]{1,0:T(8,128)(2,1)S(1)}, bf16[48,128]{1,0:T(8,128)(2,1)S(1)}, u32[]{:S(2)}, u32[]{:S(2)}) collective-permute-start(bf16[48,128]{1,0:T(8,128)(2,1)S(1)} %get-tuple-element.70), channel_id=1, source_target_pairs={{0,8},{1,9},{2,10},{3,11},{4,12},{5,13},{6,14},{7,15},{8,0},{9,1},... | collective-permute-start | bytes 36872 | tf_op jit(solution)/shard_map/ppermute | solution.py:300
  49.8 2.3 %collective-permute-start.20 = (bf16[48,128]{1,0:T(8,128)(2,1)S(1)}, bf16[48,128]{1,0:T(8,128)(2,1)S(1)}, u32[]{:S(2)}, u32[]{:S(2)}) collective-permute-start(bf16[48,128]{1,0:T(8,128)(2,1)S(1)} %get-tuple-element.71), channel_id=1, source_target_pairs={{0,10},{1,11},{2,8},{3,9},{4,14},{5,15},{6,12},{7,13},{8,2},{9,3},... | collective-permute-start | bytes 36872 | tf_op jit(solution)/shard_map/ppermute | solution.py:300
  52.1 0.0 collective-permute-done.16.refs_2_
  52.1 2.1 %collective-permute-start.21 = (bf16[48,128]{1,0:T(8,128)(2,1)S(1)}, bf16[48,128]{1,0:T(8,128)(2,1)S(1)}, u32[]{:S(2)}, u32[]{:S(2)}) collective-permute-start(bf16[48,128]{1,0:T(8,128)(2,1)S(1)} %get-tuple-element.72), channel_id=1, source_target_pairs={{0,12},{1,13},{2,14},{3,15},{4,8},{5,9},{6,10},{7,11},{8,4},{9,5},... | collective-permute-start | bytes 36872 | tf_op jit(solution)/shard_map/ppermute | solution.py:300
  54.3 1.9 %collective-permute-start.22 = (bf16[48,128]{1,0:T(8,128)(2,1)S(1)}, bf16[48,128]{1,0:T(8,128)(2,1)S(1)}, u32[]{:S(2)}, u32[]{:S(2)}) collective-permute-start(bf16[48,128]{1,0:T(8,128)(2,1)S(1)} %get-tuple-element.73), channel_id=1, source_target_pairs={{0,14},{1,15},{2,12},{3,13},{4,10},{5,11},{6,8},{7,9},{8,6},{9,7},... | collective-permute-start | bytes 36872 | tf_op jit(solution)/shard_map/ppermute | solution.py:300
  56.2 1.4 %collective-permute-done.21.refs_7_ = bf16[48,128]{1,0:T(8,128)(2,1)S(1)} collective-permute-done((bf16[48,128]{1,0:T(8,128)(2,1)S(1)}, bf16[48,128]{1,0:T(8,128)(2,1)S(1)}, u32[]{:S(2)}, u32[]{:S(2)}) %collective-permute-start.21) | collective-permute-done | bytes 12320 | tf_op jit(solution)/shard_map/ppermute | solution.py:300
  57.6 3.0 %collective-permute-done.22.refs_8_ = bf16[48,128]{1,0:T(8,128)(2,1)S(1)} collective-permute-done((bf16[48,128]{1,0:T(8,128)(2,1)S(1)}, bf16[48,128]{1,0:T(8,128)(2,1)S(1)}, u32[]{:S(2)}, u32[]{:S(2)}) %collective-permute-start.22) | collective-permute-done | bytes 12320 | tf_op jit(solution)/shard_map/ppermute | solution.py:300
  60.7 0.8 %shard_map.133 = (bf16[1,15360]{1,0:T(2,128)(2,1)}, bf16[2,15360]{1,0:T(2,128)(2,1)}) custom-call(s32[1]{0:T(128)} %bitcast.refs_0_.me_ref, bf16[48,128]{1,0:T(8,128)(2,1)S(1)} %get-tuple-element.66.refs_1_, bf16[48,128]{1,0:T(8,128)(2,1)S(1)} %collective-permute-done.16.refs_2_, bf16[48,128]{1,0:T(8,128)(2,1)S(1)} %collective-permute-done.17.refs_3_, ...), custom_call_target="tpu_custom_call" | custom-call | tf_op jit(solution)/shard_map/pallas_call | solution.py:466
  (14 shorter events, 0.1 us)
Async XLA Ops:
  0.6 23.6 %collective-permute-start.8 = (bf16[960,768]{1,0:T(8,128)(2,1)}, bf16[960,768]{1,0:T(8,128)(2,1)S(1)}, u32[]{:S(2)}, u32[]{:S(2)}) collective-permute-start(bf16[960,768]{1,0:T(8,128)(2,1)} %bitcast.7), channel_id=1, source_target_pairs={{0,1},{1,0},{2,3},{3,2},{4,5},{5,4},{6,7},{7,6},{8,9},{9,8},{10,11... | collective-permute-start | bytes 4423688 | tf_op jit(solution)/shard_map/ppermute | solution.py:303
  1.2 10.9 %collective-permute-start.4 = (bf16[128,768]{1,0:T(8,128)(2,1)}, bf16[128,768]{1,0:T(8,128)(2,1)S(1)}, u32[]{:S(2)}, u32[]{:S(2)}) collective-permute-start(bf16[128,768]{1,0:T(8,128)(2,1)} %refs_0_.1), channel_id=1, source_target_pairs={{0,2},{1,3},{2,0},{3,1},{4,6},{5,7},{6,4},{7,5},{8,10},{9,11},{10,... | collective-permute-start | bytes 589832 | tf_op jit(solution)/shard_map/ppermute | solution.py:300
  3.7 7.1 %collective-permute-start = (bf16[48,768]{1,0:T(8,128)(2,1)}, bf16[48,768]{1,0:T(8,128)(2,1)S(1)}, u32[]{:S(2)}, u32[]{:S(2)}) collective-permute-start(bf16[48,768]{1,0:T(8,128)(2,1)} %refs_1_.1), channel_id=1, source_target_pairs={{0,12},{1,13},{2,14},{3,15},{4,8},{5,9},{6,10},{7,11},{8,4},{9,5},... | collective-permute-start | bytes 221192 | tf_op jit(solution)/shard_map/ppermute | solution.py:300
  7.3 4.7 %collective-permute-start.3 = (bf16[48,768]{1,0:T(8,128)(2,1)}, bf16[48,768]{1,0:T(8,128)(2,1)S(1)}, u32[]{:S(2)}, u32[]{:S(2)}) collective-permute-start(bf16[48,768]{1,0:T(8,128)(2,1)} %refs_1_.1), channel_id=1, source_target_pairs={{0,4},{1,5},{2,6},{3,7},{4,0},{5,1},{6,2},{7,3},{8,12},{9,13},{10,... | collective-permute-start | bytes 221192 | tf_op jit(solution)/shard_map/ppermute | solution.py:300
  12.0 18.5 %copy-start = (bf16[128,768]{1,0:T(8,128)(2,1)}, bf16[128,768]{1,0:T(8,128)(2,1)S(1)}, u32[]{:S(2)}) copy-start(bf16[128,768]{1,0:T(8,128)(2,1)S(1)} %collective-permute-done.4.refs_2_.refs_0_) | copy-start | bytes 589828
  12.0 5.8 %collective-permute-start.5 = (bf16[112,768]{1,0:T(8,128)(2,1)S(1)}, bf16[112,768]{1,0:T(8,128)(2,1)S(1)}, u32[]{:S(2)}, u32[]{:S(2)}) collective-permute-start(bf16[112,768]{1,0:T(8,128)(2,1)S(1)} %shard_map.123), channel_id=1, source_target_pairs={{0,2},{1,3},{2,0},{3,1},{4,6},{5,7},{6,4},{7,5},{8,10},{9,11},{10,... | collective-permute-start | bytes 516104 | tf_op jit(solution)/shard_map/ppermute | solution.py:300
  12.5 4.4 %collective-permute-start.2 = (bf16[48,768]{1,0:T(8,128)(2,1)S(1)}, bf16[48,768]{1,0:T(8,128)(2,1)S(1)}, u32[]{:S(2)}, u32[]{:S(2)}) collective-permute-start(bf16[48,768]{1,0:T(8,128)(2,1)S(1)} %collective-permute-done.refs_0_.refs_2_), channel_id=1, source_target_pairs={{0,4},{1,5},{2,6},{3,7},{4,0},{5,1},{6,2},{7,3},{8,12},{9,13},{10,... | collective-permute-start | bytes 221192 | tf_op jit(solution)/shard_map/ppermute | solution.py:300
  14.1 10.2 %collective-permute-start.1 = (bf16[144,768]{1,0:T(8,128)(2,1)S(1)}, bf16[144,768]{1,0:T(8,128)(2,1)S(1)}, u32[]{:S(2)}, u32[]{:S(2)}) collective-permute-start(bf16[144,768]{1,0:T(8,128)(2,1)S(1)} %get-tuple-element.44.refs_1_.refs_3_), channel_id=1, source_target_pairs={{0,12},{1,13},{2,14},{3,15},{4,8},{5,9},{6,10},{7,11},{8,4},{9,5},... | collective-permute-start | bytes 663560 | tf_op jit(solution)/shard_map/ppermute | solution.py:300
  17.8 6.4 %collective-permute-start.9 = (bf16[96,768]{1,0:T(8,128)(2,1)S(1)}, bf16[96,768]{1,0:T(8,128)(2,1)S(1)}, u32[]{:S(2)}, u32[]{:S(2)}) collective-permute-start(bf16[96,768]{1,0:T(8,128)(2,1)S(1)} %shard_map.124), channel_id=1, source_target_pairs={{0,2},{1,3},{2,0},{3,1},{4,6},{5,7},{6,4},{7,5},{8,10},{9,11},{10,... | collective-permute-start | bytes 442376 | tf_op jit(solution)/shard_map/ppermute | solution.py:300
  18.6 8.6 %collective-permute-start.6 = (bf16[144,768]{1,0:T(8,128)(2,1)S(1)}, bf16[144,768]{1,0:T(8,128)(2,1)S(1)}, u32[]{:S(2)}, u32[]{:S(2)}) collective-permute-start(bf16[144,768]{1,0:T(8,128)(2,1)S(1)} %get-tuple-element.44.refs_1_.refs_3_), channel_id=1, source_target_pairs={{0,4},{1,5},{2,6},{3,7},{4,0},{5,1},{6,2},{7,3},{8,12},{9,13},{10,... | collective-permute-start | bytes 663560 | tf_op jit(solution)/shard_map/ppermute | solution.py:300
  24.3 7.7 %collective-permute-start.10 = (bf16[192,768]{1,0:T(8,128)(2,1)S(1)}, bf16[192,768]{1,0:T(8,128)(2,1)}, u32[]{:S(2)}, u32[]{:S(2)}) collective-permute-start(bf16[192,768]{1,0:T(8,128)(2,1)S(1)} %get-tuple-element.47.refs_0_.refs_5_), channel_id=1, source_target_pairs={{0,1},{1,0},{2,3},{3,2},{4,5},{5,4},{6,7},{7,6},{8,9},{9,8},{10,11... | collective-permute-start | bytes 884744 | tf_op jit(solution)/shard_map/ppermute | solution.py:303
  24.4 7.6 %collective-permute-start.11 = (bf16[192,768]{1,0:T(8,128)(2,1)S(1)}, bf16[192,768]{1,0:T(8,128)(2,1)}, u32[]{:S(2)}, u32[]{:S(2)}) collective-permute-start(bf16[192,768]{1,0:T(8,128)(2,1)S(1)} %get-tuple-element.48.refs_6_), channel_id=1, source_target_pairs={{0,1},{1,0},{2,3},{3,2},{4,5},{5,4},{6,7},{7,6},{8,9},{9,8},{10,11... | collective-permute-start | bytes 884744 | tf_op jit(solution)/shard_map/ppermute | solution.py:303
  27.2 8.4 %collective-permute-start.7 = (bf16[144,768]{1,0:T(8,128)(2,1)S(1)}, bf16[144,768]{1,0:T(8,128)(2,1)S(1)}, u32[]{:S(2)}, u32[]{:S(2)}) collective-permute-start(bf16[144,768]{1,0:T(8,128)(2,1)S(1)} %collective-permute-done.1.refs_0_.refs_2_.refs_5_), channel_id=1, source_target_pairs={{0,4},{1,5},{2,6},{3,7},{4,0},{5,1},{6,2},{7,3},{8,12},{9,13},{10,... | collective-permute-start | bytes 663560 | tf_op jit(solution)/shard_map/ppermute | solution.py:300
  27.3 9.5 %collective-permute-start.13 = (bf16[144,768]{1,0:T(8,128)(2,1)S(1)}, bf16[144,768]{1,0:T(8,128)(2,1)S(1)}, u32[]{:S(2)}, u32[]{:S(2)}) collective-permute-start(bf16[144,768]{1,0:T(8,128)(2,1)S(1)} %collective-permute-done.1.refs_0_.refs_2_.refs_5_), channel_id=1, source_target_pairs={{0,2},{1,3},{2,0},{3,1},{4,6},{5,7},{6,4},{7,5},{8,10},{9,11},{10,... | collective-permute-start | bytes 663560 | tf_op jit(solution)/shard_map/ppermute | solution.py:300
  28.5 10.2 %collective-permute-start.14 = (bf16[144,768]{1,0:T(8,128)(2,1)S(1)}, bf16[144,768]{1,0:T(8,128)(2,1)S(1)}, u32[]{:S(2)}, u32[]{:S(2)}) collective-permute-start(bf16[144,768]{1,0:T(8,128)(2,1)S(1)} %shard_map.128), channel_id=1, source_target_pairs={{0,4},{1,5},{2,6},{3,7},{4,0},{5,1},{6,2},{7,3},{8,12},{9,13},{10,... | collective-permute-start | bytes 663560 | tf_op jit(solution)/shard_map/ppermute | solution.py:300
  35.5 5.9 %collective-permute-start.12 = (bf16[144,768]{1,0:T(8,128)(2,1)S(1)}, bf16[144,768]{1,0:T(8,128)(2,1)S(1)}, u32[]{:S(2)}, u32[]{:S(2)}) collective-permute-start(bf16[144,768]{1,0:T(8,128)(2,1)S(1)} %collective-permute-done.7.refs_1_.refs_9_), channel_id=1, source_target_pairs={{0,2},{1,3},{2,0},{3,1},{4,6},{5,7},{6,4},{7,5},{8,10},{9,11},{10,... | collective-permute-start | bytes 663560 | tf_op jit(solution)/shard_map/ppermute | solution.py:300
  38.6 2.9 %copy-start.1 = (f32[15360]{0:T(1024)S(1)}, f32[15360]{0:T(1024)}, u32[]{:S(2)}) copy-start(f32[15360]{0:T(1024)} %param.18) | copy-start | bytes 184324
  43.6 1.3 %collective-permute-start.15 = (bf16[8,32,128]{2,1,0:T(8,128)(2,1)S(1)}, bf16[8,32,128]{2,1,0:T(8,128)(2,1)S(1)}, u32[]{:S(2)}, u32[]{:S(2)}) collective-permute-start(bf16[8,32,128]{2,1,0:T(8,128)(2,1)S(1)} %get-tuple-element.65), channel_id=1, source_target_pairs={{0,1},{1,0},{2,3},{3,2},{4,5},{5,4},{6,7},{7,6},{8,9},{9,8},{10,11... | collective-permute-start | bytes 196616 | tf_op jit(solution)/shard_map/ppermute | solution.py:303
  45.0 7.2 %collective-permute-start.16 = (bf16[48,128]{1,0:T(8,128)(2,1)S(1)}, bf16[48,128]{1,0:T(8,128)(2,1)S(1)}, u32[]{:S(2)}, u32[]{:S(2)}) collective-permute-start(bf16[48,128]{1,0:T(8,128)(2,1)S(1)} %get-tuple-element.67), channel_id=1, source_target_pairs={{0,2},{1,3},{2,0},{3,1},{4,6},{5,7},{6,4},{7,5},{8,10},{9,11},{10,... | collective-permute-start | bytes 36872 | tf_op jit(solution)/shard_map/ppermute | solution.py:300
  46.3 8.0 %collective-permute-start.17 = (bf16[48,128]{1,0:T(8,128)(2,1)S(1)}, bf16[48,128]{1,0:T(8,128)(2,1)S(1)}, u32[]{:S(2)}, u32[]{:S(2)}) collective-permute-start(bf16[48,128]{1,0:T(8,128)(2,1)S(1)} %get-tuple-element.68), channel_id=1, source_target_pairs={{0,4},{1,5},{2,6},{3,7},{4,0},{5,1},{6,2},{7,3},{8,12},{9,13},{10,... | collective-permute-start | bytes 36872 | tf_op jit(solution)/shard_map/ppermute | solution.py:300
  46.3 9.9 %collective-permute-start.18 = (bf16[48,128]{1,0:T(8,128)(2,1)S(1)}, bf16[48,128]{1,0:T(8,128)(2,1)S(1)}, u32[]{:S(2)}, u32[]{:S(2)}) collective-permute-start(bf16[48,128]{1,0:T(8,128)(2,1)S(1)} %get-tuple-element.69), channel_id=1, source_target_pairs={{0,6},{1,7},{2,4},{3,5},{4,2},{5,3},{6,0},{7,1},{8,14},{9,15},{10,... | collective-permute-start | bytes 36872 | tf_op jit(solution)/shard_map/ppermute | solution.py:300
  48.5 7.7 %collective-permute-start.19 = (bf16[48,128]{1,0:T(8,128)(2,1)S(1)}, bf16[48,128]{1,0:T(8,128)(2,1)S(1)}, u32[]{:S(2)}, u32[]{:S(2)}) collective-permute-start(bf16[48,128]{1,0:T(8,128)(2,1)S(1)} %get-tuple-element.70), channel_id=1, source_target_pairs={{0,8},{1,9},{2,10},{3,11},{4,12},{5,13},{6,14},{7,15},{8,0},{9,1},... | collective-permute-start | bytes 36872 | tf_op jit(solution)/shard_map/ppermute | solution.py:300
  49.8 6.3 %collective-permute-start.20 = (bf16[48,128]{1,0:T(8,128)(2,1)S(1)}, bf16[48,128]{1,0:T(8,128)(2,1)S(1)}, u32[]{:S(2)}, u32[]{:S(2)}) collective-permute-start(bf16[48,128]{1,0:T(8,128)(2,1)S(1)} %get-tuple-element.71), channel_id=1, source_target_pairs={{0,10},{1,11},{2,8},{3,9},{4,14},{5,15},{6,12},{7,13},{8,2},{9,3},... | collective-permute-start | bytes 36872 | tf_op jit(solution)/shard_map/ppermute | solution.py:300
  52.1 5.5 %collective-permute-start.21 = (bf16[48,128]{1,0:T(8,128)(2,1)S(1)}, bf16[48,128]{1,0:T(8,128)(2,1)S(1)}, u32[]{:S(2)}, u32[]{:S(2)}) collective-permute-start(bf16[48,128]{1,0:T(8,128)(2,1)S(1)} %get-tuple-element.72), channel_id=1, source_target_pairs={{0,12},{1,13},{2,14},{3,15},{4,8},{5,9},{6,10},{7,11},{8,4},{9,5},... | collective-permute-start | bytes 36872 | tf_op jit(solution)/shard_map/ppermute | solution.py:300
  54.3 6.4 %collective-permute-start.22 = (bf16[48,128]{1,0:T(8,128)(2,1)S(1)}, bf16[48,128]{1,0:T(8,128)(2,1)S(1)}, u32[]{:S(2)}, u32[]{:S(2)}) collective-permute-start(bf16[48,128]{1,0:T(8,128)(2,1)S(1)} %get-tuple-element.73), channel_id=1, source_target_pairs={{0,14},{1,15},{2,12},{3,13},{4,10},{5,11},{6,8},{7,9},{8,6},{9,7},... | collective-permute-start | bytes 36872 | tf_op jit(solution)/shard_map/ppermute | solution.py:300

commit v15 on v14

--- a/solution.py
+++ b/solution.py
@@ -252,21 +252,17 @@
         give_ref[k] = send[pl.ds(at, stride - SLOT_ROWS), :].astype(jnp.bfloat16)
 
 
-def merge_kernel(me_ref, keep_ref, got_ref, *out_refs):
-    for mask, out_ref in enumerate(out_refs):
-        chip = (me_ref[0] // 2) ^ mask
-        rows = keep_ref[chip].astype(jnp.float32)
-        other = got_ref[chip].astype(jnp.float32)
-        both = jnp.maximum(rows[SLOT_ROWS:], other)
-        out_ref[...] = jnp.concatenate([rows[:SLOT_ROWS], both], axis=0).astype(jnp.bfloat16)
-
-
-def place_kernel(tiles, me_ref, *refs):
-    parts, impacts_ref, summaries_ref = refs[:-2], refs[-2], refs[-1]
-    for mask, ref in enumerate(parts):
-        chip = (me_ref[0] // 2) ^ mask
-        rows = ref[...].astype(jnp.float32)
-        lanes = pl.ds(pl.multiple_of(chip * tiles * TILE, TILE), tiles * TILE)
+def merge_kernel(keep_ref, got_ref, out_ref):
+    out_ref[:, 0:SLOT_ROWS, :] = keep_ref[:, 0:SLOT_ROWS, :]
+    mine = keep_ref[:, SLOT_ROWS:, :].astype(jnp.float32)
+    theirs = got_ref[...].astype(jnp.float32)
+    out_ref[:, SLOT_ROWS:, :] = jnp.maximum(mine, theirs).astype(jnp.bfloat16)
+
+
+def place_kernel(tiles, rows_ref, impacts_ref, summaries_ref):
+    for chip in range(rows_ref.shape[0]):
+        rows = rows_ref[chip].astype(jnp.float32)
+        lanes = slice(chip * tiles * TILE, (chip + 1) * tiles * TILE)
         lines = [
             jnp.concatenate([rows[first + t : first + t + 1] for t in range(tiles)], axis=1)
             for first in range(0, rows.shape[0], SLOT_ROWS)
@@ -455,24 +451,27 @@
         decoder_bias.reshape(-1, TILE),
         *best,
     )
-    parts = pl.pallas_call(
+    merged = pl.pallas_call(
         merge_kernel,
-        out_shape=[shape((height, TILE), jnp.bfloat16)] * chips,
-        in_specs=[smem] + [vmem] * 2,
-        out_specs=[vmem] * chips,
+        out_shape=shape((chips, height, TILE), jnp.bfloat16),
+        in_specs=[vmem] * 2,
+        out_specs=vmem,
         compiler_params=limit,
-    )(where, keep, swap(give))
-    parts = [cross(part, mask) if mask else part for mask, part in enumerate(parts)]
+    )(keep, swap(give))
+    alike = [list(range(parity, devices, 2)) for parity in range(2)]
+    got = lax.all_to_all(
+        merged, "doc", split_axis=0, concat_axis=0, axis_index_groups=alike, tiled=True
+    )
     return pl.pallas_call(
         lambda *refs: place_kernel(tiles, *refs),
         out_shape=[
             shape((1, chips * tiles * TILE), jnp.bfloat16),
             shape((BLK_DEV, chips * tiles * TILE), jnp.bfloat16),
         ],
-        in_specs=[smem] + [vmem] * chips,
+        in_specs=[vmem],
         out_specs=[vmem] * 2,
         compiler_params=limit,
-    )(where, *parts)
+    )(got)
 
 
 def tokens_move(mesh):

time: 61.7 us -> 57 us (0.924)
  starting transfers between devices: 29.5 us -> 18.3 us
  blocking collectives: 0 us -> 11 us
  waiting for transfers between devices: 18 us -> 13.5 us
    ppermute x19 -> x12, starting transfers between devices: 28.3 us -> 17.1 us  [cross(): lax.ppermute(value, 'doc', [(i, i ^ 2 * mask) for i in range(devices)])]
    all_to_all x0 -> x1, blocking collectives: none -> 11 us  [move_tokens(): lax.all_to_all(merged, 'doc', split_axis=0, concat_axis=0, axis_index_gro...]
    ppermute x19 -> x12, waiting for transfers between devices: 16.8 us -> 12.3 us  [cross(): lax.ppermute(value, 'doc', [(i, i ^ 2 * mask) for i in range(devices)])]
  transfers between devices with their start and end apart: 23 -> 16, of which waited for: 11 -> 9; matrix products, arithmetic and copies ran while one was open for 0% -> 0% of each run, Pallas kernels for 16% -> 17%
where the time goes in v15:
time: 57 us; the launch traced here: 56.8 us
  starting transfers between devices  18.3 us (32%)
  waiting for transfers between devices  13.5 us (24%)
  Pallas kernels  12.5 us (22%)
  blocking collectives  11 us (19%)
  between operations  1.41 us (2%)
    ppermute x12, starting transfers between devices, cross(): lax.ppermute(value, 'doc', [(i, i ^ 2 * mask) for i in range(devices)])  17.1 us
    ppermute x12, waiting for transfers between devices, cross(): lax.ppermute(value, 'doc', [(i, i ^ 2 * mask) for i in range(devices)])  12.3 us
    all_to_all x1, blocking collectives, move_tokens(): lax.all_to_all(merged, 'doc', split_axis=0, concat_axis=0, axis_index_gro...  11 us
    pallas_call x2, Pallas kernels, move_tokens(): pl.pallas_call(lambda *refs: next_kernel(seq, *refs), out_shape=[best_sha...  3.58 us
    pallas_call x1, Pallas kernels, move_tokens(): pl.pallas_call(lambda *refs: first_kernel(seq, block_masks, *refs), out_s...  2.86 us
    pallas_call x1, Pallas kernels, move_tokens(): pl.pallas_call(lambda *refs: last_kernel(seq, masks, *refs), out_shape=[s...  2.13 us
    pallas_call x1, Pallas kernels, move_tokens(): pl.pallas_call(start_kernel, out_shape=[shape((seq + SLOT_ROWS, width), j...  1.71 us
    pallas_call x1, Pallas kernels, move_tokens(): pl.pallas_call(lambda *refs: fetch_kernel(2, *refs), out_shape=[shape(val...  1.39 us
  transfers between devices with their start and end apart: 16, of which 9 were waited for; matrix products, arithmetic and copies ran while one was open for 0% of the time, Pallas kernels for 17%

profile of v15, /device:TPU:0, one launch (start us, length us, event | category | flops | bytes accessed | tf_op | source)
XLA Modules:
  0.0 56.8 jit_solution(4502931468249196777)
XLA Ops:
  0.6 0.5 collective-permute-start.8
  1.2 2.6 %collective-permute-start.4 = (bf16[128,768]{1,0:T(8,128)(2,1)}, bf16[128,768]{1,0:T(8,128)(2,1)S(1)}, u32[]{:S(2)}, u32[]{:S(2)}) collective-permute-start(bf16[128,768]{1,0:T(8,128)(2,1)} %refs_0_.1), channel_id=1, source_target_pairs={{0,2},{1,3},{2,0},{3,1},{4,6},{5,7},{6,4},{7,5},{8,10},{9,11},{10,... | collective-permute-start | bytes 589832 | tf_op jit(solution)/shard_map/ppermute | solution.py:296
  3.7 3.6 %collective-permute-start = (bf16[48,768]{1,0:T(8,128)(2,1)}, bf16[48,768]{1,0:T(8,128)(2,1)S(1)}, u32[]{:S(2)}, u32[]{:S(2)}) collective-permute-start(bf16[48,768]{1,0:T(8,128)(2,1)} %refs_1_.1), channel_id=1, source_target_pairs={{0,12},{1,13},{2,14},{3,15},{4,8},{5,9},{6,10},{7,11},{8,4},{9,5},... | collective-permute-start | bytes 221192 | tf_op jit(solution)/shard_map/ppermute | solution.py:296
  7.3 0.0 collective-permute-start.3
  8.0 1.7 %shard_map.122 = (bf16[144,768]{1,0:T(8,128)(2,1)S(1)}, bf16[48,768]{1,0:T(8,128)(2,1)S(1)}, bf16[16,768]{1,0:T(8,128)(2,1)S(1)}, f32[8,768]{1,0:T(8,128)S(1)}) custom-call(s32[1,1,32]{2,1,0:T(1,128)} %tiles_ref.1, s32[1,1,32]{2,1,0:T(1,128)} %bitcast.9, s32[1,1,32]{2,1,0:T(1,128)} %slots_ref.1, s32[1]{0:T(128)S(6)} %copy.13.length_ref, ...), custom_call_target="tpu_custom_call" | custom-call | tf_op jit(solution)/shard_map/pallas_call | solution.py:335
  9.7 1.1 %collective-permute-done.refs_0_.refs_2_ = bf16[48,768]{1,0:T(8,128)(2,1)S(1)} collective-permute-done((bf16[48,768]{1,0:T(8,128)(2,1)}, bf16[48,768]{1,0:T(8,128)(2,1)S(1)}, u32[]{:S(2)}, u32[]{:S(2)}) %collective-permute-start) | collective-permute-done | bytes 73760 | tf_op jit(solution)/shard_map/ppermute | solution.py:296
  10.8 1.2 %collective-permute-done.3.refs_1_ = bf16[48,768]{1,0:T(8,128)(2,1)S(1)} collective-permute-done((bf16[48,768]{1,0:T(8,128)(2,1)}, bf16[48,768]{1,0:T(8,128)(2,1)S(1)}, u32[]{:S(2)}, u32[]{:S(2)}) %collective-permute-start.3) | collective-permute-done | bytes 73760 | tf_op jit(solution)/shard_map/ppermute | solution.py:296
  12.0 0.0 collective-permute-done.4.refs_2_.refs_0_
  12.0 0.0 copy-start
  12.0 0.5 collective-permute-start.5
  12.5 1.6 %collective-permute-start.2 = (bf16[48,768]{1,0:T(8,128)(2,1)S(1)}, bf16[48,768]{1,0:T(8,128)(2,1)S(1)}, u32[]{:S(2)}, u32[]{:S(2)}) collective-permute-start(bf16[48,768]{1,0:T(8,128)(2,1)S(1)} %collective-permute-done.refs_0_.refs_2_), channel_id=1, source_target_pairs={{0,4},{1,5},{2,6},{3,7},{4,0},{5,1},{6,2},{7,3},{8,12},{9,13},{10,... | collective-permute-start | bytes 221192 | tf_op jit(solution)/shard_map/ppermute | solution.py:296
  14.1 1.2 %collective-permute-start.1 = (bf16[144,768]{1,0:T(8,128)(2,1)S(1)}, bf16[144,768]{1,0:T(8,128)(2,1)S(1)}, u32[]{:S(2)}, u32[]{:S(2)}) collective-permute-start(bf16[144,768]{1,0:T(8,128)(2,1)S(1)} %get-tuple-element.36.refs_1_.refs_3_), channel_id=1, source_target_pairs={{0,12},{1,13},{2,14},{3,15},{4,8},{5,9},{6,10},{7,11},{8,4},{9,5},... | collective-permute-start | bytes 663560 | tf_op jit(solution)/shard_map/ppermute | solution.py:296
  15.3 1.6 %collective-permute-done.2.refs_1_.refs_3_ = bf16[48,768]{1,0:T(8,128)(2,1)S(1)} collective-permute-done((bf16[48,768]{1,0:T(8,128)(2,1)S(1)}, bf16[48,768]{1,0:T(8,128)(2,1)S(1)}, u32[]{:S(2)}, u32[]{:S(2)}) %collective-permute-start.2) | collective-permute-done | bytes 73760 | tf_op jit(solution)/shard_map/ppermute | solution.py:296
  16.9 0.9 %collective-permute-done.5.refs_4_.refs_1_ = bf16[112,768]{1,0:T(8,128)(2,1)S(1)} collective-permute-done((bf16[112,768]{1,0:T(8,128)(2,1)S(1)}, bf16[112,768]{1,0:T(8,128)(2,1)S(1)}, u32[]{:S(2)}, u32[]{:S(2)}) %collective-permute-start.5) | collective-permute-done | bytes 172064 | tf_op jit(solution)/shard_map/ppermute | solution.py:296
  17.8 0.7 %collective-permute-start.9 = (bf16[96,768]{1,0:T(8,128)(2,1)S(1)}, bf16[96,768]{1,0:T(8,128)(2,1)S(1)}, u32[]{:S(2)}, u32[]{:S(2)}) collective-permute-start(bf16[96,768]{1,0:T(8,128)(2,1)S(1)} %shard_map.124), channel_id=1, source_target_pairs={{0,2},{1,3},{2,0},{3,1},{4,6},{5,7},{6,4},{7,5},{8,10},{9,11},{10,... | collective-permute-start | bytes 442376 | tf_op jit(solution)/shard_map/ppermute | solution.py:296
  18.6 2.3 %collective-permute-start.6 = (bf16[144,768]{1,0:T(8,128)(2,1)S(1)}, bf16[144,768]{1,0:T(8,128)(2,1)S(1)}, u32[]{:S(2)}, u32[]{:S(2)}) collective-permute-start(bf16[144,768]{1,0:T(8,128)(2,1)S(1)} %get-tuple-element.36.refs_1_.refs_3_), channel_id=1, source_target_pairs={{0,4},{1,5},{2,6},{3,7},{4,0},{5,1},{6,2},{7,3},{8,12},{9,13},{10,... | collective-permute-start | bytes 663560 | tf_op jit(solution)/shard_map/ppermute | solution.py:296
  20.9 3.4 %collective-permute-done.1.refs_0_.refs_2_.refs_5_ = bf16[144,768]{1,0:T(8,128)(2,1)S(1)} collective-permute-done((bf16[144,768]{1,0:T(8,128)(2,1)S(1)}, bf16[144,768]{1,0:T(8,128)(2,1)S(1)}, u32[]{:S(2)}, u32[]{:S(2)}) %collective-permute-start.1) | collective-permute-done | bytes 221216 | tf_op jit(solution)/shard_map/ppermute | solution.py:296
  24.2 0.0 collective-permute-done.8.refs_11_.refs_7_.refs_14_
  24.2 0.0 collective-permute-done.9.refs_5_
  24.3 0.1 collective-permute-start.10
  24.4 0.5 collective-permute-start.11
  24.9 2.3 %collective-permute-done.6.refs_0_.refs_2_.refs_7_ = bf16[144,768]{1,0:T(8,128)(2,1)S(1)} collective-permute-done((bf16[144,768]{1,0:T(8,128)(2,1)S(1)}, bf16[144,768]{1,0:T(8,128)(2,1)S(1)}, u32[]{:S(2)}, u32[]{:S(2)}) %collective-permute-start.6) | collective-permute-done | bytes 221216 | tf_op jit(solution)/shard_map/ppermute | solution.py:296
  27.2 0.1 collective-permute-start.7
  27.3 1.2 %collective-permute-start.13 = (bf16[144,768]{1,0:T(8,128)(2,1)S(1)}, bf16[144,768]{1,0:T(8,128)(2,1)S(1)}, u32[]{:S(2)}, u32[]{:S(2)}) collective-permute-start(bf16[144,768]{1,0:T(8,128)(2,1)S(1)} %collective-permute-done.1.refs_0_.refs_2_.refs_5_), channel_id=1, source_target_pairs={{0,2},{1,3},{2,0},{3,1},{4,6},{5,7},{6,4},{7,5},{8,10},{9,11},{10,... | collective-permute-start | bytes 663560 | tf_op jit(solution)/shard_map/ppermute | solution.py:296
  28.5 2.1 %collective-permute-start.14 = (bf16[144,768]{1,0:T(8,128)(2,1)S(1)}, bf16[144,768]{1,0:T(8,128)(2,1)S(1)}, u32[]{:S(2)}, u32[]{:S(2)}) collective-permute-start(bf16[144,768]{1,0:T(8,128)(2,1)S(1)} %shard_map.128), channel_id=1, source_target_pairs={{0,4},{1,5},{2,6},{3,7},{4,0},{5,1},{6,2},{7,3},{8,12},{9,13},{10,... | collective-permute-start | bytes 663560 | tf_op jit(solution)/shard_map/ppermute | solution.py:296
  30.5 0.0 copy-done
  30.5 1.4 %shard_map.126 = (bf16[960,768]{1,0:T(8,128)(2,1)S(1)}, bf16[128,768]{1,0:T(8,128)(2,1)S(1)}) custom-call(bf16[192,768]{1,0:T(8,128)(2,1)S(1)} %get-tuple-element.39.refs_0_.refs_5_, bf16[960,768]{1,0:T(8,128)(2,1)} %bitcast.8, bf16[128,768]{1,0:T(8,128)(2,1)} %copy-done), custom_call_target="tpu_custom_call" | custom-call | tf_op jit(solution)/shard_map/pallas_call | solution.py:381
  31.9 0.0 collective-permute-done.10.refs_7_
  32.0 0.0 collective-permute-done.11.refs_8_
  32.0 2.9 %shard_map.127 = (f32[8,960]{1,0:T(8,128)S(1)}, f32[8,960]{1,0:T(8,128)S(1)}, bf16[768,768]{1,0:T(8,128)(2,1)S(1)}) custom-call(s32[1]{0:T(128)} %bitcast.refs_0_, bf16[144,768]{1,0:T(8,128)(2,1)S(1)} %get-tuple-element.36.refs_1_.refs_3_, bf16[128,768]{1,0:T(8,128)(2,1)S(1)} %get-tuple-element.42.refs_2_, ...), custom_call_target="tpu_custom_call" | custom-call | flops 2 | bytes 2 | tf_op jit(solution)/shard_map/pallas_call | solution.py:393
  34.8 0.7 %collective-permute-done.7.refs_1_.refs_9_ = bf16[144,768]{1,0:T(8,128)(2,1)S(1)} collective-permute-done((bf16[144,768]{1,0:T(8,128)(2,1)S(1)}, bf16[144,768]{1,0:T(8,128)(2,1)S(1)}, u32[]{:S(2)}, u32[]{:S(2)}) %collective-permute-start.7) | collective-permute-done | bytes 221216 | tf_op jit(solution)/shard_map/ppermute | solution.py:296
  35.5 1.3 %collective-permute-start.12 = (bf16[144,768]{1,0:T(8,128)(2,1)S(1)}, bf16[144,768]{1,0:T(8,128)(2,1)S(1)}, u32[]{:S(2)}, u32[]{:S(2)}) collective-permute-start(bf16[144,768]{1,0:T(8,128)(2,1)S(1)} %collective-permute-done.7.refs_1_.refs_9_), channel_id=1, source_target_pairs={{0,2},{1,3},{2,0},{3,1},{4,6},{5,7},{6,4},{7,5},{8,10},{9,11},{10,... | collective-permute-start | bytes 663560 | tf_op jit(solution)/shard_map/ppermute | solution.py:296
  36.8 0.0 collective-permute-done.13.refs_1_.refs_3_.refs_6_
  36.8 1.8 %shard_map.129 = (f32[8,960]{1,0:T(8,128)S(1)}, f32[8,960]{1,0:T(8,128)S(1)}) custom-call(bf16[144,768]{1,0:T(8,128)(2,1)S(1)} %collective-permute-done.1.refs_0_.refs_2_.refs_5_, bf16[144,768]{1,0:T(8,128)(2,1)S(1)} %collective-permute-done.13.refs_1_.refs_3_.refs_6_, bf16[144,768]{1,0:T(8,128)(2,1)S(1)} %collective-permute-done.1.refs_0_.refs_2_.refs_5_, ...), custom_call_target="tpu_custom_call" | custom-call | flops 2 | bytes 2 | tf_op jit(solution)/shard_map/pallas_call | solution.py:416
  38.6 0.0 copy-start.1
  38.6 0.0 collective-permute-done.14.refs_1_.refs_3_.refs_8_
  38.6 1.8 %shard_map.130 = (f32[8,960]{1,0:T(8,128)S(1)}, f32[8,960]{1,0:T(8,128)S(1)}) custom-call(bf16[144,768]{1,0:T(8,128)(2,1)S(1)} %collective-permute-done.6.refs_0_.refs_2_.refs_7_, bf16[144,768]{1,0:T(8,128)(2,1)S(1)} %collective-permute-done.14.refs_1_.refs_3_.refs_8_, bf16[144,768]{1,0:T(8,128)(2,1)S(1)} %collective-permute-done.6.refs_0_.refs_2_.refs_7_, ...), custom_call_target="tpu_custom_call" | custom-call | flops 2 | bytes 2 | tf_op jit(solution)/shard_map/pallas_call | solution.py:416
  40.4 1.1 %collective-permute-done.12.refs_2_.refs_10_ = bf16[144,768]{1,0:T(8,128)(2,1)S(1)} collective-permute-done((bf16[144,768]{1,0:T(8,128)(2,1)S(1)}, bf16[144,768]{1,0:T(8,128)(2,1)S(1)}, u32[]{:S(2)}, u32[]{:S(2)}) %collective-permute-start.12) | collective-permute-done | bytes 221216 | tf_op jit(solution)/shard_map/ppermute | solution.py:296
  41.5 0.0 copy-done.1
  41.5 2.1 %shard_map.131 = (bf16[8,48,128]{2,1,0:T(8,128)(2,1)S(1)}, bf16[8,32,128]{2,1,0:T(8,128)(2,1)S(1)}) custom-call(s32[1]{0:T(128)} %bitcast.refs_0_, bf16[144,768]{1,0:T(8,128)(2,1)S(1)} %collective-permute-done.7.refs_1_.refs_9_, bf16[144,768]{1,0:T(8,128)(2,1)S(1)} %collective-permute-done.12.refs_2_.refs_10_, ...), custom_call_target="tpu_custom_call" | custom-call | flops 2 | bytes 2 | tf_op jit(solution)/shard_map/pallas_call | solution.py:432
  43.6 0.1 collective-permute-start.15
  43.7 1.2 %collective-permute-done.15.got_ref = bf16[8,32,128]{2,1,0:T(8,128)(2,1)S(1)} collective-permute-done((bf16[8,32,128]{2,1,0:T(8,128)(2,1)S(1)}, bf16[8,32,128]{2,1,0:T(8,128)(2,1)S(1)}, u32[]{:S(2)}, u32[]{:S(2)}) %collective-permute-start.15) | collective-permute-done | bytes 65568 | tf_op jit(solution)/shard_map/ppermute | solution.py:299
  45.0 11.0 %all_to_all.5.refs_0_ = bf16[8,48,128]{2,1,0:T(8,128)(2,1)S(1)} all-to-all(bf16[8,48,128]{2,1,0:T(8,128)(2,1)S(1)} %shard_map.132), channel_id=1, replica_groups={{0,2,4,6,8,10,12,14},{1,3,5,7,9,11,13,15},{16,18,20,22,24,26,28,30},{17..., dimensions={0} | all-to-all | bytes 196608 | tf_op jit(solution)/shard_map/all_to_all | solution.py:462
  56.0 0.8 %shard_map.133 = (bf16[1,15360]{1,0:T(2,128)(2,1)}, bf16[2,15360]{1,0:T(2,128)(2,1)}) custom-call(bf16[8,48,128]{2,1,0:T(8,128)(2,1)S(1)} %all_to_all.5.refs_0_), custom_call_target="tpu_custom_call" | custom-call | tf_op jit(solution)/shard_map/pallas_call | solution.py:465
  (5 shorter events, 0.1 us)
Async XLA Ops:
  0.6 23.6 %collective-permute-start.8 = (bf16[960,768]{1,0:T(8,128)(2,1)}, bf16[960,768]{1,0:T(8,128)(2,1)S(1)}, u32[]{:S(2)}, u32[]{:S(2)}) collective-permute-start(bf16[960,768]{1,0:T(8,128)(2,1)} %bitcast.7), channel_id=1, source_target_pairs={{0,1},{1,0},{2,3},{3,2},{4,5},{5,4},{6,7},{7,6},{8,9},{9,8},{10,11... | collective-permute-start | bytes 4423688 | tf_op jit(solution)/shard_map/ppermute | solution.py:299
  1.2 10.9 %collective-permute-start.4 = (bf16[128,768]{1,0:T(8,128)(2,1)}, bf16[128,768]{1,0:T(8,128)(2,1)S(1)}, u32[]{:S(2)}, u32[]{:S(2)}) collective-permute-start(bf16[128,768]{1,0:T(8,128)(2,1)} %refs_0_.1), channel_id=1, source_target_pairs={{0,2},{1,3},{2,0},{3,1},{4,6},{5,7},{6,4},{7,5},{8,10},{9,11},{10,... | collective-permute-start | bytes 589832 | tf_op jit(solution)/shard_map/ppermute | solution.py:296
  3.7 7.1 %collective-permute-start = (bf16[48,768]{1,0:T(8,128)(2,1)}, bf16[48,768]{1,0:T(8,128)(2,1)S(1)}, u32[]{:S(2)}, u32[]{:S(2)}) collective-permute-start(bf16[48,768]{1,0:T(8,128)(2,1)} %refs_1_.1), channel_id=1, source_target_pairs={{0,12},{1,13},{2,14},{3,15},{4,8},{5,9},{6,10},{7,11},{8,4},{9,5},... | collective-permute-start | bytes 221192 | tf_op jit(solution)/shard_map/ppermute | solution.py:296
  7.3 4.7 %collective-permute-start.3 = (bf16[48,768]{1,0:T(8,128)(2,1)}, bf16[48,768]{1,0:T(8,128)(2,1)S(1)}, u32[]{:S(2)}, u32[]{:S(2)}) collective-permute-start(bf16[48,768]{1,0:T(8,128)(2,1)} %refs_1_.1), channel_id=1, source_target_pairs={{0,4},{1,5},{2,6},{3,7},{4,0},{5,1},{6,2},{7,3},{8,12},{9,13},{10,... | collective-permute-start | bytes 221192 | tf_op jit(solution)/shard_map/ppermute | solution.py:296
  12.0 18.5 %copy-start = (bf16[128,768]{1,0:T(8,128)(2,1)}, bf16[128,768]{1,0:T(8,128)(2,1)S(1)}, u32[]{:S(2)}) copy-start(bf16[128,768]{1,0:T(8,128)(2,1)S(1)} %collective-permute-done.4.refs_2_.refs_0_) | copy-start | bytes 589828
  12.0 5.8 %collective-permute-start.5 = (bf16[112,768]{1,0:T(8,128)(2,1)S(1)}, bf16[112,768]{1,0:T(8,128)(2,1)S(1)}, u32[]{:S(2)}, u32[]{:S(2)}) collective-permute-start(bf16[112,768]{1,0:T(8,128)(2,1)S(1)} %shard_map.123), channel_id=1, source_target_pairs={{0,2},{1,3},{2,0},{3,1},{4,6},{5,7},{6,4},{7,5},{8,10},{9,11},{10,... | collective-permute-start | bytes 516104 | tf_op jit(solution)/shard_map/ppermute | solution.py:296
  12.5 4.4 %collective-permute-start.2 = (bf16[48,768]{1,0:T(8,128)(2,1)S(1)}, bf16[48,768]{1,0:T(8,128)(2,1)S(1)}, u32[]{:S(2)}, u32[]{:S(2)}) collective-permute-start(bf16[48,768]{1,0:T(8,128)(2,1)S(1)} %collective-permute-done.refs_0_.refs_2_), channel_id=1, source_target_pairs={{0,4},{1,5},{2,6},{3,7},{4,0},{5,1},{6,2},{7,3},{8,12},{9,13},{10,... | collective-permute-start | bytes 221192 | tf_op jit(solution)/shard_map/ppermute | solution.py:296
  14.1 10.2 %collective-permute-start.1 = (bf16[144,768]{1,0:T(8,128)(2,1)S(1)}, bf16[144,768]{1,0:T(8,128)(2,1)S(1)}, u32[]{:S(2)}, u32[]{:S(2)}) collective-permute-start(bf16[144,768]{1,0:T(8,128)(2,1)S(1)} %get-tuple-element.36.refs_1_.refs_3_), channel_id=1, source_target_pairs={{0,12},{1,13},{2,14},{3,15},{4,8},{5,9},{6,10},{7,11},{8,4},{9,5},... | collective-permute-start | bytes 663560 | tf_op jit(solution)/shard_map/ppermute | solution.py:296
  17.8 6.4 %collective-permute-start.9 = (bf16[96,768]{1,0:T(8,128)(2,1)S(1)}, bf16[96,768]{1,0:T(8,128)(2,1)S(1)}, u32[]{:S(2)}, u32[]{:S(2)}) collective-permute-start(bf16[96,768]{1,0:T(8,128)(2,1)S(1)} %shard_map.124), channel_id=1, source_target_pairs={{0,2},{1,3},{2,0},{3,1},{4,6},{5,7},{6,4},{7,5},{8,10},{9,11},{10,... | collective-permute-start | bytes 442376 | tf_op jit(solution)/shard_map/ppermute | solution.py:296
  18.6 8.6 %collective-permute-start.6 = (bf16[144,768]{1,0:T(8,128)(2,1)S(1)}, bf16[144,768]{1,0:T(8,128)(2,1)S(1)}, u32[]{:S(2)}, u32[]{:S(2)}) collective-permute-start(bf16[144,768]{1,0:T(8,128)(2,1)S(1)} %get-tuple-element.36.refs_1_.refs_3_), channel_id=1, source_target_pairs={{0,4},{1,5},{2,6},{3,7},{4,0},{5,1},{6,2},{7,3},{8,12},{9,13},{10,... | collective-permute-start | bytes 663560 | tf_op jit(solution)/shard_map/ppermute | solution.py:296
  24.3 7.7 %collective-permute-start.10 = (bf16[192,768]{1,0:T(8,128)(2,1)S(1)}, bf16[192,768]{1,0:T(8,128)(2,1)}, u32[]{:S(2)}, u32[]{:S(2)}) collective-permute-start(bf16[192,768]{1,0:T(8,128)(2,1)S(1)} %get-tuple-element.39.refs_0_.refs_5_), channel_id=1, source_target_pairs={{0,1},{1,0},{2,3},{3,2},{4,5},{5,4},{6,7},{7,6},{8,9},{9,8},{10,11... | collective-permute-start | bytes 884744 | tf_op jit(solution)/shard_map/ppermute | solution.py:299
  24.4 7.6 %collective-permute-start.11 = (bf16[192,768]{1,0:T(8,128)(2,1)S(1)}, bf16[192,768]{1,0:T(8,128)(2,1)}, u32[]{:S(2)}, u32[]{:S(2)}) collective-permute-start(bf16[192,768]{1,0:T(8,128)(2,1)S(1)} %get-tuple-element.40.refs_6_), channel_id=1, source_target_pairs={{0,1},{1,0},{2,3},{3,2},{4,5},{5,4},{6,7},{7,6},{8,9},{9,8},{10,11... | collective-permute-start | bytes 884744 | tf_op jit(solution)/shard_map/ppermute | solution.py:299
  27.2 8.4 %collective-permute-start.7 = (bf16[144,768]{1,0:T(8,128)(2,1)S(1)}, bf16[144,768]{1,0:T(8,128)(2,1)S(1)}, u32[]{:S(2)}, u32[]{:S(2)}) collective-permute-start(bf16[144,768]{1,0:T(8,128)(2,1)S(1)} %collective-permute-done.1.refs_0_.refs_2_.refs_5_), channel_id=1, source_target_pairs={{0,4},{1,5},{2,6},{3,7},{4,0},{5,1},{6,2},{7,3},{8,12},{9,13},{10,... | collective-permute-start | bytes 663560 | tf_op jit(solution)/shard_map/ppermute | solution.py:296
  27.3 9.5 %collective-permute-start.13 = (bf16[144,768]{1,0:T(8,128)(2,1)S(1)}, bf16[144,768]{1,0:T(8,128)(2,1)S(1)}, u32[]{:S(2)}, u32[]{:S(2)}) collective-permute-start(bf16[144,768]{1,0:T(8,128)(2,1)S(1)} %collective-permute-done.1.refs_0_.refs_2_.refs_5_), channel_id=1, source_target_pairs={{0,2},{1,3},{2,0},{3,1},{4,6},{5,7},{6,4},{7,5},{8,10},{9,11},{10,... | collective-permute-start | bytes 663560 | tf_op jit(solution)/shard_map/ppermute | solution.py:296
  28.5 10.2 %collective-permute-start.14 = (bf16[144,768]{1,0:T(8,128)(2,1)S(1)}, bf16[144,768]{1,0:T(8,128)(2,1)S(1)}, u32[]{:S(2)}, u32[]{:S(2)}) collective-permute-start(bf16[144,768]{1,0:T(8,128)(2,1)S(1)} %shard_map.128), channel_id=1, source_target_pairs={{0,4},{1,5},{2,6},{3,7},{4,0},{5,1},{6,2},{7,3},{8,12},{9,13},{10,... | collective-permute-start | bytes 663560 | tf_op jit(solution)/shard_map/ppermute | solution.py:296
  35.5 5.9 %collective-permute-start.12 = (bf16[144,768]{1,0:T(8,128)(2,1)S(1)}, bf16[144,768]{1,0:T(8,128)(2,1)S(1)}, u32[]{:S(2)}, u32[]{:S(2)}) collective-permute-start(bf16[144,768]{1,0:T(8,128)(2,1)S(1)} %collective-permute-done.7.refs_1_.refs_9_), channel_id=1, source_target_pairs={{0,2},{1,3},{2,0},{3,1},{4,6},{5,7},{6,4},{7,5},{8,10},{9,11},{10,... | collective-permute-start | bytes 663560 | tf_op jit(solution)/shard_map/ppermute | solution.py:296
  38.6 2.9 %copy-start.1 = (f32[15360]{0:T(1024)S(1)}, f32[15360]{0:T(1024)}, u32[]{:S(2)}) copy-start(f32[15360]{0:T(1024)} %param.18) | copy-start | bytes 184324
  43.6 1.3 %collective-permute-start.15 = (bf16[8,32,128]{2,1,0:T(8,128)(2,1)S(1)}, bf16[8,32,128]{2,1,0:T(8,128)(2,1)S(1)}, u32[]{:S(2)}, u32[]{:S(2)}) collective-permute-start(bf16[8,32,128]{2,1,0:T(8,128)(2,1)S(1)} %get-tuple-element.57), channel_id=1, source_target_pairs={{0,1},{1,0},{2,3},{3,2},{4,5},{5,4},{6,7},{7,6},{8,9},{9,8},{10,11... | collective-permute-start | bytes 196616 | tf_op jit(solution)/shard_map/ppermute | solution.py:299

commit v16 on v15

--- a/solution.py
+++ b/solution.py
@@ -186,7 +186,9 @@
 
 def first_kernel(seq, masks, *refs):
     me_ref, docs, tables, refs = refs[0], refs[1:3], refs[3:5], refs[5:]
-    parts, others, params, halves, refs = refs[:2], refs[2:4], refs[4], refs[5:7], refs[7:]
+    count = len(masks) // 2
+    parts, others, refs = refs[:count], refs[count : 2 * count], refs[2 * count :]
+    params, halves, refs = refs[0], refs[1:3], refs[3:]
     bests, weight = refs[:2], refs[2]
     me = me_ref[0]
     core = me % 2
@@ -331,7 +333,7 @@
     block_6 = cross(transform_weight, 6)
     block_2 = cross(transform_weight, 2)
     theirs = swap(weight_rows)
-    docs = {1: cross(hidden_states, 1)}
+    docs = {1: cross(hidden_states, 1), 2: cross(hidden_states, 2)}
     load, block, table, params = pl.pallas_call(
         start_kernel,
         out_shape=[
@@ -361,23 +363,11 @@
     near = (block, after(block_2, block_6, docs[1]), table)
     near_pile = cross(pile(near, ((0, rows), (0, rows), (0, SLOT_ROWS))), 1)
     one, two = (0, rows), (0, 2 * rows)
-    block_4 = cross(block_6, 2)
+    one, two, below = (0, rows), (0, 2 * rows), (0, SLOT_ROWS)
+    block_4 = cross(pile((block_6, table), (one, below)), 2)
     docs[6] = cross(after(load, block_6), 6)
-    docs[2] = cross(after(load, block_4), 2)
     load_1 = pile((docs[1], near_pile), ((0, seq), (2 * rows, SLOT_ROWS)))
-    far = (block_6, after(block_4, near_pile))
-    far = pile(far, ((0, rows), (0, rows)))
-    far_pile = cross(far, 1)
-    docs[3] = cross(after(load_1, far), 2)
-    docs[4] = cross(after(docs[6], far, docs[2]), 2)
-    docs[7] = cross(docs[6], 1)
-    late = (docs[6], theirs)
-    sources = (after(block, *late), block_2, block_6, block_4, near_pile, far_pile)
-    packed = pile(sources, (one, one, one, one, two, two), (chips // 2 * rows,) * 2)
-    other_packed = [swap(part) for part in packed]
-    block_masks = [0, 2, 6, 4, 1, 3, 7, 5]
-
-    far_from = [stay(after(weight_rows, *packed)), stay(docs[1])]
+    far_from = [stay(after(weight_rows, table)), stay(docs[1])]
     mine, beside = pl.pallas_call(
         lambda *refs: fetch_kernel(2, *refs),
         out_shape=[shape(value.shape, value.dtype) for value in far_from],
@@ -385,15 +375,26 @@
         out_specs=[vmem] * 2,
         scratch_shapes=[pltpu.SemaphoreType.DMA((2,))],
         compiler_params=limit,
-    )(packed[0], *far_from)
-
-    masks = [0, 1, 6, 7, 2, 3, 4, 5]
+    )(table, *far_from)
+    far = (block_6, after(block_4, near_pile, docs[2], mine, theirs))
+    far = pile(far, (one, one))
+    far_pile = cross(far, 1)
+    docs[3] = cross(after(load_1, far), 2)
+    docs[4] = cross(after(docs[6], far), 2)
+    docs[7] = cross(docs[6], 1)
+    late = (docs[6], docs[3])
+    sources = (after(block, *late), block_2, block_6, block_4, near_pile, far_pile)
+    packed = pile(sources, (one, one, one, one, two, two), (2 * rows,) * (chips // 2))
+    other_packed = [swap(part) for part in packed]
+    block_masks = [0, 2, 6, 4, 1, 3, 7, 5]
+
+    masks = [0, 1, 2, 3, 6, 7, 4, 5]
     where = me[None]
     best_shape = shape((8, half), jnp.float32)
     *best, weight = pl.pallas_call(
         lambda *refs: first_kernel(seq, block_masks, *refs),
         out_shape=[best_shape, best_shape, shape((width, width), jnp.bfloat16)],
-        in_specs=[smem] + [vmem] * 11,
+        in_specs=[smem] + [vmem] * (7 + 2 * len(packed)),
         out_specs=[vmem] * 3,
         compiler_params=limit,
         cost_estimate=cost(2),
@@ -410,7 +411,7 @@
         theirs,
     )
     docs |= {0: load, 1: beside, 5: cross(after(docs[4], weight), 1)}
-    tables = docs | {1: near_pile}
+    tables = docs | {1: near_pile, 2: block_4}
     for first in range(2, len(masks) - 2, 2):
         pair = masks[first : first + 2]
         best += pl.pallas_call(

time: 57 us -> 62.8 us (1.10)
  local copies, waits for them, and re-layouts: 0.01 us -> 4.18 us
  Pallas kernels: 12.5 us -> 14.7 us
  starting transfers between devices: 18.3 us -> 16.1 us
  waiting for transfers between devices: 13.5 us -> 15.6 us
    unnamed x4 -> x24, local copies, waits for them, and re-layouts: 0.01 us -> 4.18 us
    ppermute x12, starting transfers between devices: 17.1 us -> 14.5 us  [cross(): lax.ppermute(value, 'doc', [(i, i ^ 2 * mask) for i in range(devices)])]
    ppermute x12, waiting for transfers between devices: 12.3 us -> 13.7 us  [cross(): lax.ppermute(value, 'doc', [(i, i ^ 2 * mask) for i in range(devices)])]
    pallas_call x1, Pallas kernels: 2.13 us -> 3.13 us  [move_tokens(): pl.pallas_call(lambda *refs: last_kernel(seq, masks, *refs), out_shape=[s...]
    pallas_call x4 -> x5, Pallas kernels: 0.08 us -> 0.91 us  [pile(): pl.pallas_call(lambda *refs: pile_kernel(parts, heights, *refs), out_shap...]
    ppermute x4 -> x6, waiting for transfers between devices: 1.25 us -> 1.94 us  [swap(): return lax.ppermute(value, 'doc', [(i, i ^ 1) for i in range(devices)])]
    ppermute x4 -> x6, starting transfers between devices: 1.16 us -> 1.61 us  [swap(): return lax.ppermute(value, 'doc', [(i, i ^ 1) for i in range(devices)])]
  transfers between devices with their start and end apart: 16 -> 18, of which waited for: 9 -> 8; matrix products, arithmetic and copies ran while one was open for 0% -> 0% of each run, Pallas kernels for 17% -> 17%
where the time goes in v16:
time: 62.8 us; the launch traced here: 62.5 us
  starting transfers between devices  16.1 us (26%)
  waiting for transfers between devices  15.6 us (25%)
  Pallas kernels  14.7 us (23%)
  blocking collectives  10.4 us (17%)
  local copies, waits for them, and re-layouts  4.18 us (7%)
  between operations  1.46 us (2%)
    ppermute x12, starting transfers between devices, cross(): lax.ppermute(value, 'doc', [(i, i ^ 2 * mask) for i in range(devices)])  14.5 us
    ppermute x12, waiting for transfers between devices, cross(): lax.ppermute(value, 'doc', [(i, i ^ 2 * mask) for i in range(devices)])  13.7 us
    all_to_all x1, blocking collectives, move_tokens(): lax.all_to_all(merged, 'doc', split_axis=0, concat_axis=0, axis_index_gro...  10.4 us
    unnamed x24, local copies, waits for them, and re-layouts  4.18 us
    pallas_call x2, Pallas kernels, move_tokens(): pl.pallas_call(lambda *refs: next_kernel(seq, *refs), out_shape=[best_sha...  3.55 us
    pallas_call x1, Pallas kernels, move_tokens(): pl.pallas_call(lambda *refs: first_kernel(seq, block_masks, *refs), out_s...  3.17 us
    pallas_call x1, Pallas kernels, move_tokens(): pl.pallas_call(lambda *refs: last_kernel(seq, masks, *refs), out_shape=[s...  3.13 us
    ppermute x6, waiting for transfers between devices, swap(): return lax.ppermute(value, 'doc', [(i, i ^ 1) for i in range(devices)])  1.94 us
  transfers between devices with their start and end apart: 18, of which 8 were waited for; matrix products, arithmetic and copies ran while one was open for 0% of the time, Pallas kernels for 17%

profile of v16, /device:TPU:0, one launch (start us, length us, event | category | flops | bytes accessed | tf_op | source)
XLA Modules:
  0.0 62.5 jit_solution(752816955611503590)
XLA Ops:
  0.6 0.5 collective-permute-start.7
  1.2 2.6 %collective-permute-start.4 = (bf16[128,768]{1,0:T(8,128)(2,1)}, bf16[128,768]{1,0:T(8,128)(2,1)S(1)}, u32[]{:S(2)}, u32[]{:S(2)}) collective-permute-start(bf16[128,768]{1,0:T(8,128)(2,1)} %refs_0_.1), channel_id=1, source_target_pairs={{0,2},{1,3},{2,0},{3,1},{4,6},{5,7},{6,4},{7,5},{8,10},{9,11},{10,... | collective-permute-start | bytes 589832 | tf_op jit(solution)/shard_map/ppermute | solution.py:298
  3.7 3.6 %collective-permute-start = (bf16[48,768]{1,0:T(8,128)(2,1)}, bf16[48,768]{1,0:T(8,128)(2,1)S(1)}, u32[]{:S(2)}, u32[]{:S(2)}) collective-permute-start(bf16[48,768]{1,0:T(8,128)(2,1)} %refs_1_.1), channel_id=1, source_target_pairs={{0,12},{1,13},{2,14},{3,15},{4,8},{5,9},{6,10},{7,11},{8,4},{9,5},... | collective-permute-start | bytes 221192 | tf_op jit(solution)/shard_map/ppermute | solution.py:298
  7.3 0.0 collective-permute-start.3
  7.3 2.0 %collective-permute-start.6 = (bf16[128,768]{1,0:T(8,128)(2,1)}, bf16[128,768]{1,0:T(8,128)(2,1)S(1)}, u32[]{:S(2)}, u32[]{:S(2)}) collective-permute-start(bf16[128,768]{1,0:T(8,128)(2,1)} %refs_0_.1), channel_id=1, source_target_pairs={{0,4},{1,5},{2,6},{3,7},{4,0},{5,1},{6,2},{7,3},{8,12},{9,13},{10,... | collective-permute-start | bytes 589832 | tf_op jit(solution)/shard_map/ppermute | solution.py:298
  10.0 1.7 %shard_map.122 = (bf16[144,768]{1,0:T(8,128)(2,1)S(1)}, bf16[48,768]{1,0:T(8,128)(2,1)S(1)}, bf16[16,768]{1,0:T(8,128)(2,1)S(1)}, f32[8,768]{1,0:T(8,128)S(1)}) custom-call(s32[1,1,32]{2,1,0:T(1,128)} %tiles_ref.1, s32[1,1,32]{2,1,0:T(1,128)} %bitcast.9, s32[1,1,32]{2,1,0:T(1,128)} %slots_ref.1, s32[1]{0:T(128)S(6)} %copy.13.length_ref, ...), custom_call_target="tpu_custom_call" | custom-call | tf_op jit(solution)/shard_map/pallas_call | solution.py:337
  11.7 0.0 collective-permute-done.refs_0_.refs_2_
  11.7 0.9 %collective-permute-done.3.refs_1_ = bf16[48,768]{1,0:T(8,128)(2,1)S(1)} collective-permute-done((bf16[48,768]{1,0:T(8,128)(2,1)}, bf16[48,768]{1,0:T(8,128)(2,1)S(1)}, u32[]{:S(2)}, u32[]{:S(2)}) %collective-permute-start.3) | collective-permute-done | bytes 73760 | tf_op jit(solution)/shard_map/ppermute | solution.py:298
  12.7 0.0 collective-permute-done.4.refs_2_.refs_0_
  12.7 0.6 collective-permute-start.5
  13.3 1.6 %collective-permute-start.2 = (bf16[64,768]{1,0:T(8,128)(2,1)S(1)}, bf16[64,768]{1,0:T(8,128)(2,1)S(1)}, u32[]{:S(2)}, u32[]{:S(2)}) collective-permute-start(bf16[64,768]{1,0:T(8,128)(2,1)S(1)} %shard_map.123), channel_id=1, source_target_pairs={{0,4},{1,5},{2,6},{3,7},{4,0},{5,1},{6,2},{7,3},{8,12},{9,13},{10,... | collective-permute-start | bytes 294920 | tf_op jit(solution)/shard_map/ppermute | solution.py:298
  14.9 0.5 collective-permute-start.1
  15.4 1.4 %shard_map.125 = (bf16[960,768]{1,0:T(8,128)(2,1)S(1)}, bf16[128,768]{1,0:T(8,128)(2,1)S(1)}) custom-call(bf16[16,768]{1,0:T(8,128)(2,1)S(1)} %get-tuple-element.33.refs_1_.refs_2_.refs_0_.refs_3_, bf16[960,768]{1,0:T(8,128)(2,1)} %bitcast.8, bf16[128,768]{1,0:T(8,128)(2,1)} %copy-done.5), custom_call_target="tpu_custom_call" | custom-call | tf_op jit(solution)/shard_map/pallas_call | solution.py:371
  16.8 0.7 %copy-done.9 = bf16[128,768]{1,0:T(8,128)(2,1)} copy-done((bf16[128,768]{1,0:T(8,128)(2,1)}, bf16[128,768]{1,0:T(8,128)(2,1)S(1)}, u32[]{:S(2)}) %copy-start.9) | copy-done | bytes 196632
  17.5 0.7 %collective-permute-done.5.refs_1_.refs_4_ = bf16[112,768]{1,0:T(8,128)(2,1)S(1)} collective-permute-done((bf16[112,768]{1,0:T(8,128)(2,1)S(1)}, bf16[112,768]{1,0:T(8,128)(2,1)S(1)}, u32[]{:S(2)}, u32[]{:S(2)}) %collective-permute-start.5) | collective-permute-done | bytes 172064 | tf_op jit(solution)/shard_map/ppermute | solution.py:298
  18.2 0.9 %copy-done.6 = bf16[128,768]{1,0:T(8,128)(2,1)S(1)} copy-done((bf16[128,768]{1,0:T(8,128)(2,1)S(1)}, bf16[128,768]{1,0:T(8,128)(2,1)}, u32[]{:S(2)}) %copy-start.6) | copy-done | bytes 196632
  19.1 2.1 %collective-permute-done.2.refs_1_.refs_3_.refs_2_.refs_5_ = bf16[64,768]{1,0:T(8,128)(2,1)S(1)} collective-permute-done((bf16[64,768]{1,0:T(8,128)(2,1)S(1)}, bf16[64,768]{1,0:T(8,128)(2,1)S(1)}, u32[]{:S(2)}, u32[]{:S(2)}) %collective-permute-start.2) | collective-permute-done | bytes 98336 | tf_op jit(solution)/shard_map/ppermute | solution.py:298
  21.2 0.0 collective-permute-done.6.refs_0_
  21.2 0.0 collective-permute-done.7.refs_15_.refs_7_.refs_14_
  21.2 0.1 collective-permute-start.9
  21.3 1.2 %collective-permute-start.10 = (bf16[96,768]{1,0:T(8,128)(2,1)S(1)}, bf16[96,768]{1,0:T(8,128)(2,1)S(1)}, u32[]{:S(2)}, u32[]{:S(2)}) collective-permute-start(bf16[96,768]{1,0:T(8,128)(2,1)S(1)} %shard_map.126), channel_id=1, source_target_pairs={{0,2},{1,3},{2,0},{3,1},{4,6},{5,7},{6,4},{7,5},{8,10},{9,11},{10,... | collective-permute-start | bytes 442376 | tf_op jit(solution)/shard_map/ppermute | solution.py:298
  22.5 2.6 %collective-permute-done.1.refs_0_.refs_2_.refs_7_ = bf16[144,768]{1,0:T(8,128)(2,1)S(1)} collective-permute-done((bf16[144,768]{1,0:T(8,128)(2,1)S(1)}, bf16[144,768]{1,0:T(8,128)(2,1)S(1)}, u32[]{:S(2)}, u32[]{:S(2)}) %collective-permute-start.1) | collective-permute-done | bytes 221216 | tf_op jit(solution)/shard_map/ppermute | solution.py:298
  25.1 0.3 collective-permute-start.8
  25.4 4.4 %collective-permute-done.9.refs_1_.refs_3_.refs_6_ = bf16[144,768]{1,0:T(8,128)(2,1)S(1)} collective-permute-done((bf16[144,768]{1,0:T(8,128)(2,1)S(1)}, bf16[144,768]{1,0:T(8,128)(2,1)S(1)}, u32[]{:S(2)}, u32[]{:S(2)}) %collective-permute-start.9) | collective-permute-done | bytes 221216 | tf_op jit(solution)/shard_map/ppermute | solution.py:298
  29.8 0.7 %copy-done = bf16[144,768]{1,0:T(8,128)(2,1)} copy-done((bf16[144,768]{1,0:T(8,128)(2,1)}, bf16[144,768]{1,0:T(8,128)(2,1)S(1)}, u32[]{:S(2)}) %copy-start) | copy-done | bytes 221208
  30.5 0.0 collective-permute-done.10.refs_5_
  30.5 0.9 %shard_map.128 = (bf16[96,768]{1,0:T(8,128)(2,1)}, bf16[96,768]{1,0:T(8,128)(2,1)}, bf16[96,768]{1,0:T(8,128)(2,1)}, bf16[96,768]{1,0:T(8,128)(2,1)}) custom-call(bf16[48,768]{1,0:T(8,128)(2,1)S(1)} %get-tuple-element.42.refs_0_, bf16[48,768]{1,0:T(8,128)(2,1)S(1)} %collective-permute-done.3.refs_1_, ...), custom_call_target="tpu_custom_call" | custom-call | tf_op jit(solution)/shard_map/pallas_call | solution.py:323
  31.4 0.0 collective-permute-start.11
  31.4 0.5 collective-permute-start.12
  31.9 0.0 collective-permute-start.13
  31.9 0.5 collective-permute-start.14
  32.4 0.7 %collective-permute-done.11.refs_9_ = bf16[96,768]{1,0:T(8,128)(2,1)} collective-permute-done((bf16[96,768]{1,0:T(8,128)(2,1)}, bf16[96,768]{1,0:T(8,128)(2,1)}, u32[]{:S(2)}, u32[]{:S(2)}) %collective-permute-start.11) | collective-permute-done | bytes 147488 | tf_op jit(solution)/shard_map/ppermute | solution.py:301
  33.1 1.2 %collective-permute-start.16 = (bf16[144,768]{1,0:T(8,128)(2,1)S(1)}, bf16[144,768]{1,0:T(8,128)(2,1)S(1)}, u32[]{:S(2)}, u32[]{:S(2)}) collective-permute-start(bf16[144,768]{1,0:T(8,128)(2,1)S(1)} %collective-permute-done.1.refs_0_.refs_2_.refs_7_), channel_id=1, source_target_pairs={{0,2},{1,3},{2,0},{3,1},{4,6},{5,7},{6,4},{7,5},{8,10},{9,11},{10,... | collective-permute-start | bytes 663560 | tf_op jit(solution)/shard_map/ppermute | solution.py:298
  34.2 0.0 collective-permute-done.12.refs_10_
  34.3 0.9 %copy-done.3 = bf16[144,768]{1,0:T(8,128)(2,1)S(1)} copy-done((bf16[144,768]{1,0:T(8,128)(2,1)S(1)}, bf16[144,768]{1,0:T(8,128)(2,1)}, u32[]{:S(2)}) %copy-start.3) | copy-done | bytes 221208
  35.2 0.9 %copy-done.10 = bf16[128,768]{1,0:T(8,128)(2,1)S(1)} copy-done((bf16[128,768]{1,0:T(8,128)(2,1)S(1)}, bf16[128,768]{1,0:T(8,128)(2,1)}, u32[]{:S(2)}) %copy-start.10) | copy-done | bytes 196632
  36.1 3.2 %shard_map.129 = (f32[8,960]{1,0:T(8,128)S(1)}, f32[8,960]{1,0:T(8,128)S(1)}, bf16[768,768]{1,0:T(8,128)(2,1)S(1)}) custom-call(s32[1]{0:T(128)} %bitcast.refs_0_, bf16[144,768]{1,0:T(8,128)(2,1)S(1)} %copy-done.3, bf16[128,768]{1,0:T(8,128)(2,1)S(1)} %copy-done.10, bf16[16,768]{1,0:T(8,128)(2,1)S(1)} %get-tuple-element.33.refs_1_.refs_2_.refs_0_.refs_3_, ...), custom_call_target="tpu_custom_call" | custom-call | flops 2 | bytes 2 | tf_op jit(solution)/shard_map/pallas_call | solution.py:394
  39.3 0.9 %collective-permute-start.15 = (bf16[144,768]{1,0:T(8,128)(2,1)}, bf16[144,768]{1,0:T(8,128)(2,1)S(1)}, u32[]{:S(2)}, u32[]{:S(2)}) collective-permute-start(bf16[144,768]{1,0:T(8,128)(2,1)} %collective-permute-done.8.refs_1_.refs_9_), channel_id=1, source_target_pairs={{0,2},{1,3},{2,0},{3,1},{4,6},{5,7},{6,4},{7,5},{8,10},{9,11},{10,... | collective-permute-start | bytes 663560 | tf_op jit(solution)/shard_map/ppermute | solution.py:298
  40.2 1.8 %shard_map.130 = (f32[8,960]{1,0:T(8,128)S(1)}, f32[8,960]{1,0:T(8,128)S(1)}) custom-call(bf16[128,768]{1,0:T(8,128)(2,1)S(1)} %copy-done.8, bf16[144,768]{1,0:T(8,128)(2,1)S(1)} %copy-done.1, bf16[64,768]{1,0:T(8,128)(2,1)S(1)} %collective-permute-done.2.refs_1_.refs_3_.refs_2_.refs_5_, bf16[144,768]{1,0:T(8,128)(2,1)S(1)} %copy-done.1, ...), custom_call_target="tpu_custom_call" | custom-call | flops 2 | bytes 2 | tf_op jit(solution)/shard_map/pallas_call | solution.py:417
  42.0 0.0 copy-start.11
  42.0 0.0 collective-permute-done.16.refs_1_.refs_3_.refs_8_
  42.0 1.8 %shard_map.131 = (f32[8,960]{1,0:T(8,128)S(1)}, f32[8,960]{1,0:T(8,128)S(1)}) custom-call(bf16[144,768]{1,0:T(8,128)(2,1)S(1)} %collective-permute-done.1.refs_0_.refs_2_.refs_7_, bf16[144,768]{1,0:T(8,128)(2,1)S(1)} %collective-permute-done.16.refs_1_.refs_3_.refs_8_, bf16[144,768]{1,0:T(8,128)(2,1)S(1)} %collective-permute-done.1.refs_0_.refs_2_.refs_7_, ...), custom_call_target="tpu_custom_call" | custom-call | flops 2 | bytes 2 | tf_op jit(solution)/shard_map/pallas_call | solution.py:417
  43.8 3.0 %collective-permute-done.15.refs_2_.refs_10_ = bf16[144,768]{1,0:T(8,128)(2,1)S(1)} collective-permute-done((bf16[144,768]{1,0:T(8,128)(2,1)}, bf16[144,768]{1,0:T(8,128)(2,1)S(1)}, u32[]{:S(2)}, u32[]{:S(2)}) %collective-permute-start.15) | collective-permute-done | bytes 221216 | tf_op jit(solution)/shard_map/ppermute | solution.py:298
  46.8 3.1 %shard_map.132 = (bf16[8,48,128]{2,1,0:T(8,128)(2,1)S(1)}, bf16[8,32,128]{2,1,0:T(8,128)(2,1)S(1)}) custom-call(s32[1]{0:T(128)} %bitcast.refs_0_, bf16[144,768]{1,0:T(8,128)(2,1)} %collective-permute-done.8.refs_1_.refs_9_, bf16[144,768]{1,0:T(8,128)(2,1)S(1)} %collective-permute-done.15.refs_2_.refs_10_, bf16[144,768]{1,0:T(8,128)(2,1)S(1)} %copy-done.4, ...), custom_call_target="tpu_custom_call" | custom-call | flops 2 | bytes 2 | tf_op jit(solution)/shard_map/pallas_call | solution.py:433
  49.9 0.1 collective-permute-start.17
  50.0 1.2 %collective-permute-done.17.got_ref = bf16[8,32,128]{2,1,0:T(8,128)(2,1)S(1)} collective-permute-done((bf16[8,32,128]{2,1,0:T(8,128)(2,1)S(1)}, bf16[8,32,128]{2,1,0:T(8,128)(2,1)S(1)}, u32[]{:S(2)}, u32[]{:S(2)}) %collective-permute-start.17) | collective-permute-done | bytes 65568 | tf_op jit(solution)/shard_map/ppermute | solution.py:301
  51.3 10.4 %all_to_all.5.refs_0_ = bf16[8,48,128]{2,1,0:T(8,128)(2,1)S(1)} all-to-all(bf16[8,48,128]{2,1,0:T(8,128)(2,1)S(1)} %shard_map.133), channel_id=1, replica_groups={{0,2,4,6,8,10,12,14},{1,3,5,7,9,11,13,15},{16,18,20,22,24,26,28,30},{17..., dimensions={0} | all-to-all | bytes 196608 | tf_op jit(solution)/shard_map/all_to_all | solution.py:463
  61.7 0.8 %shard_map.134 = (bf16[1,15360]{1,0:T(2,128)(2,1)}, bf16[2,15360]{1,0:T(2,128)(2,1)}) custom-call(bf16[8,48,128]{2,1,0:T(8,128)(2,1)S(1)} %all_to_all.5.refs_0_), custom_call_target="tpu_custom_call" | custom-call | tf_op jit(solution)/shard_map/pallas_call | solution.py:466
  (26 shorter events, 0.1 us)
Async XLA Ops:
  0.6 20.6 %collective-permute-start.7 = (bf16[960,768]{1,0:T(8,128)(2,1)}, bf16[960,768]{1,0:T(8,128)(2,1)S(1)}, u32[]{:S(2)}, u32[]{:S(2)}) collective-permute-start(bf16[960,768]{1,0:T(8,128)(2,1)} %bitcast.7), channel_id=1, source_target_pairs={{0,1},{1,0},{2,3},{3,2},{4,5},{5,4},{6,7},{7,6},{8,9},{9,8},{10,11... | collective-permute-start | bytes 4423688 | tf_op jit(solution)/shard_map/ppermute | solution.py:301
  1.2 11.5 %collective-permute-start.4 = (bf16[128,768]{1,0:T(8,128)(2,1)}, bf16[128,768]{1,0:T(8,128)(2,1)S(1)}, u32[]{:S(2)}, u32[]{:S(2)}) collective-permute-start(bf16[128,768]{1,0:T(8,128)(2,1)} %refs_0_.1), channel_id=1, source_target_pairs={{0,2},{1,3},{2,0},{3,1},{4,6},{5,7},{6,4},{7,5},{8,10},{9,11},{10,... | collective-permute-start | bytes 589832 | tf_op jit(solution)/shard_map/ppermute | solution.py:298
  3.7 8.0 %collective-permute-start = (bf16[48,768]{1,0:T(8,128)(2,1)}, bf16[48,768]{1,0:T(8,128)(2,1)S(1)}, u32[]{:S(2)}, u32[]{:S(2)}) collective-permute-start(bf16[48,768]{1,0:T(8,128)(2,1)} %refs_1_.1), channel_id=1, source_target_pairs={{0,12},{1,13},{2,14},{3,15},{4,8},{5,9},{6,10},{7,11},{8,4},{9,5},... | collective-permute-start | bytes 221192 | tf_op jit(solution)/shard_map/ppermute | solution.py:298
  7.3 5.4 %collective-permute-start.3 = (bf16[48,768]{1,0:T(8,128)(2,1)}, bf16[48,768]{1,0:T(8,128)(2,1)S(1)}, u32[]{:S(2)}, u32[]{:S(2)}) collective-permute-start(bf16[48,768]{1,0:T(8,128)(2,1)} %refs_1_.1), channel_id=1, source_target_pairs={{0,4},{1,5},{2,6},{3,7},{4,0},{5,1},{6,2},{7,3},{8,12},{9,13},{10,... | collective-permute-start | bytes 221192 | tf_op jit(solution)/shard_map/ppermute | solution.py:298
  7.3 13.9 %collective-permute-start.6 = (bf16[128,768]{1,0:T(8,128)(2,1)}, bf16[128,768]{1,0:T(8,128)(2,1)S(1)}, u32[]{:S(2)}, u32[]{:S(2)}) collective-permute-start(bf16[128,768]{1,0:T(8,128)(2,1)} %refs_0_.1), channel_id=1, source_target_pairs={{0,4},{1,5},{2,6},{3,7},{4,0},{5,1},{6,2},{7,3},{8,12},{9,13},{10,... | collective-permute-start | bytes 589832 | tf_op jit(solution)/shard_map/ppermute | solution.py:298
  11.7 9.5 %copy-start.2 = (bf16[144,768]{1,0:T(8,128)(2,1)}, bf16[144,768]{1,0:T(8,128)(2,1)S(1)}, u32[]{:S(2)}) copy-start(bf16[144,768]{1,0:T(8,128)(2,1)S(1)} %get-tuple-element.32.refs_1_.refs_3_) | copy-start | bytes 663556
  12.7 2.7 %copy-start.5 = (bf16[128,768]{1,0:T(8,128)(2,1)}, bf16[128,768]{1,0:T(8,128)(2,1)S(1)}, u32[]{:S(2)}) copy-start(bf16[128,768]{1,0:T(8,128)(2,1)S(1)} %collective-permute-done.4.refs_2_.refs_0_) | copy-start | bytes 589828
  12.7 5.5 %collective-permute-start.5 = (bf16[112,768]{1,0:T(8,128)(2,1)S(1)}, bf16[112,768]{1,0:T(8,128)(2,1)S(1)}, u32[]{:S(2)}, u32[]{:S(2)}) collective-permute-start(bf16[112,768]{1,0:T(8,128)(2,1)S(1)} %shard_map.124), channel_id=1, source_target_pairs={{0,2},{1,3},{2,0},{3,1},{4,6},{5,7},{6,4},{7,5},{8,10},{9,11},{10,... | collective-permute-start | bytes 516104 | tf_op jit(solution)/shard_map/ppermute | solution.py:298
  13.3 7.9 %collective-permute-start.2 = (bf16[64,768]{1,0:T(8,128)(2,1)S(1)}, bf16[64,768]{1,0:T(8,128)(2,1)S(1)}, u32[]{:S(2)}, u32[]{:S(2)}) collective-permute-start(bf16[64,768]{1,0:T(8,128)(2,1)S(1)} %shard_map.123), channel_id=1, source_target_pairs={{0,4},{1,5},{2,6},{3,7},{4,0},{5,1},{6,2},{7,3},{8,12},{9,13},{10,... | collective-permute-start | bytes 294920 | tf_op jit(solution)/shard_map/ppermute | solution.py:298
  14.9 10.2 %collective-permute-start.1 = (bf16[144,768]{1,0:T(8,128)(2,1)S(1)}, bf16[144,768]{1,0:T(8,128)(2,1)S(1)}, u32[]{:S(2)}, u32[]{:S(2)}) collective-permute-start(bf16[144,768]{1,0:T(8,128)(2,1)S(1)} %get-tuple-element.32.refs_1_.refs_3_), channel_id=1, source_target_pairs={{0,12},{1,13},{2,14},{3,15},{4,8},{5,9},{6,10},{7,11},{8,4},{9,5},... | collective-permute-start | bytes 663560 | tf_op jit(solution)/shard_map/ppermute | solution.py:298
  16.8 0.7 %copy-start.9 = (bf16[128,768]{1,0:T(8,128)(2,1)}, bf16[128,768]{1,0:T(8,128)(2,1)S(1)}, u32[]{:S(2)}) copy-start(bf16[128,768]{1,0:T(8,128)(2,1)S(1)} %get-tuple-element.40.refs_2_) | copy-start | bytes 589828
  18.2 0.9 %copy-start.6 = (bf16[128,768]{1,0:T(8,128)(2,1)S(1)}, bf16[128,768]{1,0:T(8,128)(2,1)}, u32[]{:S(2)}) copy-start(bf16[128,768]{1,0:T(8,128)(2,1)} %copy-done.5) | copy-start | bytes 589828
  21.2 8.6 %copy-start.7 = (bf16[128,768]{1,0:T(8,128)(2,1)}, bf16[128,768]{1,0:T(8,128)(2,1)S(1)}, u32[]{:S(2)}) copy-start(bf16[128,768]{1,0:T(8,128)(2,1)S(1)} %collective-permute-done.6.refs_0_) | copy-start | bytes 589828
  21.2 8.5 %collective-permute-start.9 = (bf16[144,768]{1,0:T(8,128)(2,1)S(1)}, bf16[144,768]{1,0:T(8,128)(2,1)S(1)}, u32[]{:S(2)}, u32[]{:S(2)}) collective-permute-start(bf16[144,768]{1,0:T(8,128)(2,1)S(1)} %shard_map.127), channel_id=1, source_target_pairs={{0,4},{1,5},{2,6},{3,7},{4,0},{5,1},{6,2},{7,3},{8,12},{9,13},{10,... | collective-permute-start | bytes 663560 | tf_op jit(solution)/shard_map/ppermute | solution.py:298
  21.3 9.2 %collective-permute-start.10 = (bf16[96,768]{1,0:T(8,128)(2,1)S(1)}, bf16[96,768]{1,0:T(8,128)(2,1)S(1)}, u32[]{:S(2)}, u32[]{:S(2)}) collective-permute-start(bf16[96,768]{1,0:T(8,128)(2,1)S(1)} %shard_map.126), channel_id=1, source_target_pairs={{0,2},{1,3},{2,0},{3,1},{4,6},{5,7},{6,4},{7,5},{8,10},{9,11},{10,... | collective-permute-start | bytes 442376 | tf_op jit(solution)/shard_map/ppermute | solution.py:298
  25.1 14.2 %collective-permute-start.8 = (bf16[144,768]{1,0:T(8,128)(2,1)S(1)}, bf16[144,768]{1,0:T(8,128)(2,1)}, u32[]{:S(2)}, u32[]{:S(2)}) collective-permute-start(bf16[144,768]{1,0:T(8,128)(2,1)S(1)} %collective-permute-done.1.refs_0_.refs_2_.refs_7_), channel_id=1, source_target_pairs={{0,4},{1,5},{2,6},{3,7},{4,0},{5,1},{6,2},{7,3},{8,12},{9,13},{10,... | collective-permute-start | bytes 663560 | tf_op jit(solution)/shard_map/ppermute | solution.py:298
  29.8 0.7 %copy-start = (bf16[144,768]{1,0:T(8,128)(2,1)}, bf16[144,768]{1,0:T(8,128)(2,1)S(1)}, u32[]{:S(2)}) copy-start(bf16[144,768]{1,0:T(8,128)(2,1)S(1)} %collective-permute-done.9.refs_1_.refs_3_.refs_6_) | copy-start | bytes 663556
  31.4 1.7 %collective-permute-start.11 = (bf16[96,768]{1,0:T(8,128)(2,1)}, bf16[96,768]{1,0:T(8,128)(2,1)}, u32[]{:S(2)}, u32[]{:S(2)}) collective-permute-start(bf16[96,768]{1,0:T(8,128)(2,1)} %get-tuple-element.43.refs_5_), channel_id=1, source_target_pairs={{0,1},{1,0},{2,3},{3,2},{4,5},{5,4},{6,7},{7,6},{8,9},{9,8},{10,11... | collective-permute-start | bytes 442376 | tf_op jit(solution)/shard_map/ppermute | solution.py:301
  31.4 2.9 %collective-permute-start.12 = (bf16[96,768]{1,0:T(8,128)(2,1)}, bf16[96,768]{1,0:T(8,128)(2,1)}, u32[]{:S(2)}, u32[]{:S(2)}) collective-permute-start(bf16[96,768]{1,0:T(8,128)(2,1)} %get-tuple-element.44.refs_6_), channel_id=1, source_target_pairs={{0,1},{1,0},{2,3},{3,2},{4,5},{5,4},{6,7},{7,6},{8,9},{9,8},{10,11... | collective-permute-start | bytes 442376 | tf_op jit(solution)/shard_map/ppermute | solution.py:301
  31.9 2.4 %collective-permute-start.13 = (bf16[96,768]{1,0:T(8,128)(2,1)}, bf16[96,768]{1,0:T(8,128)(2,1)}, u32[]{:S(2)}, u32[]{:S(2)}) collective-permute-start(bf16[96,768]{1,0:T(8,128)(2,1)} %get-tuple-element.45.refs_7_), channel_id=1, source_target_pairs={{0,1},{1,0},{2,3},{3,2},{4,5},{5,4},{6,7},{7,6},{8,9},{9,8},{10,11... | collective-permute-start | bytes 442376 | tf_op jit(solution)/shard_map/ppermute | solution.py:301
  31.9 2.4 %collective-permute-start.14 = (bf16[96,768]{1,0:T(8,128)(2,1)}, bf16[96,768]{1,0:T(8,128)(2,1)}, u32[]{:S(2)}, u32[]{:S(2)}) collective-permute-start(bf16[96,768]{1,0:T(8,128)(2,1)} %get-tuple-element.46.refs_8_), channel_id=1, source_target_pairs={{0,1},{1,0},{2,3},{3,2},{4,5},{5,4},{6,7},{7,6},{8,9},{9,8},{10,11... | collective-permute-start | bytes 442376 | tf_op jit(solution)/shard_map/ppermute | solution.py:301
  33.1 9.0 %collective-permute-start.16 = (bf16[144,768]{1,0:T(8,128)(2,1)S(1)}, bf16[144,768]{1,0:T(8,128)(2,1)S(1)}, u32[]{:S(2)}, u32[]{:S(2)}) collective-permute-start(bf16[144,768]{1,0:T(8,128)(2,1)S(1)} %collective-permute-done.1.refs_0_.refs_2_.refs_7_), channel_id=1, source_target_pairs={{0,2},{1,3},{2,0},{3,1},{4,6},{5,7},{6,4},{7,5},{8,10},{9,11},{10,... | collective-permute-start | bytes 663560 | tf_op jit(solution)/shard_map/ppermute | solution.py:298
  34.3 0.9 %copy-start.3 = (bf16[144,768]{1,0:T(8,128)(2,1)S(1)}, bf16[144,768]{1,0:T(8,128)(2,1)}, u32[]{:S(2)}) copy-start(bf16[144,768]{1,0:T(8,128)(2,1)} %copy-done.2) | copy-start | bytes 663556
  35.2 0.9 %copy-start.10 = (bf16[128,768]{1,0:T(8,128)(2,1)S(1)}, bf16[128,768]{1,0:T(8,128)(2,1)}, u32[]{:S(2)}) copy-start(bf16[128,768]{1,0:T(8,128)(2,1)} %copy-done.9) | copy-start | bytes 589828
  36.1 4.1 %copy-start.1 = (bf16[144,768]{1,0:T(8,128)(2,1)S(1)}, bf16[144,768]{1,0:T(8,128)(2,1)}, u32[]{:S(2)}) copy-start(bf16[144,768]{1,0:T(8,128)(2,1)} %copy-done) | copy-start | bytes 663556
  36.1 4.1 %copy-start.8 = (bf16[128,768]{1,0:T(8,128)(2,1)S(1)}, bf16[128,768]{1,0:T(8,128)(2,1)}, u32[]{:S(2)}) copy-start(bf16[128,768]{1,0:T(8,128)(2,1)} %copy-done.7) | copy-start | bytes 589828
  39.3 7.5 %collective-permute-start.15 = (bf16[144,768]{1,0:T(8,128)(2,1)}, bf16[144,768]{1,0:T(8,128)(2,1)S(1)}, u32[]{:S(2)}, u32[]{:S(2)}) collective-permute-start(bf16[144,768]{1,0:T(8,128)(2,1)} %collective-permute-done.8.refs_1_.refs_9_), channel_id=1, source_target_pairs={{0,2},{1,3},{2,0},{3,1},{4,6},{5,7},{6,4},{7,5},{8,10},{9,11},{10,... | collective-permute-start | bytes 663560 | tf_op jit(solution)/shard_map/ppermute | solution.py:298
  42.0 4.8 %copy-start.4 = (bf16[144,768]{1,0:T(8,128)(2,1)S(1)}, bf16[144,768]{1,0:T(8,128)(2,1)}, u32[]{:S(2)}) copy-start(bf16[144,768]{1,0:T(8,128)(2,1)} %copy-done.2) | copy-start | bytes 663556
  42.0 4.8 %copy-start.11 = (f32[15360]{0:T(1024)S(1)}, f32[15360]{0:T(1024)}, u32[]{:S(2)}) copy-start(f32[15360]{0:T(1024)} %param.18) | copy-start | bytes 184324
  49.9 1.3 %collective-permute-start.17 = (bf16[8,32,128]{2,1,0:T(8,128)(2,1)S(1)}, bf16[8,32,128]{2,1,0:T(8,128)(2,1)S(1)}, u32[]{:S(2)}, u32[]{:S(2)}) collective-permute-start(bf16[8,32,128]{2,1,0:T(8,128)(2,1)S(1)} %get-tuple-element.59), channel_id=1, source_target_pairs={{0,1},{1,0},{2,3},{3,2},{4,5},{5,4},{6,7},{7,6},{8,9},{9,8},{10,11... | collective-permute-start | bytes 196616 | tf_op jit(solution)/shard_map/ppermute | solution.py:301

commit v17 on v16

--- a/solution.py
+++ b/solution.py
@@ -130,7 +130,7 @@
     ]
 
 
-def start_kernel(tiles_ref, owners_ref, slots_ref, length_ref, *refs):
+def start_kernel(me_ref, tiles_ref, owners_ref, slots_ref, length_ref, *refs):
     hidden_ref, weight_ref, vectors = refs[0], refs[1], refs[2:5]
     load_ref, block_ref, table_ref, rows_ref, kept, sems = refs[5:]
     seq, width = hidden_ref.shape
@@ -329,6 +329,7 @@
         )(*values)
         return piled if len(heights) > 1 else piled[0]
 
+    where = me[None]
     weight_rows = jnp.swapaxes(decoder_weight[0], 0, 1)
     block_6 = cross(transform_weight, 6)
     block_2 = cross(transform_weight, 2)
@@ -342,7 +343,7 @@
             shape((SLOT_ROWS, width), jnp.bfloat16),
             shape((8, width), jnp.float32),
         ],
-        in_specs=[smem] * 4 + [hbm] * 5,
+        in_specs=[smem] * 5 + [hbm] * 5,
         out_specs=[vmem] * 4,
         scratch_shapes=[
             pltpu.VMEM((3 * width,), jnp.float32),
@@ -350,6 +351,7 @@
         ],
         compiler_params=limit,
     )(
+        where,
         stay(tile_ids),
         stay(owner_ids[..., 0]),
         stay(block_slots),
@@ -367,13 +369,13 @@
     block_4 = cross(pile((block_6, table), (one, below)), 2)
     docs[6] = cross(after(load, block_6), 6)
     load_1 = pile((docs[1], near_pile), ((0, seq), (2 * rows, SLOT_ROWS)))
-    far_from = [stay(after(weight_rows, table)), stay(docs[1])]
-    mine, beside = pl.pallas_call(
-        lambda *refs: fetch_kernel(2, *refs),
+    far_from = [stay(after(weight_rows, table))]
+    [mine] = pl.pallas_call(
+        lambda *refs: fetch_kernel(1, *refs),
         out_shape=[shape(value.shape, value.dtype) for value in far_from],
-        in_specs=[vmem] + [hbm] * 2,
-        out_specs=[vmem] * 2,
-        scratch_shapes=[pltpu.SemaphoreType.DMA((2,))],
+        in_specs=[vmem] + [hbm],
+        out_specs=[vmem],
+        scratch_shapes=[pltpu.SemaphoreType.DMA((1,))],
         compiler_params=limit,
     )(table, *far_from)
     far = (block_6, after(block_4, near_pile, docs[2], mine, theirs))
@@ -389,7 +391,6 @@
     block_masks = [0, 2, 6, 4, 1, 3, 7, 5]
 
     masks = [0, 1, 2, 3, 6, 7, 4, 5]
-    where = me[None]
     best_shape = shape((8, half), jnp.float32)
     *best, weight = pl.pallas_call(
         lambda *refs: first_kernel(seq, block_masks, *refs),
@@ -401,7 +402,7 @@
     )(
         where,
         load,
-        beside,
+        docs[1],
         table,
         near_pile,
         *packed,
@@ -410,7 +411,7 @@
         mine,
         theirs,
     )
-    docs |= {0: load, 1: beside, 5: cross(after(docs[4], weight), 1)}
+    docs |= {0: load, 5: cross(after(docs[4], weight), 1)}
     tables = docs | {1: near_pile, 2: block_4}
     for first in range(2, len(masks) - 2, 2):
         pair = masks[first : first + 2]

time: 62.8 us -> 57.9 us (0.922)
  local copies, waits for them, and re-layouts: 4.18 us -> 0.01 us
  Pallas kernels: 14.7 us -> 11.4 us
  waiting for transfers between devices: 15.6 us -> 18.9 us
    unnamed x24 -> x2, local copies, waits for them, and re-layouts: 4.18 us -> 0.01 us
    ppermute x12, waiting for transfers between devices: 13.7 us -> 17.3 us  [cross(): lax.ppermute(value, 'doc', [(i, i ^ 2 * mask) for i in range(devices)])]
    pallas_call x1, Pallas kernels: 3.17 us -> 1.81 us  [move_tokens(): pl.pallas_call(lambda *refs: first_kernel(seq, block_masks, *refs), out_s...]
    pallas_call x1, Pallas kernels: 3.13 us -> 2.12 us  [move_tokens(): pl.pallas_call(lambda *refs: last_kernel(seq, masks, *refs), out_shape=[s...]
    pallas_call x5, Pallas kernels: 0.91 us -> 0.09 us  [pile(): pl.pallas_call(lambda *refs: pile_kernel(parts, heights, *refs), out_shap...]
  transfers between devices with their start and end apart: 18 -> 18, of which waited for: 8 -> 9; matrix products, arithmetic and copies ran while one was open for 0% -> 0% of each run, Pallas kernels for 17% -> 15%
where the time goes in v17:
time: 57.9 us; the launch traced here: 57.7 us
  waiting for transfers between devices  18.9 us (33%)
  starting transfers between devices  15.9 us (27%)
  Pallas kernels  11.4 us (20%)
  blocking collectives  10 us (17%)
  between operations  1.41 us (2%)
    ppermute x12, waiting for transfers between devices, cross(): lax.ppermute(value, 'doc', [(i, i ^ 2 * mask) for i in range(devices)])  17.3 us
    ppermute x12, starting transfers between devices, cross(): lax.ppermute(value, 'doc', [(i, i ^ 2 * mask) for i in range(devices)])  14.3 us
    all_to_all x1, blocking collectives, move_tokens(): lax.all_to_all(merged, 'doc', split_axis=0, concat_axis=0, axis_index_gro...  10 us
    pallas_call x2, Pallas kernels, move_tokens(): pl.pallas_call(lambda *refs: next_kernel(seq, *refs), out_shape=[best_sha...  3.54 us
    pallas_call x1, Pallas kernels, move_tokens(): pl.pallas_call(lambda *refs: last_kernel(seq, masks, *refs), out_shape=[s...  2.12 us
    pallas_call x1, Pallas kernels, move_tokens(): pl.pallas_call(lambda *refs: first_kernel(seq, block_masks, *refs), out_s...  1.81 us
    pallas_call x1, Pallas kernels, move_tokens(): pl.pallas_call(start_kernel, out_shape=[shape((seq + SLOT_ROWS, width), j...  1.71 us
    ppermute x6, starting transfers between devices, swap(): return lax.ppermute(value, 'doc', [(i, i ^ 1) for i in range(devices)])  1.67 us
  transfers between devices with their start and end apart: 18, of which 9 were waited for; matrix products, arithmetic and copies ran while one was open for 0% of the time, Pallas kernels for 15%

profile of v17, /device:TPU:0, one launch (start us, length us, event | category | flops | bytes accessed | tf_op | source)
XLA Modules:
  0.0 57.7 jit_solution(14515706807039438641)
XLA Ops:
  0.6 0.5 collective-permute-start.7
  1.2 2.6 %collective-permute-start.4 = (bf16[128,768]{1,0:T(8,128)(2,1)}, bf16[128,768]{1,0:T(8,128)(2,1)S(1)}, u32[]{:S(2)}, u32[]{:S(2)}) collective-permute-start(bf16[128,768]{1,0:T(8,128)(2,1)} %refs_0_.1), channel_id=1, source_target_pairs={{0,2},{1,3},{2,0},{3,1},{4,6},{5,7},{6,4},{7,5},{8,10},{9,11},{10,... | collective-permute-start | bytes 589832 | tf_op jit(solution)/shard_map/ppermute | solution.py:298
  3.7 3.6 %collective-permute-start = (bf16[48,768]{1,0:T(8,128)(2,1)}, bf16[48,768]{1,0:T(8,128)(2,1)S(1)}, u32[]{:S(2)}, u32[]{:S(2)}) collective-permute-start(bf16[48,768]{1,0:T(8,128)(2,1)} %refs_1_.1), channel_id=1, source_target_pairs={{0,12},{1,13},{2,14},{3,15},{4,8},{5,9},{6,10},{7,11},{8,4},{9,5},... | collective-permute-start | bytes 221192 | tf_op jit(solution)/shard_map/ppermute | solution.py:298
  7.3 0.0 collective-permute-start.3
  7.3 2.0 %collective-permute-start.6 = (bf16[128,768]{1,0:T(8,128)(2,1)}, bf16[128,768]{1,0:T(8,128)(2,1)S(1)}, u32[]{:S(2)}, u32[]{:S(2)}) collective-permute-start(bf16[128,768]{1,0:T(8,128)(2,1)} %refs_0_.1), channel_id=1, source_target_pairs={{0,4},{1,5},{2,6},{3,7},{4,0},{5,1},{6,2},{7,3},{8,12},{9,13},{10,... | collective-permute-start | bytes 589832 | tf_op jit(solution)/shard_map/ppermute | solution.py:298
  10.0 1.7 %shard_map.122 = (bf16[144,768]{1,0:T(8,128)(2,1)S(1)}, bf16[48,768]{1,0:T(8,128)(2,1)S(1)}, bf16[16,768]{1,0:T(8,128)(2,1)S(1)}, f32[8,768]{1,0:T(8,128)S(1)}) custom-call(s32[1]{0:T(128)} %bitcast.me_ref.refs_0_, s32[1,1,32]{2,1,0:T(1,128)} %tiles_ref.1, s32[1,1,32]{2,1,0:T(1,128)} %bitcast.9, s32[1,1,32]{2,1,0:T(1,128)} %slots_ref.1, ...), custom_call_target="tpu_custom_call" | custom-call | tf_op jit(solution)/shard_map/pallas_call | solution.py:338
  11.7 0.0 collective-permute-done.refs_0_.refs_2_
  11.7 1.0 %collective-permute-done.3.refs_1_ = bf16[48,768]{1,0:T(8,128)(2,1)S(1)} collective-permute-done((bf16[48,768]{1,0:T(8,128)(2,1)}, bf16[48,768]{1,0:T(8,128)(2,1)S(1)}, u32[]{:S(2)}, u32[]{:S(2)}) %collective-permute-start.3) | collective-permute-done | bytes 73760 | tf_op jit(solution)/shard_map/ppermute | solution.py:298
  12.7 0.0 collective-permute-done.4.refs_0_.refs_2_
  12.7 0.6 %collective-permute-start.5 = (bf16[112,768]{1,0:T(8,128)(2,1)S(1)}, bf16[112,768]{1,0:T(8,128)(2,1)S(1)}, u32[]{:S(2)}, u32[]{:S(2)}) collective-permute-start(bf16[112,768]{1,0:T(8,128)(2,1)S(1)} %shard_map.124), channel_id=1, source_target_pairs={{0,2},{1,3},{2,0},{3,1},{4,6},{5,7},{6,4},{7,5},{8,10},{9,11},{10,... | collective-permute-start | bytes 516104 | tf_op jit(solution)/shard_map/ppermute | solution.py:298
  13.3 1.6 %collective-permute-start.2 = (bf16[64,768]{1,0:T(8,128)(2,1)S(1)}, bf16[64,768]{1,0:T(8,128)(2,1)S(1)}, u32[]{:S(2)}, u32[]{:S(2)}) collective-permute-start(bf16[64,768]{1,0:T(8,128)(2,1)S(1)} %shard_map.123), channel_id=1, source_target_pairs={{0,4},{1,5},{2,6},{3,7},{4,0},{5,1},{6,2},{7,3},{8,12},{9,13},{10,... | collective-permute-start | bytes 294920 | tf_op jit(solution)/shard_map/ppermute | solution.py:298
  14.9 0.5 collective-permute-start.1
  15.4 1.4 %shard_map.125.refs_14_.refs_6_.refs_13_ = bf16[960,768]{1,0:T(8,128)(2,1)S(1)} custom-call(bf16[16,768]{1,0:T(8,128)(2,1)S(1)} %get-tuple-element.31.refs_1_.refs_2_.refs_0_.refs_3_, bf16[960,768]{1,0:T(8,128)(2,1)} %bitcast.8), custom_call_target="tpu_custom_call" | custom-call | tf_op jit(solution)/shard_map/pallas_call | solution.py:373
  16.8 1.4 %collective-permute-done.5.refs_1_.refs_4_ = bf16[112,768]{1,0:T(8,128)(2,1)S(1)} collective-permute-done((bf16[112,768]{1,0:T(8,128)(2,1)S(1)}, bf16[112,768]{1,0:T(8,128)(2,1)S(1)}, u32[]{:S(2)}, u32[]{:S(2)}) %collective-permute-start.5) | collective-permute-done | bytes 172064 | tf_op jit(solution)/shard_map/ppermute | solution.py:298
  18.2 3.0 %collective-permute-done.2.refs_1_.refs_3_.refs_2_.refs_5_ = bf16[64,768]{1,0:T(8,128)(2,1)S(1)} collective-permute-done((bf16[64,768]{1,0:T(8,128)(2,1)S(1)}, bf16[64,768]{1,0:T(8,128)(2,1)S(1)}, u32[]{:S(2)}, u32[]{:S(2)}) %collective-permute-start.2) | collective-permute-done | bytes 98336 | tf_op jit(solution)/shard_map/ppermute | solution.py:298
  21.2 0.0 collective-permute-done.6.refs_0_
  21.2 0.0 collective-permute-done.7.refs_15_.refs_7_.refs_14_
  21.2 0.1 collective-permute-start.9
  21.3 0.9 %collective-permute-start.10 = (bf16[96,768]{1,0:T(8,128)(2,1)S(1)}, bf16[96,768]{1,0:T(8,128)(2,1)S(1)}, u32[]{:S(2)}, u32[]{:S(2)}) collective-permute-start(bf16[96,768]{1,0:T(8,128)(2,1)S(1)} %shard_map.126), channel_id=1, source_target_pairs={{0,2},{1,3},{2,0},{3,1},{4,6},{5,7},{6,4},{7,5},{8,10},{9,11},{10,... | collective-permute-start | bytes 442376 | tf_op jit(solution)/shard_map/ppermute | solution.py:298
  22.2 2.9 %collective-permute-done.1.refs_0_.refs_2_.refs_7_ = bf16[144,768]{1,0:T(8,128)(2,1)S(1)} collective-permute-done((bf16[144,768]{1,0:T(8,128)(2,1)S(1)}, bf16[144,768]{1,0:T(8,128)(2,1)S(1)}, u32[]{:S(2)}, u32[]{:S(2)}) %collective-permute-start.1) | collective-permute-done | bytes 221216 | tf_op jit(solution)/shard_map/ppermute | solution.py:298
  25.1 0.3 collective-permute-start.8
  25.4 4.4 %collective-permute-done.9.refs_1_.refs_3_.refs_6_ = bf16[144,768]{1,0:T(8,128)(2,1)S(1)} collective-permute-done((bf16[144,768]{1,0:T(8,128)(2,1)S(1)}, bf16[144,768]{1,0:T(8,128)(2,1)S(1)}, u32[]{:S(2)}, u32[]{:S(2)}) %collective-permute-start.9) | collective-permute-done | bytes 221216 | tf_op jit(solution)/shard_map/ppermute | solution.py:298
  29.8 0.0 collective-permute-done.10.refs_5_
  29.8 0.1 collective-permute-start.11
  29.9 0.5 collective-permute-start.12
  30.4 0.1 collective-permute-start.13
  30.5 0.4 collective-permute-start.14
  30.9 0.3 collective-permute-done.11.refs_9_
  31.2 1.2 %collective-permute-start.16 = (bf16[144,768]{1,0:T(8,128)(2,1)S(1)}, bf16[144,768]{1,0:T(8,128)(2,1)S(1)}, u32[]{:S(2)}, u32[]{:S(2)}) collective-permute-start(bf16[144,768]{1,0:T(8,128)(2,1)S(1)} %collective-permute-done.1.refs_0_.refs_2_.refs_7_), channel_id=1, source_target_pairs={{0,2},{1,3},{2,0},{3,1},{4,6},{5,7},{6,4},{7,5},{8,10},{9,11},{10,... | collective-permute-start | bytes 663560 | tf_op jit(solution)/shard_map/ppermute | solution.py:298
  32.4 0.0 collective-permute-done.12.refs_10_
  32.4 0.0 collective-permute-done.13.refs_11_
  32.4 0.0 collective-permute-done.14.refs_12_
  32.4 1.8 %shard_map.129 = (f32[8,960]{1,0:T(8,128)S(1)}, f32[8,960]{1,0:T(8,128)S(1)}, bf16[768,768]{1,0:T(8,128)(2,1)S(1)}) custom-call(s32[1]{0:T(128)} %bitcast.me_ref.refs_0_, bf16[144,768]{1,0:T(8,128)(2,1)S(1)} %get-tuple-element.30.refs_1_.refs_3_, bf16[128,768]{1,0:T(8,128)(2,1)S(1)} %collective-permute-done.4.refs_0_.refs_2_, ...), custom_call_target="tpu_custom_call" | custom-call | flops 2 | bytes 2 | tf_op jit(solution)/shard_map/pallas_call | solution.py:395
  34.3 0.0 collective-permute-done.8.refs_1_.refs_9_
  34.3 0.9 %collective-permute-start.15 = (bf16[144,768]{1,0:T(8,128)(2,1)S(1)}, bf16[144,768]{1,0:T(8,128)(2,1)S(1)}, u32[]{:S(2)}, u32[]{:S(2)}) collective-permute-start(bf16[144,768]{1,0:T(8,128)(2,1)S(1)} %collective-permute-done.8.refs_1_.refs_9_), channel_id=1, source_target_pairs={{0,2},{1,3},{2,0},{3,1},{4,6},{5,7},{6,4},{7,5},{8,10},{9,11},{10,... | collective-permute-start | bytes 663560 | tf_op jit(solution)/shard_map/ppermute | solution.py:298
  35.2 1.8 %shard_map.130 = (f32[8,960]{1,0:T(8,128)S(1)}, f32[8,960]{1,0:T(8,128)S(1)}) custom-call(bf16[128,768]{1,0:T(8,128)(2,1)S(1)} %collective-permute-done.6.refs_0_, bf16[144,768]{1,0:T(8,128)(2,1)S(1)} %collective-permute-done.9.refs_1_.refs_3_.refs_6_, bf16[64,768]{1,0:T(8,128)(2,1)S(1)} %collective-permute-done.2.refs_1_.refs_3_.refs_2_.refs_5_, ...), custom_call_target="tpu_custom_call" | custom-call | flops 2 | bytes 2 | tf_op jit(solution)/shard_map/pallas_call | solution.py:418
  36.9 0.0 copy-start
  37.0 2.6 %collective-permute-done.16.refs_1_.refs_3_.refs_8_ = bf16[144,768]{1,0:T(8,128)(2,1)S(1)} collective-permute-done((bf16[144,768]{1,0:T(8,128)(2,1)S(1)}, bf16[144,768]{1,0:T(8,128)(2,1)S(1)}, u32[]{:S(2)}, u32[]{:S(2)}) %collective-permute-start.16) | collective-permute-done | bytes 221216 | tf_op jit(solution)/shard_map/ppermute | solution.py:298
  39.5 1.8 %shard_map.131 = (f32[8,960]{1,0:T(8,128)S(1)}, f32[8,960]{1,0:T(8,128)S(1)}) custom-call(bf16[144,768]{1,0:T(8,128)(2,1)S(1)} %collective-permute-done.1.refs_0_.refs_2_.refs_7_, bf16[144,768]{1,0:T(8,128)(2,1)S(1)} %collective-permute-done.16.refs_1_.refs_3_.refs_8_, bf16[144,768]{1,0:T(8,128)(2,1)S(1)} %collective-permute-done.1.refs_0_.refs_2_.refs_7_, ...), custom_call_target="tpu_custom_call" | custom-call | flops 2 | bytes 2 | tf_op jit(solution)/shard_map/pallas_call | solution.py:418
  41.3 2.2 %collective-permute-done.15.refs_2_.refs_10_ = bf16[144,768]{1,0:T(8,128)(2,1)S(1)} collective-permute-done((bf16[144,768]{1,0:T(8,128)(2,1)S(1)}, bf16[144,768]{1,0:T(8,128)(2,1)S(1)}, u32[]{:S(2)}, u32[]{:S(2)}) %collective-permute-start.15) | collective-permute-done | bytes 221216 | tf_op jit(solution)/shard_map/ppermute | solution.py:298
  43.5 0.0 copy-done
  43.5 2.1 %shard_map.132 = (bf16[8,48,128]{2,1,0:T(8,128)(2,1)S(1)}, bf16[8,32,128]{2,1,0:T(8,128)(2,1)S(1)}) custom-call(s32[1]{0:T(128)} %bitcast.me_ref.refs_0_, bf16[144,768]{1,0:T(8,128)(2,1)S(1)} %collective-permute-done.8.refs_1_.refs_9_, bf16[144,768]{1,0:T(8,128)(2,1)S(1)} %collective-permute-done.15.refs_2_.refs_10_, ...), custom_call_target="tpu_custom_call" | custom-call | flops 2 | bytes 2 | tf_op jit(solution)/shard_map/pallas_call | solution.py:434
  45.6 0.1 collective-permute-start.17
  45.7 1.2 %collective-permute-done.17.got_ref = bf16[8,32,128]{2,1,0:T(8,128)(2,1)S(1)} collective-permute-done((bf16[8,32,128]{2,1,0:T(8,128)(2,1)S(1)}, bf16[8,32,128]{2,1,0:T(8,128)(2,1)S(1)}, u32[]{:S(2)}, u32[]{:S(2)}) %collective-permute-start.17) | collective-permute-done | bytes 65568 | tf_op jit(solution)/shard_map/ppermute | solution.py:301
  46.9 10.0 %all_to_all.5.refs_0_ = bf16[8,48,128]{2,1,0:T(8,128)(2,1)S(1)} all-to-all(bf16[8,48,128]{2,1,0:T(8,128)(2,1)S(1)} %shard_map.133), channel_id=1, replica_groups={{0,2,4,6,8,10,12,14},{1,3,5,7,9,11,13,15},{16,18,20,22,24,26,28,30},{17..., dimensions={0} | all-to-all | bytes 196608 | tf_op jit(solution)/shard_map/all_to_all | solution.py:464
  56.9 0.8 %shard_map.134 = (bf16[1,15360]{1,0:T(2,128)(2,1)}, bf16[2,15360]{1,0:T(2,128)(2,1)}) custom-call(bf16[8,48,128]{2,1,0:T(8,128)(2,1)S(1)} %all_to_all.5.refs_0_), custom_call_target="tpu_custom_call" | custom-call | tf_op jit(solution)/shard_map/pallas_call | solution.py:467
  (6 shorter events, 0.1 us)
Async XLA Ops:
  0.6 20.6 %collective-permute-start.7 = (bf16[960,768]{1,0:T(8,128)(2,1)}, bf16[960,768]{1,0:T(8,128)(2,1)S(1)}, u32[]{:S(2)}, u32[]{:S(2)}) collective-permute-start(bf16[960,768]{1,0:T(8,128)(2,1)} %bitcast.7), channel_id=1, source_target_pairs={{0,1},{1,0},{2,3},{3,2},{4,5},{5,4},{6,7},{7,6},{8,9},{9,8},{10,11... | collective-permute-start | bytes 4423688 | tf_op jit(solution)/shard_map/ppermute | solution.py:301
  1.2 11.5 %collective-permute-start.4 = (bf16[128,768]{1,0:T(8,128)(2,1)}, bf16[128,768]{1,0:T(8,128)(2,1)S(1)}, u32[]{:S(2)}, u32[]{:S(2)}) collective-permute-start(bf16[128,768]{1,0:T(8,128)(2,1)} %refs_0_.1), channel_id=1, source_target_pairs={{0,2},{1,3},{2,0},{3,1},{4,6},{5,7},{6,4},{7,5},{8,10},{9,11},{10,... | collective-permute-start | bytes 589832 | tf_op jit(solution)/shard_map/ppermute | solution.py:298
  3.7 8.0 %collective-permute-start = (bf16[48,768]{1,0:T(8,128)(2,1)}, bf16[48,768]{1,0:T(8,128)(2,1)S(1)}, u32[]{:S(2)}, u32[]{:S(2)}) collective-permute-start(bf16[48,768]{1,0:T(8,128)(2,1)} %refs_1_.1), channel_id=1, source_target_pairs={{0,12},{1,13},{2,14},{3,15},{4,8},{5,9},{6,10},{7,11},{8,4},{9,5},... | collective-permute-start | bytes 221192 | tf_op jit(solution)/shard_map/ppermute | solution.py:298
  7.3 5.4 %collective-permute-start.3 = (bf16[48,768]{1,0:T(8,128)(2,1)}, bf16[48,768]{1,0:T(8,128)(2,1)S(1)}, u32[]{:S(2)}, u32[]{:S(2)}) collective-permute-start(bf16[48,768]{1,0:T(8,128)(2,1)} %refs_1_.1), channel_id=1, source_target_pairs={{0,4},{1,5},{2,6},{3,7},{4,0},{5,1},{6,2},{7,3},{8,12},{9,13},{10,... | collective-permute-start | bytes 221192 | tf_op jit(solution)/shard_map/ppermute | solution.py:298
  7.3 13.9 %collective-permute-start.6 = (bf16[128,768]{1,0:T(8,128)(2,1)}, bf16[128,768]{1,0:T(8,128)(2,1)S(1)}, u32[]{:S(2)}, u32[]{:S(2)}) collective-permute-start(bf16[128,768]{1,0:T(8,128)(2,1)} %refs_0_.1), channel_id=1, source_target_pairs={{0,4},{1,5},{2,6},{3,7},{4,0},{5,1},{6,2},{7,3},{8,12},{9,13},{10,... | collective-permute-start | bytes 589832 | tf_op jit(solution)/shard_map/ppermute | solution.py:298
  12.7 5.5 %collective-permute-start.5 = (bf16[112,768]{1,0:T(8,128)(2,1)S(1)}, bf16[112,768]{1,0:T(8,128)(2,1)S(1)}, u32[]{:S(2)}, u32[]{:S(2)}) collective-permute-start(bf16[112,768]{1,0:T(8,128)(2,1)S(1)} %shard_map.124), channel_id=1, source_target_pairs={{0,2},{1,3},{2,0},{3,1},{4,6},{5,7},{6,4},{7,5},{8,10},{9,11},{10,... | collective-permute-start | bytes 516104 | tf_op jit(solution)/shard_map/ppermute | solution.py:298
  13.3 7.9 %collective-permute-start.2 = (bf16[64,768]{1,0:T(8,128)(2,1)S(1)}, bf16[64,768]{1,0:T(8,128)(2,1)S(1)}, u32[]{:S(2)}, u32[]{:S(2)}) collective-permute-start(bf16[64,768]{1,0:T(8,128)(2,1)S(1)} %shard_map.123), channel_id=1, source_target_pairs={{0,4},{1,5},{2,6},{3,7},{4,0},{5,1},{6,2},{7,3},{8,12},{9,13},{10,... | collective-permute-start | bytes 294920 | tf_op jit(solution)/shard_map/ppermute | solution.py:298
  14.9 10.2 %collective-permute-start.1 = (bf16[144,768]{1,0:T(8,128)(2,1)S(1)}, bf16[144,768]{1,0:T(8,128)(2,1)S(1)}, u32[]{:S(2)}, u32[]{:S(2)}) collective-permute-start(bf16[144,768]{1,0:T(8,128)(2,1)S(1)} %get-tuple-element.30.refs_1_.refs_3_), channel_id=1, source_target_pairs={{0,12},{1,13},{2,14},{3,15},{4,8},{5,9},{6,10},{7,11},{8,4},{9,5},... | collective-permute-start | bytes 663560 | tf_op jit(solution)/shard_map/ppermute | solution.py:298
  21.2 8.6 %collective-permute-start.9 = (bf16[144,768]{1,0:T(8,128)(2,1)S(1)}, bf16[144,768]{1,0:T(8,128)(2,1)S(1)}, u32[]{:S(2)}, u32[]{:S(2)}) collective-permute-start(bf16[144,768]{1,0:T(8,128)(2,1)S(1)} %shard_map.127), channel_id=1, source_target_pairs={{0,4},{1,5},{2,6},{3,7},{4,0},{5,1},{6,2},{7,3},{8,12},{9,13},{10,... | collective-permute-start | bytes 663560 | tf_op jit(solution)/shard_map/ppermute | solution.py:298
  21.3 8.5 %collective-permute-start.10 = (bf16[96,768]{1,0:T(8,128)(2,1)S(1)}, bf16[96,768]{1,0:T(8,128)(2,1)S(1)}, u32[]{:S(2)}, u32[]{:S(2)}) collective-permute-start(bf16[96,768]{1,0:T(8,128)(2,1)S(1)} %shard_map.126), channel_id=1, source_target_pairs={{0,2},{1,3},{2,0},{3,1},{4,6},{5,7},{6,4},{7,5},{8,10},{9,11},{10,... | collective-permute-start | bytes 442376 | tf_op jit(solution)/shard_map/ppermute | solution.py:298
  25.1 9.2 %collective-permute-start.8 = (bf16[144,768]{1,0:T(8,128)(2,1)S(1)}, bf16[144,768]{1,0:T(8,128)(2,1)S(1)}, u32[]{:S(2)}, u32[]{:S(2)}) collective-permute-start(bf16[144,768]{1,0:T(8,128)(2,1)S(1)} %collective-permute-done.1.refs_0_.refs_2_.refs_7_), channel_id=1, source_target_pairs={{0,4},{1,5},{2,6},{3,7},{4,0},{5,1},{6,2},{7,3},{8,12},{9,13},{10,... | collective-permute-start | bytes 663560 | tf_op jit(solution)/shard_map/ppermute | solution.py:298
  29.8 1.4 %collective-permute-start.11 = (bf16[96,768]{1,0:T(8,128)(2,1)S(1)}, bf16[96,768]{1,0:T(8,128)(2,1)S(1)}, u32[]{:S(2)}, u32[]{:S(2)}) collective-permute-start(bf16[96,768]{1,0:T(8,128)(2,1)S(1)} %get-tuple-element.39.refs_5_), channel_id=1, source_target_pairs={{0,1},{1,0},{2,3},{3,2},{4,5},{5,4},{6,7},{7,6},{8,9},{9,8},{10,11... | collective-permute-start | bytes 442376 | tf_op jit(solution)/shard_map/ppermute | solution.py:301
  29.9 2.5 %collective-permute-start.12 = (bf16[96,768]{1,0:T(8,128)(2,1)S(1)}, bf16[96,768]{1,0:T(8,128)(2,1)S(1)}, u32[]{:S(2)}, u32[]{:S(2)}) collective-permute-start(bf16[96,768]{1,0:T(8,128)(2,1)S(1)} %get-tuple-element.40.refs_6_), channel_id=1, source_target_pairs={{0,1},{1,0},{2,3},{3,2},{4,5},{5,4},{6,7},{7,6},{8,9},{9,8},{10,11... | collective-permute-start | bytes 442376 | tf_op jit(solution)/shard_map/ppermute | solution.py:301
  30.4 2.0 %collective-permute-start.13 = (bf16[96,768]{1,0:T(8,128)(2,1)S(1)}, bf16[96,768]{1,0:T(8,128)(2,1)S(1)}, u32[]{:S(2)}, u32[]{:S(2)}) collective-permute-start(bf16[96,768]{1,0:T(8,128)(2,1)S(1)} %get-tuple-element.41.refs_7_), channel_id=1, source_target_pairs={{0,1},{1,0},{2,3},{3,2},{4,5},{5,4},{6,7},{7,6},{8,9},{9,8},{10,11... | collective-permute-start | bytes 442376 | tf_op jit(solution)/shard_map/ppermute | solution.py:301
  30.5 2.0 %collective-permute-start.14 = (bf16[96,768]{1,0:T(8,128)(2,1)S(1)}, bf16[96,768]{1,0:T(8,128)(2,1)S(1)}, u32[]{:S(2)}, u32[]{:S(2)}) collective-permute-start(bf16[96,768]{1,0:T(8,128)(2,1)S(1)} %get-tuple-element.42.refs_8_), channel_id=1, source_target_pairs={{0,1},{1,0},{2,3},{3,2},{4,5},{5,4},{6,7},{7,6},{8,9},{9,8},{10,11... | collective-permute-start | bytes 442376 | tf_op jit(solution)/shard_map/ppermute | solution.py:301
  31.2 8.3 %collective-permute-start.16 = (bf16[144,768]{1,0:T(8,128)(2,1)S(1)}, bf16[144,768]{1,0:T(8,128)(2,1)S(1)}, u32[]{:S(2)}, u32[]{:S(2)}) collective-permute-start(bf16[144,768]{1,0:T(8,128)(2,1)S(1)} %collective-permute-done.1.refs_0_.refs_2_.refs_7_), channel_id=1, source_target_pairs={{0,2},{1,3},{2,0},{3,1},{4,6},{5,7},{6,4},{7,5},{8,10},{9,11},{10,... | collective-permute-start | bytes 663560 | tf_op jit(solution)/shard_map/ppermute | solution.py:298
  34.3 9.2 %collective-permute-start.15 = (bf16[144,768]{1,0:T(8,128)(2,1)S(1)}, bf16[144,768]{1,0:T(8,128)(2,1)S(1)}, u32[]{:S(2)}, u32[]{:S(2)}) collective-permute-start(bf16[144,768]{1,0:T(8,128)(2,1)S(1)} %collective-permute-done.8.refs_1_.refs_9_), channel_id=1, source_target_pairs={{0,2},{1,3},{2,0},{3,1},{4,6},{5,7},{6,4},{7,5},{8,10},{9,11},{10,... | collective-permute-start | bytes 663560 | tf_op jit(solution)/shard_map/ppermute | solution.py:298
  36.9 6.5 %copy-start = (f32[15360]{0:T(1024)S(1)}, f32[15360]{0:T(1024)}, u32[]{:S(2)}) copy-start(f32[15360]{0:T(1024)} %param.18) | copy-start | bytes 184324
  45.6 1.3 %collective-permute-start.17 = (bf16[8,32,128]{2,1,0:T(8,128)(2,1)S(1)}, bf16[8,32,128]{2,1,0:T(8,128)(2,1)S(1)}, u32[]{:S(2)}, u32[]{:S(2)}) collective-permute-start(bf16[8,32,128]{2,1,0:T(8,128)(2,1)S(1)} %get-tuple-element.55), channel_id=1, source_target_pairs={{0,1},{1,0},{2,3},{3,2},{4,5},{5,4},{6,7},{7,6},{8,9},{9,8},{10,11... | collective-permute-start | bytes 196616 | tf_op jit(solution)/shard_map/ppermute | solution.py:301

commit v18 on v17

--- a/solution.py
+++ b/solution.py
@@ -184,23 +184,20 @@
         copy.wait()
 
 
-def first_kernel(seq, masks, *refs):
+def first_kernel(seq, shard, masks, *refs):
     me_ref, docs, tables, refs = refs[0], refs[1:3], refs[3:5], refs[5:]
-    count = len(masks) // 2
+    count = len(masks) * shard // seq
     parts, others, refs = refs[:count], refs[count : 2 * count], refs[2 * count :]
     params, halves, refs = refs[0], refs[1:3], refs[3:]
     bests, weight = refs[:2], refs[2]
     me = me_ref[0]
     core = me % 2
-    rows = weight.shape[0] // (2 * len(masks))
-    for k, mask in enumerate(masks):
-        chip = (me // 2) ^ mask
-        part, place = divmod(k * rows, parts[0].shape[0])
-        block = slice(place, place + rows)
-        at = pl.multiple_of((2 * chip + core) * rows, SLOT_ROWS)
-        weight[pl.ds(at, rows), :] = parts[part][block, :]
-        at = pl.multiple_of((2 * chip + 1 - core) * rows, SLOT_ROWS)
-        weight[pl.ds(at, rows), :] = others[part][block, :]
+    for at in range(0, len(masks) * shard, SLOT_ROWS):
+        (k, inside), (part, place) = divmod(at, shard), divmod(at, seq)
+        chip = (me // 2) ^ masks[k]
+        for whose, sources in ((core, parts), (1 - core, others)):
+            to = pl.multiple_of((2 * chip + whose) * shard + inside, SLOT_ROWS)
+            weight[pl.ds(to, SLOT_ROWS), :] = sources[part][place : place + SLOT_ROWS, :]
     keep_tops(normed_rows(docs, tables, seq, weight, params), halves, bests)
 
 
@@ -362,13 +359,12 @@
         stay(norm_gain),
         stay(norm_bias),
     )
-    near = (block, after(block_2, block_6, docs[1]), table)
-    near_pile = cross(pile(near, ((0, rows), (0, rows), (0, SLOT_ROWS))), 1)
-    one, two = (0, rows), (0, 2 * rows)
     one, two, below = (0, rows), (0, 2 * rows), (0, SLOT_ROWS)
+    near = pile((block, after(block_2, block_6, docs[1]), table), (one, one, below))
+    near_pile = cross(near, 1)
     block_4 = cross(pile((block_6, table), (one, below)), 2)
     docs[6] = cross(after(load, block_6), 6)
-    load_1 = pile((docs[1], near_pile), ((0, seq), (2 * rows, SLOT_ROWS)))
+    docs[3] = cross(after(docs[2], near), 1)
     far_from = [stay(after(weight_rows, table))]
     [mine] = pl.pallas_call(
         lambda *refs: fetch_kernel(1, *refs),
@@ -378,22 +374,23 @@
         scratch_shapes=[pltpu.SemaphoreType.DMA((1,))],
         compiler_params=limit,
     )(table, *far_from)
-    far = (block_6, after(block_4, near_pile, docs[2], mine, theirs))
-    far = pile(far, (one, one))
+    far = (block_6, after(block_4, near_pile, mine, theirs))
+    far = pile(far, (one, (0, rows + SLOT_ROWS)))
     far_pile = cross(far, 1)
-    docs[3] = cross(after(load_1, far), 2)
     docs[4] = cross(after(docs[6], far), 2)
     docs[7] = cross(docs[6], 1)
-    late = (docs[6], docs[3])
-    sources = (after(block, *late), block_2, block_6, block_4, near_pile, far_pile)
-    packed = pile(sources, (one, one, one, one, two, two), (2 * rows,) * (chips // 2))
+    sources = (after(block, docs[6], docs[3]), block_2, block_6, block_4, near_pile, far_pile)
+    packed = pile(sources, (one, one, one, one, two, two), (seq,) * (chips * rows // seq))
     other_packed = [swap(part) for part in packed]
     block_masks = [0, 2, 6, 4, 1, 3, 7, 5]
 
-    masks = [0, 1, 2, 3, 6, 7, 4, 5]
+    masks = [6, 7, 0, 1, 2, 3, 4, 5]
+    docs[0] = load
+    docs[5] = cross(after(docs[4], docs[7], *other_packed), 1)
+    tables = docs | {1: near_pile, 2: block_4, 3: far_pile}
     best_shape = shape((8, half), jnp.float32)
     *best, weight = pl.pallas_call(
-        lambda *refs: first_kernel(seq, block_masks, *refs),
+        lambda *refs: first_kernel(seq, rows, block_masks, *refs),
         out_shape=[best_shape, best_shape, shape((width, width), jnp.bfloat16)],
         in_specs=[smem] + [vmem] * (7 + 2 * len(packed)),
         out_specs=[vmem] * 3,
@@ -401,18 +398,14 @@
         cost_estimate=cost(2),
     )(
         where,
-        load,
-        docs[1],
-        table,
-        near_pile,
+        *[docs[mask] for mask in masks[:2]],
+        *[tables[mask] for mask in masks[:2]],
         *packed,
         *other_packed,
         params,
         mine,
         theirs,
     )
-    docs |= {0: load, 5: cross(after(docs[4], weight), 1)}
-    tables = docs | {1: near_pile, 2: block_4}
     for first in range(2, len(masks) - 2, 2):
         pair = masks[first : first + 2]
         best += pl.pallas_call(

time: 57.9 us -> 52.8 us (0.912)
  waiting for transfers between devices: 18.9 us -> 12.8 us
  starting transfers between devices: 15.9 us -> 17 us
    ppermute x12, waiting for transfers between devices: 17.3 us -> 11.5 us  [cross(): lax.ppermute(value, 'doc', [(i, i ^ 2 * mask) for i in range(devices)])]
    ppermute x12, starting transfers between devices: 14.3 us -> 15.7 us  [cross(): lax.ppermute(value, 'doc', [(i, i ^ 2 * mask) for i in range(devices)])]
    ppermute x6 -> x5, starting transfers between devices: 1.67 us -> 1.24 us  [swap(): return lax.ppermute(value, 'doc', [(i, i ^ 1) for i in range(devices)])]
    ppermute x6 -> x5, waiting for transfers between devices: 1.6 us -> 1.25 us  [swap(): return lax.ppermute(value, 'doc', [(i, i ^ 1) for i in range(devices)])]
  transfers between devices with their start and end apart: 18 -> 17, of which waited for: 9 -> 8; matrix products, arithmetic and copies ran while one was open for 0% -> 0% of each run, Pallas kernels for 15% -> 16%
where the time goes in v18:
time: 52.8 us; the launch traced here: 52.6 us
  starting transfers between devices  17 us (32%)
  waiting for transfers between devices  12.8 us (24%)
  Pallas kernels  11.4 us (22%)
  blocking collectives  10 us (19%)
  between operations  1.41 us (3%)
    ppermute x12, starting transfers between devices, cross(): lax.ppermute(value, 'doc', [(i, i ^ 2 * mask) for i in range(devices)])  15.7 us
    ppermute x12, waiting for transfers between devices, cross(): lax.ppermute(value, 'doc', [(i, i ^ 2 * mask) for i in range(devices)])  11.5 us
    all_to_all x1, blocking collectives, move_tokens(): lax.all_to_all(merged, 'doc', split_axis=0, concat_axis=0, axis_index_gro...  10 us
    pallas_call x2, Pallas kernels, move_tokens(): pl.pallas_call(lambda *refs: next_kernel(seq, *refs), out_shape=[best_sha...  3.55 us
    pallas_call x1, Pallas kernels, move_tokens(): pl.pallas_call(lambda *refs: last_kernel(seq, masks, *refs), out_shape=[s...  2.11 us
    pallas_call x1, Pallas kernels, move_tokens(): pl.pallas_call(lambda *refs: first_kernel(seq, rows, block_masks, *refs),...  1.79 us
    pallas_call x1, Pallas kernels, move_tokens(): pl.pallas_call(start_kernel, out_shape=[shape((seq + SLOT_ROWS, width), j...  1.71 us
    pallas_call x1, Pallas kernels, move_tokens(): pl.pallas_call(lambda *refs: fetch_kernel(1, *refs), out_shape=[shape(val...  1.38 us
  transfers between devices with their start and end apart: 17, of which 8 were waited for; matrix products, arithmetic and copies ran while one was open for 0% of the time, Pallas kernels for 16%

profile of v18, /device:TPU:0, one launch (start us, length us, event | category | flops | bytes accessed | tf_op | source)
XLA Modules:
  0.0 52.6 jit_solution(2688711379274389555)
XLA Ops:
  0.6 0.5 collective-permute-start.6
  1.2 2.6 %collective-permute-start.4 = (bf16[128,768]{1,0:T(8,128)(2,1)}, bf16[128,768]{1,0:T(8,128)(2,1)S(1)}, u32[]{:S(2)}, u32[]{:S(2)}) collective-permute-start(bf16[128,768]{1,0:T(8,128)(2,1)} %refs_0_.1), channel_id=1, source_target_pairs={{0,2},{1,3},{2,0},{3,1},{4,6},{5,7},{6,4},{7,5},{8,10},{9,11},{10,... | collective-permute-start | bytes 589832 | tf_op jit(solution)/shard_map/ppermute | solution.py:295
  3.7 3.6 %collective-permute-start = (bf16[48,768]{1,0:T(8,128)(2,1)}, bf16[48,768]{1,0:T(8,128)(2,1)S(1)}, u32[]{:S(2)}, u32[]{:S(2)}) collective-permute-start(bf16[48,768]{1,0:T(8,128)(2,1)} %refs_1_.1), channel_id=1, source_target_pairs={{0,12},{1,13},{2,14},{3,15},{4,8},{5,9},{6,10},{7,11},{8,4},{9,5},... | collective-permute-start | bytes 221192 | tf_op jit(solution)/shard_map/ppermute | solution.py:295
  7.3 0.0 collective-permute-start.3
  7.3 2.0 %collective-permute-start.9 = (bf16[128,768]{1,0:T(8,128)(2,1)}, bf16[128,768]{1,0:T(8,128)(2,1)S(1)}, u32[]{:S(2)}, u32[]{:S(2)}) collective-permute-start(bf16[128,768]{1,0:T(8,128)(2,1)} %refs_0_.1), channel_id=1, source_target_pairs={{0,4},{1,5},{2,6},{3,7},{4,0},{5,1},{6,2},{7,3},{8,12},{9,13},{10,... | collective-permute-start | bytes 589832 | tf_op jit(solution)/shard_map/ppermute | solution.py:295
  10.0 1.7 %shard_map.122 = (bf16[144,768]{1,0:T(8,128)(2,1)S(1)}, bf16[48,768]{1,0:T(8,128)(2,1)S(1)}, bf16[16,768]{1,0:T(8,128)(2,1)S(1)}, f32[8,768]{1,0:T(8,128)S(1)}) custom-call(s32[1]{0:T(128)} %bitcast.me_ref.refs_0_, s32[1,1,32]{2,1,0:T(1,128)} %tiles_ref.1, s32[1,1,32]{2,1,0:T(1,128)} %bitcast.9, s32[1,1,32]{2,1,0:T(1,128)} %slots_ref.1, ...), custom_call_target="tpu_custom_call" | custom-call | tf_op jit(solution)/shard_map/pallas_call | solution.py:335
  11.7 0.0 collective-permute-done.refs_0_.refs_2_
  11.7 1.0 %collective-permute-done.3.refs_1_ = bf16[48,768]{1,0:T(8,128)(2,1)S(1)} collective-permute-done((bf16[48,768]{1,0:T(8,128)(2,1)}, bf16[48,768]{1,0:T(8,128)(2,1)S(1)}, u32[]{:S(2)}, u32[]{:S(2)}) %collective-permute-start.3) | collective-permute-done | bytes 73760 | tf_op jit(solution)/shard_map/ppermute | solution.py:295
  12.7 0.0 collective-permute-done.4.refs_1_
  12.7 0.6 %collective-permute-start.5 = (bf16[112,768]{1,0:T(8,128)(2,1)S(1)}, bf16[112,768]{1,0:T(8,128)(2,1)S(1)}, u32[]{:S(2)}, u32[]{:S(2)}) collective-permute-start(bf16[112,768]{1,0:T(8,128)(2,1)S(1)} %shard_map.124), channel_id=1, source_target_pairs={{0,2},{1,3},{2,0},{3,1},{4,6},{5,7},{6,4},{7,5},{8,10},{9,11},{10,... | collective-permute-start | bytes 516104 | tf_op jit(solution)/shard_map/ppermute | solution.py:295
  13.3 1.6 %collective-permute-start.2 = (bf16[64,768]{1,0:T(8,128)(2,1)S(1)}, bf16[64,768]{1,0:T(8,128)(2,1)S(1)}, u32[]{:S(2)}, u32[]{:S(2)}) collective-permute-start(bf16[64,768]{1,0:T(8,128)(2,1)S(1)} %shard_map.123), channel_id=1, source_target_pairs={{0,4},{1,5},{2,6},{3,7},{4,0},{5,1},{6,2},{7,3},{8,12},{9,13},{10,... | collective-permute-start | bytes 294920 | tf_op jit(solution)/shard_map/ppermute | solution.py:295
  14.9 0.5 collective-permute-start.1
  15.4 1.5 %collective-permute-done.9.refs_0_ = bf16[128,768]{1,0:T(8,128)(2,1)S(1)} collective-permute-done((bf16[128,768]{1,0:T(8,128)(2,1)}, bf16[128,768]{1,0:T(8,128)(2,1)S(1)}, u32[]{:S(2)}, u32[]{:S(2)}) %collective-permute-start.9) | collective-permute-done | bytes 196640 | tf_op jit(solution)/shard_map/ppermute | solution.py:295
  16.9 0.4 collective-permute-start.10
  17.3 1.4 %shard_map.125.refs_12_.refs_6_.refs_13_ = bf16[960,768]{1,0:T(8,128)(2,1)S(1)} custom-call(bf16[16,768]{1,0:T(8,128)(2,1)S(1)} %get-tuple-element.30.refs_1_.refs_2_.refs_0_, bf16[960,768]{1,0:T(8,128)(2,1)} %bitcast.8), custom_call_target="tpu_custom_call" | custom-call | tf_op jit(solution)/shard_map/pallas_call | solution.py:369
  18.7 4.4 %collective-permute-done.2.refs_1_.refs_3_.refs_2_.refs_7_ = bf16[64,768]{1,0:T(8,128)(2,1)S(1)} collective-permute-done((bf16[64,768]{1,0:T(8,128)(2,1)S(1)}, bf16[64,768]{1,0:T(8,128)(2,1)S(1)}, u32[]{:S(2)}, u32[]{:S(2)}) %collective-permute-start.2) | collective-permute-done | bytes 98336 | tf_op jit(solution)/shard_map/ppermute | solution.py:295
  23.1 0.0 collective-permute-done.5.refs_4_.refs_3_.refs_6_
  23.1 0.0 collective-permute-done.6.refs_13_.refs_7_.refs_14_
  23.1 0.1 collective-permute-start.11
  23.2 0.0 collective-permute-done.1.refs_1_.refs_3_
  23.2 2.0 %collective-permute-start.8 = (bf16[144,768]{1,0:T(8,128)(2,1)S(1)}, bf16[144,768]{1,0:T(8,128)(2,1)S(1)}, u32[]{:S(2)}, u32[]{:S(2)}) collective-permute-start(bf16[144,768]{1,0:T(8,128)(2,1)S(1)} %collective-permute-done.1.refs_1_.refs_3_), channel_id=1, source_target_pairs={{0,2},{1,3},{2,0},{3,1},{4,6},{5,7},{6,4},{7,5},{8,10},{9,11},{10,... | collective-permute-start | bytes 663560 | tf_op jit(solution)/shard_map/ppermute | solution.py:295
  25.2 2.0 %collective-permute-start.7 = (bf16[144,768]{1,0:T(8,128)(2,1)S(1)}, bf16[144,768]{1,0:T(8,128)(2,1)S(1)}, u32[]{:S(2)}, u32[]{:S(2)}) collective-permute-start(bf16[144,768]{1,0:T(8,128)(2,1)S(1)} %collective-permute-done.1.refs_1_.refs_3_), channel_id=1, source_target_pairs={{0,4},{1,5},{2,6},{3,7},{4,0},{5,1},{6,2},{7,3},{8,12},{9,13},{10,... | collective-permute-start | bytes 663560 | tf_op jit(solution)/shard_map/ppermute | solution.py:295
  27.1 0.0 collective-permute-done.10.refs_1_
  27.1 1.5 %collective-permute-done.11.refs_5_.refs_3_.refs_8_ = bf16[112,768]{1,0:T(8,128)(2,1)S(1)} collective-permute-done((bf16[112,768]{1,0:T(8,128)(2,1)S(1)}, bf16[112,768]{1,0:T(8,128)(2,1)S(1)}, u32[]{:S(2)}, u32[]{:S(2)}) %collective-permute-start.11) | collective-permute-done | bytes 172064 | tf_op jit(solution)/shard_map/ppermute | solution.py:295
  28.7 0.1 collective-permute-start.12
  28.7 0.5 collective-permute-start.13
  29.2 0.1 collective-permute-start.14
  29.3 1.7 %collective-permute-done.8.refs_2_.refs_4_ = bf16[144,768]{1,0:T(8,128)(2,1)S(1)} collective-permute-done((bf16[144,768]{1,0:T(8,128)(2,1)S(1)}, bf16[144,768]{1,0:T(8,128)(2,1)S(1)}, u32[]{:S(2)}, u32[]{:S(2)}) %collective-permute-start.8) | collective-permute-done | bytes 221216 | tf_op jit(solution)/shard_map/ppermute | solution.py:295
  31.0 0.1 collective-permute-done.7.refs_1_.refs_9_
  31.1 0.0 collective-permute-done.12.refs_8_
  31.1 0.0 collective-permute-done.13.refs_9_
  31.1 0.0 collective-permute-done.14.refs_10_
  31.1 0.4 collective-permute-start.15
  31.5 1.8 %shard_map.128 = (f32[8,960]{1,0:T(8,128)S(1)}, f32[8,960]{1,0:T(8,128)S(1)}, bf16[768,768]{1,0:T(8,128)(2,1)S(1)}) custom-call(s32[1]{0:T(128)} %bitcast.me_ref.refs_0_, bf16[144,768]{1,0:T(8,128)(2,1)S(1)} %collective-permute-done.1.refs_1_.refs_3_, bf16[144,768]{1,0:T(8,128)(2,1)S(1)} %collective-permute-done.8.refs_2_.refs_4_, ...), custom_call_target="tpu_custom_call" | custom-call | flops 2 | bytes 2 | tf_op jit(solution)/shard_map/pallas_call | solution.py:392
  33.3 1.8 %shard_map.129 = (f32[8,960]{1,0:T(8,128)S(1)}, f32[8,960]{1,0:T(8,128)S(1)}) custom-call(bf16[144,768]{1,0:T(8,128)(2,1)S(1)} %get-tuple-element.29.refs_0_.refs_2_.refs_5_, bf16[128,768]{1,0:T(8,128)(2,1)S(1)} %collective-permute-done.4.refs_1_, bf16[144,768]{1,0:T(8,128)(2,1)S(1)} %get-tuple-element.29.refs_0_.refs_2_.refs_5_, ...), custom_call_target="tpu_custom_call" | custom-call | flops 2 | bytes 2 | tf_op jit(solution)/shard_map/pallas_call | solution.py:411
  35.1 0.0 copy-start
  35.1 1.8 %shard_map.130 = (f32[8,960]{1,0:T(8,128)S(1)}, f32[8,960]{1,0:T(8,128)S(1)}) custom-call(bf16[128,768]{1,0:T(8,128)(2,1)S(1)} %collective-permute-done.9.refs_0_, bf16[128,768]{1,0:T(8,128)(2,1)S(1)} %collective-permute-done.10.refs_1_, bf16[64,768]{1,0:T(8,128)(2,1)S(1)} %collective-permute-done.2.refs_1_.refs_3_.refs_2_.refs_7_, ...), custom_call_target="tpu_custom_call" | custom-call | flops 2 | bytes 2 | tf_op jit(solution)/shard_map/pallas_call | solution.py:411
  36.9 1.4 %collective-permute-done.15.refs_2_.refs_10_ = bf16[144,768]{1,0:T(8,128)(2,1)S(1)} collective-permute-done((bf16[144,768]{1,0:T(8,128)(2,1)S(1)}, bf16[144,768]{1,0:T(8,128)(2,1)S(1)}, u32[]{:S(2)}, u32[]{:S(2)}) %collective-permute-start.15) | collective-permute-done | bytes 221216 | tf_op jit(solution)/shard_map/ppermute | solution.py:295
  38.3 0.0 copy-done
  38.3 2.1 %shard_map.131 = (bf16[8,48,128]{2,1,0:T(8,128)(2,1)S(1)}, bf16[8,32,128]{2,1,0:T(8,128)(2,1)S(1)}) custom-call(s32[1]{0:T(128)} %bitcast.me_ref.refs_0_, bf16[144,768]{1,0:T(8,128)(2,1)S(1)} %collective-permute-done.7.refs_1_.refs_9_, bf16[144,768]{1,0:T(8,128)(2,1)S(1)} %collective-permute-done.15.refs_2_.refs_10_, ...), custom_call_target="tpu_custom_call" | custom-call | flops 2 | bytes 2 | tf_op jit(solution)/shard_map/pallas_call | solution.py:427
  40.4 0.1 collective-permute-start.16
  40.5 1.2 %collective-permute-done.16.got_ref = bf16[8,32,128]{2,1,0:T(8,128)(2,1)S(1)} collective-permute-done((bf16[8,32,128]{2,1,0:T(8,128)(2,1)S(1)}, bf16[8,32,128]{2,1,0:T(8,128)(2,1)S(1)}, u32[]{:S(2)}, u32[]{:S(2)}) %collective-permute-start.16) | collective-permute-done | bytes 65568 | tf_op jit(solution)/shard_map/ppermute | solution.py:298
  41.8 10.0 %all_to_all.5.refs_0_ = bf16[8,48,128]{2,1,0:T(8,128)(2,1)S(1)} all-to-all(bf16[8,48,128]{2,1,0:T(8,128)(2,1)S(1)} %shard_map.132), channel_id=1, replica_groups={{0,2,4,6,8,10,12,14},{1,3,5,7,9,11,13,15},{16,18,20,22,24,26,28,30},{17..., dimensions={0} | all-to-all | bytes 196608 | tf_op jit(solution)/shard_map/all_to_all | solution.py:457
  51.8 0.8 %shard_map.133 = (bf16[1,15360]{1,0:T(2,128)(2,1)}, bf16[2,15360]{1,0:T(2,128)(2,1)}) custom-call(bf16[8,48,128]{2,1,0:T(8,128)(2,1)S(1)} %all_to_all.5.refs_0_), custom_call_target="tpu_custom_call" | custom-call | tf_op jit(solution)/shard_map/pallas_call | solution.py:460
  (5 shorter events, 0.1 us)
Async XLA Ops:
  0.6 22.4 %collective-permute-start.6 = (bf16[960,768]{1,0:T(8,128)(2,1)}, bf16[960,768]{1,0:T(8,128)(2,1)S(1)}, u32[]{:S(2)}, u32[]{:S(2)}) collective-permute-start(bf16[960,768]{1,0:T(8,128)(2,1)} %bitcast.7), channel_id=1, source_target_pairs={{0,1},{1,0},{2,3},{3,2},{4,5},{5,4},{6,7},{7,6},{8,9},{9,8},{10,11... | collective-permute-start | bytes 4423688 | tf_op jit(solution)/shard_map/ppermute | solution.py:298
  1.2 11.5 %collective-permute-start.4 = (bf16[128,768]{1,0:T(8,128)(2,1)}, bf16[128,768]{1,0:T(8,128)(2,1)S(1)}, u32[]{:S(2)}, u32[]{:S(2)}) collective-permute-start(bf16[128,768]{1,0:T(8,128)(2,1)} %refs_0_.1), channel_id=1, source_target_pairs={{0,2},{1,3},{2,0},{3,1},{4,6},{5,7},{6,4},{7,5},{8,10},{9,11},{10,... | collective-permute-start | bytes 589832 | tf_op jit(solution)/shard_map/ppermute | solution.py:295
  3.7 8.0 %collective-permute-start = (bf16[48,768]{1,0:T(8,128)(2,1)}, bf16[48,768]{1,0:T(8,128)(2,1)S(1)}, u32[]{:S(2)}, u32[]{:S(2)}) collective-permute-start(bf16[48,768]{1,0:T(8,128)(2,1)} %refs_1_.1), channel_id=1, source_target_pairs={{0,12},{1,13},{2,14},{3,15},{4,8},{5,9},{6,10},{7,11},{8,4},{9,5},... | collective-permute-start | bytes 221192 | tf_op jit(solution)/shard_map/ppermute | solution.py:295
  7.3 5.4 %collective-permute-start.3 = (bf16[48,768]{1,0:T(8,128)(2,1)}, bf16[48,768]{1,0:T(8,128)(2,1)S(1)}, u32[]{:S(2)}, u32[]{:S(2)}) collective-permute-start(bf16[48,768]{1,0:T(8,128)(2,1)} %refs_1_.1), channel_id=1, source_target_pairs={{0,4},{1,5},{2,6},{3,7},{4,0},{5,1},{6,2},{7,3},{8,12},{9,13},{10,... | collective-permute-start | bytes 221192 | tf_op jit(solution)/shard_map/ppermute | solution.py:295
  7.3 9.6 %collective-permute-start.9 = (bf16[128,768]{1,0:T(8,128)(2,1)}, bf16[128,768]{1,0:T(8,128)(2,1)S(1)}, u32[]{:S(2)}, u32[]{:S(2)}) collective-permute-start(bf16[128,768]{1,0:T(8,128)(2,1)} %refs_0_.1), channel_id=1, source_target_pairs={{0,4},{1,5},{2,6},{3,7},{4,0},{5,1},{6,2},{7,3},{8,12},{9,13},{10,... | collective-permute-start | bytes 589832 | tf_op jit(solution)/shard_map/ppermute | solution.py:295
  12.7 10.4 %collective-permute-start.5 = (bf16[112,768]{1,0:T(8,128)(2,1)S(1)}, bf16[112,768]{1,0:T(8,128)(2,1)S(1)}, u32[]{:S(2)}, u32[]{:S(2)}) collective-permute-start(bf16[112,768]{1,0:T(8,128)(2,1)S(1)} %shard_map.124), channel_id=1, source_target_pairs={{0,2},{1,3},{2,0},{3,1},{4,6},{5,7},{6,4},{7,5},{8,10},{9,11},{10,... | collective-permute-start | bytes 516104 | tf_op jit(solution)/shard_map/ppermute | solution.py:295
  13.3 9.7 %collective-permute-start.2 = (bf16[64,768]{1,0:T(8,128)(2,1)S(1)}, bf16[64,768]{1,0:T(8,128)(2,1)S(1)}, u32[]{:S(2)}, u32[]{:S(2)}) collective-permute-start(bf16[64,768]{1,0:T(8,128)(2,1)S(1)} %shard_map.123), channel_id=1, source_target_pairs={{0,4},{1,5},{2,6},{3,7},{4,0},{5,1},{6,2},{7,3},{8,12},{9,13},{10,... | collective-permute-start | bytes 294920 | tf_op jit(solution)/shard_map/ppermute | solution.py:295
  14.9 8.3 %collective-permute-start.1 = (bf16[144,768]{1,0:T(8,128)(2,1)S(1)}, bf16[144,768]{1,0:T(8,128)(2,1)S(1)}, u32[]{:S(2)}, u32[]{:S(2)}) collective-permute-start(bf16[144,768]{1,0:T(8,128)(2,1)S(1)} %get-tuple-element.29.refs_0_.refs_2_.refs_5_), channel_id=1, source_target_pairs={{0,12},{1,13},{2,14},{3,15},{4,8},{5,9},{6,10},{7,11},{8,4},{9,5},... | collective-permute-start | bytes 663560 | tf_op jit(solution)/shard_map/ppermute | solution.py:295
  16.9 10.2 %collective-permute-start.10 = (bf16[128,768]{1,0:T(8,128)(2,1)S(1)}, bf16[128,768]{1,0:T(8,128)(2,1)S(1)}, u32[]{:S(2)}, u32[]{:S(2)}) collective-permute-start(bf16[128,768]{1,0:T(8,128)(2,1)S(1)} %collective-permute-done.9.refs_0_), channel_id=1, source_target_pairs={{0,2},{1,3},{2,0},{3,1},{4,6},{5,7},{6,4},{7,5},{8,10},{9,11},{10,... | collective-permute-start | bytes 589832 | tf_op jit(solution)/shard_map/ppermute | solution.py:295
  23.1 5.5 %collective-permute-start.11 = (bf16[112,768]{1,0:T(8,128)(2,1)S(1)}, bf16[112,768]{1,0:T(8,128)(2,1)S(1)}, u32[]{:S(2)}, u32[]{:S(2)}) collective-permute-start(bf16[112,768]{1,0:T(8,128)(2,1)S(1)} %shard_map.126), channel_id=1, source_target_pairs={{0,2},{1,3},{2,0},{3,1},{4,6},{5,7},{6,4},{7,5},{8,10},{9,11},{10,... | collective-permute-start | bytes 516104 | tf_op jit(solution)/shard_map/ppermute | solution.py:295
  23.2 7.8 %collective-permute-start.8 = (bf16[144,768]{1,0:T(8,128)(2,1)S(1)}, bf16[144,768]{1,0:T(8,128)(2,1)S(1)}, u32[]{:S(2)}, u32[]{:S(2)}) collective-permute-start(bf16[144,768]{1,0:T(8,128)(2,1)S(1)} %collective-permute-done.1.refs_1_.refs_3_), channel_id=1, source_target_pairs={{0,2},{1,3},{2,0},{3,1},{4,6},{5,7},{6,4},{7,5},{8,10},{9,11},{10,... | collective-permute-start | bytes 663560 | tf_op jit(solution)/shard_map/ppermute | solution.py:295
  25.2 5.9 %collective-permute-start.7 = (bf16[144,768]{1,0:T(8,128)(2,1)S(1)}, bf16[144,768]{1,0:T(8,128)(2,1)S(1)}, u32[]{:S(2)}, u32[]{:S(2)}) collective-permute-start(bf16[144,768]{1,0:T(8,128)(2,1)S(1)} %collective-permute-done.1.refs_1_.refs_3_), channel_id=1, source_target_pairs={{0,4},{1,5},{2,6},{3,7},{4,0},{5,1},{6,2},{7,3},{8,12},{9,13},{10,... | collective-permute-start | bytes 663560 | tf_op jit(solution)/shard_map/ppermute | solution.py:295
  28.7 2.4 %collective-permute-start.12 = (bf16[128,768]{1,0:T(8,128)(2,1)S(1)}, bf16[128,768]{1,0:T(8,128)(2,1)S(1)}, u32[]{:S(2)}, u32[]{:S(2)}) collective-permute-start(bf16[128,768]{1,0:T(8,128)(2,1)S(1)} %get-tuple-element.38.refs_5_), channel_id=1, source_target_pairs={{0,1},{1,0},{2,3},{3,2},{4,5},{5,4},{6,7},{7,6},{8,9},{9,8},{10,11... | collective-permute-start | bytes 589832 | tf_op jit(solution)/shard_map/ppermute | solution.py:298
  28.7 2.4 %collective-permute-start.13 = (bf16[128,768]{1,0:T(8,128)(2,1)S(1)}, bf16[128,768]{1,0:T(8,128)(2,1)S(1)}, u32[]{:S(2)}, u32[]{:S(2)}) collective-permute-start(bf16[128,768]{1,0:T(8,128)(2,1)S(1)} %get-tuple-element.39.refs_6_), channel_id=1, source_target_pairs={{0,1},{1,0},{2,3},{3,2},{4,5},{5,4},{6,7},{7,6},{8,9},{9,8},{10,11... | collective-permute-start | bytes 589832 | tf_op jit(solution)/shard_map/ppermute | solution.py:298
  29.2 1.9 %collective-permute-start.14 = (bf16[128,768]{1,0:T(8,128)(2,1)S(1)}, bf16[128,768]{1,0:T(8,128)(2,1)S(1)}, u32[]{:S(2)}, u32[]{:S(2)}) collective-permute-start(bf16[128,768]{1,0:T(8,128)(2,1)S(1)} %get-tuple-element.40.refs_7_), channel_id=1, source_target_pairs={{0,1},{1,0},{2,3},{3,2},{4,5},{5,4},{6,7},{7,6},{8,9},{9,8},{10,11... | collective-permute-start | bytes 589832 | tf_op jit(solution)/shard_map/ppermute | solution.py:298
  31.1 7.2 %collective-permute-start.15 = (bf16[144,768]{1,0:T(8,128)(2,1)S(1)}, bf16[144,768]{1,0:T(8,128)(2,1)S(1)}, u32[]{:S(2)}, u32[]{:S(2)}) collective-permute-start(bf16[144,768]{1,0:T(8,128)(2,1)S(1)} %collective-permute-done.7.refs_1_.refs_9_), channel_id=1, source_target_pairs={{0,2},{1,3},{2,0},{3,1},{4,6},{5,7},{6,4},{7,5},{8,10},{9,11},{10,... | collective-permute-start | bytes 663560 | tf_op jit(solution)/shard_map/ppermute | solution.py:295
  35.1 3.2 %copy-start = (f32[15360]{0:T(1024)S(1)}, f32[15360]{0:T(1024)}, u32[]{:S(2)}) copy-start(f32[15360]{0:T(1024)} %param.18) | copy-start | bytes 184324
  40.4 1.3 %collective-permute-start.16 = (bf16[8,32,128]{2,1,0:T(8,128)(2,1)S(1)}, bf16[8,32,128]{2,1,0:T(8,128)(2,1)S(1)}, u32[]{:S(2)}, u32[]{:S(2)}) collective-permute-start(bf16[8,32,128]{2,1,0:T(8,128)(2,1)S(1)} %get-tuple-element.53), channel_id=1, source_target_pairs={{0,1},{1,0},{2,3},{3,2},{4,5},{5,4},{6,7},{7,6},{8,9},{9,8},{10,11... | collective-permute-start | bytes 196616 | tf_op jit(solution)/shard_map/ppermute | solution.py:298

commit v19 on v18

--- a/solution.py
+++ b/solution.py
@@ -377,14 +377,14 @@
     far = (block_6, after(block_4, near_pile, mine, theirs))
     far = pile(far, (one, (0, rows + SLOT_ROWS)))
     far_pile = cross(far, 1)
-    docs[4] = cross(after(docs[6], far), 2)
+    docs[4] = pile((cross(after(docs[6], far), 2),), ((0, seq + SLOT_ROWS),))
     docs[7] = cross(docs[6], 1)
     sources = (after(block, docs[6], docs[3]), block_2, block_6, block_4, near_pile, far_pile)
     packed = pile(sources, (one, one, one, one, two, two), (seq,) * (chips * rows // seq))
     other_packed = [swap(part) for part in packed]
     block_masks = [0, 2, 6, 4, 1, 3, 7, 5]
 
-    masks = [6, 7, 0, 1, 2, 3, 4, 5]
+    masks = [0, 1, 2, 3, 6, 7, 4, 5]
     docs[0] = load
     docs[5] = cross(after(docs[4], docs[7], *other_packed), 1)
     tables = docs | {1: near_pile, 2: block_4, 3: far_pile}

time: 52.8 us -> 54 us (1.023)
  starting transfers between devices: 17 us -> 17.7 us
    ppermute x12, starting transfers between devices: 15.7 us -> 16.5 us  [cross(): lax.ppermute(value, 'doc', [(i, i ^ 2 * mask) for i in range(devices)])]
  transfers between devices with their start and end apart: 17 -> 17, of which waited for: 8 -> 7; matrix products, arithmetic and copies ran while one was open for 0% -> 0% of each run, Pallas kernels for 16% -> 16%
where the time goes in v19:
time: 54 us; the launch traced here: 53.8 us
  starting transfers between devices  17.7 us (33%)
  waiting for transfers between devices  13.2 us (24%)
  Pallas kernels  11.4 us (21%)
  blocking collectives  10 us (19%)
  between operations  1.41 us (3%)
    ppermute x12, starting transfers between devices, cross(): lax.ppermute(value, 'doc', [(i, i ^ 2 * mask) for i in range(devices)])  16.5 us
    ppermute x12, waiting for transfers between devices, cross(): lax.ppermute(value, 'doc', [(i, i ^ 2 * mask) for i in range(devices)])  11.9 us
    all_to_all x1, blocking collectives, move_tokens(): lax.all_to_all(merged, 'doc', split_axis=0, concat_axis=0, axis_index_gro...  10 us
    pallas_call x2, Pallas kernels, move_tokens(): pl.pallas_call(lambda *refs: next_kernel(seq, *refs), out_shape=[best_sha...  3.54 us
    pallas_call x1, Pallas kernels, move_tokens(): pl.pallas_call(lambda *refs: last_kernel(seq, masks, *refs), out_shape=[s...  2.12 us
    pallas_call x1, Pallas kernels, move_tokens(): pl.pallas_call(lambda *refs: first_kernel(seq, rows, block_masks, *refs),...  1.79 us
    pallas_call x1, Pallas kernels, move_tokens(): pl.pallas_call(start_kernel, out_shape=[shape((seq + SLOT_ROWS, width), j...  1.71 us
    pallas_call x1, Pallas kernels, move_tokens(): pl.pallas_call(lambda *refs: fetch_kernel(1, *refs), out_shape=[shape(val...  1.38 us
  transfers between devices with their start and end apart: 17, of which 7 were waited for; matrix products, arithmetic and copies ran while one was open for 0% of the time, Pallas kernels for 16%

profile of v19, /device:TPU:0, one launch (start us, length us, event | category | flops | bytes accessed | tf_op | source)
XLA Modules:
  0.0 53.8 jit_solution(2855380952453354695)
XLA Ops:
  0.6 0.5 collective-permute-start.6
  1.2 2.6 %collective-permute-start.4 = (bf16[128,768]{1,0:T(8,128)(2,1)}, bf16[128,768]{1,0:T(8,128)(2,1)S(1)}, u32[]{:S(2)}, u32[]{:S(2)}) collective-permute-start(bf16[128,768]{1,0:T(8,128)(2,1)} %refs_0_.1), channel_id=1, source_target_pairs={{0,2},{1,3},{2,0},{3,1},{4,6},{5,7},{6,4},{7,5},{8,10},{9,11},{10,... | collective-permute-start | bytes 589832 | tf_op jit(solution)/shard_map/ppermute | solution.py:295
  3.7 3.6 %collective-permute-start = (bf16[48,768]{1,0:T(8,128)(2,1)}, bf16[48,768]{1,0:T(8,128)(2,1)S(1)}, u32[]{:S(2)}, u32[]{:S(2)}) collective-permute-start(bf16[48,768]{1,0:T(8,128)(2,1)} %refs_1_.1), channel_id=1, source_target_pairs={{0,12},{1,13},{2,14},{3,15},{4,8},{5,9},{6,10},{7,11},{8,4},{9,5},... | collective-permute-start | bytes 221192 | tf_op jit(solution)/shard_map/ppermute | solution.py:295
  7.3 0.0 collective-permute-start.3
  7.3 2.0 %collective-permute-start.9 = (bf16[128,768]{1,0:T(8,128)(2,1)}, bf16[128,768]{1,0:T(8,128)(2,1)S(1)}, u32[]{:S(2)}, u32[]{:S(2)}) collective-permute-start(bf16[128,768]{1,0:T(8,128)(2,1)} %refs_0_.1), channel_id=1, source_target_pairs={{0,4},{1,5},{2,6},{3,7},{4,0},{5,1},{6,2},{7,3},{8,12},{9,13},{10,... | collective-permute-start | bytes 589832 | tf_op jit(solution)/shard_map/ppermute | solution.py:295
  10.0 1.7 %shard_map.122 = (bf16[144,768]{1,0:T(8,128)(2,1)S(1)}, bf16[48,768]{1,0:T(8,128)(2,1)S(1)}, bf16[16,768]{1,0:T(8,128)(2,1)S(1)}, f32[8,768]{1,0:T(8,128)S(1)}) custom-call(s32[1]{0:T(128)} %bitcast.me_ref.refs_0_, s32[1,1,32]{2,1,0:T(1,128)} %tiles_ref.1, s32[1,1,32]{2,1,0:T(1,128)} %bitcast.9, s32[1,1,32]{2,1,0:T(1,128)} %slots_ref.1, ...), custom_call_target="tpu_custom_call" | custom-call | tf_op jit(solution)/shard_map/pallas_call | solution.py:335
  11.7 0.0 collective-permute-done.refs_0_.refs_2_
  11.7 1.0 %collective-permute-done.3.refs_1_ = bf16[48,768]{1,0:T(8,128)(2,1)S(1)} collective-permute-done((bf16[48,768]{1,0:T(8,128)(2,1)}, bf16[48,768]{1,0:T(8,128)(2,1)S(1)}, u32[]{:S(2)}, u32[]{:S(2)}) %collective-permute-start.3) | collective-permute-done | bytes 73760 | tf_op jit(solution)/shard_map/ppermute | solution.py:295
  12.7 0.0 collective-permute-done.4.refs_2_
  12.7 0.6 %collective-permute-start.5 = (bf16[112,768]{1,0:T(8,128)(2,1)S(1)}, bf16[112,768]{1,0:T(8,128)(2,1)S(1)}, u32[]{:S(2)}, u32[]{:S(2)}) collective-permute-start(bf16[112,768]{1,0:T(8,128)(2,1)S(1)} %shard_map.124), channel_id=1, source_target_pairs={{0,2},{1,3},{2,0},{3,1},{4,6},{5,7},{6,4},{7,5},{8,10},{9,11},{10,... | collective-permute-start | bytes 516104 | tf_op jit(solution)/shard_map/ppermute | solution.py:295
  13.3 1.6 %collective-permute-start.2 = (bf16[64,768]{1,0:T(8,128)(2,1)S(1)}, bf16[64,768]{1,0:T(8,128)(2,1)S(1)}, u32[]{:S(2)}, u32[]{:S(2)}) collective-permute-start(bf16[64,768]{1,0:T(8,128)(2,1)S(1)} %shard_map.123), channel_id=1, source_target_pairs={{0,4},{1,5},{2,6},{3,7},{4,0},{5,1},{6,2},{7,3},{8,12},{9,13},{10,... | collective-permute-start | bytes 294920 | tf_op jit(solution)/shard_map/ppermute | solution.py:295
  14.9 0.5 collective-permute-start.1
  15.4 1.5 %collective-permute-done.9.refs_0_ = bf16[128,768]{1,0:T(8,128)(2,1)S(1)} collective-permute-done((bf16[128,768]{1,0:T(8,128)(2,1)}, bf16[128,768]{1,0:T(8,128)(2,1)S(1)}, u32[]{:S(2)}, u32[]{:S(2)}) %collective-permute-start.9) | collective-permute-done | bytes 196640 | tf_op jit(solution)/shard_map/ppermute | solution.py:295
  16.9 0.4 collective-permute-start.10
  17.3 1.4 %shard_map.125.refs_12_.refs_6_.refs_13_ = bf16[960,768]{1,0:T(8,128)(2,1)S(1)} custom-call(bf16[16,768]{1,0:T(8,128)(2,1)S(1)} %get-tuple-element.30.refs_1_.refs_2_.refs_0_, bf16[960,768]{1,0:T(8,128)(2,1)} %bitcast.8), custom_call_target="tpu_custom_call" | custom-call | tf_op jit(solution)/shard_map/pallas_call | solution.py:369
  18.7 4.4 %collective-permute-done.2.refs_1_.refs_3_.refs_2_.refs_5_ = bf16[64,768]{1,0:T(8,128)(2,1)S(1)} collective-permute-done((bf16[64,768]{1,0:T(8,128)(2,1)S(1)}, bf16[64,768]{1,0:T(8,128)(2,1)S(1)}, u32[]{:S(2)}, u32[]{:S(2)}) %collective-permute-start.2) | collective-permute-done | bytes 98336 | tf_op jit(solution)/shard_map/ppermute | solution.py:295
  23.1 0.0 collective-permute-done.5.refs_4_
  23.1 0.0 collective-permute-done.6.refs_13_.refs_7_.refs_14_
  23.1 0.1 collective-permute-start.11
  23.2 0.0 collective-permute-done.1.refs_0_.refs_2_.refs_7_
  23.2 2.4 %collective-permute-start.7 = (bf16[144,768]{1,0:T(8,128)(2,1)S(1)}, bf16[144,768]{1,0:T(8,128)(2,1)S(1)}, u32[]{:S(2)}, u32[]{:S(2)}) collective-permute-start(bf16[144,768]{1,0:T(8,128)(2,1)S(1)} %collective-permute-done.1.refs_0_.refs_2_.refs_7_), channel_id=1, source_target_pairs={{0,4},{1,5},{2,6},{3,7},{4,0},{5,1},{6,2},{7,3},{8,12},{9,13},{10,... | collective-permute-start | bytes 663560 | tf_op jit(solution)/shard_map/ppermute | solution.py:295
  25.5 1.6 %collective-permute-start.8 = (bf16[144,768]{1,0:T(8,128)(2,1)S(1)}, bf16[144,768]{1,0:T(8,128)(2,1)S(1)}, u32[]{:S(2)}, u32[]{:S(2)}) collective-permute-start(bf16[144,768]{1,0:T(8,128)(2,1)S(1)} %collective-permute-done.1.refs_0_.refs_2_.refs_7_), channel_id=1, source_target_pairs={{0,2},{1,3},{2,0},{3,1},{4,6},{5,7},{6,4},{7,5},{8,10},{9,11},{10,... | collective-permute-start | bytes 663560 | tf_op jit(solution)/shard_map/ppermute | solution.py:295
  27.1 0.0 collective-permute-done.10.refs_1_
  27.1 2.7 %collective-permute-done.11.refs_5_.refs_3_.refs_6_ = bf16[112,768]{1,0:T(8,128)(2,1)S(1)} collective-permute-done((bf16[112,768]{1,0:T(8,128)(2,1)S(1)}, bf16[112,768]{1,0:T(8,128)(2,1)S(1)}, u32[]{:S(2)}, u32[]{:S(2)}) %collective-permute-start.11) | collective-permute-done | bytes 172064 | tf_op jit(solution)/shard_map/ppermute | solution.py:295
  29.9 0.1 collective-permute-start.12
  29.9 0.5 collective-permute-start.13
  30.4 0.1 collective-permute-start.14
  30.5 0.0 collective-permute-done.7.refs_0_
  30.5 1.6 %collective-permute-done.8.refs_1_.refs_3_.refs_8_ = bf16[144,768]{1,0:T(8,128)(2,1)S(1)} collective-permute-done((bf16[144,768]{1,0:T(8,128)(2,1)S(1)}, bf16[144,768]{1,0:T(8,128)(2,1)S(1)}, u32[]{:S(2)}, u32[]{:S(2)}) %collective-permute-start.8) | collective-permute-done | bytes 221216 | tf_op jit(solution)/shard_map/ppermute | solution.py:295
  32.2 0.0 collective-permute-done.12.refs_8_
  32.2 0.0 collective-permute-done.13.refs_9_
  32.2 0.0 collective-permute-done.14.refs_10_
  32.2 1.2 %collective-permute-start.15 = (bf16[144,768]{1,0:T(8,128)(2,1)S(1)}, bf16[144,768]{1,0:T(8,128)(2,1)S(1)}, u32[]{:S(2)}, u32[]{:S(2)}) collective-permute-start(bf16[144,768]{1,0:T(8,128)(2,1)S(1)} %shard_map.127.refs_1_.refs_9_), channel_id=1, source_target_pairs={{0,2},{1,3},{2,0},{3,1},{4,6},{5,7},{6,4},{7,5},{8,10},{9,11},{10,... | collective-permute-start | bytes 663560 | tf_op jit(solution)/shard_map/ppermute | solution.py:295
  33.4 1.8 %shard_map.129 = (f32[8,960]{1,0:T(8,128)S(1)}, f32[8,960]{1,0:T(8,128)S(1)}, bf16[768,768]{1,0:T(8,128)(2,1)S(1)}) custom-call(s32[1]{0:T(128)} %bitcast.me_ref.refs_0_, bf16[144,768]{1,0:T(8,128)(2,1)S(1)} %get-tuple-element.29.refs_1_.refs_3_, bf16[128,768]{1,0:T(8,128)(2,1)S(1)} %collective-permute-done.4.refs_2_, ...), custom_call_target="tpu_custom_call" | custom-call | flops 2 | bytes 2 | tf_op jit(solution)/shard_map/pallas_call | solution.py:392
  35.2 1.8 %shard_map.130 = (f32[8,960]{1,0:T(8,128)S(1)}, f32[8,960]{1,0:T(8,128)S(1)}) custom-call(bf16[128,768]{1,0:T(8,128)(2,1)S(1)} %collective-permute-done.9.refs_0_, bf16[128,768]{1,0:T(8,128)(2,1)S(1)} %collective-permute-done.10.refs_1_, bf16[64,768]{1,0:T(8,128)(2,1)S(1)} %collective-permute-done.2.refs_1_.refs_3_.refs_2_.refs_5_, ...), custom_call_target="tpu_custom_call" | custom-call | flops 2 | bytes 2 | tf_op jit(solution)/shard_map/pallas_call | solution.py:411
  37.0 0.0 copy-start
  37.0 1.8 %shard_map.131 = (f32[8,960]{1,0:T(8,128)S(1)}, f32[8,960]{1,0:T(8,128)S(1)}) custom-call(bf16[144,768]{1,0:T(8,128)(2,1)S(1)} %collective-permute-done.1.refs_0_.refs_2_.refs_7_, bf16[144,768]{1,0:T(8,128)(2,1)S(1)} %collective-permute-done.8.refs_1_.refs_3_.refs_8_, bf16[144,768]{1,0:T(8,128)(2,1)S(1)} %collective-permute-done.1.refs_0_.refs_2_.refs_7_, ...), custom_call_target="tpu_custom_call" | custom-call | flops 2 | bytes 2 | tf_op jit(solution)/shard_map/pallas_call | solution.py:411
  38.7 0.8 %collective-permute-done.15.refs_2_.refs_10_ = bf16[144,768]{1,0:T(8,128)(2,1)S(1)} collective-permute-done((bf16[144,768]{1,0:T(8,128)(2,1)S(1)}, bf16[144,768]{1,0:T(8,128)(2,1)S(1)}, u32[]{:S(2)}, u32[]{:S(2)}) %collective-permute-start.15) | collective-permute-done | bytes 221216 | tf_op jit(solution)/shard_map/ppermute | solution.py:295
  39.5 0.0 copy-done
  39.5 2.1 %shard_map.132 = (bf16[8,48,128]{2,1,0:T(8,128)(2,1)S(1)}, bf16[8,32,128]{2,1,0:T(8,128)(2,1)S(1)}) custom-call(s32[1]{0:T(128)} %bitcast.me_ref.refs_0_, bf16[144,768]{1,0:T(8,128)(2,1)S(1)} %shard_map.127.refs_1_.refs_9_, bf16[144,768]{1,0:T(8,128)(2,1)S(1)} %collective-permute-done.15.refs_2_.refs_10_, ...), custom_call_target="tpu_custom_call" | custom-call | flops 2 | bytes 2 | tf_op jit(solution)/shard_map/pallas_call | solution.py:427
  41.6 0.1 collective-permute-start.16
  41.7 1.2 %collective-permute-done.16.got_ref = bf16[8,32,128]{2,1,0:T(8,128)(2,1)S(1)} collective-permute-done((bf16[8,32,128]{2,1,0:T(8,128)(2,1)S(1)}, bf16[8,32,128]{2,1,0:T(8,128)(2,1)S(1)}, u32[]{:S(2)}, u32[]{:S(2)}) %collective-permute-start.16) | collective-permute-done | bytes 65568 | tf_op jit(solution)/shard_map/ppermute | solution.py:298
  43.0 10.0 %all_to_all.5.refs_0_ = bf16[8,48,128]{2,1,0:T(8,128)(2,1)S(1)} all-to-all(bf16[8,48,128]{2,1,0:T(8,128)(2,1)S(1)} %shard_map.133), channel_id=1, replica_groups={{0,2,4,6,8,10,12,14},{1,3,5,7,9,11,13,15},{16,18,20,22,24,26,28,30},{17..., dimensions={0} | all-to-all | bytes 196608 | tf_op jit(solution)/shard_map/all_to_all | solution.py:457
  53.0 0.8 %shard_map.134 = (bf16[1,15360]{1,0:T(2,128)(2,1)}, bf16[2,15360]{1,0:T(2,128)(2,1)}) custom-call(bf16[8,48,128]{2,1,0:T(8,128)(2,1)S(1)} %all_to_all.5.refs_0_), custom_call_target="tpu_custom_call" | custom-call | tf_op jit(solution)/shard_map/pallas_call | solution.py:460
  (6 shorter events, 0.1 us)
Async XLA Ops:
  0.6 22.4 %collective-permute-start.6 = (bf16[960,768]{1,0:T(8,128)(2,1)}, bf16[960,768]{1,0:T(8,128)(2,1)S(1)}, u32[]{:S(2)}, u32[]{:S(2)}) collective-permute-start(bf16[960,768]{1,0:T(8,128)(2,1)} %bitcast.7), channel_id=1, source_target_pairs={{0,1},{1,0},{2,3},{3,2},{4,5},{5,4},{6,7},{7,6},{8,9},{9,8},{10,11... | collective-permute-start | bytes 4423688 | tf_op jit(solution)/shard_map/ppermute | solution.py:298
  1.2 11.5 %collective-permute-start.4 = (bf16[128,768]{1,0:T(8,128)(2,1)}, bf16[128,768]{1,0:T(8,128)(2,1)S(1)}, u32[]{:S(2)}, u32[]{:S(2)}) collective-permute-start(bf16[128,768]{1,0:T(8,128)(2,1)} %refs_0_.1), channel_id=1, source_target_pairs={{0,2},{1,3},{2,0},{3,1},{4,6},{5,7},{6,4},{7,5},{8,10},{9,11},{10,... | collective-permute-start | bytes 589832 | tf_op jit(solution)/shard_map/ppermute | solution.py:295
  3.7 8.0 %collective-permute-start = (bf16[48,768]{1,0:T(8,128)(2,1)}, bf16[48,768]{1,0:T(8,128)(2,1)S(1)}, u32[]{:S(2)}, u32[]{:S(2)}) collective-permute-start(bf16[48,768]{1,0:T(8,128)(2,1)} %refs_1_.1), channel_id=1, source_target_pairs={{0,12},{1,13},{2,14},{3,15},{4,8},{5,9},{6,10},{7,11},{8,4},{9,5},... | collective-permute-start | bytes 221192 | tf_op jit(solution)/shard_map/ppermute | solution.py:295
  7.3 5.4 %collective-permute-start.3 = (bf16[48,768]{1,0:T(8,128)(2,1)}, bf16[48,768]{1,0:T(8,128)(2,1)S(1)}, u32[]{:S(2)}, u32[]{:S(2)}) collective-permute-start(bf16[48,768]{1,0:T(8,128)(2,1)} %refs_1_.1), channel_id=1, source_target_pairs={{0,4},{1,5},{2,6},{3,7},{4,0},{5,1},{6,2},{7,3},{8,12},{9,13},{10,... | collective-permute-start | bytes 221192 | tf_op jit(solution)/shard_map/ppermute | solution.py:295
  7.3 9.6 %collective-permute-start.9 = (bf16[128,768]{1,0:T(8,128)(2,1)}, bf16[128,768]{1,0:T(8,128)(2,1)S(1)}, u32[]{:S(2)}, u32[]{:S(2)}) collective-permute-start(bf16[128,768]{1,0:T(8,128)(2,1)} %refs_0_.1), channel_id=1, source_target_pairs={{0,4},{1,5},{2,6},{3,7},{4,0},{5,1},{6,2},{7,3},{8,12},{9,13},{10,... | collective-permute-start | bytes 589832 | tf_op jit(solution)/shard_map/ppermute | solution.py:295
  12.7 10.4 %collective-permute-start.5 = (bf16[112,768]{1,0:T(8,128)(2,1)S(1)}, bf16[112,768]{1,0:T(8,128)(2,1)S(1)}, u32[]{:S(2)}, u32[]{:S(2)}) collective-permute-start(bf16[112,768]{1,0:T(8,128)(2,1)S(1)} %shard_map.124), channel_id=1, source_target_pairs={{0,2},{1,3},{2,0},{3,1},{4,6},{5,7},{6,4},{7,5},{8,10},{9,11},{10,... | collective-permute-start | bytes 516104 | tf_op jit(solution)/shard_map/ppermute | solution.py:295
  13.3 9.7 %collective-permute-start.2 = (bf16[64,768]{1,0:T(8,128)(2,1)S(1)}, bf16[64,768]{1,0:T(8,128)(2,1)S(1)}, u32[]{:S(2)}, u32[]{:S(2)}) collective-permute-start(bf16[64,768]{1,0:T(8,128)(2,1)S(1)} %shard_map.123), channel_id=1, source_target_pairs={{0,4},{1,5},{2,6},{3,7},{4,0},{5,1},{6,2},{7,3},{8,12},{9,13},{10,... | collective-permute-start | bytes 294920 | tf_op jit(solution)/shard_map/ppermute | solution.py:295
  14.9 8.3 %collective-permute-start.1 = (bf16[144,768]{1,0:T(8,128)(2,1)S(1)}, bf16[144,768]{1,0:T(8,128)(2,1)S(1)}, u32[]{:S(2)}, u32[]{:S(2)}) collective-permute-start(bf16[144,768]{1,0:T(8,128)(2,1)S(1)} %get-tuple-element.29.refs_1_.refs_3_), channel_id=1, source_target_pairs={{0,12},{1,13},{2,14},{3,15},{4,8},{5,9},{6,10},{7,11},{8,4},{9,5},... | collective-permute-start | bytes 663560 | tf_op jit(solution)/shard_map/ppermute | solution.py:295
  16.9 10.2 %collective-permute-start.10 = (bf16[128,768]{1,0:T(8,128)(2,1)S(1)}, bf16[128,768]{1,0:T(8,128)(2,1)S(1)}, u32[]{:S(2)}, u32[]{:S(2)}) collective-permute-start(bf16[128,768]{1,0:T(8,128)(2,1)S(1)} %collective-permute-done.9.refs_0_), channel_id=1, source_target_pairs={{0,2},{1,3},{2,0},{3,1},{4,6},{5,7},{6,4},{7,5},{8,10},{9,11},{10,... | collective-permute-start | bytes 589832 | tf_op jit(solution)/shard_map/ppermute | solution.py:295
  23.1 6.7 %collective-permute-start.11 = (bf16[112,768]{1,0:T(8,128)(2,1)S(1)}, bf16[112,768]{1,0:T(8,128)(2,1)S(1)}, u32[]{:S(2)}, u32[]{:S(2)}) collective-permute-start(bf16[112,768]{1,0:T(8,128)(2,1)S(1)} %shard_map.126), channel_id=1, source_target_pairs={{0,2},{1,3},{2,0},{3,1},{4,6},{5,7},{6,4},{7,5},{8,10},{9,11},{10,... | collective-permute-start | bytes 516104 | tf_op jit(solution)/shard_map/ppermute | solution.py:295
  23.2 7.3 %collective-permute-start.7 = (bf16[144,768]{1,0:T(8,128)(2,1)S(1)}, bf16[144,768]{1,0:T(8,128)(2,1)S(1)}, u32[]{:S(2)}, u32[]{:S(2)}) collective-permute-start(bf16[144,768]{1,0:T(8,128)(2,1)S(1)} %collective-permute-done.1.refs_0_.refs_2_.refs_7_), channel_id=1, source_target_pairs={{0,4},{1,5},{2,6},{3,7},{4,0},{5,1},{6,2},{7,3},{8,12},{9,13},{10,... | collective-permute-start | bytes 663560 | tf_op jit(solution)/shard_map/ppermute | solution.py:295
  25.5 6.7 %collective-permute-start.8 = (bf16[144,768]{1,0:T(8,128)(2,1)S(1)}, bf16[144,768]{1,0:T(8,128)(2,1)S(1)}, u32[]{:S(2)}, u32[]{:S(2)}) collective-permute-start(bf16[144,768]{1,0:T(8,128)(2,1)S(1)} %collective-permute-done.1.refs_0_.refs_2_.refs_7_), channel_id=1, source_target_pairs={{0,2},{1,3},{2,0},{3,1},{4,6},{5,7},{6,4},{7,5},{8,10},{9,11},{10,... | collective-permute-start | bytes 663560 | tf_op jit(solution)/shard_map/ppermute | solution.py:295
  29.9 2.3 %collective-permute-start.12 = (bf16[128,768]{1,0:T(8,128)(2,1)S(1)}, bf16[128,768]{1,0:T(8,128)(2,1)S(1)}, u32[]{:S(2)}, u32[]{:S(2)}) collective-permute-start(bf16[128,768]{1,0:T(8,128)(2,1)S(1)} %get-tuple-element.38.refs_5_), channel_id=1, source_target_pairs={{0,1},{1,0},{2,3},{3,2},{4,5},{5,4},{6,7},{7,6},{8,9},{9,8},{10,11... | collective-permute-start | bytes 589832 | tf_op jit(solution)/shard_map/ppermute | solution.py:298
  29.9 2.3 %collective-permute-start.13 = (bf16[128,768]{1,0:T(8,128)(2,1)S(1)}, bf16[128,768]{1,0:T(8,128)(2,1)S(1)}, u32[]{:S(2)}, u32[]{:S(2)}) collective-permute-start(bf16[128,768]{1,0:T(8,128)(2,1)S(1)} %get-tuple-element.39.refs_6_), channel_id=1, source_target_pairs={{0,1},{1,0},{2,3},{3,2},{4,5},{5,4},{6,7},{7,6},{8,9},{9,8},{10,11... | collective-permute-start | bytes 589832 | tf_op jit(solution)/shard_map/ppermute | solution.py:298
  30.4 1.8 %collective-permute-start.14 = (bf16[128,768]{1,0:T(8,128)(2,1)S(1)}, bf16[128,768]{1,0:T(8,128)(2,1)S(1)}, u32[]{:S(2)}, u32[]{:S(2)}) collective-permute-start(bf16[128,768]{1,0:T(8,128)(2,1)S(1)} %get-tuple-element.40.refs_7_), channel_id=1, source_target_pairs={{0,1},{1,0},{2,3},{3,2},{4,5},{5,4},{6,7},{7,6},{8,9},{9,8},{10,11... | collective-permute-start | bytes 589832 | tf_op jit(solution)/shard_map/ppermute | solution.py:298
  32.2 7.3 %collective-permute-start.15 = (bf16[144,768]{1,0:T(8,128)(2,1)S(1)}, bf16[144,768]{1,0:T(8,128)(2,1)S(1)}, u32[]{:S(2)}, u32[]{:S(2)}) collective-permute-start(bf16[144,768]{1,0:T(8,128)(2,1)S(1)} %shard_map.127.refs_1_.refs_9_), channel_id=1, source_target_pairs={{0,2},{1,3},{2,0},{3,1},{4,6},{5,7},{6,4},{7,5},{8,10},{9,11},{10,... | collective-permute-start | bytes 663560 | tf_op jit(solution)/shard_map/ppermute | solution.py:295
  37.0 2.5 %copy-start = (f32[15360]{0:T(1024)S(1)}, f32[15360]{0:T(1024)}, u32[]{:S(2)}) copy-start(f32[15360]{0:T(1024)} %param.18) | copy-start | bytes 184324
  41.6 1.3 %collective-permute-start.16 = (bf16[8,32,128]{2,1,0:T(8,128)(2,1)S(1)}, bf16[8,32,128]{2,1,0:T(8,128)(2,1)S(1)}, u32[]{:S(2)}, u32[]{:S(2)}) collective-permute-start(bf16[8,32,128]{2,1,0:T(8,128)(2,1)S(1)} %get-tuple-element.53), channel_id=1, source_target_pairs={{0,1},{1,0},{2,3},{3,2},{4,5},{5,4},{6,7},{7,6},{8,9},{9,8},{10,11... | collective-permute-start | bytes 196616 | tf_op jit(solution)/shard_map/ppermute | solution.py:298

commit v20 on v19

--- a/solution.py
+++ b/solution.py
@@ -172,9 +172,9 @@
     return copy
 
 
-def keep_tops(normed, halves, bests):
+def keep_tops(normed, count, halves, bests):
     for w_ref, best in zip(halves, bests):
-        for j, top in enumerate(tops_of(normed, w_ref, 2)):
+        for j, top in enumerate(tops_of(normed, w_ref, count)):
             best[j : j + 1, :] = top
 
 
@@ -198,16 +198,19 @@
         for whose, sources in ((core, parts), (1 - core, others)):
             to = pl.multiple_of((2 * chip + whose) * shard + inside, SLOT_ROWS)
             weight[pl.ds(to, SLOT_ROWS), :] = sources[part][place : place + SLOT_ROWS, :]
-    keep_tops(normed_rows(docs, tables, seq, weight, params), halves, bests)
-
-
-def next_kernel(seq, *refs):
-    docs, tables, weight, params, refs = refs[:2], refs[2:4], refs[4], refs[5], refs[6:]
-    keep_tops(normed_rows(docs, tables, seq, weight, params), refs[:2], refs[2:])
-
-
-def last_kernel(seq, masks, *refs):
-    me_ref, docs, tables, refs = refs[0], refs[1:3], refs[3 : 3 + len(masks)], refs[3 + len(masks) :]
+    keep_tops(normed_rows(docs, tables, seq, weight, params), len(docs), halves, bests)
+
+
+def next_kernel(seq, count, *refs):
+    docs, tables, refs = refs[:count], refs[count : 2 * count], refs[2 * count :]
+    weight, params, refs = refs[0], refs[1], refs[2:]
+    keep_tops(normed_rows(docs, tables, seq, weight, params), count, refs[:2], refs[2:])
+
+
+def last_kernel(seq, groups, *refs):
+    masks = [mask for group in groups for mask in group]
+    me_ref, docs, refs = refs[0], refs[1 : 1 + len(groups[-1])], refs[1 + len(groups[-1]) :]
+    tables, refs = refs[: len(masks)], refs[len(masks) :]
     weight, params, halves, dbias_ref, refs = refs[0], refs[1], refs[2:4], refs[4], refs[5:]
     earlier, keep_ref, give_ref, send = refs[:-3], *refs[-3:]
     me = me_ref[0]
@@ -217,8 +220,9 @@
     normed = normed_rows(docs, docs, seq, weight, params)
     found = []
     for k, w_ref in enumerate(halves):
-        parts = [ref[0:2, :] for ref in earlier[k::2]]
-        found.append(jnp.concatenate([*parts, *tops_of(normed, w_ref, 2)], axis=0))
+        parts = [ref[0 : len(group), :] for ref, group in zip(earlier[k::2], groups)]
+        parts += tops_of(normed, w_ref, len(docs))
+        found.append(jnp.concatenate(parts, axis=0))
     low = jnp.where(core == 0, found[0], found[1])
     high = jnp.where(core == 0, found[1], found[0])
     logits = jnp.concatenate([low, high], axis=1)
@@ -331,7 +335,7 @@
     block_6 = cross(transform_weight, 6)
     block_2 = cross(transform_weight, 2)
     theirs = swap(weight_rows)
-    docs = {1: cross(hidden_states, 1), 2: cross(hidden_states, 2)}
+    docs = {1: cross(hidden_states, 1)}
     load, block, table, params = pl.pallas_call(
         start_kernel,
         out_shape=[
@@ -359,6 +363,7 @@
         stay(norm_gain),
         stay(norm_bias),
     )
+    docs[2] = cross(after(hidden_states, table), 2)
     one, two, below = (0, rows), (0, 2 * rows), (0, SLOT_ROWS)
     near = pile((block, after(block_2, block_6, docs[1]), table), (one, one, below))
     near_pile = cross(near, 1)
@@ -384,9 +389,9 @@
     other_packed = [swap(part) for part in packed]
     block_masks = [0, 2, 6, 4, 1, 3, 7, 5]
 
-    masks = [0, 1, 2, 3, 6, 7, 4, 5]
+    groups = [[0, 1], [2, 3], [6, 7, 4], [5]]
+    masks = [mask for group in groups for mask in group]
     docs[0] = load
-    docs[5] = cross(after(docs[4], docs[7], *other_packed), 1)
     tables = docs | {1: near_pile, 2: block_4, 3: far_pile}
     best_shape = shape((8, half), jnp.float32)
     *best, weight = pl.pallas_call(
@@ -406,18 +411,19 @@
         mine,
         theirs,
     )
-    for first in range(2, len(masks) - 2, 2):
-        pair = masks[first : first + 2]
+    docs[5] = cross(after(docs[4], docs[7], weight), 1)
+    tables[5] = docs[5]
+    for group in groups[1:-1]:
         best += pl.pallas_call(
-            lambda *refs: next_kernel(seq, *refs),
+            lambda *refs, count=len(group): next_kernel(seq, count, *refs),
             out_shape=[best_shape] * 2,
-            in_specs=[vmem] * 8,
+            in_specs=[vmem] * (2 * len(group) + 4),
             out_specs=[vmem] * 2,
             compiler_params=limit,
-            cost_estimate=cost(2),
+            cost_estimate=cost(len(group)),
         )(
-            *[docs[mask] for mask in pair],
-            *[tables[mask] for mask in pair],
+            *[docs[mask] for mask in group],
+            *[tables[mask] for mask in group],
             after(weight, best[-1]),
             params,
             mine,
@@ -425,19 +431,19 @@
         )
     height = (1 + BLK_DEV) * SLOT_ROWS
     keep, give = pl.pallas_call(
-        lambda *refs: last_kernel(seq, masks, *refs),
+        lambda *refs: last_kernel(seq, groups, *refs),
         out_shape=[
             shape((chips, height, TILE), jnp.bfloat16),
             shape((chips, height - SLOT_ROWS, TILE), jnp.bfloat16),
         ],
-        in_specs=[smem] + [vmem] * (2 + len(masks) + 5 + len(best)),
+        in_specs=[smem] + [vmem] * (len(groups[-1]) + len(masks) + 5 + len(best)),
         out_specs=[vmem] * 2,
         scratch_shapes=[pltpu.VMEM((devices * height, TILE), jnp.float32)],
         compiler_params=limit,
         cost_estimate=cost(2),
     )(
         where,
-        *[docs[mask] for mask in masks[-2:]],
+        *[docs[mask] for mask in groups[-1]],
         *[tables[mask] for mask in masks],
         weight,
         params,

time: 54 us -> 53.7 us (level)
  waiting for transfers between devices: 13.2 us -> 9.86 us
  starting transfers between devices: 17.7 us -> 19.6 us
  blocking collectives: 10 us -> 10.7 us
    ppermute x12, waiting for transfers between devices: 11.9 us -> 8.61 us  [cross(): lax.ppermute(value, 'doc', [(i, i ^ 2 * mask) for i in range(devices)])]
    ppermute x12, starting transfers between devices: 16.5 us -> 18.3 us  [cross(): lax.ppermute(value, 'doc', [(i, i ^ 2 * mask) for i in range(devices)])]
    all_to_all x1, blocking collectives: 10 us -> 10.7 us  [move_tokens(): lax.all_to_all(merged, 'doc', split_axis=0, concat_axis=0, axis_index_gro...]
  transfers between devices with their start and end apart: 17 -> 17, of which waited for: 7 -> 7; matrix products, arithmetic and copies ran while one was open for 0% -> 0% of each run, Pallas kernels for 16% -> 17%
where the time goes in v20:
time: 53.7 us; the launch traced here: 53.4 us
  starting transfers between devices  19.6 us (36%)
  Pallas kernels  11.9 us (22%)
  blocking collectives  10.7 us (20%)
  waiting for transfers between devices  9.86 us (18%)
  between operations  1.42 us (3%)
    ppermute x12, starting transfers between devices, cross(): lax.ppermute(value, 'doc', [(i, i ^ 2 * mask) for i in range(devices)])  18.3 us
    all_to_all x1, blocking collectives, move_tokens(): lax.all_to_all(merged, 'doc', split_axis=0, concat_axis=0, axis_index_gro...  10.7 us
    ppermute x12, waiting for transfers between devices, cross(): lax.ppermute(value, 'doc', [(i, i ^ 2 * mask) for i in range(devices)])  8.61 us
    pallas_call x2, Pallas kernels, move_tokens(): pl.pallas_call(lambda *refs, count=len(group): next_kernel(seq, count, *r...  4.18 us
    pallas_call x1, Pallas kernels, move_tokens(): pl.pallas_call(lambda *refs: last_kernel(seq, groups, *refs), out_shape=[...  1.98 us
    pallas_call x1, Pallas kernels, move_tokens(): pl.pallas_call(lambda *refs: first_kernel(seq, rows, block_masks, *refs),...  1.8 us
    pallas_call x1, Pallas kernels, move_tokens(): pl.pallas_call(start_kernel, out_shape=[shape((seq + SLOT_ROWS, width), j...  1.71 us
    pallas_call x1, Pallas kernels, move_tokens(): pl.pallas_call(lambda *refs: fetch_kernel(1, *refs), out_shape=[shape(val...  1.38 us
  transfers between devices with their start and end apart: 17, of which 7 were waited for; matrix products, arithmetic and copies ran while one was open for 0% of the time, Pallas kernels for 17%

profile of v20, /device:TPU:0, one launch (start us, length us, event | category | flops | bytes accessed | tf_op | source)
XLA Modules:
  0.0 53.4 jit_solution(7905993533452828465)
XLA Ops:
  0.6 0.5 collective-permute-start.6
  1.2 2.6 %collective-permute-start.4 = (bf16[128,768]{1,0:T(8,128)(2,1)}, bf16[128,768]{1,0:T(8,128)(2,1)S(1)}, u32[]{:S(2)}, u32[]{:S(2)}) collective-permute-start(bf16[128,768]{1,0:T(8,128)(2,1)} %refs_0_.1), channel_id=1, source_target_pairs={{0,2},{1,3},{2,0},{3,1},{4,6},{5,7},{6,4},{7,5},{8,10},{9,11},{10,... | collective-permute-start | bytes 589832 | tf_op jit(solution)/shard_map/ppermute | solution.py:299
  3.7 3.6 %collective-permute-start = (bf16[48,768]{1,0:T(8,128)(2,1)}, bf16[48,768]{1,0:T(8,128)(2,1)S(1)}, u32[]{:S(2)}, u32[]{:S(2)}) collective-permute-start(bf16[48,768]{1,0:T(8,128)(2,1)} %refs_1_.1), channel_id=1, source_target_pairs={{0,12},{1,13},{2,14},{3,15},{4,8},{5,9},{6,10},{7,11},{8,4},{9,5},... | collective-permute-start | bytes 221192 | tf_op jit(solution)/shard_map/ppermute | solution.py:299
  7.3 0.0 collective-permute-start.3
  8.0 1.7 %shard_map.122 = (bf16[144,768]{1,0:T(8,128)(2,1)S(1)}, bf16[48,768]{1,0:T(8,128)(2,1)S(1)}, bf16[16,768]{1,0:T(8,128)(2,1)S(1)}, f32[8,768]{1,0:T(8,128)S(1)}) custom-call(s32[1]{0:T(128)} %bitcast.me_ref.refs_0_, s32[1,1,32]{2,1,0:T(1,128)} %tiles_ref.1, s32[1,1,32]{2,1,0:T(1,128)} %bitcast.9, s32[1,1,32]{2,1,0:T(1,128)} %slots_ref.1, ...), custom_call_target="tpu_custom_call" | custom-call | tf_op jit(solution)/shard_map/pallas_call | solution.py:339
  9.7 2.1 %collective-permute-start.9 = (bf16[128,768]{1,0:T(8,128)(2,1)}, bf16[128,768]{1,0:T(8,128)(2,1)S(1)}, u32[]{:S(2)}, u32[]{:S(2)}) collective-permute-start(bf16[128,768]{1,0:T(8,128)(2,1)} %refs_0_.1), channel_id=1, source_target_pairs={{0,4},{1,5},{2,6},{3,7},{4,0},{5,1},{6,2},{7,3},{8,12},{9,13},{10,... | collective-permute-start | bytes 589832 | tf_op jit(solution)/shard_map/ppermute | solution.py:299
  11.8 0.0 collective-permute-done.refs_0_.refs_2_
  11.8 0.2 collective-permute-done.3.refs_1_
  12.0 0.0 collective-permute-done.4.refs_2_
  12.0 0.5 collective-permute-start.5
  12.5 1.6 %collective-permute-start.2 = (bf16[64,768]{1,0:T(8,128)(2,1)S(1)}, bf16[64,768]{1,0:T(8,128)(2,1)S(1)}, u32[]{:S(2)}, u32[]{:S(2)}) collective-permute-start(bf16[64,768]{1,0:T(8,128)(2,1)S(1)} %shard_map.123), channel_id=1, source_target_pairs={{0,4},{1,5},{2,6},{3,7},{4,0},{5,1},{6,2},{7,3},{8,12},{9,13},{10,... | collective-permute-start | bytes 294920 | tf_op jit(solution)/shard_map/ppermute | solution.py:299
  14.1 1.2 %collective-permute-start.1 = (bf16[144,768]{1,0:T(8,128)(2,1)S(1)}, bf16[144,768]{1,0:T(8,128)(2,1)S(1)}, u32[]{:S(2)}, u32[]{:S(2)}) collective-permute-start(bf16[144,768]{1,0:T(8,128)(2,1)S(1)} %get-tuple-element.30.refs_1_.refs_3_.refs_2_), channel_id=1, source_target_pairs={{0,12},{1,13},{2,14},{3,15},{4,8},{5,9},{6,10},{7,11},{8,4},{9,5},... | collective-permute-start | bytes 663560 | tf_op jit(solution)/shard_map/ppermute | solution.py:299
  15.4 2.6 %collective-permute-done.9.refs_0_ = bf16[128,768]{1,0:T(8,128)(2,1)S(1)} collective-permute-done((bf16[128,768]{1,0:T(8,128)(2,1)}, bf16[128,768]{1,0:T(8,128)(2,1)S(1)}, u32[]{:S(2)}, u32[]{:S(2)}) %collective-permute-start.9) | collective-permute-done | bytes 196640 | tf_op jit(solution)/shard_map/ppermute | solution.py:299
  17.9 0.3 collective-permute-start.10
  18.3 1.4 %shard_map.125.refs_12_.refs_6_.refs_8_ = bf16[960,768]{1,0:T(8,128)(2,1)S(1)} custom-call(bf16[16,768]{1,0:T(8,128)(2,1)S(1)} %get-tuple-element.31.refs_1_.refs_2_.refs_0_, bf16[960,768]{1,0:T(8,128)(2,1)} %bitcast.8), custom_call_target="tpu_custom_call" | custom-call | tf_op jit(solution)/shard_map/pallas_call | solution.py:374
  19.6 0.4 collective-permute-done.2.refs_1_.refs_3_.refs_2_.refs_4_
  20.0 0.0 collective-permute-done.5.refs_4_.refs_3_
  20.0 0.0 collective-permute-done.6.refs_13_.refs_7_.refs_9_
  20.1 1.4 %collective-permute-start.11 = (bf16[112,768]{1,0:T(8,128)(2,1)S(1)}, bf16[112,768]{1,0:T(8,128)(2,1)S(1)}, u32[]{:S(2)}, u32[]{:S(2)}) collective-permute-start(bf16[112,768]{1,0:T(8,128)(2,1)S(1)} %shard_map.126), channel_id=1, source_target_pairs={{0,2},{1,3},{2,0},{3,1},{4,6},{5,7},{6,4},{7,5},{8,10},{9,11},{10,... | collective-permute-start | bytes 516104 | tf_op jit(solution)/shard_map/ppermute | solution.py:299
  21.5 2.1 %collective-permute-done.1.refs_0_.refs_3_.refs_6_ = bf16[144,768]{1,0:T(8,128)(2,1)S(1)} collective-permute-done((bf16[144,768]{1,0:T(8,128)(2,1)S(1)}, bf16[144,768]{1,0:T(8,128)(2,1)S(1)}, u32[]{:S(2)}, u32[]{:S(2)}) %collective-permute-start.1) | collective-permute-done | bytes 221216 | tf_op jit(solution)/shard_map/ppermute | solution.py:299
  23.6 1.9 %collective-permute-start.7 = (bf16[144,768]{1,0:T(8,128)(2,1)S(1)}, bf16[144,768]{1,0:T(8,128)(2,1)S(1)}, u32[]{:S(2)}, u32[]{:S(2)}) collective-permute-start(bf16[144,768]{1,0:T(8,128)(2,1)S(1)} %collective-permute-done.1.refs_0_.refs_3_.refs_6_), channel_id=1, source_target_pairs={{0,4},{1,5},{2,6},{3,7},{4,0},{5,1},{6,2},{7,3},{8,12},{9,13},{10,... | collective-permute-start | bytes 663560 | tf_op jit(solution)/shard_map/ppermute | solution.py:299
  25.5 1.7 %collective-permute-start.8 = (bf16[144,768]{1,0:T(8,128)(2,1)S(1)}, bf16[144,768]{1,0:T(8,128)(2,1)S(1)}, u32[]{:S(2)}, u32[]{:S(2)}) collective-permute-start(bf16[144,768]{1,0:T(8,128)(2,1)S(1)} %collective-permute-done.1.refs_0_.refs_3_.refs_6_), channel_id=1, source_target_pairs={{0,2},{1,3},{2,0},{3,1},{4,6},{5,7},{6,4},{7,5},{8,10},{9,11},{10,... | collective-permute-start | bytes 663560 | tf_op jit(solution)/shard_map/ppermute | solution.py:299
  27.1 0.0 collective-permute-done.10.refs_1_
  27.1 0.0 collective-permute-done.11.refs_5_.refs_3_
  27.2 0.1 collective-permute-start.12
  27.3 0.5 collective-permute-start.13
  27.8 0.1 collective-permute-start.14
  27.9 1.9 %collective-permute-done.7.refs_0_ = bf16[144,768]{1,0:T(8,128)(2,1)S(1)} collective-permute-done((bf16[144,768]{1,0:T(8,128)(2,1)S(1)}, bf16[144,768]{1,0:T(8,128)(2,1)S(1)}, u32[]{:S(2)}, u32[]{:S(2)}) %collective-permute-start.7) | collective-permute-done | bytes 221216 | tf_op jit(solution)/shard_map/ppermute | solution.py:299
  29.7 0.0 collective-permute-done.12.refs_8_
  29.8 0.0 collective-permute-done.13.refs_9_
  29.8 0.0 collective-permute-done.14.refs_10_
  29.8 1.8 %shard_map.129 = (f32[8,960]{1,0:T(8,128)S(1)}, f32[8,960]{1,0:T(8,128)S(1)}, bf16[768,768]{1,0:T(8,128)(2,1)S(1)}) custom-call(s32[1]{0:T(128)} %bitcast.me_ref.refs_0_, bf16[144,768]{1,0:T(8,128)(2,1)S(1)} %get-tuple-element.30.refs_1_.refs_3_.refs_2_, bf16[128,768]{1,0:T(8,128)(2,1)S(1)} %collective-permute-done.4.refs_2_, ...), custom_call_target="tpu_custom_call" | custom-call | flops 2 | bytes 2 | tf_op jit(solution)/shard_map/pallas_call | solution.py:397
  31.6 0.0 collective-permute-done.8.refs_1_.refs_4_.refs_7_
  31.6 1.5 %collective-permute-start.15 = (bf16[144,768]{1,0:T(8,128)(2,1)S(1)}, bf16[144,768]{1,0:T(8,128)(2,1)S(1)}, u32[]{:S(2)}, u32[]{:S(2)}) collective-permute-start(bf16[144,768]{1,0:T(8,128)(2,1)S(1)} %shard_map.127.refs_2_.refs_5_.refs_8_), channel_id=1, source_target_pairs={{0,2},{1,3},{2,0},{3,1},{4,6},{5,7},{6,4},{7,5},{8,10},{9,11},{10,... | collective-permute-start | bytes 663560 | tf_op jit(solution)/shard_map/ppermute | solution.py:299
  33.1 1.8 %shard_map.130 = (f32[8,960]{1,0:T(8,128)S(1)}, f32[8,960]{1,0:T(8,128)S(1)}) custom-call(bf16[128,768]{1,0:T(8,128)(2,1)S(1)} %collective-permute-done.9.refs_0_, bf16[128,768]{1,0:T(8,128)(2,1)S(1)} %collective-permute-done.10.refs_1_, bf16[64,768]{1,0:T(8,128)(2,1)S(1)} %collective-permute-done.2.refs_1_.refs_3_.refs_2_.refs_4_, ...), custom_call_target="tpu_custom_call" | custom-call | flops 2 | bytes 2 | tf_op jit(solution)/shard_map/pallas_call | solution.py:417
  34.8 0.0 copy-start
  34.9 2.4 %shard_map.131 = (f32[8,960]{1,0:T(8,128)S(1)}, f32[8,960]{1,0:T(8,128)S(1)}) custom-call(bf16[144,768]{1,0:T(8,128)(2,1)S(1)} %collective-permute-done.1.refs_0_.refs_3_.refs_6_, bf16[144,768]{1,0:T(8,128)(2,1)S(1)} %collective-permute-done.8.refs_1_.refs_4_.refs_7_, bf16[144,768]{1,0:T(8,128)(2,1)S(1)} %shard_map.127.refs_2_.refs_5_.refs_8_, ...), custom_call_target="tpu_custom_call" | custom-call | flops 3 | bytes 3 | tf_op jit(solution)/shard_map/pallas_call | solution.py:417
  37.3 1.4 %collective-permute-done.15.refs_1_.refs_9_ = bf16[144,768]{1,0:T(8,128)(2,1)S(1)} collective-permute-done((bf16[144,768]{1,0:T(8,128)(2,1)S(1)}, bf16[144,768]{1,0:T(8,128)(2,1)S(1)}, u32[]{:S(2)}, u32[]{:S(2)}) %collective-permute-start.15) | collective-permute-done | bytes 221216 | tf_op jit(solution)/shard_map/ppermute | solution.py:299
  38.7 0.0 copy-done
  38.7 2.0 %shard_map.132 = (bf16[8,48,128]{2,1,0:T(8,128)(2,1)S(1)}, bf16[8,32,128]{2,1,0:T(8,128)(2,1)S(1)}) custom-call(s32[1]{0:T(128)} %bitcast.me_ref.refs_0_, bf16[144,768]{1,0:T(8,128)(2,1)S(1)} %collective-permute-done.15.refs_1_.refs_9_, bf16[144,768]{1,0:T(8,128)(2,1)S(1)} %get-tuple-element.30.refs_1_.refs_3_.refs_2_, ...), custom_call_target="tpu_custom_call" | custom-call | flops 2 | bytes 2 | tf_op jit(solution)/shard_map/pallas_call | solution.py:433
  40.7 0.1 collective-permute-start.16
  40.8 1.2 %collective-permute-done.16.got_ref = bf16[8,32,128]{2,1,0:T(8,128)(2,1)S(1)} collective-permute-done((bf16[8,32,128]{2,1,0:T(8,128)(2,1)S(1)}, bf16[8,32,128]{2,1,0:T(8,128)(2,1)S(1)}, u32[]{:S(2)}, u32[]{:S(2)}) %collective-permute-start.16) | collective-permute-done | bytes 65568 | tf_op jit(solution)/shard_map/ppermute | solution.py:302
  42.0 10.7 %all_to_all.5.refs_0_ = bf16[8,48,128]{2,1,0:T(8,128)(2,1)S(1)} all-to-all(bf16[8,48,128]{2,1,0:T(8,128)(2,1)S(1)} %shard_map.133), channel_id=1, replica_groups={{0,2,4,6,8,10,12,14},{1,3,5,7,9,11,13,15},{16,18,20,22,24,26,28,30},{17..., dimensions={0} | all-to-all | bytes 196608 | tf_op jit(solution)/shard_map/all_to_all | solution.py:463
  52.7 0.8 %shard_map.134 = (bf16[1,15360]{1,0:T(2,128)(2,1)}, bf16[2,15360]{1,0:T(2,128)(2,1)}) custom-call(bf16[8,48,128]{2,1,0:T(8,128)(2,1)S(1)} %all_to_all.5.refs_0_), custom_call_target="tpu_custom_call" | custom-call | tf_op jit(solution)/shard_map/pallas_call | solution.py:466
  (6 shorter events, 0.1 us)
Async XLA Ops:
  0.6 19.4 %collective-permute-start.6 = (bf16[960,768]{1,0:T(8,128)(2,1)}, bf16[960,768]{1,0:T(8,128)(2,1)S(1)}, u32[]{:S(2)}, u32[]{:S(2)}) collective-permute-start(bf16[960,768]{1,0:T(8,128)(2,1)} %bitcast.7), channel_id=1, source_target_pairs={{0,1},{1,0},{2,3},{3,2},{4,5},{5,4},{6,7},{7,6},{8,9},{9,8},{10,11... | collective-permute-start | bytes 4423688 | tf_op jit(solution)/shard_map/ppermute | solution.py:302
  1.2 10.9 %collective-permute-start.4 = (bf16[128,768]{1,0:T(8,128)(2,1)}, bf16[128,768]{1,0:T(8,128)(2,1)S(1)}, u32[]{:S(2)}, u32[]{:S(2)}) collective-permute-start(bf16[128,768]{1,0:T(8,128)(2,1)} %refs_0_.1), channel_id=1, source_target_pairs={{0,2},{1,3},{2,0},{3,1},{4,6},{5,7},{6,4},{7,5},{8,10},{9,11},{10,... | collective-permute-start | bytes 589832 | tf_op jit(solution)/shard_map/ppermute | solution.py:299
  3.7 8.1 %collective-permute-start = (bf16[48,768]{1,0:T(8,128)(2,1)}, bf16[48,768]{1,0:T(8,128)(2,1)S(1)}, u32[]{:S(2)}, u32[]{:S(2)}) collective-permute-start(bf16[48,768]{1,0:T(8,128)(2,1)} %refs_1_.1), channel_id=1, source_target_pairs={{0,12},{1,13},{2,14},{3,15},{4,8},{5,9},{6,10},{7,11},{8,4},{9,5},... | collective-permute-start | bytes 221192 | tf_op jit(solution)/shard_map/ppermute | solution.py:299
  7.3 4.7 %collective-permute-start.3 = (bf16[48,768]{1,0:T(8,128)(2,1)}, bf16[48,768]{1,0:T(8,128)(2,1)S(1)}, u32[]{:S(2)}, u32[]{:S(2)}) collective-permute-start(bf16[48,768]{1,0:T(8,128)(2,1)} %refs_1_.1), channel_id=1, source_target_pairs={{0,4},{1,5},{2,6},{3,7},{4,0},{5,1},{6,2},{7,3},{8,12},{9,13},{10,... | collective-permute-start | bytes 221192 | tf_op jit(solution)/shard_map/ppermute | solution.py:299
  9.7 8.2 %collective-permute-start.9 = (bf16[128,768]{1,0:T(8,128)(2,1)}, bf16[128,768]{1,0:T(8,128)(2,1)S(1)}, u32[]{:S(2)}, u32[]{:S(2)}) collective-permute-start(bf16[128,768]{1,0:T(8,128)(2,1)} %refs_0_.1), channel_id=1, source_target_pairs={{0,4},{1,5},{2,6},{3,7},{4,0},{5,1},{6,2},{7,3},{8,12},{9,13},{10,... | collective-permute-start | bytes 589832 | tf_op jit(solution)/shard_map/ppermute | solution.py:299
  12.0 8.0 %collective-permute-start.5 = (bf16[112,768]{1,0:T(8,128)(2,1)S(1)}, bf16[112,768]{1,0:T(8,128)(2,1)S(1)}, u32[]{:S(2)}, u32[]{:S(2)}) collective-permute-start(bf16[112,768]{1,0:T(8,128)(2,1)S(1)} %shard_map.124), channel_id=1, source_target_pairs={{0,2},{1,3},{2,0},{3,1},{4,6},{5,7},{6,4},{7,5},{8,10},{9,11},{10,... | collective-permute-start | bytes 516104 | tf_op jit(solution)/shard_map/ppermute | solution.py:299
  12.5 7.5 %collective-permute-start.2 = (bf16[64,768]{1,0:T(8,128)(2,1)S(1)}, bf16[64,768]{1,0:T(8,128)(2,1)S(1)}, u32[]{:S(2)}, u32[]{:S(2)}) collective-permute-start(bf16[64,768]{1,0:T(8,128)(2,1)S(1)} %shard_map.123), channel_id=1, source_target_pairs={{0,4},{1,5},{2,6},{3,7},{4,0},{5,1},{6,2},{7,3},{8,12},{9,13},{10,... | collective-permute-start | bytes 294920 | tf_op jit(solution)/shard_map/ppermute | solution.py:299
  14.1 9.5 %collective-permute-start.1 = (bf16[144,768]{1,0:T(8,128)(2,1)S(1)}, bf16[144,768]{1,0:T(8,128)(2,1)S(1)}, u32[]{:S(2)}, u32[]{:S(2)}) collective-permute-start(bf16[144,768]{1,0:T(8,128)(2,1)S(1)} %get-tuple-element.30.refs_1_.refs_3_.refs_2_), channel_id=1, source_target_pairs={{0,12},{1,13},{2,14},{3,15},{4,8},{5,9},{6,10},{7,11},{8,4},{9,5},... | collective-permute-start | bytes 663560 | tf_op jit(solution)/shard_map/ppermute | solution.py:299
  17.9 9.2 %collective-permute-start.10 = (bf16[128,768]{1,0:T(8,128)(2,1)S(1)}, bf16[128,768]{1,0:T(8,128)(2,1)S(1)}, u32[]{:S(2)}, u32[]{:S(2)}) collective-permute-start(bf16[128,768]{1,0:T(8,128)(2,1)S(1)} %collective-permute-done.9.refs_0_), channel_id=1, source_target_pairs={{0,2},{1,3},{2,0},{3,1},{4,6},{5,7},{6,4},{7,5},{8,10},{9,11},{10,... | collective-permute-start | bytes 589832 | tf_op jit(solution)/shard_map/ppermute | solution.py:299
  20.1 7.1 %collective-permute-start.11 = (bf16[112,768]{1,0:T(8,128)(2,1)S(1)}, bf16[112,768]{1,0:T(8,128)(2,1)S(1)}, u32[]{:S(2)}, u32[]{:S(2)}) collective-permute-start(bf16[112,768]{1,0:T(8,128)(2,1)S(1)} %shard_map.126), channel_id=1, source_target_pairs={{0,2},{1,3},{2,0},{3,1},{4,6},{5,7},{6,4},{7,5},{8,10},{9,11},{10,... | collective-permute-start | bytes 516104 | tf_op jit(solution)/shard_map/ppermute | solution.py:299
  23.6 6.1 %collective-permute-start.7 = (bf16[144,768]{1,0:T(8,128)(2,1)S(1)}, bf16[144,768]{1,0:T(8,128)(2,1)S(1)}, u32[]{:S(2)}, u32[]{:S(2)}) collective-permute-start(bf16[144,768]{1,0:T(8,128)(2,1)S(1)} %collective-permute-done.1.refs_0_.refs_3_.refs_6_), channel_id=1, source_target_pairs={{0,4},{1,5},{2,6},{3,7},{4,0},{5,1},{6,2},{7,3},{8,12},{9,13},{10,... | collective-permute-start | bytes 663560 | tf_op jit(solution)/shard_map/ppermute | solution.py:299
  25.5 6.1 %collective-permute-start.8 = (bf16[144,768]{1,0:T(8,128)(2,1)S(1)}, bf16[144,768]{1,0:T(8,128)(2,1)S(1)}, u32[]{:S(2)}, u32[]{:S(2)}) collective-permute-start(bf16[144,768]{1,0:T(8,128)(2,1)S(1)} %collective-permute-done.1.refs_0_.refs_3_.refs_6_), channel_id=1, source_target_pairs={{0,2},{1,3},{2,0},{3,1},{4,6},{5,7},{6,4},{7,5},{8,10},{9,11},{10,... | collective-permute-start | bytes 663560 | tf_op jit(solution)/shard_map/ppermute | solution.py:299
  27.2 2.6 %collective-permute-start.12 = (bf16[128,768]{1,0:T(8,128)(2,1)S(1)}, bf16[128,768]{1,0:T(8,128)(2,1)S(1)}, u32[]{:S(2)}, u32[]{:S(2)}) collective-permute-start(bf16[128,768]{1,0:T(8,128)(2,1)S(1)} %get-tuple-element.40.refs_5_), channel_id=1, source_target_pairs={{0,1},{1,0},{2,3},{3,2},{4,5},{5,4},{6,7},{7,6},{8,9},{9,8},{10,11... | collective-permute-start | bytes 589832 | tf_op jit(solution)/shard_map/ppermute | solution.py:302
  27.3 2.5 %collective-permute-start.13 = (bf16[128,768]{1,0:T(8,128)(2,1)S(1)}, bf16[128,768]{1,0:T(8,128)(2,1)S(1)}, u32[]{:S(2)}, u32[]{:S(2)}) collective-permute-start(bf16[128,768]{1,0:T(8,128)(2,1)S(1)} %get-tuple-element.41.refs_6_), channel_id=1, source_target_pairs={{0,1},{1,0},{2,3},{3,2},{4,5},{5,4},{6,7},{7,6},{8,9},{9,8},{10,11... | collective-permute-start | bytes 589832 | tf_op jit(solution)/shard_map/ppermute | solution.py:302
  27.8 2.0 %collective-permute-start.14 = (bf16[128,768]{1,0:T(8,128)(2,1)S(1)}, bf16[128,768]{1,0:T(8,128)(2,1)S(1)}, u32[]{:S(2)}, u32[]{:S(2)}) collective-permute-start(bf16[128,768]{1,0:T(8,128)(2,1)S(1)} %get-tuple-element.42.refs_7_), channel_id=1, source_target_pairs={{0,1},{1,0},{2,3},{3,2},{4,5},{5,4},{6,7},{7,6},{8,9},{9,8},{10,11... | collective-permute-start | bytes 589832 | tf_op jit(solution)/shard_map/ppermute | solution.py:302
  31.6 7.1 %collective-permute-start.15 = (bf16[144,768]{1,0:T(8,128)(2,1)S(1)}, bf16[144,768]{1,0:T(8,128)(2,1)S(1)}, u32[]{:S(2)}, u32[]{:S(2)}) collective-permute-start(bf16[144,768]{1,0:T(8,128)(2,1)S(1)} %shard_map.127.refs_2_.refs_5_.refs_8_), channel_id=1, source_target_pairs={{0,2},{1,3},{2,0},{3,1},{4,6},{5,7},{6,4},{7,5},{8,10},{9,11},{10,... | collective-permute-start | bytes 663560 | tf_op jit(solution)/shard_map/ppermute | solution.py:299
  34.8 3.9 %copy-start = (f32[15360]{0:T(1024)S(1)}, f32[15360]{0:T(1024)}, u32[]{:S(2)}) copy-start(f32[15360]{0:T(1024)} %param.18) | copy-start | bytes 184324
  40.7 1.3 %collective-permute-start.16 = (bf16[8,32,128]{2,1,0:T(8,128)(2,1)S(1)}, bf16[8,32,128]{2,1,0:T(8,128)(2,1)S(1)}, u32[]{:S(2)}, u32[]{:S(2)}) collective-permute-start(bf16[8,32,128]{2,1,0:T(8,128)(2,1)S(1)} %get-tuple-element.55), channel_id=1, source_target_pairs={{0,1},{1,0},{2,3},{3,2},{4,5},{5,4},{6,7},{7,6},{8,9},{9,8},{10,11... | collective-permute-start | bytes 196616 | tf_op jit(solution)/shard_map/ppermute | solution.py:302

commit v21 on v20

--- a/solution.py
+++ b/solution.py
@@ -335,7 +335,7 @@
     block_6 = cross(transform_weight, 6)
     block_2 = cross(transform_weight, 2)
     theirs = swap(weight_rows)
-    docs = {1: cross(hidden_states, 1)}
+    docs = {1: cross(hidden_states, 1), 2: cross(hidden_states, 2)}
     load, block, table, params = pl.pallas_call(
         start_kernel,
         out_shape=[
@@ -363,7 +363,6 @@
         stay(norm_gain),
         stay(norm_bias),
     )
-    docs[2] = cross(after(hidden_states, table), 2)
     one, two, below = (0, rows), (0, 2 * rows), (0, SLOT_ROWS)
     near = pile((block, after(block_2, block_6, docs[1]), table), (one, one, below))
     near_pile = cross(near, 1)
@@ -379,7 +378,7 @@
         scratch_shapes=[pltpu.SemaphoreType.DMA((1,))],
         compiler_params=limit,
     )(table, *far_from)
-    far = (block_6, after(block_4, near_pile, mine, theirs))
+    far = (block_6, after(block_4, near_pile, docs[6], mine, theirs))
     far = pile(far, (one, (0, rows + SLOT_ROWS)))
     far_pile = cross(far, 1)
     docs[4] = pile((cross(after(docs[6], far), 2),), ((0, seq + SLOT_ROWS),))
@@ -411,7 +410,7 @@
         mine,
         theirs,
     )
-    docs[5] = cross(after(docs[4], docs[7], weight), 1)
+    docs[5] = cross(after(docs[4], weight), 1)
     tables[5] = docs[5]
     for group in groups[1:-1]:
         best += pl.pallas_call(

time: 53.7 us -> 57.5 us (1.071)
  waiting for transfers between devices: 9.86 us -> 18.9 us
  starting transfers between devices: 19.6 us -> 15.6 us
  blocking collectives: 10.7 us -> 9.51 us
    ppermute x12, waiting for transfers between devices: 8.61 us -> 16.2 us  [cross(): lax.ppermute(value, 'doc', [(i, i ^ 2 * mask) for i in range(devices)])]
    ppermute x12, starting transfers between devices: 18.3 us -> 14.4 us  [cross(): lax.ppermute(value, 'doc', [(i, i ^ 2 * mask) for i in range(devices)])]
    ppermute x5, waiting for transfers between devices: 1.25 us -> 2.63 us  [swap(): return lax.ppermute(value, 'doc', [(i, i ^ 1) for i in range(devices)])]
    all_to_all x1, blocking collectives: 10.7 us -> 9.51 us  [move_tokens(): lax.all_to_all(merged, 'doc', split_axis=0, concat_axis=0, axis_index_gro...]
  transfers between devices with their start and end apart: 17 -> 17, of which waited for: 7 -> 10; matrix products, arithmetic and copies ran while one was open for 0% -> 0% of each run, Pallas kernels for 17% -> 16%
where the time goes in v21:
time: 57.5 us; the launch traced here: 57.3 us
  waiting for transfers between devices  18.9 us (33%)
  starting transfers between devices  15.6 us (27%)
  Pallas kernels  11.9 us (21%)
  blocking collectives  9.51 us (17%)
  between operations  1.41 us (2%)
    ppermute x12, waiting for transfers between devices, cross(): lax.ppermute(value, 'doc', [(i, i ^ 2 * mask) for i in range(devices)])  16.2 us
    ppermute x12, starting transfers between devices, cross(): lax.ppermute(value, 'doc', [(i, i ^ 2 * mask) for i in range(devices)])  14.4 us
    all_to_all x1, blocking collectives, move_tokens(): lax.all_to_all(merged, 'doc', split_axis=0, concat_axis=0, axis_index_gro...  9.51 us
    pallas_call x2, Pallas kernels, move_tokens(): pl.pallas_call(lambda *refs, count=len(group): next_kernel(seq, count, *r...  4.19 us
    ppermute x5, waiting for transfers between devices, swap(): return lax.ppermute(value, 'doc', [(i, i ^ 1) for i in range(devices)])  2.63 us
    pallas_call x1, Pallas kernels, move_tokens(): pl.pallas_call(lambda *refs: last_kernel(seq, groups, *refs), out_shape=[...  1.98 us
    pallas_call x1, Pallas kernels, move_tokens(): pl.pallas_call(lambda *refs: first_kernel(seq, rows, block_masks, *refs),...  1.78 us
    pallas_call x1, Pallas kernels, move_tokens(): pl.pallas_call(start_kernel, out_shape=[shape((seq + SLOT_ROWS, width), j...  1.71 us
  transfers between devices with their start and end apart: 17, of which 10 were waited for; matrix products, arithmetic and copies ran while one was open for 0% of the time, Pallas kernels for 16%

profile of v21, /device:TPU:0, one launch (start us, length us, event | category | flops | bytes accessed | tf_op | source)
XLA Modules:
  0.0 57.3 jit_solution(8420952960334682903)
XLA Ops:
  0.6 0.5 collective-permute-start.6
  1.2 2.6 %collective-permute-start.4 = (bf16[128,768]{1,0:T(8,128)(2,1)}, bf16[128,768]{1,0:T(8,128)(2,1)S(1)}, u32[]{:S(2)}, u32[]{:S(2)}) collective-permute-start(bf16[128,768]{1,0:T(8,128)(2,1)} %refs_0_.1), channel_id=1, source_target_pairs={{0,2},{1,3},{2,0},{3,1},{4,6},{5,7},{6,4},{7,5},{8,10},{9,11},{10,... | collective-permute-start | bytes 589832 | tf_op jit(solution)/shard_map/ppermute | solution.py:299
  3.7 3.6 %collective-permute-start = (bf16[48,768]{1,0:T(8,128)(2,1)}, bf16[48,768]{1,0:T(8,128)(2,1)S(1)}, u32[]{:S(2)}, u32[]{:S(2)}) collective-permute-start(bf16[48,768]{1,0:T(8,128)(2,1)} %refs_1_.1), channel_id=1, source_target_pairs={{0,12},{1,13},{2,14},{3,15},{4,8},{5,9},{6,10},{7,11},{8,4},{9,5},... | collective-permute-start | bytes 221192 | tf_op jit(solution)/shard_map/ppermute | solution.py:299
  7.3 0.0 collective-permute-start.3
  7.3 2.0 %collective-permute-start.8 = (bf16[128,768]{1,0:T(8,128)(2,1)}, bf16[128,768]{1,0:T(8,128)(2,1)S(1)}, u32[]{:S(2)}, u32[]{:S(2)}) collective-permute-start(bf16[128,768]{1,0:T(8,128)(2,1)} %refs_0_.1), channel_id=1, source_target_pairs={{0,4},{1,5},{2,6},{3,7},{4,0},{5,1},{6,2},{7,3},{8,12},{9,13},{10,... | collective-permute-start | bytes 589832 | tf_op jit(solution)/shard_map/ppermute | solution.py:299
  10.0 1.7 %shard_map.122 = (bf16[144,768]{1,0:T(8,128)(2,1)S(1)}, bf16[48,768]{1,0:T(8,128)(2,1)S(1)}, bf16[16,768]{1,0:T(8,128)(2,1)S(1)}, f32[8,768]{1,0:T(8,128)S(1)}) custom-call(s32[1]{0:T(128)} %bitcast.me_ref.refs_0_, s32[1,1,32]{2,1,0:T(1,128)} %tiles_ref.1, s32[1,1,32]{2,1,0:T(1,128)} %bitcast.9, s32[1,1,32]{2,1,0:T(1,128)} %slots_ref.1, ...), custom_call_target="tpu_custom_call" | custom-call | tf_op jit(solution)/shard_map/pallas_call | solution.py:339
  11.7 0.0 collective-permute-done.refs_0_.refs_2_
  11.7 2.7 %collective-permute-start.1 = (bf16[144,768]{1,0:T(8,128)(2,1)S(1)}, bf16[144,768]{1,0:T(8,128)(2,1)S(1)}, u32[]{:S(2)}, u32[]{:S(2)}) collective-permute-start(bf16[144,768]{1,0:T(8,128)(2,1)S(1)} %get-tuple-element.29.refs_1_.refs_3_.refs_2_), channel_id=1, source_target_pairs={{0,12},{1,13},{2,14},{3,15},{4,8},{5,9},{6,10},{7,11},{8,4},{9,5},... | collective-permute-start | bytes 663560 | tf_op jit(solution)/shard_map/ppermute | solution.py:299
  14.4 0.0 collective-permute-done.3.refs_1_
  14.4 0.0 collective-permute-done.4.refs_2_
  14.5 0.6 %collective-permute-start.5 = (bf16[112,768]{1,0:T(8,128)(2,1)S(1)}, bf16[112,768]{1,0:T(8,128)(2,1)S(1)}, u32[]{:S(2)}, u32[]{:S(2)}) collective-permute-start(bf16[112,768]{1,0:T(8,128)(2,1)S(1)} %shard_map.124), channel_id=1, source_target_pairs={{0,2},{1,3},{2,0},{3,1},{4,6},{5,7},{6,4},{7,5},{8,10},{9,11},{10,... | collective-permute-start | bytes 516104 | tf_op jit(solution)/shard_map/ppermute | solution.py:299
  15.1 0.1 collective-permute-start.2
  15.2 6.0 %collective-permute-done.8.refs_0_ = bf16[128,768]{1,0:T(8,128)(2,1)S(1)} collective-permute-done((bf16[128,768]{1,0:T(8,128)(2,1)}, bf16[128,768]{1,0:T(8,128)(2,1)S(1)}, u32[]{:S(2)}, u32[]{:S(2)}) %collective-permute-start.8) | collective-permute-done | bytes 196640 | tf_op jit(solution)/shard_map/ppermute | solution.py:299
  21.1 0.0 collective-permute-start.9
  21.1 1.4 %shard_map.125.refs_12_.refs_6_.refs_8_ = bf16[960,768]{1,0:T(8,128)(2,1)S(1)} custom-call(bf16[16,768]{1,0:T(8,128)(2,1)S(1)} %get-tuple-element.30.refs_1_.refs_2_.refs_0_, bf16[960,768]{1,0:T(8,128)(2,1)} %bitcast.8), custom_call_target="tpu_custom_call" | custom-call | tf_op jit(solution)/shard_map/pallas_call | solution.py:373
  22.5 0.5 collective-permute-done.2.refs_1_.refs_3_.refs_2_.refs_4_
  23.1 0.0 collective-permute-done.1.refs_0_.refs_3_.refs_6_
  23.1 0.0 collective-permute-done.5.refs_4_.refs_3_
  23.1 0.0 collective-permute-done.6.refs_13_.refs_7_.refs_9_
  23.1 1.6 %collective-permute-start.10 = (bf16[112,768]{1,0:T(8,128)(2,1)S(1)}, bf16[112,768]{1,0:T(8,128)(2,1)S(1)}, u32[]{:S(2)}, u32[]{:S(2)}) collective-permute-start(bf16[112,768]{1,0:T(8,128)(2,1)S(1)} %shard_map.126), channel_id=1, source_target_pairs={{0,2},{1,3},{2,0},{3,1},{4,6},{5,7},{6,4},{7,5},{8,10},{9,11},{10,... | collective-permute-start | bytes 516104 | tf_op jit(solution)/shard_map/ppermute | solution.py:299
  24.7 0.5 collective-permute-start.7
  25.1 3.3 %collective-permute-done.9.refs_1_ = bf16[128,768]{1,0:T(8,128)(2,1)S(1)} collective-permute-done((bf16[128,768]{1,0:T(8,128)(2,1)S(1)}, bf16[128,768]{1,0:T(8,128)(2,1)S(1)}, u32[]{:S(2)}, u32[]{:S(2)}) %collective-permute-start.9) | collective-permute-done | bytes 196640 | tf_op jit(solution)/shard_map/ppermute | solution.py:299
  28.4 2.1 %collective-permute-done.10.refs_5_.refs_3_ = bf16[112,768]{1,0:T(8,128)(2,1)S(1)} collective-permute-done((bf16[112,768]{1,0:T(8,128)(2,1)S(1)}, bf16[112,768]{1,0:T(8,128)(2,1)S(1)}, u32[]{:S(2)}, u32[]{:S(2)}) %collective-permute-start.10) | collective-permute-done | bytes 172064 | tf_op jit(solution)/shard_map/ppermute | solution.py:299
  30.5 0.1 collective-permute-start.11
  30.6 0.5 collective-permute-start.12
  31.1 0.1 collective-permute-start.13
  31.2 0.0 collective-permute-start.15
  31.2 0.0 collective-permute-done.7.refs_0_
  31.2 0.8 %collective-permute-done.11.refs_8_ = bf16[128,768]{1,0:T(8,128)(2,1)S(1)} collective-permute-done((bf16[128,768]{1,0:T(8,128)(2,1)S(1)}, bf16[128,768]{1,0:T(8,128)(2,1)S(1)}, u32[]{:S(2)}, u32[]{:S(2)}) %collective-permute-start.11) | collective-permute-done | bytes 196640 | tf_op jit(solution)/shard_map/ppermute | solution.py:302
  32.0 0.3 collective-permute-done.12.refs_9_
  32.3 0.3 collective-permute-done.13.refs_10_
  32.6 1.8 %shard_map.129 = (f32[8,960]{1,0:T(8,128)S(1)}, f32[8,960]{1,0:T(8,128)S(1)}, bf16[768,768]{1,0:T(8,128)(2,1)S(1)}) custom-call(s32[1]{0:T(128)} %bitcast.me_ref.refs_0_, bf16[144,768]{1,0:T(8,128)(2,1)S(1)} %get-tuple-element.29.refs_1_.refs_3_.refs_2_, bf16[128,768]{1,0:T(8,128)(2,1)S(1)} %collective-permute-done.4.refs_2_, ...), custom_call_target="tpu_custom_call" | custom-call | flops 2 | bytes 2 | tf_op jit(solution)/shard_map/pallas_call | solution.py:396
  34.4 0.7 %collective-permute-start.14 = (bf16[144,768]{1,0:T(8,128)(2,1)S(1)}, bf16[144,768]{1,0:T(8,128)(2,1)S(1)}, u32[]{:S(2)}, u32[]{:S(2)}) collective-permute-start(bf16[144,768]{1,0:T(8,128)(2,1)S(1)} %shard_map.127.refs_2_.refs_5_.refs_8_), channel_id=1, source_target_pairs={{0,2},{1,3},{2,0},{3,1},{4,6},{5,7},{6,4},{7,5},{8,10},{9,11},{10,... | collective-permute-start | bytes 663560 | tf_op jit(solution)/shard_map/ppermute | solution.py:299
  35.1 1.8 %shard_map.130 = (f32[8,960]{1,0:T(8,128)S(1)}, f32[8,960]{1,0:T(8,128)S(1)}) custom-call(bf16[128,768]{1,0:T(8,128)(2,1)S(1)} %collective-permute-done.8.refs_0_, bf16[128,768]{1,0:T(8,128)(2,1)S(1)} %collective-permute-done.9.refs_1_, bf16[64,768]{1,0:T(8,128)(2,1)S(1)} %collective-permute-done.2.refs_1_.refs_3_.refs_2_.refs_4_, ...), custom_call_target="tpu_custom_call" | custom-call | flops 2 | bytes 2 | tf_op jit(solution)/shard_map/pallas_call | solution.py:416
  36.9 0.0 copy-start
  36.9 2.5 %collective-permute-done.15.refs_1_.refs_4_.refs_7_ = bf16[144,768]{1,0:T(8,128)(2,1)S(1)} collective-permute-done((bf16[144,768]{1,0:T(8,128)(2,1)S(1)}, bf16[144,768]{1,0:T(8,128)(2,1)S(1)}, u32[]{:S(2)}, u32[]{:S(2)}) %collective-permute-start.15) | collective-permute-done | bytes 221216 | tf_op jit(solution)/shard_map/ppermute | solution.py:299
  39.4 2.4 %shard_map.131 = (f32[8,960]{1,0:T(8,128)S(1)}, f32[8,960]{1,0:T(8,128)S(1)}) custom-call(bf16[144,768]{1,0:T(8,128)(2,1)S(1)} %collective-permute-done.1.refs_0_.refs_3_.refs_6_, bf16[144,768]{1,0:T(8,128)(2,1)S(1)} %collective-permute-done.15.refs_1_.refs_4_.refs_7_, bf16[144,768]{1,0:T(8,128)(2,1)S(1)} %shard_map.127.refs_2_.refs_5_.refs_8_, ...), custom_call_target="tpu_custom_call" | custom-call | flops 3 | bytes 3 | tf_op jit(solution)/shard_map/pallas_call | solution.py:416
  41.8 1.9 %collective-permute-done.14.refs_1_.refs_9_ = bf16[144,768]{1,0:T(8,128)(2,1)S(1)} collective-permute-done((bf16[144,768]{1,0:T(8,128)(2,1)S(1)}, bf16[144,768]{1,0:T(8,128)(2,1)S(1)}, u32[]{:S(2)}, u32[]{:S(2)}) %collective-permute-start.14) | collective-permute-done | bytes 221216 | tf_op jit(solution)/shard_map/ppermute | solution.py:299
  43.7 0.0 copy-done
  43.7 2.0 %shard_map.132 = (bf16[8,48,128]{2,1,0:T(8,128)(2,1)S(1)}, bf16[8,32,128]{2,1,0:T(8,128)(2,1)S(1)}) custom-call(s32[1]{0:T(128)} %bitcast.me_ref.refs_0_, bf16[144,768]{1,0:T(8,128)(2,1)S(1)} %collective-permute-done.14.refs_1_.refs_9_, bf16[144,768]{1,0:T(8,128)(2,1)S(1)} %get-tuple-element.29.refs_1_.refs_3_.refs_2_, ...), custom_call_target="tpu_custom_call" | custom-call | flops 2 | bytes 2 | tf_op jit(solution)/shard_map/pallas_call | solution.py:432
  45.7 0.1 collective-permute-start.16
  45.8 1.2 %collective-permute-done.16.got_ref = bf16[8,32,128]{2,1,0:T(8,128)(2,1)S(1)} collective-permute-done((bf16[8,32,128]{2,1,0:T(8,128)(2,1)S(1)}, bf16[8,32,128]{2,1,0:T(8,128)(2,1)S(1)}, u32[]{:S(2)}, u32[]{:S(2)}) %collective-permute-start.16) | collective-permute-done | bytes 65568 | tf_op jit(solution)/shard_map/ppermute | solution.py:302
  47.0 9.5 %all_to_all.5.refs_0_ = bf16[8,48,128]{2,1,0:T(8,128)(2,1)S(1)} all-to-all(bf16[8,48,128]{2,1,0:T(8,128)(2,1)S(1)} %shard_map.133), channel_id=1, replica_groups={{0,2,4,6,8,10,12,14},{1,3,5,7,9,11,13,15},{16,18,20,22,24,26,28,30},{17..., dimensions={0} | all-to-all | bytes 196608 | tf_op jit(solution)/shard_map/all_to_all | solution.py:462
  56.6 0.8 %shard_map.134 = (bf16[1,15360]{1,0:T(2,128)(2,1)}, bf16[2,15360]{1,0:T(2,128)(2,1)}) custom-call(bf16[8,48,128]{2,1,0:T(8,128)(2,1)S(1)} %all_to_all.5.refs_0_), custom_call_target="tpu_custom_call" | custom-call | tf_op jit(solution)/shard_map/pallas_call | solution.py:465
  (6 shorter events, 0.1 us)
Async XLA Ops:
  0.6 22.4 %collective-permute-start.6 = (bf16[960,768]{1,0:T(8,128)(2,1)}, bf16[960,768]{1,0:T(8,128)(2,1)S(1)}, u32[]{:S(2)}, u32[]{:S(2)}) collective-permute-start(bf16[960,768]{1,0:T(8,128)(2,1)} %bitcast.7), channel_id=1, source_target_pairs={{0,1},{1,0},{2,3},{3,2},{4,5},{5,4},{6,7},{7,6},{8,9},{9,8},{10,11... | collective-permute-start | bytes 4423688 | tf_op jit(solution)/shard_map/ppermute | solution.py:302
  1.2 13.3 %collective-permute-start.4 = (bf16[128,768]{1,0:T(8,128)(2,1)}, bf16[128,768]{1,0:T(8,128)(2,1)S(1)}, u32[]{:S(2)}, u32[]{:S(2)}) collective-permute-start(bf16[128,768]{1,0:T(8,128)(2,1)} %refs_0_.1), channel_id=1, source_target_pairs={{0,2},{1,3},{2,0},{3,1},{4,6},{5,7},{6,4},{7,5},{8,10},{9,11},{10,... | collective-permute-start | bytes 589832 | tf_op jit(solution)/shard_map/ppermute | solution.py:299
  3.7 8.0 %collective-permute-start = (bf16[48,768]{1,0:T(8,128)(2,1)}, bf16[48,768]{1,0:T(8,128)(2,1)S(1)}, u32[]{:S(2)}, u32[]{:S(2)}) collective-permute-start(bf16[48,768]{1,0:T(8,128)(2,1)} %refs_1_.1), channel_id=1, source_target_pairs={{0,12},{1,13},{2,14},{3,15},{4,8},{5,9},{6,10},{7,11},{8,4},{9,5},... | collective-permute-start | bytes 221192 | tf_op jit(solution)/shard_map/ppermute | solution.py:299
  7.3 7.1 %collective-permute-start.3 = (bf16[48,768]{1,0:T(8,128)(2,1)}, bf16[48,768]{1,0:T(8,128)(2,1)S(1)}, u32[]{:S(2)}, u32[]{:S(2)}) collective-permute-start(bf16[48,768]{1,0:T(8,128)(2,1)} %refs_1_.1), channel_id=1, source_target_pairs={{0,4},{1,5},{2,6},{3,7},{4,0},{5,1},{6,2},{7,3},{8,12},{9,13},{10,... | collective-permute-start | bytes 221192 | tf_op jit(solution)/shard_map/ppermute | solution.py:299
  7.3 13.8 %collective-permute-start.8 = (bf16[128,768]{1,0:T(8,128)(2,1)}, bf16[128,768]{1,0:T(8,128)(2,1)S(1)}, u32[]{:S(2)}, u32[]{:S(2)}) collective-permute-start(bf16[128,768]{1,0:T(8,128)(2,1)} %refs_0_.1), channel_id=1, source_target_pairs={{0,4},{1,5},{2,6},{3,7},{4,0},{5,1},{6,2},{7,3},{8,12},{9,13},{10,... | collective-permute-start | bytes 589832 | tf_op jit(solution)/shard_map/ppermute | solution.py:299
  11.7 11.3 %collective-permute-start.1 = (bf16[144,768]{1,0:T(8,128)(2,1)S(1)}, bf16[144,768]{1,0:T(8,128)(2,1)S(1)}, u32[]{:S(2)}, u32[]{:S(2)}) collective-permute-start(bf16[144,768]{1,0:T(8,128)(2,1)S(1)} %get-tuple-element.29.refs_1_.refs_3_.refs_2_), channel_id=1, source_target_pairs={{0,12},{1,13},{2,14},{3,15},{4,8},{5,9},{6,10},{7,11},{8,4},{9,5},... | collective-permute-start | bytes 663560 | tf_op jit(solution)/shard_map/ppermute | solution.py:299
  14.5 8.6 %collective-permute-start.5 = (bf16[112,768]{1,0:T(8,128)(2,1)S(1)}, bf16[112,768]{1,0:T(8,128)(2,1)S(1)}, u32[]{:S(2)}, u32[]{:S(2)}) collective-permute-start(bf16[112,768]{1,0:T(8,128)(2,1)S(1)} %shard_map.124), channel_id=1, source_target_pairs={{0,2},{1,3},{2,0},{3,1},{4,6},{5,7},{6,4},{7,5},{8,10},{9,11},{10,... | collective-permute-start | bytes 516104 | tf_op jit(solution)/shard_map/ppermute | solution.py:299
  15.1 8.0 %collective-permute-start.2 = (bf16[64,768]{1,0:T(8,128)(2,1)S(1)}, bf16[64,768]{1,0:T(8,128)(2,1)S(1)}, u32[]{:S(2)}, u32[]{:S(2)}) collective-permute-start(bf16[64,768]{1,0:T(8,128)(2,1)S(1)} %shard_map.123), channel_id=1, source_target_pairs={{0,4},{1,5},{2,6},{3,7},{4,0},{5,1},{6,2},{7,3},{8,12},{9,13},{10,... | collective-permute-start | bytes 294920 | tf_op jit(solution)/shard_map/ppermute | solution.py:299
  21.1 7.3 %collective-permute-start.9 = (bf16[128,768]{1,0:T(8,128)(2,1)S(1)}, bf16[128,768]{1,0:T(8,128)(2,1)S(1)}, u32[]{:S(2)}, u32[]{:S(2)}) collective-permute-start(bf16[128,768]{1,0:T(8,128)(2,1)S(1)} %collective-permute-done.8.refs_0_), channel_id=1, source_target_pairs={{0,2},{1,3},{2,0},{3,1},{4,6},{5,7},{6,4},{7,5},{8,10},{9,11},{10,... | collective-permute-start | bytes 589832 | tf_op jit(solution)/shard_map/ppermute | solution.py:299
  23.1 7.4 %collective-permute-start.10 = (bf16[112,768]{1,0:T(8,128)(2,1)S(1)}, bf16[112,768]{1,0:T(8,128)(2,1)S(1)}, u32[]{:S(2)}, u32[]{:S(2)}) collective-permute-start(bf16[112,768]{1,0:T(8,128)(2,1)S(1)} %shard_map.126), channel_id=1, source_target_pairs={{0,2},{1,3},{2,0},{3,1},{4,6},{5,7},{6,4},{7,5},{8,10},{9,11},{10,... | collective-permute-start | bytes 516104 | tf_op jit(solution)/shard_map/ppermute | solution.py:299
  24.7 6.5 %collective-permute-start.7 = (bf16[144,768]{1,0:T(8,128)(2,1)S(1)}, bf16[144,768]{1,0:T(8,128)(2,1)S(1)}, u32[]{:S(2)}, u32[]{:S(2)}) collective-permute-start(bf16[144,768]{1,0:T(8,128)(2,1)S(1)} %collective-permute-done.1.refs_0_.refs_3_.refs_6_), channel_id=1, source_target_pairs={{0,4},{1,5},{2,6},{3,7},{4,0},{5,1},{6,2},{7,3},{8,12},{9,13},{10,... | collective-permute-start | bytes 663560 | tf_op jit(solution)/shard_map/ppermute | solution.py:299
  30.5 1.5 %collective-permute-start.11 = (bf16[128,768]{1,0:T(8,128)(2,1)S(1)}, bf16[128,768]{1,0:T(8,128)(2,1)S(1)}, u32[]{:S(2)}, u32[]{:S(2)}) collective-permute-start(bf16[128,768]{1,0:T(8,128)(2,1)S(1)} %get-tuple-element.38.refs_5_), channel_id=1, source_target_pairs={{0,1},{1,0},{2,3},{3,2},{4,5},{5,4},{6,7},{7,6},{8,9},{9,8},{10,11... | collective-permute-start | bytes 589832 | tf_op jit(solution)/shard_map/ppermute | solution.py:302
  30.6 1.7 %collective-permute-start.12 = (bf16[128,768]{1,0:T(8,128)(2,1)S(1)}, bf16[128,768]{1,0:T(8,128)(2,1)S(1)}, u32[]{:S(2)}, u32[]{:S(2)}) collective-permute-start(bf16[128,768]{1,0:T(8,128)(2,1)S(1)} %get-tuple-element.39.refs_6_), channel_id=1, source_target_pairs={{0,1},{1,0},{2,3},{3,2},{4,5},{5,4},{6,7},{7,6},{8,9},{9,8},{10,11... | collective-permute-start | bytes 589832 | tf_op jit(solution)/shard_map/ppermute | solution.py:302
  31.1 1.5 %collective-permute-start.13 = (bf16[128,768]{1,0:T(8,128)(2,1)S(1)}, bf16[128,768]{1,0:T(8,128)(2,1)S(1)}, u32[]{:S(2)}, u32[]{:S(2)}) collective-permute-start(bf16[128,768]{1,0:T(8,128)(2,1)S(1)} %get-tuple-element.40.refs_7_), channel_id=1, source_target_pairs={{0,1},{1,0},{2,3},{3,2},{4,5},{5,4},{6,7},{7,6},{8,9},{9,8},{10,11... | collective-permute-start | bytes 589832 | tf_op jit(solution)/shard_map/ppermute | solution.py:302
  31.2 8.2 %collective-permute-start.15 = (bf16[144,768]{1,0:T(8,128)(2,1)S(1)}, bf16[144,768]{1,0:T(8,128)(2,1)S(1)}, u32[]{:S(2)}, u32[]{:S(2)}) collective-permute-start(bf16[144,768]{1,0:T(8,128)(2,1)S(1)} %collective-permute-done.1.refs_0_.refs_3_.refs_6_), channel_id=1, source_target_pairs={{0,2},{1,3},{2,0},{3,1},{4,6},{5,7},{6,4},{7,5},{8,10},{9,11},{10,... | collective-permute-start | bytes 663560 | tf_op jit(solution)/shard_map/ppermute | solution.py:299
  34.4 9.3 %collective-permute-start.14 = (bf16[144,768]{1,0:T(8,128)(2,1)S(1)}, bf16[144,768]{1,0:T(8,128)(2,1)S(1)}, u32[]{:S(2)}, u32[]{:S(2)}) collective-permute-start(bf16[144,768]{1,0:T(8,128)(2,1)S(1)} %shard_map.127.refs_2_.refs_5_.refs_8_), channel_id=1, source_target_pairs={{0,2},{1,3},{2,0},{3,1},{4,6},{5,7},{6,4},{7,5},{8,10},{9,11},{10,... | collective-permute-start | bytes 663560 | tf_op jit(solution)/shard_map/ppermute | solution.py:299
  36.9 6.8 %copy-start = (f32[15360]{0:T(1024)S(1)}, f32[15360]{0:T(1024)}, u32[]{:S(2)}) copy-start(f32[15360]{0:T(1024)} %param.18) | copy-start | bytes 184324
  45.7 1.3 %collective-permute-start.16 = (bf16[8,32,128]{2,1,0:T(8,128)(2,1)S(1)}, bf16[8,32,128]{2,1,0:T(8,128)(2,1)S(1)}, u32[]{:S(2)}, u32[]{:S(2)}) collective-permute-start(bf16[8,32,128]{2,1,0:T(8,128)(2,1)S(1)} %get-tuple-element.53), channel_id=1, source_target_pairs={{0,1},{1,0},{2,3},{3,2},{4,5},{5,4},{6,7},{7,6},{8,9},{9,8},{10,11... | collective-permute-start | bytes 196616 | tf_op jit(solution)/shard_map/ppermute | solution.py:302

commit v22 on v21

--- a/solution.py
+++ b/solution.py
@@ -184,8 +184,9 @@
         copy.wait()
 
 
-def first_kernel(seq, shard, masks, *refs):
-    me_ref, docs, tables, refs = refs[0], refs[1:3], refs[3:5], refs[5:]
+def first_kernel(seq, shard, masks, count, *refs):
+    me_ref, docs, refs = refs[0], refs[1 : 1 + count], refs[1 + count :]
+    tables, refs = refs[:count], refs[count:]
     count = len(masks) * shard // seq
     parts, others, refs = refs[:count], refs[count : 2 * count], refs[2 * count :]
     params, halves, refs = refs[0], refs[1:3], refs[3:]
@@ -378,40 +379,39 @@
         scratch_shapes=[pltpu.SemaphoreType.DMA((1,))],
         compiler_params=limit,
     )(table, *far_from)
-    far = (block_6, after(block_4, near_pile, docs[6], mine, theirs))
+    far = (block_6, after(block_4, near_pile, mine, theirs))
     far = pile(far, (one, (0, rows + SLOT_ROWS)))
     far_pile = cross(far, 1)
-    docs[4] = pile((cross(after(docs[6], far), 2),), ((0, seq + SLOT_ROWS),))
+    docs[4] = cross(after(docs[6], far), 2)
     docs[7] = cross(docs[6], 1)
     sources = (after(block, docs[6], docs[3]), block_2, block_6, block_4, near_pile, far_pile)
     packed = pile(sources, (one, one, one, one, two, two), (seq,) * (chips * rows // seq))
     other_packed = [swap(part) for part in packed]
     block_masks = [0, 2, 6, 4, 1, 3, 7, 5]
 
-    groups = [[0, 1], [2, 3], [6, 7, 4], [5]]
+    groups = [[6, 7, 0], [1, 2, 3], [4, 5]]
     masks = [mask for group in groups for mask in group]
     docs[0] = load
+    docs[5] = cross(after(docs[4], docs[7], *other_packed), 1)
     tables = docs | {1: near_pile, 2: block_4, 3: far_pile}
     best_shape = shape((8, half), jnp.float32)
     *best, weight = pl.pallas_call(
-        lambda *refs: first_kernel(seq, rows, block_masks, *refs),
+        lambda *refs: first_kernel(seq, rows, block_masks, len(groups[0]), *refs),
         out_shape=[best_shape, best_shape, shape((width, width), jnp.bfloat16)],
-        in_specs=[smem] + [vmem] * (7 + 2 * len(packed)),
+        in_specs=[smem] + [vmem] * (2 * len(groups[0]) + 3 + 2 * len(packed)),
         out_specs=[vmem] * 3,
         compiler_params=limit,
         cost_estimate=cost(2),
     )(
         where,
-        *[docs[mask] for mask in masks[:2]],
-        *[tables[mask] for mask in masks[:2]],
+        *[docs[mask] for mask in groups[0]],
+        *[tables[mask] for mask in groups[0]],
         *packed,
         *other_packed,
         params,
         mine,
         theirs,
     )
-    docs[5] = cross(after(docs[4], weight), 1)
-    tables[5] = docs[5]
     for group in groups[1:-1]:
         best += pl.pallas_call(
             lambda *refs, count=len(group): next_kernel(seq, count, *refs),

time: 57.5 us -> 52.8 us (0.918)
  waiting for transfers between devices: 18.9 us -> 13.2 us
  starting transfers between devices: 15.6 us -> 17 us
  Pallas kernels: 11.9 us -> 10.9 us
    ppermute x12, waiting for transfers between devices: 16.2 us -> 12 us  [cross(): lax.ppermute(value, 'doc', [(i, i ^ 2 * mask) for i in range(devices)])]
    pallas_call x2 -> x1, Pallas kernels: 4.19 us -> 2.42 us  [move_tokens(): pl.pallas_call(lambda *refs, count=len(group): next_kernel(seq, count, *r...]
    ppermute x5, waiting for transfers between devices: 2.63 us -> 1.25 us  [swap(): return lax.ppermute(value, 'doc', [(i, i ^ 1) for i in range(devices)])]
    ppermute x12, starting transfers between devices: 14.4 us -> 15.7 us  [cross(): lax.ppermute(value, 'doc', [(i, i ^ 2 * mask) for i in range(devices)])]
    pallas_call x1, Pallas kernels: 1.78 us -> 2.45 us  [move_tokens(): pl.pallas_call(lambda *refs: first_kernel(seq, rows, block_masks, len(gro...]
  transfers between devices with their start and end apart: 17 -> 17, of which waited for: 10 -> 8; matrix products, arithmetic and copies ran while one was open for 0% -> 0% of each run, Pallas kernels for 16% -> 15%
where the time goes in v22:
time: 52.8 us; the launch traced here: 52.6 us
  starting transfers between devices  17 us (32%)
  waiting for transfers between devices  13.2 us (25%)
  Pallas kernels  10.9 us (21%)
  blocking collectives  10 us (19%)
  between operations  1.4 us (3%)
    ppermute x12, starting transfers between devices, cross(): lax.ppermute(value, 'doc', [(i, i ^ 2 * mask) for i in range(devices)])  15.7 us
    ppermute x12, waiting for transfers between devices, cross(): lax.ppermute(value, 'doc', [(i, i ^ 2 * mask) for i in range(devices)])  12 us
    all_to_all x1, blocking collectives, move_tokens(): lax.all_to_all(merged, 'doc', split_axis=0, concat_axis=0, axis_index_gro...  10 us
    pallas_call x1, Pallas kernels, move_tokens(): pl.pallas_call(lambda *refs: first_kernel(seq, rows, block_masks, len(gro...  2.45 us
    pallas_call x1, Pallas kernels, move_tokens(): pl.pallas_call(lambda *refs, count=len(group): next_kernel(seq, count, *r...  2.42 us
    pallas_call x1, Pallas kernels, move_tokens(): pl.pallas_call(lambda *refs: last_kernel(seq, groups, *refs), out_shape=[...  2.13 us
    pallas_call x1, Pallas kernels, move_tokens(): pl.pallas_call(start_kernel, out_shape=[shape((seq + SLOT_ROWS, width), j...  1.71 us
    pallas_call x1, Pallas kernels, move_tokens(): pl.pallas_call(lambda *refs: fetch_kernel(1, *refs), out_shape=[shape(val...  1.38 us
  transfers between devices with their start and end apart: 17, of which 8 were waited for; matrix products, arithmetic and copies ran while one was open for 0% of the time, Pallas kernels for 15%

profile of v22, /device:TPU:0, one launch (start us, length us, event | category | flops | bytes accessed | tf_op | source)
XLA Modules:
  0.0 52.6 jit_solution(15063575196964863513)
XLA Ops:
  0.6 0.5 collective-permute-start.6
  1.2 2.6 %collective-permute-start.4 = (bf16[128,768]{1,0:T(8,128)(2,1)}, bf16[128,768]{1,0:T(8,128)(2,1)S(1)}, u32[]{:S(2)}, u32[]{:S(2)}) collective-permute-start(bf16[128,768]{1,0:T(8,128)(2,1)} %refs_0_.1), channel_id=1, source_target_pairs={{0,2},{1,3},{2,0},{3,1},{4,6},{5,7},{6,4},{7,5},{8,10},{9,11},{10,... | collective-permute-start | bytes 589832 | tf_op jit(solution)/shard_map/ppermute | solution.py:300
  3.7 3.6 %collective-permute-start = (bf16[48,768]{1,0:T(8,128)(2,1)}, bf16[48,768]{1,0:T(8,128)(2,1)S(1)}, u32[]{:S(2)}, u32[]{:S(2)}) collective-permute-start(bf16[48,768]{1,0:T(8,128)(2,1)} %refs_1_.1), channel_id=1, source_target_pairs={{0,12},{1,13},{2,14},{3,15},{4,8},{5,9},{6,10},{7,11},{8,4},{9,5},... | collective-permute-start | bytes 221192 | tf_op jit(solution)/shard_map/ppermute | solution.py:300
  7.3 0.0 collective-permute-start.3
  7.3 2.0 %collective-permute-start.9 = (bf16[128,768]{1,0:T(8,128)(2,1)}, bf16[128,768]{1,0:T(8,128)(2,1)S(1)}, u32[]{:S(2)}, u32[]{:S(2)}) collective-permute-start(bf16[128,768]{1,0:T(8,128)(2,1)} %refs_0_.1), channel_id=1, source_target_pairs={{0,4},{1,5},{2,6},{3,7},{4,0},{5,1},{6,2},{7,3},{8,12},{9,13},{10,... | collective-permute-start | bytes 589832 | tf_op jit(solution)/shard_map/ppermute | solution.py:300
  10.0 1.7 %shard_map.122 = (bf16[144,768]{1,0:T(8,128)(2,1)S(1)}, bf16[48,768]{1,0:T(8,128)(2,1)S(1)}, bf16[16,768]{1,0:T(8,128)(2,1)S(1)}, f32[8,768]{1,0:T(8,128)S(1)}) custom-call(s32[1]{0:T(128)} %bitcast.me_ref.refs_0_, s32[1,1,32]{2,1,0:T(1,128)} %tiles_ref.1, s32[1,1,32]{2,1,0:T(1,128)} %bitcast.9, s32[1,1,32]{2,1,0:T(1,128)} %slots_ref.1, ...), custom_call_target="tpu_custom_call" | custom-call | tf_op jit(solution)/shard_map/pallas_call | solution.py:340
  11.7 0.0 collective-permute-done.refs_0_.refs_2_
  11.7 1.0 %collective-permute-done.3.refs_1_ = bf16[48,768]{1,0:T(8,128)(2,1)S(1)} collective-permute-done((bf16[48,768]{1,0:T(8,128)(2,1)}, bf16[48,768]{1,0:T(8,128)(2,1)S(1)}, u32[]{:S(2)}, u32[]{:S(2)}) %collective-permute-start.3) | collective-permute-done | bytes 73760 | tf_op jit(solution)/shard_map/ppermute | solution.py:300
  12.7 0.0 collective-permute-done.4.refs_0_
  12.7 0.6 %collective-permute-start.5 = (bf16[112,768]{1,0:T(8,128)(2,1)S(1)}, bf16[112,768]{1,0:T(8,128)(2,1)S(1)}, u32[]{:S(2)}, u32[]{:S(2)}) collective-permute-start(bf16[112,768]{1,0:T(8,128)(2,1)S(1)} %shard_map.124), channel_id=1, source_target_pairs={{0,2},{1,3},{2,0},{3,1},{4,6},{5,7},{6,4},{7,5},{8,10},{9,11},{10,... | collective-permute-start | bytes 516104 | tf_op jit(solution)/shard_map/ppermute | solution.py:300
  13.3 1.6 %collective-permute-start.2 = (bf16[64,768]{1,0:T(8,128)(2,1)S(1)}, bf16[64,768]{1,0:T(8,128)(2,1)S(1)}, u32[]{:S(2)}, u32[]{:S(2)}) collective-permute-start(bf16[64,768]{1,0:T(8,128)(2,1)S(1)} %shard_map.123), channel_id=1, source_target_pairs={{0,4},{1,5},{2,6},{3,7},{4,0},{5,1},{6,2},{7,3},{8,12},{9,13},{10,... | collective-permute-start | bytes 294920 | tf_op jit(solution)/shard_map/ppermute | solution.py:300
  14.9 0.5 collective-permute-start.1
  15.4 1.5 %collective-permute-done.9.refs_1_ = bf16[128,768]{1,0:T(8,128)(2,1)S(1)} collective-permute-done((bf16[128,768]{1,0:T(8,128)(2,1)}, bf16[128,768]{1,0:T(8,128)(2,1)S(1)}, u32[]{:S(2)}, u32[]{:S(2)}) %collective-permute-start.9) | collective-permute-done | bytes 196640 | tf_op jit(solution)/shard_map/ppermute | solution.py:300
  16.9 0.4 collective-permute-start.10
  17.3 1.4 %shard_map.125.refs_14_.refs_8_.refs_13_ = bf16[960,768]{1,0:T(8,128)(2,1)S(1)} custom-call(bf16[16,768]{1,0:T(8,128)(2,1)S(1)} %get-tuple-element.27.refs_1_.refs_2_.refs_0_, bf16[960,768]{1,0:T(8,128)(2,1)} %bitcast.8), custom_call_target="tpu_custom_call" | custom-call | tf_op jit(solution)/shard_map/pallas_call | solution.py:374
  18.7 4.4 %collective-permute-done.2.refs_1_.refs_3_.refs_4_.refs_7_ = bf16[64,768]{1,0:T(8,128)(2,1)S(1)} collective-permute-done((bf16[64,768]{1,0:T(8,128)(2,1)S(1)}, bf16[64,768]{1,0:T(8,128)(2,1)S(1)}, u32[]{:S(2)}, u32[]{:S(2)}) %collective-permute-start.2) | collective-permute-done | bytes 98336 | tf_op jit(solution)/shard_map/ppermute | solution.py:300
  23.1 0.0 collective-permute-done.5.refs_4_.refs_3_.refs_6_
  23.1 0.0 collective-permute-done.6.refs_15_.refs_9_.refs_14_
  23.1 0.1 collective-permute-start.11
  23.2 0.0 collective-permute-done.1.refs_1_.refs_4_.refs_3_
  23.2 2.0 %collective-permute-start.8 = (bf16[144,768]{1,0:T(8,128)(2,1)S(1)}, bf16[144,768]{1,0:T(8,128)(2,1)S(1)}, u32[]{:S(2)}, u32[]{:S(2)}) collective-permute-start(bf16[144,768]{1,0:T(8,128)(2,1)S(1)} %collective-permute-done.1.refs_1_.refs_4_.refs_3_), channel_id=1, source_target_pairs={{0,2},{1,3},{2,0},{3,1},{4,6},{5,7},{6,4},{7,5},{8,10},{9,11},{10,... | collective-permute-start | bytes 663560 | tf_op jit(solution)/shard_map/ppermute | solution.py:300
  25.2 2.0 %collective-permute-start.7 = (bf16[144,768]{1,0:T(8,128)(2,1)S(1)}, bf16[144,768]{1,0:T(8,128)(2,1)S(1)}, u32[]{:S(2)}, u32[]{:S(2)}) collective-permute-start(bf16[144,768]{1,0:T(8,128)(2,1)S(1)} %collective-permute-done.1.refs_1_.refs_4_.refs_3_), channel_id=1, source_target_pairs={{0,4},{1,5},{2,6},{3,7},{4,0},{5,1},{6,2},{7,3},{8,12},{9,13},{10,... | collective-permute-start | bytes 663560 | tf_op jit(solution)/shard_map/ppermute | solution.py:300
  27.1 0.0 collective-permute-done.10.refs_2_
  27.1 1.5 %collective-permute-done.11.refs_5_.refs_8_ = bf16[112,768]{1,0:T(8,128)(2,1)S(1)} collective-permute-done((bf16[112,768]{1,0:T(8,128)(2,1)S(1)}, bf16[112,768]{1,0:T(8,128)(2,1)S(1)}, u32[]{:S(2)}, u32[]{:S(2)}) %collective-permute-start.11) | collective-permute-done | bytes 172064 | tf_op jit(solution)/shard_map/ppermute | solution.py:300
  28.7 0.1 collective-permute-start.12
  28.7 0.5 collective-permute-start.13
  29.2 0.1 collective-permute-start.14
  29.3 1.7 %collective-permute-done.8.refs_2_.refs_5_.refs_4_ = bf16[144,768]{1,0:T(8,128)(2,1)S(1)} collective-permute-done((bf16[144,768]{1,0:T(8,128)(2,1)S(1)}, bf16[144,768]{1,0:T(8,128)(2,1)S(1)}, u32[]{:S(2)}, u32[]{:S(2)}) %collective-permute-start.8) | collective-permute-done | bytes 221216 | tf_op jit(solution)/shard_map/ppermute | solution.py:300
  31.0 0.1 collective-permute-done.7.refs_1_.refs_9_
  31.1 0.0 collective-permute-done.12.refs_10_
  31.1 0.0 collective-permute-done.13.refs_11_
  31.1 0.0 collective-permute-done.14.refs_12_
  31.1 0.4 collective-permute-start.15
  31.5 2.4 %shard_map.128 = (f32[8,960]{1,0:T(8,128)S(1)}, f32[8,960]{1,0:T(8,128)S(1)}, bf16[768,768]{1,0:T(8,128)(2,1)S(1)}) custom-call(s32[1]{0:T(128)} %bitcast.me_ref.refs_0_, bf16[144,768]{1,0:T(8,128)(2,1)S(1)} %collective-permute-done.1.refs_1_.refs_4_.refs_3_, bf16[144,768]{1,0:T(8,128)(2,1)S(1)} %collective-permute-done.8.refs_2_.refs_5_.refs_4_, ...), custom_call_target="tpu_custom_call" | custom-call | flops 2 | bytes 2 | tf_op jit(solution)/shard_map/pallas_call | solution.py:398
  34.0 0.0 copy-start
  34.0 2.4 %shard_map.129 = (f32[8,960]{1,0:T(8,128)S(1)}, f32[8,960]{1,0:T(8,128)S(1)}) custom-call(bf16[128,768]{1,0:T(8,128)(2,1)S(1)} %collective-permute-done.4.refs_0_, bf16[128,768]{1,0:T(8,128)(2,1)S(1)} %collective-permute-done.9.refs_1_, bf16[128,768]{1,0:T(8,128)(2,1)S(1)} %collective-permute-done.10.refs_2_, ...), custom_call_target="tpu_custom_call" | custom-call | flops 3 | bytes 3 | tf_op jit(solution)/shard_map/pallas_call | solution.py:416
  36.4 1.9 %collective-permute-done.15.refs_2_.refs_10_ = bf16[144,768]{1,0:T(8,128)(2,1)S(1)} collective-permute-done((bf16[144,768]{1,0:T(8,128)(2,1)S(1)}, bf16[144,768]{1,0:T(8,128)(2,1)S(1)}, u32[]{:S(2)}, u32[]{:S(2)}) %collective-permute-start.15) | collective-permute-done | bytes 221216 | tf_op jit(solution)/shard_map/ppermute | solution.py:300
  38.3 0.0 copy-done
  38.3 2.1 %shard_map.130 = (bf16[8,48,128]{2,1,0:T(8,128)(2,1)S(1)}, bf16[8,32,128]{2,1,0:T(8,128)(2,1)S(1)}) custom-call(s32[1]{0:T(128)} %bitcast.me_ref.refs_0_, bf16[144,768]{1,0:T(8,128)(2,1)S(1)} %collective-permute-done.7.refs_1_.refs_9_, bf16[144,768]{1,0:T(8,128)(2,1)S(1)} %collective-permute-done.15.refs_2_.refs_10_, ...), custom_call_target="tpu_custom_call" | custom-call | flops 2 | bytes 2 | tf_op jit(solution)/shard_map/pallas_call | solution.py:432
  40.4 0.1 collective-permute-start.16
  40.5 1.2 %collective-permute-done.16.got_ref = bf16[8,32,128]{2,1,0:T(8,128)(2,1)S(1)} collective-permute-done((bf16[8,32,128]{2,1,0:T(8,128)(2,1)S(1)}, bf16[8,32,128]{2,1,0:T(8,128)(2,1)S(1)}, u32[]{:S(2)}, u32[]{:S(2)}) %collective-permute-start.16) | collective-permute-done | bytes 65568 | tf_op jit(solution)/shard_map/ppermute | solution.py:303
  41.8 10.0 %all_to_all.5.refs_0_ = bf16[8,48,128]{2,1,0:T(8,128)(2,1)S(1)} all-to-all(bf16[8,48,128]{2,1,0:T(8,128)(2,1)S(1)} %shard_map.131), channel_id=1, replica_groups={{0,2,4,6,8,10,12,14},{1,3,5,7,9,11,13,15},{16,18,20,22,24,26,28,30},{17..., dimensions={0} | all-to-all | bytes 196608 | tf_op jit(solution)/shard_map/all_to_all | solution.py:462
  51.8 0.8 %shard_map.132 = (bf16[1,15360]{1,0:T(2,128)(2,1)}, bf16[2,15360]{1,0:T(2,128)(2,1)}) custom-call(bf16[8,48,128]{2,1,0:T(8,128)(2,1)S(1)} %all_to_all.5.refs_0_), custom_call_target="tpu_custom_call" | custom-call | tf_op jit(solution)/shard_map/pallas_call | solution.py:465
  (5 shorter events, 0.1 us)
Async XLA Ops:
  0.6 22.4 %collective-permute-start.6 = (bf16[960,768]{1,0:T(8,128)(2,1)}, bf16[960,768]{1,0:T(8,128)(2,1)S(1)}, u32[]{:S(2)}, u32[]{:S(2)}) collective-permute-start(bf16[960,768]{1,0:T(8,128)(2,1)} %bitcast.7), channel_id=1, source_target_pairs={{0,1},{1,0},{2,3},{3,2},{4,5},{5,4},{6,7},{7,6},{8,9},{9,8},{10,11... | collective-permute-start | bytes 4423688 | tf_op jit(solution)/shard_map/ppermute | solution.py:303
  1.2 11.5 %collective-permute-start.4 = (bf16[128,768]{1,0:T(8,128)(2,1)}, bf16[128,768]{1,0:T(8,128)(2,1)S(1)}, u32[]{:S(2)}, u32[]{:S(2)}) collective-permute-start(bf16[128,768]{1,0:T(8,128)(2,1)} %refs_0_.1), channel_id=1, source_target_pairs={{0,2},{1,3},{2,0},{3,1},{4,6},{5,7},{6,4},{7,5},{8,10},{9,11},{10,... | collective-permute-start | bytes 589832 | tf_op jit(solution)/shard_map/ppermute | solution.py:300
  3.7 8.0 %collective-permute-start = (bf16[48,768]{1,0:T(8,128)(2,1)}, bf16[48,768]{1,0:T(8,128)(2,1)S(1)}, u32[]{:S(2)}, u32[]{:S(2)}) collective-permute-start(bf16[48,768]{1,0:T(8,128)(2,1)} %refs_1_.1), channel_id=1, source_target_pairs={{0,12},{1,13},{2,14},{3,15},{4,8},{5,9},{6,10},{7,11},{8,4},{9,5},... | collective-permute-start | bytes 221192 | tf_op jit(solution)/shard_map/ppermute | solution.py:300
  7.3 5.4 %collective-permute-start.3 = (bf16[48,768]{1,0:T(8,128)(2,1)}, bf16[48,768]{1,0:T(8,128)(2,1)S(1)}, u32[]{:S(2)}, u32[]{:S(2)}) collective-permute-start(bf16[48,768]{1,0:T(8,128)(2,1)} %refs_1_.1), channel_id=1, source_target_pairs={{0,4},{1,5},{2,6},{3,7},{4,0},{5,1},{6,2},{7,3},{8,12},{9,13},{10,... | collective-permute-start | bytes 221192 | tf_op jit(solution)/shard_map/ppermute | solution.py:300
  7.3 9.6 %collective-permute-start.9 = (bf16[128,768]{1,0:T(8,128)(2,1)}, bf16[128,768]{1,0:T(8,128)(2,1)S(1)}, u32[]{:S(2)}, u32[]{:S(2)}) collective-permute-start(bf16[128,768]{1,0:T(8,128)(2,1)} %refs_0_.1), channel_id=1, source_target_pairs={{0,4},{1,5},{2,6},{3,7},{4,0},{5,1},{6,2},{7,3},{8,12},{9,13},{10,... | collective-permute-start | bytes 589832 | tf_op jit(solution)/shard_map/ppermute | solution.py:300
  12.7 10.4 %collective-permute-start.5 = (bf16[112,768]{1,0:T(8,128)(2,1)S(1)}, bf16[112,768]{1,0:T(8,128)(2,1)S(1)}, u32[]{:S(2)}, u32[]{:S(2)}) collective-permute-start(bf16[112,768]{1,0:T(8,128)(2,1)S(1)} %shard_map.124), channel_id=1, source_target_pairs={{0,2},{1,3},{2,0},{3,1},{4,6},{5,7},{6,4},{7,5},{8,10},{9,11},{10,... | collective-permute-start | bytes 516104 | tf_op jit(solution)/shard_map/ppermute | solution.py:300
  13.3 9.7 %collective-permute-start.2 = (bf16[64,768]{1,0:T(8,128)(2,1)S(1)}, bf16[64,768]{1,0:T(8,128)(2,1)S(1)}, u32[]{:S(2)}, u32[]{:S(2)}) collective-permute-start(bf16[64,768]{1,0:T(8,128)(2,1)S(1)} %shard_map.123), channel_id=1, source_target_pairs={{0,4},{1,5},{2,6},{3,7},{4,0},{5,1},{6,2},{7,3},{8,12},{9,13},{10,... | collective-permute-start | bytes 294920 | tf_op jit(solution)/shard_map/ppermute | solution.py:300
  14.9 8.3 %collective-permute-start.1 = (bf16[144,768]{1,0:T(8,128)(2,1)S(1)}, bf16[144,768]{1,0:T(8,128)(2,1)S(1)}, u32[]{:S(2)}, u32[]{:S(2)}) collective-permute-start(bf16[144,768]{1,0:T(8,128)(2,1)S(1)} %get-tuple-element.26.refs_3_.refs_6_.refs_5_), channel_id=1, source_target_pairs={{0,12},{1,13},{2,14},{3,15},{4,8},{5,9},{6,10},{7,11},{8,4},{9,5},... | collective-permute-start | bytes 663560 | tf_op jit(solution)/shard_map/ppermute | solution.py:300
  16.9 10.2 %collective-permute-start.10 = (bf16[128,768]{1,0:T(8,128)(2,1)S(1)}, bf16[128,768]{1,0:T(8,128)(2,1)S(1)}, u32[]{:S(2)}, u32[]{:S(2)}) collective-permute-start(bf16[128,768]{1,0:T(8,128)(2,1)S(1)} %collective-permute-done.9.refs_1_), channel_id=1, source_target_pairs={{0,2},{1,3},{2,0},{3,1},{4,6},{5,7},{6,4},{7,5},{8,10},{9,11},{10,... | collective-permute-start | bytes 589832 | tf_op jit(solution)/shard_map/ppermute | solution.py:300
  23.1 5.5 %collective-permute-start.11 = (bf16[112,768]{1,0:T(8,128)(2,1)S(1)}, bf16[112,768]{1,0:T(8,128)(2,1)S(1)}, u32[]{:S(2)}, u32[]{:S(2)}) collective-permute-start(bf16[112,768]{1,0:T(8,128)(2,1)S(1)} %shard_map.126), channel_id=1, source_target_pairs={{0,2},{1,3},{2,0},{3,1},{4,6},{5,7},{6,4},{7,5},{8,10},{9,11},{10,... | collective-permute-start | bytes 516104 | tf_op jit(solution)/shard_map/ppermute | solution.py:300
  23.2 7.8 %collective-permute-start.8 = (bf16[144,768]{1,0:T(8,128)(2,1)S(1)}, bf16[144,768]{1,0:T(8,128)(2,1)S(1)}, u32[]{:S(2)}, u32[]{:S(2)}) collective-permute-start(bf16[144,768]{1,0:T(8,128)(2,1)S(1)} %collective-permute-done.1.refs_1_.refs_4_.refs_3_), channel_id=1, source_target_pairs={{0,2},{1,3},{2,0},{3,1},{4,6},{5,7},{6,4},{7,5},{8,10},{9,11},{10,... | collective-permute-start | bytes 663560 | tf_op jit(solution)/shard_map/ppermute | solution.py:300
  25.2 5.9 %collective-permute-start.7 = (bf16[144,768]{1,0:T(8,128)(2,1)S(1)}, bf16[144,768]{1,0:T(8,128)(2,1)S(1)}, u32[]{:S(2)}, u32[]{:S(2)}) collective-permute-start(bf16[144,768]{1,0:T(8,128)(2,1)S(1)} %collective-permute-done.1.refs_1_.refs_4_.refs_3_), channel_id=1, source_target_pairs={{0,4},{1,5},{2,6},{3,7},{4,0},{5,1},{6,2},{7,3},{8,12},{9,13},{10,... | collective-permute-start | bytes 663560 | tf_op jit(solution)/shard_map/ppermute | solution.py:300
  28.7 2.4 %collective-permute-start.12 = (bf16[128,768]{1,0:T(8,128)(2,1)S(1)}, bf16[128,768]{1,0:T(8,128)(2,1)S(1)}, u32[]{:S(2)}, u32[]{:S(2)}) collective-permute-start(bf16[128,768]{1,0:T(8,128)(2,1)S(1)} %get-tuple-element.35.refs_7_), channel_id=1, source_target_pairs={{0,1},{1,0},{2,3},{3,2},{4,5},{5,4},{6,7},{7,6},{8,9},{9,8},{10,11... | collective-permute-start | bytes 589832 | tf_op jit(solution)/shard_map/ppermute | solution.py:303
  28.7 2.4 %collective-permute-start.13 = (bf16[128,768]{1,0:T(8,128)(2,1)S(1)}, bf16[128,768]{1,0:T(8,128)(2,1)S(1)}, u32[]{:S(2)}, u32[]{:S(2)}) collective-permute-start(bf16[128,768]{1,0:T(8,128)(2,1)S(1)} %get-tuple-element.36.refs_8_), channel_id=1, source_target_pairs={{0,1},{1,0},{2,3},{3,2},{4,5},{5,4},{6,7},{7,6},{8,9},{9,8},{10,11... | collective-permute-start | bytes 589832 | tf_op jit(solution)/shard_map/ppermute | solution.py:303
  29.2 1.9 %collective-permute-start.14 = (bf16[128,768]{1,0:T(8,128)(2,1)S(1)}, bf16[128,768]{1,0:T(8,128)(2,1)S(1)}, u32[]{:S(2)}, u32[]{:S(2)}) collective-permute-start(bf16[128,768]{1,0:T(8,128)(2,1)S(1)} %get-tuple-element.37.refs_9_), channel_id=1, source_target_pairs={{0,1},{1,0},{2,3},{3,2},{4,5},{5,4},{6,7},{7,6},{8,9},{9,8},{10,11... | collective-permute-start | bytes 589832 | tf_op jit(solution)/shard_map/ppermute | solution.py:303
  31.1 7.2 %collective-permute-start.15 = (bf16[144,768]{1,0:T(8,128)(2,1)S(1)}, bf16[144,768]{1,0:T(8,128)(2,1)S(1)}, u32[]{:S(2)}, u32[]{:S(2)}) collective-permute-start(bf16[144,768]{1,0:T(8,128)(2,1)S(1)} %collective-permute-done.7.refs_1_.refs_9_), channel_id=1, source_target_pairs={{0,2},{1,3},{2,0},{3,1},{4,6},{5,7},{6,4},{7,5},{8,10},{9,11},{10,... | collective-permute-start | bytes 663560 | tf_op jit(solution)/shard_map/ppermute | solution.py:300
  34.0 4.3 %copy-start = (f32[15360]{0:T(1024)S(1)}, f32[15360]{0:T(1024)}, u32[]{:S(2)}) copy-start(f32[15360]{0:T(1024)} %param.18) | copy-start | bytes 184324
  40.4 1.3 %collective-permute-start.16 = (bf16[8,32,128]{2,1,0:T(8,128)(2,1)S(1)}, bf16[8,32,128]{2,1,0:T(8,128)(2,1)S(1)}, u32[]{:S(2)}, u32[]{:S(2)}) collective-permute-start(bf16[8,32,128]{2,1,0:T(8,128)(2,1)S(1)} %get-tuple-element.47), channel_id=1, source_target_pairs={{0,1},{1,0},{2,3},{3,2},{4,5},{5,4},{6,7},{7,6},{8,9},{9,8},{10,11... | collective-permute-start | bytes 196616 | tf_op jit(solution)/shard_map/ppermute | solution.py:303

commit v23 on v22

--- a/solution.py
+++ b/solution.py
@@ -370,7 +370,7 @@
     block_4 = cross(pile((block_6, table), (one, below)), 2)
     docs[6] = cross(after(load, block_6), 6)
     docs[3] = cross(after(docs[2], near), 1)
-    far_from = [stay(after(weight_rows, table))]
+    far_from = [stay(after(weight_rows, near))]
     [mine] = pl.pallas_call(
         lambda *refs: fetch_kernel(1, *refs),
         out_shape=[shape(value.shape, value.dtype) for value in far_from],
@@ -379,7 +379,7 @@
         scratch_shapes=[pltpu.SemaphoreType.DMA((1,))],
         compiler_params=limit,
     )(table, *far_from)
-    far = (block_6, after(block_4, near_pile, mine, theirs))
+    far = (block_6, after(block_4, mine, theirs))
     far = pile(far, (one, (0, rows + SLOT_ROWS)))
     far_pile = cross(far, 1)
     docs[4] = cross(after(docs[6], far), 2)

time: 52.8 us -> 56.6 us (1.072)
  waiting for transfers between devices: 13.2 us -> 17.2 us
    ppermute x12, waiting for transfers between devices: 12 us -> 15.9 us  [cross(): lax.ppermute(value, 'doc', [(i, i ^ 2 * mask) for i in range(devices)])]
  transfers between devices with their start and end apart: 17 -> 17, of which waited for: 8 -> 7; matrix products, arithmetic and copies ran while one was open for 0% -> 0% of each run, Pallas kernels for 15% -> 14%
where the time goes in v23:
time: 56.6 us; the launch traced here: 56.4 us
  starting transfers between devices  17.4 us (31%)
  waiting for transfers between devices  17.2 us (30%)
  Pallas kernels  11 us (19%)
  blocking collectives  9.51 us (17%)
  between operations  1.41 us (2%)
    ppermute x12, starting transfers between devices, cross(): lax.ppermute(value, 'doc', [(i, i ^ 2 * mask) for i in range(devices)])  16.1 us
    ppermute x12, waiting for transfers between devices, cross(): lax.ppermute(value, 'doc', [(i, i ^ 2 * mask) for i in range(devices)])  15.9 us
    all_to_all x1, blocking collectives, move_tokens(): lax.all_to_all(merged, 'doc', split_axis=0, concat_axis=0, axis_index_gro...  9.51 us
    pallas_call x1, Pallas kernels, move_tokens(): pl.pallas_call(lambda *refs: first_kernel(seq, rows, block_masks, len(gro...  2.45 us
    pallas_call x1, Pallas kernels, move_tokens(): pl.pallas_call(lambda *refs, count=len(group): next_kernel(seq, count, *r...  2.42 us
    pallas_call x1, Pallas kernels, move_tokens(): pl.pallas_call(lambda *refs: last_kernel(seq, groups, *refs), out_shape=[...  2.13 us
    pallas_call x1, Pallas kernels, move_tokens(): pl.pallas_call(start_kernel, out_shape=[shape((seq + SLOT_ROWS, width), j...  1.71 us
    pallas_call x1, Pallas kernels, move_tokens(): pl.pallas_call(lambda *refs: fetch_kernel(1, *refs), out_shape=[shape(val...  1.38 us
  transfers between devices with their start and end apart: 17, of which 7 were waited for; matrix products, arithmetic and copies ran while one was open for 0% of the time, Pallas kernels for 14%

profile of v23, /device:TPU:0, one launch (start us, length us, event | category | flops | bytes accessed | tf_op | source)
XLA Modules:
  0.0 56.4 jit_solution(4624157958564524598)
XLA Ops:
  0.6 0.5 collective-permute-start.5
  1.2 2.6 %collective-permute-start.4 = (bf16[128,768]{1,0:T(8,128)(2,1)}, bf16[128,768]{1,0:T(8,128)(2,1)S(1)}, u32[]{:S(2)}, u32[]{:S(2)}) collective-permute-start(bf16[128,768]{1,0:T(8,128)(2,1)} %refs_0_.1), channel_id=1, source_target_pairs={{0,2},{1,3},{2,0},{3,1},{4,6},{5,7},{6,4},{7,5},{8,10},{9,11},{10,... | collective-permute-start | bytes 589832 | tf_op jit(solution)/shard_map/ppermute | solution.py:300
  3.7 1.6 %collective-permute-start.8 = (bf16[128,768]{1,0:T(8,128)(2,1)}, bf16[128,768]{1,0:T(8,128)(2,1)S(1)}, u32[]{:S(2)}, u32[]{:S(2)}) collective-permute-start(bf16[128,768]{1,0:T(8,128)(2,1)} %refs_0_.1), channel_id=1, source_target_pairs={{0,4},{1,5},{2,6},{3,7},{4,0},{5,1},{6,2},{7,3},{8,12},{9,13},{10,... | collective-permute-start | bytes 589832 | tf_op jit(solution)/shard_map/ppermute | solution.py:300
  5.3 2.5 %collective-permute-start = (bf16[48,768]{1,0:T(8,128)(2,1)}, bf16[48,768]{1,0:T(8,128)(2,1)S(1)}, u32[]{:S(2)}, u32[]{:S(2)}) collective-permute-start(bf16[48,768]{1,0:T(8,128)(2,1)} %refs_1_.1), channel_id=1, source_target_pairs={{0,12},{1,13},{2,14},{3,15},{4,8},{5,9},{6,10},{7,11},{8,4},{9,5},... | collective-permute-start | bytes 221192 | tf_op jit(solution)/shard_map/ppermute | solution.py:300
  7.8 0.7 %collective-permute-start.3 = (bf16[48,768]{1,0:T(8,128)(2,1)}, bf16[48,768]{1,0:T(8,128)(2,1)S(1)}, u32[]{:S(2)}, u32[]{:S(2)}) collective-permute-start(bf16[48,768]{1,0:T(8,128)(2,1)} %refs_1_.1), channel_id=1, source_target_pairs={{0,4},{1,5},{2,6},{3,7},{4,0},{5,1},{6,2},{7,3},{8,12},{9,13},{10,... | collective-permute-start | bytes 221192 | tf_op jit(solution)/shard_map/ppermute | solution.py:300
  9.1 1.7 %shard_map.122 = (bf16[144,768]{1,0:T(8,128)(2,1)S(1)}, bf16[48,768]{1,0:T(8,128)(2,1)S(1)}, bf16[16,768]{1,0:T(8,128)(2,1)S(1)}, f32[8,768]{1,0:T(8,128)S(1)}) custom-call(s32[1]{0:T(128)} %bitcast.me_ref.refs_0_, s32[1,1,32]{2,1,0:T(1,128)} %tiles_ref.1, s32[1,1,32]{2,1,0:T(1,128)} %bitcast.9, s32[1,1,32]{2,1,0:T(1,128)} %slots_ref.1, ...), custom_call_target="tpu_custom_call" | custom-call | tf_op jit(solution)/shard_map/pallas_call | solution.py:340
  10.8 4.5 %collective-permute-done.refs_0_.refs_2_ = bf16[48,768]{1,0:T(8,128)(2,1)S(1)} collective-permute-done((bf16[48,768]{1,0:T(8,128)(2,1)}, bf16[48,768]{1,0:T(8,128)(2,1)S(1)}, u32[]{:S(2)}, u32[]{:S(2)}) %collective-permute-start) | collective-permute-done | bytes 73760 | tf_op jit(solution)/shard_map/ppermute | solution.py:300
  15.3 0.1 collective-permute-start.2
  15.4 0.0 collective-permute-done.3.refs_1_
  15.4 2.3 %collective-permute-start.1 = (bf16[144,768]{1,0:T(8,128)(2,1)S(1)}, bf16[144,768]{1,0:T(8,128)(2,1)S(1)}, u32[]{:S(2)}, u32[]{:S(2)}) collective-permute-start(bf16[144,768]{1,0:T(8,128)(2,1)S(1)} %get-tuple-element.26.refs_3_.refs_6_.refs_5_), channel_id=1, source_target_pairs={{0,12},{1,13},{2,14},{3,15},{4,8},{5,9},{6,10},{7,11},{8,4},{9,5},... | collective-permute-start | bytes 663560 | tf_op jit(solution)/shard_map/ppermute | solution.py:300
  17.7 0.0 collective-permute-done.4.refs_0_
  17.7 0.0 collective-permute-done.8.refs_1_
  17.7 0.6 %collective-permute-start.9 = (bf16[128,768]{1,0:T(8,128)(2,1)S(1)}, bf16[128,768]{1,0:T(8,128)(2,1)S(1)}, u32[]{:S(2)}, u32[]{:S(2)}) collective-permute-start(bf16[128,768]{1,0:T(8,128)(2,1)S(1)} %collective-permute-done.8.refs_1_), channel_id=1, source_target_pairs={{0,2},{1,3},{2,0},{3,1},{4,6},{5,7},{6,4},{7,5},{8,10},{9,11},{10,... | collective-permute-start | bytes 589832 | tf_op jit(solution)/shard_map/ppermute | solution.py:300
  18.3 1.5 %collective-permute-start.10 = (bf16[112,768]{1,0:T(8,128)(2,1)S(1)}, bf16[112,768]{1,0:T(8,128)(2,1)S(1)}, u32[]{:S(2)}, u32[]{:S(2)}) collective-permute-start(bf16[112,768]{1,0:T(8,128)(2,1)S(1)} %shard_map.124), channel_id=1, source_target_pairs={{0,2},{1,3},{2,0},{3,1},{4,6},{5,7},{6,4},{7,5},{8,10},{9,11},{10,... | collective-permute-start | bytes 516104 | tf_op jit(solution)/shard_map/ppermute | solution.py:300
  19.8 1.4 %shard_map.125.refs_14_.refs_8_.refs_13_ = bf16[960,768]{1,0:T(8,128)(2,1)S(1)} custom-call(bf16[16,768]{1,0:T(8,128)(2,1)S(1)} %get-tuple-element.27.refs_1_.refs_2_.refs_0_, bf16[960,768]{1,0:T(8,128)(2,1)} %bitcast.8), custom_call_target="tpu_custom_call" | custom-call | tf_op jit(solution)/shard_map/pallas_call | solution.py:374
  21.2 3.3 %collective-permute-done.2.refs_1_.refs_3_.refs_4_.refs_7_ = bf16[64,768]{1,0:T(8,128)(2,1)S(1)} collective-permute-done((bf16[64,768]{1,0:T(8,128)(2,1)S(1)}, bf16[64,768]{1,0:T(8,128)(2,1)S(1)}, u32[]{:S(2)}, u32[]{:S(2)}) %collective-permute-start.2) | collective-permute-done | bytes 98336 | tf_op jit(solution)/shard_map/ppermute | solution.py:300
  24.5 0.0 collective-permute-done.5.refs_15_.refs_9_.refs_14_
  24.5 0.6 %collective-permute-start.11 = (bf16[112,768]{1,0:T(8,128)(2,1)S(1)}, bf16[112,768]{1,0:T(8,128)(2,1)S(1)}, u32[]{:S(2)}, u32[]{:S(2)}) collective-permute-start(bf16[112,768]{1,0:T(8,128)(2,1)S(1)} %shard_map.126), channel_id=1, source_target_pairs={{0,2},{1,3},{2,0},{3,1},{4,6},{5,7},{6,4},{7,5},{8,10},{9,11},{10,... | collective-permute-start | bytes 516104 | tf_op jit(solution)/shard_map/ppermute | solution.py:300
  25.1 0.0 collective-permute-done.1.refs_1_.refs_4_.refs_3_
  25.1 1.5 %collective-permute-start.7 = (bf16[144,768]{1,0:T(8,128)(2,1)S(1)}, bf16[144,768]{1,0:T(8,128)(2,1)S(1)}, u32[]{:S(2)}, u32[]{:S(2)}) collective-permute-start(bf16[144,768]{1,0:T(8,128)(2,1)S(1)} %collective-permute-done.1.refs_1_.refs_4_.refs_3_), channel_id=1, source_target_pairs={{0,2},{1,3},{2,0},{3,1},{4,6},{5,7},{6,4},{7,5},{8,10},{9,11},{10,... | collective-permute-start | bytes 663560 | tf_op jit(solution)/shard_map/ppermute | solution.py:300
  26.6 1.7 %collective-permute-start.6 = (bf16[144,768]{1,0:T(8,128)(2,1)S(1)}, bf16[144,768]{1,0:T(8,128)(2,1)S(1)}, u32[]{:S(2)}, u32[]{:S(2)}) collective-permute-start(bf16[144,768]{1,0:T(8,128)(2,1)S(1)} %collective-permute-done.1.refs_1_.refs_4_.refs_3_), channel_id=1, source_target_pairs={{0,4},{1,5},{2,6},{3,7},{4,0},{5,1},{6,2},{7,3},{8,12},{9,13},{10,... | collective-permute-start | bytes 663560 | tf_op jit(solution)/shard_map/ppermute | solution.py:300
  28.3 0.0 collective-permute-done.9.refs_2_
  28.3 1.0 %collective-permute-done.10.refs_4_.refs_3_.refs_6_ = bf16[112,768]{1,0:T(8,128)(2,1)S(1)} collective-permute-done((bf16[112,768]{1,0:T(8,128)(2,1)S(1)}, bf16[112,768]{1,0:T(8,128)(2,1)S(1)}, u32[]{:S(2)}, u32[]{:S(2)}) %collective-permute-start.10) | collective-permute-done | bytes 172064 | tf_op jit(solution)/shard_map/ppermute | solution.py:300
  29.3 3.7 %collective-permute-done.11.refs_5_.refs_8_ = bf16[112,768]{1,0:T(8,128)(2,1)S(1)} collective-permute-done((bf16[112,768]{1,0:T(8,128)(2,1)S(1)}, bf16[112,768]{1,0:T(8,128)(2,1)S(1)}, u32[]{:S(2)}, u32[]{:S(2)}) %collective-permute-start.11) | collective-permute-done | bytes 172064 | tf_op jit(solution)/shard_map/ppermute | solution.py:300
  33.0 0.1 collective-permute-start.12
  33.1 0.5 collective-permute-start.13
  33.6 0.1 collective-permute-start.14
  33.7 2.1 %collective-permute-done.7.refs_2_.refs_5_.refs_4_ = bf16[144,768]{1,0:T(8,128)(2,1)S(1)} collective-permute-done((bf16[144,768]{1,0:T(8,128)(2,1)S(1)}, bf16[144,768]{1,0:T(8,128)(2,1)S(1)}, u32[]{:S(2)}, u32[]{:S(2)}) %collective-permute-start.7) | collective-permute-done | bytes 221216 | tf_op jit(solution)/shard_map/ppermute | solution.py:300
  35.7 0.0 collective-permute-done.6.refs_1_.refs_9_
  35.7 0.0 collective-permute-done.12.refs_10_
  35.7 0.0 collective-permute-done.13.refs_11_
  35.7 0.0 collective-permute-done.14.refs_12_
  35.8 0.6 %collective-permute-start.15 = (bf16[144,768]{1,0:T(8,128)(2,1)S(1)}, bf16[144,768]{1,0:T(8,128)(2,1)S(1)}, u32[]{:S(2)}, u32[]{:S(2)}) collective-permute-start(bf16[144,768]{1,0:T(8,128)(2,1)S(1)} %collective-permute-done.6.refs_1_.refs_9_), channel_id=1, source_target_pairs={{0,2},{1,3},{2,0},{3,1},{4,6},{5,7},{6,4},{7,5},{8,10},{9,11},{10,... | collective-permute-start | bytes 663560 | tf_op jit(solution)/shard_map/ppermute | solution.py:300
  36.4 2.4 %shard_map.128 = (f32[8,960]{1,0:T(8,128)S(1)}, f32[8,960]{1,0:T(8,128)S(1)}, bf16[768,768]{1,0:T(8,128)(2,1)S(1)}) custom-call(s32[1]{0:T(128)} %bitcast.me_ref.refs_0_, bf16[144,768]{1,0:T(8,128)(2,1)S(1)} %collective-permute-done.1.refs_1_.refs_4_.refs_3_, bf16[144,768]{1,0:T(8,128)(2,1)S(1)} %collective-permute-done.7.refs_2_.refs_5_.refs_4_, ...), custom_call_target="tpu_custom_call" | custom-call | flops 2 | bytes 2 | tf_op jit(solution)/shard_map/pallas_call | solution.py:398
  38.8 0.0 copy-start
  38.8 2.4 %shard_map.129 = (f32[8,960]{1,0:T(8,128)S(1)}, f32[8,960]{1,0:T(8,128)S(1)}) custom-call(bf16[128,768]{1,0:T(8,128)(2,1)S(1)} %collective-permute-done.4.refs_0_, bf16[128,768]{1,0:T(8,128)(2,1)S(1)} %collective-permute-done.8.refs_1_, bf16[128,768]{1,0:T(8,128)(2,1)S(1)} %collective-permute-done.9.refs_2_, ...), custom_call_target="tpu_custom_call" | custom-call | flops 3 | bytes 3 | tf_op jit(solution)/shard_map/pallas_call | solution.py:416
  41.3 1.4 %collective-permute-done.15.refs_2_.refs_10_ = bf16[144,768]{1,0:T(8,128)(2,1)S(1)} collective-permute-done((bf16[144,768]{1,0:T(8,128)(2,1)S(1)}, bf16[144,768]{1,0:T(8,128)(2,1)S(1)}, u32[]{:S(2)}, u32[]{:S(2)}) %collective-permute-start.15) | collective-permute-done | bytes 221216 | tf_op jit(solution)/shard_map/ppermute | solution.py:300
  42.6 0.0 copy-done
  42.6 2.1 %shard_map.130 = (bf16[8,48,128]{2,1,0:T(8,128)(2,1)S(1)}, bf16[8,32,128]{2,1,0:T(8,128)(2,1)S(1)}) custom-call(s32[1]{0:T(128)} %bitcast.me_ref.refs_0_, bf16[144,768]{1,0:T(8,128)(2,1)S(1)} %collective-permute-done.6.refs_1_.refs_9_, bf16[144,768]{1,0:T(8,128)(2,1)S(1)} %collective-permute-done.15.refs_2_.refs_10_, ...), custom_call_target="tpu_custom_call" | custom-call | flops 2 | bytes 2 | tf_op jit(solution)/shard_map/pallas_call | solution.py:432
  44.8 0.1 collective-permute-start.16
  44.9 1.2 %collective-permute-done.16.got_ref = bf16[8,32,128]{2,1,0:T(8,128)(2,1)S(1)} collective-permute-done((bf16[8,32,128]{2,1,0:T(8,128)(2,1)S(1)}, bf16[8,32,128]{2,1,0:T(8,128)(2,1)S(1)}, u32[]{:S(2)}, u32[]{:S(2)}) %collective-permute-start.16) | collective-permute-done | bytes 65568 | tf_op jit(solution)/shard_map/ppermute | solution.py:303
  46.1 9.5 %all_to_all.5.refs_0_ = bf16[8,48,128]{2,1,0:T(8,128)(2,1)S(1)} all-to-all(bf16[8,48,128]{2,1,0:T(8,128)(2,1)S(1)} %shard_map.131), channel_id=1, replica_groups={{0,2,4,6,8,10,12,14},{1,3,5,7,9,11,13,15},{16,18,20,22,24,26,28,30},{17..., dimensions={0} | all-to-all | bytes 196608 | tf_op jit(solution)/shard_map/all_to_all | solution.py:462
  55.6 0.8 %shard_map.132 = (bf16[1,15360]{1,0:T(2,128)(2,1)}, bf16[2,15360]{1,0:T(2,128)(2,1)}) custom-call(bf16[8,48,128]{2,1,0:T(8,128)(2,1)S(1)} %all_to_all.5.refs_0_), custom_call_target="tpu_custom_call" | custom-call | tf_op jit(solution)/shard_map/pallas_call | solution.py:465
  (5 shorter events, 0.1 us)
Async XLA Ops:
  0.6 23.8 %collective-permute-start.5 = (bf16[960,768]{1,0:T(8,128)(2,1)}, bf16[960,768]{1,0:T(8,128)(2,1)S(1)}, u32[]{:S(2)}, u32[]{:S(2)}) collective-permute-start(bf16[960,768]{1,0:T(8,128)(2,1)} %bitcast.7), channel_id=1, source_target_pairs={{0,1},{1,0},{2,3},{3,2},{4,5},{5,4},{6,7},{7,6},{8,9},{9,8},{10,11... | collective-permute-start | bytes 4423688 | tf_op jit(solution)/shard_map/ppermute | solution.py:303
  1.2 16.5 %collective-permute-start.4 = (bf16[128,768]{1,0:T(8,128)(2,1)}, bf16[128,768]{1,0:T(8,128)(2,1)S(1)}, u32[]{:S(2)}, u32[]{:S(2)}) collective-permute-start(bf16[128,768]{1,0:T(8,128)(2,1)} %refs_0_.1), channel_id=1, source_target_pairs={{0,2},{1,3},{2,0},{3,1},{4,6},{5,7},{6,4},{7,5},{8,10},{9,11},{10,... | collective-permute-start | bytes 589832 | tf_op jit(solution)/shard_map/ppermute | solution.py:300
  3.7 14.0 %collective-permute-start.8 = (bf16[128,768]{1,0:T(8,128)(2,1)}, bf16[128,768]{1,0:T(8,128)(2,1)S(1)}, u32[]{:S(2)}, u32[]{:S(2)}) collective-permute-start(bf16[128,768]{1,0:T(8,128)(2,1)} %refs_0_.1), channel_id=1, source_target_pairs={{0,4},{1,5},{2,6},{3,7},{4,0},{5,1},{6,2},{7,3},{8,12},{9,13},{10,... | collective-permute-start | bytes 589832 | tf_op jit(solution)/shard_map/ppermute | solution.py:300
  5.3 10.0 %collective-permute-start = (bf16[48,768]{1,0:T(8,128)(2,1)}, bf16[48,768]{1,0:T(8,128)(2,1)S(1)}, u32[]{:S(2)}, u32[]{:S(2)}) collective-permute-start(bf16[48,768]{1,0:T(8,128)(2,1)} %refs_1_.1), channel_id=1, source_target_pairs={{0,12},{1,13},{2,14},{3,15},{4,8},{5,9},{6,10},{7,11},{8,4},{9,5},... | collective-permute-start | bytes 221192 | tf_op jit(solution)/shard_map/ppermute | solution.py:300
  7.8 7.6 %collective-permute-start.3 = (bf16[48,768]{1,0:T(8,128)(2,1)}, bf16[48,768]{1,0:T(8,128)(2,1)S(1)}, u32[]{:S(2)}, u32[]{:S(2)}) collective-permute-start(bf16[48,768]{1,0:T(8,128)(2,1)} %refs_1_.1), channel_id=1, source_target_pairs={{0,4},{1,5},{2,6},{3,7},{4,0},{5,1},{6,2},{7,3},{8,12},{9,13},{10,... | collective-permute-start | bytes 221192 | tf_op jit(solution)/shard_map/ppermute | solution.py:300
  15.3 9.2 %collective-permute-start.2 = (bf16[64,768]{1,0:T(8,128)(2,1)S(1)}, bf16[64,768]{1,0:T(8,128)(2,1)S(1)}, u32[]{:S(2)}, u32[]{:S(2)}) collective-permute-start(bf16[64,768]{1,0:T(8,128)(2,1)S(1)} %shard_map.123), channel_id=1, source_target_pairs={{0,4},{1,5},{2,6},{3,7},{4,0},{5,1},{6,2},{7,3},{8,12},{9,13},{10,... | collective-permute-start | bytes 294920 | tf_op jit(solution)/shard_map/ppermute | solution.py:300
  15.4 9.7 %collective-permute-start.1 = (bf16[144,768]{1,0:T(8,128)(2,1)S(1)}, bf16[144,768]{1,0:T(8,128)(2,1)S(1)}, u32[]{:S(2)}, u32[]{:S(2)}) collective-permute-start(bf16[144,768]{1,0:T(8,128)(2,1)S(1)} %get-tuple-element.26.refs_3_.refs_6_.refs_5_), channel_id=1, source_target_pairs={{0,12},{1,13},{2,14},{3,15},{4,8},{5,9},{6,10},{7,11},{8,4},{9,5},... | collective-permute-start | bytes 663560 | tf_op jit(solution)/shard_map/ppermute | solution.py:300
  17.7 10.6 %collective-permute-start.9 = (bf16[128,768]{1,0:T(8,128)(2,1)S(1)}, bf16[128,768]{1,0:T(8,128)(2,1)S(1)}, u32[]{:S(2)}, u32[]{:S(2)}) collective-permute-start(bf16[128,768]{1,0:T(8,128)(2,1)S(1)} %collective-permute-done.8.refs_1_), channel_id=1, source_target_pairs={{0,2},{1,3},{2,0},{3,1},{4,6},{5,7},{6,4},{7,5},{8,10},{9,11},{10,... | collective-permute-start | bytes 589832 | tf_op jit(solution)/shard_map/ppermute | solution.py:300
  18.3 11.0 %collective-permute-start.10 = (bf16[112,768]{1,0:T(8,128)(2,1)S(1)}, bf16[112,768]{1,0:T(8,128)(2,1)S(1)}, u32[]{:S(2)}, u32[]{:S(2)}) collective-permute-start(bf16[112,768]{1,0:T(8,128)(2,1)S(1)} %shard_map.124), channel_id=1, source_target_pairs={{0,2},{1,3},{2,0},{3,1},{4,6},{5,7},{6,4},{7,5},{8,10},{9,11},{10,... | collective-permute-start | bytes 516104 | tf_op jit(solution)/shard_map/ppermute | solution.py:300
  24.5 8.5 %collective-permute-start.11 = (bf16[112,768]{1,0:T(8,128)(2,1)S(1)}, bf16[112,768]{1,0:T(8,128)(2,1)S(1)}, u32[]{:S(2)}, u32[]{:S(2)}) collective-permute-start(bf16[112,768]{1,0:T(8,128)(2,1)S(1)} %shard_map.126), channel_id=1, source_target_pairs={{0,2},{1,3},{2,0},{3,1},{4,6},{5,7},{6,4},{7,5},{8,10},{9,11},{10,... | collective-permute-start | bytes 516104 | tf_op jit(solution)/shard_map/ppermute | solution.py:300
  25.1 10.7 %collective-permute-start.7 = (bf16[144,768]{1,0:T(8,128)(2,1)S(1)}, bf16[144,768]{1,0:T(8,128)(2,1)S(1)}, u32[]{:S(2)}, u32[]{:S(2)}) collective-permute-start(bf16[144,768]{1,0:T(8,128)(2,1)S(1)} %collective-permute-done.1.refs_1_.refs_4_.refs_3_), channel_id=1, source_target_pairs={{0,2},{1,3},{2,0},{3,1},{4,6},{5,7},{6,4},{7,5},{8,10},{9,11},{10,... | collective-permute-start | bytes 663560 | tf_op jit(solution)/shard_map/ppermute | solution.py:300
  26.6 9.2 %collective-permute-start.6 = (bf16[144,768]{1,0:T(8,128)(2,1)S(1)}, bf16[144,768]{1,0:T(8,128)(2,1)S(1)}, u32[]{:S(2)}, u32[]{:S(2)}) collective-permute-start(bf16[144,768]{1,0:T(8,128)(2,1)S(1)} %collective-permute-done.1.refs_1_.refs_4_.refs_3_), channel_id=1, source_target_pairs={{0,4},{1,5},{2,6},{3,7},{4,0},{5,1},{6,2},{7,3},{8,12},{9,13},{10,... | collective-permute-start | bytes 663560 | tf_op jit(solution)/shard_map/ppermute | solution.py:300
  33.0 2.7 %collective-permute-start.12 = (bf16[128,768]{1,0:T(8,128)(2,1)S(1)}, bf16[128,768]{1,0:T(8,128)(2,1)S(1)}, u32[]{:S(2)}, u32[]{:S(2)}) collective-permute-start(bf16[128,768]{1,0:T(8,128)(2,1)S(1)} %get-tuple-element.35.refs_7_), channel_id=1, source_target_pairs={{0,1},{1,0},{2,3},{3,2},{4,5},{5,4},{6,7},{7,6},{8,9},{9,8},{10,11... | collective-permute-start | bytes 589832 | tf_op jit(solution)/shard_map/ppermute | solution.py:303
  33.1 2.7 %collective-permute-start.13 = (bf16[128,768]{1,0:T(8,128)(2,1)S(1)}, bf16[128,768]{1,0:T(8,128)(2,1)S(1)}, u32[]{:S(2)}, u32[]{:S(2)}) collective-permute-start(bf16[128,768]{1,0:T(8,128)(2,1)S(1)} %get-tuple-element.36.refs_8_), channel_id=1, source_target_pairs={{0,1},{1,0},{2,3},{3,2},{4,5},{5,4},{6,7},{7,6},{8,9},{9,8},{10,11... | collective-permute-start | bytes 589832 | tf_op jit(solution)/shard_map/ppermute | solution.py:303
  33.6 2.2 %collective-permute-start.14 = (bf16[128,768]{1,0:T(8,128)(2,1)S(1)}, bf16[128,768]{1,0:T(8,128)(2,1)S(1)}, u32[]{:S(2)}, u32[]{:S(2)}) collective-permute-start(bf16[128,768]{1,0:T(8,128)(2,1)S(1)} %get-tuple-element.37.refs_9_), channel_id=1, source_target_pairs={{0,1},{1,0},{2,3},{3,2},{4,5},{5,4},{6,7},{7,6},{8,9},{9,8},{10,11... | collective-permute-start | bytes 589832 | tf_op jit(solution)/shard_map/ppermute | solution.py:303
  35.8 6.9 %collective-permute-start.15 = (bf16[144,768]{1,0:T(8,128)(2,1)S(1)}, bf16[144,768]{1,0:T(8,128)(2,1)S(1)}, u32[]{:S(2)}, u32[]{:S(2)}) collective-permute-start(bf16[144,768]{1,0:T(8,128)(2,1)S(1)} %collective-permute-done.6.refs_1_.refs_9_), channel_id=1, source_target_pairs={{0,2},{1,3},{2,0},{3,1},{4,6},{5,7},{6,4},{7,5},{8,10},{9,11},{10,... | collective-permute-start | bytes 663560 | tf_op jit(solution)/shard_map/ppermute | solution.py:300
  38.8 3.8 %copy-start = (f32[15360]{0:T(1024)S(1)}, f32[15360]{0:T(1024)}, u32[]{:S(2)}) copy-start(f32[15360]{0:T(1024)} %param.18) | copy-start | bytes 184324
  44.8 1.3 %collective-permute-start.16 = (bf16[8,32,128]{2,1,0:T(8,128)(2,1)S(1)}, bf16[8,32,128]{2,1,0:T(8,128)(2,1)S(1)}, u32[]{:S(2)}, u32[]{:S(2)}) collective-permute-start(bf16[8,32,128]{2,1,0:T(8,128)(2,1)S(1)} %get-tuple-element.47), channel_id=1, source_target_pairs={{0,1},{1,0},{2,3},{3,2},{4,5},{5,4},{6,7},{7,6},{8,9},{9,8},{10,11... | collective-permute-start | bytes 196616 | tf_op jit(solution)/shard_map/ppermute | solution.py:303

commit v24 on v22

--- a/solution.py
+++ b/solution.py
@@ -392,7 +392,7 @@
     groups = [[6, 7, 0], [1, 2, 3], [4, 5]]
     masks = [mask for group in groups for mask in group]
     docs[0] = load
-    docs[5] = cross(after(docs[4], docs[7], *other_packed), 1)
+    docs[5] = cross(after(docs[4], *other_packed), 1)
     tables = docs | {1: near_pile, 2: block_4, 3: far_pile}
     best_shape = shape((8, half), jnp.float32)
     *best, weight = pl.pallas_call(
@@ -401,7 +401,7 @@
         in_specs=[smem] + [vmem] * (2 * len(groups[0]) + 3 + 2 * len(packed)),
         out_specs=[vmem] * 3,
         compiler_params=limit,
-        cost_estimate=cost(2),
+        cost_estimate=cost(3 * 10**9),
     )(
         where,
         *[docs[mask] for mask in groups[0]],

time: 52.8 us -> 53.5 us (1.013)
  waiting for transfers between devices: 13.2 us -> 14.8 us
    ppermute x5, waiting for transfers between devices: 1.25 us -> 2.65 us  [swap(): return lax.ppermute(value, 'doc', [(i, i ^ 1) for i in range(devices)])]
  transfers between devices with their start and end apart: 17 -> 17, of which waited for: 8 -> 10; matrix products, arithmetic and copies ran while one was open for 0% -> 0% of each run, Pallas kernels for 15% -> 15%
where the time goes in v24:
time: 53.5 us; the launch traced here: 53.3 us
  starting transfers between devices  16.6 us (31%)
  waiting for transfers between devices  14.8 us (28%)
  Pallas kernels  11 us (21%)
  blocking collectives  9.51 us (18%)
  between operations  1.4 us (3%)
    ppermute x12, starting transfers between devices, cross(): lax.ppermute(value, 'doc', [(i, i ^ 2 * mask) for i in range(devices)])  15.3 us
    ppermute x12, waiting for transfers between devices, cross(): lax.ppermute(value, 'doc', [(i, i ^ 2 * mask) for i in range(devices)])  12.2 us
    all_to_all x1, blocking collectives, move_tokens(): lax.all_to_all(merged, 'doc', split_axis=0, concat_axis=0, axis_index_gro...  9.51 us
    ppermute x5, waiting for transfers between devices, swap(): return lax.ppermute(value, 'doc', [(i, i ^ 1) for i in range(devices)])  2.65 us
    pallas_call x1, Pallas kernels, move_tokens(): pl.pallas_call(lambda *refs: first_kernel(seq, rows, block_masks, len(gro...  2.45 us
    pallas_call x1, Pallas kernels, move_tokens(): pl.pallas_call(lambda *refs, count=len(group): next_kernel(seq, count, *r...  2.42 us
    pallas_call x1, Pallas kernels, move_tokens(): pl.pallas_call(lambda *refs: last_kernel(seq, groups, *refs), out_shape=[...  2.13 us
    pallas_call x1, Pallas kernels, move_tokens(): pl.pallas_call(start_kernel, out_shape=[shape((seq + SLOT_ROWS, width), j...  1.71 us
  transfers between devices with their start and end apart: 17, of which 10 were waited for; matrix products, arithmetic and copies ran while one was open for 0% of the time, Pallas kernels for 15%

profile of v24, /device:TPU:0, one launch (start us, length us, event | category | flops | bytes accessed | tf_op | source)
XLA Modules:
  0.0 53.3 jit_solution(4437354410692093114)
XLA Ops:
  0.6 0.5 collective-permute-start.6
  1.2 2.6 %collective-permute-start.4 = (bf16[128,768]{1,0:T(8,128)(2,1)}, bf16[128,768]{1,0:T(8,128)(2,1)S(1)}, u32[]{:S(2)}, u32[]{:S(2)}) collective-permute-start(bf16[128,768]{1,0:T(8,128)(2,1)} %refs_0_.1), channel_id=1, source_target_pairs={{0,2},{1,3},{2,0},{3,1},{4,6},{5,7},{6,4},{7,5},{8,10},{9,11},{10,... | collective-permute-start | bytes 589832 | tf_op jit(solution)/shard_map/ppermute | solution.py:300
  3.7 3.6 %collective-permute-start = (bf16[48,768]{1,0:T(8,128)(2,1)}, bf16[48,768]{1,0:T(8,128)(2,1)S(1)}, u32[]{:S(2)}, u32[]{:S(2)}) collective-permute-start(bf16[48,768]{1,0:T(8,128)(2,1)} %refs_1_.1), channel_id=1, source_target_pairs={{0,12},{1,13},{2,14},{3,15},{4,8},{5,9},{6,10},{7,11},{8,4},{9,5},... | collective-permute-start | bytes 221192 | tf_op jit(solution)/shard_map/ppermute | solution.py:300
  7.3 0.0 collective-permute-start.3
  7.3 2.0 %collective-permute-start.8 = (bf16[128,768]{1,0:T(8,128)(2,1)}, bf16[128,768]{1,0:T(8,128)(2,1)S(1)}, u32[]{:S(2)}, u32[]{:S(2)}) collective-permute-start(bf16[128,768]{1,0:T(8,128)(2,1)} %refs_0_.1), channel_id=1, source_target_pairs={{0,4},{1,5},{2,6},{3,7},{4,0},{5,1},{6,2},{7,3},{8,12},{9,13},{10,... | collective-permute-start | bytes 589832 | tf_op jit(solution)/shard_map/ppermute | solution.py:300
  10.0 1.7 %shard_map.122 = (bf16[144,768]{1,0:T(8,128)(2,1)S(1)}, bf16[48,768]{1,0:T(8,128)(2,1)S(1)}, bf16[16,768]{1,0:T(8,128)(2,1)S(1)}, f32[8,768]{1,0:T(8,128)S(1)}) custom-call(s32[1]{0:T(128)} %bitcast.me_ref.refs_0_, s32[1,1,32]{2,1,0:T(1,128)} %tiles_ref.1, s32[1,1,32]{2,1,0:T(1,128)} %bitcast.9, s32[1,1,32]{2,1,0:T(1,128)} %slots_ref.1, ...), custom_call_target="tpu_custom_call" | custom-call | tf_op jit(solution)/shard_map/pallas_call | solution.py:340
  11.7 0.0 collective-permute-done.refs_0_.refs_2_
  11.7 1.0 %collective-permute-done.3.refs_1_ = bf16[48,768]{1,0:T(8,128)(2,1)S(1)} collective-permute-done((bf16[48,768]{1,0:T(8,128)(2,1)}, bf16[48,768]{1,0:T(8,128)(2,1)S(1)}, u32[]{:S(2)}, u32[]{:S(2)}) %collective-permute-start.3) | collective-permute-done | bytes 73760 | tf_op jit(solution)/shard_map/ppermute | solution.py:300
  12.7 0.0 collective-permute-done.4.refs_0_
  12.7 0.6 %collective-permute-start.5 = (bf16[112,768]{1,0:T(8,128)(2,1)S(1)}, bf16[112,768]{1,0:T(8,128)(2,1)S(1)}, u32[]{:S(2)}, u32[]{:S(2)}) collective-permute-start(bf16[112,768]{1,0:T(8,128)(2,1)S(1)} %shard_map.124), channel_id=1, source_target_pairs={{0,2},{1,3},{2,0},{3,1},{4,6},{5,7},{6,4},{7,5},{8,10},{9,11},{10,... | collective-permute-start | bytes 516104 | tf_op jit(solution)/shard_map/ppermute | solution.py:300
  13.3 1.6 %collective-permute-start.2 = (bf16[64,768]{1,0:T(8,128)(2,1)S(1)}, bf16[64,768]{1,0:T(8,128)(2,1)S(1)}, u32[]{:S(2)}, u32[]{:S(2)}) collective-permute-start(bf16[64,768]{1,0:T(8,128)(2,1)S(1)} %shard_map.123), channel_id=1, source_target_pairs={{0,4},{1,5},{2,6},{3,7},{4,0},{5,1},{6,2},{7,3},{8,12},{9,13},{10,... | collective-permute-start | bytes 294920 | tf_op jit(solution)/shard_map/ppermute | solution.py:300
  14.9 0.5 collective-permute-start.1
  15.4 1.5 %collective-permute-done.8.refs_1_ = bf16[128,768]{1,0:T(8,128)(2,1)S(1)} collective-permute-done((bf16[128,768]{1,0:T(8,128)(2,1)}, bf16[128,768]{1,0:T(8,128)(2,1)S(1)}, u32[]{:S(2)}, u32[]{:S(2)}) %collective-permute-start.8) | collective-permute-done | bytes 196640 | tf_op jit(solution)/shard_map/ppermute | solution.py:300
  16.9 0.4 collective-permute-start.9
  17.3 1.4 %shard_map.125.refs_14_.refs_8_.refs_13_ = bf16[960,768]{1,0:T(8,128)(2,1)S(1)} custom-call(bf16[16,768]{1,0:T(8,128)(2,1)S(1)} %get-tuple-element.27.refs_1_.refs_2_.refs_0_, bf16[960,768]{1,0:T(8,128)(2,1)} %bitcast.8), custom_call_target="tpu_custom_call" | custom-call | tf_op jit(solution)/shard_map/pallas_call | solution.py:374
  18.7 4.4 %collective-permute-done.2.refs_1_.refs_3_.refs_4_.refs_7_ = bf16[64,768]{1,0:T(8,128)(2,1)S(1)} collective-permute-done((bf16[64,768]{1,0:T(8,128)(2,1)S(1)}, bf16[64,768]{1,0:T(8,128)(2,1)S(1)}, u32[]{:S(2)}, u32[]{:S(2)}) %collective-permute-start.2) | collective-permute-done | bytes 98336 | tf_op jit(solution)/shard_map/ppermute | solution.py:300
  23.1 0.0 collective-permute-done.5.refs_4_.refs_3_.refs_6_
  23.1 0.0 collective-permute-done.6.refs_15_.refs_9_.refs_14_
  23.1 0.1 collective-permute-start.10
  23.2 0.0 collective-permute-done.1.refs_1_.refs_4_.refs_3_
  23.2 2.4 %collective-permute-start.7 = (bf16[144,768]{1,0:T(8,128)(2,1)S(1)}, bf16[144,768]{1,0:T(8,128)(2,1)S(1)}, u32[]{:S(2)}, u32[]{:S(2)}) collective-permute-start(bf16[144,768]{1,0:T(8,128)(2,1)S(1)} %collective-permute-done.1.refs_1_.refs_4_.refs_3_), channel_id=1, source_target_pairs={{0,4},{1,5},{2,6},{3,7},{4,0},{5,1},{6,2},{7,3},{8,12},{9,13},{10,... | collective-permute-start | bytes 663560 | tf_op jit(solution)/shard_map/ppermute | solution.py:300
  25.5 1.6 %collective-permute-start.15 = (bf16[144,768]{1,0:T(8,128)(2,1)S(1)}, bf16[144,768]{1,0:T(8,128)(2,1)S(1)}, u32[]{:S(2)}, u32[]{:S(2)}) collective-permute-start(bf16[144,768]{1,0:T(8,128)(2,1)S(1)} %collective-permute-done.1.refs_1_.refs_4_.refs_3_), channel_id=1, source_target_pairs={{0,2},{1,3},{2,0},{3,1},{4,6},{5,7},{6,4},{7,5},{8,10},{9,11},{10,... | collective-permute-start | bytes 663560 | tf_op jit(solution)/shard_map/ppermute | solution.py:300
  27.1 0.0 collective-permute-done.9.refs_2_
  27.1 2.7 %collective-permute-done.10.refs_5_.refs_8_ = bf16[112,768]{1,0:T(8,128)(2,1)S(1)} collective-permute-done((bf16[112,768]{1,0:T(8,128)(2,1)S(1)}, bf16[112,768]{1,0:T(8,128)(2,1)S(1)}, u32[]{:S(2)}, u32[]{:S(2)}) %collective-permute-start.10) | collective-permute-done | bytes 172064 | tf_op jit(solution)/shard_map/ppermute | solution.py:300
  29.9 0.1 collective-permute-start.11
  29.9 0.5 collective-permute-start.12
  30.4 0.1 collective-permute-start.13
  30.5 0.0 collective-permute-done.7.refs_1_.refs_9_
  30.5 0.8 %collective-permute-done.11.refs_10_ = bf16[128,768]{1,0:T(8,128)(2,1)S(1)} collective-permute-done((bf16[128,768]{1,0:T(8,128)(2,1)S(1)}, bf16[128,768]{1,0:T(8,128)(2,1)S(1)}, u32[]{:S(2)}, u32[]{:S(2)}) %collective-permute-start.11) | collective-permute-done | bytes 196640 | tf_op jit(solution)/shard_map/ppermute | solution.py:303
  31.4 0.3 collective-permute-done.12.refs_11_
  31.6 0.3 collective-permute-done.13.refs_12_
  31.9 0.0 collective-permute-start.14
  31.9 0.2 collective-permute-done.15.refs_2_.refs_5_.refs_4_
  32.2 2.5 %shard_map.128 = (f32[8,960]{1,0:T(8,128)S(1)}, f32[8,960]{1,0:T(8,128)S(1)}, bf16[768,768]{1,0:T(8,128)(2,1)S(1)}) custom-call(s32[1]{0:T(128)} %bitcast.me_ref.refs_0_, bf16[144,768]{1,0:T(8,128)(2,1)S(1)} %collective-permute-done.1.refs_1_.refs_4_.refs_3_, bf16[144,768]{1,0:T(8,128)(2,1)S(1)} %collective-permute-done.15.refs_2_.refs_5_.refs_4_, ...), custom_call_target="tpu_custom_call" | custom-call | flops 3000000000 | bytes 3000000000 | tf_op jit(solution)/shard_map/pallas_call | solution.py:398
  34.6 0.0 copy-start
  34.7 2.4 %shard_map.129 = (f32[8,960]{1,0:T(8,128)S(1)}, f32[8,960]{1,0:T(8,128)S(1)}) custom-call(bf16[128,768]{1,0:T(8,128)(2,1)S(1)} %collective-permute-done.4.refs_0_, bf16[128,768]{1,0:T(8,128)(2,1)S(1)} %collective-permute-done.8.refs_1_, bf16[128,768]{1,0:T(8,128)(2,1)S(1)} %collective-permute-done.9.refs_2_, ...), custom_call_target="tpu_custom_call" | custom-call | flops 3 | bytes 3 | tf_op jit(solution)/shard_map/pallas_call | solution.py:416
  37.1 2.4 %collective-permute-done.14.refs_2_.refs_10_ = bf16[144,768]{1,0:T(8,128)(2,1)S(1)} collective-permute-done((bf16[144,768]{1,0:T(8,128)(2,1)S(1)}, bf16[144,768]{1,0:T(8,128)(2,1)S(1)}, u32[]{:S(2)}, u32[]{:S(2)}) %collective-permute-start.14) | collective-permute-done | bytes 221216 | tf_op jit(solution)/shard_map/ppermute | solution.py:300
  39.5 0.0 copy-done
  39.5 2.1 %shard_map.130 = (bf16[8,48,128]{2,1,0:T(8,128)(2,1)S(1)}, bf16[8,32,128]{2,1,0:T(8,128)(2,1)S(1)}) custom-call(s32[1]{0:T(128)} %bitcast.me_ref.refs_0_, bf16[144,768]{1,0:T(8,128)(2,1)S(1)} %collective-permute-done.7.refs_1_.refs_9_, bf16[144,768]{1,0:T(8,128)(2,1)S(1)} %collective-permute-done.14.refs_2_.refs_10_, ...), custom_call_target="tpu_custom_call" | custom-call | flops 2 | bytes 2 | tf_op jit(solution)/shard_map/pallas_call | solution.py:432
  41.6 0.1 collective-permute-start.16
  41.7 1.2 %collective-permute-done.16.got_ref = bf16[8,32,128]{2,1,0:T(8,128)(2,1)S(1)} collective-permute-done((bf16[8,32,128]{2,1,0:T(8,128)(2,1)S(1)}, bf16[8,32,128]{2,1,0:T(8,128)(2,1)S(1)}, u32[]{:S(2)}, u32[]{:S(2)}) %collective-permute-start.16) | collective-permute-done | bytes 65568 | tf_op jit(solution)/shard_map/ppermute | solution.py:303
  43.0 9.5 %all_to_all.5.refs_0_ = bf16[8,48,128]{2,1,0:T(8,128)(2,1)S(1)} all-to-all(bf16[8,48,128]{2,1,0:T(8,128)(2,1)S(1)} %shard_map.131), channel_id=1, replica_groups={{0,2,4,6,8,10,12,14},{1,3,5,7,9,11,13,15},{16,18,20,22,24,26,28,30},{17..., dimensions={0} | all-to-all | bytes 196608 | tf_op jit(solution)/shard_map/all_to_all | solution.py:462
  52.5 0.8 %shard_map.132 = (bf16[1,15360]{1,0:T(2,128)(2,1)}, bf16[2,15360]{1,0:T(2,128)(2,1)}) custom-call(bf16[8,48,128]{2,1,0:T(8,128)(2,1)S(1)} %all_to_all.5.refs_0_), custom_call_target="tpu_custom_call" | custom-call | tf_op jit(solution)/shard_map/pallas_call | solution.py:465
  (5 shorter events, 0.1 us)
Async XLA Ops:
  0.6 22.4 %collective-permute-start.6 = (bf16[960,768]{1,0:T(8,128)(2,1)}, bf16[960,768]{1,0:T(8,128)(2,1)S(1)}, u32[]{:S(2)}, u32[]{:S(2)}) collective-permute-start(bf16[960,768]{1,0:T(8,128)(2,1)} %bitcast.7), channel_id=1, source_target_pairs={{0,1},{1,0},{2,3},{3,2},{4,5},{5,4},{6,7},{7,6},{8,9},{9,8},{10,11... | collective-permute-start | bytes 4423688 | tf_op jit(solution)/shard_map/ppermute | solution.py:303
  1.2 11.5 %collective-permute-start.4 = (bf16[128,768]{1,0:T(8,128)(2,1)}, bf16[128,768]{1,0:T(8,128)(2,1)S(1)}, u32[]{:S(2)}, u32[]{:S(2)}) collective-permute-start(bf16[128,768]{1,0:T(8,128)(2,1)} %refs_0_.1), channel_id=1, source_target_pairs={{0,2},{1,3},{2,0},{3,1},{4,6},{5,7},{6,4},{7,5},{8,10},{9,11},{10,... | collective-permute-start | bytes 589832 | tf_op jit(solution)/shard_map/ppermute | solution.py:300
  3.7 8.0 %collective-permute-start = (bf16[48,768]{1,0:T(8,128)(2,1)}, bf16[48,768]{1,0:T(8,128)(2,1)S(1)}, u32[]{:S(2)}, u32[]{:S(2)}) collective-permute-start(bf16[48,768]{1,0:T(8,128)(2,1)} %refs_1_.1), channel_id=1, source_target_pairs={{0,12},{1,13},{2,14},{3,15},{4,8},{5,9},{6,10},{7,11},{8,4},{9,5},... | collective-permute-start | bytes 221192 | tf_op jit(solution)/shard_map/ppermute | solution.py:300
  7.3 5.4 %collective-permute-start.3 = (bf16[48,768]{1,0:T(8,128)(2,1)}, bf16[48,768]{1,0:T(8,128)(2,1)S(1)}, u32[]{:S(2)}, u32[]{:S(2)}) collective-permute-start(bf16[48,768]{1,0:T(8,128)(2,1)} %refs_1_.1), channel_id=1, source_target_pairs={{0,4},{1,5},{2,6},{3,7},{4,0},{5,1},{6,2},{7,3},{8,12},{9,13},{10,... | collective-permute-start | bytes 221192 | tf_op jit(solution)/shard_map/ppermute | solution.py:300
  7.3 9.6 %collective-permute-start.8 = (bf16[128,768]{1,0:T(8,128)(2,1)}, bf16[128,768]{1,0:T(8,128)(2,1)S(1)}, u32[]{:S(2)}, u32[]{:S(2)}) collective-permute-start(bf16[128,768]{1,0:T(8,128)(2,1)} %refs_0_.1), channel_id=1, source_target_pairs={{0,4},{1,5},{2,6},{3,7},{4,0},{5,1},{6,2},{7,3},{8,12},{9,13},{10,... | collective-permute-start | bytes 589832 | tf_op jit(solution)/shard_map/ppermute | solution.py:300
  12.7 10.4 %collective-permute-start.5 = (bf16[112,768]{1,0:T(8,128)(2,1)S(1)}, bf16[112,768]{1,0:T(8,128)(2,1)S(1)}, u32[]{:S(2)}, u32[]{:S(2)}) collective-permute-start(bf16[112,768]{1,0:T(8,128)(2,1)S(1)} %shard_map.124), channel_id=1, source_target_pairs={{0,2},{1,3},{2,0},{3,1},{4,6},{5,7},{6,4},{7,5},{8,10},{9,11},{10,... | collective-permute-start | bytes 516104 | tf_op jit(solution)/shard_map/ppermute | solution.py:300
  13.3 9.7 %collective-permute-start.2 = (bf16[64,768]{1,0:T(8,128)(2,1)S(1)}, bf16[64,768]{1,0:T(8,128)(2,1)S(1)}, u32[]{:S(2)}, u32[]{:S(2)}) collective-permute-start(bf16[64,768]{1,0:T(8,128)(2,1)S(1)} %shard_map.123), channel_id=1, source_target_pairs={{0,4},{1,5},{2,6},{3,7},{4,0},{5,1},{6,2},{7,3},{8,12},{9,13},{10,... | collective-permute-start | bytes 294920 | tf_op jit(solution)/shard_map/ppermute | solution.py:300
  14.9 8.3 %collective-permute-start.1 = (bf16[144,768]{1,0:T(8,128)(2,1)S(1)}, bf16[144,768]{1,0:T(8,128)(2,1)S(1)}, u32[]{:S(2)}, u32[]{:S(2)}) collective-permute-start(bf16[144,768]{1,0:T(8,128)(2,1)S(1)} %get-tuple-element.26.refs_3_.refs_6_.refs_5_), channel_id=1, source_target_pairs={{0,12},{1,13},{2,14},{3,15},{4,8},{5,9},{6,10},{7,11},{8,4},{9,5},... | collective-permute-start | bytes 663560 | tf_op jit(solution)/shard_map/ppermute | solution.py:300
  16.9 10.2 %collective-permute-start.9 = (bf16[128,768]{1,0:T(8,128)(2,1)S(1)}, bf16[128,768]{1,0:T(8,128)(2,1)S(1)}, u32[]{:S(2)}, u32[]{:S(2)}) collective-permute-start(bf16[128,768]{1,0:T(8,128)(2,1)S(1)} %collective-permute-done.8.refs_1_), channel_id=1, source_target_pairs={{0,2},{1,3},{2,0},{3,1},{4,6},{5,7},{6,4},{7,5},{8,10},{9,11},{10,... | collective-permute-start | bytes 589832 | tf_op jit(solution)/shard_map/ppermute | solution.py:300
  23.1 6.7 %collective-permute-start.10 = (bf16[112,768]{1,0:T(8,128)(2,1)S(1)}, bf16[112,768]{1,0:T(8,128)(2,1)S(1)}, u32[]{:S(2)}, u32[]{:S(2)}) collective-permute-start(bf16[112,768]{1,0:T(8,128)(2,1)S(1)} %shard_map.126), channel_id=1, source_target_pairs={{0,2},{1,3},{2,0},{3,1},{4,6},{5,7},{6,4},{7,5},{8,10},{9,11},{10,... | collective-permute-start | bytes 516104 | tf_op jit(solution)/shard_map/ppermute | solution.py:300
  23.2 7.3 %collective-permute-start.7 = (bf16[144,768]{1,0:T(8,128)(2,1)S(1)}, bf16[144,768]{1,0:T(8,128)(2,1)S(1)}, u32[]{:S(2)}, u32[]{:S(2)}) collective-permute-start(bf16[144,768]{1,0:T(8,128)(2,1)S(1)} %collective-permute-done.1.refs_1_.refs_4_.refs_3_), channel_id=1, source_target_pairs={{0,4},{1,5},{2,6},{3,7},{4,0},{5,1},{6,2},{7,3},{8,12},{9,13},{10,... | collective-permute-start | bytes 663560 | tf_op jit(solution)/shard_map/ppermute | solution.py:300
  25.5 6.7 %collective-permute-start.15 = (bf16[144,768]{1,0:T(8,128)(2,1)S(1)}, bf16[144,768]{1,0:T(8,128)(2,1)S(1)}, u32[]{:S(2)}, u32[]{:S(2)}) collective-permute-start(bf16[144,768]{1,0:T(8,128)(2,1)S(1)} %collective-permute-done.1.refs_1_.refs_4_.refs_3_), channel_id=1, source_target_pairs={{0,2},{1,3},{2,0},{3,1},{4,6},{5,7},{6,4},{7,5},{8,10},{9,11},{10,... | collective-permute-start | bytes 663560 | tf_op jit(solution)/shard_map/ppermute | solution.py:300
  29.9 1.5 %collective-permute-start.11 = (bf16[128,768]{1,0:T(8,128)(2,1)S(1)}, bf16[128,768]{1,0:T(8,128)(2,1)S(1)}, u32[]{:S(2)}, u32[]{:S(2)}) collective-permute-start(bf16[128,768]{1,0:T(8,128)(2,1)S(1)} %get-tuple-element.35.refs_7_), channel_id=1, source_target_pairs={{0,1},{1,0},{2,3},{3,2},{4,5},{5,4},{6,7},{7,6},{8,9},{9,8},{10,11... | collective-permute-start | bytes 589832 | tf_op jit(solution)/shard_map/ppermute | solution.py:303
  29.9 1.7 %collective-permute-start.12 = (bf16[128,768]{1,0:T(8,128)(2,1)S(1)}, bf16[128,768]{1,0:T(8,128)(2,1)S(1)}, u32[]{:S(2)}, u32[]{:S(2)}) collective-permute-start(bf16[128,768]{1,0:T(8,128)(2,1)S(1)} %get-tuple-element.36.refs_8_), channel_id=1, source_target_pairs={{0,1},{1,0},{2,3},{3,2},{4,5},{5,4},{6,7},{7,6},{8,9},{9,8},{10,11... | collective-permute-start | bytes 589832 | tf_op jit(solution)/shard_map/ppermute | solution.py:303
  30.4 1.5 %collective-permute-start.13 = (bf16[128,768]{1,0:T(8,128)(2,1)S(1)}, bf16[128,768]{1,0:T(8,128)(2,1)S(1)}, u32[]{:S(2)}, u32[]{:S(2)}) collective-permute-start(bf16[128,768]{1,0:T(8,128)(2,1)S(1)} %get-tuple-element.37.refs_9_), channel_id=1, source_target_pairs={{0,1},{1,0},{2,3},{3,2},{4,5},{5,4},{6,7},{7,6},{8,9},{9,8},{10,11... | collective-permute-start | bytes 589832 | tf_op jit(solution)/shard_map/ppermute | solution.py:303
  31.9 7.6 %collective-permute-start.14 = (bf16[144,768]{1,0:T(8,128)(2,1)S(1)}, bf16[144,768]{1,0:T(8,128)(2,1)S(1)}, u32[]{:S(2)}, u32[]{:S(2)}) collective-permute-start(bf16[144,768]{1,0:T(8,128)(2,1)S(1)} %collective-permute-done.7.refs_1_.refs_9_), channel_id=1, source_target_pairs={{0,2},{1,3},{2,0},{3,1},{4,6},{5,7},{6,4},{7,5},{8,10},{9,11},{10,... | collective-permute-start | bytes 663560 | tf_op jit(solution)/shard_map/ppermute | solution.py:300
  34.6 4.9 %copy-start = (f32[15360]{0:T(1024)S(1)}, f32[15360]{0:T(1024)}, u32[]{:S(2)}) copy-start(f32[15360]{0:T(1024)} %param.18) | copy-start | bytes 184324
  41.6 1.3 %collective-permute-start.16 = (bf16[8,32,128]{2,1,0:T(8,128)(2,1)S(1)}, bf16[8,32,128]{2,1,0:T(8,128)(2,1)S(1)}, u32[]{:S(2)}, u32[]{:S(2)}) collective-permute-start(bf16[8,32,128]{2,1,0:T(8,128)(2,1)S(1)} %get-tuple-element.47), channel_id=1, source_target_pairs={{0,1},{1,0},{2,3},{3,2},{4,5},{5,4},{6,7},{7,6},{8,9},{9,8},{10,11... | collective-permute-start | bytes 196616 | tf_op jit(solution)/shard_map/ppermute | solution.py:303

commit v25 on v22

--- a/solution.py
+++ b/solution.py
@@ -389,7 +389,7 @@
     other_packed = [swap(part) for part in packed]
     block_masks = [0, 2, 6, 4, 1, 3, 7, 5]
 
-    groups = [[6, 7, 0], [1, 2, 3], [4, 5]]
+    groups = [[6, 7, 0, 1, 2, 3, 4], [5]]
     masks = [mask for group in groups for mask in group]
     docs[0] = load
     docs[5] = cross(after(docs[4], docs[7], *other_packed), 1)

time: 52.8 us -> 53 us (level)
  waiting for transfers between devices: 13.2 us -> 8.75 us
  starting transfers between devices: 17 us -> 20.3 us
  blocking collectives: 10 us -> 11.3 us
    ppermute x12, waiting for transfers between devices: 12 us -> 7.5 us  [cross(): lax.ppermute(value, 'doc', [(i, i ^ 2 * mask) for i in range(devices)])]
    ppermute x12, starting transfers between devices: 15.7 us -> 19 us  [cross(): lax.ppermute(value, 'doc', [(i, i ^ 2 * mask) for i in range(devices)])]
    pallas_call x1, Pallas kernels: 2.45 us -> 5.08 us  [move_tokens(): pl.pallas_call(lambda *refs: first_kernel(seq, rows, block_masks, len(gro...]
    pallas_call x1 -> x0, Pallas kernels: 2.42 us -> none  [move_tokens(): pl.pallas_call(lambda *refs, count=len(group): next_kernel(seq, count, *r...]
    all_to_all x1, blocking collectives: 10 us -> 11.3 us  [move_tokens(): lax.all_to_all(merged, 'doc', split_axis=0, concat_axis=0, axis_index_gro...]
  transfers between devices with their start and end apart: 17 -> 17, of which waited for: 8 -> 8; matrix products, arithmetic and copies ran while one was open for 0% -> 0% of each run, Pallas kernels for 15% -> 16%
where the time goes in v25:
time: 53 us; the launch traced here: 52.8 us
  starting transfers between devices  20.3 us (38%)
  blocking collectives  11.3 us (21%)
  Pallas kernels  11 us (21%)
  waiting for transfers between devices  8.75 us (17%)
  between operations  1.39 us (3%)
    ppermute x12, starting transfers between devices, cross(): lax.ppermute(value, 'doc', [(i, i ^ 2 * mask) for i in range(devices)])  19 us
    all_to_all x1, blocking collectives, move_tokens(): lax.all_to_all(merged, 'doc', split_axis=0, concat_axis=0, axis_index_gro...  11.3 us
    ppermute x12, waiting for transfers between devices, cross(): lax.ppermute(value, 'doc', [(i, i ^ 2 * mask) for i in range(devices)])  7.5 us
    pallas_call x1, Pallas kernels, move_tokens(): pl.pallas_call(lambda *refs: first_kernel(seq, rows, block_masks, len(gro...  5.08 us
    pallas_call x1, Pallas kernels, move_tokens(): pl.pallas_call(lambda *refs: last_kernel(seq, groups, *refs), out_shape=[...  2 us
    pallas_call x1, Pallas kernels, move_tokens(): pl.pallas_call(start_kernel, out_shape=[shape((seq + SLOT_ROWS, width), j...  1.71 us
    pallas_call x1, Pallas kernels, move_tokens(): pl.pallas_call(lambda *refs: fetch_kernel(1, *refs), out_shape=[shape(val...  1.38 us
    ppermute x5, waiting for transfers between devices, swap(): return lax.ppermute(value, 'doc', [(i, i ^ 1) for i in range(devices)])  1.25 us
  transfers between devices with their start and end apart: 17, of which 8 were waited for; matrix products, arithmetic and copies ran while one was open for 0% of the time, Pallas kernels for 16%

profile of v25, /device:TPU:0, one launch (start us, length us, event | category | flops | bytes accessed | tf_op | source)
XLA Modules:
  0.0 52.8 jit_solution(5950523175528429292)
XLA Ops:
  0.6 0.5 collective-permute-start.6
  1.2 2.6 %collective-permute-start.4 = (bf16[128,768]{1,0:T(8,128)(2,1)}, bf16[128,768]{1,0:T(8,128)(2,1)S(1)}, u32[]{:S(2)}, u32[]{:S(2)}) collective-permute-start(bf16[128,768]{1,0:T(8,128)(2,1)} %refs_0_.1), channel_id=1, source_target_pairs={{0,2},{1,3},{2,0},{3,1},{4,6},{5,7},{6,4},{7,5},{8,10},{9,11},{10,... | collective-permute-start | bytes 589832 | tf_op jit(solution)/shard_map/ppermute | solution.py:300
  3.7 1.6 %collective-permute-start.3 = (bf16[48,768]{1,0:T(8,128)(2,1)}, bf16[48,768]{1,0:T(8,128)(2,1)S(1)}, u32[]{:S(2)}, u32[]{:S(2)}) collective-permute-start(bf16[48,768]{1,0:T(8,128)(2,1)} %refs_1_.1), channel_id=1, source_target_pairs={{0,4},{1,5},{2,6},{3,7},{4,0},{5,1},{6,2},{7,3},{8,12},{9,13},{10,... | collective-permute-start | bytes 221192 | tf_op jit(solution)/shard_map/ppermute | solution.py:300
  5.3 2.5 %collective-permute-start = (bf16[48,768]{1,0:T(8,128)(2,1)}, bf16[48,768]{1,0:T(8,128)(2,1)S(1)}, u32[]{:S(2)}, u32[]{:S(2)}) collective-permute-start(bf16[48,768]{1,0:T(8,128)(2,1)} %refs_1_.1), channel_id=1, source_target_pairs={{0,12},{1,13},{2,14},{3,15},{4,8},{5,9},{6,10},{7,11},{8,4},{9,5},... | collective-permute-start | bytes 221192 | tf_op jit(solution)/shard_map/ppermute | solution.py:300
  7.8 0.7 %collective-permute-start.9 = (bf16[128,768]{1,0:T(8,128)(2,1)}, bf16[128,768]{1,0:T(8,128)(2,1)S(1)}, u32[]{:S(2)}, u32[]{:S(2)}) collective-permute-start(bf16[128,768]{1,0:T(8,128)(2,1)} %refs_0_.1), channel_id=1, source_target_pairs={{0,4},{1,5},{2,6},{3,7},{4,0},{5,1},{6,2},{7,3},{8,12},{9,13},{10,... | collective-permute-start | bytes 589832 | tf_op jit(solution)/shard_map/ppermute | solution.py:300
  9.1 1.7 %shard_map.122 = (bf16[144,768]{1,0:T(8,128)(2,1)S(1)}, bf16[48,768]{1,0:T(8,128)(2,1)S(1)}, bf16[16,768]{1,0:T(8,128)(2,1)S(1)}, f32[8,768]{1,0:T(8,128)S(1)}) custom-call(s32[1]{0:T(128)} %bitcast.me_ref.refs_0_, s32[1,1,32]{2,1,0:T(1,128)} %tiles_ref.1, s32[1,1,32]{2,1,0:T(1,128)} %bitcast.9, s32[1,1,32]{2,1,0:T(1,128)} %slots_ref.1, ...), custom_call_target="tpu_custom_call" | custom-call | tf_op jit(solution)/shard_map/pallas_call | solution.py:340
  10.8 0.0 collective-permute-done.3.refs_1_
  10.8 1.6 %collective-permute-done.refs_0_.refs_2_ = bf16[48,768]{1,0:T(8,128)(2,1)S(1)} collective-permute-done((bf16[48,768]{1,0:T(8,128)(2,1)}, bf16[48,768]{1,0:T(8,128)(2,1)S(1)}, u32[]{:S(2)}, u32[]{:S(2)}) %collective-permute-start) | collective-permute-done | bytes 73760 | tf_op jit(solution)/shard_map/ppermute | solution.py:300
  12.5 0.0 collective-permute-done.4.refs_4_
  12.5 0.6 %collective-permute-start.5 = (bf16[112,768]{1,0:T(8,128)(2,1)S(1)}, bf16[112,768]{1,0:T(8,128)(2,1)S(1)}, u32[]{:S(2)}, u32[]{:S(2)}) collective-permute-start(bf16[112,768]{1,0:T(8,128)(2,1)S(1)} %shard_map.124), channel_id=1, source_target_pairs={{0,2},{1,3},{2,0},{3,1},{4,6},{5,7},{6,4},{7,5},{8,10},{9,11},{10,... | collective-permute-start | bytes 516104 | tf_op jit(solution)/shard_map/ppermute | solution.py:300
  13.1 0.1 collective-permute-start.2
  13.2 2.5 %collective-permute-start.1 = (bf16[144,768]{1,0:T(8,128)(2,1)S(1)}, bf16[144,768]{1,0:T(8,128)(2,1)S(1)}, u32[]{:S(2)}, u32[]{:S(2)}) collective-permute-start(bf16[144,768]{1,0:T(8,128)(2,1)S(1)} %get-tuple-element.23.refs_3_.refs_10_.refs_4_), channel_id=1, source_target_pairs={{0,12},{1,13},{2,14},{3,15},{4,8},{5,9},{6,10},{7,11},{8,4},{9,5},... | collective-permute-start | bytes 663560 | tf_op jit(solution)/shard_map/ppermute | solution.py:300
  15.7 0.6 %collective-permute-done.9.refs_5_ = bf16[128,768]{1,0:T(8,128)(2,1)S(1)} collective-permute-done((bf16[128,768]{1,0:T(8,128)(2,1)}, bf16[128,768]{1,0:T(8,128)(2,1)S(1)}, u32[]{:S(2)}, u32[]{:S(2)}) %collective-permute-start.9) | collective-permute-done | bytes 196640 | tf_op jit(solution)/shard_map/ppermute | solution.py:300
  16.3 0.9 %collective-permute-start.10 = (bf16[128,768]{1,0:T(8,128)(2,1)S(1)}, bf16[128,768]{1,0:T(8,128)(2,1)S(1)}, u32[]{:S(2)}, u32[]{:S(2)}) collective-permute-start(bf16[128,768]{1,0:T(8,128)(2,1)S(1)} %collective-permute-done.9.refs_5_), channel_id=1, source_target_pairs={{0,2},{1,3},{2,0},{3,1},{4,6},{5,7},{6,4},{7,5},{8,10},{9,11},{10,... | collective-permute-start | bytes 589832 | tf_op jit(solution)/shard_map/ppermute | solution.py:300
  17.2 1.4 %shard_map.125.refs_22_.refs_12_ = bf16[960,768]{1,0:T(8,128)(2,1)S(1)} custom-call(bf16[16,768]{1,0:T(8,128)(2,1)S(1)} %get-tuple-element.24.refs_1_.refs_2_.refs_0_, bf16[960,768]{1,0:T(8,128)(2,1)} %bitcast.8), custom_call_target="tpu_custom_call" | custom-call | tf_op jit(solution)/shard_map/pallas_call | solution.py:374
  18.6 0.1 collective-permute-done.2.refs_1_.refs_3_.refs_12_.refs_6_
  18.7 0.0 collective-permute-done.5.refs_4_.refs_11_.refs_5_
  18.7 0.0 collective-permute-done.6.refs_23_.refs_13_
  18.7 3.1 %collective-permute-start.11 = (bf16[112,768]{1,0:T(8,128)(2,1)S(1)}, bf16[112,768]{1,0:T(8,128)(2,1)S(1)}, u32[]{:S(2)}, u32[]{:S(2)}) collective-permute-start(bf16[112,768]{1,0:T(8,128)(2,1)S(1)} %shard_map.126), channel_id=1, source_target_pairs={{0,2},{1,3},{2,0},{3,1},{4,6},{5,7},{6,4},{7,5},{8,10},{9,11},{10,... | collective-permute-start | bytes 516104 | tf_op jit(solution)/shard_map/ppermute | solution.py:300
  21.8 1.2 %collective-permute-done.1.refs_1_.refs_8_.refs_2_ = bf16[144,768]{1,0:T(8,128)(2,1)S(1)} collective-permute-done((bf16[144,768]{1,0:T(8,128)(2,1)S(1)}, bf16[144,768]{1,0:T(8,128)(2,1)S(1)}, u32[]{:S(2)}, u32[]{:S(2)}) %collective-permute-start.1) | collective-permute-done | bytes 221216 | tf_op jit(solution)/shard_map/ppermute | solution.py:300
  23.0 0.7 %collective-permute-start.8 = (bf16[144,768]{1,0:T(8,128)(2,1)S(1)}, bf16[144,768]{1,0:T(8,128)(2,1)S(1)}, u32[]{:S(2)}, u32[]{:S(2)}) collective-permute-start(bf16[144,768]{1,0:T(8,128)(2,1)S(1)} %collective-permute-done.1.refs_1_.refs_8_.refs_2_), channel_id=1, source_target_pairs={{0,2},{1,3},{2,0},{3,1},{4,6},{5,7},{6,4},{7,5},{8,10},{9,11},{10,... | collective-permute-start | bytes 663560 | tf_op jit(solution)/shard_map/ppermute | solution.py:300
  23.7 3.5 %collective-permute-start.7 = (bf16[144,768]{1,0:T(8,128)(2,1)S(1)}, bf16[144,768]{1,0:T(8,128)(2,1)S(1)}, u32[]{:S(2)}, u32[]{:S(2)}) collective-permute-start(bf16[144,768]{1,0:T(8,128)(2,1)S(1)} %collective-permute-done.1.refs_1_.refs_8_.refs_2_), channel_id=1, source_target_pairs={{0,4},{1,5},{2,6},{3,7},{4,0},{5,1},{6,2},{7,3},{8,12},{9,13},{10,... | collective-permute-start | bytes 663560 | tf_op jit(solution)/shard_map/ppermute | solution.py:300
  27.2 0.0 collective-permute-done.10.refs_6_
  27.2 0.0 collective-permute-done.11.refs_5_.refs_13_.refs_7_
  27.2 0.1 collective-permute-start.12
  27.3 0.5 collective-permute-start.13
  27.8 0.1 collective-permute-start.14
  27.9 2.7 %collective-permute-done.8.refs_2_.refs_9_.refs_3_ = bf16[144,768]{1,0:T(8,128)(2,1)S(1)} collective-permute-done((bf16[144,768]{1,0:T(8,128)(2,1)S(1)}, bf16[144,768]{1,0:T(8,128)(2,1)S(1)}, u32[]{:S(2)}, u32[]{:S(2)}) %collective-permute-start.8) | collective-permute-done | bytes 221216 | tf_op jit(solution)/shard_map/ppermute | solution.py:300
  30.6 0.7 %collective-permute-done.7.refs_7_.refs_14_.refs_8_ = bf16[144,768]{1,0:T(8,128)(2,1)S(1)} collective-permute-done((bf16[144,768]{1,0:T(8,128)(2,1)S(1)}, bf16[144,768]{1,0:T(8,128)(2,1)S(1)}, u32[]{:S(2)}, u32[]{:S(2)}) %collective-permute-start.7) | collective-permute-done | bytes 221216 | tf_op jit(solution)/shard_map/ppermute | solution.py:300
  31.3 0.0 collective-permute-done.12.refs_18_
  31.3 0.0 collective-permute-done.13.refs_19_
  31.3 0.0 collective-permute-done.14.refs_20_
  31.3 0.4 collective-permute-start.15
  31.7 0.0 copy-start
  31.7 5.1 %shard_map.128 = (f32[8,960]{1,0:T(8,128)S(1)}, f32[8,960]{1,0:T(8,128)S(1)}, bf16[768,768]{1,0:T(8,128)(2,1)S(1)}) custom-call(s32[1]{0:T(128)} %bitcast.me_ref.refs_0_, bf16[144,768]{1,0:T(8,128)(2,1)S(1)} %collective-permute-done.1.refs_1_.refs_8_.refs_2_, bf16[144,768]{1,0:T(8,128)(2,1)S(1)} %collective-permute-done.8.refs_2_.refs_9_.refs_3_, ...), custom_call_target="tpu_custom_call" | custom-call | flops 2 | bytes 2 | tf_op jit(solution)/shard_map/pallas_call | solution.py:398
  36.8 0.5 %collective-permute-done.15.refs_1_.refs_9_ = bf16[144,768]{1,0:T(8,128)(2,1)S(1)} collective-permute-done((bf16[144,768]{1,0:T(8,128)(2,1)S(1)}, bf16[144,768]{1,0:T(8,128)(2,1)S(1)}, u32[]{:S(2)}, u32[]{:S(2)}) %collective-permute-start.15) | collective-permute-done | bytes 221216 | tf_op jit(solution)/shard_map/ppermute | solution.py:300
  37.3 0.0 copy-done
  37.3 2.0 %shard_map.129 = (bf16[8,48,128]{2,1,0:T(8,128)(2,1)S(1)}, bf16[8,32,128]{2,1,0:T(8,128)(2,1)S(1)}) custom-call(s32[1]{0:T(128)} %bitcast.me_ref.refs_0_, bf16[144,768]{1,0:T(8,128)(2,1)S(1)} %collective-permute-done.15.refs_1_.refs_9_, bf16[144,768]{1,0:T(8,128)(2,1)S(1)} %collective-permute-done.1.refs_1_.refs_8_.refs_2_, ...), custom_call_target="tpu_custom_call" | custom-call | flops 2 | bytes 2 | tf_op jit(solution)/shard_map/pallas_call | solution.py:432
  39.3 0.1 collective-permute-start.16
  39.4 1.2 %collective-permute-done.16.got_ref = bf16[8,32,128]{2,1,0:T(8,128)(2,1)S(1)} collective-permute-done((bf16[8,32,128]{2,1,0:T(8,128)(2,1)S(1)}, bf16[8,32,128]{2,1,0:T(8,128)(2,1)S(1)}, u32[]{:S(2)}, u32[]{:S(2)}) %collective-permute-start.16) | collective-permute-done | bytes 65568 | tf_op jit(solution)/shard_map/ppermute | solution.py:303
  40.7 11.3 %all_to_all.5.refs_0_ = bf16[8,48,128]{2,1,0:T(8,128)(2,1)S(1)} all-to-all(bf16[8,48,128]{2,1,0:T(8,128)(2,1)S(1)} %shard_map.130), channel_id=1, replica_groups={{0,2,4,6,8,10,12,14},{1,3,5,7,9,11,13,15},{16,18,20,22,24,26,28,30},{17..., dimensions={0} | all-to-all | bytes 196608 | tf_op jit(solution)/shard_map/all_to_all | solution.py:462
  52.0 0.8 %shard_map.131 = (bf16[1,15360]{1,0:T(2,128)(2,1)}, bf16[2,15360]{1,0:T(2,128)(2,1)}) custom-call(bf16[8,48,128]{2,1,0:T(8,128)(2,1)S(1)} %all_to_all.5.refs_0_), custom_call_target="tpu_custom_call" | custom-call | tf_op jit(solution)/shard_map/pallas_call | solution.py:465
  (5 shorter events, 0.1 us)
Async XLA Ops:
  0.6 18.0 %collective-permute-start.6 = (bf16[960,768]{1,0:T(8,128)(2,1)}, bf16[960,768]{1,0:T(8,128)(2,1)S(1)}, u32[]{:S(2)}, u32[]{:S(2)}) collective-permute-start(bf16[960,768]{1,0:T(8,128)(2,1)} %bitcast.7), channel_id=1, source_target_pairs={{0,1},{1,0},{2,3},{3,2},{4,5},{5,4},{6,7},{7,6},{8,9},{9,8},{10,11... | collective-permute-start | bytes 4423688 | tf_op jit(solution)/shard_map/ppermute | solution.py:303
  1.2 11.3 %collective-permute-start.4 = (bf16[128,768]{1,0:T(8,128)(2,1)}, bf16[128,768]{1,0:T(8,128)(2,1)S(1)}, u32[]{:S(2)}, u32[]{:S(2)}) collective-permute-start(bf16[128,768]{1,0:T(8,128)(2,1)} %refs_0_.1), channel_id=1, source_target_pairs={{0,2},{1,3},{2,0},{3,1},{4,6},{5,7},{6,4},{7,5},{8,10},{9,11},{10,... | collective-permute-start | bytes 589832 | tf_op jit(solution)/shard_map/ppermute | solution.py:300
  3.7 7.1 %collective-permute-start.3 = (bf16[48,768]{1,0:T(8,128)(2,1)}, bf16[48,768]{1,0:T(8,128)(2,1)S(1)}, u32[]{:S(2)}, u32[]{:S(2)}) collective-permute-start(bf16[48,768]{1,0:T(8,128)(2,1)} %refs_1_.1), channel_id=1, source_target_pairs={{0,4},{1,5},{2,6},{3,7},{4,0},{5,1},{6,2},{7,3},{8,12},{9,13},{10,... | collective-permute-start | bytes 221192 | tf_op jit(solution)/shard_map/ppermute | solution.py:300
  5.3 7.2 %collective-permute-start = (bf16[48,768]{1,0:T(8,128)(2,1)}, bf16[48,768]{1,0:T(8,128)(2,1)S(1)}, u32[]{:S(2)}, u32[]{:S(2)}) collective-permute-start(bf16[48,768]{1,0:T(8,128)(2,1)} %refs_1_.1), channel_id=1, source_target_pairs={{0,12},{1,13},{2,14},{3,15},{4,8},{5,9},{6,10},{7,11},{8,4},{9,5},... | collective-permute-start | bytes 221192 | tf_op jit(solution)/shard_map/ppermute | solution.py:300
  7.8 8.5 %collective-permute-start.9 = (bf16[128,768]{1,0:T(8,128)(2,1)}, bf16[128,768]{1,0:T(8,128)(2,1)S(1)}, u32[]{:S(2)}, u32[]{:S(2)}) collective-permute-start(bf16[128,768]{1,0:T(8,128)(2,1)} %refs_0_.1), channel_id=1, source_target_pairs={{0,4},{1,5},{2,6},{3,7},{4,0},{5,1},{6,2},{7,3},{8,12},{9,13},{10,... | collective-permute-start | bytes 589832 | tf_op jit(solution)/shard_map/ppermute | solution.py:300
  12.5 6.2 %collective-permute-start.5 = (bf16[112,768]{1,0:T(8,128)(2,1)S(1)}, bf16[112,768]{1,0:T(8,128)(2,1)S(1)}, u32[]{:S(2)}, u32[]{:S(2)}) collective-permute-start(bf16[112,768]{1,0:T(8,128)(2,1)S(1)} %shard_map.124), channel_id=1, source_target_pairs={{0,2},{1,3},{2,0},{3,1},{4,6},{5,7},{6,4},{7,5},{8,10},{9,11},{10,... | collective-permute-start | bytes 516104 | tf_op jit(solution)/shard_map/ppermute | solution.py:300
  13.1 5.6 %collective-permute-start.2 = (bf16[64,768]{1,0:T(8,128)(2,1)S(1)}, bf16[64,768]{1,0:T(8,128)(2,1)S(1)}, u32[]{:S(2)}, u32[]{:S(2)}) collective-permute-start(bf16[64,768]{1,0:T(8,128)(2,1)S(1)} %shard_map.123), channel_id=1, source_target_pairs={{0,4},{1,5},{2,6},{3,7},{4,0},{5,1},{6,2},{7,3},{8,12},{9,13},{10,... | collective-permute-start | bytes 294920 | tf_op jit(solution)/shard_map/ppermute | solution.py:300
  13.2 9.8 %collective-permute-start.1 = (bf16[144,768]{1,0:T(8,128)(2,1)S(1)}, bf16[144,768]{1,0:T(8,128)(2,1)S(1)}, u32[]{:S(2)}, u32[]{:S(2)}) collective-permute-start(bf16[144,768]{1,0:T(8,128)(2,1)S(1)} %get-tuple-element.23.refs_3_.refs_10_.refs_4_), channel_id=1, source_target_pairs={{0,12},{1,13},{2,14},{3,15},{4,8},{5,9},{6,10},{7,11},{8,4},{9,5},... | collective-permute-start | bytes 663560 | tf_op jit(solution)/shard_map/ppermute | solution.py:300
  16.3 10.8 %collective-permute-start.10 = (bf16[128,768]{1,0:T(8,128)(2,1)S(1)}, bf16[128,768]{1,0:T(8,128)(2,1)S(1)}, u32[]{:S(2)}, u32[]{:S(2)}) collective-permute-start(bf16[128,768]{1,0:T(8,128)(2,1)S(1)} %collective-permute-done.9.refs_5_), channel_id=1, source_target_pairs={{0,2},{1,3},{2,0},{3,1},{4,6},{5,7},{6,4},{7,5},{8,10},{9,11},{10,... | collective-permute-start | bytes 589832 | tf_op jit(solution)/shard_map/ppermute | solution.py:300
  18.7 8.5 %collective-permute-start.11 = (bf16[112,768]{1,0:T(8,128)(2,1)S(1)}, bf16[112,768]{1,0:T(8,128)(2,1)S(1)}, u32[]{:S(2)}, u32[]{:S(2)}) collective-permute-start(bf16[112,768]{1,0:T(8,128)(2,1)S(1)} %shard_map.126), channel_id=1, source_target_pairs={{0,2},{1,3},{2,0},{3,1},{4,6},{5,7},{6,4},{7,5},{8,10},{9,11},{10,... | collective-permute-start | bytes 516104 | tf_op jit(solution)/shard_map/ppermute | solution.py:300
  23.0 7.6 %collective-permute-start.8 = (bf16[144,768]{1,0:T(8,128)(2,1)S(1)}, bf16[144,768]{1,0:T(8,128)(2,1)S(1)}, u32[]{:S(2)}, u32[]{:S(2)}) collective-permute-start(bf16[144,768]{1,0:T(8,128)(2,1)S(1)} %collective-permute-done.1.refs_1_.refs_8_.refs_2_), channel_id=1, source_target_pairs={{0,2},{1,3},{2,0},{3,1},{4,6},{5,7},{6,4},{7,5},{8,10},{9,11},{10,... | collective-permute-start | bytes 663560 | tf_op jit(solution)/shard_map/ppermute | solution.py:300
  23.7 7.6 %collective-permute-start.7 = (bf16[144,768]{1,0:T(8,128)(2,1)S(1)}, bf16[144,768]{1,0:T(8,128)(2,1)S(1)}, u32[]{:S(2)}, u32[]{:S(2)}) collective-permute-start(bf16[144,768]{1,0:T(8,128)(2,1)S(1)} %collective-permute-done.1.refs_1_.refs_8_.refs_2_), channel_id=1, source_target_pairs={{0,4},{1,5},{2,6},{3,7},{4,0},{5,1},{6,2},{7,3},{8,12},{9,13},{10,... | collective-permute-start | bytes 663560 | tf_op jit(solution)/shard_map/ppermute | solution.py:300
  27.2 4.1 %collective-permute-start.12 = (bf16[128,768]{1,0:T(8,128)(2,1)S(1)}, bf16[128,768]{1,0:T(8,128)(2,1)S(1)}, u32[]{:S(2)}, u32[]{:S(2)}) collective-permute-start(bf16[128,768]{1,0:T(8,128)(2,1)S(1)} %get-tuple-element.32.refs_15_), channel_id=1, source_target_pairs={{0,1},{1,0},{2,3},{3,2},{4,5},{5,4},{6,7},{7,6},{8,9},{9,8},{10,11... | collective-permute-start | bytes 589832 | tf_op jit(solution)/shard_map/ppermute | solution.py:303
  27.3 4.0 %collective-permute-start.13 = (bf16[128,768]{1,0:T(8,128)(2,1)S(1)}, bf16[128,768]{1,0:T(8,128)(2,1)S(1)}, u32[]{:S(2)}, u32[]{:S(2)}) collective-permute-start(bf16[128,768]{1,0:T(8,128)(2,1)S(1)} %get-tuple-element.33.refs_16_), channel_id=1, source_target_pairs={{0,1},{1,0},{2,3},{3,2},{4,5},{5,4},{6,7},{7,6},{8,9},{9,8},{10,11... | collective-permute-start | bytes 589832 | tf_op jit(solution)/shard_map/ppermute | solution.py:303
  27.8 3.5 %collective-permute-start.14 = (bf16[128,768]{1,0:T(8,128)(2,1)S(1)}, bf16[128,768]{1,0:T(8,128)(2,1)S(1)}, u32[]{:S(2)}, u32[]{:S(2)}) collective-permute-start(bf16[128,768]{1,0:T(8,128)(2,1)S(1)} %get-tuple-element.34.refs_17_), channel_id=1, source_target_pairs={{0,1},{1,0},{2,3},{3,2},{4,5},{5,4},{6,7},{7,6},{8,9},{9,8},{10,11... | collective-permute-start | bytes 589832 | tf_op jit(solution)/shard_map/ppermute | solution.py:303
  31.3 6.0 %collective-permute-start.15 = (bf16[144,768]{1,0:T(8,128)(2,1)S(1)}, bf16[144,768]{1,0:T(8,128)(2,1)S(1)}, u32[]{:S(2)}, u32[]{:S(2)}) collective-permute-start(bf16[144,768]{1,0:T(8,128)(2,1)S(1)} %collective-permute-done.7.refs_7_.refs_14_.refs_8_), channel_id=1, source_target_pairs={{0,2},{1,3},{2,0},{3,1},{4,6},{5,7},{6,4},{7,5},{8,10},{9,11},{10,... | collective-permute-start | bytes 663560 | tf_op jit(solution)/shard_map/ppermute | solution.py:300
  31.7 5.6 %copy-start = (f32[15360]{0:T(1024)S(1)}, f32[15360]{0:T(1024)}, u32[]{:S(2)}) copy-start(f32[15360]{0:T(1024)} %param.18) | copy-start | bytes 184324
  39.3 1.3 %collective-permute-start.16 = (bf16[8,32,128]{2,1,0:T(8,128)(2,1)S(1)}, bf16[8,32,128]{2,1,0:T(8,128)(2,1)S(1)}, u32[]{:S(2)}, u32[]{:S(2)}) collective-permute-start(bf16[8,32,128]{2,1,0:T(8,128)(2,1)S(1)} %get-tuple-element.41), channel_id=1, source_target_pairs={{0,1},{1,0},{2,3},{3,2},{4,5},{5,4},{6,7},{7,6},{8,9},{9,8},{10,11... | collective-permute-start | bytes 196616 | tf_op jit(solution)/shard_map/ppermute | solution.py:303

commit v26 on v25

--- a/solution.py
+++ b/solution.py
@@ -389,7 +389,7 @@
     other_packed = [swap(part) for part in packed]
     block_masks = [0, 2, 6, 4, 1, 3, 7, 5]
 
-    groups = [[6, 7, 0, 1, 2, 3, 4], [5]]
+    groups = [[6, 7, 0, 1, 2, 3], [4, 5]]
     masks = [mask for group in groups for mask in group]
     docs[0] = load
     docs[5] = cross(after(docs[4], docs[7], *other_packed), 1)

time: 53 us -> 52.8 us (level)
  waiting for transfers between devices: 8.75 us -> 13.7 us
  starting transfers between devices: 20.3 us -> 17 us
  blocking collectives: 11.3 us -> 10 us
    ppermute x12, waiting for transfers between devices: 7.5 us -> 12.5 us  [cross(): lax.ppermute(value, 'doc', [(i, i ^ 2 * mask) for i in range(devices)])]
    ppermute x12, starting transfers between devices: 19 us -> 15.7 us  [cross(): lax.ppermute(value, 'doc', [(i, i ^ 2 * mask) for i in range(devices)])]
    all_to_all x1, blocking collectives: 11.3 us -> 10 us  [move_tokens(): lax.all_to_all(merged, 'doc', split_axis=0, concat_axis=0, axis_index_gro...]
    pallas_call x1, Pallas kernels: 5.08 us -> 4.42 us  [move_tokens(): pl.pallas_call(lambda *refs: first_kernel(seq, rows, block_masks, len(gro...]
  transfers between devices with their start and end apart: 17 -> 17, of which waited for: 8 -> 8; matrix products, arithmetic and copies ran while one was open for 0% -> 0% of each run, Pallas kernels for 16% -> 14%
where the time goes in v26:
time: 52.8 us; the launch traced here: 52.6 us
  starting transfers between devices  17 us (32%)
  waiting for transfers between devices  13.7 us (26%)
  Pallas kernels  10.5 us (20%)
  blocking collectives  10 us (19%)
  between operations  1.39 us (3%)
    ppermute x12, starting transfers between devices, cross(): lax.ppermute(value, 'doc', [(i, i ^ 2 * mask) for i in range(devices)])  15.7 us
    ppermute x12, waiting for transfers between devices, cross(): lax.ppermute(value, 'doc', [(i, i ^ 2 * mask) for i in range(devices)])  12.5 us
    all_to_all x1, blocking collectives, move_tokens(): lax.all_to_all(merged, 'doc', split_axis=0, concat_axis=0, axis_index_gro...  10 us
    pallas_call x1, Pallas kernels, move_tokens(): pl.pallas_call(lambda *refs: first_kernel(seq, rows, block_masks, len(gro...  4.42 us
    pallas_call x1, Pallas kernels, move_tokens(): pl.pallas_call(lambda *refs: last_kernel(seq, groups, *refs), out_shape=[...  2.13 us
    pallas_call x1, Pallas kernels, move_tokens(): pl.pallas_call(start_kernel, out_shape=[shape((seq + SLOT_ROWS, width), j...  1.71 us
    pallas_call x1, Pallas kernels, move_tokens(): pl.pallas_call(lambda *refs: fetch_kernel(1, *refs), out_shape=[shape(val...  1.38 us
    ppermute x5, waiting for transfers between devices, swap(): return lax.ppermute(value, 'doc', [(i, i ^ 1) for i in range(devices)])  1.25 us
  transfers between devices with their start and end apart: 17, of which 8 were waited for; matrix products, arithmetic and copies ran while one was open for 0% of the time, Pallas kernels for 14%

profile of v26, /device:TPU:0, one launch (start us, length us, event | category | flops | bytes accessed | tf_op | source)
XLA Modules:
  0.0 52.6 jit_solution(7303841064366078397)
XLA Ops:
  0.6 0.5 collective-permute-start.6
  1.2 2.6 %collective-permute-start.4 = (bf16[128,768]{1,0:T(8,128)(2,1)}, bf16[128,768]{1,0:T(8,128)(2,1)S(1)}, u32[]{:S(2)}, u32[]{:S(2)}) collective-permute-start(bf16[128,768]{1,0:T(8,128)(2,1)} %refs_0_.1), channel_id=1, source_target_pairs={{0,2},{1,3},{2,0},{3,1},{4,6},{5,7},{6,4},{7,5},{8,10},{9,11},{10,... | collective-permute-start | bytes 589832 | tf_op jit(solution)/shard_map/ppermute | solution.py:300
  3.7 3.6 %collective-permute-start = (bf16[48,768]{1,0:T(8,128)(2,1)}, bf16[48,768]{1,0:T(8,128)(2,1)S(1)}, u32[]{:S(2)}, u32[]{:S(2)}) collective-permute-start(bf16[48,768]{1,0:T(8,128)(2,1)} %refs_1_.1), channel_id=1, source_target_pairs={{0,12},{1,13},{2,14},{3,15},{4,8},{5,9},{6,10},{7,11},{8,4},{9,5},... | collective-permute-start | bytes 221192 | tf_op jit(solution)/shard_map/ppermute | solution.py:300
  7.3 0.0 collective-permute-start.3
  7.3 2.0 %collective-permute-start.9 = (bf16[128,768]{1,0:T(8,128)(2,1)}, bf16[128,768]{1,0:T(8,128)(2,1)S(1)}, u32[]{:S(2)}, u32[]{:S(2)}) collective-permute-start(bf16[128,768]{1,0:T(8,128)(2,1)} %refs_0_.1), channel_id=1, source_target_pairs={{0,4},{1,5},{2,6},{3,7},{4,0},{5,1},{6,2},{7,3},{8,12},{9,13},{10,... | collective-permute-start | bytes 589832 | tf_op jit(solution)/shard_map/ppermute | solution.py:300
  10.0 1.7 %shard_map.122 = (bf16[144,768]{1,0:T(8,128)(2,1)S(1)}, bf16[48,768]{1,0:T(8,128)(2,1)S(1)}, bf16[16,768]{1,0:T(8,128)(2,1)S(1)}, f32[8,768]{1,0:T(8,128)S(1)}) custom-call(s32[1]{0:T(128)} %bitcast.me_ref.refs_0_, s32[1,1,32]{2,1,0:T(1,128)} %tiles_ref.1, s32[1,1,32]{2,1,0:T(1,128)} %bitcast.9, s32[1,1,32]{2,1,0:T(1,128)} %slots_ref.1, ...), custom_call_target="tpu_custom_call" | custom-call | tf_op jit(solution)/shard_map/pallas_call | solution.py:340
  11.7 0.0 collective-permute-done.refs_0_.refs_2_
  11.7 1.0 %collective-permute-done.3.refs_1_ = bf16[48,768]{1,0:T(8,128)(2,1)S(1)} collective-permute-done((bf16[48,768]{1,0:T(8,128)(2,1)}, bf16[48,768]{1,0:T(8,128)(2,1)S(1)}, u32[]{:S(2)}, u32[]{:S(2)}) %collective-permute-start.3) | collective-permute-done | bytes 73760 | tf_op jit(solution)/shard_map/ppermute | solution.py:300
  12.7 0.0 collective-permute-done.4.refs_4_
  12.7 0.6 %collective-permute-start.5 = (bf16[112,768]{1,0:T(8,128)(2,1)S(1)}, bf16[112,768]{1,0:T(8,128)(2,1)S(1)}, u32[]{:S(2)}, u32[]{:S(2)}) collective-permute-start(bf16[112,768]{1,0:T(8,128)(2,1)S(1)} %shard_map.124), channel_id=1, source_target_pairs={{0,2},{1,3},{2,0},{3,1},{4,6},{5,7},{6,4},{7,5},{8,10},{9,11},{10,... | collective-permute-start | bytes 516104 | tf_op jit(solution)/shard_map/ppermute | solution.py:300
  13.3 1.6 %collective-permute-start.2 = (bf16[64,768]{1,0:T(8,128)(2,1)S(1)}, bf16[64,768]{1,0:T(8,128)(2,1)S(1)}, u32[]{:S(2)}, u32[]{:S(2)}) collective-permute-start(bf16[64,768]{1,0:T(8,128)(2,1)S(1)} %shard_map.123), channel_id=1, source_target_pairs={{0,4},{1,5},{2,6},{3,7},{4,0},{5,1},{6,2},{7,3},{8,12},{9,13},{10,... | collective-permute-start | bytes 294920 | tf_op jit(solution)/shard_map/ppermute | solution.py:300
  14.9 0.5 collective-permute-start.1
  15.4 1.5 %collective-permute-done.9.refs_5_ = bf16[128,768]{1,0:T(8,128)(2,1)S(1)} collective-permute-done((bf16[128,768]{1,0:T(8,128)(2,1)}, bf16[128,768]{1,0:T(8,128)(2,1)S(1)}, u32[]{:S(2)}, u32[]{:S(2)}) %collective-permute-start.9) | collective-permute-done | bytes 196640 | tf_op jit(solution)/shard_map/ppermute | solution.py:300
  16.9 0.4 collective-permute-start.10
  17.3 1.4 %shard_map.125.refs_20_.refs_13_ = bf16[960,768]{1,0:T(8,128)(2,1)S(1)} custom-call(bf16[16,768]{1,0:T(8,128)(2,1)S(1)} %get-tuple-element.24.refs_1_.refs_2_.refs_0_, bf16[960,768]{1,0:T(8,128)(2,1)} %bitcast.8), custom_call_target="tpu_custom_call" | custom-call | tf_op jit(solution)/shard_map/pallas_call | solution.py:374
  18.7 4.4 %collective-permute-done.2.refs_1_.refs_3_.refs_11_.refs_7_ = bf16[64,768]{1,0:T(8,128)(2,1)S(1)} collective-permute-done((bf16[64,768]{1,0:T(8,128)(2,1)S(1)}, bf16[64,768]{1,0:T(8,128)(2,1)S(1)}, u32[]{:S(2)}, u32[]{:S(2)}) %collective-permute-start.2) | collective-permute-done | bytes 98336 | tf_op jit(solution)/shard_map/ppermute | solution.py:300
  23.1 0.0 collective-permute-done.5.refs_4_.refs_10_.refs_6_
  23.1 0.0 collective-permute-done.6.refs_21_.refs_14_
  23.1 0.1 collective-permute-start.11
  23.2 0.0 collective-permute-done.1.refs_1_.refs_7_.refs_3_
  23.2 2.0 %collective-permute-start.8 = (bf16[144,768]{1,0:T(8,128)(2,1)S(1)}, bf16[144,768]{1,0:T(8,128)(2,1)S(1)}, u32[]{:S(2)}, u32[]{:S(2)}) collective-permute-start(bf16[144,768]{1,0:T(8,128)(2,1)S(1)} %collective-permute-done.1.refs_1_.refs_7_.refs_3_), channel_id=1, source_target_pairs={{0,2},{1,3},{2,0},{3,1},{4,6},{5,7},{6,4},{7,5},{8,10},{9,11},{10,... | collective-permute-start | bytes 663560 | tf_op jit(solution)/shard_map/ppermute | solution.py:300
  25.2 2.0 %collective-permute-start.7 = (bf16[144,768]{1,0:T(8,128)(2,1)S(1)}, bf16[144,768]{1,0:T(8,128)(2,1)S(1)}, u32[]{:S(2)}, u32[]{:S(2)}) collective-permute-start(bf16[144,768]{1,0:T(8,128)(2,1)S(1)} %collective-permute-done.1.refs_1_.refs_7_.refs_3_), channel_id=1, source_target_pairs={{0,4},{1,5},{2,6},{3,7},{4,0},{5,1},{6,2},{7,3},{8,12},{9,13},{10,... | collective-permute-start | bytes 663560 | tf_op jit(solution)/shard_map/ppermute | solution.py:300
  27.1 0.0 collective-permute-done.10.refs_6_
  27.1 1.5 %collective-permute-done.11.refs_5_.refs_12_.refs_8_ = bf16[112,768]{1,0:T(8,128)(2,1)S(1)} collective-permute-done((bf16[112,768]{1,0:T(8,128)(2,1)S(1)}, bf16[112,768]{1,0:T(8,128)(2,1)S(1)}, u32[]{:S(2)}, u32[]{:S(2)}) %collective-permute-start.11) | collective-permute-done | bytes 172064 | tf_op jit(solution)/shard_map/ppermute | solution.py:300
  28.7 0.1 collective-permute-start.12
  28.7 0.5 collective-permute-start.13
  29.2 0.1 collective-permute-start.14
  29.3 1.7 %collective-permute-done.8.refs_2_.refs_8_.refs_4_ = bf16[144,768]{1,0:T(8,128)(2,1)S(1)} collective-permute-done((bf16[144,768]{1,0:T(8,128)(2,1)S(1)}, bf16[144,768]{1,0:T(8,128)(2,1)S(1)}, u32[]{:S(2)}, u32[]{:S(2)}) %collective-permute-start.8) | collective-permute-done | bytes 221216 | tf_op jit(solution)/shard_map/ppermute | solution.py:300
  31.0 0.1 collective-permute-done.7.refs_1_.refs_9_
  31.1 0.0 collective-permute-done.12.refs_16_
  31.1 0.0 collective-permute-done.13.refs_17_
  31.1 0.0 collective-permute-done.14.refs_18_
  31.1 0.4 collective-permute-start.15
  31.5 0.0 copy-start
  31.5 4.4 %shard_map.128 = (f32[8,960]{1,0:T(8,128)S(1)}, f32[8,960]{1,0:T(8,128)S(1)}, bf16[768,768]{1,0:T(8,128)(2,1)S(1)}) custom-call(s32[1]{0:T(128)} %bitcast.me_ref.refs_0_, bf16[144,768]{1,0:T(8,128)(2,1)S(1)} %collective-permute-done.1.refs_1_.refs_7_.refs_3_, bf16[144,768]{1,0:T(8,128)(2,1)S(1)} %collective-permute-done.8.refs_2_.refs_8_.refs_4_, ...), custom_call_target="tpu_custom_call" | custom-call | flops 2 | bytes 2 | tf_op jit(solution)/shard_map/pallas_call | solution.py:398
  36.0 2.3 %collective-permute-done.15.refs_2_.refs_10_ = bf16[144,768]{1,0:T(8,128)(2,1)S(1)} collective-permute-done((bf16[144,768]{1,0:T(8,128)(2,1)S(1)}, bf16[144,768]{1,0:T(8,128)(2,1)S(1)}, u32[]{:S(2)}, u32[]{:S(2)}) %collective-permute-start.15) | collective-permute-done | bytes 221216 | tf_op jit(solution)/shard_map/ppermute | solution.py:300
  38.3 0.0 copy-done
  38.3 2.1 %shard_map.129 = (bf16[8,48,128]{2,1,0:T(8,128)(2,1)S(1)}, bf16[8,32,128]{2,1,0:T(8,128)(2,1)S(1)}) custom-call(s32[1]{0:T(128)} %bitcast.me_ref.refs_0_, bf16[144,768]{1,0:T(8,128)(2,1)S(1)} %collective-permute-done.7.refs_1_.refs_9_, bf16[144,768]{1,0:T(8,128)(2,1)S(1)} %collective-permute-done.15.refs_2_.refs_10_, ...), custom_call_target="tpu_custom_call" | custom-call | flops 2 | bytes 2 | tf_op jit(solution)/shard_map/pallas_call | solution.py:432
  40.4 0.1 collective-permute-start.16
  40.5 1.2 %collective-permute-done.16.got_ref = bf16[8,32,128]{2,1,0:T(8,128)(2,1)S(1)} collective-permute-done((bf16[8,32,128]{2,1,0:T(8,128)(2,1)S(1)}, bf16[8,32,128]{2,1,0:T(8,128)(2,1)S(1)}, u32[]{:S(2)}, u32[]{:S(2)}) %collective-permute-start.16) | collective-permute-done | bytes 65568 | tf_op jit(solution)/shard_map/ppermute | solution.py:303
  41.8 10.0 %all_to_all.5.refs_0_ = bf16[8,48,128]{2,1,0:T(8,128)(2,1)S(1)} all-to-all(bf16[8,48,128]{2,1,0:T(8,128)(2,1)S(1)} %shard_map.130), channel_id=1, replica_groups={{0,2,4,6,8,10,12,14},{1,3,5,7,9,11,13,15},{16,18,20,22,24,26,28,30},{17..., dimensions={0} | all-to-all | bytes 196608 | tf_op jit(solution)/shard_map/all_to_all | solution.py:462
  51.8 0.8 %shard_map.131 = (bf16[1,15360]{1,0:T(2,128)(2,1)}, bf16[2,15360]{1,0:T(2,128)(2,1)}) custom-call(bf16[8,48,128]{2,1,0:T(8,128)(2,1)S(1)} %all_to_all.5.refs_0_), custom_call_target="tpu_custom_call" | custom-call | tf_op jit(solution)/shard_map/pallas_call | solution.py:465
  (5 shorter events, 0.1 us)
Async XLA Ops:
  0.6 22.4 %collective-permute-start.6 = (bf16[960,768]{1,0:T(8,128)(2,1)}, bf16[960,768]{1,0:T(8,128)(2,1)S(1)}, u32[]{:S(2)}, u32[]{:S(2)}) collective-permute-start(bf16[960,768]{1,0:T(8,128)(2,1)} %bitcast.7), channel_id=1, source_target_pairs={{0,1},{1,0},{2,3},{3,2},{4,5},{5,4},{6,7},{7,6},{8,9},{9,8},{10,11... | collective-permute-start | bytes 4423688 | tf_op jit(solution)/shard_map/ppermute | solution.py:303
  1.2 11.5 %collective-permute-start.4 = (bf16[128,768]{1,0:T(8,128)(2,1)}, bf16[128,768]{1,0:T(8,128)(2,1)S(1)}, u32[]{:S(2)}, u32[]{:S(2)}) collective-permute-start(bf16[128,768]{1,0:T(8,128)(2,1)} %refs_0_.1), channel_id=1, source_target_pairs={{0,2},{1,3},{2,0},{3,1},{4,6},{5,7},{6,4},{7,5},{8,10},{9,11},{10,... | collective-permute-start | bytes 589832 | tf_op jit(solution)/shard_map/ppermute | solution.py:300
  3.7 8.0 %collective-permute-start = (bf16[48,768]{1,0:T(8,128)(2,1)}, bf16[48,768]{1,0:T(8,128)(2,1)S(1)}, u32[]{:S(2)}, u32[]{:S(2)}) collective-permute-start(bf16[48,768]{1,0:T(8,128)(2,1)} %refs_1_.1), channel_id=1, source_target_pairs={{0,12},{1,13},{2,14},{3,15},{4,8},{5,9},{6,10},{7,11},{8,4},{9,5},... | collective-permute-start | bytes 221192 | tf_op jit(solution)/shard_map/ppermute | solution.py:300
  7.3 5.4 %collective-permute-start.3 = (bf16[48,768]{1,0:T(8,128)(2,1)}, bf16[48,768]{1,0:T(8,128)(2,1)S(1)}, u32[]{:S(2)}, u32[]{:S(2)}) collective-permute-start(bf16[48,768]{1,0:T(8,128)(2,1)} %refs_1_.1), channel_id=1, source_target_pairs={{0,4},{1,5},{2,6},{3,7},{4,0},{5,1},{6,2},{7,3},{8,12},{9,13},{10,... | collective-permute-start | bytes 221192 | tf_op jit(solution)/shard_map/ppermute | solution.py:300
  7.3 9.6 %collective-permute-start.9 = (bf16[128,768]{1,0:T(8,128)(2,1)}, bf16[128,768]{1,0:T(8,128)(2,1)S(1)}, u32[]{:S(2)}, u32[]{:S(2)}) collective-permute-start(bf16[128,768]{1,0:T(8,128)(2,1)} %refs_0_.1), channel_id=1, source_target_pairs={{0,4},{1,5},{2,6},{3,7},{4,0},{5,1},{6,2},{7,3},{8,12},{9,13},{10,... | collective-permute-start | bytes 589832 | tf_op jit(solution)/shard_map/ppermute | solution.py:300
  12.7 10.4 %collective-permute-start.5 = (bf16[112,768]{1,0:T(8,128)(2,1)S(1)}, bf16[112,768]{1,0:T(8,128)(2,1)S(1)}, u32[]{:S(2)}, u32[]{:S(2)}) collective-permute-start(bf16[112,768]{1,0:T(8,128)(2,1)S(1)} %shard_map.124), channel_id=1, source_target_pairs={{0,2},{1,3},{2,0},{3,1},{4,6},{5,7},{6,4},{7,5},{8,10},{9,11},{10,... | collective-permute-start | bytes 516104 | tf_op jit(solution)/shard_map/ppermute | solution.py:300
  13.3 9.7 %collective-permute-start.2 = (bf16[64,768]{1,0:T(8,128)(2,1)S(1)}, bf16[64,768]{1,0:T(8,128)(2,1)S(1)}, u32[]{:S(2)}, u32[]{:S(2)}) collective-permute-start(bf16[64,768]{1,0:T(8,128)(2,1)S(1)} %shard_map.123), channel_id=1, source_target_pairs={{0,4},{1,5},{2,6},{3,7},{4,0},{5,1},{6,2},{7,3},{8,12},{9,13},{10,... | collective-permute-start | bytes 294920 | tf_op jit(solution)/shard_map/ppermute | solution.py:300
  14.9 8.3 %collective-permute-start.1 = (bf16[144,768]{1,0:T(8,128)(2,1)S(1)}, bf16[144,768]{1,0:T(8,128)(2,1)S(1)}, u32[]{:S(2)}, u32[]{:S(2)}) collective-permute-start(bf16[144,768]{1,0:T(8,128)(2,1)S(1)} %get-tuple-element.23.refs_3_.refs_9_.refs_5_), channel_id=1, source_target_pairs={{0,12},{1,13},{2,14},{3,15},{4,8},{5,9},{6,10},{7,11},{8,4},{9,5},... | collective-permute-start | bytes 663560 | tf_op jit(solution)/shard_map/ppermute | solution.py:300
  16.9 10.2 %collective-permute-start.10 = (bf16[128,768]{1,0:T(8,128)(2,1)S(1)}, bf16[128,768]{1,0:T(8,128)(2,1)S(1)}, u32[]{:S(2)}, u32[]{:S(2)}) collective-permute-start(bf16[128,768]{1,0:T(8,128)(2,1)S(1)} %collective-permute-done.9.refs_5_), channel_id=1, source_target_pairs={{0,2},{1,3},{2,0},{3,1},{4,6},{5,7},{6,4},{7,5},{8,10},{9,11},{10,... | collective-permute-start | bytes 589832 | tf_op jit(solution)/shard_map/ppermute | solution.py:300
  23.1 5.5 %collective-permute-start.11 = (bf16[112,768]{1,0:T(8,128)(2,1)S(1)}, bf16[112,768]{1,0:T(8,128)(2,1)S(1)}, u32[]{:S(2)}, u32[]{:S(2)}) collective-permute-start(bf16[112,768]{1,0:T(8,128)(2,1)S(1)} %shard_map.126), channel_id=1, source_target_pairs={{0,2},{1,3},{2,0},{3,1},{4,6},{5,7},{6,4},{7,5},{8,10},{9,11},{10,... | collective-permute-start | bytes 516104 | tf_op jit(solution)/shard_map/ppermute | solution.py:300
  23.2 7.8 %collective-permute-start.8 = (bf16[144,768]{1,0:T(8,128)(2,1)S(1)}, bf16[144,768]{1,0:T(8,128)(2,1)S(1)}, u32[]{:S(2)}, u32[]{:S(2)}) collective-permute-start(bf16[144,768]{1,0:T(8,128)(2,1)S(1)} %collective-permute-done.1.refs_1_.refs_7_.refs_3_), channel_id=1, source_target_pairs={{0,2},{1,3},{2,0},{3,1},{4,6},{5,7},{6,4},{7,5},{8,10},{9,11},{10,... | collective-permute-start | bytes 663560 | tf_op jit(solution)/shard_map/ppermute | solution.py:300
  25.2 5.9 %collective-permute-start.7 = (bf16[144,768]{1,0:T(8,128)(2,1)S(1)}, bf16[144,768]{1,0:T(8,128)(2,1)S(1)}, u32[]{:S(2)}, u32[]{:S(2)}) collective-permute-start(bf16[144,768]{1,0:T(8,128)(2,1)S(1)} %collective-permute-done.1.refs_1_.refs_7_.refs_3_), channel_id=1, source_target_pairs={{0,4},{1,5},{2,6},{3,7},{4,0},{5,1},{6,2},{7,3},{8,12},{9,13},{10,... | collective-permute-start | bytes 663560 | tf_op jit(solution)/shard_map/ppermute | solution.py:300
  28.7 2.4 %collective-permute-start.12 = (bf16[128,768]{1,0:T(8,128)(2,1)S(1)}, bf16[128,768]{1,0:T(8,128)(2,1)S(1)}, u32[]{:S(2)}, u32[]{:S(2)}) collective-permute-start(bf16[128,768]{1,0:T(8,128)(2,1)S(1)} %get-tuple-element.32.refs_13_), channel_id=1, source_target_pairs={{0,1},{1,0},{2,3},{3,2},{4,5},{5,4},{6,7},{7,6},{8,9},{9,8},{10,11... | collective-permute-start | bytes 589832 | tf_op jit(solution)/shard_map/ppermute | solution.py:303
  28.7 2.4 %collective-permute-start.13 = (bf16[128,768]{1,0:T(8,128)(2,1)S(1)}, bf16[128,768]{1,0:T(8,128)(2,1)S(1)}, u32[]{:S(2)}, u32[]{:S(2)}) collective-permute-start(bf16[128,768]{1,0:T(8,128)(2,1)S(1)} %get-tuple-element.33.refs_14_), channel_id=1, source_target_pairs={{0,1},{1,0},{2,3},{3,2},{4,5},{5,4},{6,7},{7,6},{8,9},{9,8},{10,11... | collective-permute-start | bytes 589832 | tf_op jit(solution)/shard_map/ppermute | solution.py:303
  29.2 1.9 %collective-permute-start.14 = (bf16[128,768]{1,0:T(8,128)(2,1)S(1)}, bf16[128,768]{1,0:T(8,128)(2,1)S(1)}, u32[]{:S(2)}, u32[]{:S(2)}) collective-permute-start(bf16[128,768]{1,0:T(8,128)(2,1)S(1)} %get-tuple-element.34.refs_15_), channel_id=1, source_target_pairs={{0,1},{1,0},{2,3},{3,2},{4,5},{5,4},{6,7},{7,6},{8,9},{9,8},{10,11... | collective-permute-start | bytes 589832 | tf_op jit(solution)/shard_map/ppermute | solution.py:303
  31.1 7.2 %collective-permute-start.15 = (bf16[144,768]{1,0:T(8,128)(2,1)S(1)}, bf16[144,768]{1,0:T(8,128)(2,1)S(1)}, u32[]{:S(2)}, u32[]{:S(2)}) collective-permute-start(bf16[144,768]{1,0:T(8,128)(2,1)S(1)} %collective-permute-done.7.refs_1_.refs_9_), channel_id=1, source_target_pairs={{0,2},{1,3},{2,0},{3,1},{4,6},{5,7},{6,4},{7,5},{8,10},{9,11},{10,... | collective-permute-start | bytes 663560 | tf_op jit(solution)/shard_map/ppermute | solution.py:300
  31.5 6.8 %copy-start = (f32[15360]{0:T(1024)S(1)}, f32[15360]{0:T(1024)}, u32[]{:S(2)}) copy-start(f32[15360]{0:T(1024)} %param.18) | copy-start | bytes 184324
  40.4 1.3 %collective-permute-start.16 = (bf16[8,32,128]{2,1,0:T(8,128)(2,1)S(1)}, bf16[8,32,128]{2,1,0:T(8,128)(2,1)S(1)}, u32[]{:S(2)}, u32[]{:S(2)}) collective-permute-start(bf16[8,32,128]{2,1,0:T(8,128)(2,1)S(1)} %get-tuple-element.41), channel_id=1, source_target_pairs={{0,1},{1,0},{2,3},{3,2},{4,5},{5,4},{6,7},{7,6},{8,9},{9,8},{10,11... | collective-permute-start | bytes 196616 | tf_op jit(solution)/shard_map/ppermute | solution.py:303
